TPU v7x, 32 devices: a whole 2x2x4 slice. The times are simulated.
32 devices in a mesh: groups: 2 (over y), tensor: 16 (over z, x, core).
Axes of the slice: x: 2, y: 2, z: 4, core: 2. Of those that a mesh axis runs over, the one named last changes fastest.
Arguments:
- input_hidden: bfloat16 [128, 8192], P(('groups', 'tensor')), parts along dimension 0, may hold values from -6 to 6
- input_norm_gain: bfloat16 [8192], replicated, may hold values from 0.099609375 to 1.8984375
- request_adapter: int32 [128, 1], P(('groups', 'tensor')), parts along dimension 0, may hold values from 0 to 31; in each aligned block of 64 rows (0 to 63, 64 to 127, ...) at most 16 rows name the same one
- adapter_storage: int32 [32], replicated, may hold values from 0 to 31, each once
- lengths: int32 [128], P(('groups', 'tensor')), parts along dimension 0, may hold values from 1 to 384, as said below
- projection_weight: bfloat16 [8192, 10240], P(None, 'tensor'), may hold values from -0.0625 to 0.0625
- output_weight: bfloat16 [8192, 8192], P(None, 'tensor'), may hold values from -0.0625 to 0.0625
- adapter_down: bfloat16 [32, 8192, 64], P('tensor'), may hold values from -0.0625 to 0.0625
- projection_up_adapter: bfloat16 [32, 16, 10240], P(None, None, 'tensor'), may hold values from -1.5 to 1.5
- output_up_adapter: bfloat16 [32, 16, 8192], P(None, None, 'tensor'), may hold values from -1.5 to 1.5
- cache_keys: bfloat16 [128, 8, 384, 128], P(('groups', 'tensor')), parts along dimension 0, may hold values from -64 to 64
- cache_values: bfloat16 [128, 8, 384, 128], P(('groups', 'tensor')), parts along dimension 0, may hold values from -12 to 12
Outputs:
- attn_output: bfloat16 [128, 8192], P(('groups', 'tensor')), parts along dimension 0
There are 2 independent parts, one for each index of `groups`. A program takes and returns all parts, laid end to end along the dimension named above; an argument that names none is the same for every part. Nothing has to cross between parts.
Inputs may be any that keep to these rules, and one draw needn't show every extreme that they name: `request_adapter`: among the requests of one replica no adapter is named more than 16 times, a bound that some block reaches. `lengths`: some request of every draw has all 384 positions filled.
All inputs are finite; a program needn't handle non-finite values.
Results may differ from a plain program's by a relative error of at most 0.012.
The roundings to bfloat16 on the way count: a program that leaves them out, or rounds other values in their place, can miss the bound.
Values may be sent and summed in bfloat16 or wider, within the bound.
No kernel may reach another device: no remote copies, remote signals or barrier semaphores. Data moves between devices by JAX's collectives and lax.ppermute only.
A program may use at most 128 MiB of HBM per device.

v0:
```python
import jax
import jax.numpy as jnp
from jax import lax
from jax.sharding import PartitionSpec as P

MOST = 16


eps = 1e-05


def local(
    input_hidden,
    input_norm_gain,
    request_adapter,
    adapter_storage,
    lengths,
    projection_weight,
    output_weight,
    adapter_down,
    projection_up_adapter,
    output_up_adapter,
    cache_keys,
    cache_values,
):
    my_index = lax.axis_index("tensor")
    model_width = input_hidden.shape[1]
    local_rows = input_hidden.shape[0]
    rank_extent = projection_up_adapter.shape[1]
    count_held = adapter_down.shape[0]
    kv_heads = cache_keys.shape[1]
    context = cache_keys.shape[2]
    head_dim = cache_keys.shape[3]
    kv_width = kv_heads * head_dim
    hidden32 = input_hidden.astype(jnp.float32)
    power = jnp.mean(hidden32 * hidden32, axis=1, keepdims=True)
    normed = (hidden32 * lax.rsqrt(power + eps) * input_norm_gain.astype(jnp.float32)).astype(
        jnp.bfloat16
    )
    normed_all, gathered_adapters = (
        lax.all_gather(normed, "tensor", axis=0, tiled=True),
        lax.all_gather(request_adapter[:, 0], "tensor", axis=0, tiled=True),
    )
    total_rows = normed_all.shape[0]
    adapter_range = jnp.arange(adapter_storage.shape[0], dtype=jnp.int32)
    row_range = jnp.arange(total_rows, dtype=jnp.int32)

    def down_terms(rows, lower_limit, upper_limit):
        summed = jnp.zeros((total_rows, upper_limit - lower_limit), jnp.float32)
        for local_slot_index in range(count_held):
            storage = my_index * count_held + local_slot_index
            adapter_name = jnp.sum(jnp.where(adapter_storage == storage, adapter_range, 0))
            ranked = jnp.argsort(
                (gathered_adapters != adapter_name).astype(jnp.int32), stable=True
            )[:MOST]
            usable = gathered_adapters[ranked] == adapter_name
            products = jnp.dot(
                rows[ranked],
                adapter_down[local_slot_index, :, lower_limit:upper_limit],
                preferred_element_type=jnp.float32,
            )
            placed = ((ranked[:, None] == row_range[None, :]) & usable[:, None]).astype(jnp.float32)
            summed = summed + jnp.dot(placed.T, products, precision=lax.Precision.HIGHEST)
        return summed

    down_qkv = lax.psum(down_terms(normed_all, 0, 3 * rank_extent), "tensor").astype(jnp.bfloat16)
    columns = projection_weight.shape[1]
    column_ids = my_index * columns + jnp.arange(columns, dtype=jnp.int32)
    segment = (column_ids >= model_width).astype(jnp.int32) + (
        column_ids >= model_width + kv_width
    ).astype(jnp.int32)
    selector = (segment[None, :] == jnp.arange(3, dtype=jnp.int32)[:, None]).astype(jnp.float32)
    base = jnp.dot(normed_all, projection_weight, preferred_element_type=jnp.float32)
    lifted = jnp.einsum(
        "rsk,rkc->rsc",
        down_qkv.reshape(total_rows, 3, rank_extent),
        projection_up_adapter[gathered_adapters],
        preferred_element_type=jnp.float32,
    )
    qkv_columns = (base + jnp.sum(lifted * selector[None], axis=1)).astype(jnp.bfloat16)
    qkv_mine = lax.all_to_all(qkv_columns, "tensor", split_axis=0, concat_axis=1, tiled=True)
    groups_per = model_width // head_dim // kv_heads
    query = qkv_mine[:, 0:model_width].reshape(local_rows, kv_heads, groups_per, head_dim)
    key_new = qkv_mine[:, model_width : model_width + kv_width].reshape(
        local_rows, kv_heads, head_dim
    )
    value_new = qkv_mine[:, model_width + kv_width :].reshape(local_rows, kv_heads, head_dim)
    scale = head_dim ** (-0.5)
    scores = (
        jnp.einsum("bhgd,bhpd->bhgp", query, cache_keys, preferred_element_type=jnp.float32) * scale
    )
    live = jnp.arange(context, dtype=jnp.int32)[None, :] < lengths[:, None]
    scores = jnp.where(live[:, None, None, :], scores, -1e30)
    own = jnp.einsum("bhgd,bhd->bhg", query, key_new, preferred_element_type=jnp.float32) * scale
    peak = jnp.maximum(jnp.max(scores, axis=3), own)
    weights = jnp.exp(scores - peak[..., None])
    own_weight = jnp.exp(own - peak)
    denominator = jnp.sum(weights, axis=3) + own_weight
    probs = (weights / denominator[..., None]).astype(jnp.bfloat16)
    own_prob = (own_weight / denominator).astype(jnp.bfloat16)
    mixed = jnp.einsum("bhgp,bhpd->bhgd", probs, cache_values, preferred_element_type=jnp.float32)
    mixed = (
        mixed
        + own_prob.astype(jnp.float32)[..., None] * value_new.astype(jnp.float32)[:, :, None, :]
    )
    attended = mixed.reshape(local_rows, model_width).astype(jnp.bfloat16)
    attended_all = lax.all_gather(attended, "tensor", axis=0, tiled=True)
    output_down = lax.psum(
        down_terms(attended_all, 3 * rank_extent, 4 * rank_extent), "tensor"
    ).astype(jnp.bfloat16)
    projected = jnp.dot(attended_all, output_weight, preferred_element_type=jnp.float32)
    projected = projected + jnp.einsum(
        "xt,xtq->xq",
        output_down,
        output_up_adapter[gathered_adapters],
        preferred_element_type=jnp.float32,
    )
    return lax.all_to_all(
        projected.astype(jnp.bfloat16), "tensor", split_axis=0, concat_axis=1, tiled=True
    )


def solution(mesh):
    return jax.shard_map(
        local,
        mesh=mesh,
        in_specs=(
            P(("groups", "tensor"), None),
            P(),
            P(("groups", "tensor"), None),
            P(),
            P(("groups", "tensor")),
            P(None, "tensor"),
            P(None, "tensor"),
            P("tensor", None, None),
            P(None, None, "tensor"),
            P(None, None, "tensor"),
            P(("groups", "tensor"), None, None, None),
            P(("groups", "tensor"), None, None, None),
        ),
        out_specs=P(("groups", "tensor"), None),
        check_vma=False,
    )
```

profile of v0, /device:TPU:0, one launch (start us, length us, event | category | flops | bytes accessed | tf_op | source)
XLA Modules:
  0.0 247.4 jit_solution(8879484586663239447)
XLA Ops:
  6.5 0.0 copy-start
  6.5 0.0 all-gather.6.cloned.1.call-start
  6.5 0.9 convert_element_type.80
  7.4 1.1 fusion.20
  8.5 1.6 fusion.23
  10.1 0.0 all-gather.6.cloned.1.call-update
  10.1 1.3 dynamic-slice
  12.2 0.8 bitcast_dynamic-update-slice_fusion
  12.9 13.7 %all-reduce = s32[64]{0:T(128)S(1)} all-reduce(s32[64]{0:T(128)S(1)} %bitcast_dynamic-update-slice_fusion), channel_id=2, replica_groups=mesh['groups'=2,'tensor'=16] {'tensor'}, use_global_device_ids=true, to_apply=%add | all-reduce | flops 64 | bytes 512 | tf_op jit(solution)/shard_map/all_gather | solution.py:42
  26.6 1.3 fusion.51
  27.9 1.2 compare_convert_fusion
  29.1 2.1 sort.35
  31.2 0.7 gather_fusion
  31.9 2.1 sort.36
  34.0 0.7 gather_fusion.2
  34.7 2.9 %gather_fusion.4 = bf16[64,16,640]{2,1,0:T(8,128)(2,1)} fusion(bf16[32,16,640]{2,1,0:T(8,128)(2,1)} %param.20, s32[1024]{0:T(1024)S(1)} %pad_clamp_fusion), kind=kCustom, calls=%fused_computation.4 | custom fusion | bytes 2621696 | tf_op jit(solution)/shard_map/gather | solution.py:77
  37.6 0.6 broadcast_compare_fusion.1
  38.2 0.6 broadcast_compare_fusion
  38.8 13.5 %all-gather.6.cloned.1.call-done = bf16[16,4,8192]{2,1,0:T(4,128)(2,1)} async-done(((bf16[1,4,8192]{2,1,0:T(4,128)(2,1)}), bf16[16,4,8192]{2,1,0:T(4,128)(2,1)}) %all-gather.6.cloned.1.call-update) | async-done | bytes 1048592 | tf_op jit(solution)/shard_map/all_gather | solution.py:41
  52.3 2.1 reshape.173
  54.4 3.0 %gather_fusion.1 = bf16[16,8192]{1,0:T(8,128)(2,1)} fusion(bf16[64,8192]{1,0:T(8,128)(2,1)} %reshape.173, s32[1024]{0:T(1024)S(1)} %pad_clamp_fusion.2), kind=kCustom, calls=%fused_computation.1 | custom fusion | bytes 524352 | tf_op jit(solution)/shard_map/gather | solution.py:58
  57.4 2.3 gather_fusion.3
  59.8 1.5 fusion.7
  61.3 1.5 fusion.5
  62.7 0.2 fusion.34
  63.0 0.2 convolution_add_fusion.3
  63.2 59.6 %psum.14 = bf16[64,48]{0,1:T(8,128)(2,1)S(1)} all-reduce(f32[64,48]{0,1:T(8,128)S(1)} %convolution_add_fusion.3), channel_id=1, replica_groups=mesh['groups'=2,'tensor'=16] {'tensor'}, use_global_device_ids=true, to_apply=%region_5.6 | all-reduce | flops 3072 | bytes 18432 | tf_op jit(solution)/shard_map/psum | solution.py:66
  122.8 0.1 copy.17
  123.0 1.9 fusion
  124.8 0.0 copy-start.2
  124.9 6.1 %fusion.2 = bf16[64,640]{1,0:T(8,128)(2,1)S(1)} fusion(f32[64,640]{1,0:T(8,128)S(1)} %fusion, bf16[64,8192]{1,0:T(8,128)(2,1)} %reshape.173, bf16[8192,640]{1,0:T(8,128)(2,1)} %param.17), kind=kOutput, calls=%fused_computation.15 | convolution fusion | flops 671170560 | bytes 11780096 | tf_op jit(solution)/shard_map/dot_general | solution.py:73
  131.0 0.6 all_to_all.28
  131.7 3.5 %all-to-all-start = ((bf16[16,4,640]{2,1,0:T(4,128)(2,1)}), bf16[16,4,640]{2,1,0:T(4,128)(2,1)S(1)}, u32[]{:S(2)}, u32[]{:S(2)}) async-start(bf16[16,4,640]{2,1,0:T(4,128)(2,1)} %all_to_all.28), calls=%async_computation | async-start | bytes 163840 | tf_op jit(solution)/shard_map/all_to_all | solution.py:81
  135.2 0.0 all-gather.8.cloned.1.call-start
  135.2 0.0 copy-done.2
  135.2 0.1 iota_compare_fusion.3
  135.3 7.0 %all-to-all-done = bf16[16,4,640]{2,1,0:T(4,128)(2,1)S(1)} async-done(((bf16[16,4,640]{2,1,0:T(4,128)(2,1)}), bf16[16,4,640]{2,1,0:T(4,128)(2,1)S(1)}, u32[]{:S(2)}, u32[]{:S(2)}) %all-to-all-start) | async-done | bytes 81952 | tf_op jit(solution)/shard_map/all_to_all | solution.py:81
  142.3 0.0 copy-start.1
  142.4 0.1 fusion.24
  142.5 0.0 copy-done
  142.5 1.3 fusion.54
  143.8 0.2 fusion.11
  144.1 0.2 copy-done.1
  144.2 0.7 fusion.3
  144.9 0.7 reshape.174
  145.6 0.0 all-gather.8.cloned.1.call-update
  145.6 2.7 %gather_fusion.7 = bf16[64,16,512]{2,1,0:T(8,128)(2,1)} fusion(bf16[32,16,512]{2,1,0:T(8,128)(2,1)} %param.21, s32[1024]{0:T(1024)S(1)} %pad_clamp_fusion), kind=kCustom, calls=%fused_computation.7 | custom fusion | bytes 2097408 | tf_op jit(solution)/shard_map/gather | solution.py:115
  148.3 32.8 %all-gather.8.cloned.1.call-done = bf16[16,4,8192]{2,1,0:T(4,128)(2,1)} async-done(((bf16[1,4,8192]{2,1,0:T(4,128)(2,1)}), bf16[16,4,8192]{2,1,0:T(4,128)(2,1)}) %all-gather.8.cloned.1.call-update) | async-done | bytes 1048592 | tf_op jit(solution)/shard_map/all_gather | solution.py:107
  181.1 2.2 reshape.175
  183.2 2.3 gather_fusion.6
  185.6 3.0 %gather_fusion.5 = bf16[16,8192]{1,0:T(8,128)(2,1)} fusion(bf16[64,8192]{1,0:T(8,128)(2,1)} %reshape.175, s32[1024]{0:T(1024)S(1)} %pad_clamp_fusion.2), kind=kCustom, calls=%fused_computation.5 | custom fusion | bytes 524352 | tf_op jit(solution)/shard_map/gather | solution.py:58
  188.6 1.2 fusion.12
  189.7 1.3 fusion.14
  191.0 0.2 fusion.32
  191.2 0.2 convolution_add_fusion.4
  191.4 32.1 %psum.15 = bf16[64,16]{0,1:T(8,128)(2,1)S(1)} all-reduce(f32[64,16]{0,1:T(8,128)S(1)} %convolution_add_fusion.4), channel_id=1, replica_groups=mesh['groups'=2,'tensor'=16] {'tensor'}, use_global_device_ids=true, to_apply=%region_9.10 | all-reduce | flops 1024 | bytes 6144 | tf_op jit(solution)/shard_map/psum | solution.py:108
  223.5 0.1 copy.21
  223.7 1.5 fusion.55
  225.2 5.3 %fusion.4 = bf16[64,512]{1,0:T(8,128)(2,1)S(1)} fusion(bf16[64,8192]{1,0:T(8,128)(2,1)} %reshape.175, bf16[8192,512]{1,0:T(8,128)(2,1)} %param.18, f32[64,1,512]{2,1,0:T(1,128)S(1)} %fusion.55), kind=kOutput, calls=%fused_computation.17 | convolution fusion | flops 536936448 | bytes 9633792 | tf_op jit(solution)/shard_map/dot_general | solution.py:111
  230.5 9.5 %all_to_all.38 = bf16[16,4,512]{2,1,0:T(4,128)(2,1)S(1)} all-to-all(bf16[16,4,512]{2,1,0:T(4,128)(2,1)S(1)} %all_to_all.32), channel_id=1, replica_groups=mesh['groups'=2,'tensor'=16] {'tensor'}, dimensions={0} | all-to-all | bytes 131072 | tf_op jit(solution)/shard_map/all_to_all | solution.py:118
  239.9 0.6 copy.40
  (19 shorter events, 0.2 us)
Async XLA Ops:
  6.5 136.0 %copy-start = (bf16[4,8,384,128]{3,2,1,0:T(8,128)(2,1)S(1)}, bf16[4,8,384,128]{3,2,1,0:T(8,128)(2,1)}, u32[]{:S(2)}) copy-start(bf16[4,8,384,128]{3,2,1,0:T(8,128)(2,1)} %param.22) | copy-start | bytes 9437188
  6.5 45.8 %all-gather.6.cloned.1.call-start = ((), (), s32[]{:S(2)}) async-start(), calls=%async_computation.2 | async-start | bytes 1114112 | tf_op jit(solution)/shard_map/all_gather | solution.py:41
  124.8 10.4 %copy-start.2 = (s32[4]{0:T(128)S(1)}, s32[4]{0:T(128)}, u32[]{:S(2)}) copy-start(s32[4]{0:T(128)} %param.16) | copy-start | bytes 52
  131.7 10.6 %all-to-all-start = ((bf16[16,4,640]{2,1,0:T(4,128)(2,1)}), bf16[16,4,640]{2,1,0:T(4,128)(2,1)S(1)}, u32[]{:S(2)}, u32[]{:S(2)}) async-start(bf16[16,4,640]{2,1,0:T(4,128)(2,1)} %all_to_all.28), calls=%async_computation | async-start | bytes 163840 | tf_op jit(solution)/shard_map/all_to_all | solution.py:81
  135.2 45.9 %all-gather.8.cloned.1.call-start = ((), (), s32[]{:S(2)}) async-start(), calls=%async_computation.3 | async-start | bytes 1114112 | tf_op jit(solution)/shard_map/all_gather | solution.py:107
  142.3 1.9 copy-start.1
Sparse Core Ops, SparseCore 0:
  10.2 42.0 all-gather.5
  145.8 35.2 all-gather.7
where the time goes:
time: 248 us; the launch traced here: 247 us
  blocking collectives  115 us (46%)
  waiting for transfers between devices  53.3 us (21%)
  local copies, waits for them, and re-layouts  26.3 us (11%)
  matrix products  23.2 us (9%)
  between operations  14.3 us (6%)
  other arithmetic  11.9 us (5%)
  starting transfers between devices  3.55 us (1%)
    psum x1, blocking collectives, local(): lax.psum(down_terms(normed_all, 0, 3 * rank_extent), 'tensor')  59.6 us
    all_gather x1, waiting for transfers between devices, local(): attended_all = lax.all_gather(attended, 'tensor', axis=0, tiled=True)  32.8 us
    psum x1, blocking collectives, local(): lax.psum(down_terms(attended_all, 3 * rank_extent, 4 * rank_extent), 'ten...  32.1 us
    all_gather x1, blocking collectives, local(): lax.all_gather(request_adapter[:, 0], 'tensor', axis=0, tiled=True)  13.7 us
    all_gather x1, waiting for transfers between devices, local(): lax.all_gather(normed, 'tensor', axis=0, tiled=True)  13.5 us
    gather x4, local copies, waits for them, and re-layouts, down_terms(): rows[ranked]  10.6 us
    all_to_all x1, blocking collectives, local(): lax.all_to_all(projected.astype(jnp.bfloat16), 'tensor', split_axis=0, co...  9.48 us
    unnamed x15, local copies, waits for them, and re-layouts  7.88 us
  transfers between devices with their start and end apart: 3, of which 3 were waited for; matrix products, arithmetic and copies ran while one was open for 7% of the time, Pallas kernels for 0%

commit v1 on v0

v1 whole, which is shorter than its diff:
```python
import jax
import jax.numpy as jnp
from jax import lax
from jax.sharding import PartitionSpec as P

eps = 1e-05
AXIS = "tensor"


def swap(x, count, offset):
    return lax.ppermute(x, AXIS, [(i, i ^ offset) for i in range(count)])


def gather_rows(x, count):
    step = count // 4
    held = [jnp.concatenate([x] + [swap(x, count, k * step) for k in (1, 2, 3)], axis=0)]
    order = [[0, step, 2 * step, 3 * step]]
    step //= 2
    while step:
        held = held + [swap(h, count, step) for h in held]
        order = order + [[j ^ step for j in o] for o in order]
        step //= 2
    return jnp.concatenate(held, axis=0), sum(order, [])


def sum_over(x, count):
    step = count
    while step > 1:
        radix = 4 if step % 4 == 0 else 2
        step //= radix
        others = [swap(x, count, k * step) for k in range(1, radix)]
        for other in others:
            x = x + other
    return x


def local(
    input_hidden,
    input_norm_gain,
    request_adapter,
    adapter_storage,
    lengths,
    projection_weight,
    output_weight,
    adapter_down,
    projection_up_adapter,
    output_up_adapter,
    cache_keys,
    cache_values,
    *,
    count,
):
    me = lax.axis_index(AXIS)
    model_width = input_hidden.shape[1]
    local_rows = input_hidden.shape[0]
    adapters, rank = projection_up_adapter.shape[:2]
    held = adapter_down.shape[0]
    kv_heads, context, head_dim = cache_keys.shape[1:]
    kv_width = kv_heads * head_dim
    total = local_rows * count

    hidden32 = input_hidden.astype(jnp.float32)
    power = jnp.mean(hidden32 * hidden32, axis=1, keepdims=True)
    normed = (hidden32 * lax.rsqrt(power + eps) * input_norm_gain.astype(jnp.float32)).astype(
        jnp.bfloat16
    )
    ids = jnp.broadcast_to(request_adapter.astype(jnp.bfloat16), (local_rows, 128))
    rows, order = gather_rows(jnp.concatenate([normed, ids], axis=1), count)
    ids = rows[:, model_width].astype(jnp.int32)
    normed_all = rows[:, :model_width]

    devices = me ^ jnp.array(order, jnp.int32)
    place = (devices[:, None] * local_rows + jnp.arange(local_rows, dtype=jnp.int32)).reshape(-1)
    to_place = (jnp.arange(total, dtype=jnp.int32)[:, None] == place[None, :]).astype(jnp.bfloat16)
    named = ids[:, None] == jnp.arange(adapters, dtype=jnp.int32)[None, :]
    slots = jnp.sum(jnp.where(named, adapter_storage[None, :], 0), axis=1)
    spread = jnp.repeat(named, rank, axis=1)

    def move(matrix, x):
        return jnp.dot(matrix, x, preferred_element_type=jnp.float32).astype(jnp.bfloat16)

    def downs(x, low, high):
        summed = jnp.zeros((total, high - low), jnp.float32)
        for s in range(held):
            product = jnp.dot(x, adapter_down[s, :, low:high], preferred_element_type=jnp.float32)
            summed = jnp.where((slots == me * held + s)[:, None], product, summed)
        mine = move(to_place, summed.astype(jnp.bfloat16))
        return move(to_place.T, sum_over(mine, count))

    def lift(down, up):
        wide = jnp.where(spread, jnp.tile(down, (1, adapters)), 0)
        return jnp.dot(
            wide, up.reshape(adapters * rank, up.shape[2]), preferred_element_type=jnp.float32
        )

    down_qkv = downs(normed_all, 0, 3 * rank)
    columns = projection_weight.shape[1]
    column_ids = me * columns + jnp.arange(columns, dtype=jnp.int32)
    segment = (column_ids >= model_width).astype(jnp.int32) + (
        column_ids >= model_width + kv_width
    ).astype(jnp.int32)
    base = jnp.dot(normed_all, projection_weight, preferred_element_type=jnp.float32)
    for g in range(3):
        lifted = lift(down_qkv[:, g * rank : (g + 1) * rank], projection_up_adapter)
        base = base + jnp.where((segment == g)[None, :], lifted, 0.0)
    qkv_columns = move(to_place, base.astype(jnp.bfloat16))
    qkv_mine = lax.all_to_all(qkv_columns, AXIS, split_axis=0, concat_axis=1, tiled=True)

    groups_per = model_width // head_dim // kv_heads
    query = qkv_mine[:, 0:model_width].reshape(local_rows, kv_heads, groups_per, head_dim)
    key_new = qkv_mine[:, model_width : model_width + kv_width].reshape(
        local_rows, kv_heads, head_dim
    )
    value_new = qkv_mine[:, model_width + kv_width :].reshape(local_rows, kv_heads, head_dim)
    scale = head_dim ** (-0.5)
    scores = (
        jnp.einsum("bhgd,bhpd->bhgp", query, cache_keys, preferred_element_type=jnp.float32) * scale
    )
    live = jnp.arange(context, dtype=jnp.int32)[None, :] < lengths[:, None]
    scores = jnp.where(live[:, None, None, :], scores, -1e30)
    own = jnp.einsum("bhgd,bhd->bhg", query, key_new, preferred_element_type=jnp.float32) * scale
    peak = jnp.maximum(jnp.max(scores, axis=3), own)
    weights = jnp.exp(scores - peak[..., None])
    own_weight = jnp.exp(own - peak)
    denominator = jnp.sum(weights, axis=3) + own_weight
    probs = (weights / denominator[..., None]).astype(jnp.bfloat16)
    own_prob = (own_weight / denominator).astype(jnp.bfloat16)
    mixed = jnp.einsum("bhgp,bhpd->bhgd", probs, cache_values, preferred_element_type=jnp.float32)
    mixed = (
        mixed
        + own_prob.astype(jnp.float32)[..., None] * value_new.astype(jnp.float32)[:, :, None, :]
    )
    attended = mixed.reshape(local_rows, model_width).astype(jnp.bfloat16)

    attended_all, _ = gather_rows(attended, count)
    output_down = downs(attended_all, 3 * rank, 4 * rank)
    projected = jnp.dot(attended_all, output_weight, preferred_element_type=jnp.float32)
    projected = projected + lift(output_down, output_up_adapter)
    sent = move(to_place, projected.astype(jnp.bfloat16))
    return lax.all_to_all(sent, AXIS, split_axis=0, concat_axis=1, tiled=True)


def solution(mesh):
    count = mesh.shape[AXIS]

    def body(*arrays):
        return local(*arrays, count=count)

    return jax.shard_map(
        body,
        mesh=mesh,
        in_specs=(
            P(("groups", "tensor"), None),
            P(),
            P(("groups", "tensor"), None),
            P(),
            P(("groups", "tensor")),
            P(None, "tensor"),
            P(None, "tensor"),
            P("tensor", None, None),
            P(None, None, "tensor"),
            P(None, None, "tensor"),
            P(("groups", "tensor"), None, None, None),
            P(("groups", "tensor"), None, None, None),
        ),
        out_specs=P(("groups", "tensor"), None),
        check_vma=False,
    )
```

time: 248 us -> 137 us (0.55)
  blocking collectives: 115 us -> 10.5 us
  starting transfers between devices: 3.55 us -> 28.8 us
  waiting for transfers between devices: 53.3 us -> 38.7 us
  between operations: 14.3 us -> 0.33 us
  local copies, waits for them, and re-layouts: 26.3 us -> 21.9 us
  matrix products: 23.2 us -> 27.3 us
  other arithmetic: 11.9 us -> 7.83 us
    psum x2 -> x0, blocking collectives: 91.7 us -> none  [the longest x1 59.6 us: local(): lax.psum(down_terms(normed_all, 0, 3 * rank_extent), 'tensor')]
    all_gather x2 -> x0, waiting for transfers between devices: 46.2 us -> none  [the longest x1 32.8 us: local(): attended_all = lax.all_gather(attended, 'tensor', axis=0, tiled=True)]
    ppermute x0 -> x24, waiting for transfers between devices: none -> 32.3 us  [swap(): return lax.ppermute(x, AXIS, [(i, i ^ offset) for i in range(count)])]
    ppermute x0 -> x24, starting transfers between devices: none -> 25.3 us  [swap(): return lax.ppermute(x, AXIS, [(i, i ^ offset) for i in range(count)])]
    concatenate x0 -> x2, local copies, waits for them, and re-layouts: none -> 17.8 us  [gather_rows(): return (jnp.concatenate(held, axis=0), sum(order, []))]
    gather x8 -> x0, local copies, waits for them, and re-layouts: 17.5 us -> none  [the longest x4 10.6 us: down_terms(): rows[ranked]]
    all_gather x1 -> x0, blocking collectives: 13.7 us -> none  [local(): lax.all_gather(request_adapter[:, 0], 'tensor', axis=0, tiled=True)]
    unnamed x15 -> x38, local copies, waits for them, and re-layouts: 7.88 us -> 2.51 us
  transfers between devices with their start and end apart: 3 -> 25, of which waited for: 3 -> 15; matrix products, arithmetic and copies ran while one was open for 7% -> 3% of each run, Pallas kernels for 0% -> 0%
where the time goes in v1:
time: 137 us; the launch traced here: 135 us
  waiting for transfers between devices  38.7 us (28%)
  starting transfers between devices  28.8 us (21%)
  matrix products  27.3 us (20%)
  local copies, waits for them, and re-layouts  21.9 us (16%)
  blocking collectives  10.5 us (8%)
  other arithmetic  7.83 us (6%)
    ppermute x24, waiting for transfers between devices, swap(): return lax.ppermute(x, AXIS, [(i, i ^ offset) for i in range(count)])  32.3 us
    ppermute x24, starting transfers between devices, swap(): return lax.ppermute(x, AXIS, [(i, i ^ offset) for i in range(count)])  25.3 us
    concatenate x2, local copies, waits for them, and re-layouts, gather_rows(): return (jnp.concatenate(held, axis=0), sum(order, []))  17.8 us
    dot_general x6, matrix products, move(): jnp.dot(matrix, x, preferred_element_type=jnp.float32).astype(jnp.bfloat16)  15.7 us
    all_to_all x1, blocking collectives, local(): return lax.all_to_all(sent, AXIS, split_axis=0, concat_axis=1, tiled=True)  10.5 us
    all_to_all x1, waiting for transfers between devices, local(): lax.all_to_all(qkv_columns, AXIS, split_axis=0, concat_axis=1, tiled=True)  6.38 us
    dot_general x4, matrix products, lift(): jnp.dot(wide, up.reshape(adapters * rank, up.shape[2]), preferred_element...  5.96 us
    all_to_all x1, starting transfers between devices, local(): lax.all_to_all(qkv_columns, AXIS, split_axis=0, concat_axis=1, tiled=True)  3.5 us
  transfers between devices with their start and end apart: 25, of which 15 were waited for; matrix products, arithmetic and copies ran while one was open for 3% of the time, Pallas kernels for 0%

profile of v1, /device:TPU:0, one launch (start us, length us, event | category | flops | bytes accessed | tf_op | source)
XLA Modules:
  0.0 135.3 jit_solution(9612418133411086484)
XLA Ops:
  0.0 0.9 convert_element_type.102
  0.9 1.1 fusion.34
  2.0 0.7 convert_bitcast_fusion.1
  2.7 0.9 fusion.36
  3.7 3.1 %collective-permute-start = (bf16[4,8320]{1,0:T(4,128)(2,1)S(1)}, bf16[4,8320]{1,0:T(4,128)(2,1)S(1)}, u32[]{:S(2)}, u32[]{:S(2)}) collective-permute-start(bf16[4,8320]{1,0:T(4,128)(2,1)S(1)} %pad_maximum_fusion.2), channel_id=1, source_target_pairs={{0,4},{1,5},{2,6},{3,7},{4,0},{5,1},{6,2},{7,3},{8,12},{9,13},{10,... | collective-permute-start | bytes 199688 | tf_op jit(solution)/shard_map/ppermute | solution.py:11
  6.8 2.6 %collective-permute-start.1 = (bf16[4,8320]{1,0:T(4,128)(2,1)S(1)}, bf16[4,8320]{1,0:T(4,128)(2,1)S(1)}, u32[]{:S(2)}, u32[]{:S(2)}) collective-permute-start(bf16[4,8320]{1,0:T(4,128)(2,1)S(1)} %pad_maximum_fusion.2), channel_id=1, source_target_pairs={{0,8},{1,9},{2,10},{3,11},{4,12},{5,13},{6,14},{7,15},{8,0},{9,1},... | collective-permute-start | bytes 199688 | tf_op jit(solution)/shard_map/ppermute | solution.py:11
  9.4 4.7 %collective-permute-done.1 = bf16[4,8320]{1,0:T(4,128)(2,1)S(1)} collective-permute-done((bf16[4,8320]{1,0:T(4,128)(2,1)S(1)}, bf16[4,8320]{1,0:T(4,128)(2,1)S(1)}, u32[]{:S(2)}, u32[]{:S(2)}) %collective-permute-start.1) | collective-permute-done | bytes 66592 | tf_op jit(solution)/shard_map/ppermute | solution.py:11
  14.1 1.4 %collective-permute-done.2 = bf16[4,8320]{1,0:T(4,128)(2,1)S(1)} collective-permute-done((bf16[4,8320]{1,0:T(4,128)(2,1)S(1)}, bf16[4,8320]{1,0:T(4,128)(2,1)S(1)}, u32[]{:S(2)}, u32[]{:S(2)}) %collective-permute-start.2) | collective-permute-done | bytes 66592 | tf_op jit(solution)/shard_map/ppermute | solution.py:11
  15.6 0.2 pad_maximum_fusion
  15.7 1.6 %collective-permute-start.3 = (bf16[16,8320]{1,0:T(8,128)(2,1)S(1)}, bf16[16,8320]{1,0:T(8,128)(2,1)}, u32[]{:S(2)}, u32[]{:S(2)}) collective-permute-start(bf16[16,8320]{1,0:T(8,128)(2,1)S(1)} %pad_maximum_fusion), channel_id=1, source_target_pairs={{0,2},{1,3},{2,0},{3,1},{4,6},{5,7},{6,4},{7,5},{8,10},{9,11},{10,... | collective-permute-start | bytes 798728 | tf_op jit(solution)/shard_map/ppermute | solution.py:11
  17.3 0.7 xor_multiply_fusion
  17.9 4.4 %collective-permute-done.3 = bf16[16,8320]{1,0:T(8,128)(2,1)} collective-permute-done((bf16[16,8320]{1,0:T(8,128)(2,1)S(1)}, bf16[16,8320]{1,0:T(8,128)(2,1)}, u32[]{:S(2)}, u32[]{:S(2)}) %collective-permute-start.3) | collective-permute-done | bytes 266272 | tf_op jit(solution)/shard_map/ppermute | solution.py:11
  22.3 0.7 iota_add_fusion
  23.0 0.8 add.118
  23.8 0.6 fusion.73
  24.4 11.4 %concatenate.19 = bf16[64,8320]{1,0:T(8,128)(2,1)} concatenate(bf16[4,8320]{1,0:T(4,128)(2,1)S(1)} %pad_maximum_fusion.2, bf16[4,8320]{1,0:T(4,128)(2,1)S(1)} %collective-permute-done, bf16[4,8320]{1,0:T(4,128)(2,1)} %copy-done.2, bf16[4,8320]{1,0:T(4,128)(2,1)} %copy-done.3, bf16[16,8320]{1,0:T(8,128)(2,1)} %collective-permute-done.3, bf16[16,8320]{1,0:T(8,128)(2,1)} %collective-permute-done.4, ...), dimensions={0} | concatenate | bytes 2129920 | tf_op jit(solution)/shard_map/concatenate | solution.py:23
  35.9 0.8 convert_reduce_fusion
  36.8 1.9 %convolution_select_fusion = bf16[64,48]{0,1:T(8,128)(2,1)S(1)} fusion(bf16[64,8320]{1,0:T(8,128)(2,1)} %concatenate.19, bf16[2,8192,64]{1,2,0:T(8,128)(2,1)} %param.20, pred[64]{0:T(512)(128)(4,1)S(1)} %get-tuple-element.13), kind=kOutput, calls=%fused_computation.21 | convolution fusion | flops 50334720 | bytes 1841216 | tf_op jit(solution)/shard_map/dot_general | solution.py:85
  38.7 2.0 %convolution_convert_fusion.2 = bf16[64,48]{0,1:T(8,128)(2,1)S(1)} fusion(bf16[64,48]{0,1:T(8,128)(2,1)S(1)} %convolution_select_fusion, bf16[64,8320]{1,0:T(8,128)(2,1)} %concatenate.19, bf16[2,8192,64]{1,2,0:T(8,128)(2,1)} %param.20, s32[64]{0:T(128)S(1)} %add.118, pred[64]{0:T(512)(128)(4,1)S(1)} %get-tuple-element.12), kind=kOutput, calls=%fused_computation.25 | convolution fusion | flops 50735104 | bytes 1847616 | tf_op jit(solution)/shard_map/dot_general | solution.py:80
  40.7 0.8 collective-permute-start.6
  41.5 2.0 %collective-permute-start.7 = (bf16[64,48]{0,1:T(8,128)(2,1)S(1)}, bf16[64,48]{0,1:T(8,128)(2,1)S(1)}, u32[]{:S(2)}, u32[]{:S(2)}) collective-permute-start(bf16[64,48]{0,1:T(8,128)(2,1)S(1)} %convolution_convert_fusion.2), channel_id=1, source_target_pairs={{0,8},{1,9},{2,10},{3,11},{4,12},{5,13},{6,14},{7,15},{8,0},{9,1},... | collective-permute-start | bytes 18440 | tf_op jit(solution)/shard_map/ppermute | solution.py:11
  43.5 1.7 %collective-permute-start.8 = (bf16[64,48]{0,1:T(8,128)(2,1)S(1)}, bf16[64,48]{0,1:T(8,128)(2,1)S(1)}, u32[]{:S(2)}, u32[]{:S(2)}) collective-permute-start(bf16[64,48]{0,1:T(8,128)(2,1)S(1)} %convolution_convert_fusion.2), channel_id=1, source_target_pairs={{0,12},{1,13},{2,14},{3,15},{4,8},{5,9},{6,10},{7,11},{8,4},{9,5},... | collective-permute-start | bytes 18440 | tf_op jit(solution)/shard_map/ppermute | solution.py:11
  45.2 1.0 collective-permute-done.7
  46.2 2.8 %collective-permute-done.8 = bf16[64,48]{0,1:T(8,128)(2,1)S(1)} collective-permute-done((bf16[64,48]{0,1:T(8,128)(2,1)S(1)}, bf16[64,48]{0,1:T(8,128)(2,1)S(1)}, u32[]{:S(2)}, u32[]{:S(2)}) %collective-permute-start.8) | collective-permute-done | bytes 6176 | tf_op jit(solution)/shard_map/ppermute | solution.py:11
  49.0 1.5 %collective-permute-start.10 = (bf16[64,48]{0,1:T(8,128)(2,1)S(1)}, bf16[64,48]{0,1:T(8,128)(2,1)S(1)}, u32[]{:S(2)}, u32[]{:S(2)}) collective-permute-start(bf16[64,48]{0,1:T(8,128)(2,1)S(1)} %add_add_fusion), channel_id=1, source_target_pairs={{0,2},{1,3},{2,0},{3,1},{4,6},{5,7},{6,4},{7,5},{8,10},{9,11},{10,... | collective-permute-start | bytes 18440 | tf_op jit(solution)/shard_map/ppermute | solution.py:11
  50.5 0.6 collective-permute-start.9
  51.1 1.5 %collective-permute-done.10 = bf16[64,48]{0,1:T(8,128)(2,1)S(1)} collective-permute-done((bf16[64,48]{0,1:T(8,128)(2,1)S(1)}, bf16[64,48]{0,1:T(8,128)(2,1)S(1)}, u32[]{:S(2)}, u32[]{:S(2)}) %collective-permute-start.10) | collective-permute-done | bytes 6176 | tf_op jit(solution)/shard_map/ppermute | solution.py:11
  52.7 0.9 collective-permute-done.11
  53.7 1.3 fusion.3
  55.1 1.3 fusion.2
  56.5 2.0 %fusion.1 = f32[64,640]{1,0:T(8,128)} fusion(bf16[32,16,640]{2,1,0:T(8,128)(2,1)} %param.21, pred[64,32]{0,1:T(8,128)(4,1)S(1)} %iota_compare_fusion.7, pred[640]{0:T(1024)(128)(4,1)S(1)} %copy-done.10, bf16[64,16]{0,1:T(8,128)(2,1)S(1)} %get-tuple-element.10), kind=kOutput, calls=%fused_computation.3 | convolution fusion | flops 42016768 | bytes 823936 | tf_op jit(solution)/shard_map/dot_general | solution.py:92
  58.5 6.3 %fusion.8 = bf16[64,640]{1,0:T(8,128)(2,1)S(1)} fusion(f32[64,640]{1,0:T(8,128)} %fusion.1, f32[64,640]{1,0:T(8,128)S(1)} %fusion.2, f32[64,640]{1,0:T(8,128)S(1)} %fusion.3, bf16[8192,640]{1,0:T(8,128)(2,1)} %param.18, bf16[64,8320]{1,0:T(8,128)(2,1)} %concatenate.19, s32[64]{0:T(128)} %copy-done.8), kind=kOutput, calls=%fused_computation.16 | convolution fusion | flops 676540416 | bytes 12108288 | tf_op jit(solution)/shard_map/dot_general | solution.py:80
  64.7 0.7 all_to_all.28
  65.4 3.5 %all-to-all-start = ((bf16[16,4,640]{2,1,0:T(4,128)(2,1)}), bf16[16,4,640]{2,1,0:T(4,128)(2,1)S(1)}, u32[]{:S(2)}, u32[]{:S(2)}) async-start(bf16[16,4,640]{2,1,0:T(4,128)(2,1)} %all_to_all.28), calls=%async_computation | async-start | bytes 163840 | tf_op jit(solution)/shard_map/all_to_all | solution.py:107
  68.9 0.7 iota_compare_fusion.8
  69.6 6.4 %all-to-all-done = bf16[16,4,640]{2,1,0:T(4,128)(2,1)S(1)} async-done(((bf16[16,4,640]{2,1,0:T(4,128)(2,1)}), bf16[16,4,640]{2,1,0:T(4,128)(2,1)S(1)}, u32[]{:S(2)}, u32[]{:S(2)}) %all-to-all-start) | async-done | bytes 81952 | tf_op jit(solution)/shard_map/all_to_all | solution.py:107
  76.3 1.3 fusion.84
  77.5 0.2 fusion.25
  77.8 0.3 copy-done.1
  78.1 0.7 fusion.11
  79.0 1.1 collective-permute-start.13
  80.1 3.3 %collective-permute-start.14 = (bf16[4,8192]{1,0:T(4,128)(2,1)S(1)}, bf16[4,8192]{1,0:T(4,128)(2,1)S(1)}, u32[]{:S(2)}, u32[]{:S(2)}) collective-permute-start(bf16[4,8192]{1,0:T(4,128)(2,1)S(1)} %bitcast.73), channel_id=1, source_target_pairs={{0,12},{1,13},{2,14},{3,15},{4,8},{5,9},{6,10},{7,11},{8,4},{9,5},... | collective-permute-start | bytes 196616 | tf_op jit(solution)/shard_map/ppermute | solution.py:11
  83.4 0.4 collective-permute-done.12
  83.8 3.5 %collective-permute-done.13 = bf16[4,8192]{1,0:T(4,128)(2,1)S(1)} collective-permute-done((bf16[4,8192]{1,0:T(4,128)(2,1)S(1)}, bf16[4,8192]{1,0:T(4,128)(2,1)S(1)}, u32[]{:S(2)}, u32[]{:S(2)}) %collective-permute-start.13) | collective-permute-done | bytes 65568 | tf_op jit(solution)/shard_map/ppermute | solution.py:11
  87.5 0.7 collective-permute-start.15
  88.2 5.7 %collective-permute-done.15 = bf16[16,8192]{1,0:T(8,128)(2,1)S(1)} collective-permute-done((bf16[16,8192]{1,0:T(8,128)(2,1)S(1)}, bf16[16,8192]{1,0:T(8,128)(2,1)S(1)}, u32[]{:S(2)}, u32[]{:S(2)}) %collective-permute-start.15) | collective-permute-done | bytes 262176 | tf_op jit(solution)/shard_map/ppermute | solution.py:11
  93.9 0.7 copy-done.4
  94.6 0.7 copy-done.5
  95.3 0.3 collective-permute-done.17
  95.6 6.4 %concatenate.21 = bf16[64,8192]{1,0:T(8,128)(2,1)} concatenate(bf16[4,8192]{1,0:T(4,128)(2,1)S(1)} %bitcast.75, bf16[4,8192]{1,0:T(4,128)(2,1)S(1)} %collective-permute-done.12, bf16[4,8192]{1,0:T(4,128)(2,1)S(1)} %collective-permute-done.13, bf16[4,8192]{1,0:T(4,128)(2,1)S(1)} %collective-permute-done.14, bf16[16,8192]{1,0:T(8,128)(2,1)} %copy-done.4, ...), dimensions={0} | concatenate | bytes 2097152 | tf_op jit(solution)/shard_map/concatenate | solution.py:23
  101.9 1.6 %convolution_select_fusion.2 = bf16[64,16]{0,1:T(8,128)(2,1)S(1)} fusion(bf16[64,8192]{1,0:T(8,128)(2,1)} %concatenate.21, bf16[2,8192,64]{1,2,0:T(8,128)(2,1)} %param.20, pred[64]{0:T(512)(128)(4,1)S(1)} %copy-done.15), kind=kOutput, calls=%fused_computation.26 | convolution fusion | flops 16778240 | bytes 1312832 | tf_op jit(solution)/shard_map/dot_general | solution.py:85
  103.6 1.7 %convolution_convert_fusion.4 = bf16[64,16]{0,1:T(8,128)(2,1)S(1)} fusion(bf16[64,16]{0,1:T(8,128)(2,1)S(1)} %convolution_select_fusion.2, bf16[64,8192]{1,0:T(8,128)(2,1)} %concatenate.21, bf16[2,8192,64]{1,2,0:T(8,128)(2,1)} %param.20, s32[64]{0:T(128)S(1)} %copy-done.9, pred[64]{0:T(512)(128)(4,1)S(1)} %copy-done.13), kind=kOutput, calls=%fused_computation.30 | convolution fusion | flops 16914432 | bytes 1315136 | tf_op jit(solution)/shard_map/dot_general | solution.py:80
  105.3 2.1 %collective-permute-start.18 = (bf16[64,16]{0,1:T(8,128)(2,1)S(1)}, bf16[64,16]{0,1:T(8,128)(2,1)S(1)}, u32[]{:S(2)}, u32[]{:S(2)}) collective-permute-start(bf16[64,16]{0,1:T(8,128)(2,1)S(1)} %convolution_convert_fusion.4), channel_id=1, source_target_pairs={{0,4},{1,5},{2,6},{3,7},{4,0},{5,1},{6,2},{7,3},{8,12},{9,13},{10,... | collective-permute-start | bytes 6152 | tf_op jit(solution)/shard_map/ppermute | solution.py:11
  107.4 0.8 collective-permute-start.19
  108.2 1.6 %collective-permute-start.20 = (bf16[64,16]{0,1:T(8,128)(2,1)S(1)}, bf16[64,16]{0,1:T(8,128)(2,1)S(1)}, u32[]{:S(2)}, u32[]{:S(2)}) collective-permute-start(bf16[64,16]{0,1:T(8,128)(2,1)S(1)} %convolution_convert_fusion.4), channel_id=1, source_target_pairs={{0,12},{1,13},{2,14},{3,15},{4,8},{5,9},{6,10},{7,11},{8,4},{9,5},... | collective-permute-start | bytes 6152 | tf_op jit(solution)/shard_map/ppermute | solution.py:11
  109.8 2.1 %collective-permute-done.19 = bf16[64,16]{0,1:T(8,128)(2,1)S(1)} collective-permute-done((bf16[64,16]{0,1:T(8,128)(2,1)S(1)}, bf16[64,16]{0,1:T(8,128)(2,1)S(1)}, u32[]{:S(2)}, u32[]{:S(2)}) %collective-permute-start.19) | collective-permute-done | bytes 2080 | tf_op jit(solution)/shard_map/ppermute | solution.py:11
  111.9 1.7 %collective-permute-done.20 = bf16[64,16]{0,1:T(8,128)(2,1)S(1)} collective-permute-done((bf16[64,16]{0,1:T(8,128)(2,1)S(1)}, bf16[64,16]{0,1:T(8,128)(2,1)S(1)}, u32[]{:S(2)}, u32[]{:S(2)}) %collective-permute-start.20) | collective-permute-done | bytes 2080 | tf_op jit(solution)/shard_map/ppermute | solution.py:11
  113.6 0.3 collective-permute-start.22
  113.9 1.6 %collective-permute-start.23 = (bf16[64,16]{0,1:T(8,128)(2,1)S(1)}, bf16[64,16]{0,1:T(8,128)(2,1)S(1)}, u32[]{:S(2)}, u32[]{:S(2)}) collective-permute-start(bf16[64,16]{0,1:T(8,128)(2,1)S(1)} %add_add_fusion.1), channel_id=1, source_target_pairs={{0,3},{1,2},{2,1},{3,0},{4,7},{5,6},{6,5},{7,4},{8,11},{9,10},{10,... | collective-permute-start | bytes 6152 | tf_op jit(solution)/shard_map/ppermute | solution.py:11
  115.5 1.8 %collective-permute-done.22 = bf16[64,16]{0,1:T(8,128)(2,1)S(1)} collective-permute-done((bf16[64,16]{0,1:T(8,128)(2,1)S(1)}, bf16[64,16]{0,1:T(8,128)(2,1)S(1)}, u32[]{:S(2)}, u32[]{:S(2)}) %collective-permute-start.22) | collective-permute-done | bytes 2080 | tf_op jit(solution)/shard_map/ppermute | solution.py:11
  117.4 1.3 convolution_bitcast_fusion.3
  118.7 5.4 %convolution_convert_fusion = bf16[64,512]{1,0:T(8,128)(2,1)S(1)} fusion(f32[64,512]{1,0:T(8,128)S(1)} %convolution_bitcast_fusion.3, bf16[64,8192]{1,0:T(8,128)(2,1)} %concatenate.21, bf16[8192,512]{1,0:T(8,128)(2,1)} %param.19, s32[64]{0:T(128)S(1)} %copy-done.9), kind=kOutput, calls=%fused_computation.19 | convolution fusion | flops 541167616 | bytes 9634048 | tf_op jit(solution)/shard_map/dot_general | solution.py:80
  124.2 10.5 %all_to_all.38 = bf16[16,4,512]{2,1,0:T(4,128)(2,1)S(1)} all-to-all(bf16[16,4,512]{2,1,0:T(4,128)(2,1)S(1)} %all_to_all.32), channel_id=1, replica_groups=mesh['groups'=2,'tensor'=16] {'tensor'}, dimensions={0} | all-to-all | bytes 131072 | tf_op jit(solution)/shard_map/all_to_all | solution.py:140
  134.7 0.6 copy.43
  (71 shorter events, 1.2 us)
Async XLA Ops:
  0.0 76.2 %copy-start = (bf16[4,8,384,128]{3,2,1,0:T(8,128)(2,1)S(1)}, bf16[4,8,384,128]{3,2,1,0:T(8,128)(2,1)}, u32[]{:S(2)}) copy-start(bf16[4,8,384,128]{3,2,1,0:T(8,128)(2,1)} %param.23) | copy-start | bytes 9437188
  3.7 5.7 %collective-permute-start = (bf16[4,8320]{1,0:T(4,128)(2,1)S(1)}, bf16[4,8320]{1,0:T(4,128)(2,1)S(1)}, u32[]{:S(2)}, u32[]{:S(2)}) collective-permute-start(bf16[4,8320]{1,0:T(4,128)(2,1)S(1)} %pad_maximum_fusion.2), channel_id=1, source_target_pairs={{0,4},{1,5},{2,6},{3,7},{4,0},{5,1},{6,2},{7,3},{8,12},{9,13},{10,... | collective-permute-start | bytes 199688 | tf_op jit(solution)/shard_map/ppermute | solution.py:11
  6.8 7.3 %collective-permute-start.1 = (bf16[4,8320]{1,0:T(4,128)(2,1)S(1)}, bf16[4,8320]{1,0:T(4,128)(2,1)S(1)}, u32[]{:S(2)}, u32[]{:S(2)}) collective-permute-start(bf16[4,8320]{1,0:T(4,128)(2,1)S(1)} %pad_maximum_fusion.2), channel_id=1, source_target_pairs={{0,8},{1,9},{2,10},{3,11},{4,12},{5,13},{6,14},{7,15},{8,0},{9,1},... | collective-permute-start | bytes 199688 | tf_op jit(solution)/shard_map/ppermute | solution.py:11
  9.4 6.2 %collective-permute-start.2 = (bf16[4,8320]{1,0:T(4,128)(2,1)S(1)}, bf16[4,8320]{1,0:T(4,128)(2,1)S(1)}, u32[]{:S(2)}, u32[]{:S(2)}) collective-permute-start(bf16[4,8320]{1,0:T(4,128)(2,1)S(1)} %pad_maximum_fusion.2), channel_id=1, source_target_pairs={{0,12},{1,13},{2,14},{3,15},{4,8},{5,9},{6,10},{7,11},{8,4},{9,5},... | collective-permute-start | bytes 199688 | tf_op jit(solution)/shard_map/ppermute | solution.py:11
  14.1 1.6 %copy-start.2 = (bf16[4,8320]{1,0:T(4,128)(2,1)}, bf16[4,8320]{1,0:T(4,128)(2,1)S(1)}, u32[]{:S(2)}) copy-start(bf16[4,8320]{1,0:T(4,128)(2,1)S(1)} %collective-permute-done.1) | copy-start | bytes 199684
  15.6 1.7 %copy-start.3 = (bf16[4,8320]{1,0:T(4,128)(2,1)}, bf16[4,8320]{1,0:T(4,128)(2,1)S(1)}, u32[]{:S(2)}) copy-start(bf16[4,8320]{1,0:T(4,128)(2,1)S(1)} %collective-permute-done.2) | copy-start | bytes 199684
  15.7 6.6 %collective-permute-start.3 = (bf16[16,8320]{1,0:T(8,128)(2,1)S(1)}, bf16[16,8320]{1,0:T(8,128)(2,1)}, u32[]{:S(2)}, u32[]{:S(2)}) collective-permute-start(bf16[16,8320]{1,0:T(8,128)(2,1)S(1)} %pad_maximum_fusion), channel_id=1, source_target_pairs={{0,2},{1,3},{2,0},{3,1},{4,6},{5,7},{6,4},{7,5},{8,10},{9,11},{10,... | collective-permute-start | bytes 798728 | tf_op jit(solution)/shard_map/ppermute | solution.py:11
  17.9 6.5 %collective-permute-start.4 = (bf16[16,8320]{1,0:T(8,128)(2,1)S(1)}, bf16[16,8320]{1,0:T(8,128)(2,1)}, u32[]{:S(2)}, u32[]{:S(2)}) collective-permute-start(bf16[16,8320]{1,0:T(8,128)(2,1)S(1)} %pad_maximum_fusion), channel_id=1, source_target_pairs={{0,1},{1,0},{2,3},{3,2},{4,5},{5,4},{6,7},{7,6},{8,9},{9,8},{10,11... | collective-permute-start | bytes 798728 | tf_op jit(solution)/shard_map/ppermute | solution.py:11
  22.3 2.1 %collective-permute-start.5 = (bf16[16,8320]{1,0:T(8,128)(2,1)}, bf16[16,8320]{1,0:T(8,128)(2,1)}, u32[]{:S(2)}, u32[]{:S(2)}) collective-permute-start(bf16[16,8320]{1,0:T(8,128)(2,1)} %collective-permute-done.3), channel_id=1, source_target_pairs={{0,1},{1,0},{2,3},{3,2},{4,5},{5,4},{6,7},{7,6},{8,9},{9,8},{10,11... | collective-permute-start | bytes 798728 | tf_op jit(solution)/shard_map/ppermute | solution.py:11
  23.8 29.8 %copy-start.8 = (s32[64]{0:T(128)}, s32[64]{0:T(128)S(1)}, u32[]{:S(2)}) copy-start(s32[64]{0:T(128)S(1)} %add.118) | copy-start | bytes 772
  24.4 12.3 %copy-start.16 = (s32[32]{0:T(128)S(1)}, s32[32]{0:T(128)}, u32[]{:S(2)}) copy-start(s32[32]{0:T(128)} %param.16) | copy-start | bytes 388
  36.8 3.9 %copy-start.12 = (pred[64]{0:T(512)(128)(4,1)}, pred[64]{0:T(512)(128)(4,1)S(1)}, u32[]{:S(2)}) copy-start(pred[64]{0:T(512)(128)(4,1)S(1)} %get-tuple-element.12) | copy-start | bytes 196
  36.8 3.9 %copy-start.14 = (pred[64]{0:T(512)(128)(4,1)}, pred[64]{0:T(512)(128)(4,1)S(1)}, u32[]{:S(2)}) copy-start(pred[64]{0:T(512)(128)(4,1)S(1)} %get-tuple-element.13) | copy-start | bytes 196
  38.7 16.4 %copy-start.11 = (pred[640]{0:T(1024)(128)(4,1)S(1)}, pred[640]{0:T(1024)(128)(4,1)}, u32[]{:S(2)}) copy-start(pred[640]{0:T(1024)(128)(4,1)} %get-tuple-element.17) | copy-start | bytes 1924
  38.7 17.7 %copy-start.10 = (pred[640]{0:T(1024)(128)(4,1)S(1)}, pred[640]{0:T(1024)(128)(4,1)}, u32[]{:S(2)}) copy-start(pred[640]{0:T(1024)(128)(4,1)} %get-tuple-element.16) | copy-start | bytes 1924
  40.7 4.5 %collective-permute-start.6 = (bf16[64,48]{0,1:T(8,128)(2,1)S(1)}, bf16[64,48]{0,1:T(8,128)(2,1)S(1)}, u32[]{:S(2)}, u32[]{:S(2)}) collective-permute-start(bf16[64,48]{0,1:T(8,128)(2,1)S(1)} %convolution_convert_fusion.2), channel_id=1, source_target_pairs={{0,4},{1,5},{2,6},{3,7},{4,0},{5,1},{6,2},{7,3},{8,12},{9,13},{10,... | collective-permute-start | bytes 18440 | tf_op jit(solution)/shard_map/ppermute | solution.py:11
  41.5 4.6 %collective-permute-start.7 = (bf16[64,48]{0,1:T(8,128)(2,1)S(1)}, bf16[64,48]{0,1:T(8,128)(2,1)S(1)}, u32[]{:S(2)}, u32[]{:S(2)}) collective-permute-start(bf16[64,48]{0,1:T(8,128)(2,1)S(1)} %convolution_convert_fusion.2), channel_id=1, source_target_pairs={{0,8},{1,9},{2,10},{3,11},{4,12},{5,13},{6,14},{7,15},{8,0},{9,1},... | collective-permute-start | bytes 18440 | tf_op jit(solution)/shard_map/ppermute | solution.py:11
  43.5 5.5 %collective-permute-start.8 = (bf16[64,48]{0,1:T(8,128)(2,1)S(1)}, bf16[64,48]{0,1:T(8,128)(2,1)S(1)}, u32[]{:S(2)}, u32[]{:S(2)}) collective-permute-start(bf16[64,48]{0,1:T(8,128)(2,1)S(1)} %convolution_convert_fusion.2), channel_id=1, source_target_pairs={{0,12},{1,13},{2,14},{3,15},{4,8},{5,9},{6,10},{7,11},{8,4},{9,5},... | collective-permute-start | bytes 18440 | tf_op jit(solution)/shard_map/ppermute | solution.py:11
  49.0 3.7 %collective-permute-start.10 = (bf16[64,48]{0,1:T(8,128)(2,1)S(1)}, bf16[64,48]{0,1:T(8,128)(2,1)S(1)}, u32[]{:S(2)}, u32[]{:S(2)}) collective-permute-start(bf16[64,48]{0,1:T(8,128)(2,1)S(1)} %add_add_fusion), channel_id=1, source_target_pairs={{0,2},{1,3},{2,0},{3,1},{4,6},{5,7},{6,4},{7,5},{8,10},{9,11},{10,... | collective-permute-start | bytes 18440 | tf_op jit(solution)/shard_map/ppermute | solution.py:11
  50.5 3.1 %collective-permute-start.11 = (bf16[64,48]{0,1:T(8,128)(2,1)S(1)}, bf16[64,48]{0,1:T(8,128)(2,1)S(1)}, u32[]{:S(2)}, u32[]{:S(2)}) collective-permute-start(bf16[64,48]{0,1:T(8,128)(2,1)S(1)} %add_add_fusion), channel_id=1, source_target_pairs={{0,3},{1,2},{2,1},{3,0},{4,7},{5,6},{6,5},{7,4},{8,11},{9,10},{10,... | collective-permute-start | bytes 18440 | tf_op jit(solution)/shard_map/ppermute | solution.py:11
  50.5 3.1 %collective-permute-start.9 = (bf16[64,48]{0,1:T(8,128)(2,1)S(1)}, bf16[64,48]{0,1:T(8,128)(2,1)S(1)}, u32[]{:S(2)}, u32[]{:S(2)}) collective-permute-start(bf16[64,48]{0,1:T(8,128)(2,1)S(1)} %add_add_fusion), channel_id=1, source_target_pairs={{0,1},{1,0},{2,3},{3,2},{4,5},{5,4},{6,7},{7,6},{8,9},{9,8},{10,11... | collective-permute-start | bytes 18440 | tf_op jit(solution)/shard_map/ppermute | solution.py:11
  51.1 5.3 %copy-start.6 = (pred[64,32]{0,1:T(8,128)(4,1)}, pred[64,32]{0,1:T(8,128)(4,1)S(1)}, u32[]{:S(2)}) copy-start(pred[64,32]{0,1:T(8,128)(4,1)S(1)} %iota_compare_fusion.7) | copy-start | bytes 6148
  65.4 10.6 %all-to-all-start = ((bf16[16,4,640]{2,1,0:T(4,128)(2,1)}), bf16[16,4,640]{2,1,0:T(4,128)(2,1)S(1)}, u32[]{:S(2)}, u32[]{:S(2)}) async-start(bf16[16,4,640]{2,1,0:T(4,128)(2,1)} %all_to_all.28), calls=%async_computation | async-start | bytes 163840 | tf_op jit(solution)/shard_map/all_to_all | solution.py:107
  76.2 1.9 %copy-start.1 = (bf16[4,8,384,128]{3,2,1,0:T(8,128)(2,1)S(1)}, bf16[4,8,384,128]{3,2,1,0:T(8,128)(2,1)}, u32[]{:S(2)}) copy-start(bf16[4,8,384,128]{3,2,1,0:T(8,128)(2,1)} %param.24) | copy-start | bytes 9437188
  78.8 23.1 %copy-start.15 = (pred[64]{0:T(512)(128)(4,1)S(1)}, pred[64]{0:T(512)(128)(4,1)}, u32[]{:S(2)}) copy-start(pred[64]{0:T(512)(128)(4,1)} %copy-done.14) | copy-start | bytes 196
  78.9 24.7 %copy-start.9 = (s32[64]{0:T(128)S(1)}, s32[64]{0:T(128)}, u32[]{:S(2)}) copy-start(s32[64]{0:T(128)} %copy-done.8) | copy-start | bytes 772
  78.9 24.7 %copy-start.13 = (pred[64]{0:T(512)(128)(4,1)S(1)}, pred[64]{0:T(512)(128)(4,1)}, u32[]{:S(2)}) copy-start(pred[64]{0:T(512)(128)(4,1)} %copy-done.12) | copy-start | bytes 196
  78.9 4.8 %collective-permute-start.12 = (bf16[4,8192]{1,0:T(4,128)(2,1)S(1)}, bf16[4,8192]{1,0:T(4,128)(2,1)S(1)}, u32[]{:S(2)}, u32[]{:S(2)}) collective-permute-start(bf16[4,8192]{1,0:T(4,128)(2,1)S(1)} %bitcast.71), channel_id=1, source_target_pairs={{0,4},{1,5},{2,6},{3,7},{4,0},{5,1},{6,2},{7,3},{8,12},{9,13},{10,... | collective-permute-start | bytes 196616 | tf_op jit(solution)/shard_map/ppermute | solution.py:11
  79.0 8.3 %collective-permute-start.13 = (bf16[4,8192]{1,0:T(4,128)(2,1)S(1)}, bf16[4,8192]{1,0:T(4,128)(2,1)S(1)}, u32[]{:S(2)}, u32[]{:S(2)}) collective-permute-start(bf16[4,8192]{1,0:T(4,128)(2,1)S(1)} %bitcast.72), channel_id=1, source_target_pairs={{0,8},{1,9},{2,10},{3,11},{4,12},{5,13},{6,14},{7,15},{8,0},{9,1},... | collective-permute-start | bytes 196616 | tf_op jit(solution)/shard_map/ppermute | solution.py:11
  80.1 7.2 %collective-permute-start.14 = (bf16[4,8192]{1,0:T(4,128)(2,1)S(1)}, bf16[4,8192]{1,0:T(4,128)(2,1)S(1)}, u32[]{:S(2)}, u32[]{:S(2)}) collective-permute-start(bf16[4,8192]{1,0:T(4,128)(2,1)S(1)} %bitcast.73), channel_id=1, source_target_pairs={{0,12},{1,13},{2,14},{3,15},{4,8},{5,9},{6,10},{7,11},{8,4},{9,5},... | collective-permute-start | bytes 196616 | tf_op jit(solution)/shard_map/ppermute | solution.py:11
  87.5 30.0 %copy-start.7 = (pred[64,32]{0,1:T(8,128)(4,1)S(1)}, pred[64,32]{0,1:T(8,128)(4,1)}, u32[]{:S(2)}) copy-start(pred[64,32]{0,1:T(8,128)(4,1)} %copy-done.6) | copy-start | bytes 6148
  87.5 6.4 %collective-permute-start.15 = (bf16[16,8192]{1,0:T(8,128)(2,1)S(1)}, bf16[16,8192]{1,0:T(8,128)(2,1)S(1)}, u32[]{:S(2)}, u32[]{:S(2)}) collective-permute-start(bf16[16,8192]{1,0:T(8,128)(2,1)S(1)} %pad_maximum_fusion.1), channel_id=1, source_target_pairs={{0,2},{1,3},{2,0},{3,1},{4,6},{5,7},{6,4},{7,5},{8,10},{9,11},{10,... | collective-permute-start | bytes 786440 | tf_op jit(solution)/shard_map/ppermute | solution.py:11
  88.2 5.7 %collective-permute-start.16 = (bf16[16,8192]{1,0:T(8,128)(2,1)S(1)}, bf16[16,8192]{1,0:T(8,128)(2,1)S(1)}, u32[]{:S(2)}, u32[]{:S(2)}) collective-permute-start(bf16[16,8192]{1,0:T(8,128)(2,1)S(1)} %pad_maximum_fusion.1), channel_id=1, source_target_pairs={{0,1},{1,0},{2,3},{3,2},{4,5},{5,4},{6,7},{7,6},{8,9},{9,8},{10,11... | collective-permute-start | bytes 786440 | tf_op jit(solution)/shard_map/ppermute | solution.py:11
  93.9 0.7 copy-start.4
  93.9 1.7 %collective-permute-start.17 = (bf16[16,8192]{1,0:T(8,128)(2,1)S(1)}, bf16[16,8192]{1,0:T(8,128)(2,1)}, u32[]{:S(2)}, u32[]{:S(2)}) collective-permute-start(bf16[16,8192]{1,0:T(8,128)(2,1)S(1)} %collective-permute-done.15), channel_id=1, source_target_pairs={{0,1},{1,0},{2,3},{3,2},{4,5},{5,4},{6,7},{7,6},{8,9},{9,8},{10,11... | collective-permute-start | bytes 786440 | tf_op jit(solution)/shard_map/ppermute | solution.py:11
  94.6 0.7 copy-start.5
  105.3 4.4 %collective-permute-start.18 = (bf16[64,16]{0,1:T(8,128)(2,1)S(1)}, bf16[64,16]{0,1:T(8,128)(2,1)S(1)}, u32[]{:S(2)}, u32[]{:S(2)}) collective-permute-start(bf16[64,16]{0,1:T(8,128)(2,1)S(1)} %convolution_convert_fusion.4), channel_id=1, source_target_pairs={{0,4},{1,5},{2,6},{3,7},{4,0},{5,1},{6,2},{7,3},{8,12},{9,13},{10,... | collective-permute-start | bytes 6152 | tf_op jit(solution)/shard_map/ppermute | solution.py:11
  107.4 4.5 %collective-permute-start.19 = (bf16[64,16]{0,1:T(8,128)(2,1)S(1)}, bf16[64,16]{0,1:T(8,128)(2,1)S(1)}, u32[]{:S(2)}, u32[]{:S(2)}) collective-permute-start(bf16[64,16]{0,1:T(8,128)(2,1)S(1)} %convolution_convert_fusion.4), channel_id=1, source_target_pairs={{0,8},{1,9},{2,10},{3,11},{4,12},{5,13},{6,14},{7,15},{8,0},{9,1},... | collective-permute-start | bytes 6152 | tf_op jit(solution)/shard_map/ppermute | solution.py:11
  108.2 5.4 %collective-permute-start.20 = (bf16[64,16]{0,1:T(8,128)(2,1)S(1)}, bf16[64,16]{0,1:T(8,128)(2,1)S(1)}, u32[]{:S(2)}, u32[]{:S(2)}) collective-permute-start(bf16[64,16]{0,1:T(8,128)(2,1)S(1)} %convolution_convert_fusion.4), channel_id=1, source_target_pairs={{0,12},{1,13},{2,14},{3,15},{4,8},{5,9},{6,10},{7,11},{8,4},{9,5},... | collective-permute-start | bytes 6152 | tf_op jit(solution)/shard_map/ppermute | solution.py:11
  113.6 1.9 %collective-permute-start.21 = (bf16[64,16]{0,1:T(8,128)(2,1)S(1)}, bf16[64,16]{0,1:T(8,128)(2,1)S(1)}, u32[]{:S(2)}, u32[]{:S(2)}) collective-permute-start(bf16[64,16]{0,1:T(8,128)(2,1)S(1)} %add_add_fusion.1), channel_id=1, source_target_pairs={{0,1},{1,0},{2,3},{3,2},{4,5},{5,4},{6,7},{7,6},{8,9},{9,8},{10,11... | collective-permute-start | bytes 6152 | tf_op jit(solution)/shard_map/ppermute | solution.py:11
  113.6 3.7 %collective-permute-start.22 = (bf16[64,16]{0,1:T(8,128)(2,1)S(1)}, bf16[64,16]{0,1:T(8,128)(2,1)S(1)}, u32[]{:S(2)}, u32[]{:S(2)}) collective-permute-start(bf16[64,16]{0,1:T(8,128)(2,1)S(1)} %add_add_fusion.1), channel_id=1, source_target_pairs={{0,2},{1,3},{2,0},{3,1},{4,6},{5,7},{6,4},{7,5},{8,10},{9,11},{10,... | collective-permute-start | bytes 6152 | tf_op jit(solution)/shard_map/ppermute | solution.py:11
  113.9 3.4 %collective-permute-start.23 = (bf16[64,16]{0,1:T(8,128)(2,1)S(1)}, bf16[64,16]{0,1:T(8,128)(2,1)S(1)}, u32[]{:S(2)}, u32[]{:S(2)}) collective-permute-start(bf16[64,16]{0,1:T(8,128)(2,1)S(1)} %add_add_fusion.1), channel_id=1, source_target_pairs={{0,3},{1,2},{2,1},{3,0},{4,7},{5,6},{6,5},{7,4},{8,11},{9,10},{10,... | collective-permute-start | bytes 6152 | tf_op jit(solution)/shard_map/ppermute | solution.py:11

commit v2 on v1

v2 whole, which is shorter than its diff:
```python
import functools

import jax
import jax.numpy as jnp
from jax import lax
from jax.experimental import pallas as pl
from jax.experimental.pallas import tpu as pltpu
from jax.sharding import PartitionSpec as P

eps = 1e-05
AXIS = "tensor"
LANES = 128
VMEM = pltpu.VMEM
SMEM = pltpu.SMEM


def swap(x, count, offset):
    return lax.ppermute(x, AXIS, [(i, i ^ offset) for i in range(count)])


def gather_rows(x, count):
    step = count // 4
    held = [jnp.concatenate([x] + [swap(x, count, k * step) for k in (1, 2, 3)], axis=0)]
    step //= 2
    while step:
        held = held + [swap(h, count, step) for h in held]
        step //= 2
    return held


def place_of(row, me, count, rows):
    block = row // rows
    source = (block % 4) * (count // 4)
    piece, step = block // 4, count // 8
    while step:
        source = source + (piece % 2) * step
        piece, step = piece // 2, step // 2
    return (source ^ me) * rows + row % rows


def limit(total):
    return (16 if total <= 64 else 60) * 1024 * 1024


def spec(space=VMEM):
    return pl.BlockSpec(memory_space=space)


def norm_kernel(hidden_ref, gain_ref, ids_ref, out_ref):
    rows, width = hidden_ref.shape
    hidden = hidden_ref[...].astype(jnp.float32)
    power = jnp.sum(hidden * hidden, axis=1, keepdims=True) / width
    gain = gain_ref[...].astype(jnp.float32)
    out_ref[:, :width] = (hidden * lax.rsqrt(power + eps) * gain).astype(jnp.bfloat16)
    row = lax.broadcasted_iota(jnp.int32, (rows, LANES), 0)
    ids = jnp.zeros((rows, LANES), jnp.float32)
    for r in range(rows):
        ids = jnp.where(row == r, ids_ref[r].astype(jnp.float32), ids)
    out_ref[:, width:] = ids.astype(jnp.bfloat16)


def down_kernel(count, rows, pieces, first, *refs):
    storage_ref, me_ref, down_ref = refs[:3]
    piece_refs, refs = refs[3 : 3 + pieces], refs[3 + pieces :]
    if first:
        out_ref, ids_out_ref = refs
    else:
        ids_ref, out_ref = refs
    total = count * rows
    held, rank, width = down_ref.shape
    me = me_ref[0]
    adapters = storage_ref.shape[0]
    if first:
        ids = jnp.concatenate([p[:, width:] for p in piece_refs], axis=0).astype(jnp.float32)
        ids_out_ref[...] = ids
    else:
        ids = ids_ref[...]
    chunk = 1024
    sums = [jnp.zeros((total, rank), jnp.float32) for _ in range(held)]
    for k in range(0, width, chunk):
        x = jnp.concatenate([p[:, k : k + chunk] for p in piece_refs], axis=0)
        for s in range(held):
            sums[s] = sums[s] + lax.dot_general(
                x,
                down_ref[s, :, k : k + chunk],
                (((1,), (1,)), ((), ())),
                preferred_element_type=jnp.float32,
            )
    chosen = jnp.zeros((total, rank), jnp.float32)
    for s in range(held):
        name = lax.fori_loop(
            0,
            adapters,
            lambda a, found, s=s: jnp.where(storage_ref[a] == me * held + s, a, found),
            jnp.int32(0),
        )
        chosen = jnp.where(ids[:, :rank] == name.astype(jnp.float32), sums[s], chosen)
    lane = lax.broadcasted_iota(jnp.int32, (total, total), 1)
    sub = lax.broadcasted_iota(jnp.int32, (total, total), 0)
    order = jnp.where(place_of(lane, me, count, rows) == sub, 1.0, 0.0).astype(jnp.bfloat16)
    out_ref[...] = jnp.dot(
        order, chosen.astype(jnp.bfloat16), preferred_element_type=jnp.float32
    ).astype(jnp.bfloat16)


def base_kernel(pieces, *refs):
    weight_ref, out_ref = refs[pieces], refs[pieces + 1]
    x = jnp.concatenate([p[...] for p in refs[:pieces]], axis=0)
    term = jnp.dot(x, weight_ref[...], preferred_element_type=jnp.float32)

    @pl.when(pl.program_id(0) == 0)
    def _():
        out_ref[...] = term

    @pl.when(pl.program_id(0) > 0)
    def _():
        out_ref[...] += term


def lift_kernel(count, rows, parts, bounds, *refs):
    me_ref, down_ref, ids_ref, up_ref = refs[:4]
    base_refs, out_ref = refs[4 : 4 + parts], refs[4 + parts]
    total = count * rows
    me = me_ref[0]
    adapters, rank, columns = up_ref.shape
    wide = adapters * rank
    value = base_refs[0][...]
    for b in base_refs[1:]:
        value = value + b[...]
    lane = lax.broadcasted_iota(jnp.int32, (total, total), 1)
    sub = lax.broadcasted_iota(jnp.int32, (total, total), 0)
    back = jnp.where(place_of(sub, me, count, rows) == lane, 1.0, 0.0).astype(jnp.bfloat16)
    order = jnp.where(place_of(lane, me, count, rows) == sub, 1.0, 0.0).astype(jnp.bfloat16)
    down = jnp.dot(back, down_ref[...], preferred_element_type=jnp.float32).astype(jnp.bfloat16)
    groups = down.shape[1] // rank
    up = up_ref[...].reshape(wide, columns)
    spread_at = lax.broadcasted_iota(jnp.int32, (groups * rank, wide), 1)
    spread_from = lax.broadcasted_iota(jnp.int32, (groups * rank, wide), 0)
    own = lax.broadcasted_iota(jnp.int32, (total, wide), 1) // rank
    named = own.astype(jnp.float32) == ids_ref[:, :1]
    column = lax.broadcasted_iota(jnp.int32, (total, columns), 1) + me * columns
    for g in range(groups):
        spread = jnp.where(spread_at % rank + g * rank == spread_from, 1.0, 0.0).astype(
            jnp.bfloat16
        )
        copies = jnp.dot(down, spread, preferred_element_type=jnp.float32)
        chosen = jnp.where(named, copies, 0.0).astype(jnp.bfloat16)
        lifted = jnp.dot(chosen, up, preferred_element_type=jnp.float32)
        low, high = bounds[g], bounds[g + 1]
        value = value + jnp.where((column >= low) & (column < high), lifted, 0.0)
    placed = jnp.dot(
        order, value.astype(jnp.bfloat16), preferred_element_type=jnp.float32
    ).astype(jnp.bfloat16)
    for d in range(count):
        out_ref[d] = placed[d * rows : (d + 1) * rows]


def local(
    input_hidden,
    input_norm_gain,
    request_adapter,
    adapter_storage,
    lengths,
    projection_weight,
    output_weight,
    adapter_down,
    projection_up_adapter,
    output_up_adapter,
    cache_keys,
    cache_values,
    *,
    count,
):
    me = lax.axis_index(AXIS).astype(jnp.int32).reshape(1)
    rows, width = input_hidden.shape
    rank = projection_up_adapter.shape[1]
    held = adapter_down.shape[0]
    kv_heads, context, head_dim = cache_keys.shape[1:]
    kv_width = kv_heads * head_dim
    total = rows * count
    params = pltpu.CompilerParams(vmem_limit_bytes=limit(total))
    down_maps = jnp.swapaxes(adapter_down, 1, 2)

    normed = pl.pallas_call(
        norm_kernel,
        out_shape=jax.ShapeDtypeStruct((rows, width + LANES), jnp.bfloat16),
        in_specs=[spec(), spec(), spec(SMEM)],
        out_specs=spec(),
        compiler_params=params,
        name="norm",
    )(input_hidden, input_norm_gain.reshape(1, width), request_adapter.reshape(rows))

    def downs(pieces, low, high, ids):
        ranks = high - low
        first = ids is None
        down_spec = pl.BlockSpec((held, ranks, width), lambda i: (0, low // ranks, 0))
        shapes = [jax.ShapeDtypeStruct((total, ranks), jnp.bfloat16)]
        if first:
            shapes.append(jax.ShapeDtypeStruct((total, LANES), jnp.float32))
        return pl.pallas_call(
            functools.partial(down_kernel, count, rows, len(pieces), first),
            grid=(1,),
            out_shape=shapes,
            in_specs=[spec(SMEM), spec(SMEM), down_spec]
            + [spec()] * (len(pieces) + (0 if first else 1)),
            out_specs=[spec()] * len(shapes),
            compiler_params=params,
            cost_estimate=pl.CostEstimate(
                flops=2 * total * width * held * ranks,
                bytes_accessed=2 * width * (held * ranks + total),
                transcendentals=0,
            ),
            name="down",
        )(adapter_storage, me, down_maps, *pieces, *([] if first else [ids]))

    def base(pieces, weight, part, parts):
        columns = weight.shape[1]
        chunk = 1024
        steps = width // chunk // parts
        piece_rows = pieces[0].shape[0]
        return pl.pallas_call(
            functools.partial(base_kernel, len(pieces)),
            grid=(steps,),
            out_shape=jax.ShapeDtypeStruct((total, columns), jnp.float32),
            in_specs=[pl.BlockSpec((piece_rows, chunk), lambda i: (0, part * steps + i))]
            * len(pieces)
            + [pl.BlockSpec((chunk, columns), lambda i: (part * steps + i, 0))],
            out_specs=pl.BlockSpec((total, columns), lambda i: (0, 0)),
            compiler_params=params,
            cost_estimate=pl.CostEstimate(
                flops=2 * total * width * columns // parts,
                bytes_accessed=2 * width * columns // parts,
                transcendentals=0,
            ),
            name="base",
        )(*pieces, weight)

    def lift(down, ids, up, bases, bounds):
        columns = up.shape[2]
        return pl.pallas_call(
            functools.partial(lift_kernel, count, rows, len(bases), bounds),
            out_shape=jax.ShapeDtypeStruct((count, rows, columns), jnp.bfloat16),
            in_specs=[spec(SMEM)] + [spec()] * (3 + len(bases)),
            out_specs=spec(),
            compiler_params=params,
            name="lift",
        )(me, down, ids, up, *bases)

    def project(pieces, ids, low, high, weight, up, bounds):
        down = downs(pieces, low, high, ids)
        if ids is None:
            down, ids = down
        else:
            (down,) = down
        parts, step, bases = 4, count, []
        part = 0
        while step > 1:
            step //= 2
            other = swap(down, count, step)
            if part < parts:
                bases.append(base(pieces, weight, part, parts))
                part += 1
            down = down + other
        columns = lift(down, ids, up, bases, bounds)
        mine = lax.all_to_all(columns, AXIS, split_axis=0, concat_axis=0, tiled=True)
        return jnp.swapaxes(mine, 0, 1).reshape(rows, -1), ids

    bounds = (0, width, width + kv_width, width + 2 * kv_width)
    qkv_mine, ids = project(
        gather_rows(normed, count),
        None,
        0,
        3 * rank,
        projection_weight,
        projection_up_adapter,
        bounds,
    )

    groups_per = width // head_dim // kv_heads
    query = qkv_mine[:, 0:width].reshape(rows, kv_heads, groups_per, head_dim)
    key_new = qkv_mine[:, width : width + kv_width].reshape(rows, kv_heads, head_dim)
    value_new = qkv_mine[:, width + kv_width :].reshape(rows, kv_heads, head_dim)
    scale = head_dim ** (-0.5)
    scores = (
        jnp.einsum("bhgd,bhpd->bhgp", query, cache_keys, preferred_element_type=jnp.float32) * scale
    )
    live = jnp.arange(context, dtype=jnp.int32)[None, :] < lengths[:, None]
    scores = jnp.where(live[:, None, None, :], scores, -1e30)
    own = jnp.einsum("bhgd,bhd->bhg", query, key_new, preferred_element_type=jnp.float32) * scale
    peak = jnp.maximum(jnp.max(scores, axis=3), own)
    weights = jnp.exp(scores - peak[..., None])
    own_weight = jnp.exp(own - peak)
    denominator = jnp.sum(weights, axis=3) + own_weight
    probs = (weights / denominator[..., None]).astype(jnp.bfloat16)
    own_prob = (own_weight / denominator).astype(jnp.bfloat16)
    mixed = jnp.einsum("bhgp,bhpd->bhgd", probs, cache_values, preferred_element_type=jnp.float32)
    mixed = (
        mixed
        + own_prob.astype(jnp.float32)[..., None] * value_new.astype(jnp.float32)[:, :, None, :]
    )
    attended = mixed.reshape(rows, width).astype(jnp.bfloat16)

    output, _ = project(
        gather_rows(attended, count),
        ids,
        3 * rank,
        4 * rank,
        output_weight,
        output_up_adapter,
        (0, width),
    )
    return output


def solution(mesh):
    count = mesh.shape[AXIS]

    def body(*arrays):
        return local(*arrays, count=count)

    return jax.shard_map(
        body,
        mesh=mesh,
        in_specs=(
            P(("groups", "tensor"), None),
            P(),
            P(("groups", "tensor"), None),
            P(),
            P(("groups", "tensor")),
            P(None, "tensor"),
            P(None, "tensor"),
            P("tensor", None, None),
            P(None, None, "tensor"),
            P(None, None, "tensor"),
            P(("groups", "tensor"), None, None, None),
            P(("groups", "tensor"), None, None, None),
        ),
        out_specs=P(("groups", "tensor"), None),
        check_vma=False,
    )
```

time: 137 us -> 107 us (0.78)
  matrix products: 27.3 us -> 2.11 us
  Pallas kernels: 0 us -> 16.7 us
  local copies, waits for them, and re-layouts: 21.9 us -> 13 us
  other arithmetic: 7.83 us -> 0.72 us
  starting transfers between devices: 28.8 us -> 24.3 us
    dot_general x12 -> x0, matrix products: 25.1 us -> none  [the longest x6 15.7 us: move(): jnp.dot(matrix, x, preferred_element_type=jnp.float32).astype(jnp.bfloat16)]
    concatenate x2 -> x0, local copies, waits for them, and re-layouts: 17.8 us -> none  [gather_rows(): return (jnp.concatenate(held, axis=0), sum(order, []))]
    pallas_call x0 -> x13, Pallas kernels: none -> 16.7 us  [the longest x8 9.12 us: base(): pl.pallas_call(functools.partial(base_kernel, len(pieces)), grid=(steps,)...]
    unnamed x38 -> x30, local copies, waits for them, and re-layouts: 2.51 us -> 12.1 us
    ppermute x24 -> x20, starting transfers between devices: 25.3 us -> 20.8 us  [swap(): return lax.ppermute(x, AXIS, [(i, i ^ offset) for i in range(count)])]
    convert_element_type x2 -> x0, other arithmetic: 1.81 us -> none  [the longest x1 0.94 us: local(): (hidden32 * lax.rsqrt(power + eps) * input_norm_gain.astype(jnp.float32))...]
    ppermute x24 -> x20, waiting for transfers between devices: 32.3 us -> 30.9 us  [swap(): return lax.ppermute(x, AXIS, [(i, i ^ offset) for i in range(count)])]
    eq x5 -> x0, other arithmetic: 1.45 us -> none  [the longest x2 0.83 us: local(): named = ids[:, None] == jnp.arange(adapters, dtype=jnp.int32)[None, :]]
  transfers between devices with their start and end apart: 25 -> 21, of which waited for: 15 -> 14; matrix products, arithmetic and copies ran while one was open for 3% -> 0% of each run, Pallas kernels for 0% -> 9%
where the time goes in v2:
time: 107 us; the launch traced here: 106 us
  waiting for transfers between devices  37.9 us (35%)
  starting transfers between devices  24.3 us (23%)
  Pallas kernels  16.7 us (16%)
  local copies, waits for them, and re-layouts  13 us (12%)
  blocking collectives  10.9 us (10%)
  matrix products  2.11 us (2%)
    ppermute x20, waiting for transfers between devices, swap(): return lax.ppermute(x, AXIS, [(i, i ^ offset) for i in range(count)])  30.9 us
    ppermute x20, starting transfers between devices, swap(): return lax.ppermute(x, AXIS, [(i, i ^ offset) for i in range(count)])  20.8 us
    unnamed x30, local copies, waits for them, and re-layouts  12.1 us
    all_to_all x1, blocking collectives, project(): lax.all_to_all(columns, AXIS, split_axis=0, concat_axis=0, tiled=True)  10.9 us
    pallas_call x8, Pallas kernels, base(): pl.pallas_call(functools.partial(base_kernel, len(pieces)), grid=(steps,)...  9.12 us
    all_to_all x1, waiting for transfers between devices, project(): lax.all_to_all(columns, AXIS, split_axis=0, concat_axis=0, tiled=True)  7.02 us
    pallas_call x2, Pallas kernels, downs(): pl.pallas_call(functools.partial(down_kernel, count, rows, len(pieces), f...  4.58 us
    all_to_all x1, starting transfers between devices, project(): lax.all_to_all(columns, AXIS, split_axis=0, concat_axis=0, tiled=True)  3.5 us
  transfers between devices with their start and end apart: 21, of which 14 were waited for; matrix products, arithmetic and copies ran while one was open for 0% of the time, Pallas kernels for 9%

profile of v2, /device:TPU:0, one launch (start us, length us, event | category | flops | bytes accessed | tf_op | source)
XLA Modules:
  0.0 105.9 jit_solution(3376077096599915360)
XLA Ops:
  0.0 0.9 reshape.52.gain_ref
  0.9 0.0 copy-start.7
  0.9 0.9 copy-done.7
  1.8 0.7 copy-done.10
  2.5 0.7 norm.1
  3.2 3.1 %collective-permute-start = (bf16[4,8320]{1,0:T(4,128)(2,1)S(1)}, bf16[4,8320]{1,0:T(4,128)(2,1)S(1)}, u32[]{:S(2)}, u32[]{:S(2)}) collective-permute-start(bf16[4,8320]{1,0:T(4,128)(2,1)S(1)} %norm.1), channel_id=1, source_target_pairs={{0,4},{1,5},{2,6},{3,7},{4,0},{5,1},{6,2},{7,3},{8,12},{9,13},{10,... | collective-permute-start | bytes 199688 | tf_op jit(solution)/shard_map/ppermute | solution.py:18
  6.3 2.6 %collective-permute-start.1 = (bf16[4,8320]{1,0:T(4,128)(2,1)S(1)}, bf16[4,8320]{1,0:T(4,128)(2,1)S(1)}, u32[]{:S(2)}, u32[]{:S(2)}) collective-permute-start(bf16[4,8320]{1,0:T(4,128)(2,1)S(1)} %norm.1), channel_id=1, source_target_pairs={{0,8},{1,9},{2,10},{3,11},{4,12},{5,13},{6,14},{7,15},{8,0},{9,1},... | collective-permute-start | bytes 199688 | tf_op jit(solution)/shard_map/ppermute | solution.py:18
  8.9 4.7 %collective-permute-done.1 = bf16[4,8320]{1,0:T(4,128)(2,1)S(1)} collective-permute-done((bf16[4,8320]{1,0:T(4,128)(2,1)S(1)}, bf16[4,8320]{1,0:T(4,128)(2,1)S(1)}, u32[]{:S(2)}, u32[]{:S(2)}) %collective-permute-start.1) | collective-permute-done | bytes 66592 | tf_op jit(solution)/shard_map/ppermute | solution.py:18
  13.6 1.4 %collective-permute-done.2 = bf16[4,8320]{1,0:T(4,128)(2,1)S(1)} collective-permute-done((bf16[4,8320]{1,0:T(4,128)(2,1)S(1)}, bf16[4,8320]{1,0:T(4,128)(2,1)S(1)}, u32[]{:S(2)}, u32[]{:S(2)}) %collective-permute-start.2) | collective-permute-done | bytes 66592 | tf_op jit(solution)/shard_map/ppermute | solution.py:18
  15.0 0.2 pad_maximum_fusion.refs_3_.refs_0_
  15.2 1.6 %collective-permute-start.3 = (bf16[16,8320]{1,0:T(8,128)(2,1)S(1)}, bf16[16,8320]{1,0:T(8,128)(2,1)}, u32[]{:S(2)}, u32[]{:S(2)}) collective-permute-start(bf16[16,8320]{1,0:T(8,128)(2,1)S(1)} %pad_maximum_fusion.refs_3_.refs_0_), channel_id=1, source_target_pairs={{0,2},{1,3},{2,0},{3,1},{4,6},{5,7},{6,4},{7,5},{8,10},{9,11},{10,... | collective-permute-start | bytes 798728 | tf_op jit(solution)/shard_map/ppermute | solution.py:18
  16.8 5.0 %collective-permute-done.3.refs_4_.refs_1_ = bf16[16,8320]{1,0:T(8,128)(2,1)} collective-permute-done((bf16[16,8320]{1,0:T(8,128)(2,1)S(1)}, bf16[16,8320]{1,0:T(8,128)(2,1)}, u32[]{:S(2)}, u32[]{:S(2)}) %collective-permute-start.3) | collective-permute-done | bytes 266272 | tf_op jit(solution)/shard_map/ppermute | solution.py:18
  21.8 1.9 %collective-permute-done.5.refs_6_.refs_3_ = bf16[16,8320]{1,0:T(8,128)(2,1)} collective-permute-done((bf16[16,8320]{1,0:T(8,128)(2,1)}, bf16[16,8320]{1,0:T(8,128)(2,1)}, u32[]{:S(2)}, u32[]{:S(2)}) %collective-permute-start.5) | collective-permute-done | bytes 266272 | tf_op jit(solution)/shard_map/ppermute | solution.py:18
  23.7 1.6 %copy-done.3 = bf16[2,8192,64]{1,2,0:T(8,128)(2,1)S(1)} copy-done((bf16[2,8192,64]{1,2,0:T(8,128)(2,1)S(1)}, bf16[2,8192,64]{1,2,0:T(8,128)(2,1)}, u32[]{:S(2)}) %copy-start.3) | copy-done | bytes 2097176
  25.3 0.7 copy-done.8
  25.9 2.5 %down.2 = (bf16[64,48]{1,0:T(8,128)(2,1)S(1)}, f32[64,128]{1,0:T(8,128)S(1)}) custom-call(s32[32]{0:T(128)S(1)} %copy-done.8, s32[1]{0:T(128)} %bitcast.refs_1_.refs_0_, bf16[2,64,8192]{2,1,0:T(8,128)(2,1)S(1)} %bitcast.35, bf16[16,8320]{1,0:T(8,128)(2,1)S(1)} %pad_maximum_fusion.refs_3_.refs_0_, bf16[16,8320]{1,0:T(8,128)(2,1)} %collective-permute-done.3.refs_4_.refs_1_, ...), custom_call_target="tpu_custom_call" | custom-call | flops 100663296 | bytes 2621440 | tf_op jit(solution)/shard_map/down/pallas_call | solution.py:200
  28.5 2.1 %collective-permute-start.6 = (bf16[64,48]{1,0:T(8,128)(2,1)S(1)}, bf16[64,48]{1,0:T(8,128)(2,1)S(1)}, u32[]{:S(2)}, u32[]{:S(2)}) collective-permute-start(bf16[64,48]{1,0:T(8,128)(2,1)S(1)} %get-tuple-element.7), channel_id=1, source_target_pairs={{0,8},{1,9},{2,10},{3,11},{4,12},{5,13},{6,14},{7,15},{8,0},{9,1},... | collective-permute-start | bytes 18440 | tf_op jit(solution)/shard_map/ppermute | solution.py:18
  30.6 4.0 %copy-done.1 = bf16[8192,640]{1,0:T(8,128)(2,1)S(1)} copy-done((bf16[8192,640]{1,0:T(8,128)(2,1)S(1)}, bf16[8192,640]{1,0:T(8,128)(2,1)}, u32[]{:S(2)}) %copy-start.1) | copy-done | bytes 10485784
  34.5 1.6 %base.11.refs_7_ = f32[64,640]{1,0:T(8,128)S(1)} custom-call(bf16[16,8320]{1,0:T(8,128)(2,1)S(1)} %pad_maximum_fusion.refs_3_.refs_0_, bf16[16,8320]{1,0:T(8,128)(2,1)} %collective-permute-done.3.refs_4_.refs_1_, bf16[16,8320]{1,0:T(8,128)(2,1)} %collective-permute-done.4.refs_5_.refs_2_, bf16[16,8320]{1,0:T(8,128)(2,1)} %collective-permute-done.5.refs_6_.refs_3_, ...), custom_call_target="tpu_custom_call" | custom-call | flops 167772160 | bytes 2621440 | tf_op jit(solution)/shard_map/base/pallas_call | solution.py:221
  36.1 0.3 collective-permute-start.7
  36.4 1.6 %base.10.refs_6_ = f32[64,640]{1,0:T(8,128)S(1)} custom-call(bf16[16,8320]{1,0:T(8,128)(2,1)S(1)} %pad_maximum_fusion.refs_3_.refs_0_, bf16[16,8320]{1,0:T(8,128)(2,1)} %collective-permute-done.3.refs_4_.refs_1_, bf16[16,8320]{1,0:T(8,128)(2,1)} %collective-permute-done.4.refs_5_.refs_2_, bf16[16,8320]{1,0:T(8,128)(2,1)} %collective-permute-done.5.refs_6_.refs_3_, ...), custom_call_target="tpu_custom_call" | custom-call | flops 167772160 | bytes 2621440 | tf_op jit(solution)/shard_map/base/pallas_call | solution.py:221
  38.0 1.9 %collective-permute-done.7 = bf16[64,48]{1,0:T(8,128)(2,1)S(1)} collective-permute-done((bf16[64,48]{1,0:T(8,128)(2,1)S(1)}, bf16[64,48]{1,0:T(8,128)(2,1)S(1)}, u32[]{:S(2)}, u32[]{:S(2)}) %collective-permute-start.7) | collective-permute-done | bytes 6176 | tf_op jit(solution)/shard_map/ppermute | solution.py:18
  40.0 1.6 %collective-permute-start.8 = (bf16[64,48]{1,0:T(8,128)(2,1)S(1)}, bf16[64,48]{1,0:T(8,128)(2,1)S(1)}, u32[]{:S(2)}, u32[]{:S(2)}) collective-permute-start(bf16[64,48]{1,0:T(8,128)(2,1)S(1)} %add.31), channel_id=1, source_target_pairs={{0,2},{1,3},{2,0},{3,1},{4,6},{5,7},{6,4},{7,5},{8,10},{9,11},{10,... | collective-permute-start | bytes 18440 | tf_op jit(solution)/shard_map/ppermute | solution.py:18
  41.5 1.6 %base.9.refs_5_ = f32[64,640]{1,0:T(8,128)S(1)} custom-call(bf16[16,8320]{1,0:T(8,128)(2,1)S(1)} %pad_maximum_fusion.refs_3_.refs_0_, bf16[16,8320]{1,0:T(8,128)(2,1)} %collective-permute-done.3.refs_4_.refs_1_, bf16[16,8320]{1,0:T(8,128)(2,1)} %collective-permute-done.4.refs_5_.refs_2_, bf16[16,8320]{1,0:T(8,128)(2,1)} %collective-permute-done.5.refs_6_.refs_3_, ...), custom_call_target="tpu_custom_call" | custom-call | flops 167772160 | bytes 2621440 | tf_op jit(solution)/shard_map/base/pallas_call | solution.py:221
  43.1 0.7 collective-permute-done.8
  43.8 0.1 collective-permute-start.9
  43.9 1.7 %base.8.refs_4_ = f32[64,640]{1,0:T(8,128)S(1)} custom-call(bf16[16,8320]{1,0:T(8,128)(2,1)S(1)} %pad_maximum_fusion.refs_3_.refs_0_, bf16[16,8320]{1,0:T(8,128)(2,1)} %collective-permute-done.3.refs_4_.refs_1_, bf16[16,8320]{1,0:T(8,128)(2,1)} %collective-permute-done.4.refs_5_.refs_2_, bf16[16,8320]{1,0:T(8,128)(2,1)} %collective-permute-done.5.refs_6_.refs_3_, ...), custom_call_target="tpu_custom_call" | custom-call | flops 167772160 | bytes 2621440 | tf_op jit(solution)/shard_map/base/pallas_call | solution.py:221
  45.6 1.7 %lift.2 = bf16[16,4,640]{2,1,0:T(4,128)(2,1)} custom-call(s32[1]{0:T(128)} %bitcast.refs_1_.refs_0_, bf16[64,48]{1,0:T(8,128)(2,1)S(1)} %add.33.refs_1_, f32[64,128]{1,0:T(8,128)S(1)} %get-tuple-element.8.refs_2_.refs_7_, bf16[32,16,640]{2,1,0:T(8,128)(2,1)S(1)} %copy-done.5, f32[64,640]{1,0:T(8,128)S(1)} %base.8.refs_4_, f32[64,640]{1,0:T(8,128)S(1)} %base.9.refs_5_, ...), custom_call_target="tpu_custom_call" | custom-call | tf_op jit(solution)/shard_map/lift/pallas_call | solution.py:240
  47.3 3.5 %all-to-all-start = ((bf16[16,4,640]{2,1,0:T(4,128)(2,1)}), bf16[16,4,640]{2,1,0:T(4,128)(2,1)S(1)}, u32[]{:S(2)}, u32[]{:S(2)}) async-start(bf16[16,4,640]{2,1,0:T(4,128)(2,1)} %lift.2), calls=%async_computation | async-start | bytes 163840 | tf_op jit(solution)/shard_map/all_to_all | solution.py:265
  50.8 0.1 iota_compare_fusion
  50.9 7.0 %all-to-all-done = bf16[16,4,640]{2,1,0:T(4,128)(2,1)S(1)} async-done(((bf16[16,4,640]{2,1,0:T(4,128)(2,1)}), bf16[16,4,640]{2,1,0:T(4,128)(2,1)S(1)}, u32[]{:S(2)}, u32[]{:S(2)}) %all-to-all-start) | async-done | bytes 81952 | tf_op jit(solution)/shard_map/all_to_all | solution.py:265
  57.9 0.0 copy-start.11
  58.0 0.1 fusion.6
  58.1 1.3 %fusion.13 = (f32[4,8,8]{2,1,0:T(8,128)S(1)}, f32[4,8,8,384]{3,2,1,0:T(8,128)S(1)}) fusion(bf16[4,8,384,128]{3,2,1,0:T(8,128)(2,1)S(1)} %copy-done, bf16[1,4,64,128]{3,1,2,0:T(4,128)(2,1)S(1)} %slice_bitcast_fusion, pred[4,384]{1,0:T(4,128)(4,1)S(1)} %iota_compare_fusion), kind=kOutput, calls=%fused_computation.27 | convolution fusion | flops 25460480 | bytes 3607040 | tf_op jit(solution)/shard_map/bhgd,bhpd->bhgp/dot_general | solution.py:285
  59.4 0.2 fusion.3
  59.7 0.2 copy-done.11
  59.8 0.7 fusion.2
  60.5 0.1 copy.30
  60.6 0.1 collective-permute-start.10
  60.7 1.1 %collective-permute-start.11 = (bf16[4,8192]{1,0:T(4,128)(2,1)S(1)}, bf16[4,8192]{1,0:T(4,128)(2,1)S(1)}, u32[]{:S(2)}, u32[]{:S(2)}) collective-permute-start(bf16[4,8192]{1,0:T(4,128)(2,1)S(1)} %bitcast.42), channel_id=1, source_target_pairs={{0,8},{1,9},{2,10},{3,11},{4,12},{5,13},{6,14},{7,15},{8,0},{9,1},... | collective-permute-start | bytes 196616 | tf_op jit(solution)/shard_map/ppermute | solution.py:18
  61.8 3.3 %collective-permute-start.12 = (bf16[4,8192]{1,0:T(4,128)(2,1)S(1)}, bf16[4,8192]{1,0:T(4,128)(2,1)S(1)}, u32[]{:S(2)}, u32[]{:S(2)}) collective-permute-start(bf16[4,8192]{1,0:T(4,128)(2,1)S(1)} %bitcast.43), channel_id=1, source_target_pairs={{0,12},{1,13},{2,14},{3,15},{4,8},{5,9},{6,10},{7,11},{8,4},{9,5},... | collective-permute-start | bytes 196616 | tf_op jit(solution)/shard_map/ppermute | solution.py:18
  65.1 0.4 collective-permute-done.10
  65.5 3.5 %collective-permute-done.11 = bf16[4,8192]{1,0:T(4,128)(2,1)S(1)} collective-permute-done((bf16[4,8192]{1,0:T(4,128)(2,1)S(1)}, bf16[4,8192]{1,0:T(4,128)(2,1)S(1)}, u32[]{:S(2)}, u32[]{:S(2)}) %collective-permute-start.11) | collective-permute-done | bytes 65568 | tf_op jit(solution)/shard_map/ppermute | solution.py:18
  69.0 0.2 pad_maximum_fusion.1.refs_3_.refs_0_
  69.1 0.7 collective-permute-start.13
  69.9 5.7 %collective-permute-done.13.refs_4_.refs_1_ = bf16[16,8192]{1,0:T(8,128)(2,1)S(1)} collective-permute-done((bf16[16,8192]{1,0:T(8,128)(2,1)S(1)}, bf16[16,8192]{1,0:T(8,128)(2,1)S(1)}, u32[]{:S(2)}, u32[]{:S(2)}) %collective-permute-start.13) | collective-permute-done | bytes 262176 | tf_op jit(solution)/shard_map/ppermute | solution.py:18
  75.6 1.5 %collective-permute-done.15.refs_6_.refs_3_ = bf16[16,8192]{1,0:T(8,128)(2,1)S(1)} collective-permute-done((bf16[16,8192]{1,0:T(8,128)(2,1)S(1)}, bf16[16,8192]{1,0:T(8,128)(2,1)S(1)}, u32[]{:S(2)}, u32[]{:S(2)}) %collective-permute-start.15) | collective-permute-done | bytes 262176 | tf_op jit(solution)/shard_map/ppermute | solution.py:18
  77.1 2.0 %down.3 = bf16[64,16]{1,0:T(8,128)(2,1)S(1)} custom-call(s32[32]{0:T(128)S(1)} %copy-done.9, s32[1]{0:T(128)} %bitcast.refs_1_.refs_0_, bf16[2,64,8192]{2,1,0:T(8,128)(2,1)S(1)} %bitcast.36, bf16[16,8192]{1,0:T(8,128)(2,1)S(1)} %pad_maximum_fusion.1.refs_3_.refs_0_, bf16[16,8192]{1,0:T(8,128)(2,1)S(1)} %collective-permute-done.13.refs_4_.refs_1_, ...), custom_call_target="tpu_custom_call" | custom-call | flops 33554432 | bytes 1572864 | tf_op jit(solution)/shard_map/down/pallas_call | solution.py:200
  79.1 1.6 %collective-permute-start.16 = (bf16[64,16]{1,0:T(8,128)(2,1)S(1)}, bf16[64,16]{1,0:T(8,128)(2,1)S(1)}, u32[]{:S(2)}, u32[]{:S(2)}) collective-permute-start(bf16[64,16]{1,0:T(8,128)(2,1)S(1)} %down.3), channel_id=1, source_target_pairs={{0,8},{1,9},{2,10},{3,11},{4,12},{5,13},{6,14},{7,15},{8,0},{9,1},... | collective-permute-start | bytes 6152 | tf_op jit(solution)/shard_map/ppermute | solution.py:18
  80.8 3.4 %copy-done.2 = bf16[8192,512]{1,0:T(8,128)(2,1)S(1)} copy-done((bf16[8192,512]{1,0:T(8,128)(2,1)S(1)}, bf16[8192,512]{1,0:T(8,128)(2,1)}, u32[]{:S(2)}) %copy-start.2) | copy-done | bytes 8388632
  84.2 0.7 base.15.refs_7_
  84.9 1.2 %collective-permute-start.17 = (bf16[64,16]{1,0:T(8,128)(2,1)S(1)}, bf16[64,16]{1,0:T(8,128)(2,1)S(1)}, u32[]{:S(2)}, u32[]{:S(2)}) collective-permute-start(bf16[64,16]{1,0:T(8,128)(2,1)S(1)} %add.36), channel_id=1, source_target_pairs={{0,4},{1,5},{2,6},{3,7},{4,0},{5,1},{6,2},{7,3},{8,12},{9,13},{10,... | collective-permute-start | bytes 6152 | tf_op jit(solution)/shard_map/ppermute | solution.py:18
  86.1 0.7 base.14.refs_6_
  86.8 1.9 %collective-permute-done.17 = bf16[64,16]{1,0:T(8,128)(2,1)S(1)} collective-permute-done((bf16[64,16]{1,0:T(8,128)(2,1)S(1)}, bf16[64,16]{1,0:T(8,128)(2,1)S(1)}, u32[]{:S(2)}, u32[]{:S(2)}) %collective-permute-start.17) | collective-permute-done | bytes 2080 | tf_op jit(solution)/shard_map/ppermute | solution.py:18
  88.7 1.4 %collective-permute-start.18 = (bf16[64,16]{1,0:T(8,128)(2,1)S(1)}, bf16[64,16]{1,0:T(8,128)(2,1)S(1)}, u32[]{:S(2)}, u32[]{:S(2)}) collective-permute-start(bf16[64,16]{1,0:T(8,128)(2,1)S(1)} %add.37), channel_id=1, source_target_pairs={{0,2},{1,3},{2,0},{3,1},{4,6},{5,7},{6,4},{7,5},{8,10},{9,11},{10,... | collective-permute-start | bytes 6152 | tf_op jit(solution)/shard_map/ppermute | solution.py:18
  90.1 0.7 base.13.refs_5_
  90.8 1.7 %collective-permute-done.18 = bf16[64,16]{1,0:T(8,128)(2,1)S(1)} collective-permute-done((bf16[64,16]{1,0:T(8,128)(2,1)S(1)}, bf16[64,16]{1,0:T(8,128)(2,1)S(1)}, u32[]{:S(2)}, u32[]{:S(2)}) %collective-permute-start.18) | collective-permute-done | bytes 2080 | tf_op jit(solution)/shard_map/ppermute | solution.py:18
  92.5 0.0 copy-start.6
  92.5 0.1 collective-permute-start.19
  92.6 0.7 base.12.refs_4_
  93.3 0.5 collective-permute-done.19
  93.8 0.6 lift.3
  94.4 10.9 %all_to_all.10 = bf16[16,4,512]{2,1,0:T(4,128)(2,1)S(1)} all-to-all(bf16[16,4,512]{2,1,0:T(4,128)(2,1)S(1)} %lift.3), channel_id=1, replica_groups=mesh['groups'=2,'tensor'=16] {'tensor'}, dimensions={0} | all-to-all | bytes 131072 | tf_op jit(solution)/shard_map/all_to_all | solution.py:265
  105.3 0.6 copy.33
  (42 shorter events, 0.2 us)
Async XLA Ops:
  0.0 58.1 %copy-start = (bf16[4,8,384,128]{3,2,1,0:T(8,128)(2,1)S(1)}, bf16[4,8,384,128]{3,2,1,0:T(8,128)(2,1)}, u32[]{:S(2)}) copy-start(bf16[4,8,384,128]{3,2,1,0:T(8,128)(2,1)} %param.22) | copy-start | bytes 9437188
  0.9 0.9 copy-start.7
  1.8 0.7 copy-start.10
  3.2 5.7 %collective-permute-start = (bf16[4,8320]{1,0:T(4,128)(2,1)S(1)}, bf16[4,8320]{1,0:T(4,128)(2,1)S(1)}, u32[]{:S(2)}, u32[]{:S(2)}) collective-permute-start(bf16[4,8320]{1,0:T(4,128)(2,1)S(1)} %norm.1), channel_id=1, source_target_pairs={{0,4},{1,5},{2,6},{3,7},{4,0},{5,1},{6,2},{7,3},{8,12},{9,13},{10,... | collective-permute-start | bytes 199688 | tf_op jit(solution)/shard_map/ppermute | solution.py:18
  6.3 7.3 %collective-permute-start.1 = (bf16[4,8320]{1,0:T(4,128)(2,1)S(1)}, bf16[4,8320]{1,0:T(4,128)(2,1)S(1)}, u32[]{:S(2)}, u32[]{:S(2)}) collective-permute-start(bf16[4,8320]{1,0:T(4,128)(2,1)S(1)} %norm.1), channel_id=1, source_target_pairs={{0,8},{1,9},{2,10},{3,11},{4,12},{5,13},{6,14},{7,15},{8,0},{9,1},... | collective-permute-start | bytes 199688 | tf_op jit(solution)/shard_map/ppermute | solution.py:18
  8.9 6.2 %collective-permute-start.2 = (bf16[4,8320]{1,0:T(4,128)(2,1)S(1)}, bf16[4,8320]{1,0:T(4,128)(2,1)S(1)}, u32[]{:S(2)}, u32[]{:S(2)}) collective-permute-start(bf16[4,8320]{1,0:T(4,128)(2,1)S(1)} %norm.1), channel_id=1, source_target_pairs={{0,12},{1,13},{2,14},{3,15},{4,8},{5,9},{6,10},{7,11},{8,4},{9,5},... | collective-permute-start | bytes 199688 | tf_op jit(solution)/shard_map/ppermute | solution.py:18
  15.2 6.6 %collective-permute-start.3 = (bf16[16,8320]{1,0:T(8,128)(2,1)S(1)}, bf16[16,8320]{1,0:T(8,128)(2,1)}, u32[]{:S(2)}, u32[]{:S(2)}) collective-permute-start(bf16[16,8320]{1,0:T(8,128)(2,1)S(1)} %pad_maximum_fusion.refs_3_.refs_0_), channel_id=1, source_target_pairs={{0,2},{1,3},{2,0},{3,1},{4,6},{5,7},{6,4},{7,5},{8,10},{9,11},{10,... | collective-permute-start | bytes 798728 | tf_op jit(solution)/shard_map/ppermute | solution.py:18
  16.8 5.1 %collective-permute-start.4 = (bf16[16,8320]{1,0:T(8,128)(2,1)S(1)}, bf16[16,8320]{1,0:T(8,128)(2,1)}, u32[]{:S(2)}, u32[]{:S(2)}) collective-permute-start(bf16[16,8320]{1,0:T(8,128)(2,1)S(1)} %pad_maximum_fusion.refs_3_.refs_0_), channel_id=1, source_target_pairs={{0,1},{1,0},{2,3},{3,2},{4,5},{5,4},{6,7},{7,6},{8,9},{9,8},{10,11... | collective-permute-start | bytes 798728 | tf_op jit(solution)/shard_map/ppermute | solution.py:18
  21.8 1.9 %collective-permute-start.5 = (bf16[16,8320]{1,0:T(8,128)(2,1)}, bf16[16,8320]{1,0:T(8,128)(2,1)}, u32[]{:S(2)}, u32[]{:S(2)}) collective-permute-start(bf16[16,8320]{1,0:T(8,128)(2,1)} %collective-permute-done.3.refs_4_.refs_1_), channel_id=1, source_target_pairs={{0,1},{1,0},{2,3},{3,2},{4,5},{5,4},{6,7},{7,6},{8,9},{9,8},{10,11... | collective-permute-start | bytes 798728 | tf_op jit(solution)/shard_map/ppermute | solution.py:18
  23.7 1.6 %copy-start.3 = (bf16[2,8192,64]{1,2,0:T(8,128)(2,1)S(1)}, bf16[2,8192,64]{1,2,0:T(8,128)(2,1)}, u32[]{:S(2)}) copy-start(bf16[2,8192,64]{1,2,0:T(8,128)(2,1)} %param.19) | copy-start | bytes 6291460
  25.3 0.7 copy-start.8
  28.5 7.6 %collective-permute-start.6 = (bf16[64,48]{1,0:T(8,128)(2,1)S(1)}, bf16[64,48]{1,0:T(8,128)(2,1)S(1)}, u32[]{:S(2)}, u32[]{:S(2)}) collective-permute-start(bf16[64,48]{1,0:T(8,128)(2,1)S(1)} %get-tuple-element.7), channel_id=1, source_target_pairs={{0,8},{1,9},{2,10},{3,11},{4,12},{5,13},{6,14},{7,15},{8,0},{9,1},... | collective-permute-start | bytes 18440 | tf_op jit(solution)/shard_map/ppermute | solution.py:18
  30.6 4.0 %copy-start.1 = (bf16[8192,640]{1,0:T(8,128)(2,1)S(1)}, bf16[8192,640]{1,0:T(8,128)(2,1)}, u32[]{:S(2)}) copy-start(bf16[8192,640]{1,0:T(8,128)(2,1)} %refs_4_.11) | copy-start | bytes 31457284
  36.1 3.8 %collective-permute-start.7 = (bf16[64,48]{1,0:T(8,128)(2,1)S(1)}, bf16[64,48]{1,0:T(8,128)(2,1)S(1)}, u32[]{:S(2)}, u32[]{:S(2)}) collective-permute-start(bf16[64,48]{1,0:T(8,128)(2,1)S(1)} %add.30), channel_id=1, source_target_pairs={{0,4},{1,5},{2,6},{3,7},{4,0},{5,1},{6,2},{7,3},{8,12},{9,13},{10,... | collective-permute-start | bytes 18440 | tf_op jit(solution)/shard_map/ppermute | solution.py:18
  40.0 3.8 %collective-permute-start.8 = (bf16[64,48]{1,0:T(8,128)(2,1)S(1)}, bf16[64,48]{1,0:T(8,128)(2,1)S(1)}, u32[]{:S(2)}, u32[]{:S(2)}) collective-permute-start(bf16[64,48]{1,0:T(8,128)(2,1)S(1)} %add.31), channel_id=1, source_target_pairs={{0,2},{1,3},{2,0},{3,1},{4,6},{5,7},{6,4},{7,5},{8,10},{9,11},{10,... | collective-permute-start | bytes 18440 | tf_op jit(solution)/shard_map/ppermute | solution.py:18
  43.8 1.8 %copy-start.5 = (bf16[32,16,640]{2,1,0:T(8,128)(2,1)S(1)}, bf16[32,16,640]{2,1,0:T(8,128)(2,1)}, u32[]{:S(2)}) copy-start(bf16[32,16,640]{2,1,0:T(8,128)(2,1)} %refs_3_.2) | copy-start | bytes 1966084
  43.8 7.0 %copy-start.12 = (s32[4]{0:T(128)S(1)}, s32[4]{0:T(128)}, u32[]{:S(2)}) copy-start(s32[4]{0:T(128)} %param.16) | copy-start | bytes 52
  43.8 1.7 %collective-permute-start.9 = (bf16[64,48]{1,0:T(8,128)(2,1)S(1)}, bf16[64,48]{1,0:T(8,128)(2,1)S(1)}, u32[]{:S(2)}, u32[]{:S(2)}) collective-permute-start(bf16[64,48]{1,0:T(8,128)(2,1)S(1)} %add.32), channel_id=1, source_target_pairs={{0,1},{1,0},{2,3},{3,2},{4,5},{5,4},{6,7},{7,6},{8,9},{9,8},{10,11... | collective-permute-start | bytes 18440 | tf_op jit(solution)/shard_map/ppermute | solution.py:18
  47.3 10.6 %all-to-all-start = ((bf16[16,4,640]{2,1,0:T(4,128)(2,1)}), bf16[16,4,640]{2,1,0:T(4,128)(2,1)S(1)}, u32[]{:S(2)}, u32[]{:S(2)}) async-start(bf16[16,4,640]{2,1,0:T(4,128)(2,1)} %lift.2), calls=%async_computation | async-start | bytes 163840 | tf_op jit(solution)/shard_map/all_to_all | solution.py:265
  57.9 1.9 %copy-start.11 = (bf16[4,8,384,128]{3,2,1,0:T(8,128)(2,1)S(1)}, bf16[4,8,384,128]{3,2,1,0:T(8,128)(2,1)}, u32[]{:S(2)}) copy-start(bf16[4,8,384,128]{3,2,1,0:T(8,128)(2,1)} %param.23) | copy-start | bytes 9437188
  59.4 17.7 %copy-start.4 = (bf16[2,8192,64]{1,2,0:T(8,128)(2,1)S(1)}, bf16[2,8192,64]{1,2,0:T(8,128)(2,1)}, u32[]{:S(2)}) copy-start(bf16[2,8192,64]{1,2,0:T(8,128)(2,1)} %param.19) | copy-start | bytes 6291460
  59.4 17.7 %copy-start.9 = (s32[32]{0:T(128)S(1)}, s32[32]{0:T(128)}, u32[]{:S(2)}) copy-start(s32[32]{0:T(128)} %refs_0_.3) | copy-start | bytes 388
  60.6 4.8 %collective-permute-start.10 = (bf16[4,8192]{1,0:T(4,128)(2,1)S(1)}, bf16[4,8192]{1,0:T(4,128)(2,1)S(1)}, u32[]{:S(2)}, u32[]{:S(2)}) collective-permute-start(bf16[4,8192]{1,0:T(4,128)(2,1)S(1)} %bitcast.41), channel_id=1, source_target_pairs={{0,4},{1,5},{2,6},{3,7},{4,0},{5,1},{6,2},{7,3},{8,12},{9,13},{10,... | collective-permute-start | bytes 196616 | tf_op jit(solution)/shard_map/ppermute | solution.py:18
  60.7 8.3 %collective-permute-start.11 = (bf16[4,8192]{1,0:T(4,128)(2,1)S(1)}, bf16[4,8192]{1,0:T(4,128)(2,1)S(1)}, u32[]{:S(2)}, u32[]{:S(2)}) collective-permute-start(bf16[4,8192]{1,0:T(4,128)(2,1)S(1)} %bitcast.42), channel_id=1, source_target_pairs={{0,8},{1,9},{2,10},{3,11},{4,12},{5,13},{6,14},{7,15},{8,0},{9,1},... | collective-permute-start | bytes 196616 | tf_op jit(solution)/shard_map/ppermute | solution.py:18
  61.8 7.2 %collective-permute-start.12 = (bf16[4,8192]{1,0:T(4,128)(2,1)S(1)}, bf16[4,8192]{1,0:T(4,128)(2,1)S(1)}, u32[]{:S(2)}, u32[]{:S(2)}) collective-permute-start(bf16[4,8192]{1,0:T(4,128)(2,1)S(1)} %bitcast.43), channel_id=1, source_target_pairs={{0,12},{1,13},{2,14},{3,15},{4,8},{5,9},{6,10},{7,11},{8,4},{9,5},... | collective-permute-start | bytes 196616 | tf_op jit(solution)/shard_map/ppermute | solution.py:18
  69.1 6.4 %collective-permute-start.13 = (bf16[16,8192]{1,0:T(8,128)(2,1)S(1)}, bf16[16,8192]{1,0:T(8,128)(2,1)S(1)}, u32[]{:S(2)}, u32[]{:S(2)}) collective-permute-start(bf16[16,8192]{1,0:T(8,128)(2,1)S(1)} %pad_maximum_fusion.1.refs_3_.refs_0_), channel_id=1, source_target_pairs={{0,2},{1,3},{2,0},{3,1},{4,6},{5,7},{6,4},{7,5},{8,10},{9,11},{10,... | collective-permute-start | bytes 786440 | tf_op jit(solution)/shard_map/ppermute | solution.py:18
  69.9 5.7 %collective-permute-start.14 = (bf16[16,8192]{1,0:T(8,128)(2,1)S(1)}, bf16[16,8192]{1,0:T(8,128)(2,1)S(1)}, u32[]{:S(2)}, u32[]{:S(2)}) collective-permute-start(bf16[16,8192]{1,0:T(8,128)(2,1)S(1)} %pad_maximum_fusion.1.refs_3_.refs_0_), channel_id=1, source_target_pairs={{0,1},{1,0},{2,3},{3,2},{4,5},{5,4},{6,7},{7,6},{8,9},{9,8},{10,11... | collective-permute-start | bytes 786440 | tf_op jit(solution)/shard_map/ppermute | solution.py:18
  75.6 1.5 %collective-permute-start.15 = (bf16[16,8192]{1,0:T(8,128)(2,1)S(1)}, bf16[16,8192]{1,0:T(8,128)(2,1)S(1)}, u32[]{:S(2)}, u32[]{:S(2)}) collective-permute-start(bf16[16,8192]{1,0:T(8,128)(2,1)S(1)} %collective-permute-done.13.refs_4_.refs_1_), channel_id=1, source_target_pairs={{0,1},{1,0},{2,3},{3,2},{4,5},{5,4},{6,7},{7,6},{8,9},{9,8},{10,11... | collective-permute-start | bytes 786440 | tf_op jit(solution)/shard_map/ppermute | solution.py:18
  79.1 5.7 %collective-permute-start.16 = (bf16[64,16]{1,0:T(8,128)(2,1)S(1)}, bf16[64,16]{1,0:T(8,128)(2,1)S(1)}, u32[]{:S(2)}, u32[]{:S(2)}) collective-permute-start(bf16[64,16]{1,0:T(8,128)(2,1)S(1)} %down.3), channel_id=1, source_target_pairs={{0,8},{1,9},{2,10},{3,11},{4,12},{5,13},{6,14},{7,15},{8,0},{9,1},... | collective-permute-start | bytes 6152 | tf_op jit(solution)/shard_map/ppermute | solution.py:18
  80.8 3.4 %copy-start.2 = (bf16[8192,512]{1,0:T(8,128)(2,1)S(1)}, bf16[8192,512]{1,0:T(8,128)(2,1)}, u32[]{:S(2)}) copy-start(bf16[8192,512]{1,0:T(8,128)(2,1)} %refs_4_.15) | copy-start | bytes 25165828
  84.9 3.8 %collective-permute-start.17 = (bf16[64,16]{1,0:T(8,128)(2,1)S(1)}, bf16[64,16]{1,0:T(8,128)(2,1)S(1)}, u32[]{:S(2)}, u32[]{:S(2)}) collective-permute-start(bf16[64,16]{1,0:T(8,128)(2,1)S(1)} %add.36), channel_id=1, source_target_pairs={{0,4},{1,5},{2,6},{3,7},{4,0},{5,1},{6,2},{7,3},{8,12},{9,13},{10,... | collective-permute-start | bytes 6152 | tf_op jit(solution)/shard_map/ppermute | solution.py:18
  88.7 3.8 %collective-permute-start.18 = (bf16[64,16]{1,0:T(8,128)(2,1)S(1)}, bf16[64,16]{1,0:T(8,128)(2,1)S(1)}, u32[]{:S(2)}, u32[]{:S(2)}) collective-permute-start(bf16[64,16]{1,0:T(8,128)(2,1)S(1)} %add.37), channel_id=1, source_target_pairs={{0,2},{1,3},{2,0},{3,1},{4,6},{5,7},{6,4},{7,5},{8,10},{9,11},{10,... | collective-permute-start | bytes 6152 | tf_op jit(solution)/shard_map/ppermute | solution.py:18
  92.5 1.3 %copy-start.6 = (bf16[32,16,512]{2,1,0:T(8,128)(2,1)S(1)}, bf16[32,16,512]{2,1,0:T(8,128)(2,1)}, u32[]{:S(2)}) copy-start(bf16[32,16,512]{2,1,0:T(8,128)(2,1)} %refs_3_.3) | copy-start | bytes 1572868
  92.5 1.2 %collective-permute-start.19 = (bf16[64,16]{1,0:T(8,128)(2,1)S(1)}, bf16[64,16]{1,0:T(8,128)(2,1)S(1)}, u32[]{:S(2)}, u32[]{:S(2)}) collective-permute-start(bf16[64,16]{1,0:T(8,128)(2,1)S(1)} %add.38), channel_id=1, source_target_pairs={{0,1},{1,0},{2,3},{3,2},{4,5},{5,4},{6,7},{7,6},{8,9},{9,8},{10,11... | collective-permute-start | bytes 6152 | tf_op jit(solution)/shard_map/ppermute | solution.py:18

commit v3 on v2

v3 whole, which is shorter than its diff:
```python
import functools

import jax
import jax.numpy as jnp
from jax import lax
from jax.experimental import pallas as pl
from jax.experimental.pallas import tpu as pltpu
from jax.sharding import PartitionSpec as P

eps = 1e-05
AXIS = "tensor"
LANES = 128
VMEM = pltpu.VMEM
SMEM = pltpu.SMEM


def swap(x, count, offset):
    return lax.ppermute(x, AXIS, [(i, i ^ offset) for i in range(count)])


def exchange(x, groups=None):
    return lax.all_to_all(
        x, AXIS, split_axis=0, concat_axis=0, axis_index_groups=groups, tiled=True
    )


def gather_rows(x, count):
    step = count // 4
    far, middle, near = (swap(x, count, k * step) for k in (3, 2, 1))
    parts = [x, near, middle, far]
    step //= 2
    held = [jnp.concatenate(parts, axis=0)]
    if step:
        across = [swap(p, count, step) for p in (x, far, near, middle)]
        held.append(jnp.concatenate([across[i] for i in (0, 2, 3, 1)], axis=0))
        step //= 2
    while step:
        held = held + [swap(h, count, step) for h in held]
        step //= 2
    return held


def place_of(row, me, count, rows):
    block = row // rows
    source = (block % 4) * (count // 4)
    piece, step = block // 4, count // 8
    while step:
        source = source + (piece % 2) * step
        piece, step = piece // 2, step // 2
    return (source ^ me) * rows + row % rows


def limit(total):
    return (10 if total <= 64 else 60) * 1024 * 1024


def spec(space=VMEM):
    return pl.BlockSpec(memory_space=space)


def iota(shape, dim):
    return lax.broadcasted_iota(jnp.int32, shape, dim)


def one_hot(condition):
    return jnp.where(condition, 1.0, 0.0).astype(jnp.bfloat16)


def setup_kernel(count, rows, held, storage_ref, order_ref, back_ref, names_ref):
    total = count * rows
    me = lax.axis_index(AXIS)
    row, column = iota((total, total), 0), iota((total, total), 1)
    order_ref[...] = one_hot(place_of(column, me, count, rows) == row)
    back_ref[...] = one_hot(place_of(row, me, count, rows) == column)
    for s in range(held):
        name = lax.fori_loop(
            0,
            storage_ref.shape[0],
            lambda a, found, s=s: jnp.where(storage_ref[a] == me * held + s, a, found),
            jnp.int32(0),
        )
        names_ref[s] = jnp.full((8, LANES), name, jnp.int32).astype(jnp.float32)


def norm_kernel(hidden_hbm, gain_hbm, ids_hbm, out_ref, hidden_ref, gain_ref, ids_ref, sems):
    copies = [
        pltpu.make_async_copy(source, target, sems.at[i])
        for i, (source, target) in enumerate(
            ((hidden_hbm, hidden_ref), (gain_hbm, gain_ref), (ids_hbm, ids_ref))
        )
    ]
    for copy in copies:
        copy.start()
    for copy in copies:
        copy.wait()
    rows, width = hidden_ref.shape
    hidden = hidden_ref[...].astype(jnp.float32)
    power = jnp.sum(hidden * hidden, axis=1, keepdims=True) / width
    gain = gain_ref[...].reshape(1, width).astype(jnp.float32)
    out_ref[:, :width] = (hidden * lax.rsqrt(power + eps) * gain).astype(jnp.bfloat16)
    row = iota((rows, LANES), 0)
    ids = jnp.zeros((rows, LANES), jnp.float32)
    for r in range(rows):
        ids = jnp.where(row == r, ids_ref[r].astype(jnp.float32), ids)
    out_ref[:, width:] = ids.astype(jnp.bfloat16)


NT = (((1,), (1,)), ((), ()))


def down_kernel(pieces, first, *refs):
    names_ref, back_ref, down_ref = refs[:3]
    piece_refs, refs = refs[3 : 3 + pieces], refs[3 + pieces :]
    if first:
        out_ref, ids_out_ref = refs
    else:
        ids_ref, out_ref = refs
    total = back_ref.shape[0]
    held, rank, width = down_ref.shape
    if first:
        ids = jnp.concatenate([p[:, width:] for p in piece_refs], axis=0)
        ids_out_ref[...] = ids
    else:
        ids = ids_ref[...]
    chunk = 1024
    sums = jnp.zeros((held * rank, total), jnp.float32)
    for k in range(0, width, chunk):
        x = jnp.concatenate([p[:, k : k + chunk] for p in piece_refs], axis=0)
        maps = down_ref[:, :, k : k + chunk].reshape(held * rank, chunk)
        sums = sums + lax.dot_general(maps, x, NT, preferred_element_type=jnp.float32)
    first_lane = one_hot(iota((16, LANES), 1) == 0)
    across = lax.dot_general(first_lane, ids, NT, preferred_element_type=jnp.float32)
    chosen = jnp.zeros((rank, total), jnp.float32)
    for s in range(held):
        mine = across[:1] == names_ref[s, :1, :1]
        chosen = jnp.where(mine, sums[s * rank : (s + 1) * rank], chosen)
    placed = jnp.dot(
        chosen.astype(jnp.bfloat16), back_ref[...], preferred_element_type=jnp.float32
    )
    lanes = out_ref.shape[2]
    folds = lanes // total
    part = rank // folds
    folded = [placed[f * part : (f + 1) * part] for f in range(folds)]
    value = jnp.concatenate(folded, axis=1).astype(jnp.bfloat16)
    for d in range(out_ref.shape[0]):
        out_ref[d] = value


def base_kernel(pieces, *refs):
    weight_ref, out_ref = refs[pieces], refs[pieces + 1]
    x = jnp.concatenate([p[...] for p in refs[:pieces]], axis=0)
    columns = weight_ref.shape[1]
    for c in range(0, columns, 512):
        at = slice(c, min(c + 512, columns))
        term = jnp.dot(x, weight_ref[:, at], preferred_element_type=jnp.float32)

        @pl.when(pl.program_id(0) == 0)
        def _():
            out_ref[:, at] = term

        @pl.when(pl.program_id(0) > 0)
        def _():
            out_ref[:, at] += term


def lift_kernel(rows, bounds, rank, *refs):
    down_ref, ids_ref, order_ref, back_ref, up_ref, base_ref, out_ref, sum_ref = refs
    total = order_ref.shape[0]
    me = lax.axis_index(AXIS)
    adapters, per, columns = up_ref.shape
    wide = adapters * per
    folded = down_ref[0].astype(jnp.float32)
    for d in range(1, down_ref.shape[0]):
        folded = folded + down_ref[d].astype(jnp.float32)
    folds = folded.shape[1] // total
    down = jnp.concatenate([folded[:, f * total : (f + 1) * total] for f in range(folds)], axis=0)
    down = lax.dot_general(
        back_ref[...], down.astype(jnp.bfloat16), NT, preferred_element_type=jnp.float32
    ).astype(jnp.bfloat16)
    named = (iota((total, wide), 1) // per).astype(jnp.float32) == ids_ref[:, :1].astype(
        jnp.float32
    )
    start = me * columns
    sum_ref[...] = base_ref[...]
    for g in range(rank // per):
        low, high = bounds[g], bounds[g + 1]

        @pl.when((start < high) & (start + columns > low))
        def _():
            at = iota((rank, wide), 1) % per + g * per
            spread = one_hot(at == iota((rank, wide), 0))
            copies = jnp.dot(down, spread, preferred_element_type=jnp.float32)
            chosen = jnp.where(named, copies, 0.0).astype(jnp.bfloat16)
            for c in range(0, columns, 512):
                end = min(c + 512, columns)
                up = up_ref[:, :, c:end].reshape(wide, end - c)
                lifted = jnp.dot(chosen, up, preferred_element_type=jnp.float32)
                column = iota((total, end - c), 1) + (start + c)
                inside = (column >= low) & (column < high)
                sum_ref[:, c:end] += jnp.where(inside, lifted, 0.0)

    placed = jnp.dot(
        order_ref[...], sum_ref[...].astype(jnp.bfloat16), preferred_element_type=jnp.float32
    ).astype(jnp.bfloat16)
    for d in range(total // rows):
        out_ref[d] = placed[d * rows : (d + 1) * rows]


def local(
    input_hidden,
    input_norm_gain,
    request_adapter,
    adapter_storage,
    lengths,
    projection_weight,
    output_weight,
    adapter_down,
    projection_up_adapter,
    output_up_adapter,
    cache_keys,
    cache_values,
    *,
    count,
):
    rows, width = input_hidden.shape
    rank = projection_up_adapter.shape[1]
    held = adapter_down.shape[0]
    kv_heads, context, head_dim = cache_keys.shape[1:]
    kv_width = kv_heads * head_dim
    total = rows * count
    params = pltpu.CompilerParams(vmem_limit_bytes=limit(total))
    down_maps = jnp.swapaxes(adapter_down, 1, 2)
    bf16, f32 = jnp.bfloat16, jnp.float32

    normed = pl.pallas_call(
        norm_kernel,
        out_shape=jax.ShapeDtypeStruct((rows, width + LANES), bf16),
        in_specs=[spec(pltpu.HBM)] * 3,
        out_specs=spec(),
        scratch_shapes=[
            VMEM((rows, width), bf16),
            VMEM((width,), bf16),
            SMEM((rows,), jnp.int32),
            pltpu.SemaphoreType.DMA((3,)),
        ],
        compiler_params=params,
        name="norm",
    )(input_hidden, input_norm_gain, request_adapter.reshape(rows))

    order, back, names = pl.pallas_call(
        functools.partial(setup_kernel, count, rows, held),
        out_shape=[
            jax.ShapeDtypeStruct((total, total), bf16),
            jax.ShapeDtypeStruct((total, total), bf16),
            jax.ShapeDtypeStruct((held, 8, LANES), f32),
        ],
        in_specs=[spec(SMEM)],
        out_specs=[spec()] * 3,
        compiler_params=params,
        name="setup",
    )(adapter_storage)

    def downs(pieces, low, high, ids, copies):
        ranks = high - low
        first = ids is None
        lanes = max(LANES, total)
        down_spec = pl.BlockSpec((held, ranks, width), lambda i: (0, low // ranks, 0))
        shapes = [jax.ShapeDtypeStruct((copies, ranks * total // lanes, lanes), bf16)]
        if first:
            shapes.append(jax.ShapeDtypeStruct((total, LANES), bf16))
        return pl.pallas_call(
            functools.partial(down_kernel, len(pieces), first),
            grid=(1,),
            out_shape=shapes,
            in_specs=[spec(), spec(), down_spec]
            + [spec()] * (len(pieces) + (0 if first else 1)),
            out_specs=[spec()] * len(shapes),
            compiler_params=params,
            cost_estimate=pl.CostEstimate(
                flops=2 * total * width * held * ranks,
                bytes_accessed=2 * width * (held * ranks + total),
                transcendentals=0,
            ),
            name="down",
        )(names, back, down_maps, *pieces, *([] if first else [ids]))

    def base(pieces, weight):
        columns = weight.shape[1]
        chunk = 1024
        piece_rows = pieces[0].shape[0]
        return pl.pallas_call(
            functools.partial(base_kernel, len(pieces)),
            grid=(width // chunk,),
            out_shape=jax.ShapeDtypeStruct((total, columns), f32),
            in_specs=[pl.BlockSpec((piece_rows, chunk), lambda i: (0, i))] * len(pieces)
            + [pl.BlockSpec((chunk, columns), lambda i: (i, 0))],
            out_specs=pl.BlockSpec((total, columns), lambda i: (0, 0)),
            compiler_params=params,
            cost_estimate=pl.CostEstimate(
                flops=2 * total * width * columns,
                bytes_accessed=2 * width * columns,
                transcendentals=0,
            ),
            name="base",
        )(*pieces, weight)

    def lift(down, ids, up, base_term, bounds, ranks):
        columns = up.shape[2]
        return pl.pallas_call(
            functools.partial(lift_kernel, rows, bounds, ranks),
            out_shape=jax.ShapeDtypeStruct((count, rows, columns), bf16),
            in_specs=[spec()] * 6,
            out_specs=spec(),
            scratch_shapes=[VMEM((total, columns), f32)],
            compiler_params=params,
            name="lift",
        )(down, ids, order, back, up, base_term)

    def project(pieces, ids, low, high, weight, up, bounds):
        if ids is None:
            down, ids = downs(pieces, low, high, ids, count)
            down = exchange(down)
        else:
            outer = [[i + j for i in range(0, count, 4)] for j in range(4)]
            inner = [[i + j for j in range(4)] for i in range(0, count, 4)]
            (down,) = downs(pieces, low, high, ids, count // 4)
            down = jnp.sum(exchange(down, outer).astype(f32), axis=0).astype(bf16)
            down = exchange(jnp.broadcast_to(down[None], (4,) + down.shape), inner)
        base_term = base(pieces, weight)
        columns = lift(down, ids, up, base_term, bounds, high - low)
        mine = exchange(columns)
        return jnp.swapaxes(mine, 0, 1).reshape(rows, -1), ids

    bounds = (0, width, width + kv_width, width + 2 * kv_width)
    qkv_mine, ids = project(
        gather_rows(normed, count),
        None,
        0,
        3 * rank,
        projection_weight,
        projection_up_adapter,
        bounds,
    )

    groups_per = width // head_dim // kv_heads
    query = qkv_mine[:, 0:width].reshape(rows, kv_heads, groups_per, head_dim)
    key_new = qkv_mine[:, width : width + kv_width].reshape(rows, kv_heads, head_dim)
    value_new = qkv_mine[:, width + kv_width :].reshape(rows, kv_heads, head_dim)
    scale = head_dim ** (-0.5)
    scores = (
        jnp.einsum("bhgd,bhpd->bhgp", query, cache_keys, preferred_element_type=jnp.float32) * scale
    )
    live = jnp.arange(context, dtype=jnp.int32)[None, :] < lengths[:, None]
    scores = jnp.where(live[:, None, None, :], scores, -1e30)
    own = jnp.einsum("bhgd,bhd->bhg", query, key_new, preferred_element_type=jnp.float32) * scale
    peak = jnp.maximum(jnp.max(scores, axis=3), own)
    weights = jnp.exp(scores - peak[..., None])
    own_weight = jnp.exp(own - peak)
    denominator = jnp.sum(weights, axis=3) + own_weight
    probs = (weights / denominator[..., None]).astype(jnp.bfloat16)
    own_prob = (own_weight / denominator).astype(jnp.bfloat16)
    mixed = jnp.einsum("bhgp,bhpd->bhgd", probs, cache_values, preferred_element_type=jnp.float32)
    mixed = (
        mixed
        + own_prob.astype(jnp.float32)[..., None] * value_new.astype(jnp.float32)[:, :, None, :]
    )
    attended = mixed.reshape(rows, width).astype(jnp.bfloat16)

    output, _ = project(
        gather_rows(attended, count),
        ids,
        3 * rank,
        4 * rank,
        output_weight,
        output_up_adapter,
        (0, width),
    )
    return output


def solution(mesh):
    count = mesh.shape[AXIS]

    def body(*arrays):
        return local(*arrays, count=count)

    return jax.shard_map(
        body,
        mesh=mesh,
        in_specs=(
            P(("groups", "tensor"), None),
            P(),
            P(("groups", "tensor"), None),
            P(),
            P(("groups", "tensor")),
            P(None, "tensor"),
            P(None, "tensor"),
            P("tensor", None, None),
            P(None, None, "tensor"),
            P(None, None, "tensor"),
            P(("groups", "tensor"), None, None, None),
            P(("groups", "tensor"), None, None, None),
        ),
        out_specs=P(("groups", "tensor"), None),
        check_vma=False,
    )
```

time: 107 us -> 117 us (1.093)
  waiting for transfers between devices: 37.9 us -> 20.1 us
  local copies, waits for them, and re-layouts: 13 us -> 26.7 us
  starting transfers between devices: 24.3 us -> 32.5 us
  blocking collectives: 10.9 us -> 18 us
  Pallas kernels: 16.7 us -> 14.1 us
    ppermute x20 -> x18, waiting for transfers between devices: 30.9 us -> 13.7 us  [swap(): return lax.ppermute(x, AXIS, [(i, i ^ offset) for i in range(count)])]
    unnamed x30 -> x68, local copies, waits for them, and re-layouts: 12.1 us -> 26.1 us
    all_to_all x1 -> x3, starting transfers between devices: 3.5 us -> 14.5 us  [exchange(): lax.all_to_all(x, AXIS, split_axis=0, concat_axis=0, axis_index_groups=gr...]
    all_to_all x1 -> x2, blocking collectives: 10.9 us -> 18 us  [exchange(): lax.all_to_all(x, AXIS, split_axis=0, concat_axis=0, axis_index_groups=gr...]
    ppermute x20 -> x18, starting transfers between devices: 20.8 us -> 18 us  [swap(): return lax.ppermute(x, AXIS, [(i, i ^ offset) for i in range(count)])]
    pallas_call x12 -> x7, Pallas kernels: 15.9 us -> 13.3 us  [the longest x2 8.13 us: base(): pl.pallas_call(functools.partial(base_kernel, len(pieces)), grid=(width /...]
    all_to_all x1 -> x3, waiting for transfers between devices: 7.02 us -> 6.42 us  [exchange(): lax.all_to_all(x, AXIS, split_axis=0, concat_axis=0, axis_index_groups=gr...]
  transfers between devices with their start and end apart: 21 -> 21, of which waited for: 14 -> 11; matrix products, arithmetic and copies ran while one was open for 0% -> 1% of each run, Pallas kernels for 9% -> 8%
where the time goes in v3:
time: 117 us; the launch traced here: 116 us
  starting transfers between devices  32.5 us (28%)
  local copies, waits for them, and re-layouts  26.7 us (23%)
  waiting for transfers between devices  20.1 us (17%)
  blocking collectives  18 us (15%)
  Pallas kernels  14.1 us (12%)
  matrix products  2.11 us (2%)
  other arithmetic  1.64 us (1%)
    unnamed x68, local copies, waits for them, and re-layouts  26.1 us
    ppermute x18, starting transfers between devices, swap(): return lax.ppermute(x, AXIS, [(i, i ^ offset) for i in range(count)])  18 us
    all_to_all x2, blocking collectives, exchange(): lax.all_to_all(x, AXIS, split_axis=0, concat_axis=0, axis_index_groups=gr...  18 us
    all_to_all x3, starting transfers between devices, exchange(): lax.all_to_all(x, AXIS, split_axis=0, concat_axis=0, axis_index_groups=gr...  14.5 us
    ppermute x18, waiting for transfers between devices, swap(): return lax.ppermute(x, AXIS, [(i, i ^ offset) for i in range(count)])  13.7 us
    pallas_call x2, Pallas kernels, base(): pl.pallas_call(functools.partial(base_kernel, len(pieces)), grid=(width /...  8.13 us
    all_to_all x3, waiting for transfers between devices, exchange(): lax.all_to_all(x, AXIS, split_axis=0, concat_axis=0, axis_index_groups=gr...  6.42 us
    pallas_call x2, Pallas kernels, lift(): pl.pallas_call(functools.partial(lift_kernel, rows, bounds, ranks), out_s...  2.66 us
  transfers between devices with their start and end apart: 21, of which 11 were waited for; matrix products, arithmetic and copies ran while one was open for 1% of the time, Pallas kernels for 8%

profile of v3, /device:TPU:0, one launch (start us, length us, event | category | flops | bytes accessed | tf_op | source)
XLA Modules:
  0.0 115.6 jit_solution(14274590604987241569)
XLA Ops:
  0.0 1.0 copy-done.27
  1.0 0.7 copy-done.28
  1.7 0.7 copy-done.29
  2.4 0.8 norm.1
  3.2 5.1 %collective-permute-start.2 = (bf16[4,8320]{1,0:T(4,128)(2,1)S(1)}, bf16[4,8320]{1,0:T(4,128)(2,1)S(1)}, u32[]{:S(2)}, u32[]{:S(2)}) collective-permute-start(bf16[4,8320]{1,0:T(4,128)(2,1)S(1)} %norm.1), channel_id=1, source_target_pairs={{0,12},{1,13},{2,14},{3,15},{4,8},{5,9},{6,10},{7,11},{8,4},{9,5},... | collective-permute-start | bytes 199688 | tf_op jit(solution)/shard_map/ppermute | solution.py:18
  8.3 0.6 collective-permute-start
  9.0 1.6 %collective-permute-start.3 = (bf16[4,8320]{1,0:T(4,128)(2,1)S(1)}, bf16[4,8320]{1,0:T(4,128)(2,1)S(1)}, u32[]{:S(2)}, u32[]{:S(2)}) collective-permute-start(bf16[4,8320]{1,0:T(4,128)(2,1)S(1)} %norm.1), channel_id=1, source_target_pairs={{0,2},{1,3},{2,0},{3,1},{4,6},{5,7},{6,4},{7,5},{8,10},{9,11},{10,... | collective-permute-start | bytes 199688 | tf_op jit(solution)/shard_map/ppermute | solution.py:18
  10.6 0.3 collective-permute-done.2
  10.9 1.9 %collective-permute-start.6 = (bf16[4,8320]{1,0:T(4,128)(2,1)S(1)}, bf16[4,8320]{1,0:T(4,128)(2,1)S(1)}, u32[]{:S(2)}, u32[]{:S(2)}) collective-permute-start(bf16[4,8320]{1,0:T(4,128)(2,1)S(1)} %collective-permute-done.2), channel_id=1, source_target_pairs={{0,2},{1,3},{2,0},{3,1},{4,6},{5,7},{6,4},{7,5},{8,10},{9,11},{10,... | collective-permute-start | bytes 199688 | tf_op jit(solution)/shard_map/ppermute | solution.py:18
  12.8 1.2 %collective-permute-done.1 = bf16[4,8320]{1,0:T(4,128)(2,1)S(1)} collective-permute-done((bf16[4,8320]{1,0:T(4,128)(2,1)S(1)}, bf16[4,8320]{1,0:T(4,128)(2,1)S(1)}, u32[]{:S(2)}, u32[]{:S(2)}) %collective-permute-start.1) | collective-permute-done | bytes 66592 | tf_op jit(solution)/shard_map/ppermute | solution.py:18
  14.0 1.5 %collective-permute-start.5 = (bf16[4,8320]{1,0:T(4,128)(2,1)S(1)}, bf16[4,8320]{1,0:T(4,128)(2,1)S(1)}, u32[]{:S(2)}, u32[]{:S(2)}) collective-permute-start(bf16[4,8320]{1,0:T(4,128)(2,1)S(1)} %collective-permute-done.1), channel_id=1, source_target_pairs={{0,2},{1,3},{2,0},{3,1},{4,6},{5,7},{6,4},{7,5},{8,10},{9,11},{10,... | collective-permute-start | bytes 199688 | tf_op jit(solution)/shard_map/ppermute | solution.py:18
  15.5 0.5 collective-permute-start.4
  16.3 2.6 %collective-permute-done.5 = bf16[4,8320]{1,0:T(4,128)(2,1)S(1)} collective-permute-done((bf16[4,8320]{1,0:T(4,128)(2,1)S(1)}, bf16[4,8320]{1,0:T(4,128)(2,1)S(1)}, u32[]{:S(2)}, u32[]{:S(2)}) %collective-permute-start.5) | collective-permute-done | bytes 66592 | tf_op jit(solution)/shard_map/ppermute | solution.py:18
  18.9 0.9 collective-permute-done.4
  20.0 0.7 copy-done.30
  20.7 1.3 %setup.1 = (bf16[64,64]{1,0:T(8,128)(2,1)S(1)}, bf16[64,64]{1,0:T(8,128)(2,1)S(1)}, f32[2,8,128]{2,1,0:T(8,128)S(1)}) custom-call(s32[32]{0:T(128)S(1)} %copy-done.30), custom_call_target="tpu_custom_call" | custom-call | tf_op jit(solution)/shard_map/setup/pallas_call | solution.py:250
  22.0 0.6 copy-done.24
  22.6 1.8 %copy-done.3 = bf16[2,8192,64]{1,2,0:T(8,128)(2,1)S(1)} copy-done((bf16[2,8192,64]{1,2,0:T(8,128)(2,1)S(1)}, bf16[2,8192,64]{1,2,0:T(8,128)(2,1)}, u32[]{:S(2)}) %copy-start.3) | copy-done | bytes 2097176
  24.4 0.7 down.2
  25.2 0.6 copy-done.23
  25.8 4.3 %all-to-all-start = ((bf16[16,24,128]{2,1,0:T(8,128)(2,1)}), bf16[16,24,128]{2,1,0:T(8,128)(2,1)S(1)}, u32[]{:S(2)}, u32[]{:S(2)}) async-start(bf16[16,24,128]{2,1,0:T(8,128)(2,1)} %copy-done.23), calls=%async_computation | async-start | bytes 196608 | tf_op jit(solution)/shard_map/all_to_all | solution.py:22
  30.1 4.0 %copy-done.1 = bf16[8192,640]{1,0:T(8,128)(2,1)S(1)} copy-done((bf16[8192,640]{1,0:T(8,128)(2,1)S(1)}, bf16[8192,640]{1,0:T(8,128)(2,1)}, u32[]{:S(2)}) %copy-start.1) | copy-done | bytes 10485784
  34.1 0.9 copy-done.6
  35.1 0.9 copy-done.10
  36.0 0.9 copy-done.12
  37.0 5.4 %base.2.refs_5_ = f32[64,640]{1,0:T(8,128)S(1)} custom-call(bf16[16,8320]{1,0:T(8,128)(2,1)S(1)} %pad_maximum_fusion.refs_3_.refs_0_, bf16[16,8320]{1,0:T(8,128)(2,1)S(1)} %copy-done.6, bf16[16,8320]{1,0:T(8,128)(2,1)S(1)} %copy-done.10, bf16[16,8320]{1,0:T(8,128)(2,1)S(1)} %copy-done.12, bf16[8192,640]{1,0:T(8,128)(2,1)S(1)} %copy-done.1), custom_call_target="tpu_custom_call" | custom-call | flops 671088640 | bytes 10485760 | tf_op jit(solution)/shard_map/base/pallas_call | solution.py:291
  42.4 0.7 copy-done.18
  43.1 1.1 copy-done.17
  44.2 0.9 copy-done.19
  45.1 0.7 copy-done.25
  45.8 1.3 %lift.2 = bf16[16,4,640]{2,1,0:T(4,128)(2,1)} custom-call(bf16[16,24,128]{2,1,0:T(8,128)(2,1)S(1)} %all-to-all-done.refs_0_, bf16[64,128]{1,0:T(8,128)(2,1)S(1)} %get-tuple-element.13.refs_1_.refs_7_, bf16[64,64]{1,0:T(8,128)(2,1)S(1)} %copy-done.25, bf16[64,64]{1,0:T(8,128)(2,1)S(1)} %get-tuple-element.11.refs_1_.refs_3_, ...), custom_call_target="tpu_custom_call" | custom-call | tf_op jit(solution)/shard_map/lift/pallas_call | solution.py:309
  47.1 6.3 %all-to-all-start.1 = ((bf16[16,4,640]{2,1,0:T(4,128)(2,1)}), bf16[16,4,640]{2,1,0:T(4,128)(2,1)S(1)}, u32[]{:S(2)}, u32[]{:S(2)}) async-start(bf16[16,4,640]{2,1,0:T(4,128)(2,1)} %lift.2), calls=%async_computation.1 | async-start | bytes 163840 | tf_op jit(solution)/shard_map/all_to_all | solution.py:22
  53.5 0.7 iota_compare_fusion
  54.2 6.4 %all-to-all-done.1 = bf16[16,4,640]{2,1,0:T(4,128)(2,1)S(1)} async-done(((bf16[16,4,640]{2,1,0:T(4,128)(2,1)}), bf16[16,4,640]{2,1,0:T(4,128)(2,1)S(1)}, u32[]{:S(2)}, u32[]{:S(2)}) %all-to-all-start.1) | async-done | bytes 81952 | tf_op jit(solution)/shard_map/all_to_all | solution.py:22
  60.9 1.3 %fusion.13 = (f32[4,8,8]{2,1,0:T(8,128)S(1)}, f32[4,8,8,384]{3,2,1,0:T(8,128)S(1)}) fusion(bf16[4,8,384,128]{3,2,1,0:T(8,128)(2,1)S(1)} %copy-done, bf16[1,4,64,128]{3,1,2,0:T(4,128)(2,1)S(1)} %slice_bitcast_fusion, pred[4,384]{1,0:T(4,128)(4,1)S(1)} %iota_compare_fusion), kind=kOutput, calls=%fused_computation.29 | convolution fusion | flops 25460480 | bytes 3607040 | tf_op jit(solution)/shard_map/bhgd,bhpd->bhgp/dot_general | solution.py:351
  62.1 0.2 fusion.3
  62.4 0.2 copy-done.31
  62.6 0.7 fusion.2
  63.4 0.7 collective-permute-start.11
  64.0 0.8 collective-permute-start.10
  64.8 3.0 %collective-permute-start.9 = (bf16[4,8192]{1,0:T(4,128)(2,1)S(1)}, bf16[4,8192]{1,0:T(4,128)(2,1)S(1)}, u32[]{:S(2)}, u32[]{:S(2)}) collective-permute-start(bf16[4,8192]{1,0:T(4,128)(2,1)S(1)} %bitcast.42), channel_id=1, source_target_pairs={{0,4},{1,5},{2,6},{3,7},{4,0},{5,1},{6,2},{7,3},{8,12},{9,13},{10,... | collective-permute-start | bytes 196616 | tf_op jit(solution)/shard_map/ppermute | solution.py:18
  67.8 2.4 %collective-permute-done.11 = bf16[4,8192]{1,0:T(4,128)(2,1)S(1)} collective-permute-done((bf16[4,8192]{1,0:T(4,128)(2,1)S(1)}, bf16[4,8192]{1,0:T(4,128)(2,1)S(1)}, u32[]{:S(2)}, u32[]{:S(2)}) %collective-permute-start.11) | collective-permute-done | bytes 65568 | tf_op jit(solution)/shard_map/ppermute | solution.py:18
  70.2 1.3 %collective-permute-done.10 = bf16[4,8192]{1,0:T(4,128)(2,1)S(1)} collective-permute-done((bf16[4,8192]{1,0:T(4,128)(2,1)S(1)}, bf16[4,8192]{1,0:T(4,128)(2,1)S(1)}, u32[]{:S(2)}, u32[]{:S(2)}) %collective-permute-start.10) | collective-permute-done | bytes 65568 | tf_op jit(solution)/shard_map/ppermute | solution.py:18
  71.5 0.7 collective-permute-start.14
  72.2 1.3 %collective-permute-start.13 = (bf16[4,8192]{1,0:T(4,128)(2,1)S(1)}, bf16[4,8192]{1,0:T(4,128)(2,1)S(1)}, u32[]{:S(2)}, u32[]{:S(2)}) collective-permute-start(bf16[4,8192]{1,0:T(4,128)(2,1)S(1)} %collective-permute-done.9), channel_id=1, source_target_pairs={{0,2},{1,3},{2,0},{3,1},{4,6},{5,7},{6,4},{7,5},{8,10},{9,11},{10,... | collective-permute-start | bytes 196616 | tf_op jit(solution)/shard_map/ppermute | solution.py:18
  73.8 1.1 collective-permute-done.15
  74.9 1.6 %collective-permute-done.14 = bf16[4,8192]{1,0:T(4,128)(2,1)S(1)} collective-permute-done((bf16[4,8192]{1,0:T(4,128)(2,1)S(1)}, bf16[4,8192]{1,0:T(4,128)(2,1)S(1)}, u32[]{:S(2)}, u32[]{:S(2)}) %collective-permute-start.14) | collective-permute-done | bytes 65568 | tf_op jit(solution)/shard_map/ppermute | solution.py:18
  76.5 0.8 collective-permute-done.13
  77.6 1.5 %collective-permute-done.17.refs_6_.refs_3_ = bf16[16,8192]{1,0:T(8,128)(2,1)S(1)} collective-permute-done((bf16[16,8192]{1,0:T(8,128)(2,1)S(1)}, bf16[16,8192]{1,0:T(8,128)(2,1)S(1)}, u32[]{:S(2)}, u32[]{:S(2)}) %collective-permute-start.17) | collective-permute-done | bytes 262176 | tf_op jit(solution)/shard_map/ppermute | solution.py:18
  79.1 0.5 down.3
  79.8 7.9 %all_to_all.25 = bf16[4,8,128]{2,1,0:T(8,128)(2,1)S(1)} all-to-all(bf16[4,8,128]{2,1,0:T(8,128)(2,1)S(1)} %down.3), channel_id=1, replica_groups={{0,4,8,12},{1,5,9,13},{2,6,10,14},{3,7,11,15},{16,20,24,28},{17,21,25,2..., dimensions={0} | all-to-all | bytes 16384 | tf_op jit(solution)/shard_map/all_to_all | solution.py:22
  87.7 0.6 broadcast_in_dim.16
  88.3 3.8 %all-to-all-start.3 = ((bf16[4,8,128]{2,1,0:T(8,128)(2,1)}), bf16[4,8,128]{2,1,0:T(8,128)(2,1)}, u32[]{:S(2)}, u32[]{:S(2)}) async-start(bf16[4,8,128]{2,1,0:T(8,128)(2,1)} %broadcast_in_dim.16), calls=%async_computation.3 | async-start | bytes 16384 | tf_op jit(solution)/shard_map/all_to_all | solution.py:22
  92.1 3.4 %copy-done.2 = bf16[8192,512]{1,0:T(8,128)(2,1)S(1)} copy-done((bf16[8192,512]{1,0:T(8,128)(2,1)S(1)}, bf16[8192,512]{1,0:T(8,128)(2,1)}, u32[]{:S(2)}) %copy-start.2) | copy-done | bytes 8388632
  95.5 0.9 copy-done.8
  96.5 0.9 copy-done.14
  97.4 0.9 copy-done.16
  98.4 2.7 %base.3.refs_5_ = f32[64,512]{1,0:T(8,128)S(1)} custom-call(bf16[16,8192]{1,0:T(8,128)(2,1)S(1)} %pad_maximum_fusion.2.refs_3_.refs_0_, bf16[16,8192]{1,0:T(8,128)(2,1)S(1)} %copy-done.8, bf16[16,8192]{1,0:T(8,128)(2,1)S(1)} %copy-done.14, bf16[16,8192]{1,0:T(8,128)(2,1)S(1)} %copy-done.16, bf16[8192,512]{1,0:T(8,128)(2,1)S(1)} %copy-done.2), custom_call_target="tpu_custom_call" | custom-call | flops 536870912 | bytes 8388608 | tf_op jit(solution)/shard_map/base/pallas_call | solution.py:291
  101.1 1.0 copy-done.20
  102.1 0.7 copy-done.22
  102.8 0.7 copy-done.26
  103.6 1.3 %lift.3 = bf16[16,4,512]{2,1,0:T(4,128)(2,1)S(1)} custom-call(bf16[4,8,128]{2,1,0:T(8,128)(2,1)} %all-to-all-done.3.refs_0_, bf16[64,128]{1,0:T(8,128)(2,1)S(1)} %copy-done.22, bf16[64,64]{1,0:T(8,128)(2,1)S(1)} %copy-done.26, bf16[64,64]{1,0:T(8,128)(2,1)S(1)} %get-tuple-element.11.refs_1_.refs_3_, bf16[32,16,512]{2,1,0:T(8,128)(2,1)S(1)} %copy-done.20, ...), custom_call_target="tpu_custom_call" | custom-call | tf_op jit(solution)/shard_map/lift/pallas_call | solution.py:309
  104.9 10.1 %all_to_all.26 = bf16[16,4,512]{2,1,0:T(4,128)(2,1)S(1)} all-to-all(bf16[16,4,512]{2,1,0:T(4,128)(2,1)S(1)} %lift.3), channel_id=1, replica_groups=mesh['groups'=2,'tensor'=16] {'tensor'}, dimensions={0} | all-to-all | bytes 131072 | tf_op jit(solution)/shard_map/all_to_all | solution.py:22
  115.0 0.6 copy.33
  (71 shorter events, 1.6 us)
Async XLA Ops:
  0.0 60.9 %copy-start = (bf16[4,8,384,128]{3,2,1,0:T(8,128)(2,1)S(1)}, bf16[4,8,384,128]{3,2,1,0:T(8,128)(2,1)}, u32[]{:S(2)}) copy-start(bf16[4,8,384,128]{3,2,1,0:T(8,128)(2,1)} %param.22) | copy-start | bytes 9437188
  0.0 1.0 copy-start.27
  1.0 0.7 copy-start.28
  1.7 0.7 copy-start.29
  3.2 7.7 %collective-permute-start.2 = (bf16[4,8320]{1,0:T(4,128)(2,1)S(1)}, bf16[4,8320]{1,0:T(4,128)(2,1)S(1)}, u32[]{:S(2)}, u32[]{:S(2)}) collective-permute-start(bf16[4,8320]{1,0:T(4,128)(2,1)S(1)} %norm.1), channel_id=1, source_target_pairs={{0,12},{1,13},{2,14},{3,15},{4,8},{5,9},{6,10},{7,11},{8,4},{9,5},... | collective-permute-start | bytes 199688 | tf_op jit(solution)/shard_map/ppermute | solution.py:18
  8.3 5.7 %collective-permute-start.1 = (bf16[4,8320]{1,0:T(4,128)(2,1)S(1)}, bf16[4,8320]{1,0:T(4,128)(2,1)S(1)}, u32[]{:S(2)}, u32[]{:S(2)}) collective-permute-start(bf16[4,8320]{1,0:T(4,128)(2,1)S(1)} %norm.1), channel_id=1, source_target_pairs={{0,8},{1,9},{2,10},{3,11},{4,12},{5,13},{6,14},{7,15},{8,0},{9,1},... | collective-permute-start | bytes 199688 | tf_op jit(solution)/shard_map/ppermute | solution.py:18
  8.3 7.2 %collective-permute-start = (bf16[4,8320]{1,0:T(4,128)(2,1)S(1)}, bf16[4,8320]{1,0:T(4,128)(2,1)S(1)}, u32[]{:S(2)}, u32[]{:S(2)}) collective-permute-start(bf16[4,8320]{1,0:T(4,128)(2,1)S(1)} %norm.1), channel_id=1, source_target_pairs={{0,4},{1,5},{2,6},{3,7},{4,0},{5,1},{6,2},{7,3},{8,12},{9,13},{10,... | collective-permute-start | bytes 199688 | tf_op jit(solution)/shard_map/ppermute | solution.py:18
  9.0 7.3 %collective-permute-start.3 = (bf16[4,8320]{1,0:T(4,128)(2,1)S(1)}, bf16[4,8320]{1,0:T(4,128)(2,1)S(1)}, u32[]{:S(2)}, u32[]{:S(2)}) collective-permute-start(bf16[4,8320]{1,0:T(4,128)(2,1)S(1)} %norm.1), channel_id=1, source_target_pairs={{0,2},{1,3},{2,0},{3,1},{4,6},{5,7},{6,4},{7,5},{8,10},{9,11},{10,... | collective-permute-start | bytes 199688 | tf_op jit(solution)/shard_map/ppermute | solution.py:18
  10.9 5.4 %collective-permute-start.6 = (bf16[4,8320]{1,0:T(4,128)(2,1)S(1)}, bf16[4,8320]{1,0:T(4,128)(2,1)S(1)}, u32[]{:S(2)}, u32[]{:S(2)}) collective-permute-start(bf16[4,8320]{1,0:T(4,128)(2,1)S(1)} %collective-permute-done.2), channel_id=1, source_target_pairs={{0,2},{1,3},{2,0},{3,1},{4,6},{5,7},{6,4},{7,5},{8,10},{9,11},{10,... | collective-permute-start | bytes 199688 | tf_op jit(solution)/shard_map/ppermute | solution.py:18
  14.0 4.9 %collective-permute-start.5 = (bf16[4,8320]{1,0:T(4,128)(2,1)S(1)}, bf16[4,8320]{1,0:T(4,128)(2,1)S(1)}, u32[]{:S(2)}, u32[]{:S(2)}) collective-permute-start(bf16[4,8320]{1,0:T(4,128)(2,1)S(1)} %collective-permute-done.1), channel_id=1, source_target_pairs={{0,2},{1,3},{2,0},{3,1},{4,6},{5,7},{6,4},{7,5},{8,10},{9,11},{10,... | collective-permute-start | bytes 199688 | tf_op jit(solution)/shard_map/ppermute | solution.py:18
  15.5 4.3 %collective-permute-start.4 = (bf16[4,8320]{1,0:T(4,128)(2,1)S(1)}, bf16[4,8320]{1,0:T(4,128)(2,1)S(1)}, u32[]{:S(2)}, u32[]{:S(2)}) collective-permute-start(bf16[4,8320]{1,0:T(4,128)(2,1)S(1)} %collective-permute-done), channel_id=1, source_target_pairs={{0,2},{1,3},{2,0},{3,1},{4,6},{5,7},{6,4},{7,5},{8,10},{9,11},{10,... | collective-permute-start | bytes 199688 | tf_op jit(solution)/shard_map/ppermute | solution.py:18
  16.2 6.4 %collective-permute-start.7 = (bf16[16,8320]{1,0:T(8,128)(2,1)S(1)}, bf16[16,8320]{1,0:T(8,128)(2,1)S(1)}, u32[]{:S(2)}, u32[]{:S(2)}) collective-permute-start(bf16[16,8320]{1,0:T(8,128)(2,1)S(1)} %pad_maximum_fusion.refs_3_.refs_0_), channel_id=1, source_target_pairs={{0,1},{1,0},{2,3},{3,2},{4,5},{5,4},{6,7},{7,6},{8,9},{9,8},{10,11... | collective-permute-start | bytes 798728 | tf_op jit(solution)/shard_map/ppermute | solution.py:18
  19.9 5.2 %copy-start.5 = (bf16[16,8320]{1,0:T(8,128)(2,1)}, bf16[16,8320]{1,0:T(8,128)(2,1)S(1)}, u32[]{:S(2)}) copy-start(bf16[16,8320]{1,0:T(8,128)(2,1)S(1)} %pad_maximum_fusion.1.refs_4_.refs_1_) | copy-start | bytes 798724
  19.9 2.6 %collective-permute-start.8 = (bf16[16,8320]{1,0:T(8,128)(2,1)S(1)}, bf16[16,8320]{1,0:T(8,128)(2,1)S(1)}, u32[]{:S(2)}, u32[]{:S(2)}) collective-permute-start(bf16[16,8320]{1,0:T(8,128)(2,1)S(1)} %pad_maximum_fusion.1.refs_4_.refs_1_), channel_id=1, source_target_pairs={{0,1},{1,0},{2,3},{3,2},{4,5},{5,4},{6,7},{7,6},{8,9},{9,8},{10,11... | collective-permute-start | bytes 798728 | tf_op jit(solution)/shard_map/ppermute | solution.py:18
  20.0 0.7 copy-start.30
  22.0 0.6 copy-start.24
  22.6 2.6 %copy-start.9 = (bf16[16,8320]{1,0:T(8,128)(2,1)}, bf16[16,8320]{1,0:T(8,128)(2,1)S(1)}, u32[]{:S(2)}) copy-start(bf16[16,8320]{1,0:T(8,128)(2,1)S(1)} %collective-permute-done.7.refs_5_.refs_2_) | copy-start | bytes 798724
  22.6 2.6 %copy-start.11 = (bf16[16,8320]{1,0:T(8,128)(2,1)}, bf16[16,8320]{1,0:T(8,128)(2,1)S(1)}, u32[]{:S(2)}) copy-start(bf16[16,8320]{1,0:T(8,128)(2,1)S(1)} %collective-permute-done.8.refs_6_.refs_3_) | copy-start | bytes 798724
  22.6 1.8 %copy-start.3 = (bf16[2,8192,64]{1,2,0:T(8,128)(2,1)S(1)}, bf16[2,8192,64]{1,2,0:T(8,128)(2,1)}, u32[]{:S(2)}) copy-start(bf16[2,8192,64]{1,2,0:T(8,128)(2,1)} %param.19) | copy-start | bytes 6291460
  25.2 0.6 copy-start.23
  25.8 53.3 %copy-start.21 = (bf16[64,128]{1,0:T(8,128)(2,1)}, bf16[64,128]{1,0:T(8,128)(2,1)S(1)}, u32[]{:S(2)}) copy-start(bf16[64,128]{1,0:T(8,128)(2,1)S(1)} %get-tuple-element.13.refs_1_.refs_7_) | copy-start | bytes 49156
  25.8 17.3 %all-to-all-start = ((bf16[16,24,128]{2,1,0:T(8,128)(2,1)}), bf16[16,24,128]{2,1,0:T(8,128)(2,1)S(1)}, u32[]{:S(2)}, u32[]{:S(2)}) async-start(bf16[16,24,128]{2,1,0:T(8,128)(2,1)} %copy-done.23), calls=%async_computation | async-start | bytes 196608 | tf_op jit(solution)/shard_map/all_to_all | solution.py:22
  30.1 4.0 %copy-start.1 = (bf16[8192,640]{1,0:T(8,128)(2,1)S(1)}, bf16[8192,640]{1,0:T(8,128)(2,1)}, u32[]{:S(2)}) copy-start(bf16[8192,640]{1,0:T(8,128)(2,1)} %refs_4_.4) | copy-start | bytes 31457284
  34.1 1.0 copy-start.6
  35.1 1.0 copy-start.10
  36.0 1.0 copy-start.12
  42.4 0.7 copy-start.18
  43.1 1.1 copy-start.17
  44.2 0.9 copy-start.19
  45.1 0.7 copy-start.25
  47.1 13.5 %all-to-all-start.1 = ((bf16[16,4,640]{2,1,0:T(4,128)(2,1)}), bf16[16,4,640]{2,1,0:T(4,128)(2,1)S(1)}, u32[]{:S(2)}, u32[]{:S(2)}) async-start(bf16[16,4,640]{2,1,0:T(4,128)(2,1)} %lift.2), calls=%async_computation.1 | async-start | bytes 163840 | tf_op jit(solution)/shard_map/all_to_all | solution.py:22
  60.7 1.9 %copy-start.31 = (bf16[4,8,384,128]{3,2,1,0:T(8,128)(2,1)S(1)}, bf16[4,8,384,128]{3,2,1,0:T(8,128)(2,1)}, u32[]{:S(2)}) copy-start(bf16[4,8,384,128]{3,2,1,0:T(8,128)(2,1)} %param.23) | copy-start | bytes 9437188
  62.1 16.9 %copy-start.4 = (bf16[2,8192,64]{1,2,0:T(8,128)(2,1)S(1)}, bf16[2,8192,64]{1,2,0:T(8,128)(2,1)}, u32[]{:S(2)}) copy-start(bf16[2,8192,64]{1,2,0:T(8,128)(2,1)} %param.19) | copy-start | bytes 6291460
  63.4 6.8 %collective-permute-start.11 = (bf16[4,8192]{1,0:T(4,128)(2,1)S(1)}, bf16[4,8192]{1,0:T(4,128)(2,1)S(1)}, u32[]{:S(2)}, u32[]{:S(2)}) collective-permute-start(bf16[4,8192]{1,0:T(4,128)(2,1)S(1)} %bitcast.40), channel_id=1, source_target_pairs={{0,12},{1,13},{2,14},{3,15},{4,8},{5,9},{6,10},{7,11},{8,4},{9,5},... | collective-permute-start | bytes 196616 | tf_op jit(solution)/shard_map/ppermute | solution.py:18
  64.0 7.5 %collective-permute-start.10 = (bf16[4,8192]{1,0:T(4,128)(2,1)S(1)}, bf16[4,8192]{1,0:T(4,128)(2,1)S(1)}, u32[]{:S(2)}, u32[]{:S(2)}) collective-permute-start(bf16[4,8192]{1,0:T(4,128)(2,1)S(1)} %bitcast.41), channel_id=1, source_target_pairs={{0,8},{1,9},{2,10},{3,11},{4,12},{5,13},{6,14},{7,15},{8,0},{9,1},... | collective-permute-start | bytes 196616 | tf_op jit(solution)/shard_map/ppermute | solution.py:18
  64.8 7.4 %collective-permute-start.9 = (bf16[4,8192]{1,0:T(4,128)(2,1)S(1)}, bf16[4,8192]{1,0:T(4,128)(2,1)S(1)}, u32[]{:S(2)}, u32[]{:S(2)}) collective-permute-start(bf16[4,8192]{1,0:T(4,128)(2,1)S(1)} %bitcast.42), channel_id=1, source_target_pairs={{0,4},{1,5},{2,6},{3,7},{4,0},{5,1},{6,2},{7,3},{8,12},{9,13},{10,... | collective-permute-start | bytes 196616 | tf_op jit(solution)/shard_map/ppermute | solution.py:18
  67.8 6.0 %collective-permute-start.12 = (bf16[4,8192]{1,0:T(4,128)(2,1)S(1)}, bf16[4,8192]{1,0:T(4,128)(2,1)S(1)}, u32[]{:S(2)}, u32[]{:S(2)}) collective-permute-start(bf16[4,8192]{1,0:T(4,128)(2,1)S(1)} %bitcast.43), channel_id=1, source_target_pairs={{0,2},{1,3},{2,0},{3,1},{4,6},{5,7},{6,4},{7,5},{8,10},{9,11},{10,... | collective-permute-start | bytes 196616 | tf_op jit(solution)/shard_map/ppermute | solution.py:18
  70.2 4.7 %collective-permute-start.15 = (bf16[4,8192]{1,0:T(4,128)(2,1)S(1)}, bf16[4,8192]{1,0:T(4,128)(2,1)S(1)}, u32[]{:S(2)}, u32[]{:S(2)}) collective-permute-start(bf16[4,8192]{1,0:T(4,128)(2,1)S(1)} %collective-permute-done.11), channel_id=1, source_target_pairs={{0,2},{1,3},{2,0},{3,1},{4,6},{5,7},{6,4},{7,5},{8,10},{9,11},{10,... | collective-permute-start | bytes 196616 | tf_op jit(solution)/shard_map/ppermute | solution.py:18
  71.5 5.0 %collective-permute-start.14 = (bf16[4,8192]{1,0:T(4,128)(2,1)S(1)}, bf16[4,8192]{1,0:T(4,128)(2,1)S(1)}, u32[]{:S(2)}, u32[]{:S(2)}) collective-permute-start(bf16[4,8192]{1,0:T(4,128)(2,1)S(1)} %collective-permute-done.10), channel_id=1, source_target_pairs={{0,2},{1,3},{2,0},{3,1},{4,6},{5,7},{6,4},{7,5},{8,10},{9,11},{10,... | collective-permute-start | bytes 196616 | tf_op jit(solution)/shard_map/ppermute | solution.py:18
  72.2 5.0 %collective-permute-start.13 = (bf16[4,8192]{1,0:T(4,128)(2,1)S(1)}, bf16[4,8192]{1,0:T(4,128)(2,1)S(1)}, u32[]{:S(2)}, u32[]{:S(2)}) collective-permute-start(bf16[4,8192]{1,0:T(4,128)(2,1)S(1)} %collective-permute-done.9), channel_id=1, source_target_pairs={{0,2},{1,3},{2,0},{3,1},{4,6},{5,7},{6,4},{7,5},{8,10},{9,11},{10,... | collective-permute-start | bytes 196616 | tf_op jit(solution)/shard_map/ppermute | solution.py:18
  73.7 3.8 %collective-permute-start.16 = (bf16[16,8192]{1,0:T(8,128)(2,1)S(1)}, bf16[16,8192]{1,0:T(8,128)(2,1)S(1)}, u32[]{:S(2)}, u32[]{:S(2)}) collective-permute-start(bf16[16,8192]{1,0:T(8,128)(2,1)S(1)} %pad_maximum_fusion.2.refs_3_.refs_0_), channel_id=1, source_target_pairs={{0,1},{1,0},{2,3},{3,2},{4,5},{5,4},{6,7},{7,6},{8,9},{9,8},{10,11... | collective-permute-start | bytes 786440 | tf_op jit(solution)/shard_map/ppermute | solution.py:18
  77.4 2.1 %copy-start.7 = (bf16[16,8192]{1,0:T(8,128)(2,1)}, bf16[16,8192]{1,0:T(8,128)(2,1)S(1)}, u32[]{:S(2)}) copy-start(bf16[16,8192]{1,0:T(8,128)(2,1)S(1)} %pad_maximum_fusion.3.refs_4_.refs_1_) | copy-start | bytes 786436
  77.5 1.6 %collective-permute-start.17 = (bf16[16,8192]{1,0:T(8,128)(2,1)S(1)}, bf16[16,8192]{1,0:T(8,128)(2,1)S(1)}, u32[]{:S(2)}, u32[]{:S(2)}) collective-permute-start(bf16[16,8192]{1,0:T(8,128)(2,1)S(1)} %pad_maximum_fusion.3.refs_4_.refs_1_), channel_id=1, source_target_pairs={{0,1},{1,0},{2,3},{3,2},{4,5},{5,4},{6,7},{7,6},{8,9},{9,8},{10,11... | collective-permute-start | bytes 786440 | tf_op jit(solution)/shard_map/ppermute | solution.py:18
  77.5 2.0 %copy-start.13 = (bf16[16,8192]{1,0:T(8,128)(2,1)}, bf16[16,8192]{1,0:T(8,128)(2,1)S(1)}, u32[]{:S(2)}) copy-start(bf16[16,8192]{1,0:T(8,128)(2,1)S(1)} %collective-permute-done.16.refs_5_.refs_2_) | copy-start | bytes 786436
  79.1 0.7 copy-start.15
  88.3 12.8 %all-to-all-start.3 = ((bf16[4,8,128]{2,1,0:T(8,128)(2,1)}), bf16[4,8,128]{2,1,0:T(8,128)(2,1)}, u32[]{:S(2)}, u32[]{:S(2)}) async-start(bf16[4,8,128]{2,1,0:T(8,128)(2,1)} %broadcast_in_dim.16), calls=%async_computation.3 | async-start | bytes 16384 | tf_op jit(solution)/shard_map/all_to_all | solution.py:22
  92.1 3.4 %copy-start.2 = (bf16[8192,512]{1,0:T(8,128)(2,1)S(1)}, bf16[8192,512]{1,0:T(8,128)(2,1)}, u32[]{:S(2)}) copy-start(bf16[8192,512]{1,0:T(8,128)(2,1)} %refs_4_.6) | copy-start | bytes 25165828
  95.5 0.9 copy-start.8
  96.5 0.9 copy-start.14
  97.4 0.9 copy-start.16
  101.1 1.0 copy-start.20
  102.1 0.7 copy-start.22
  102.8 0.7 copy-start.26

commit v4 on v3

v4 whole, which is shorter than its diff:
```python
import functools

import jax
import jax.numpy as jnp
from jax import lax
from jax.experimental import pallas as pl
from jax.experimental.pallas import tpu as pltpu
from jax.sharding import PartitionSpec as P

eps = 1e-05
AXIS = "tensor"
LANES = 128
VMEM = pltpu.VMEM
SMEM = pltpu.SMEM


def swap(x, count, offset):
    return lax.ppermute(x, AXIS, [(i, i ^ offset) for i in range(count)])


def exchange(x, groups=None):
    return lax.all_to_all(
        x, AXIS, split_axis=0, concat_axis=0, axis_index_groups=groups, tiled=True
    )


def gather_rows(x, count):
    step = count // 4
    far, middle, near = (swap(x, count, k * step) for k in (3, 2, 1))
    step //= 2
    held = [jnp.concatenate([x, near, middle, far], axis=0)]
    across = [swap(p, count, step) for p in (x, far, near, middle)]
    held.append(jnp.concatenate([across[i] for i in (0, 2, 3, 1)], axis=0))
    step //= 2
    while step > 1:
        held = held + [swap(h, count, step) for h in held]
        step //= 2
    return held, held + [swap(h, count, 1) for h in held]


def place_of(row, me, count, rows):
    block = row // rows
    source = (block % 4) * (count // 4)
    piece, step = block // 4, count // 8
    while step:
        source = source + (piece % 2) * step
        piece, step = piece // 2, step // 2
    return (source ^ me) * rows + row % rows


def limit(total, room):
    if not room:
        return 60 * 1024 * 1024
    return (16 if total <= 64 else 60) * 1024 * 1024


def spec(space=VMEM):
    return pl.BlockSpec(memory_space=space)


def iota(shape, dim):
    return lax.broadcasted_iota(jnp.int32, shape, dim)


def one_hot(condition):
    return jnp.where(condition, 1.0, 0.0).astype(jnp.bfloat16)


def norm_kernel(
    hidden_hbm, gain_hbm, names_hbm, slots_hbm, out_ref, hidden_ref, gain_ref, names_ref, slots_ref, sems
):
    copies = [
        pltpu.make_async_copy(source, target, sems.at[i])
        for i, (source, target) in enumerate(
            (
                (hidden_hbm, hidden_ref),
                (gain_hbm, gain_ref),
                (names_hbm, names_ref),
                (slots_hbm, slots_ref),
            )
        )
    ]
    for copy in copies:
        copy.start()
    for copy in copies:
        copy.wait()
    rows, width = hidden_ref.shape
    hidden = hidden_ref[...].astype(jnp.float32)
    power = jnp.sum(hidden * hidden, axis=1, keepdims=True) / width
    gain = gain_ref[...].reshape(1, width).astype(jnp.float32)
    out_ref[:, :width] = (hidden * lax.rsqrt(power + eps) * gain).astype(jnp.bfloat16)
    row, lane = iota((rows, LANES), 0), iota((rows, LANES), 1)
    tags = jnp.zeros((rows, LANES), jnp.float32)
    for r in range(rows):
        name = names_ref[r]
        tag = jnp.where(lane < LANES // 2, name, slots_ref[name]).astype(jnp.float32)
        tags = jnp.where(row == r, tag, tags)
    out_ref[:, width:] = tags.astype(jnp.bfloat16)


NT = (((1,), (1,)), ((), ()))


def down_kernel(count, rows, pieces, *refs):
    map_refs, piece_refs = refs[:2], refs[2 : 2 + pieces]
    tag_refs, out_ref = refs[2 + pieces : 2 + 2 * pieces], refs[2 + 2 * pieces]
    me = lax.axis_index(AXIS)
    held, rank, width = map_refs[0].shape
    total, half = count * rows, count * rows // 2
    chunk = 1024
    sums = jnp.zeros((2 * held * rank, half), jnp.float32)
    for k in range(0, width, chunk):
        x = jnp.concatenate([p[:, k : k + chunk] for p in piece_refs], axis=0)
        maps = jnp.concatenate(
            [m[:, :, k : k + chunk].reshape(held * rank, chunk) for m in map_refs], axis=0
        )
        sums = sums + lax.dot_general(maps, x, NT, preferred_element_type=jnp.float32)
    tags = jnp.concatenate([t[...] for t in tag_refs], axis=0)
    pick = one_hot(iota((16, LANES), 1) == LANES // 2)
    slots = lax.dot_general(pick, tags, NT, preferred_element_type=jnp.float32)[:1]
    chosen = jnp.zeros((rank, half), jnp.float32)
    for m in range(2):
        for s in range(held):
            slot = ((me ^ m) * held + s).astype(jnp.float32)
            at = (m * held + s) * rank
            chosen = jnp.where(slots == slot, sums[at : at + rank], chosen)
    row, column = iota((half, total), 0), iota((half, total), 1)
    back = one_hot(place_of(row, me, count, rows) == column)
    placed = jnp.dot(chosen.astype(jnp.bfloat16), back, preferred_element_type=jnp.float32)
    folds = out_ref.shape[2] // total
    part = rank // folds
    folded = [placed[f * part : (f + 1) * part] for f in range(folds)]
    value = jnp.concatenate(folded, axis=1).astype(jnp.bfloat16)
    for d in range(count):
        out_ref[d] = value


def base_kernel(pieces, *refs):
    weight_ref, _, out_ref = refs[pieces:]
    x = jnp.concatenate([p[...] for p in refs[:pieces]], axis=0)
    total, depth = x.shape
    columns = weight_ref.shape[1]
    whole = columns // 256 * 256
    terms = []
    if whole:
        terms.append(jnp.dot(x, weight_ref[:, :whole], preferred_element_type=jnp.float32))
    if columns - whole == 128:
        half = depth // 2
        left = jnp.concatenate([x[:, :half], x[:, half:]], axis=0)
        right = jnp.concatenate(
            [weight_ref[:half, whole:], weight_ref[half:, whole:]], axis=1
        )
        both = jnp.dot(left, right, preferred_element_type=jnp.float32)
        terms.append(both[:total, :128] + both[total:, 128:])
    elif columns > whole:
        terms.append(jnp.dot(x, weight_ref[:, whole:], preferred_element_type=jnp.float32))
    term = terms[0] if len(terms) == 1 else jnp.concatenate(terms, axis=1)

    @pl.when(pl.program_id(0) == 0)
    def _():
        out_ref[...] = term

    @pl.when(pl.program_id(0) > 0)
    def _():
        out_ref[...] += term


def lift_kernel(count, rows, pieces, bounds, rank, *refs):
    tag_refs, refs = refs[:pieces], refs[pieces:]
    down_ref, up_ref, base_ref, out_ref, sum_ref = refs
    total = count * rows
    me = lax.axis_index(AXIS)
    adapters, per, columns = up_ref.shape
    wide = adapters * per
    row, column = iota((total, total), 0), iota((total, total), 1)
    order = one_hot(place_of(column, me, count, rows) == row)
    back = one_hot(place_of(row, me, count, rows) == column)
    folded = down_ref[0].astype(jnp.float32)
    for d in range(1, count):
        folded = folded + down_ref[d].astype(jnp.float32)
    folds = folded.shape[1] // total
    down = jnp.concatenate([folded[:, f * total : (f + 1) * total] for f in range(folds)], axis=0)
    down = lax.dot_general(
        back, down.astype(jnp.bfloat16), NT, preferred_element_type=jnp.float32
    ).astype(jnp.bfloat16)
    names = jnp.concatenate([t[...] for t in tag_refs], axis=0).astype(jnp.float32)[:, :1]
    named = (iota((total, wide), 1) // per).astype(jnp.float32) == names
    start = me * columns
    sum_ref[...] = base_ref[...]
    for g in range(rank // per):
        low, high = bounds[g], bounds[g + 1]

        @pl.when((start < high) & (start + columns > low))
        def _():
            at = iota((rank, wide), 1) % per + g * per
            spread = one_hot(at == iota((rank, wide), 0))
            copies = jnp.dot(down, spread, preferred_element_type=jnp.float32)
            chosen = jnp.where(named, copies, 0.0).astype(jnp.bfloat16)
            up = up_ref[...].reshape(wide, columns)
            lifted = jnp.dot(chosen, up, preferred_element_type=jnp.float32)
            at = iota((total, columns), 1) + start
            sum_ref[...] += jnp.where((at >= low) & (at < high), lifted, 0.0)

    placed = jnp.dot(
        order, sum_ref[...].astype(jnp.bfloat16), preferred_element_type=jnp.float32
    ).astype(jnp.bfloat16)
    for d in range(count):
        out_ref[d] = placed[d * rows : (d + 1) * rows]


def local(
    input_hidden,
    input_norm_gain,
    request_adapter,
    adapter_storage,
    lengths,
    projection_weight,
    output_weight,
    adapter_down,
    projection_up_adapter,
    output_up_adapter,
    cache_keys,
    cache_values,
    *,
    count,
):
    rows, width = input_hidden.shape
    rank = projection_up_adapter.shape[1]
    held = adapter_down.shape[0]
    kv_heads, context, head_dim = cache_keys.shape[1:]
    kv_width = kv_heads * head_dim
    total = rows * count
    bf16, f32 = jnp.bfloat16, jnp.float32
    roomy = pltpu.CompilerParams(vmem_limit_bytes=limit(total, True))
    full = pltpu.CompilerParams(vmem_limit_bytes=limit(total, False))
    own_maps = jnp.swapaxes(adapter_down, 1, 2)
    sibling_maps = jnp.swapaxes(swap(adapter_down, count, 1), 1, 2)

    normed = pl.pallas_call(
        norm_kernel,
        out_shape=jax.ShapeDtypeStruct((rows, width + LANES), bf16),
        in_specs=[spec(pltpu.HBM)] * 4,
        out_specs=spec(),
        scratch_shapes=[
            VMEM((rows, width), bf16),
            VMEM((width,), bf16),
            SMEM((rows,), jnp.int32),
            SMEM(adapter_storage.shape, jnp.int32),
            pltpu.SemaphoreType.DMA((4,)),
        ],
        compiler_params=full,
        cost_estimate=pl.CostEstimate(flops=0, bytes_accessed=1 << 24, transcendentals=0),
        name="norm",
    )(input_hidden, input_norm_gain, request_adapter.reshape(rows), adapter_storage)

    def tag_specs(pieces):
        return [pl.BlockSpec((p.shape[0], LANES), lambda i: (0, width // LANES)) for p in pieces]

    def downs(pieces, tagged, low, high):
        ranks = high - low
        lanes = max(LANES, total)
        down_spec = pl.BlockSpec((held, ranks, width), lambda i: (0, low // ranks, 0))
        return pl.pallas_call(
            functools.partial(down_kernel, count, rows, len(pieces)),
            grid=(1,),
            out_shape=jax.ShapeDtypeStruct((count, ranks * total // lanes, lanes), bf16),
            in_specs=[down_spec] * 2
            + [pl.BlockSpec((p.shape[0], width), lambda i: (0, 0)) for p in pieces]
            + tag_specs(tagged),
            out_specs=spec(),
            compiler_params=roomy,
            cost_estimate=pl.CostEstimate(
                flops=2 * total * width * held * ranks,
                bytes_accessed=2 * width * (2 * held * ranks + total),
                transcendentals=0,
            ),
            name="down",
        )(own_maps, sibling_maps, *pieces, *tagged)

    def base(pieces, weight, after):
        columns = weight.shape[1]
        chunk = 1024
        return pl.pallas_call(
            functools.partial(base_kernel, len(pieces)),
            grid=(width // chunk,),
            out_shape=jax.ShapeDtypeStruct((total, columns), f32),
            in_specs=[pl.BlockSpec((p.shape[0], chunk), lambda i: (0, i)) for p in pieces]
            + [pl.BlockSpec((chunk, columns), lambda i: (i, 0)), spec(pl.ANY)],
            out_specs=pl.BlockSpec((total, columns), lambda i: (0, 0)),
            compiler_params=full,
            cost_estimate=pl.CostEstimate(
                flops=2 * total * width * columns,
                bytes_accessed=2 * width * columns,
                transcendentals=0,
            ),
            name="base",
        )(*pieces, weight, after)

    def lift(down, tagged, up, base_term, bounds, ranks):
        columns = up.shape[2]
        whole = lambda x: pl.BlockSpec(x.shape, lambda i: (0,) * x.ndim)
        return pl.pallas_call(
            functools.partial(lift_kernel, count, rows, len(tagged), bounds, ranks),
            grid=(1,),
            out_shape=jax.ShapeDtypeStruct((count, rows, columns), bf16),
            in_specs=tag_specs(tagged) + [whole(down), whole(up), whole(base_term)],
            out_specs=pl.BlockSpec((count, rows, columns), lambda i: (0, 0, 0)),
            scratch_shapes=[VMEM((total, columns), f32)],
            compiler_params=full,
            name="lift",
        )(*tagged, down, up, base_term)

    def project(x, tagged, low, high, weight, up, bounds):
        column, pieces = gather_rows(x, count)
        tagged = pieces if tagged is None else tagged
        mine = downs(column, tagged[: len(column)], low, high)
        down = exchange(mine)
        base_term = base(pieces, weight, mine)
        columns = lift(down, tagged, up, base_term, bounds, high - low)
        mine = exchange(columns)
        return jnp.swapaxes(mine, 0, 1).reshape(rows, -1), tagged

    bounds = (0, width, width + kv_width, width + 2 * kv_width)
    qkv_mine, tagged = project(
        normed, None, 0, 3 * rank, projection_weight, projection_up_adapter, bounds
    )

    groups_per = width // head_dim // kv_heads
    query = qkv_mine[:, 0:width].reshape(rows, kv_heads, groups_per, head_dim)
    key_new = qkv_mine[:, width : width + kv_width].reshape(rows, kv_heads, head_dim)
    value_new = qkv_mine[:, width + kv_width :].reshape(rows, kv_heads, head_dim)
    scale = head_dim ** (-0.5)
    scores = (
        jnp.einsum("bhgd,bhpd->bhgp", query, cache_keys, preferred_element_type=jnp.float32) * scale
    )
    live = jnp.arange(context, dtype=jnp.int32)[None, :] < lengths[:, None]
    scores = jnp.where(live[:, None, None, :], scores, -1e30)
    own = jnp.einsum("bhgd,bhd->bhg", query, key_new, preferred_element_type=jnp.float32) * scale
    peak = jnp.maximum(jnp.max(scores, axis=3), own)
    weights = jnp.exp(scores - peak[..., None])
    own_weight = jnp.exp(own - peak)
    denominator = jnp.sum(weights, axis=3) + own_weight
    probs = (weights / denominator[..., None]).astype(jnp.bfloat16)
    own_prob = (own_weight / denominator).astype(jnp.bfloat16)
    mixed = jnp.einsum("bhgp,bhpd->bhgd", probs, cache_values, preferred_element_type=jnp.float32)
    mixed = (
        mixed
        + own_prob.astype(jnp.float32)[..., None] * value_new.astype(jnp.float32)[:, :, None, :]
    )
    attended = mixed.reshape(rows, width).astype(jnp.bfloat16)

    output, _ = project(
        attended, tagged, 3 * rank, 4 * rank, output_weight, output_up_adapter, (0, width)
    )
    return output


def solution(mesh):
    count = mesh.shape[AXIS]

    def body(*arrays):
        return local(*arrays, count=count)

    return jax.shard_map(
        body,
        mesh=mesh,
        in_specs=(
            P(("groups", "tensor"), None),
            P(),
            P(("groups", "tensor"), None),
            P(),
            P(("groups", "tensor")),
            P(None, "tensor"),
            P(None, "tensor"),
            P("tensor", None, None),
            P(None, None, "tensor"),
            P(None, None, "tensor"),
            P(("groups", "tensor"), None, None, None),
            P(("groups", "tensor"), None, None, None),
        ),
        out_specs=P(("groups", "tensor"), None),
        check_vma=False,
    )
```

time: 117 us -> 103 us (0.88)
  local copies, waits for them, and re-layouts: 26.7 us -> 5.12 us
  Pallas kernels: 14.1 us -> 28.3 us
  blocking collectives: 18 us -> 12.9 us
  other arithmetic: 1.64 us -> 3.28 us
  waiting for transfers between devices: 20.1 us -> 18.6 us
    unnamed x68 -> x28, local copies, waits for them, and re-layouts: 26.1 us -> 5.11 us
    pallas_call x2, Pallas kernels: 8.13 us -> 16.4 us  [base(): pl.pallas_call(functools.partial(base_kernel, len(pieces)), grid=(width /...]
    all_to_all x2 -> x1, blocking collectives: 18 us -> 12.9 us  [exchange(): lax.all_to_all(x, AXIS, split_axis=0, concat_axis=0, axis_index_groups=gr...]
    pallas_call x5 -> x4, Pallas kernels: 5.12 us -> 10.1 us  [the longest x2 5.17 us: downs(): pl.pallas_call(functools.partial(down_kernel, count, rows, len(pieces)),...]
    ppermute x18 -> x19, waiting for transfers between devices: 13.7 us -> 11.6 us  [swap(): return lax.ppermute(x, AXIS, [(i, i ^ offset) for i in range(count)])]
    concatenate x2, other arithmetic: 0.32 us -> 1.74 us  [gather_rows(): held.append(jnp.concatenate([across[i] for i in (0, 2, 3, 1)], axis=0))]
    ppermute x18 -> x19, starting transfers between devices: 18 us -> 17.9 us  [swap(): return lax.ppermute(x, AXIS, [(i, i ^ offset) for i in range(count)])]
  transfers between devices with their start and end apart: 21 -> 22, of which waited for: 11 -> 10; matrix products, arithmetic and copies ran while one was open for 1% -> 3% of each run, Pallas kernels for 8% -> 21%
where the time goes in v4:
time: 103 us
  starting transfers between devices  32.1 us (31%)
  Pallas kernels  28.3 us (27%)
  waiting for transfers between devices  18.6 us (18%)
  blocking collectives  12.9 us (13%)
  local copies, waits for them, and re-layouts  5.12 us (5%)
  other arithmetic  3.28 us (3%)
  matrix products  2.12 us (2%)
    ppermute x19, starting transfers between devices, swap(): return lax.ppermute(x, AXIS, [(i, i ^ offset) for i in range(count)])  17.9 us
    pallas_call x2, Pallas kernels, base(): pl.pallas_call(functools.partial(base_kernel, len(pieces)), grid=(width /...  16.4 us
    all_to_all x3, starting transfers between devices, exchange(): lax.all_to_all(x, AXIS, split_axis=0, concat_axis=0, axis_index_groups=gr...  14.2 us
    all_to_all x1, blocking collectives, exchange(): lax.all_to_all(x, AXIS, split_axis=0, concat_axis=0, axis_index_groups=gr...  12.9 us
    ppermute x19, waiting for transfers between devices, swap(): return lax.ppermute(x, AXIS, [(i, i ^ offset) for i in range(count)])  11.6 us
    all_to_all x3, waiting for transfers between devices, exchange(): lax.all_to_all(x, AXIS, split_axis=0, concat_axis=0, axis_index_groups=gr...  7.07 us
    pallas_call x2, Pallas kernels, downs(): pl.pallas_call(functools.partial(down_kernel, count, rows, len(pieces)),...  5.17 us
    unnamed x28, local copies, waits for them, and re-layouts  5.11 us
  transfers between devices with their start and end apart: 22, of which 10 were waited for; matrix products, arithmetic and copies ran while one was open for 3% of the time, Pallas kernels for 21%

profile of v4, /device:TPU:0, one launch (start us, length us, event | category | flops | bytes accessed | tf_op | source)
XLA Modules:
  0.0 102.6 jit_solution(17682799256101729573)
XLA Ops:
  0.0 1.8 %norm.1 = bf16[4,8320]{1,0:T(4,128)(2,1)} custom-call(bf16[4,8192]{1,0:T(4,128)(2,1)} %hidden_hbm.1, bf16[8192]{0:T(1024)(128)(2,1)} %gain_hbm.1, s32[4]{0:T(128)} %bitcast.50, s32[32]{0:T(128)} %slots_hbm.1), custom_call_target="tpu_custom_call" | custom-call | bytes 16777216 | tf_op jit(solution)/shard_map/norm/pallas_call | solution.py:239
  1.9 5.1 %collective-permute-start.2 = (bf16[4,8320]{1,0:T(4,128)(2,1)}, bf16[4,8320]{1,0:T(4,128)(2,1)S(1)}, u32[]{:S(2)}, u32[]{:S(2)}) collective-permute-start(bf16[4,8320]{1,0:T(4,128)(2,1)} %norm.1), channel_id=1, source_target_pairs={{0,12},{1,13},{2,14},{3,15},{4,8},{5,9},{6,10},{7,11},{8,4},{9,5},... | collective-permute-start | bytes 199688 | tf_op jit(solution)/shard_map/ppermute | solution.py:18
  7.0 0.0 collective-permute-start.1
  7.0 0.6 collective-permute-start
  7.6 1.6 %collective-permute-start.3 = (bf16[4,8320]{1,0:T(4,128)(2,1)}, bf16[4,8320]{1,0:T(4,128)(2,1)S(1)}, u32[]{:S(2)}, u32[]{:S(2)}) collective-permute-start(bf16[4,8320]{1,0:T(4,128)(2,1)} %norm.1), channel_id=1, source_target_pairs={{0,2},{1,3},{2,0},{3,1},{4,6},{5,7},{6,4},{7,5},{8,10},{9,11},{10,... | collective-permute-start | bytes 199688 | tf_op jit(solution)/shard_map/ppermute | solution.py:18
  9.3 0.0 collective-permute-start.9
  9.3 0.6 collective-permute-done.2
  9.8 1.8 %collective-permute-start.6 = (bf16[4,8320]{1,0:T(4,128)(2,1)S(1)}, bf16[4,8320]{1,0:T(4,128)(2,1)S(1)}, u32[]{:S(2)}, u32[]{:S(2)}) collective-permute-start(bf16[4,8320]{1,0:T(4,128)(2,1)S(1)} %collective-permute-done.2), channel_id=1, source_target_pairs={{0,2},{1,3},{2,0},{3,1},{4,6},{5,7},{6,4},{7,5},{8,10},{9,11},{10,... | collective-permute-start | bytes 199688 | tf_op jit(solution)/shard_map/ppermute | solution.py:18
  11.6 1.2 %collective-permute-done.1 = bf16[4,8320]{1,0:T(4,128)(2,1)S(1)} collective-permute-done((bf16[4,8320]{1,0:T(4,128)(2,1)}, bf16[4,8320]{1,0:T(4,128)(2,1)S(1)}, u32[]{:S(2)}, u32[]{:S(2)}) %collective-permute-start.1) | collective-permute-done | bytes 66592 | tf_op jit(solution)/shard_map/ppermute | solution.py:18
  12.9 1.5 %collective-permute-start.5 = (bf16[4,8320]{1,0:T(4,128)(2,1)S(1)}, bf16[4,8320]{1,0:T(4,128)(2,1)S(1)}, u32[]{:S(2)}, u32[]{:S(2)}) collective-permute-start(bf16[4,8320]{1,0:T(4,128)(2,1)S(1)} %collective-permute-done.1), channel_id=1, source_target_pairs={{0,2},{1,3},{2,0},{3,1},{4,6},{5,7},{6,4},{7,5},{8,10},{9,11},{10,... | collective-permute-start | bytes 199688 | tf_op jit(solution)/shard_map/ppermute | solution.py:18
  14.4 0.0 collective-permute-done
  14.4 0.5 collective-permute-start.4
  14.9 1.0 %pad_maximum_fusion.refs_2_.refs_4_.refs_0_ = bf16[16,8320]{1,0:T(8,128)(2,1)S(1)} fusion(bf16[4,8320]{1,0:T(4,128)(2,1)S(1)} %collective-permute-done.2, bf16[4,8320]{1,0:T(4,128)(2,1)S(1)} %collective-permute-done.1, bf16[4,8320]{1,0:T(4,128)(2,1)S(1)} %collective-permute-done, bf16[4,8320]{1,0:T(4,128)(2,1)} %norm.1), kind=kLoop, calls=%fused_computation.8 | loop fusion | flops 1064960 | bytes 532480 | tf_op jit(solution)/shard_map/concatenate | solution.py:31
  15.9 0.0 collective-permute-done.3
  16.0 0.1 collective-permute-start.7
  16.0 0.0 collective-permute-done.6
  16.0 1.7 %collective-permute-done.5 = bf16[4,8320]{1,0:T(4,128)(2,1)S(1)} collective-permute-done((bf16[4,8320]{1,0:T(4,128)(2,1)S(1)}, bf16[4,8320]{1,0:T(4,128)(2,1)S(1)}, u32[]{:S(2)}, u32[]{:S(2)}) %collective-permute-start.5) | collective-permute-done | bytes 66592 | tf_op jit(solution)/shard_map/ppermute | solution.py:18
  17.7 0.9 collective-permute-done.4
  18.6 0.9 pad_maximum_fusion.1.refs_3_.refs_5_.refs_1_
  19.5 0.0 collective-permute-start.8
  19.5 1.6 %copy-done.3 = bf16[2,8192,64]{1,2,0:T(8,128)(2,1)S(1)} copy-done((bf16[2,8192,64]{1,2,0:T(8,128)(2,1)S(1)}, bf16[2,8192,64]{1,2,0:T(8,128)(2,1)}, u32[]{:S(2)}) %copy-start.3) | copy-done | bytes 2097176
  21.1 2.9 %down.2.refs_5_ = bf16[16,24,128]{2,1,0:T(8,128)(2,1)} custom-call(bf16[2,64,8192]{2,1,0:T(8,128)(2,1)S(1)} %bitcast.35, bf16[2,64,8192]{2,1,0:T(8,128)(2,1)S(1)} %bitcast.37, bf16[16,8320]{1,0:T(8,128)(2,1)S(1)} %pad_maximum_fusion.refs_2_.refs_4_.refs_0_, bf16[16,8320]{1,0:T(8,128)(2,1)} %pad_maximum_fusion.1.refs_3_.refs_5_.refs_1_, ...), custom_call_target="tpu_custom_call" | custom-call | flops 100663296 | bytes 4194304 | tf_op jit(solution)/shard_map/down/pallas_call | solution.py:263
  24.1 1.3 %copy-done.5 = bf16[2,8192,64]{1,2,0:T(8,128)(2,1)} copy-done((bf16[2,8192,64]{1,2,0:T(8,128)(2,1)}, bf16[2,8192,64]{1,2,0:T(8,128)(2,1)S(1)}, u32[]{:S(2)}) %copy-start.5) | copy-done | bytes 2097176
  25.4 4.4 %all-to-all-start = ((bf16[16,24,128]{2,1,0:T(8,128)(2,1)}), bf16[16,24,128]{2,1,0:T(8,128)(2,1)S(1)}, u32[]{:S(2)}, u32[]{:S(2)}) async-start(bf16[16,24,128]{2,1,0:T(8,128)(2,1)} %down.2.refs_5_), calls=%async_computation | async-start | bytes 196608 | tf_op jit(solution)/shard_map/all_to_all | solution.py:22
  29.8 0.0 copy-start.11
  29.8 8.6 %base.2.refs_6_ = f32[64,640]{1,0:T(8,128)} custom-call(bf16[16,8320]{1,0:T(8,128)(2,1)} %copy-done.1, bf16[16,8320]{1,0:T(8,128)(2,1)} %pad_maximum_fusion.1.refs_3_.refs_5_.refs_1_, bf16[16,8320]{1,0:T(8,128)(2,1)} %collective-permute-done.7.refs_2_, bf16[16,8320]{1,0:T(8,128)(2,1)} %collective-permute-done.8.refs_3_, bf16[8192,640]{1,0:T(8,128)(2,1)} %refs_4_.2, ...), custom_call_target="tpu_custom_call" | custom-call | flops 671088640 | bytes 10485760 | tf_op jit(solution)/shard_map/base/pallas_call | solution.py:283
  38.4 0.6 copy-done.9
  39.1 2.5 %lift.2 = bf16[16,4,640]{2,1,0:T(4,128)(2,1)} custom-call(bf16[16,8320]{1,0:T(8,128)(2,1)} %copy-done.1, bf16[16,8320]{1,0:T(8,128)(2,1)} %pad_maximum_fusion.1.refs_3_.refs_5_.refs_1_, bf16[16,8320]{1,0:T(8,128)(2,1)} %collective-permute-done.7.refs_2_, bf16[16,8320]{1,0:T(8,128)(2,1)} %collective-permute-done.8.refs_3_, bf16[16,24,128]{2,1,0:T(8,128)(2,1)} %copy-done.9, ...), custom_call_target="tpu_custom_call" | custom-call | tf_op jit(solution)/shard_map/lift/pallas_call | solution.py:302
  41.6 6.3 %all-to-all-start.1 = ((bf16[16,4,640]{2,1,0:T(4,128)(2,1)}), bf16[16,4,640]{2,1,0:T(4,128)(2,1)S(1)}, u32[]{:S(2)}, u32[]{:S(2)}) async-start(bf16[16,4,640]{2,1,0:T(4,128)(2,1)} %lift.2), calls=%async_computation.1 | async-start | bytes 163840 | tf_op jit(solution)/shard_map/all_to_all | solution.py:22
  47.9 0.1 iota_compare_fusion
  48.0 7.1 %all-to-all-done.1 = bf16[16,4,640]{2,1,0:T(4,128)(2,1)S(1)} async-done(((bf16[16,4,640]{2,1,0:T(4,128)(2,1)}), bf16[16,4,640]{2,1,0:T(4,128)(2,1)S(1)}, u32[]{:S(2)}, u32[]{:S(2)}) %all-to-all-start.1) | async-done | bytes 81952 | tf_op jit(solution)/shard_map/all_to_all | solution.py:22
  55.1 0.0 copy-start.8
  55.1 0.1 fusion.6
  55.3 0.0 copy-done
  55.3 1.3 %fusion.13 = (f32[4,8,8]{2,1,0:T(8,128)S(1)}, f32[4,8,8,384]{3,2,1,0:T(8,128)S(1)}) fusion(bf16[4,8,384,128]{3,2,1,0:T(8,128)(2,1)S(1)} %copy-done, bf16[1,4,64,128]{3,1,2,0:T(4,128)(2,1)S(1)} %slice_bitcast_fusion, pred[4,384]{1,0:T(4,128)(4,1)S(1)} %iota_compare_fusion), kind=kOutput, calls=%fused_computation.29 | convolution fusion | flops 25460480 | bytes 3607040 | tf_op jit(solution)/shard_map/bhgd,bhpd->bhgp/dot_general | solution.py:334
  56.6 0.2 fusion.3
  56.8 0.2 copy-done.8
  57.0 0.7 fusion.2
  57.7 0.1 copy.30
  57.8 0.7 collective-permute-start.12
  58.5 0.8 collective-permute-start.11
  59.3 3.0 %collective-permute-start.10 = (bf16[4,8192]{1,0:T(4,128)(2,1)S(1)}, bf16[4,8192]{1,0:T(4,128)(2,1)S(1)}, u32[]{:S(2)}, u32[]{:S(2)}) collective-permute-start(bf16[4,8192]{1,0:T(4,128)(2,1)S(1)} %bitcast.44), channel_id=1, source_target_pairs={{0,4},{1,5},{2,6},{3,7},{4,0},{5,1},{6,2},{7,3},{8,12},{9,13},{10,... | collective-permute-start | bytes 196616 | tf_op jit(solution)/shard_map/ppermute | solution.py:18
  62.2 0.0 collective-permute-start.13
  62.2 2.4 %collective-permute-done.12 = bf16[4,8192]{1,0:T(4,128)(2,1)S(1)} collective-permute-done((bf16[4,8192]{1,0:T(4,128)(2,1)S(1)}, bf16[4,8192]{1,0:T(4,128)(2,1)S(1)}, u32[]{:S(2)}, u32[]{:S(2)}) %collective-permute-start.12) | collective-permute-done | bytes 65568 | tf_op jit(solution)/shard_map/ppermute | solution.py:18
  64.6 1.3 %collective-permute-done.11 = bf16[4,8192]{1,0:T(4,128)(2,1)S(1)} collective-permute-done((bf16[4,8192]{1,0:T(4,128)(2,1)S(1)}, bf16[4,8192]{1,0:T(4,128)(2,1)S(1)}, u32[]{:S(2)}, u32[]{:S(2)}) %collective-permute-start.11) | collective-permute-done | bytes 65568 | tf_op jit(solution)/shard_map/ppermute | solution.py:18
  65.9 0.7 collective-permute-start.15
  66.7 0.0 collective-permute-done.10
  66.7 1.3 %collective-permute-start.14 = (bf16[4,8192]{1,0:T(4,128)(2,1)S(1)}, bf16[4,8192]{1,0:T(4,128)(2,1)S(1)}, u32[]{:S(2)}, u32[]{:S(2)}) collective-permute-start(bf16[4,8192]{1,0:T(4,128)(2,1)S(1)} %collective-permute-done.10), channel_id=1, source_target_pairs={{0,2},{1,3},{2,0},{3,1},{4,6},{5,7},{6,4},{7,5},{8,10},{9,11},{10,... | collective-permute-start | bytes 196616 | tf_op jit(solution)/shard_map/ppermute | solution.py:18
  68.0 0.2 pad_maximum_fusion.2.refs_2_.refs_0_
  68.1 0.1 collective-permute-start.17
  68.2 0.0 collective-permute-done.13
  68.2 1.1 %collective-permute-done.16 = bf16[4,8192]{1,0:T(4,128)(2,1)S(1)} collective-permute-done((bf16[4,8192]{1,0:T(4,128)(2,1)S(1)}, bf16[4,8192]{1,0:T(4,128)(2,1)S(1)}, u32[]{:S(2)}, u32[]{:S(2)}) %collective-permute-start.16) | collective-permute-done | bytes 65568 | tf_op jit(solution)/shard_map/ppermute | solution.py:18
  69.3 1.6 %collective-permute-done.15 = bf16[4,8192]{1,0:T(4,128)(2,1)S(1)} collective-permute-done((bf16[4,8192]{1,0:T(4,128)(2,1)S(1)}, bf16[4,8192]{1,0:T(4,128)(2,1)S(1)}, u32[]{:S(2)}, u32[]{:S(2)}) %collective-permute-start.15) | collective-permute-done | bytes 65568 | tf_op jit(solution)/shard_map/ppermute | solution.py:18
  70.9 0.8 collective-permute-done.14
  71.7 0.9 pad_maximum_fusion.3.refs_3_.refs_1_
  72.6 2.2 %down.3.refs_5_ = bf16[16,8,128]{2,1,0:T(8,128)(2,1)} custom-call(bf16[2,64,8192]{2,1,0:T(8,128)(2,1)S(1)} %bitcast.36, bf16[2,64,8192]{2,1,0:T(8,128)(2,1)S(1)} %bitcast.38, bf16[16,8192]{1,0:T(8,128)(2,1)S(1)} %pad_maximum_fusion.2.refs_2_.refs_0_, bf16[16,8192]{1,0:T(8,128)(2,1)} %pad_maximum_fusion.3.refs_3_.refs_1_, bf16[16,8320]{1,0:T(8,128)(2,1)S(1)} %copy-done.2, ...), custom_call_target="tpu_custom_call" | custom-call | flops 33554432 | bytes 2097152 | tf_op jit(solution)/shard_map/down/pallas_call | solution.py:263
  74.8 3.5 %all-to-all-start.2 = ((bf16[16,8,128]{2,1,0:T(8,128)(2,1)}), bf16[16,8,128]{2,1,0:T(8,128)(2,1)S(1)}, u32[]{:S(2)}, u32[]{:S(2)}) async-start(bf16[16,8,128]{2,1,0:T(8,128)(2,1)} %down.3.refs_5_), calls=%async_computation.2 | async-start | bytes 65536 | tf_op jit(solution)/shard_map/all_to_all | solution.py:22
  78.3 0.0 collective-permute-done.17.refs_2_
  78.4 7.8 %base.3.refs_6_ = f32[64,512]{1,0:T(8,128)} custom-call(bf16[16,8192]{1,0:T(8,128)(2,1)} %copy-done.7, bf16[16,8192]{1,0:T(8,128)(2,1)} %pad_maximum_fusion.3.refs_3_.refs_1_, bf16[16,8192]{1,0:T(8,128)(2,1)} %collective-permute-done.17.refs_2_, bf16[16,8192]{1,0:T(8,128)(2,1)} %collective-permute-done.18.refs_3_, bf16[8192,512]{1,0:T(8,128)(2,1)} %refs_4_.3, ...), custom_call_target="tpu_custom_call" | custom-call | flops 536870912 | bytes 8388608 | tf_op jit(solution)/shard_map/base/pallas_call | solution.py:283
  86.1 0.0 all-to-all-done.2.refs_4_
  86.1 0.6 copy-done.10
  86.7 2.4 %lift.3 = bf16[16,4,512]{2,1,0:T(4,128)(2,1)} custom-call(bf16[16,8320]{1,0:T(8,128)(2,1)} %copy-done.1, bf16[16,8320]{1,0:T(8,128)(2,1)} %pad_maximum_fusion.1.refs_3_.refs_5_.refs_1_, bf16[16,8320]{1,0:T(8,128)(2,1)} %collective-permute-done.7.refs_2_, bf16[16,8320]{1,0:T(8,128)(2,1)} %collective-permute-done.8.refs_3_, bf16[16,8,128]{2,1,0:T(8,128)(2,1)} %copy-done.10, ...), custom_call_target="tpu_custom_call" | custom-call | tf_op jit(solution)/shard_map/lift/pallas_call | solution.py:302
  89.1 12.9 %all_to_all.20 = bf16[16,4,512]{2,1,0:T(4,128)(2,1)S(1)} all-to-all(bf16[16,4,512]{2,1,0:T(4,128)(2,1)} %lift.3), channel_id=1, replica_groups=mesh['groups'=2,'tensor'=16] {'tensor'}, dimensions={0} | all-to-all | bytes 131072 | tf_op jit(solution)/shard_map/all_to_all | solution.py:22
  102.0 0.6 copy.33
  (29 shorter events, 0.1 us)
Async XLA Ops:
  0.0 55.3 %copy-start = (bf16[4,8,384,128]{3,2,1,0:T(8,128)(2,1)S(1)}, bf16[4,8,384,128]{3,2,1,0:T(8,128)(2,1)}, u32[]{:S(2)}) copy-start(bf16[4,8,384,128]{3,2,1,0:T(8,128)(2,1)} %param.22) | copy-start | bytes 9437188
  1.9 8.0 %collective-permute-start.2 = (bf16[4,8320]{1,0:T(4,128)(2,1)}, bf16[4,8320]{1,0:T(4,128)(2,1)S(1)}, u32[]{:S(2)}, u32[]{:S(2)}) collective-permute-start(bf16[4,8320]{1,0:T(4,128)(2,1)} %norm.1), channel_id=1, source_target_pairs={{0,12},{1,13},{2,14},{3,15},{4,8},{5,9},{6,10},{7,11},{8,4},{9,5},... | collective-permute-start | bytes 199688 | tf_op jit(solution)/shard_map/ppermute | solution.py:18
  7.0 5.9 %collective-permute-start.1 = (bf16[4,8320]{1,0:T(4,128)(2,1)}, bf16[4,8320]{1,0:T(4,128)(2,1)S(1)}, u32[]{:S(2)}, u32[]{:S(2)}) collective-permute-start(bf16[4,8320]{1,0:T(4,128)(2,1)} %norm.1), channel_id=1, source_target_pairs={{0,8},{1,9},{2,10},{3,11},{4,12},{5,13},{6,14},{7,15},{8,0},{9,1},... | collective-permute-start | bytes 199688 | tf_op jit(solution)/shard_map/ppermute | solution.py:18
  7.0 7.4 %collective-permute-start = (bf16[4,8320]{1,0:T(4,128)(2,1)}, bf16[4,8320]{1,0:T(4,128)(2,1)S(1)}, u32[]{:S(2)}, u32[]{:S(2)}) collective-permute-start(bf16[4,8320]{1,0:T(4,128)(2,1)} %norm.1), channel_id=1, source_target_pairs={{0,4},{1,5},{2,6},{3,7},{4,0},{5,1},{6,2},{7,3},{8,12},{9,13},{10,... | collective-permute-start | bytes 199688 | tf_op jit(solution)/shard_map/ppermute | solution.py:18
  7.6 8.3 %collective-permute-start.3 = (bf16[4,8320]{1,0:T(4,128)(2,1)}, bf16[4,8320]{1,0:T(4,128)(2,1)S(1)}, u32[]{:S(2)}, u32[]{:S(2)}) collective-permute-start(bf16[4,8320]{1,0:T(4,128)(2,1)} %norm.1), channel_id=1, source_target_pairs={{0,2},{1,3},{2,0},{3,1},{4,6},{5,7},{6,4},{7,5},{8,10},{9,11},{10,... | collective-permute-start | bytes 199688 | tf_op jit(solution)/shard_map/ppermute | solution.py:18
  9.3 10.3 %collective-permute-start.9 = (bf16[2,8192,64]{1,2,0:T(8,128)(2,1)}, bf16[2,8192,64]{1,2,0:T(8,128)(2,1)S(1)}, u32[]{:S(2)}, u32[]{:S(2)}) collective-permute-start(bf16[2,8192,64]{1,2,0:T(8,128)(2,1)} %param.19), channel_id=1, source_target_pairs={{0,1},{1,0},{2,3},{3,2},{4,5},{5,4},{6,7},{7,6},{8,9},{9,8},{10,11... | collective-permute-start | bytes 6291464 | tf_op jit(solution)/shard_map/ppermute | solution.py:18
  9.8 6.2 %collective-permute-start.6 = (bf16[4,8320]{1,0:T(4,128)(2,1)S(1)}, bf16[4,8320]{1,0:T(4,128)(2,1)S(1)}, u32[]{:S(2)}, u32[]{:S(2)}) collective-permute-start(bf16[4,8320]{1,0:T(4,128)(2,1)S(1)} %collective-permute-done.2), channel_id=1, source_target_pairs={{0,2},{1,3},{2,0},{3,1},{4,6},{5,7},{6,4},{7,5},{8,10},{9,11},{10,... | collective-permute-start | bytes 199688 | tf_op jit(solution)/shard_map/ppermute | solution.py:18
  12.9 4.9 %collective-permute-start.5 = (bf16[4,8320]{1,0:T(4,128)(2,1)S(1)}, bf16[4,8320]{1,0:T(4,128)(2,1)S(1)}, u32[]{:S(2)}, u32[]{:S(2)}) collective-permute-start(bf16[4,8320]{1,0:T(4,128)(2,1)S(1)} %collective-permute-done.1), channel_id=1, source_target_pairs={{0,2},{1,3},{2,0},{3,1},{4,6},{5,7},{6,4},{7,5},{8,10},{9,11},{10,... | collective-permute-start | bytes 199688 | tf_op jit(solution)/shard_map/ppermute | solution.py:18
  14.4 4.3 %collective-permute-start.4 = (bf16[4,8320]{1,0:T(4,128)(2,1)S(1)}, bf16[4,8320]{1,0:T(4,128)(2,1)S(1)}, u32[]{:S(2)}, u32[]{:S(2)}) collective-permute-start(bf16[4,8320]{1,0:T(4,128)(2,1)S(1)} %collective-permute-done), channel_id=1, source_target_pairs={{0,2},{1,3},{2,0},{3,1},{4,6},{5,7},{6,4},{7,5},{8,10},{9,11},{10,... | collective-permute-start | bytes 199688 | tf_op jit(solution)/shard_map/ppermute | solution.py:18
  15.9 13.9 %copy-start.1 = (bf16[16,8320]{1,0:T(8,128)(2,1)}, bf16[16,8320]{1,0:T(8,128)(2,1)S(1)}, u32[]{:S(2)}) copy-start(bf16[16,8320]{1,0:T(8,128)(2,1)S(1)} %pad_maximum_fusion.refs_2_.refs_4_.refs_0_) | copy-start | bytes 798724
  16.0 13.8 %collective-permute-start.7 = (bf16[16,8320]{1,0:T(8,128)(2,1)S(1)}, bf16[16,8320]{1,0:T(8,128)(2,1)}, u32[]{:S(2)}, u32[]{:S(2)}) collective-permute-start(bf16[16,8320]{1,0:T(8,128)(2,1)S(1)} %pad_maximum_fusion.refs_2_.refs_4_.refs_0_), channel_id=1, source_target_pairs={{0,1},{1,0},{2,3},{3,2},{4,5},{5,4},{6,7},{7,6},{8,9},{9,8},{10,11... | collective-permute-start | bytes 798728 | tf_op jit(solution)/shard_map/ppermute | solution.py:18
  19.5 10.3 %collective-permute-start.8 = (bf16[16,8320]{1,0:T(8,128)(2,1)}, bf16[16,8320]{1,0:T(8,128)(2,1)}, u32[]{:S(2)}, u32[]{:S(2)}) collective-permute-start(bf16[16,8320]{1,0:T(8,128)(2,1)} %pad_maximum_fusion.1.refs_3_.refs_5_.refs_1_), channel_id=1, source_target_pairs={{0,1},{1,0},{2,3},{3,2},{4,5},{5,4},{6,7},{7,6},{8,9},{9,8},{10,11... | collective-permute-start | bytes 798728 | tf_op jit(solution)/shard_map/ppermute | solution.py:18
  19.5 1.6 %copy-start.3 = (bf16[2,8192,64]{1,2,0:T(8,128)(2,1)S(1)}, bf16[2,8192,64]{1,2,0:T(8,128)(2,1)}, u32[]{:S(2)}) copy-start(bf16[2,8192,64]{1,2,0:T(8,128)(2,1)} %param.19) | copy-start | bytes 6291460
  24.1 1.4 %copy-start.5 = (bf16[2,8192,64]{1,2,0:T(8,128)(2,1)}, bf16[2,8192,64]{1,2,0:T(8,128)(2,1)S(1)}, u32[]{:S(2)}) copy-start(bf16[2,8192,64]{1,2,0:T(8,128)(2,1)S(1)} %collective-permute-done.9) | copy-start | bytes 6291460
  25.4 13.0 %all-to-all-start = ((bf16[16,24,128]{2,1,0:T(8,128)(2,1)}), bf16[16,24,128]{2,1,0:T(8,128)(2,1)S(1)}, u32[]{:S(2)}, u32[]{:S(2)}) async-start(bf16[16,24,128]{2,1,0:T(8,128)(2,1)} %down.2.refs_5_), calls=%async_computation | async-start | bytes 196608 | tf_op jit(solution)/shard_map/all_to_all | solution.py:22
  29.8 18.1 %copy-start.11 = (s32[4]{0:T(128)S(1)}, s32[4]{0:T(128)}, u32[]{:S(2)}) copy-start(s32[4]{0:T(128)} %param.16) | copy-start | bytes 52
  38.4 0.6 copy-start.9
  41.6 13.5 %all-to-all-start.1 = ((bf16[16,4,640]{2,1,0:T(4,128)(2,1)}), bf16[16,4,640]{2,1,0:T(4,128)(2,1)S(1)}, u32[]{:S(2)}, u32[]{:S(2)}) async-start(bf16[16,4,640]{2,1,0:T(4,128)(2,1)} %lift.2), calls=%async_computation.1 | async-start | bytes 163840 | tf_op jit(solution)/shard_map/all_to_all | solution.py:22
  55.1 1.9 %copy-start.8 = (bf16[4,8,384,128]{3,2,1,0:T(8,128)(2,1)S(1)}, bf16[4,8,384,128]{3,2,1,0:T(8,128)(2,1)}, u32[]{:S(2)}) copy-start(bf16[4,8,384,128]{3,2,1,0:T(8,128)(2,1)} %param.23) | copy-start | bytes 9437188
  56.5 16.0 %copy-start.2 = (bf16[16,8320]{1,0:T(8,128)(2,1)S(1)}, bf16[16,8320]{1,0:T(8,128)(2,1)}, u32[]{:S(2)}) copy-start(bf16[16,8320]{1,0:T(8,128)(2,1)} %copy-done.1) | copy-start | bytes 798724
  56.5 16.0 %copy-start.4 = (bf16[2,8192,64]{1,2,0:T(8,128)(2,1)S(1)}, bf16[2,8192,64]{1,2,0:T(8,128)(2,1)}, u32[]{:S(2)}) copy-start(bf16[2,8192,64]{1,2,0:T(8,128)(2,1)} %param.19) | copy-start | bytes 6291460
  56.6 16.0 %copy-start.6 = (bf16[2,8192,64]{1,2,0:T(8,128)(2,1)S(1)}, bf16[2,8192,64]{1,2,0:T(8,128)(2,1)}, u32[]{:S(2)}) copy-start(bf16[2,8192,64]{1,2,0:T(8,128)(2,1)} %copy-done.5) | copy-start | bytes 6291460
  57.8 6.8 %collective-permute-start.12 = (bf16[4,8192]{1,0:T(4,128)(2,1)S(1)}, bf16[4,8192]{1,0:T(4,128)(2,1)S(1)}, u32[]{:S(2)}, u32[]{:S(2)}) collective-permute-start(bf16[4,8192]{1,0:T(4,128)(2,1)S(1)} %bitcast.42), channel_id=1, source_target_pairs={{0,12},{1,13},{2,14},{3,15},{4,8},{5,9},{6,10},{7,11},{8,4},{9,5},... | collective-permute-start | bytes 196616 | tf_op jit(solution)/shard_map/ppermute | solution.py:18
  58.5 7.5 %collective-permute-start.11 = (bf16[4,8192]{1,0:T(4,128)(2,1)S(1)}, bf16[4,8192]{1,0:T(4,128)(2,1)S(1)}, u32[]{:S(2)}, u32[]{:S(2)}) collective-permute-start(bf16[4,8192]{1,0:T(4,128)(2,1)S(1)} %bitcast.43), channel_id=1, source_target_pairs={{0,8},{1,9},{2,10},{3,11},{4,12},{5,13},{6,14},{7,15},{8,0},{9,1},... | collective-permute-start | bytes 196616 | tf_op jit(solution)/shard_map/ppermute | solution.py:18
  59.3 7.4 %collective-permute-start.10 = (bf16[4,8192]{1,0:T(4,128)(2,1)S(1)}, bf16[4,8192]{1,0:T(4,128)(2,1)S(1)}, u32[]{:S(2)}, u32[]{:S(2)}) collective-permute-start(bf16[4,8192]{1,0:T(4,128)(2,1)S(1)} %bitcast.44), channel_id=1, source_target_pairs={{0,4},{1,5},{2,6},{3,7},{4,0},{5,1},{6,2},{7,3},{8,12},{9,13},{10,... | collective-permute-start | bytes 196616 | tf_op jit(solution)/shard_map/ppermute | solution.py:18
  62.2 6.0 %collective-permute-start.13 = (bf16[4,8192]{1,0:T(4,128)(2,1)S(1)}, bf16[4,8192]{1,0:T(4,128)(2,1)S(1)}, u32[]{:S(2)}, u32[]{:S(2)}) collective-permute-start(bf16[4,8192]{1,0:T(4,128)(2,1)S(1)} %bitcast.45), channel_id=1, source_target_pairs={{0,2},{1,3},{2,0},{3,1},{4,6},{5,7},{6,4},{7,5},{8,10},{9,11},{10,... | collective-permute-start | bytes 196616 | tf_op jit(solution)/shard_map/ppermute | solution.py:18
  64.6 4.7 %collective-permute-start.16 = (bf16[4,8192]{1,0:T(4,128)(2,1)S(1)}, bf16[4,8192]{1,0:T(4,128)(2,1)S(1)}, u32[]{:S(2)}, u32[]{:S(2)}) collective-permute-start(bf16[4,8192]{1,0:T(4,128)(2,1)S(1)} %collective-permute-done.12), channel_id=1, source_target_pairs={{0,2},{1,3},{2,0},{3,1},{4,6},{5,7},{6,4},{7,5},{8,10},{9,11},{10,... | collective-permute-start | bytes 196616 | tf_op jit(solution)/shard_map/ppermute | solution.py:18
  65.9 5.0 %collective-permute-start.15 = (bf16[4,8192]{1,0:T(4,128)(2,1)S(1)}, bf16[4,8192]{1,0:T(4,128)(2,1)S(1)}, u32[]{:S(2)}, u32[]{:S(2)}) collective-permute-start(bf16[4,8192]{1,0:T(4,128)(2,1)S(1)} %collective-permute-done.11), channel_id=1, source_target_pairs={{0,2},{1,3},{2,0},{3,1},{4,6},{5,7},{6,4},{7,5},{8,10},{9,11},{10,... | collective-permute-start | bytes 196616 | tf_op jit(solution)/shard_map/ppermute | solution.py:18
  66.7 5.0 %collective-permute-start.14 = (bf16[4,8192]{1,0:T(4,128)(2,1)S(1)}, bf16[4,8192]{1,0:T(4,128)(2,1)S(1)}, u32[]{:S(2)}, u32[]{:S(2)}) collective-permute-start(bf16[4,8192]{1,0:T(4,128)(2,1)S(1)} %collective-permute-done.10), channel_id=1, source_target_pairs={{0,2},{1,3},{2,0},{3,1},{4,6},{5,7},{6,4},{7,5},{8,10},{9,11},{10,... | collective-permute-start | bytes 196616 | tf_op jit(solution)/shard_map/ppermute | solution.py:18
  68.1 10.2 %copy-start.7 = (bf16[16,8192]{1,0:T(8,128)(2,1)}, bf16[16,8192]{1,0:T(8,128)(2,1)S(1)}, u32[]{:S(2)}) copy-start(bf16[16,8192]{1,0:T(8,128)(2,1)S(1)} %pad_maximum_fusion.2.refs_2_.refs_0_) | copy-start | bytes 786436
  68.1 10.2 %collective-permute-start.17 = (bf16[16,8192]{1,0:T(8,128)(2,1)S(1)}, bf16[16,8192]{1,0:T(8,128)(2,1)}, u32[]{:S(2)}, u32[]{:S(2)}) collective-permute-start(bf16[16,8192]{1,0:T(8,128)(2,1)S(1)} %pad_maximum_fusion.2.refs_2_.refs_0_), channel_id=1, source_target_pairs={{0,1},{1,0},{2,3},{3,2},{4,5},{5,4},{6,7},{7,6},{8,9},{9,8},{10,11... | collective-permute-start | bytes 786440 | tf_op jit(solution)/shard_map/ppermute | solution.py:18
  72.6 5.8 %collective-permute-start.18 = (bf16[16,8192]{1,0:T(8,128)(2,1)}, bf16[16,8192]{1,0:T(8,128)(2,1)}, u32[]{:S(2)}, u32[]{:S(2)}) collective-permute-start(bf16[16,8192]{1,0:T(8,128)(2,1)} %pad_maximum_fusion.3.refs_3_.refs_1_), channel_id=1, source_target_pairs={{0,1},{1,0},{2,3},{3,2},{4,5},{5,4},{6,7},{7,6},{8,9},{9,8},{10,11... | collective-permute-start | bytes 786440 | tf_op jit(solution)/shard_map/ppermute | solution.py:18
  74.8 11.3 %all-to-all-start.2 = ((bf16[16,8,128]{2,1,0:T(8,128)(2,1)}), bf16[16,8,128]{2,1,0:T(8,128)(2,1)S(1)}, u32[]{:S(2)}, u32[]{:S(2)}) async-start(bf16[16,8,128]{2,1,0:T(8,128)(2,1)} %down.3.refs_5_), calls=%async_computation.2 | async-start | bytes 65536 | tf_op jit(solution)/shard_map/all_to_all | solution.py:22
  86.1 0.6 copy-start.10

commit v5 on v4

--- a/solution.py
+++ b/solution.py
@@ -22,6 +22,21 @@
     return lax.all_to_all(
         x, AXIS, split_axis=0, concat_axis=0, axis_index_groups=groups, tiled=True
     )
+
+
+def sum_over(x, count, beside):
+    step, turn, terms = count, 0, []
+    while step > 1:
+        radix = 4 if step % 4 == 0 else 2
+        step //= radix
+        others = [swap(x, count, k * step) for k in range(1, radix)]
+        terms.append(beside(turn, x))
+        for other in others:
+            x = x + other
+        if terms[-1] is not None:
+            x, terms[-1] = lax.optimization_barrier((x, terms[-1]))
+        turn += 1
+    return x, [t for t in terms if t is not None]
 
 
 def gather_rows(x, count):
@@ -48,10 +63,8 @@
     return (source ^ me) * rows + row % rows
 
 
-def limit(total, room):
-    if not room:
-        return 60 * 1024 * 1024
-    return (16 if total <= 64 else 60) * 1024 * 1024
+def limit(total, megabytes):
+    return (megabytes if total <= 64 else 60) * 1024 * 1024
 
 
 def spec(space=VMEM):
@@ -101,19 +114,30 @@
 NT = (((1,), (1,)), ((), ()))
 
 
-def down_kernel(count, rows, pieces, *refs):
-    map_refs, piece_refs = refs[:2], refs[2 : 2 + pieces]
-    tag_refs, out_ref = refs[2 + pieces : 2 + 2 * pieces], refs[2 + 2 * pieces]
+def down_kernel(count, rows, pieces, low, *refs):
+    maps_hbm, piece_refs = refs[:2], refs[2 : 2 + pieces]
+    tag_refs, (out_ref, maps_ref, sems) = refs[2 + pieces : 2 + 2 * pieces], refs[2 + 2 * pieces :]
     me = lax.axis_index(AXIS)
-    held, rank, width = map_refs[0].shape
+    _, held, rank, width = maps_ref.shape
     total, half = count * rows, count * rows // 2
-    chunk = 1024
+    chunk = 2048
+    copies = []
+    for k in range(0, width, chunk):
+        for m in range(2):
+            copies.append(
+                pltpu.make_async_copy(
+                    maps_hbm[m].at[:, low : low + rank, k : k + chunk],
+                    maps_ref.at[m, :, :, k : k + chunk],
+                    sems.at[len(copies)],
+                )
+            )
+            copies[-1].start()
     sums = jnp.zeros((2 * held * rank, half), jnp.float32)
     for k in range(0, width, chunk):
+        for m in range(2):
+            copies[k // chunk * 2 + m].wait()
         x = jnp.concatenate([p[:, k : k + chunk] for p in piece_refs], axis=0)
-        maps = jnp.concatenate(
-            [m[:, :, k : k + chunk].reshape(held * rank, chunk) for m in map_refs], axis=0
-        )
+        maps = maps_ref[:, :, :, k : k + chunk].reshape(2 * held * rank, chunk)
         sums = sums + lax.dot_general(maps, x, NT, preferred_element_type=jnp.float32)
     tags = jnp.concatenate([t[...] for t in tag_refs], axis=0)
     pick = one_hot(iota((16, LANES), 1) == LANES // 2)
@@ -127,47 +151,58 @@
     row, column = iota((half, total), 0), iota((half, total), 1)
     back = one_hot(place_of(row, me, count, rows) == column)
     placed = jnp.dot(chosen.astype(jnp.bfloat16), back, preferred_element_type=jnp.float32)
-    folds = out_ref.shape[2] // total
+    folds = out_ref.shape[1] // total
     part = rank // folds
     folded = [placed[f * part : (f + 1) * part] for f in range(folds)]
     value = jnp.concatenate(folded, axis=1).astype(jnp.bfloat16)
-    for d in range(count):
-        out_ref[d] = value
-
-
-def base_kernel(pieces, *refs):
-    weight_ref, _, out_ref = refs[pieces:]
-    x = jnp.concatenate([p[...] for p in refs[:pieces]], axis=0)
-    total, depth = x.shape
-    columns = weight_ref.shape[1]
+    out_ref[...] = value
+
+
+def base_kernel(pieces, part, *refs):
+    weight_hbm, _, out_ref, weight_ref, sems = refs[pieces:]
+    total, columns = out_ref.shape
     whole = columns // 256 * 256
-    terms = []
-    if whole:
-        terms.append(jnp.dot(x, weight_ref[:, :whole], preferred_element_type=jnp.float32))
-    if columns - whole == 128:
-        half = depth // 2
-        left = jnp.concatenate([x[:, :half], x[:, half:]], axis=0)
-        right = jnp.concatenate(
-            [weight_ref[:half, whole:], weight_ref[half:, whole:]], axis=1
+    depth = weight_ref.shape[0]
+    chunk = 1024
+    copies = [
+        pltpu.make_async_copy(
+            weight_hbm.at[part * depth + k : part * depth + k + chunk],
+            weight_ref.at[k : k + chunk],
+            sems.at[k // chunk],
         )
-        both = jnp.dot(left, right, preferred_element_type=jnp.float32)
-        terms.append(both[:total, :128] + both[total:, 128:])
-    elif columns > whole:
-        terms.append(jnp.dot(x, weight_ref[:, whole:], preferred_element_type=jnp.float32))
-    term = terms[0] if len(terms) == 1 else jnp.concatenate(terms, axis=1)
-
-    @pl.when(pl.program_id(0) == 0)
-    def _():
-        out_ref[...] = term
-
-    @pl.when(pl.program_id(0) > 0)
-    def _():
-        out_ref[...] += term
+        for k in range(0, depth, chunk)
+    ]
+    for copy in copies:
+        copy.start()
+    for k in range(0, depth, chunk):
+        at = part * depth + k
+        x = jnp.concatenate([p[:, at : at + chunk] for p in refs[:pieces]], axis=0)
+        copies[k // chunk].wait()
+        terms = []
+        if whole:
+            weight = weight_ref[k : k + chunk, :whole]
+            terms.append(jnp.dot(x, weight, preferred_element_type=jnp.float32))
+        if columns - whole == 128:
+            half = chunk // 2
+            left = jnp.concatenate([x[:, :half], x[:, half:]], axis=0)
+            right = [weight_ref[k + h : k + h + half, whole:] for h in (0, half)]
+            both = jnp.dot(
+                left, jnp.concatenate(right, axis=1), preferred_element_type=jnp.float32
+            )
+            terms.append(both[:total, :128] + both[total:, 128:])
+        elif columns > whole:
+            weight = weight_ref[k : k + chunk, whole:]
+            terms.append(jnp.dot(x, weight, preferred_element_type=jnp.float32))
+        term = terms[0] if len(terms) == 1 else jnp.concatenate(terms, axis=1)
+        if k == 0:
+            out_ref[...] = term
+        else:
+            out_ref[...] += term
 
 
 def lift_kernel(count, rows, pieces, bounds, rank, *refs):
     tag_refs, refs = refs[:pieces], refs[pieces:]
-    down_ref, up_ref, base_ref, out_ref, sum_ref = refs
+    (down_ref, up_ref), base_refs, (out_ref, sum_ref) = refs[:2], refs[2:-2], refs[-2:]
     total = count * rows
     me = lax.axis_index(AXIS)
     adapters, per, columns = up_ref.shape
@@ -175,9 +210,7 @@
     row, column = iota((total, total), 0), iota((total, total), 1)
     order = one_hot(place_of(column, me, count, rows) == row)
     back = one_hot(place_of(row, me, count, rows) == column)
-    folded = down_ref[0].astype(jnp.float32)
-    for d in range(1, count):
-        folded = folded + down_ref[d].astype(jnp.float32)
+    folded = down_ref[...].astype(jnp.float32)
     folds = folded.shape[1] // total
     down = jnp.concatenate([folded[:, f * total : (f + 1) * total] for f in range(folds)], axis=0)
     down = lax.dot_general(
@@ -186,7 +219,10 @@
     names = jnp.concatenate([t[...] for t in tag_refs], axis=0).astype(jnp.float32)[:, :1]
     named = (iota((total, wide), 1) // per).astype(jnp.float32) == names
     start = me * columns
-    sum_ref[...] = base_ref[...]
+    value = base_refs[0][...]
+    for b in base_refs[1:]:
+        value = value + b[...]
+    sum_ref[...] = value
     for g in range(rank // per):
         low, high = bounds[g], bounds[g + 1]
 
@@ -231,8 +267,12 @@
     kv_width = kv_heads * head_dim
     total = rows * count
     bf16, f32 = jnp.bfloat16, jnp.float32
-    roomy = pltpu.CompilerParams(vmem_limit_bytes=limit(total, True))
-    full = pltpu.CompilerParams(vmem_limit_bytes=limit(total, False))
+    roomy = pltpu.CompilerParams(vmem_limit_bytes=limit(total, 16))
+    tight = {
+        projection_weight.shape[1]: pltpu.CompilerParams(vmem_limit_bytes=limit(total, 52)),
+        output_weight.shape[1]: pltpu.CompilerParams(vmem_limit_bytes=limit(total, 52)),
+    }
+    full = pltpu.CompilerParams(vmem_limit_bytes=limit(total, 60))
     own_maps = jnp.swapaxes(adapter_down, 1, 2)
     sibling_maps = jnp.swapaxes(swap(adapter_down, count, 1), 1, 2)
 
@@ -249,26 +289,28 @@
             pltpu.SemaphoreType.DMA((4,)),
         ],
         compiler_params=full,
-        cost_estimate=pl.CostEstimate(flops=0, bytes_accessed=1 << 24, transcendentals=0),
         name="norm",
     )(input_hidden, input_norm_gain, request_adapter.reshape(rows), adapter_storage)
 
     def tag_specs(pieces):
         return [pl.BlockSpec((p.shape[0], LANES), lambda i: (0, width // LANES)) for p in pieces]
 
-    def downs(pieces, tagged, low, high):
+    def downs(pieces, tagged, low, high, columns):
         ranks = high - low
         lanes = max(LANES, total)
-        down_spec = pl.BlockSpec((held, ranks, width), lambda i: (0, low // ranks, 0))
         return pl.pallas_call(
-            functools.partial(down_kernel, count, rows, len(pieces)),
+            functools.partial(down_kernel, count, rows, len(pieces), low),
             grid=(1,),
-            out_shape=jax.ShapeDtypeStruct((count, ranks * total // lanes, lanes), bf16),
-            in_specs=[down_spec] * 2
+            out_shape=jax.ShapeDtypeStruct((ranks * total // lanes, lanes), bf16),
+            in_specs=[spec(pl.ANY)] * 2
             + [pl.BlockSpec((p.shape[0], width), lambda i: (0, 0)) for p in pieces]
             + tag_specs(tagged),
             out_specs=spec(),
-            compiler_params=roomy,
+            scratch_shapes=[
+                VMEM((2, held, ranks, width), bf16),
+                pltpu.SemaphoreType.DMA((2 * (width // 2048),)),
+            ],
+            compiler_params=tight[columns],
             cost_estimate=pl.CostEstimate(
                 flops=2 * total * width * held * ranks,
                 bytes_accessed=2 * width * (2 * held * ranks + total),
@@ -277,46 +319,52 @@
             name="down",
         )(own_maps, sibling_maps, *pieces, *tagged)
 
-    def base(pieces, weight, after):
+    def base(pieces, weight, after, part, parts):
         columns = weight.shape[1]
-        chunk = 1024
         return pl.pallas_call(
-            functools.partial(base_kernel, len(pieces)),
-            grid=(width // chunk,),
+            functools.partial(base_kernel, len(pieces), part),
             out_shape=jax.ShapeDtypeStruct((total, columns), f32),
-            in_specs=[pl.BlockSpec((p.shape[0], chunk), lambda i: (0, i)) for p in pieces]
-            + [pl.BlockSpec((chunk, columns), lambda i: (i, 0)), spec(pl.ANY)],
-            out_specs=pl.BlockSpec((total, columns), lambda i: (0, 0)),
-            compiler_params=full,
+            in_specs=[spec()] * len(pieces) + [spec(pl.ANY)] * 2,
+            out_specs=spec(),
+            scratch_shapes=[
+                VMEM((width // parts, columns), bf16),
+                pltpu.SemaphoreType.DMA((width // parts // 1024,)),
+            ],
+            compiler_params=tight[columns],
             cost_estimate=pl.CostEstimate(
-                flops=2 * total * width * columns,
-                bytes_accessed=2 * width * columns,
+                flops=2 * total * width * columns // parts,
+                bytes_accessed=2 * width * columns // parts,
                 transcendentals=0,
             ),
             name="base",
         )(*pieces, weight, after)
 
-    def lift(down, tagged, up, base_term, bounds, ranks):
+    def lift(down, tagged, up, base_terms, bounds, ranks):
         columns = up.shape[2]
         whole = lambda x: pl.BlockSpec(x.shape, lambda i: (0,) * x.ndim)
+        operands = [down, up] + base_terms
         return pl.pallas_call(
             functools.partial(lift_kernel, count, rows, len(tagged), bounds, ranks),
             grid=(1,),
             out_shape=jax.ShapeDtypeStruct((count, rows, columns), bf16),
-            in_specs=tag_specs(tagged) + [whole(down), whole(up), whole(base_term)],
+            in_specs=tag_specs(tagged) + [whole(x) for x in operands],
             out_specs=pl.BlockSpec((count, rows, columns), lambda i: (0, 0, 0)),
             scratch_shapes=[VMEM((total, columns), f32)],
-            compiler_params=full,
+            compiler_params=roomy,
             name="lift",
-        )(*tagged, down, up, base_term)
+        )(*tagged, *operands)
 
     def project(x, tagged, low, high, weight, up, bounds):
         column, pieces = gather_rows(x, count)
         tagged = pieces if tagged is None else tagged
-        mine = downs(column, tagged[: len(column)], low, high)
-        down = exchange(mine)
-        base_term = base(pieces, weight, mine)
-        columns = lift(down, tagged, up, base_term, bounds, high - low)
+        parts = 2
+
+        def beside(turn, after):
+            return base(pieces, weight, after, turn, parts) if turn < parts else None
+
+        down = downs(column, tagged[: len(column)], low, high, weight.shape[1])
+        down, base_terms = sum_over(down, count, beside)
+        columns = lift(down, tagged, up, base_terms, bounds, high - low)
         mine = exchange(columns)
         return jnp.swapaxes(mine, 0, 1).reshape(rows, -1), tagged
 
@@ -333,6 +381,7 @@
     scores = (
         jnp.einsum("bhgd,bhpd->bhgp", query, cache_keys, preferred_element_type=jnp.float32) * scale
     )
+    lengths, query = lax.optimization_barrier((lengths, query))
     live = jnp.arange(context, dtype=jnp.int32)[None, :] < lengths[:, None]
     scores = jnp.where(live[:, None, None, :], scores, -1e30)
     own = jnp.einsum("bhgd,bhd->bhg", query, key_new, preferred_element_type=jnp.float32) * scale

time: 103 us -> 92.9 us (0.902)
  blocking collectives: 12.9 us -> 22 us
  Pallas kernels: 28.3 us -> 19.9 us
  waiting for transfers between devices: 18.6 us -> 13.2 us
  local copies, waits for them, and re-layouts: 5.12 us -> 2.23 us
  other arithmetic: 3.28 us -> 1.9 us
  starting transfers between devices: 32.1 us -> 30.8 us
    all_to_all x3 -> x0, starting transfers between devices: 14.2 us -> none  [exchange(): lax.all_to_all(x, AXIS, split_axis=0, concat_axis=0, axis_index_groups=gr...]
    ppermute x19 -> x31, starting transfers between devices: 17.9 us -> 30.8 us  [swap(): return lax.ppermute(x, AXIS, [(i, i ^ offset) for i in range(count)])]
    all_to_all x1 -> x2, blocking collectives: 12.9 us -> 22 us  [exchange(): lax.all_to_all(x, AXIS, split_axis=0, concat_axis=0, axis_index_groups=gr...]
    all_to_all x3 -> x0, waiting for transfers between devices: 7.07 us -> none  [exchange(): lax.all_to_all(x, AXIS, split_axis=0, concat_axis=0, axis_index_groups=gr...]
    pallas_call x4 -> x6, Pallas kernels: 21.5 us -> 16.7 us  [the longest x4 11.1 us: base(): pl.pallas_call(functools.partial(base_kernel, len(pieces), part), out_sha...]
    pallas_call x2, Pallas kernels: 4.88 us -> 1.31 us  [lift(): pl.pallas_call(functools.partial(lift_kernel, count, rows, len(tagged), b...]
    unnamed x28 -> x29, local copies, waits for them, and re-layouts: 5.11 us -> 2.22 us
    ppermute x19 -> x31, waiting for transfers between devices: 11.6 us -> 13.2 us  [swap(): return lax.ppermute(x, AXIS, [(i, i ^ offset) for i in range(count)])]
  transfers between devices with their start and end apart: 22 -> 31, of which waited for: 10 -> 12; matrix products, arithmetic and copies ran while one was open for 3% -> 2% of each run, Pallas kernels for 21% -> 15%
where the time goes in v5:
time: 92.9 us; the launch traced here: 92.6 us
  starting transfers between devices  30.8 us (33%)
  blocking collectives  22 us (24%)
  Pallas kernels  19.9 us (21%)
  waiting for transfers between devices  13.2 us (14%)
  local copies, waits for them, and re-layouts  2.23 us (2%)
  matrix products  2.12 us (2%)
  other arithmetic  1.9 us (2%)
    ppermute x31, starting transfers between devices, swap(): return lax.ppermute(x, AXIS, [(i, i ^ offset) for i in range(count)])  30.8 us
    all_to_all x2, blocking collectives, exchange(): lax.all_to_all(x, AXIS, split_axis=0, concat_axis=0, axis_index_groups=gr...  22 us
    ppermute x31, waiting for transfers between devices, swap(): return lax.ppermute(x, AXIS, [(i, i ^ offset) for i in range(count)])  13.2 us
    pallas_call x4, Pallas kernels, base(): pl.pallas_call(functools.partial(base_kernel, len(pieces), part), out_sha...  11.1 us
    pallas_call x2, Pallas kernels, downs(): pl.pallas_call(functools.partial(down_kernel, count, rows, len(pieces), l...  5.66 us
    unnamed x29, local copies, waits for them, and re-layouts  2.22 us
  transfers between devices with their start and end apart: 31, of which 12 were waited for; matrix products, arithmetic and copies ran while one was open for 2% of the time, Pallas kernels for 15%

profile of v5, /device:TPU:0, one launch (start us, length us, event | category | flops | bytes accessed | tf_op | source)
XLA Modules:
  0.0 92.6 jit_solution(11606822457199177348)
XLA Ops:
  0.0 1.8 %norm.1 = bf16[4,8320]{1,0:T(4,128)(2,1)} custom-call(bf16[4,8192]{1,0:T(4,128)(2,1)} %hidden_hbm.1, bf16[8192]{0:T(1024)(128)(2,1)} %gain_hbm.1, s32[4]{0:T(128)} %bitcast.51, s32[32]{0:T(128)} %slots_hbm.1), custom_call_target="tpu_custom_call" | custom-call | tf_op jit(solution)/shard_map/norm/pallas_call | solution.py:279
  1.9 5.1 %collective-permute-start.2 = (bf16[4,8320]{1,0:T(4,128)(2,1)}, bf16[4,8320]{1,0:T(4,128)(2,1)S(1)}, u32[]{:S(2)}, u32[]{:S(2)}) collective-permute-start(bf16[4,8320]{1,0:T(4,128)(2,1)} %norm.1), channel_id=1, source_target_pairs={{0,12},{1,13},{2,14},{3,15},{4,8},{5,9},{6,10},{7,11},{8,4},{9,5},... | collective-permute-start | bytes 199688 | tf_op jit(solution)/shard_map/ppermute | solution.py:18
  7.0 0.6 collective-permute-start
  7.6 1.6 %collective-permute-start.3 = (bf16[4,8320]{1,0:T(4,128)(2,1)}, bf16[4,8320]{1,0:T(4,128)(2,1)S(1)}, u32[]{:S(2)}, u32[]{:S(2)}) collective-permute-start(bf16[4,8320]{1,0:T(4,128)(2,1)} %norm.1), channel_id=1, source_target_pairs={{0,2},{1,3},{2,0},{3,1},{4,6},{5,7},{6,4},{7,5},{8,10},{9,11},{10,... | collective-permute-start | bytes 199688 | tf_op jit(solution)/shard_map/ppermute | solution.py:18
  9.2 0.6 collective-permute-done.2
  9.8 1.8 %collective-permute-start.6 = (bf16[4,8320]{1,0:T(4,128)(2,1)S(1)}, bf16[4,8320]{1,0:T(4,128)(2,1)S(1)}, u32[]{:S(2)}, u32[]{:S(2)}) collective-permute-start(bf16[4,8320]{1,0:T(4,128)(2,1)S(1)} %collective-permute-done.2), channel_id=1, source_target_pairs={{0,2},{1,3},{2,0},{3,1},{4,6},{5,7},{6,4},{7,5},{8,10},{9,11},{10,... | collective-permute-start | bytes 199688 | tf_op jit(solution)/shard_map/ppermute | solution.py:18
  11.6 1.2 %collective-permute-done.1 = bf16[4,8320]{1,0:T(4,128)(2,1)S(1)} collective-permute-done((bf16[4,8320]{1,0:T(4,128)(2,1)}, bf16[4,8320]{1,0:T(4,128)(2,1)S(1)}, u32[]{:S(2)}, u32[]{:S(2)}) %collective-permute-start.1) | collective-permute-done | bytes 66592 | tf_op jit(solution)/shard_map/ppermute | solution.py:18
  12.9 1.5 %collective-permute-start.5 = (bf16[4,8320]{1,0:T(4,128)(2,1)S(1)}, bf16[4,8320]{1,0:T(4,128)(2,1)S(1)}, u32[]{:S(2)}, u32[]{:S(2)}) collective-permute-start(bf16[4,8320]{1,0:T(4,128)(2,1)S(1)} %collective-permute-done.1), channel_id=1, source_target_pairs={{0,2},{1,3},{2,0},{3,1},{4,6},{5,7},{6,4},{7,5},{8,10},{9,11},{10,... | collective-permute-start | bytes 199688 | tf_op jit(solution)/shard_map/ppermute | solution.py:18
  14.4 0.5 collective-permute-start.4
  14.9 1.0 %pad_maximum_fusion.refs_2_.refs_4_.refs_0_ = bf16[16,8320]{1,0:T(8,128)(2,1)S(1)} fusion(bf16[4,8320]{1,0:T(4,128)(2,1)S(1)} %collective-permute-done.2, bf16[4,8320]{1,0:T(4,128)(2,1)S(1)} %collective-permute-done.1, bf16[4,8320]{1,0:T(4,128)(2,1)S(1)} %collective-permute-done, bf16[4,8320]{1,0:T(4,128)(2,1)} %norm.1), kind=kLoop, calls=%fused_computation.8 | loop fusion | flops 1064960 | bytes 532480 | tf_op jit(solution)/shard_map/concatenate | solution.py:46
  15.9 0.1 collective-permute-start.7
  16.0 1.7 %collective-permute-done.5 = bf16[4,8320]{1,0:T(4,128)(2,1)S(1)} collective-permute-done((bf16[4,8320]{1,0:T(4,128)(2,1)S(1)}, bf16[4,8320]{1,0:T(4,128)(2,1)S(1)}, u32[]{:S(2)}, u32[]{:S(2)}) %collective-permute-start.5) | collective-permute-done | bytes 66592 | tf_op jit(solution)/shard_map/ppermute | solution.py:18
  17.7 0.9 collective-permute-done.4
  18.6 0.2 pad_maximum_fusion.1.refs_3_.refs_5_.refs_1_
  18.8 0.1 collective-permute-start.8
  18.9 1.3 %copy-done.9 = bf16[2,8192,64]{1,2,0:T(8,128)(2,1)} copy-done((bf16[2,8192,64]{1,2,0:T(8,128)(2,1)}, bf16[2,8192,64]{1,2,0:T(8,128)(2,1)S(1)}, u32[]{:S(2)}) %copy-start.9) | copy-done | bytes 2097176
  20.3 3.5 %down.2.refs_5_ = bf16[24,128]{1,0:T(8,128)(2,1)S(1)} custom-call(bf16[2,64,8192]{2,1,0:T(8,128)(2,1)} %bitcast.35, bf16[2,64,8192]{2,1,0:T(8,128)(2,1)} %bitcast.37, bf16[16,8320]{1,0:T(8,128)(2,1)S(1)} %pad_maximum_fusion.refs_2_.refs_4_.refs_0_, bf16[16,8320]{1,0:T(8,128)(2,1)S(1)} %pad_maximum_fusion.1.refs_3_.refs_5_.refs_1_, ...), custom_call_target="tpu_custom_call" | custom-call | flops 100663296 | bytes 4194304 | tf_op jit(solution)/shard_map/down/pallas_call | solution.py:301
  23.8 2.8 %collective-permute-start.12 = (bf16[24,128]{1,0:T(8,128)(2,1)S(1)}, bf16[24,128]{1,0:T(8,128)(2,1)S(1)}, u32[]{:S(2)}, u32[]{:S(2)}) collective-permute-start(bf16[24,128]{1,0:T(8,128)(2,1)S(1)} %down.2.refs_5_), channel_id=1, source_target_pairs={{0,12},{1,13},{2,14},{3,15},{4,8},{5,9},{6,10},{7,11},{8,4},{9,5},... | collective-permute-start | bytes 18440 | tf_op jit(solution)/shard_map/ppermute | solution.py:18
  26.6 1.7 %collective-permute-start.10 = (bf16[24,128]{1,0:T(8,128)(2,1)S(1)}, bf16[24,128]{1,0:T(8,128)(2,1)S(1)}, u32[]{:S(2)}, u32[]{:S(2)}) collective-permute-start(bf16[24,128]{1,0:T(8,128)(2,1)S(1)} %down.2.refs_5_), channel_id=1, source_target_pairs={{0,4},{1,5},{2,6},{3,7},{4,0},{5,1},{6,2},{7,3},{8,12},{9,13},{10,... | collective-permute-start | bytes 18440 | tf_op jit(solution)/shard_map/ppermute | solution.py:18
  28.2 3.1 %base.4.refs_6_ = f32[64,640]{1,0:T(8,128)S(1)} custom-call(bf16[16,8320]{1,0:T(8,128)(2,1)S(1)} %pad_maximum_fusion.refs_2_.refs_4_.refs_0_, bf16[16,8320]{1,0:T(8,128)(2,1)S(1)} %pad_maximum_fusion.1.refs_3_.refs_5_.refs_1_, bf16[16,8320]{1,0:T(8,128)(2,1)S(1)} %collective-permute-done.7.refs_2_, bf16[16,8320]{1,0:T(8,128)(2,1)S(1)} %collective-permute-done.8.refs_3_, ...), custom_call_target="tpu_custom_call" | custom-call | flops 335544320 | bytes 5242880 | tf_op jit(solution)/shard_map/base/pallas_call | solution.py:324
  31.4 0.0 copy-start.11
  31.4 0.4 collective-permute-start.15
  31.8 1.0 %collective-permute-start.14 = (bf16[24,128]{1,0:T(8,128)(2,1)S(1)}, bf16[24,128]{1,0:T(8,128)(2,1)S(1)}, u32[]{:S(2)}, u32[]{:S(2)}) collective-permute-start(bf16[24,128]{1,0:T(8,128)(2,1)S(1)} %add_add_fusion.1.refs_5_), channel_id=1, source_target_pairs={{0,2},{1,3},{2,0},{3,1},{4,6},{5,7},{6,4},{7,5},{8,10},{9,11},{10,... | collective-permute-start | bytes 18440 | tf_op jit(solution)/shard_map/ppermute | solution.py:18
  32.8 0.6 collective-permute-start.13
  33.4 2.9 %base.5.refs_7_ = f32[64,640]{1,0:T(8,128)S(1)} custom-call(bf16[16,8320]{1,0:T(8,128)(2,1)S(1)} %pad_maximum_fusion.refs_2_.refs_4_.refs_0_, bf16[16,8320]{1,0:T(8,128)(2,1)S(1)} %pad_maximum_fusion.1.refs_3_.refs_5_.refs_1_, bf16[16,8320]{1,0:T(8,128)(2,1)S(1)} %collective-permute-done.7.refs_2_, bf16[16,8320]{1,0:T(8,128)(2,1)S(1)} %collective-permute-done.8.refs_3_, ...), custom_call_target="tpu_custom_call" | custom-call | flops 335544320 | bytes 5242880 | tf_op jit(solution)/shard_map/base/pallas_call | solution.py:324
  36.4 0.7 lift.2
  37.1 11.5 %all_to_all.10 = bf16[16,4,640]{2,1,0:T(4,128)(2,1)S(1)} all-to-all(bf16[16,4,640]{2,1,0:T(4,128)(2,1)S(1)} %lift.2), channel_id=1, replica_groups=mesh['groups'=2,'tensor'=16] {'tensor'}, dimensions={0} | all-to-all | bytes 163840 | tf_op jit(solution)/shard_map/all_to_all | solution.py:22
  48.7 0.0 copy-start.10
  48.7 0.1 iota_compare_fusion
  48.8 0.1 fusion.9
  48.9 0.0 copy-done
  49.0 1.3 %fusion.8 = (f32[4,8,8]{2,1,0:T(8,128)S(1)}, f32[4,8,8,384]{3,2,1,0:T(8,128)S(1)}) fusion(bf16[4,8,384,128]{3,2,1,0:T(8,128)(2,1)S(1)} %copy-done, bf16[1,4,64,128]{3,1,2,0:T(4,128)(2,1)S(1)} %slice_bitcast_fusion, pred[4,384]{1,0:T(4,128)(4,1)S(1)} %iota_compare_fusion), kind=kOutput, calls=%fused_computation.29 | convolution fusion | flops 25460480 | bytes 3607040 | tf_op jit(solution)/shard_map/bhgd,bhpd->bhgp/dot_general | solution.py:382
  50.2 0.2 fusion.3
  50.5 0.1 copy-done.10
  50.6 0.7 fusion.2
  51.3 0.1 copy.24
  51.4 0.7 collective-permute-start.18
  52.0 0.8 collective-permute-start.17
  52.8 3.0 %collective-permute-start.16 = (bf16[4,8192]{1,0:T(4,128)(2,1)S(1)}, bf16[4,8192]{1,0:T(4,128)(2,1)S(1)}, u32[]{:S(2)}, u32[]{:S(2)}) collective-permute-start(bf16[4,8192]{1,0:T(4,128)(2,1)S(1)} %bitcast.44), channel_id=1, source_target_pairs={{0,4},{1,5},{2,6},{3,7},{4,0},{5,1},{6,2},{7,3},{8,12},{9,13},{10,... | collective-permute-start | bytes 196616 | tf_op jit(solution)/shard_map/ppermute | solution.py:18
  55.8 2.4 %collective-permute-done.18 = bf16[4,8192]{1,0:T(4,128)(2,1)S(1)} collective-permute-done((bf16[4,8192]{1,0:T(4,128)(2,1)S(1)}, bf16[4,8192]{1,0:T(4,128)(2,1)S(1)}, u32[]{:S(2)}, u32[]{:S(2)}) %collective-permute-start.18) | collective-permute-done | bytes 65568 | tf_op jit(solution)/shard_map/ppermute | solution.py:18
  58.2 1.3 %collective-permute-done.17 = bf16[4,8192]{1,0:T(4,128)(2,1)S(1)} collective-permute-done((bf16[4,8192]{1,0:T(4,128)(2,1)S(1)}, bf16[4,8192]{1,0:T(4,128)(2,1)S(1)}, u32[]{:S(2)}, u32[]{:S(2)}) %collective-permute-start.17) | collective-permute-done | bytes 65568 | tf_op jit(solution)/shard_map/ppermute | solution.py:18
  59.5 0.7 collective-permute-start.21
  60.2 1.3 %collective-permute-start.20 = (bf16[4,8192]{1,0:T(4,128)(2,1)S(1)}, bf16[4,8192]{1,0:T(4,128)(2,1)S(1)}, u32[]{:S(2)}, u32[]{:S(2)}) collective-permute-start(bf16[4,8192]{1,0:T(4,128)(2,1)S(1)} %collective-permute-done.16), channel_id=1, source_target_pairs={{0,2},{1,3},{2,0},{3,1},{4,6},{5,7},{6,4},{7,5},{8,10},{9,11},{10,... | collective-permute-start | bytes 196616 | tf_op jit(solution)/shard_map/ppermute | solution.py:18
  61.5 0.2 pad_maximum_fusion.2.refs_2_.refs_0_
  61.7 0.1 collective-permute-start.26
  61.8 1.1 %collective-permute-done.22 = bf16[4,8192]{1,0:T(4,128)(2,1)S(1)} collective-permute-done((bf16[4,8192]{1,0:T(4,128)(2,1)S(1)}, bf16[4,8192]{1,0:T(4,128)(2,1)S(1)}, u32[]{:S(2)}, u32[]{:S(2)}) %collective-permute-start.22) | collective-permute-done | bytes 65568 | tf_op jit(solution)/shard_map/ppermute | solution.py:18
  62.9 1.6 %collective-permute-done.21 = bf16[4,8192]{1,0:T(4,128)(2,1)S(1)} collective-permute-done((bf16[4,8192]{1,0:T(4,128)(2,1)S(1)}, bf16[4,8192]{1,0:T(4,128)(2,1)S(1)}, u32[]{:S(2)}, u32[]{:S(2)}) %collective-permute-start.21) | collective-permute-done | bytes 65568 | tf_op jit(solution)/shard_map/ppermute | solution.py:18
  64.5 0.8 collective-permute-done.20
  65.3 0.2 pad_maximum_fusion.3.refs_3_.refs_1_
  65.4 0.1 collective-permute-start.27
  65.5 2.2 %down.3.refs_5_ = bf16[8,128]{1,0:T(8,128)(2,1)S(1)} custom-call(bf16[2,64,8192]{2,1,0:T(8,128)(2,1)} %bitcast.36, bf16[2,64,8192]{2,1,0:T(8,128)(2,1)} %bitcast.38, bf16[16,8192]{1,0:T(8,128)(2,1)S(1)} %pad_maximum_fusion.2.refs_2_.refs_0_, bf16[16,8192]{1,0:T(8,128)(2,1)S(1)} %pad_maximum_fusion.3.refs_3_.refs_1_, ...), custom_call_target="tpu_custom_call" | custom-call | flops 33554432 | bytes 2097152 | tf_op jit(solution)/shard_map/down/pallas_call | solution.py:301
  67.7 1.1 %collective-permute-start.25 = (bf16[8,128]{1,0:T(8,128)(2,1)S(1)}, bf16[8,128]{1,0:T(8,128)(2,1)S(1)}, u32[]{:S(2)}, u32[]{:S(2)}) collective-permute-start(bf16[8,128]{1,0:T(8,128)(2,1)S(1)} %down.3.refs_5_), channel_id=1, source_target_pairs={{0,12},{1,13},{2,14},{3,15},{4,8},{5,9},{6,10},{7,11},{8,4},{9,5},... | collective-permute-start | bytes 6152 | tf_op jit(solution)/shard_map/ppermute | solution.py:18
  68.8 3.3 %collective-permute-start.23 = (bf16[8,128]{1,0:T(8,128)(2,1)S(1)}, bf16[8,128]{1,0:T(8,128)(2,1)S(1)}, u32[]{:S(2)}, u32[]{:S(2)}) collective-permute-start(bf16[8,128]{1,0:T(8,128)(2,1)S(1)} %down.3.refs_5_), channel_id=1, source_target_pairs={{0,4},{1,5},{2,6},{3,7},{4,0},{5,1},{6,2},{7,3},{8,12},{9,13},{10,... | collective-permute-start | bytes 6152 | tf_op jit(solution)/shard_map/ppermute | solution.py:18
  72.1 1.0 %collective-permute-done.25 = bf16[8,128]{1,0:T(8,128)(2,1)S(1)} collective-permute-done((bf16[8,128]{1,0:T(8,128)(2,1)S(1)}, bf16[8,128]{1,0:T(8,128)(2,1)S(1)}, u32[]{:S(2)}, u32[]{:S(2)}) %collective-permute-start.25) | collective-permute-done | bytes 2080 | tf_op jit(solution)/shard_map/ppermute | solution.py:18
  73.1 0.1 collective-permute-done.24
  73.3 0.4 collective-permute-done.23
  73.7 2.5 %base.6.refs_6_ = f32[64,512]{1,0:T(8,128)S(1)} custom-call(bf16[16,8192]{1,0:T(8,128)(2,1)S(1)} %pad_maximum_fusion.2.refs_2_.refs_0_, bf16[16,8192]{1,0:T(8,128)(2,1)S(1)} %pad_maximum_fusion.3.refs_3_.refs_1_, bf16[16,8192]{1,0:T(8,128)(2,1)S(1)} %collective-permute-done.26.refs_2_, bf16[16,8192]{1,0:T(8,128)(2,1)S(1)} %collective-permute-done.27.refs_3_, ...), custom_call_target="tpu_custom_call" | custom-call | flops 268435456 | bytes 4194304 | tf_op jit(solution)/shard_map/base/pallas_call | solution.py:324
  76.3 0.1 collective-permute-start.30
  76.3 1.0 %collective-permute-start.29 = (bf16[8,128]{1,0:T(8,128)(2,1)S(1)}, bf16[8,128]{1,0:T(8,128)(2,1)S(1)}, u32[]{:S(2)}, u32[]{:S(2)}) collective-permute-start(bf16[8,128]{1,0:T(8,128)(2,1)S(1)} %add_add_fusion.3.refs_5_), channel_id=1, source_target_pairs={{0,2},{1,3},{2,0},{3,1},{4,6},{5,7},{6,4},{7,5},{8,10},{9,11},{10,... | collective-permute-start | bytes 6152 | tf_op jit(solution)/shard_map/ppermute | solution.py:18
  77.3 0.9 collective-permute-start.28
  78.2 2.5 %base.7.refs_7_ = f32[64,512]{1,0:T(8,128)S(1)} custom-call(bf16[16,8192]{1,0:T(8,128)(2,1)S(1)} %pad_maximum_fusion.2.refs_2_.refs_0_, bf16[16,8192]{1,0:T(8,128)(2,1)S(1)} %pad_maximum_fusion.3.refs_3_.refs_1_, bf16[16,8192]{1,0:T(8,128)(2,1)S(1)} %collective-permute-done.26.refs_2_, bf16[16,8192]{1,0:T(8,128)(2,1)S(1)} %collective-permute-done.27.refs_3_, ...), custom_call_target="tpu_custom_call" | custom-call | flops 268435456 | bytes 4194304 | tf_op jit(solution)/shard_map/base/pallas_call | solution.py:324
  80.8 0.6 lift.3
  81.4 10.5 %all_to_all.11 = bf16[16,4,512]{2,1,0:T(4,128)(2,1)S(1)} all-to-all(bf16[16,4,512]{2,1,0:T(4,128)(2,1)S(1)} %lift.3), channel_id=1, replica_groups=mesh['groups'=2,'tensor'=16] {'tensor'}, dimensions={0} | all-to-all | bytes 131072 | tf_op jit(solution)/shard_map/all_to_all | solution.py:22
  91.9 0.6 copy.28
  (55 shorter events, 0.2 us)
Async XLA Ops:
  0.0 48.9 %copy-start = (bf16[4,8,384,128]{3,2,1,0:T(8,128)(2,1)S(1)}, bf16[4,8,384,128]{3,2,1,0:T(8,128)(2,1)}, u32[]{:S(2)}) copy-start(bf16[4,8,384,128]{3,2,1,0:T(8,128)(2,1)} %param.22) | copy-start | bytes 9437188
  1.9 8.0 %collective-permute-start.2 = (bf16[4,8320]{1,0:T(4,128)(2,1)}, bf16[4,8320]{1,0:T(4,128)(2,1)S(1)}, u32[]{:S(2)}, u32[]{:S(2)}) collective-permute-start(bf16[4,8320]{1,0:T(4,128)(2,1)} %norm.1), channel_id=1, source_target_pairs={{0,12},{1,13},{2,14},{3,15},{4,8},{5,9},{6,10},{7,11},{8,4},{9,5},... | collective-permute-start | bytes 199688 | tf_op jit(solution)/shard_map/ppermute | solution.py:18
  7.0 5.9 %collective-permute-start.1 = (bf16[4,8320]{1,0:T(4,128)(2,1)}, bf16[4,8320]{1,0:T(4,128)(2,1)S(1)}, u32[]{:S(2)}, u32[]{:S(2)}) collective-permute-start(bf16[4,8320]{1,0:T(4,128)(2,1)} %norm.1), channel_id=1, source_target_pairs={{0,8},{1,9},{2,10},{3,11},{4,12},{5,13},{6,14},{7,15},{8,0},{9,1},... | collective-permute-start | bytes 199688 | tf_op jit(solution)/shard_map/ppermute | solution.py:18
  7.0 7.4 %collective-permute-start = (bf16[4,8320]{1,0:T(4,128)(2,1)}, bf16[4,8320]{1,0:T(4,128)(2,1)S(1)}, u32[]{:S(2)}, u32[]{:S(2)}) collective-permute-start(bf16[4,8320]{1,0:T(4,128)(2,1)} %norm.1), channel_id=1, source_target_pairs={{0,4},{1,5},{2,6},{3,7},{4,0},{5,1},{6,2},{7,3},{8,12},{9,13},{10,... | collective-permute-start | bytes 199688 | tf_op jit(solution)/shard_map/ppermute | solution.py:18
  7.6 8.3 %collective-permute-start.3 = (bf16[4,8320]{1,0:T(4,128)(2,1)}, bf16[4,8320]{1,0:T(4,128)(2,1)S(1)}, u32[]{:S(2)}, u32[]{:S(2)}) collective-permute-start(bf16[4,8320]{1,0:T(4,128)(2,1)} %norm.1), channel_id=1, source_target_pairs={{0,2},{1,3},{2,0},{3,1},{4,6},{5,7},{6,4},{7,5},{8,10},{9,11},{10,... | collective-permute-start | bytes 199688 | tf_op jit(solution)/shard_map/ppermute | solution.py:18
  9.2 9.6 %collective-permute-start.9 = (bf16[2,8192,64]{1,2,0:T(8,128)(2,1)}, bf16[2,8192,64]{1,2,0:T(8,128)(2,1)S(1)}, u32[]{:S(2)}, u32[]{:S(2)}) collective-permute-start(bf16[2,8192,64]{1,2,0:T(8,128)(2,1)} %param.19), channel_id=1, source_target_pairs={{0,1},{1,0},{2,3},{3,2},{4,5},{5,4},{6,7},{7,6},{8,9},{9,8},{10,11... | collective-permute-start | bytes 6291464 | tf_op jit(solution)/shard_map/ppermute | solution.py:18
  9.8 6.2 %collective-permute-start.6 = (bf16[4,8320]{1,0:T(4,128)(2,1)S(1)}, bf16[4,8320]{1,0:T(4,128)(2,1)S(1)}, u32[]{:S(2)}, u32[]{:S(2)}) collective-permute-start(bf16[4,8320]{1,0:T(4,128)(2,1)S(1)} %collective-permute-done.2), channel_id=1, source_target_pairs={{0,2},{1,3},{2,0},{3,1},{4,6},{5,7},{6,4},{7,5},{8,10},{9,11},{10,... | collective-permute-start | bytes 199688 | tf_op jit(solution)/shard_map/ppermute | solution.py:18
  12.9 4.9 %collective-permute-start.5 = (bf16[4,8320]{1,0:T(4,128)(2,1)S(1)}, bf16[4,8320]{1,0:T(4,128)(2,1)S(1)}, u32[]{:S(2)}, u32[]{:S(2)}) collective-permute-start(bf16[4,8320]{1,0:T(4,128)(2,1)S(1)} %collective-permute-done.1), channel_id=1, source_target_pairs={{0,2},{1,3},{2,0},{3,1},{4,6},{5,7},{6,4},{7,5},{8,10},{9,11},{10,... | collective-permute-start | bytes 199688 | tf_op jit(solution)/shard_map/ppermute | solution.py:18
  14.4 4.3 %collective-permute-start.4 = (bf16[4,8320]{1,0:T(4,128)(2,1)S(1)}, bf16[4,8320]{1,0:T(4,128)(2,1)S(1)}, u32[]{:S(2)}, u32[]{:S(2)}) collective-permute-start(bf16[4,8320]{1,0:T(4,128)(2,1)S(1)} %collective-permute-done), channel_id=1, source_target_pairs={{0,2},{1,3},{2,0},{3,1},{4,6},{5,7},{6,4},{7,5},{8,10},{9,11},{10,... | collective-permute-start | bytes 199688 | tf_op jit(solution)/shard_map/ppermute | solution.py:18
  15.9 12.3 %collective-permute-start.7 = (bf16[16,8320]{1,0:T(8,128)(2,1)S(1)}, bf16[16,8320]{1,0:T(8,128)(2,1)S(1)}, u32[]{:S(2)}, u32[]{:S(2)}) collective-permute-start(bf16[16,8320]{1,0:T(8,128)(2,1)S(1)} %pad_maximum_fusion.refs_2_.refs_4_.refs_0_), channel_id=1, source_target_pairs={{0,1},{1,0},{2,3},{3,2},{4,5},{5,4},{6,7},{7,6},{8,9},{9,8},{10,11... | collective-permute-start | bytes 798728 | tf_op jit(solution)/shard_map/ppermute | solution.py:18
  18.8 17.6 %copy-start.1 = (bf16[16,8320]{1,0:T(8,128)(2,1)}, bf16[16,8320]{1,0:T(8,128)(2,1)S(1)}, u32[]{:S(2)}) copy-start(bf16[16,8320]{1,0:T(8,128)(2,1)S(1)} %pad_maximum_fusion.1.refs_3_.refs_5_.refs_1_) | copy-start | bytes 798724
  18.8 9.4 %collective-permute-start.8 = (bf16[16,8320]{1,0:T(8,128)(2,1)S(1)}, bf16[16,8320]{1,0:T(8,128)(2,1)S(1)}, u32[]{:S(2)}, u32[]{:S(2)}) collective-permute-start(bf16[16,8320]{1,0:T(8,128)(2,1)S(1)} %pad_maximum_fusion.1.refs_3_.refs_5_.refs_1_), channel_id=1, source_target_pairs={{0,1},{1,0},{2,3},{3,2},{4,5},{5,4},{6,7},{7,6},{8,9},{9,8},{10,11... | collective-permute-start | bytes 798728 | tf_op jit(solution)/shard_map/ppermute | solution.py:18
  18.9 1.4 %copy-start.9 = (bf16[2,8192,64]{1,2,0:T(8,128)(2,1)}, bf16[2,8192,64]{1,2,0:T(8,128)(2,1)S(1)}, u32[]{:S(2)}) copy-start(bf16[2,8192,64]{1,2,0:T(8,128)(2,1)S(1)} %collective-permute-done.9) | copy-start | bytes 6291460
  23.8 7.6 %collective-permute-start.12 = (bf16[24,128]{1,0:T(8,128)(2,1)S(1)}, bf16[24,128]{1,0:T(8,128)(2,1)S(1)}, u32[]{:S(2)}, u32[]{:S(2)}) collective-permute-start(bf16[24,128]{1,0:T(8,128)(2,1)S(1)} %down.2.refs_5_), channel_id=1, source_target_pairs={{0,12},{1,13},{2,14},{3,15},{4,8},{5,9},{6,10},{7,11},{8,4},{9,5},... | collective-permute-start | bytes 18440 | tf_op jit(solution)/shard_map/ppermute | solution.py:18
  26.6 4.8 %collective-permute-start.11 = (bf16[24,128]{1,0:T(8,128)(2,1)S(1)}, bf16[24,128]{1,0:T(8,128)(2,1)S(1)}, u32[]{:S(2)}, u32[]{:S(2)}) collective-permute-start(bf16[24,128]{1,0:T(8,128)(2,1)S(1)} %down.2.refs_5_), channel_id=1, source_target_pairs={{0,8},{1,9},{2,10},{3,11},{4,12},{5,13},{6,14},{7,15},{8,0},{9,1},... | collective-permute-start | bytes 18440 | tf_op jit(solution)/shard_map/ppermute | solution.py:18
  26.6 4.8 %collective-permute-start.10 = (bf16[24,128]{1,0:T(8,128)(2,1)S(1)}, bf16[24,128]{1,0:T(8,128)(2,1)S(1)}, u32[]{:S(2)}, u32[]{:S(2)}) collective-permute-start(bf16[24,128]{1,0:T(8,128)(2,1)S(1)} %down.2.refs_5_), channel_id=1, source_target_pairs={{0,4},{1,5},{2,6},{3,7},{4,0},{5,1},{6,2},{7,3},{8,12},{9,13},{10,... | collective-permute-start | bytes 18440 | tf_op jit(solution)/shard_map/ppermute | solution.py:18
  28.2 8.2 %copy-start.3 = (bf16[16,8320]{1,0:T(8,128)(2,1)}, bf16[16,8320]{1,0:T(8,128)(2,1)S(1)}, u32[]{:S(2)}) copy-start(bf16[16,8320]{1,0:T(8,128)(2,1)S(1)} %collective-permute-done.7.refs_2_) | copy-start | bytes 798724
  28.2 8.2 %copy-start.5 = (bf16[16,8320]{1,0:T(8,128)(2,1)}, bf16[16,8320]{1,0:T(8,128)(2,1)S(1)}, u32[]{:S(2)}) copy-start(bf16[16,8320]{1,0:T(8,128)(2,1)S(1)} %collective-permute-done.8.refs_3_) | copy-start | bytes 798724
  31.4 5.0 %copy-start.7 = (bf16[32,16,640]{2,1,0:T(8,128)(2,1)S(1)}, bf16[32,16,640]{2,1,0:T(8,128)(2,1)}, u32[]{:S(2)}) copy-start(bf16[32,16,640]{2,1,0:T(8,128)(2,1)} %refs_5_.2) | copy-start | bytes 1966084
  31.4 17.3 %copy-start.11 = (s32[4]{0:T(128)S(1)}, s32[4]{0:T(128)}, u32[]{:S(2)}) copy-start(s32[4]{0:T(128)} %param.16) | copy-start | bytes 52
  31.4 4.9 %collective-permute-start.15 = (bf16[24,128]{1,0:T(8,128)(2,1)S(1)}, bf16[24,128]{1,0:T(8,128)(2,1)S(1)}, u32[]{:S(2)}, u32[]{:S(2)}) collective-permute-start(bf16[24,128]{1,0:T(8,128)(2,1)S(1)} %add_add_fusion.1.refs_5_), channel_id=1, source_target_pairs={{0,3},{1,2},{2,1},{3,0},{4,7},{5,6},{6,5},{7,4},{8,11},{9,10},{10,... | collective-permute-start | bytes 18440 | tf_op jit(solution)/shard_map/ppermute | solution.py:18
  31.8 4.5 %collective-permute-start.14 = (bf16[24,128]{1,0:T(8,128)(2,1)S(1)}, bf16[24,128]{1,0:T(8,128)(2,1)S(1)}, u32[]{:S(2)}, u32[]{:S(2)}) collective-permute-start(bf16[24,128]{1,0:T(8,128)(2,1)S(1)} %add_add_fusion.1.refs_5_), channel_id=1, source_target_pairs={{0,2},{1,3},{2,0},{3,1},{4,6},{5,7},{6,4},{7,5},{8,10},{9,11},{10,... | collective-permute-start | bytes 18440 | tf_op jit(solution)/shard_map/ppermute | solution.py:18
  32.8 3.5 %collective-permute-start.13 = (bf16[24,128]{1,0:T(8,128)(2,1)S(1)}, bf16[24,128]{1,0:T(8,128)(2,1)S(1)}, u32[]{:S(2)}, u32[]{:S(2)}) collective-permute-start(bf16[24,128]{1,0:T(8,128)(2,1)S(1)} %add_add_fusion.1.refs_5_), channel_id=1, source_target_pairs={{0,1},{1,0},{2,3},{3,2},{4,5},{5,4},{6,7},{7,6},{8,9},{9,8},{10,11... | collective-permute-start | bytes 18440 | tf_op jit(solution)/shard_map/ppermute | solution.py:18
  48.7 1.9 %copy-start.10 = (bf16[4,8,384,128]{3,2,1,0:T(8,128)(2,1)S(1)}, bf16[4,8,384,128]{3,2,1,0:T(8,128)(2,1)}, u32[]{:S(2)}) copy-start(bf16[4,8,384,128]{3,2,1,0:T(8,128)(2,1)} %param.23) | copy-start | bytes 9437188
  50.2 15.3 %copy-start.2 = (bf16[16,8320]{1,0:T(8,128)(2,1)S(1)}, bf16[16,8320]{1,0:T(8,128)(2,1)}, u32[]{:S(2)}) copy-start(bf16[16,8320]{1,0:T(8,128)(2,1)} %copy-done.1) | copy-start | bytes 798724
  51.4 6.8 %collective-permute-start.18 = (bf16[4,8192]{1,0:T(4,128)(2,1)S(1)}, bf16[4,8192]{1,0:T(4,128)(2,1)S(1)}, u32[]{:S(2)}, u32[]{:S(2)}) collective-permute-start(bf16[4,8192]{1,0:T(4,128)(2,1)S(1)} %bitcast.42), channel_id=1, source_target_pairs={{0,12},{1,13},{2,14},{3,15},{4,8},{5,9},{6,10},{7,11},{8,4},{9,5},... | collective-permute-start | bytes 196616 | tf_op jit(solution)/shard_map/ppermute | solution.py:18
  52.0 7.5 %collective-permute-start.17 = (bf16[4,8192]{1,0:T(4,128)(2,1)S(1)}, bf16[4,8192]{1,0:T(4,128)(2,1)S(1)}, u32[]{:S(2)}, u32[]{:S(2)}) collective-permute-start(bf16[4,8192]{1,0:T(4,128)(2,1)S(1)} %bitcast.43), channel_id=1, source_target_pairs={{0,8},{1,9},{2,10},{3,11},{4,12},{5,13},{6,14},{7,15},{8,0},{9,1},... | collective-permute-start | bytes 196616 | tf_op jit(solution)/shard_map/ppermute | solution.py:18
  52.8 7.4 %collective-permute-start.16 = (bf16[4,8192]{1,0:T(4,128)(2,1)S(1)}, bf16[4,8192]{1,0:T(4,128)(2,1)S(1)}, u32[]{:S(2)}, u32[]{:S(2)}) collective-permute-start(bf16[4,8192]{1,0:T(4,128)(2,1)S(1)} %bitcast.44), channel_id=1, source_target_pairs={{0,4},{1,5},{2,6},{3,7},{4,0},{5,1},{6,2},{7,3},{8,12},{9,13},{10,... | collective-permute-start | bytes 196616 | tf_op jit(solution)/shard_map/ppermute | solution.py:18
  55.8 6.0 %collective-permute-start.19 = (bf16[4,8192]{1,0:T(4,128)(2,1)S(1)}, bf16[4,8192]{1,0:T(4,128)(2,1)S(1)}, u32[]{:S(2)}, u32[]{:S(2)}) collective-permute-start(bf16[4,8192]{1,0:T(4,128)(2,1)S(1)} %bitcast.45), channel_id=1, source_target_pairs={{0,2},{1,3},{2,0},{3,1},{4,6},{5,7},{6,4},{7,5},{8,10},{9,11},{10,... | collective-permute-start | bytes 196616 | tf_op jit(solution)/shard_map/ppermute | solution.py:18
  58.2 4.7 %collective-permute-start.22 = (bf16[4,8192]{1,0:T(4,128)(2,1)S(1)}, bf16[4,8192]{1,0:T(4,128)(2,1)S(1)}, u32[]{:S(2)}, u32[]{:S(2)}) collective-permute-start(bf16[4,8192]{1,0:T(4,128)(2,1)S(1)} %collective-permute-done.18), channel_id=1, source_target_pairs={{0,2},{1,3},{2,0},{3,1},{4,6},{5,7},{6,4},{7,5},{8,10},{9,11},{10,... | collective-permute-start | bytes 196616 | tf_op jit(solution)/shard_map/ppermute | solution.py:18
  59.5 5.0 %collective-permute-start.21 = (bf16[4,8192]{1,0:T(4,128)(2,1)S(1)}, bf16[4,8192]{1,0:T(4,128)(2,1)S(1)}, u32[]{:S(2)}, u32[]{:S(2)}) collective-permute-start(bf16[4,8192]{1,0:T(4,128)(2,1)S(1)} %collective-permute-done.17), channel_id=1, source_target_pairs={{0,2},{1,3},{2,0},{3,1},{4,6},{5,7},{6,4},{7,5},{8,10},{9,11},{10,... | collective-permute-start | bytes 196616 | tf_op jit(solution)/shard_map/ppermute | solution.py:18
  60.2 5.0 %collective-permute-start.20 = (bf16[4,8192]{1,0:T(4,128)(2,1)S(1)}, bf16[4,8192]{1,0:T(4,128)(2,1)S(1)}, u32[]{:S(2)}, u32[]{:S(2)}) collective-permute-start(bf16[4,8192]{1,0:T(4,128)(2,1)S(1)} %collective-permute-done.16), channel_id=1, source_target_pairs={{0,2},{1,3},{2,0},{3,1},{4,6},{5,7},{6,4},{7,5},{8,10},{9,11},{10,... | collective-permute-start | bytes 196616 | tf_op jit(solution)/shard_map/ppermute | solution.py:18
  61.7 12.0 %collective-permute-start.26 = (bf16[16,8192]{1,0:T(8,128)(2,1)S(1)}, bf16[16,8192]{1,0:T(8,128)(2,1)S(1)}, u32[]{:S(2)}, u32[]{:S(2)}) collective-permute-start(bf16[16,8192]{1,0:T(8,128)(2,1)S(1)} %pad_maximum_fusion.2.refs_2_.refs_0_), channel_id=1, source_target_pairs={{0,1},{1,0},{2,3},{3,2},{4,5},{5,4},{6,7},{7,6},{8,9},{9,8},{10,11... | collective-permute-start | bytes 786440 | tf_op jit(solution)/shard_map/ppermute | solution.py:18
  65.4 8.3 %collective-permute-start.27 = (bf16[16,8192]{1,0:T(8,128)(2,1)S(1)}, bf16[16,8192]{1,0:T(8,128)(2,1)S(1)}, u32[]{:S(2)}, u32[]{:S(2)}) collective-permute-start(bf16[16,8192]{1,0:T(8,128)(2,1)S(1)} %pad_maximum_fusion.3.refs_3_.refs_1_), channel_id=1, source_target_pairs={{0,1},{1,0},{2,3},{3,2},{4,5},{5,4},{6,7},{7,6},{8,9},{9,8},{10,11... | collective-permute-start | bytes 786440 | tf_op jit(solution)/shard_map/ppermute | solution.py:18
  67.7 5.4 %collective-permute-start.25 = (bf16[8,128]{1,0:T(8,128)(2,1)S(1)}, bf16[8,128]{1,0:T(8,128)(2,1)S(1)}, u32[]{:S(2)}, u32[]{:S(2)}) collective-permute-start(bf16[8,128]{1,0:T(8,128)(2,1)S(1)} %down.3.refs_5_), channel_id=1, source_target_pairs={{0,12},{1,13},{2,14},{3,15},{4,8},{5,9},{6,10},{7,11},{8,4},{9,5},... | collective-permute-start | bytes 6152 | tf_op jit(solution)/shard_map/ppermute | solution.py:18
  68.8 4.5 %collective-permute-start.24 = (bf16[8,128]{1,0:T(8,128)(2,1)S(1)}, bf16[8,128]{1,0:T(8,128)(2,1)S(1)}, u32[]{:S(2)}, u32[]{:S(2)}) collective-permute-start(bf16[8,128]{1,0:T(8,128)(2,1)S(1)} %down.3.refs_5_), channel_id=1, source_target_pairs={{0,8},{1,9},{2,10},{3,11},{4,12},{5,13},{6,14},{7,15},{8,0},{9,1},... | collective-permute-start | bytes 6152 | tf_op jit(solution)/shard_map/ppermute | solution.py:18
  68.8 4.9 %collective-permute-start.23 = (bf16[8,128]{1,0:T(8,128)(2,1)S(1)}, bf16[8,128]{1,0:T(8,128)(2,1)S(1)}, u32[]{:S(2)}, u32[]{:S(2)}) collective-permute-start(bf16[8,128]{1,0:T(8,128)(2,1)S(1)} %down.3.refs_5_), channel_id=1, source_target_pairs={{0,4},{1,5},{2,6},{3,7},{4,0},{5,1},{6,2},{7,3},{8,12},{9,13},{10,... | collective-permute-start | bytes 6152 | tf_op jit(solution)/shard_map/ppermute | solution.py:18
  76.2 4.5 %copy-start.4 = (bf16[16,8320]{1,0:T(8,128)(2,1)S(1)}, bf16[16,8320]{1,0:T(8,128)(2,1)}, u32[]{:S(2)}) copy-start(bf16[16,8320]{1,0:T(8,128)(2,1)} %copy-done.3) | copy-start | bytes 798724
  76.2 4.5 %copy-start.6 = (bf16[16,8320]{1,0:T(8,128)(2,1)S(1)}, bf16[16,8320]{1,0:T(8,128)(2,1)}, u32[]{:S(2)}) copy-start(bf16[16,8320]{1,0:T(8,128)(2,1)} %copy-done.5) | copy-start | bytes 798724
  76.3 4.5 %copy-start.8 = (bf16[32,16,512]{2,1,0:T(8,128)(2,1)S(1)}, bf16[32,16,512]{2,1,0:T(8,128)(2,1)}, u32[]{:S(2)}) copy-start(bf16[32,16,512]{2,1,0:T(8,128)(2,1)} %refs_5_.3) | copy-start | bytes 1572868
  76.3 4.4 %collective-permute-start.30 = (bf16[8,128]{1,0:T(8,128)(2,1)S(1)}, bf16[8,128]{1,0:T(8,128)(2,1)S(1)}, u32[]{:S(2)}, u32[]{:S(2)}) collective-permute-start(bf16[8,128]{1,0:T(8,128)(2,1)S(1)} %add_add_fusion.3.refs_5_), channel_id=1, source_target_pairs={{0,3},{1,2},{2,1},{3,0},{4,7},{5,6},{6,5},{7,4},{8,11},{9,10},{10,... | collective-permute-start | bytes 6152 | tf_op jit(solution)/shard_map/ppermute | solution.py:18
  76.3 4.4 %collective-permute-start.29 = (bf16[8,128]{1,0:T(8,128)(2,1)S(1)}, bf16[8,128]{1,0:T(8,128)(2,1)S(1)}, u32[]{:S(2)}, u32[]{:S(2)}) collective-permute-start(bf16[8,128]{1,0:T(8,128)(2,1)S(1)} %add_add_fusion.3.refs_5_), channel_id=1, source_target_pairs={{0,2},{1,3},{2,0},{3,1},{4,6},{5,7},{6,4},{7,5},{8,10},{9,11},{10,... | collective-permute-start | bytes 6152 | tf_op jit(solution)/shard_map/ppermute | solution.py:18
  77.3 3.4 %collective-permute-start.28 = (bf16[8,128]{1,0:T(8,128)(2,1)S(1)}, bf16[8,128]{1,0:T(8,128)(2,1)S(1)}, u32[]{:S(2)}, u32[]{:S(2)}) collective-permute-start(bf16[8,128]{1,0:T(8,128)(2,1)S(1)} %add_add_fusion.3.refs_5_), channel_id=1, source_target_pairs={{0,1},{1,0},{2,3},{3,2},{4,5},{5,4},{6,7},{7,6},{8,9},{9,8},{10,11... | collective-permute-start | bytes 6152 | tf_op jit(solution)/shard_map/ppermute | solution.py:18

commit v6 on v5

--- a/solution.py
+++ b/solution.py
@@ -30,11 +30,12 @@
         radix = 4 if step % 4 == 0 else 2
         step //= radix
         others = [swap(x, count, k * step) for k in range(1, radix)]
-        terms.append(beside(turn, x))
+        term = beside(turn, x)
+        if term is not None:
+            *others, term = lax.optimization_barrier((*others, term))
+        terms.append(term)
         for other in others:
             x = x + other
-        if terms[-1] is not None:
-            x, terms[-1] = lax.optimization_barrier((x, terms[-1]))
         turn += 1
     return x, [t for t in terms if t is not None]
 
@@ -80,8 +81,20 @@
 
 
 def norm_kernel(
-    hidden_hbm, gain_hbm, names_hbm, slots_hbm, out_ref, hidden_ref, gain_ref, names_ref, slots_ref, sems
+    hidden_hbm,
+    gain_hbm,
+    names_hbm,
+    slots_hbm,
+    maps_hbm,
+    out_ref,
+    maps_ref,
+    hidden_ref,
+    gain_ref,
+    names_ref,
+    slots_ref,
+    sems,
 ):
+    ranks = maps_ref.shape[1]
     copies = [
         pltpu.make_async_copy(source, target, sems.at[i])
         for i, (source, target) in enumerate(
@@ -90,12 +103,13 @@
                 (gain_hbm, gain_ref),
                 (names_hbm, names_ref),
                 (slots_hbm, slots_ref),
+                (maps_hbm.at[:, :ranks], maps_ref),
             )
         )
     ]
     for copy in copies:
         copy.start()
-    for copy in copies:
+    for copy in copies[:-1]:
         copy.wait()
     rows, width = hidden_ref.shape
     hidden = hidden_ref[...].astype(jnp.float32)
@@ -109,36 +123,30 @@
         tag = jnp.where(lane < LANES // 2, name, slots_ref[name]).astype(jnp.float32)
         tags = jnp.where(row == r, tag, tags)
     out_ref[:, width:] = tags.astype(jnp.bfloat16)
+    copies[-1].wait()
 
 
 NT = (((1,), (1,)), ((), ()))
 
 
-def down_kernel(count, rows, pieces, low, *refs):
-    maps_hbm, piece_refs = refs[:2], refs[2 : 2 + pieces]
-    tag_refs, (out_ref, maps_ref, sems) = refs[2 + pieces : 2 + 2 * pieces], refs[2 + 2 * pieces :]
+def down_kernel(count, rows, pieces, ranks, *refs):
+    map_refs, piece_refs = refs[:2], refs[2 : 2 + pieces]
+    tag_refs, out_refs = refs[2 + pieces : 2 + 2 * pieces], refs[2 + 2 * pieces :]
+    out_ref = out_refs[0]
     me = lax.axis_index(AXIS)
-    _, held, rank, width = maps_ref.shape
+    held, _, width = map_refs[0].shape
+    rank = ranks[1] - ranks[0]
     total, half = count * rows, count * rows // 2
-    chunk = 2048
-    copies = []
-    for k in range(0, width, chunk):
-        for m in range(2):
-            copies.append(
-                pltpu.make_async_copy(
-                    maps_hbm[m].at[:, low : low + rank, k : k + chunk],
-                    maps_ref.at[m, :, :, k : k + chunk],
-                    sems.at[len(copies)],
-                )
-            )
-            copies[-1].start()
+    chunk = 1024
     sums = jnp.zeros((2 * held * rank, half), jnp.float32)
     for k in range(0, width, chunk):
-        for m in range(2):
-            copies[k // chunk * 2 + m].wait()
         x = jnp.concatenate([p[:, k : k + chunk] for p in piece_refs], axis=0)
-        maps = maps_ref[:, :, :, k : k + chunk].reshape(2 * held * rank, chunk)
+        maps = jnp.concatenate(
+            [m[:, :rank, k : k + chunk].reshape(held * rank, chunk) for m in map_refs], axis=0
+        )
         sums = sums + lax.dot_general(maps, x, NT, preferred_element_type=jnp.float32)
+    if len(out_refs) > 1:
+        out_refs[1][...] = map_refs[1][:, rank:]
     tags = jnp.concatenate([t[...] for t in tag_refs], axis=0)
     pick = one_hot(iota((16, LANES), 1) == LANES // 2)
     slots = lax.dot_general(pick, tags, NT, preferred_element_type=jnp.float32)[:1]
@@ -163,7 +171,7 @@
     total, columns = out_ref.shape
     whole = columns // 256 * 256
     depth = weight_ref.shape[0]
-    chunk = 1024
+    chunk = 512
     copies = [
         pltpu.make_async_copy(
             weight_hbm.at[part * depth + k : part * depth + k + chunk],
@@ -272,52 +280,57 @@
         projection_weight.shape[1]: pltpu.CompilerParams(vmem_limit_bytes=limit(total, 52)),
         output_weight.shape[1]: pltpu.CompilerParams(vmem_limit_bytes=limit(total, 52)),
     }
-    full = pltpu.CompilerParams(vmem_limit_bytes=limit(total, 60))
+    full = pltpu.CompilerParams(vmem_limit_bytes=limit(total, 58))
     own_maps = jnp.swapaxes(adapter_down, 1, 2)
     sibling_maps = jnp.swapaxes(swap(adapter_down, count, 1), 1, 2)
 
-    normed = pl.pallas_call(
+    normed, first_maps = pl.pallas_call(
         norm_kernel,
-        out_shape=jax.ShapeDtypeStruct((rows, width + LANES), bf16),
-        in_specs=[spec(pltpu.HBM)] * 4,
-        out_specs=spec(),
+        out_shape=[
+            VMEM((rows, width + LANES), bf16),
+            VMEM((held, 3 * rank, width), bf16),
+        ],
+        in_specs=[spec(pltpu.HBM)] * 5,
+        out_specs=[spec()] * 2,
         scratch_shapes=[
             VMEM((rows, width), bf16),
             VMEM((width,), bf16),
             SMEM((rows,), jnp.int32),
             SMEM(adapter_storage.shape, jnp.int32),
-            pltpu.SemaphoreType.DMA((4,)),
+            pltpu.SemaphoreType.DMA((5,)),
         ],
         compiler_params=full,
         name="norm",
-    )(input_hidden, input_norm_gain, request_adapter.reshape(rows), adapter_storage)
+    )(input_hidden, input_norm_gain, request_adapter.reshape(rows), adapter_storage, own_maps)
 
     def tag_specs(pieces):
         return [pl.BlockSpec((p.shape[0], LANES), lambda i: (0, width // LANES)) for p in pieces]
 
-    def downs(pieces, tagged, low, high, columns):
+    def downs(own, sibling, pieces, tagged, low, high):
         ranks = high - low
         lanes = max(LANES, total)
+        whole = lambda x: pl.BlockSpec(x.shape, lambda i: (0,) * x.ndim)
+        own_spec = pl.BlockSpec((held, ranks, width), lambda i: (0, low // ranks, 0))
+        shapes = [jax.ShapeDtypeStruct((ranks * total // lanes, lanes), bf16)]
+        if low == 0:
+            rest = sibling.shape[1] - ranks
+            shapes.append(jax.ShapeDtypeStruct((held, rest, width), bf16))
         return pl.pallas_call(
-            functools.partial(down_kernel, count, rows, len(pieces), low),
+            functools.partial(down_kernel, count, rows, len(pieces), (low, high)),
             grid=(1,),
-            out_shape=jax.ShapeDtypeStruct((ranks * total // lanes, lanes), bf16),
-            in_specs=[spec(pl.ANY)] * 2
+            out_shape=shapes,
+            in_specs=[own_spec, whole(sibling)]
             + [pl.BlockSpec((p.shape[0], width), lambda i: (0, 0)) for p in pieces]
             + tag_specs(tagged),
-            out_specs=spec(),
-            scratch_shapes=[
-                VMEM((2, held, ranks, width), bf16),
-                pltpu.SemaphoreType.DMA((2 * (width // 2048),)),
-            ],
-            compiler_params=tight[columns],
+            out_specs=[whole(x) for x in shapes],
+            compiler_params=roomy,
             cost_estimate=pl.CostEstimate(
                 flops=2 * total * width * held * ranks,
                 bytes_accessed=2 * width * (2 * held * ranks + total),
                 transcendentals=0,
             ),
             name="down",
-        )(own_maps, sibling_maps, *pieces, *tagged)
+        )(own, sibling, *pieces, *tagged)
 
     def base(pieces, weight, after, part, parts):
         columns = weight.shape[1]
@@ -328,12 +341,12 @@
             out_specs=spec(),
             scratch_shapes=[
                 VMEM((width // parts, columns), bf16),
-                pltpu.SemaphoreType.DMA((width // parts // 1024,)),
+                pltpu.SemaphoreType.DMA((width // parts // 512,)),
             ],
             compiler_params=tight[columns],
             cost_estimate=pl.CostEstimate(
                 flops=2 * total * width * columns // parts,
-                bytes_accessed=2 * width * columns // parts,
+                bytes_accessed=4 * width * columns // parts,
                 transcendentals=0,
             ),
             name="base",
@@ -354,7 +367,7 @@
             name="lift",
         )(*tagged, *operands)
 
-    def project(x, tagged, low, high, weight, up, bounds):
+    def project(x, tagged, maps, low, high, weight, up, bounds):
         column, pieces = gather_rows(x, count)
         tagged = pieces if tagged is None else tagged
         parts = 2
@@ -362,15 +375,22 @@
         def beside(turn, after):
             return base(pieces, weight, after, turn, parts) if turn < parts else None
 
-        down = downs(column, tagged[: len(column)], low, high, weight.shape[1])
+        down, *rest = downs(*maps, column, tagged[: len(column)], low, high)
         down, base_terms = sum_over(down, count, beside)
         columns = lift(down, tagged, up, base_terms, bounds, high - low)
         mine = exchange(columns)
-        return jnp.swapaxes(mine, 0, 1).reshape(rows, -1), tagged
+        return jnp.swapaxes(mine, 0, 1).reshape(rows, -1), tagged, rest
 
     bounds = (0, width, width + kv_width, width + 2 * kv_width)
-    qkv_mine, tagged = project(
-        normed, None, 0, 3 * rank, projection_weight, projection_up_adapter, bounds
+    qkv_mine, tagged, rest = project(
+        normed,
+        None,
+        (first_maps, sibling_maps),
+        0,
+        3 * rank,
+        projection_weight,
+        projection_up_adapter,
+        bounds,
     )
 
     groups_per = width // head_dim // kv_heads
@@ -398,8 +418,15 @@
     )
     attended = mixed.reshape(rows, width).astype(jnp.bfloat16)
 
-    output, _ = project(
-        attended, tagged, 3 * rank, 4 * rank, output_weight, output_up_adapter, (0, width)
+    output, _, _ = project(
+        attended,
+        tagged,
+        (own_maps, rest[0]),
+        3 * rank,
+        4 * rank,
+        output_weight,
+        output_up_adapter,
+        (0, width),
     )
     return output
 

time: 92.9 us -> 89.7 us (0.966)
  Pallas kernels: 19.9 us -> 16.2 us
    pallas_call x3, Pallas kernels: 7.5 us -> 3.25 us  [the longest x1 1.65 us: local(): pl.pallas_call(norm_kernel, out_shape=[VMEM((rows, width + LANES), bf16),...]
    ppermute x31, starting transfers between devices: 30.8 us -> 31.7 us  [swap(): return lax.ppermute(x, AXIS, [(i, i ^ offset) for i in range(count)])]
    unnamed x29 -> x35, local copies, waits for them, and re-layouts: 2.22 us -> 1.65 us
  transfers between devices with their start and end apart: 31 -> 31, of which waited for: 12 -> 9; matrix products, arithmetic and copies ran while one was open for 2% -> 1% of each run, Pallas kernels for 15% -> 15%
where the time goes in v6:
time: 89.7 us; the launch traced here: 89.4 us
  starting transfers between devices  31.7 us (35%)
  blocking collectives  21.8 us (24%)
  Pallas kernels  16.2 us (18%)
  waiting for transfers between devices  12.3 us (14%)
  matrix products  2.98 us (3%)
  local copies, waits for them, and re-layouts  2.27 us (3%)
  other arithmetic  1.61 us (2%)
    ppermute x31, starting transfers between devices, swap(): return lax.ppermute(x, AXIS, [(i, i ^ offset) for i in range(count)])  31.7 us
    all_to_all x2, blocking collectives, exchange(): lax.all_to_all(x, AXIS, split_axis=0, concat_axis=0, axis_index_groups=gr...  21.8 us
    ppermute x31, waiting for transfers between devices, swap(): return lax.ppermute(x, AXIS, [(i, i ^ offset) for i in range(count)])  12.3 us
    pallas_call x4, Pallas kernels, base(): pl.pallas_call(functools.partial(base_kernel, len(pieces), part), out_sha...  11.6 us
  transfers between devices with their start and end apart: 31, of which 9 were waited for; matrix products, arithmetic and copies ran while one was open for 1% of the time, Pallas kernels for 15%

profile of v6, /device:TPU:0, one launch (start us, length us, event | category | flops | bytes accessed | tf_op | source)
XLA Modules:
  0.0 89.4 jit_solution(14598253090523831781)
XLA Ops:
  0.0 1.6 %norm.1 = (bf16[4,8320]{1,0:T(4,128)(2,1)S(1)}, bf16[2,48,8192]{2,1,0:T(8,128)(2,1)S(1)}) custom-call(bf16[4,8192]{1,0:T(4,128)(2,1)} %hidden_hbm.1, bf16[8192]{0:T(1024)(128)(2,1)} %gain_hbm.1, s32[4]{0:T(128)} %bitcast.50, s32[32]{0:T(128)} %slots_hbm.1, bf16[2,64,8192]{2,1,0:T(8,128)(2,1)} %bitcast.35), custom_call_target="tpu_custom_call" | custom-call | tf_op jit(solution)/shard_map/norm/pallas_call | solution.py:287
  1.7 3.1 %collective-permute-start = (bf16[4,8320]{1,0:T(4,128)(2,1)S(1)}, bf16[4,8320]{1,0:T(4,128)(2,1)S(1)}, u32[]{:S(2)}, u32[]{:S(2)}) collective-permute-start(bf16[4,8320]{1,0:T(4,128)(2,1)S(1)} %get-tuple-element.27), channel_id=1, source_target_pairs={{0,4},{1,5},{2,6},{3,7},{4,0},{5,1},{6,2},{7,3},{8,12},{9,13},{10,... | collective-permute-start | bytes 199688 | tf_op jit(solution)/shard_map/ppermute | solution.py:18
  4.7 2.6 %collective-permute-start.1 = (bf16[4,8320]{1,0:T(4,128)(2,1)S(1)}, bf16[4,8320]{1,0:T(4,128)(2,1)S(1)}, u32[]{:S(2)}, u32[]{:S(2)}) collective-permute-start(bf16[4,8320]{1,0:T(4,128)(2,1)S(1)} %get-tuple-element.27), channel_id=1, source_target_pairs={{0,8},{1,9},{2,10},{3,11},{4,12},{5,13},{6,14},{7,15},{8,0},{9,1},... | collective-permute-start | bytes 199688 | tf_op jit(solution)/shard_map/ppermute | solution.py:18
  7.3 1.7 %collective-permute-start.3 = (bf16[4,8320]{1,0:T(4,128)(2,1)S(1)}, bf16[4,8320]{1,0:T(4,128)(2,1)S(1)}, u32[]{:S(2)}, u32[]{:S(2)}) collective-permute-start(bf16[4,8320]{1,0:T(4,128)(2,1)S(1)} %get-tuple-element.27), channel_id=1, source_target_pairs={{0,2},{1,3},{2,0},{3,1},{4,6},{5,7},{6,4},{7,5},{8,10},{9,11},{10,... | collective-permute-start | bytes 199688 | tf_op jit(solution)/shard_map/ppermute | solution.py:18
  9.1 0.3 collective-permute-start.4
  9.4 2.7 %collective-permute-done.1 = bf16[4,8320]{1,0:T(4,128)(2,1)S(1)} collective-permute-done((bf16[4,8320]{1,0:T(4,128)(2,1)S(1)}, bf16[4,8320]{1,0:T(4,128)(2,1)S(1)}, u32[]{:S(2)}, u32[]{:S(2)}) %collective-permute-start.1) | collective-permute-done | bytes 66592 | tf_op jit(solution)/shard_map/ppermute | solution.py:18
  12.1 1.5 %collective-permute-start.5 = (bf16[4,8320]{1,0:T(4,128)(2,1)S(1)}, bf16[4,8320]{1,0:T(4,128)(2,1)S(1)}, u32[]{:S(2)}, u32[]{:S(2)}) collective-permute-start(bf16[4,8320]{1,0:T(4,128)(2,1)S(1)} %collective-permute-done.1), channel_id=1, source_target_pairs={{0,2},{1,3},{2,0},{3,1},{4,6},{5,7},{6,4},{7,5},{8,10},{9,11},{10,... | collective-permute-start | bytes 199688 | tf_op jit(solution)/shard_map/ppermute | solution.py:18
  13.6 1.4 %collective-permute-start.6 = (bf16[4,8320]{1,0:T(4,128)(2,1)S(1)}, bf16[4,8320]{1,0:T(4,128)(2,1)S(1)}, u32[]{:S(2)}, u32[]{:S(2)}) collective-permute-start(bf16[4,8320]{1,0:T(4,128)(2,1)S(1)} %collective-permute-done.2), channel_id=1, source_target_pairs={{0,2},{1,3},{2,0},{3,1},{4,6},{5,7},{6,4},{7,5},{8,10},{9,11},{10,... | collective-permute-start | bytes 199688 | tf_op jit(solution)/shard_map/ppermute | solution.py:18
  15.0 0.2 pad_maximum_fusion.refs_2_.refs_4_.refs_0_
  15.2 0.1 collective-permute-start.7
  15.3 1.1 %collective-permute-done.5 = bf16[4,8320]{1,0:T(4,128)(2,1)S(1)} collective-permute-done((bf16[4,8320]{1,0:T(4,128)(2,1)S(1)}, bf16[4,8320]{1,0:T(4,128)(2,1)S(1)}, u32[]{:S(2)}, u32[]{:S(2)}) %collective-permute-start.5) | collective-permute-done | bytes 66592 | tf_op jit(solution)/shard_map/ppermute | solution.py:18
  16.4 1.5 %collective-permute-done.6 = bf16[4,8320]{1,0:T(4,128)(2,1)S(1)} collective-permute-done((bf16[4,8320]{1,0:T(4,128)(2,1)S(1)}, bf16[4,8320]{1,0:T(4,128)(2,1)S(1)}, u32[]{:S(2)}, u32[]{:S(2)}) %collective-permute-start.6) | collective-permute-done | bytes 66592 | tf_op jit(solution)/shard_map/ppermute | solution.py:18
  17.8 0.2 pad_maximum_fusion.1.refs_3_.refs_5_.refs_1_
  18.0 0.1 collective-permute-start.8
  18.1 1.1 %down.2 = (bf16[24,128]{1,0:T(8,128)(2,1)S(1)}, bf16[2,16,8192]{2,1,0:T(8,128)(2,1)S(1)}) custom-call(bf16[2,48,8192]{2,1,0:T(8,128)(2,1)S(1)} %get-tuple-element.28.refs_0_, bf16[2,64,8192]{2,1,0:T(8,128)(2,1)S(1)} %bitcast.37, bf16[16,8320]{1,0:T(8,128)(2,1)S(1)} %pad_maximum_fusion.refs_2_.refs_4_.refs_0_, ...), custom_call_target="tpu_custom_call" | custom-call | flops 100663296 | bytes 4194304 | tf_op jit(solution)/shard_map/down/pallas_call | solution.py:318
  19.2 0.8 copy-done.10
  20.1 0.4 collective-permute-start.10
  20.4 3.4 %collective-permute-start.11 = (bf16[24,128]{1,0:T(8,128)(2,1)S(1)}, bf16[24,128]{1,0:T(8,128)(2,1)S(1)}, u32[]{:S(2)}, u32[]{:S(2)}) collective-permute-start(bf16[24,128]{1,0:T(8,128)(2,1)S(1)} %get-tuple-element.30.refs_5_), channel_id=1, source_target_pairs={{0,8},{1,9},{2,10},{3,11},{4,12},{5,13},{6,14},{7,15},{8,0},{9,1},... | collective-permute-start | bytes 18440 | tf_op jit(solution)/shard_map/ppermute | solution.py:18
  23.8 0.6 collective-permute-start.12
  24.5 3.5 %base.4.refs_6_ = f32[64,640]{1,0:T(8,128)S(1)} custom-call(bf16[16,8320]{1,0:T(8,128)(2,1)S(1)} %pad_maximum_fusion.refs_2_.refs_4_.refs_0_, bf16[16,8320]{1,0:T(8,128)(2,1)S(1)} %pad_maximum_fusion.1.refs_3_.refs_5_.refs_1_, bf16[16,8320]{1,0:T(8,128)(2,1)S(1)} %collective-permute-done.7.refs_2_, bf16[16,8320]{1,0:T(8,128)(2,1)S(1)} %collective-permute-done.8.refs_3_, ...), custom_call_target="tpu_custom_call" | custom-call | flops 335544320 | bytes 10485760 | tf_op jit(solution)/shard_map/base/pallas_call | solution.py:337
  28.0 1.3 %collective-permute-done.12 = bf16[24,128]{1,0:T(8,128)(2,1)S(1)} collective-permute-done((bf16[24,128]{1,0:T(8,128)(2,1)S(1)}, bf16[24,128]{1,0:T(8,128)(2,1)S(1)}, u32[]{:S(2)}, u32[]{:S(2)}) %collective-permute-start.12) | collective-permute-done | bytes 6176 | tf_op jit(solution)/shard_map/ppermute | solution.py:18
  29.3 0.0 copy-start.8
  29.3 0.0 copy-start.14
  29.3 0.1 collective-permute-start.13
  29.4 0.8 collective-permute-start.14
  30.1 1.1 %collective-permute-start.15 = (bf16[24,128]{1,0:T(8,128)(2,1)S(1)}, bf16[24,128]{1,0:T(8,128)(2,1)S(1)}, u32[]{:S(2)}, u32[]{:S(2)}) collective-permute-start(bf16[24,128]{1,0:T(8,128)(2,1)S(1)} %add_add_fusion.1.refs_5_), channel_id=1, source_target_pairs={{0,3},{1,2},{2,1},{3,0},{4,7},{5,6},{6,5},{7,4},{8,11},{9,10},{10,... | collective-permute-start | bytes 18440 | tf_op jit(solution)/shard_map/ppermute | solution.py:18
  31.2 3.3 %base.5.refs_7_ = f32[64,640]{1,0:T(8,128)S(1)} custom-call(bf16[16,8320]{1,0:T(8,128)(2,1)S(1)} %pad_maximum_fusion.refs_2_.refs_4_.refs_0_, bf16[16,8320]{1,0:T(8,128)(2,1)S(1)} %pad_maximum_fusion.1.refs_3_.refs_5_.refs_1_, bf16[16,8320]{1,0:T(8,128)(2,1)S(1)} %collective-permute-done.7.refs_2_, bf16[16,8320]{1,0:T(8,128)(2,1)S(1)} %collective-permute-done.8.refs_3_, ...), custom_call_target="tpu_custom_call" | custom-call | flops 335544320 | bytes 10485760 | tf_op jit(solution)/shard_map/base/pallas_call | solution.py:337
  34.6 0.7 lift.2
  35.3 10.8 %all_to_all.10 = bf16[16,4,640]{2,1,0:T(4,128)(2,1)S(1)} all-to-all(bf16[16,4,640]{2,1,0:T(4,128)(2,1)S(1)} %lift.2), channel_id=1, replica_groups=mesh['groups'=2,'tensor'=16] {'tensor'}, dimensions={0} | all-to-all | bytes 163840 | tf_op jit(solution)/shard_map/all_to_all | solution.py:22
  46.1 0.6 convert_bitcast_fusion
  46.7 0.6 reshape.54
  47.3 0.1 iota_compare_fusion
  47.4 1.0 %fusion.9 = f32[4,8,1,8]{3,2,1,0:T(1,128)S(1)} fusion(bf16[4,8,8,128]{3,2,1,0:T(8,128)(2,1)S(1)} %bitcast.49, bf16[4,8,128,1]{2,3,1,0:T(2,128)(2,1)} %reshape.54), kind=kOutput, calls=%fused_computation.30 | convolution fusion | flops 65536 | bytes 74752 | tf_op jit(solution)/shard_map/bhgd,bhd->bhg/dot_general | solution.py:407
  48.4 1.3 %fusion.8 = (f32[4,8,8]{2,1,0:T(8,128)S(1)}, f32[4,8,8,384]{3,2,1,0:T(8,128)S(1)}) fusion(bf16[4,8,384,128]{3,2,1,0:T(8,128)(2,1)S(1)} %copy-done, bf16[1,4,64,128]{3,1,2,0:T(4,128)(2,1)S(1)} %slice_bitcast_fusion, pred[4,384]{1,0:T(4,128)(4,1)S(1)} %iota_compare_fusion), kind=kOutput, calls=%fused_computation.29 | convolution fusion | flops 25460480 | bytes 3607040 | tf_op jit(solution)/shard_map/bhgd,bhpd->bhgp/dot_general | solution.py:402
  49.7 0.2 fusion.3
  50.0 0.7 fusion.2
  50.7 0.1 copy.24
  50.8 0.1 collective-permute-start.16
  50.9 1.2 %collective-permute-start.17 = (bf16[4,8192]{1,0:T(4,128)(2,1)S(1)}, bf16[4,8192]{1,0:T(4,128)(2,1)S(1)}, u32[]{:S(2)}, u32[]{:S(2)}) collective-permute-start(bf16[4,8192]{1,0:T(4,128)(2,1)S(1)} %bitcast.42), channel_id=1, source_target_pairs={{0,8},{1,9},{2,10},{3,11},{4,12},{5,13},{6,14},{7,15},{8,0},{9,1},... | collective-permute-start | bytes 196616 | tf_op jit(solution)/shard_map/ppermute | solution.py:18
  52.0 3.2 %collective-permute-start.18 = (bf16[4,8192]{1,0:T(4,128)(2,1)S(1)}, bf16[4,8192]{1,0:T(4,128)(2,1)S(1)}, u32[]{:S(2)}, u32[]{:S(2)}) collective-permute-start(bf16[4,8192]{1,0:T(4,128)(2,1)S(1)} %bitcast.43), channel_id=1, source_target_pairs={{0,12},{1,13},{2,14},{3,15},{4,8},{5,9},{6,10},{7,11},{8,4},{9,5},... | collective-permute-start | bytes 196616 | tf_op jit(solution)/shard_map/ppermute | solution.py:18
  55.3 0.4 collective-permute-done.16
  55.7 1.6 %collective-permute-start.20 = (bf16[4,8192]{1,0:T(4,128)(2,1)S(1)}, bf16[4,8192]{1,0:T(4,128)(2,1)S(1)}, u32[]{:S(2)}, u32[]{:S(2)}) collective-permute-start(bf16[4,8192]{1,0:T(4,128)(2,1)S(1)} %collective-permute-done.16), channel_id=1, source_target_pairs={{0,2},{1,3},{2,0},{3,1},{4,6},{5,7},{6,4},{7,5},{8,10},{9,11},{10,... | collective-permute-start | bytes 196616 | tf_op jit(solution)/shard_map/ppermute | solution.py:18
  57.3 1.9 %collective-permute-done.17 = bf16[4,8192]{1,0:T(4,128)(2,1)S(1)} collective-permute-done((bf16[4,8192]{1,0:T(4,128)(2,1)S(1)}, bf16[4,8192]{1,0:T(4,128)(2,1)S(1)}, u32[]{:S(2)}, u32[]{:S(2)}) %collective-permute-start.17) | collective-permute-done | bytes 65568 | tf_op jit(solution)/shard_map/ppermute | solution.py:18
  59.2 0.7 collective-permute-start.21
  59.8 1.4 %collective-permute-start.22 = (bf16[4,8192]{1,0:T(4,128)(2,1)S(1)}, bf16[4,8192]{1,0:T(4,128)(2,1)S(1)}, u32[]{:S(2)}, u32[]{:S(2)}) collective-permute-start(bf16[4,8192]{1,0:T(4,128)(2,1)S(1)} %collective-permute-done.18), channel_id=1, source_target_pairs={{0,2},{1,3},{2,0},{3,1},{4,6},{5,7},{6,4},{7,5},{8,10},{9,11},{10,... | collective-permute-start | bytes 196616 | tf_op jit(solution)/shard_map/ppermute | solution.py:18
  61.2 0.2 pad_maximum_fusion.2.refs_2_.refs_0_
  61.4 0.1 collective-permute-start.26
  61.5 2.0 %collective-permute-done.21 = bf16[4,8192]{1,0:T(4,128)(2,1)S(1)} collective-permute-done((bf16[4,8192]{1,0:T(4,128)(2,1)S(1)}, bf16[4,8192]{1,0:T(4,128)(2,1)S(1)}, u32[]{:S(2)}, u32[]{:S(2)}) %collective-permute-start.21) | collective-permute-done | bytes 65568 | tf_op jit(solution)/shard_map/ppermute | solution.py:18
  63.4 0.7 collective-permute-done.22
  64.1 0.2 pad_maximum_fusion.3.refs_3_.refs_1_
  64.3 0.1 collective-permute-start.27
  64.4 0.5 down.3.refs_5_
  64.9 0.6 collective-permute-start.23
  65.6 1.6 %collective-permute-start.24 = (bf16[8,128]{1,0:T(8,128)(2,1)S(1)}, bf16[8,128]{1,0:T(8,128)(2,1)S(1)}, u32[]{:S(2)}, u32[]{:S(2)}) collective-permute-start(bf16[8,128]{1,0:T(8,128)(2,1)S(1)} %down.3.refs_5_), channel_id=1, source_target_pairs={{0,8},{1,9},{2,10},{3,11},{4,12},{5,13},{6,14},{7,15},{8,0},{9,1},... | collective-permute-start | bytes 6152 | tf_op jit(solution)/shard_map/ppermute | solution.py:18
  67.2 2.2 %collective-permute-start.25 = (bf16[8,128]{1,0:T(8,128)(2,1)S(1)}, bf16[8,128]{1,0:T(8,128)(2,1)S(1)}, u32[]{:S(2)}, u32[]{:S(2)}) collective-permute-start(bf16[8,128]{1,0:T(8,128)(2,1)S(1)} %down.3.refs_5_), channel_id=1, source_target_pairs={{0,12},{1,13},{2,14},{3,15},{4,8},{5,9},{6,10},{7,11},{8,4},{9,5},... | collective-permute-start | bytes 6152 | tf_op jit(solution)/shard_map/ppermute | solution.py:18
  69.4 2.4 %base.6.refs_6_ = f32[64,512]{1,0:T(8,128)S(1)} custom-call(bf16[16,8192]{1,0:T(8,128)(2,1)S(1)} %pad_maximum_fusion.2.refs_2_.refs_0_, bf16[16,8192]{1,0:T(8,128)(2,1)S(1)} %pad_maximum_fusion.3.refs_3_.refs_1_, bf16[16,8192]{1,0:T(8,128)(2,1)S(1)} %collective-permute-done.26.refs_2_, bf16[16,8192]{1,0:T(8,128)(2,1)S(1)} %collective-permute-done.27.refs_3_, ...), custom_call_target="tpu_custom_call" | custom-call | flops 268435456 | bytes 8388608 | tf_op jit(solution)/shard_map/base/pallas_call | solution.py:337
  71.9 0.7 collective-permute-done.25
  72.6 0.1 collective-permute-start.28
  72.7 0.8 collective-permute-start.29
  73.4 1.1 %collective-permute-start.30 = (bf16[8,128]{1,0:T(8,128)(2,1)S(1)}, bf16[8,128]{1,0:T(8,128)(2,1)S(1)}, u32[]{:S(2)}, u32[]{:S(2)}) collective-permute-start(bf16[8,128]{1,0:T(8,128)(2,1)S(1)} %add_add_fusion.3.refs_5_), channel_id=1, source_target_pairs={{0,3},{1,2},{2,1},{3,0},{4,7},{5,6},{6,5},{7,4},{8,11},{9,10},{10,... | collective-permute-start | bytes 6152 | tf_op jit(solution)/shard_map/ppermute | solution.py:18
  74.5 2.4 %base.7.refs_7_ = f32[64,512]{1,0:T(8,128)S(1)} custom-call(bf16[16,8192]{1,0:T(8,128)(2,1)S(1)} %pad_maximum_fusion.2.refs_2_.refs_0_, bf16[16,8192]{1,0:T(8,128)(2,1)S(1)} %pad_maximum_fusion.3.refs_3_.refs_1_, bf16[16,8192]{1,0:T(8,128)(2,1)S(1)} %collective-permute-done.26.refs_2_, bf16[16,8192]{1,0:T(8,128)(2,1)S(1)} %collective-permute-done.27.refs_3_, ...), custom_call_target="tpu_custom_call" | custom-call | flops 268435456 | bytes 8388608 | tf_op jit(solution)/shard_map/base/pallas_call | solution.py:337
  77.0 0.6 lift.3
  77.7 11.1 %all_to_all.11 = bf16[16,4,512]{2,1,0:T(4,128)(2,1)S(1)} all-to-all(bf16[16,4,512]{2,1,0:T(4,128)(2,1)S(1)} %lift.3), channel_id=1, replica_groups=mesh['groups'=2,'tensor'=16] {'tensor'}, dimensions={0} | all-to-all | bytes 131072 | tf_op jit(solution)/shard_map/all_to_all | solution.py:22
  88.7 0.6 copy.28
  (61 shorter events, 0.2 us)
Async XLA Ops:
  0.0 48.4 %copy-start = (bf16[4,8,384,128]{3,2,1,0:T(8,128)(2,1)S(1)}, bf16[4,8,384,128]{3,2,1,0:T(8,128)(2,1)}, u32[]{:S(2)}) copy-start(bf16[4,8,384,128]{3,2,1,0:T(8,128)(2,1)} %param.22) | copy-start | bytes 9437188
  1.7 7.4 %collective-permute-start = (bf16[4,8320]{1,0:T(4,128)(2,1)S(1)}, bf16[4,8320]{1,0:T(4,128)(2,1)S(1)}, u32[]{:S(2)}, u32[]{:S(2)}) collective-permute-start(bf16[4,8320]{1,0:T(4,128)(2,1)S(1)} %get-tuple-element.27), channel_id=1, source_target_pairs={{0,4},{1,5},{2,6},{3,7},{4,0},{5,1},{6,2},{7,3},{8,12},{9,13},{10,... | collective-permute-start | bytes 199688 | tf_op jit(solution)/shard_map/ppermute | solution.py:18
  4.7 7.3 %collective-permute-start.1 = (bf16[4,8320]{1,0:T(4,128)(2,1)S(1)}, bf16[4,8320]{1,0:T(4,128)(2,1)S(1)}, u32[]{:S(2)}, u32[]{:S(2)}) collective-permute-start(bf16[4,8320]{1,0:T(4,128)(2,1)S(1)} %get-tuple-element.27), channel_id=1, source_target_pairs={{0,8},{1,9},{2,10},{3,11},{4,12},{5,13},{6,14},{7,15},{8,0},{9,1},... | collective-permute-start | bytes 199688 | tf_op jit(solution)/shard_map/ppermute | solution.py:18
  7.3 6.2 %collective-permute-start.2 = (bf16[4,8320]{1,0:T(4,128)(2,1)S(1)}, bf16[4,8320]{1,0:T(4,128)(2,1)S(1)}, u32[]{:S(2)}, u32[]{:S(2)}) collective-permute-start(bf16[4,8320]{1,0:T(4,128)(2,1)S(1)} %get-tuple-element.27), channel_id=1, source_target_pairs={{0,12},{1,13},{2,14},{3,15},{4,8},{5,9},{6,10},{7,11},{8,4},{9,5},... | collective-permute-start | bytes 199688 | tf_op jit(solution)/shard_map/ppermute | solution.py:18
  7.3 7.8 %collective-permute-start.3 = (bf16[4,8320]{1,0:T(4,128)(2,1)S(1)}, bf16[4,8320]{1,0:T(4,128)(2,1)S(1)}, u32[]{:S(2)}, u32[]{:S(2)}) collective-permute-start(bf16[4,8320]{1,0:T(4,128)(2,1)S(1)} %get-tuple-element.27), channel_id=1, source_target_pairs={{0,2},{1,3},{2,0},{3,1},{4,6},{5,7},{6,4},{7,5},{8,10},{9,11},{10,... | collective-permute-start | bytes 199688 | tf_op jit(solution)/shard_map/ppermute | solution.py:18
  9.1 9.1 %collective-permute-start.9 = (bf16[2,8192,64]{1,2,0:T(8,128)(2,1)}, bf16[2,8192,64]{1,2,0:T(8,128)(2,1)S(1)}, u32[]{:S(2)}, u32[]{:S(2)}) collective-permute-start(bf16[2,8192,64]{1,2,0:T(8,128)(2,1)} %param.19), channel_id=1, source_target_pairs={{0,1},{1,0},{2,3},{3,2},{4,5},{5,4},{6,7},{7,6},{8,9},{9,8},{10,11... | collective-permute-start | bytes 6291464 | tf_op jit(solution)/shard_map/ppermute | solution.py:18
  9.1 6.2 %collective-permute-start.4 = (bf16[4,8320]{1,0:T(4,128)(2,1)S(1)}, bf16[4,8320]{1,0:T(4,128)(2,1)S(1)}, u32[]{:S(2)}, u32[]{:S(2)}) collective-permute-start(bf16[4,8320]{1,0:T(4,128)(2,1)S(1)} %collective-permute-done), channel_id=1, source_target_pairs={{0,2},{1,3},{2,0},{3,1},{4,6},{5,7},{6,4},{7,5},{8,10},{9,11},{10,... | collective-permute-start | bytes 199688 | tf_op jit(solution)/shard_map/ppermute | solution.py:18
  12.1 4.3 %collective-permute-start.5 = (bf16[4,8320]{1,0:T(4,128)(2,1)S(1)}, bf16[4,8320]{1,0:T(4,128)(2,1)S(1)}, u32[]{:S(2)}, u32[]{:S(2)}) collective-permute-start(bf16[4,8320]{1,0:T(4,128)(2,1)S(1)} %collective-permute-done.1), channel_id=1, source_target_pairs={{0,2},{1,3},{2,0},{3,1},{4,6},{5,7},{6,4},{7,5},{8,10},{9,11},{10,... | collective-permute-start | bytes 199688 | tf_op jit(solution)/shard_map/ppermute | solution.py:18
  13.6 4.3 %collective-permute-start.6 = (bf16[4,8320]{1,0:T(4,128)(2,1)S(1)}, bf16[4,8320]{1,0:T(4,128)(2,1)S(1)}, u32[]{:S(2)}, u32[]{:S(2)}) collective-permute-start(bf16[4,8320]{1,0:T(4,128)(2,1)S(1)} %collective-permute-done.2), channel_id=1, source_target_pairs={{0,2},{1,3},{2,0},{3,1},{4,6},{5,7},{6,4},{7,5},{8,10},{9,11},{10,... | collective-permute-start | bytes 199688 | tf_op jit(solution)/shard_map/ppermute | solution.py:18
  15.2 9.3 %collective-permute-start.7 = (bf16[16,8320]{1,0:T(8,128)(2,1)S(1)}, bf16[16,8320]{1,0:T(8,128)(2,1)S(1)}, u32[]{:S(2)}, u32[]{:S(2)}) collective-permute-start(bf16[16,8320]{1,0:T(8,128)(2,1)S(1)} %pad_maximum_fusion.refs_2_.refs_4_.refs_0_), channel_id=1, source_target_pairs={{0,1},{1,0},{2,3},{3,2},{4,5},{5,4},{6,7},{7,6},{8,9},{9,8},{10,11... | collective-permute-start | bytes 798728 | tf_op jit(solution)/shard_map/ppermute | solution.py:18
  18.0 16.6 %copy-start.1 = (bf16[16,8320]{1,0:T(8,128)(2,1)}, bf16[16,8320]{1,0:T(8,128)(2,1)S(1)}, u32[]{:S(2)}) copy-start(bf16[16,8320]{1,0:T(8,128)(2,1)S(1)} %pad_maximum_fusion.1.refs_3_.refs_5_.refs_1_) | copy-start | bytes 798724
  18.0 6.4 %collective-permute-start.8 = (bf16[16,8320]{1,0:T(8,128)(2,1)S(1)}, bf16[16,8320]{1,0:T(8,128)(2,1)S(1)}, u32[]{:S(2)}, u32[]{:S(2)}) collective-permute-start(bf16[16,8320]{1,0:T(8,128)(2,1)S(1)} %pad_maximum_fusion.1.refs_3_.refs_5_.refs_1_), channel_id=1, source_target_pairs={{0,1},{1,0},{2,3},{3,2},{4,5},{5,4},{6,7},{7,6},{8,9},{9,8},{10,11... | collective-permute-start | bytes 798728 | tf_op jit(solution)/shard_map/ppermute | solution.py:18
  19.2 0.9 copy-start.10
  20.1 7.9 %collective-permute-start.10 = (bf16[24,128]{1,0:T(8,128)(2,1)S(1)}, bf16[24,128]{1,0:T(8,128)(2,1)S(1)}, u32[]{:S(2)}, u32[]{:S(2)}) collective-permute-start(bf16[24,128]{1,0:T(8,128)(2,1)S(1)} %get-tuple-element.30.refs_5_), channel_id=1, source_target_pairs={{0,4},{1,5},{2,6},{3,7},{4,0},{5,1},{6,2},{7,3},{8,12},{9,13},{10,... | collective-permute-start | bytes 18440 | tf_op jit(solution)/shard_map/ppermute | solution.py:18
  20.4 7.6 %collective-permute-start.11 = (bf16[24,128]{1,0:T(8,128)(2,1)S(1)}, bf16[24,128]{1,0:T(8,128)(2,1)S(1)}, u32[]{:S(2)}, u32[]{:S(2)}) collective-permute-start(bf16[24,128]{1,0:T(8,128)(2,1)S(1)} %get-tuple-element.30.refs_5_), channel_id=1, source_target_pairs={{0,8},{1,9},{2,10},{3,11},{4,12},{5,13},{6,14},{7,15},{8,0},{9,1},... | collective-permute-start | bytes 18440 | tf_op jit(solution)/shard_map/ppermute | solution.py:18
  23.8 5.4 %collective-permute-start.12 = (bf16[24,128]{1,0:T(8,128)(2,1)S(1)}, bf16[24,128]{1,0:T(8,128)(2,1)S(1)}, u32[]{:S(2)}, u32[]{:S(2)}) collective-permute-start(bf16[24,128]{1,0:T(8,128)(2,1)S(1)} %get-tuple-element.30.refs_5_), channel_id=1, source_target_pairs={{0,12},{1,13},{2,14},{3,15},{4,8},{5,9},{6,10},{7,11},{8,4},{9,5},... | collective-permute-start | bytes 18440 | tf_op jit(solution)/shard_map/ppermute | solution.py:18
  24.4 10.1 %copy-start.4 = (bf16[16,8320]{1,0:T(8,128)(2,1)}, bf16[16,8320]{1,0:T(8,128)(2,1)S(1)}, u32[]{:S(2)}) copy-start(bf16[16,8320]{1,0:T(8,128)(2,1)S(1)} %collective-permute-done.7.refs_2_) | copy-start | bytes 798724
  24.5 10.1 %copy-start.6 = (bf16[16,8320]{1,0:T(8,128)(2,1)}, bf16[16,8320]{1,0:T(8,128)(2,1)S(1)}, u32[]{:S(2)}) copy-start(bf16[16,8320]{1,0:T(8,128)(2,1)S(1)} %collective-permute-done.8.refs_3_) | copy-start | bytes 798724
  29.3 5.4 %copy-start.8 = (bf16[32,16,640]{2,1,0:T(8,128)(2,1)S(1)}, bf16[32,16,640]{2,1,0:T(8,128)(2,1)}, u32[]{:S(2)}) copy-start(bf16[32,16,640]{2,1,0:T(8,128)(2,1)} %refs_5_.2) | copy-start | bytes 1966084
  29.3 18.1 %copy-start.14 = (s32[4]{0:T(128)S(1)}, s32[4]{0:T(128)}, u32[]{:S(2)}) copy-start(s32[4]{0:T(128)} %param.16) | copy-start | bytes 52
  29.3 5.3 %collective-permute-start.13 = (bf16[24,128]{1,0:T(8,128)(2,1)S(1)}, bf16[24,128]{1,0:T(8,128)(2,1)S(1)}, u32[]{:S(2)}, u32[]{:S(2)}) collective-permute-start(bf16[24,128]{1,0:T(8,128)(2,1)S(1)} %add_add_fusion.1.refs_5_), channel_id=1, source_target_pairs={{0,1},{1,0},{2,3},{3,2},{4,5},{5,4},{6,7},{7,6},{8,9},{9,8},{10,11... | collective-permute-start | bytes 18440 | tf_op jit(solution)/shard_map/ppermute | solution.py:18
  29.4 5.2 %collective-permute-start.14 = (bf16[24,128]{1,0:T(8,128)(2,1)S(1)}, bf16[24,128]{1,0:T(8,128)(2,1)S(1)}, u32[]{:S(2)}, u32[]{:S(2)}) collective-permute-start(bf16[24,128]{1,0:T(8,128)(2,1)S(1)} %add_add_fusion.1.refs_5_), channel_id=1, source_target_pairs={{0,2},{1,3},{2,0},{3,1},{4,6},{5,7},{6,4},{7,5},{8,10},{9,11},{10,... | collective-permute-start | bytes 18440 | tf_op jit(solution)/shard_map/ppermute | solution.py:18
  30.1 4.4 %collective-permute-start.15 = (bf16[24,128]{1,0:T(8,128)(2,1)S(1)}, bf16[24,128]{1,0:T(8,128)(2,1)S(1)}, u32[]{:S(2)}, u32[]{:S(2)}) collective-permute-start(bf16[24,128]{1,0:T(8,128)(2,1)S(1)} %add_add_fusion.1.refs_5_), channel_id=1, source_target_pairs={{0,3},{1,2},{2,1},{3,0},{4,7},{5,6},{6,5},{7,4},{8,11},{9,10},{10,... | collective-permute-start | bytes 18440 | tf_op jit(solution)/shard_map/ppermute | solution.py:18
  47.3 2.7 %copy-start.13 = (f32[1,4,8,128]{3,1,2,0:T(4,128)S(1)}, f32[1,4,8,128]{3,1,2,0:T(4,128)}, u32[]{:S(2)}) copy-start(f32[1,4,8,128]{3,1,2,0:T(4,128)} %get-tuple-element.49) | copy-start | bytes 49156
  47.3 2.7 %copy-start.12 = (bf16[4,8,384,128]{3,2,1,0:T(8,128)(2,1)S(1)}, bf16[4,8,384,128]{3,2,1,0:T(8,128)(2,1)}, u32[]{:S(2)}) copy-start(bf16[4,8,384,128]{3,2,1,0:T(8,128)(2,1)} %param.23) | copy-start | bytes 9437188
  49.7 14.7 %copy-start.2 = (bf16[16,8320]{1,0:T(8,128)(2,1)S(1)}, bf16[16,8320]{1,0:T(8,128)(2,1)}, u32[]{:S(2)}) copy-start(bf16[16,8320]{1,0:T(8,128)(2,1)} %copy-done.1) | copy-start | bytes 798724
  49.7 14.7 %copy-start.3 = (bf16[2,8192,64]{1,2,0:T(8,128)(2,1)S(1)}, bf16[2,8192,64]{1,2,0:T(8,128)(2,1)}, u32[]{:S(2)}) copy-start(bf16[2,8192,64]{1,2,0:T(8,128)(2,1)} %param.19) | copy-start | bytes 6291460
  49.7 14.7 %copy-start.11 = (bf16[2,16,8192]{2,1,0:T(8,128)(2,1)S(1)}, bf16[2,16,8192]{2,1,0:T(8,128)(2,1)}, u32[]{:S(2)}) copy-start(bf16[2,16,8192]{2,1,0:T(8,128)(2,1)} %copy-done.10) | copy-start | bytes 1572868
  50.8 4.8 %collective-permute-start.16 = (bf16[4,8192]{1,0:T(4,128)(2,1)S(1)}, bf16[4,8192]{1,0:T(4,128)(2,1)S(1)}, u32[]{:S(2)}, u32[]{:S(2)}) collective-permute-start(bf16[4,8192]{1,0:T(4,128)(2,1)S(1)} %bitcast.41), channel_id=1, source_target_pairs={{0,4},{1,5},{2,6},{3,7},{4,0},{5,1},{6,2},{7,3},{8,12},{9,13},{10,... | collective-permute-start | bytes 196616 | tf_op jit(solution)/shard_map/ppermute | solution.py:18
  50.9 8.3 %collective-permute-start.17 = (bf16[4,8192]{1,0:T(4,128)(2,1)S(1)}, bf16[4,8192]{1,0:T(4,128)(2,1)S(1)}, u32[]{:S(2)}, u32[]{:S(2)}) collective-permute-start(bf16[4,8192]{1,0:T(4,128)(2,1)S(1)} %bitcast.42), channel_id=1, source_target_pairs={{0,8},{1,9},{2,10},{3,11},{4,12},{5,13},{6,14},{7,15},{8,0},{9,1},... | collective-permute-start | bytes 196616 | tf_op jit(solution)/shard_map/ppermute | solution.py:18
  52.0 7.8 %collective-permute-start.18 = (bf16[4,8192]{1,0:T(4,128)(2,1)S(1)}, bf16[4,8192]{1,0:T(4,128)(2,1)S(1)}, u32[]{:S(2)}, u32[]{:S(2)}) collective-permute-start(bf16[4,8192]{1,0:T(4,128)(2,1)S(1)} %bitcast.43), channel_id=1, source_target_pairs={{0,12},{1,13},{2,14},{3,15},{4,8},{5,9},{6,10},{7,11},{8,4},{9,5},... | collective-permute-start | bytes 196616 | tf_op jit(solution)/shard_map/ppermute | solution.py:18
  55.3 6.2 %collective-permute-start.19 = (bf16[4,8192]{1,0:T(4,128)(2,1)S(1)}, bf16[4,8192]{1,0:T(4,128)(2,1)S(1)}, u32[]{:S(2)}, u32[]{:S(2)}) collective-permute-start(bf16[4,8192]{1,0:T(4,128)(2,1)S(1)} %bitcast.44), channel_id=1, source_target_pairs={{0,2},{1,3},{2,0},{3,1},{4,6},{5,7},{6,4},{7,5},{8,10},{9,11},{10,... | collective-permute-start | bytes 196616 | tf_op jit(solution)/shard_map/ppermute | solution.py:18
  55.7 5.8 %collective-permute-start.20 = (bf16[4,8192]{1,0:T(4,128)(2,1)S(1)}, bf16[4,8192]{1,0:T(4,128)(2,1)S(1)}, u32[]{:S(2)}, u32[]{:S(2)}) collective-permute-start(bf16[4,8192]{1,0:T(4,128)(2,1)S(1)} %collective-permute-done.16), channel_id=1, source_target_pairs={{0,2},{1,3},{2,0},{3,1},{4,6},{5,7},{6,4},{7,5},{8,10},{9,11},{10,... | collective-permute-start | bytes 196616 | tf_op jit(solution)/shard_map/ppermute | solution.py:18
  59.2 4.3 %collective-permute-start.21 = (bf16[4,8192]{1,0:T(4,128)(2,1)S(1)}, bf16[4,8192]{1,0:T(4,128)(2,1)S(1)}, u32[]{:S(2)}, u32[]{:S(2)}) collective-permute-start(bf16[4,8192]{1,0:T(4,128)(2,1)S(1)} %collective-permute-done.17), channel_id=1, source_target_pairs={{0,2},{1,3},{2,0},{3,1},{4,6},{5,7},{6,4},{7,5},{8,10},{9,11},{10,... | collective-permute-start | bytes 196616 | tf_op jit(solution)/shard_map/ppermute | solution.py:18
  59.8 4.3 %collective-permute-start.22 = (bf16[4,8192]{1,0:T(4,128)(2,1)S(1)}, bf16[4,8192]{1,0:T(4,128)(2,1)S(1)}, u32[]{:S(2)}, u32[]{:S(2)}) collective-permute-start(bf16[4,8192]{1,0:T(4,128)(2,1)S(1)} %collective-permute-done.18), channel_id=1, source_target_pairs={{0,2},{1,3},{2,0},{3,1},{4,6},{5,7},{6,4},{7,5},{8,10},{9,11},{10,... | collective-permute-start | bytes 196616 | tf_op jit(solution)/shard_map/ppermute | solution.py:18
  61.4 8.0 %collective-permute-start.26 = (bf16[16,8192]{1,0:T(8,128)(2,1)S(1)}, bf16[16,8192]{1,0:T(8,128)(2,1)S(1)}, u32[]{:S(2)}, u32[]{:S(2)}) collective-permute-start(bf16[16,8192]{1,0:T(8,128)(2,1)S(1)} %pad_maximum_fusion.2.refs_2_.refs_0_), channel_id=1, source_target_pairs={{0,1},{1,0},{2,3},{3,2},{4,5},{5,4},{6,7},{7,6},{8,9},{9,8},{10,11... | collective-permute-start | bytes 786440 | tf_op jit(solution)/shard_map/ppermute | solution.py:18
  64.3 5.1 %collective-permute-start.27 = (bf16[16,8192]{1,0:T(8,128)(2,1)S(1)}, bf16[16,8192]{1,0:T(8,128)(2,1)S(1)}, u32[]{:S(2)}, u32[]{:S(2)}) collective-permute-start(bf16[16,8192]{1,0:T(8,128)(2,1)S(1)} %pad_maximum_fusion.3.refs_3_.refs_1_), channel_id=1, source_target_pairs={{0,1},{1,0},{2,3},{3,2},{4,5},{5,4},{6,7},{7,6},{8,9},{9,8},{10,11... | collective-permute-start | bytes 786440 | tf_op jit(solution)/shard_map/ppermute | solution.py:18
  64.9 6.9 %collective-permute-start.23 = (bf16[8,128]{1,0:T(8,128)(2,1)S(1)}, bf16[8,128]{1,0:T(8,128)(2,1)S(1)}, u32[]{:S(2)}, u32[]{:S(2)}) collective-permute-start(bf16[8,128]{1,0:T(8,128)(2,1)S(1)} %down.3.refs_5_), channel_id=1, source_target_pairs={{0,4},{1,5},{2,6},{3,7},{4,0},{5,1},{6,2},{7,3},{8,12},{9,13},{10,... | collective-permute-start | bytes 6152 | tf_op jit(solution)/shard_map/ppermute | solution.py:18
  65.6 6.3 %collective-permute-start.24 = (bf16[8,128]{1,0:T(8,128)(2,1)S(1)}, bf16[8,128]{1,0:T(8,128)(2,1)S(1)}, u32[]{:S(2)}, u32[]{:S(2)}) collective-permute-start(bf16[8,128]{1,0:T(8,128)(2,1)S(1)} %down.3.refs_5_), channel_id=1, source_target_pairs={{0,8},{1,9},{2,10},{3,11},{4,12},{5,13},{6,14},{7,15},{8,0},{9,1},... | collective-permute-start | bytes 6152 | tf_op jit(solution)/shard_map/ppermute | solution.py:18
  67.2 5.4 %collective-permute-start.25 = (bf16[8,128]{1,0:T(8,128)(2,1)S(1)}, bf16[8,128]{1,0:T(8,128)(2,1)S(1)}, u32[]{:S(2)}, u32[]{:S(2)}) collective-permute-start(bf16[8,128]{1,0:T(8,128)(2,1)S(1)} %down.3.refs_5_), channel_id=1, source_target_pairs={{0,12},{1,13},{2,14},{3,15},{4,8},{5,9},{6,10},{7,11},{8,4},{9,5},... | collective-permute-start | bytes 6152 | tf_op jit(solution)/shard_map/ppermute | solution.py:18
  72.6 4.4 %copy-start.5 = (bf16[16,8320]{1,0:T(8,128)(2,1)S(1)}, bf16[16,8320]{1,0:T(8,128)(2,1)}, u32[]{:S(2)}) copy-start(bf16[16,8320]{1,0:T(8,128)(2,1)} %copy-done.4) | copy-start | bytes 798724
  72.6 4.5 %copy-start.7 = (bf16[16,8320]{1,0:T(8,128)(2,1)S(1)}, bf16[16,8320]{1,0:T(8,128)(2,1)}, u32[]{:S(2)}) copy-start(bf16[16,8320]{1,0:T(8,128)(2,1)} %copy-done.6) | copy-start | bytes 798724
  72.6 4.5 %copy-start.9 = (bf16[32,16,512]{2,1,0:T(8,128)(2,1)S(1)}, bf16[32,16,512]{2,1,0:T(8,128)(2,1)}, u32[]{:S(2)}) copy-start(bf16[32,16,512]{2,1,0:T(8,128)(2,1)} %refs_5_.3) | copy-start | bytes 1572868
  72.6 4.4 %collective-permute-start.28 = (bf16[8,128]{1,0:T(8,128)(2,1)S(1)}, bf16[8,128]{1,0:T(8,128)(2,1)S(1)}, u32[]{:S(2)}, u32[]{:S(2)}) collective-permute-start(bf16[8,128]{1,0:T(8,128)(2,1)S(1)} %add_add_fusion.3.refs_5_), channel_id=1, source_target_pairs={{0,1},{1,0},{2,3},{3,2},{4,5},{5,4},{6,7},{7,6},{8,9},{9,8},{10,11... | collective-permute-start | bytes 6152 | tf_op jit(solution)/shard_map/ppermute | solution.py:18
  72.7 4.3 %collective-permute-start.29 = (bf16[8,128]{1,0:T(8,128)(2,1)S(1)}, bf16[8,128]{1,0:T(8,128)(2,1)S(1)}, u32[]{:S(2)}, u32[]{:S(2)}) collective-permute-start(bf16[8,128]{1,0:T(8,128)(2,1)S(1)} %add_add_fusion.3.refs_5_), channel_id=1, source_target_pairs={{0,2},{1,3},{2,0},{3,1},{4,6},{5,7},{6,4},{7,5},{8,10},{9,11},{10,... | collective-permute-start | bytes 6152 | tf_op jit(solution)/shard_map/ppermute | solution.py:18
  73.4 3.6 %collective-permute-start.30 = (bf16[8,128]{1,0:T(8,128)(2,1)S(1)}, bf16[8,128]{1,0:T(8,128)(2,1)S(1)}, u32[]{:S(2)}, u32[]{:S(2)}) collective-permute-start(bf16[8,128]{1,0:T(8,128)(2,1)S(1)} %add_add_fusion.3.refs_5_), channel_id=1, source_target_pairs={{0,3},{1,2},{2,1},{3,0},{4,7},{5,6},{6,5},{7,4},{8,11},{9,10},{10,... | collective-permute-start | bytes 6152 | tf_op jit(solution)/shard_map/ppermute | solution.py:18

commit v7 on v6

--- a/solution.py
+++ b/solution.py
@@ -40,18 +40,22 @@
     return x, [t for t in terms if t is not None]
 
 
-def gather_rows(x, count):
+def gather_rows(x, count, beside, other=None):
     step = count // 4
     far, middle, near = (swap(x, count, k * step) for k in (3, 2, 1))
+    if other is not None:
+        middle, other = lax.optimization_barrier((middle, other))
+        other = swap(other, count, 1)
     step //= 2
     held = [jnp.concatenate([x, near, middle, far], axis=0)]
     across = [swap(p, count, step) for p in (x, far, near, middle)]
+    *across, result = lax.optimization_barrier((*across, beside(held[0])))
     held.append(jnp.concatenate([across[i] for i in (0, 2, 3, 1)], axis=0))
     step //= 2
     while step > 1:
         held = held + [swap(h, count, step) for h in held]
         step //= 2
-    return held, held + [swap(h, count, 1) for h in held]
+    return held, held + [swap(h, count, 1) for h in held], result, other
 
 
 def place_of(row, me, count, rows):
@@ -64,12 +68,12 @@
     return (source ^ me) * rows + row % rows
 
 
-def limit(total, megabytes):
-    return (megabytes if total <= 64 else 60) * 1024 * 1024
-
-
 def spec(space=VMEM):
     return pl.BlockSpec(memory_space=space)
+
+
+def hbm(x):
+    return pltpu.with_memory_space_constraint(x, pltpu.HBM)
 
 
 def iota(shape, dim):
@@ -86,8 +90,10 @@
     names_hbm,
     slots_hbm,
     maps_hbm,
+    weight_hbm,
     out_ref,
     maps_ref,
+    weight_ref,
     hidden_ref,
     gain_ref,
     names_ref,
@@ -104,12 +110,13 @@
                 (names_hbm, names_ref),
                 (slots_hbm, slots_ref),
                 (maps_hbm.at[:, :ranks], maps_ref),
+                (weight_hbm.at[: weight_ref.shape[0]], weight_ref),
             )
         )
     ]
     for copy in copies:
         copy.start()
-    for copy in copies[:-1]:
+    for copy in copies[:4]:
         copy.wait()
     rows, width = hidden_ref.shape
     hidden = hidden_ref[...].astype(jnp.float32)
@@ -123,7 +130,8 @@
         tag = jnp.where(lane < LANES // 2, name, slots_ref[name]).astype(jnp.float32)
         tags = jnp.where(row == r, tag, tags)
     out_ref[:, width:] = tags.astype(jnp.bfloat16)
-    copies[-1].wait()
+    for copy in copies[4:]:
+        copy.wait()
 
 
 NT = (((1,), (1,)), ((), ()))
@@ -166,40 +174,58 @@
     out_ref[...] = value
 
 
-def base_kernel(pieces, part, *refs):
-    weight_hbm, _, out_ref, weight_ref, sems = refs[pieces:]
-    total, columns = out_ref.shape
-    whole = columns // 256 * 256
-    depth = weight_ref.shape[0]
+def load_kernel(start, after_ref, weight_hbm, out_ref, sems):
+    rows = out_ref.shape[0]
     chunk = 512
     copies = [
         pltpu.make_async_copy(
-            weight_hbm.at[part * depth + k : part * depth + k + chunk],
+            weight_hbm.at[start + k : start + k + chunk],
+            out_ref.at[k : k + chunk],
+            sems.at[k // chunk],
+        )
+        for k in range(0, rows, chunk)
+    ]
+    for copy in copies:
+        copy.start()
+    for copy in copies:
+        copy.wait()
+
+
+def base_kernel(pieces, start, *refs):
+    ready_ref, weight_hbm, _, out_ref, weight_ref, sems = refs[pieces:]
+    total, columns = out_ref.shape
+    whole = columns // 256 * 256
+    ready = ready_ref.shape[0]
+    chunk = 1024
+    copies = [
+        pltpu.make_async_copy(
+            weight_hbm.at[start + ready + k : start + ready + k + chunk],
             weight_ref.at[k : k + chunk],
             sems.at[k // chunk],
         )
-        for k in range(0, depth, chunk)
+        for k in range(0, weight_ref.shape[0], chunk)
     ]
     for copy in copies:
         copy.start()
-    for k in range(0, depth, chunk):
-        at = part * depth + k
-        x = jnp.concatenate([p[:, at : at + chunk] for p in refs[:pieces]], axis=0)
-        copies[k // chunk].wait()
+    for k in range(0, ready + weight_ref.shape[0], chunk):
+        x = jnp.concatenate([p[:, start + k : start + k + chunk] for p in refs[:pieces]], axis=0)
+        from_ref, at = (ready_ref, k) if k < ready else (weight_ref, k - ready)
+        if k >= ready:
+            copies[at // chunk].wait()
         terms = []
         if whole:
-            weight = weight_ref[k : k + chunk, :whole]
+            weight = from_ref[at : at + chunk, :whole]
             terms.append(jnp.dot(x, weight, preferred_element_type=jnp.float32))
         if columns - whole == 128:
             half = chunk // 2
             left = jnp.concatenate([x[:, :half], x[:, half:]], axis=0)
-            right = [weight_ref[k + h : k + h + half, whole:] for h in (0, half)]
+            right = [from_ref[at + h : at + h + half, whole:] for h in (0, half)]
             both = jnp.dot(
                 left, jnp.concatenate(right, axis=1), preferred_element_type=jnp.float32
             )
             terms.append(both[:total, :128] + both[total:, 128:])
         elif columns > whole:
-            weight = weight_ref[k : k + chunk, whole:]
+            weight = from_ref[at : at + chunk, whole:]
             terms.append(jnp.dot(x, weight, preferred_element_type=jnp.float32))
         term = terms[0] if len(terms) == 1 else jnp.concatenate(terms, axis=1)
         if k == 0:
@@ -252,6 +278,48 @@
         out_ref[d] = placed[d * rows : (d + 1) * rows]
 
 
+def attend_kernel(lengths_ref, qkv_ref, keys_ref, values_ref, out_ref):
+    rows, kv_heads, context, dim = keys_ref.shape
+    width = out_ref.shape[1]
+    groups = width // dim // kv_heads
+    mixed_rows = groups * rows
+    request = iota((mixed_rows, 1), 0) % rows
+    length = jnp.zeros((mixed_rows, 1), jnp.int32)
+    for b in range(rows):
+        length = jnp.where(request == b, lengths_ref[b], length)
+    live = iota((mixed_rows, context), 1) < length
+    scale = dim ** (-0.5)
+
+    def columns(at):
+        return qkv_ref[:, at : at + dim].astype(jnp.float32)
+
+    for h in range(kv_heads):
+        at = [(h * groups + g) * dim for g in range(groups)]
+        query = jnp.concatenate([columns(a) for a in at], axis=0)
+        key = jnp.concatenate([columns(width + h * dim)] * groups, axis=0)
+        value = jnp.concatenate([columns(width + (kv_heads + h) * dim)] * groups, axis=0)
+        half = query.astype(jnp.bfloat16)
+        scores = jnp.zeros((mixed_rows, context), jnp.float32)
+        for b in range(rows):
+            one = lax.dot_general(half, keys_ref[b, h], NT, preferred_element_type=jnp.float32)
+            scores = jnp.where(request == b, one, scores)
+        scores = jnp.where(live, scores * scale, -1e30)
+        own = jnp.sum(query * key, axis=1, keepdims=True) * scale
+        peak = jnp.maximum(jnp.max(scores, axis=1, keepdims=True), own)
+        weights = jnp.exp(scores - peak)
+        own_weight = jnp.exp(own - peak)
+        denominator = jnp.sum(weights, axis=1, keepdims=True) + own_weight
+        probs = (weights / denominator).astype(jnp.bfloat16)
+        own_prob = (own_weight / denominator).astype(jnp.bfloat16).astype(jnp.float32)
+        mixed = jnp.zeros((mixed_rows, dim), jnp.float32)
+        for b in range(rows):
+            one = jnp.dot(probs, values_ref[b, h], preferred_element_type=jnp.float32)
+            mixed = jnp.where(request == b, one, mixed)
+        mixed = (mixed + own_prob * value).astype(jnp.bfloat16)
+        for g in range(groups):
+            out_ref[:, at[g] : at[g] + dim] = mixed[g * rows : (g + 1) * rows]
+
+
 def local(
     input_hidden,
     input_norm_gain,
@@ -275,33 +343,35 @@
     kv_width = kv_heads * head_dim
     total = rows * count
     bf16, f32 = jnp.bfloat16, jnp.float32
-    roomy = pltpu.CompilerParams(vmem_limit_bytes=limit(total, 16))
-    tight = {
-        projection_weight.shape[1]: pltpu.CompilerParams(vmem_limit_bytes=limit(total, 52)),
-        output_weight.shape[1]: pltpu.CompilerParams(vmem_limit_bytes=limit(total, 52)),
-    }
-    full = pltpu.CompilerParams(vmem_limit_bytes=limit(total, 58))
+    params = pltpu.CompilerParams(vmem_limit_bytes=(16 if total <= 64 else 60) * 1024 * 1024)
     own_maps = jnp.swapaxes(adapter_down, 1, 2)
-    sibling_maps = jnp.swapaxes(swap(adapter_down, count, 1), 1, 2)
-
-    normed, first_maps = pl.pallas_call(
+
+    normed, first_maps, first_rows = pl.pallas_call(
         norm_kernel,
         out_shape=[
             VMEM((rows, width + LANES), bf16),
             VMEM((held, 3 * rank, width), bf16),
+            VMEM((1024, projection_weight.shape[1]), bf16),
         ],
-        in_specs=[spec(pltpu.HBM)] * 5,
-        out_specs=[spec()] * 2,
+        in_specs=[spec(pltpu.HBM)] * 6,
+        out_specs=[spec()] * 3,
         scratch_shapes=[
             VMEM((rows, width), bf16),
             VMEM((width,), bf16),
             SMEM((rows,), jnp.int32),
             SMEM(adapter_storage.shape, jnp.int32),
-            pltpu.SemaphoreType.DMA((5,)),
+            pltpu.SemaphoreType.DMA((6,)),
         ],
-        compiler_params=full,
+        compiler_params=params,
         name="norm",
-    )(input_hidden, input_norm_gain, request_adapter.reshape(rows), adapter_storage, own_maps)
+    )(
+        hbm(input_hidden),
+        hbm(input_norm_gain),
+        hbm(request_adapter.reshape(rows)),
+        hbm(adapter_storage),
+        hbm(own_maps),
+        hbm(projection_weight),
+    )
 
     def tag_specs(pieces):
         return [pl.BlockSpec((p.shape[0], LANES), lambda i: (0, width // LANES)) for p in pieces]
@@ -323,7 +393,7 @@
             + [pl.BlockSpec((p.shape[0], width), lambda i: (0, 0)) for p in pieces]
             + tag_specs(tagged),
             out_specs=[whole(x) for x in shapes],
-            compiler_params=roomy,
+            compiler_params=params,
             cost_estimate=pl.CostEstimate(
                 flops=2 * total * width * held * ranks,
                 bytes_accessed=2 * width * (2 * held * ranks + total),
@@ -332,25 +402,41 @@
             name="down",
         )(own, sibling, *pieces, *tagged)
 
-    def base(pieces, weight, after, part, parts):
+    def load(after, weight, start, length):
         columns = weight.shape[1]
         return pl.pallas_call(
-            functools.partial(base_kernel, len(pieces), part),
+            functools.partial(load_kernel, start),
+            out_shape=VMEM((length, columns), bf16),
+            in_specs=[spec(pl.ANY), spec(pltpu.HBM)],
+            out_specs=spec(),
+            scratch_shapes=[pltpu.SemaphoreType.DMA((length // 512,))],
+            compiler_params=params,
+            cost_estimate=pl.CostEstimate(
+                flops=0, bytes_accessed=4 * length * columns, transcendentals=0
+            ),
+            name="load",
+        )(after, hbm(weight))
+
+    def base(pieces, weight, after, start, ready, length):
+        columns = weight.shape[1]
+        stream = length - ready.shape[0]
+        return pl.pallas_call(
+            functools.partial(base_kernel, len(pieces), start),
             out_shape=jax.ShapeDtypeStruct((total, columns), f32),
-            in_specs=[spec()] * len(pieces) + [spec(pl.ANY)] * 2,
+            in_specs=[spec()] * (len(pieces) + 1) + [spec(pltpu.HBM), spec(pl.ANY)],
             out_specs=spec(),
             scratch_shapes=[
-                VMEM((width // parts, columns), bf16),
-                pltpu.SemaphoreType.DMA((width // parts // 512,)),
+                VMEM((stream, columns), bf16),
+                pltpu.SemaphoreType.DMA((stream // 1024,)),
             ],
-            compiler_params=tight[columns],
+            compiler_params=params,
             cost_estimate=pl.CostEstimate(
-                flops=2 * total * width * columns // parts,
-                bytes_accessed=4 * width * columns // parts,
+                flops=2 * total * length * columns,
+                bytes_accessed=4 * length * columns,
                 transcendentals=0,
             ),
             name="base",
-        )(*pieces, weight, after)
+        )(*pieces, ready, hbm(weight), after)
 
     def lift(down, tagged, up, base_terms, bounds, ranks):
         columns = up.shape[2]
@@ -363,20 +449,28 @@
             in_specs=tag_specs(tagged) + [whole(x) for x in operands],
             out_specs=pl.BlockSpec((count, rows, columns), lambda i: (0, 0, 0)),
             scratch_shapes=[VMEM((total, columns), f32)],
-            compiler_params=roomy,
+            compiler_params=params,
             name="lift",
         )(*tagged, *operands)
 
-    def project(x, tagged, maps, low, high, weight, up, bounds):
-        column, pieces = gather_rows(x, count)
+    def project(x, tagged, own, sibling, ready, low, high, weight, up, bounds):
+        half, quarter = width // 2, width // 4
+
+        def beside(rows_here):
+            last = load(rows_here, weight, half, quarter)
+            return (load(rows_here, weight, 0, 1024) if ready is None else ready), last
+
+        column, pieces, loaded, swapped = gather_rows(x, count, beside, sibling[0])
         tagged = pieces if tagged is None else tagged
-        parts = 2
-
-        def beside(turn, after):
-            return base(pieces, weight, after, turn, parts) if turn < parts else None
-
-        down, *rest = downs(*maps, column, tagged[: len(column)], low, high)
-        down, base_terms = sum_over(down, count, beside)
+        theirs = sibling[1] if swapped is None else jnp.swapaxes(swapped, 1, 2)
+
+        def term(turn, after):
+            if turn > 1:
+                return None
+            return base(pieces, weight, after, turn * half, loaded[turn], half)
+
+        down, *rest = downs(own, theirs, column, tagged[: len(column)], low, high)
+        down, base_terms = sum_over(down, count, term)
         columns = lift(down, tagged, up, base_terms, bounds, high - low)
         mine = exchange(columns)
         return jnp.swapaxes(mine, 0, 1).reshape(rows, -1), tagged, rest
@@ -385,43 +479,34 @@
     qkv_mine, tagged, rest = project(
         normed,
         None,
-        (first_maps, sibling_maps),
+        first_maps,
+        (adapter_down, None),
+        first_rows,
         0,
         3 * rank,
         projection_weight,
         projection_up_adapter,
         bounds,
     )
-
-    groups_per = width // head_dim // kv_heads
-    query = qkv_mine[:, 0:width].reshape(rows, kv_heads, groups_per, head_dim)
-    key_new = qkv_mine[:, width : width + kv_width].reshape(rows, kv_heads, head_dim)
-    value_new = qkv_mine[:, width + kv_width :].reshape(rows, kv_heads, head_dim)
-    scale = head_dim ** (-0.5)
-    scores = (
-        jnp.einsum("bhgd,bhpd->bhgp", query, cache_keys, preferred_element_type=jnp.float32) * scale
-    )
-    lengths, query = lax.optimization_barrier((lengths, query))
-    live = jnp.arange(context, dtype=jnp.int32)[None, :] < lengths[:, None]
-    scores = jnp.where(live[:, None, None, :], scores, -1e30)
-    own = jnp.einsum("bhgd,bhd->bhg", query, key_new, preferred_element_type=jnp.float32) * scale
-    peak = jnp.maximum(jnp.max(scores, axis=3), own)
-    weights = jnp.exp(scores - peak[..., None])
-    own_weight = jnp.exp(own - peak)
-    denominator = jnp.sum(weights, axis=3) + own_weight
-    probs = (weights / denominator[..., None]).astype(jnp.bfloat16)
-    own_prob = (own_weight / denominator).astype(jnp.bfloat16)
-    mixed = jnp.einsum("bhgp,bhpd->bhgd", probs, cache_values, preferred_element_type=jnp.float32)
-    mixed = (
-        mixed
-        + own_prob.astype(jnp.float32)[..., None] * value_new.astype(jnp.float32)[:, :, None, :]
-    )
-    attended = mixed.reshape(rows, width).astype(jnp.bfloat16)
-
+    attended = pl.pallas_call(
+        attend_kernel,
+        out_shape=jax.ShapeDtypeStruct((rows, width), bf16),
+        in_specs=[spec(SMEM)] + [spec()] * 3,
+        out_specs=spec(),
+        compiler_params=params,
+        cost_estimate=pl.CostEstimate(
+            flops=4 * rows * width * context,
+            bytes_accessed=4 * cache_keys.size,
+            transcendentals=rows * width // head_dim * context,
+        ),
+        name="attend",
+    )(lengths, qkv_mine, cache_keys, cache_values)
     output, _, _ = project(
         attended,
         tagged,
-        (own_maps, rest[0]),
+        own_maps,
+        (None, rest[0]),
+        None,
         3 * rank,
         4 * rank,
         output_weight,

time: 89.7 us -> 88.6 us (0.988)
  Pallas kernels: 16.2 us -> 23.7 us
  matrix products: 2.98 us -> 0 us
  waiting for transfers between devices: 12.3 us -> 9.96 us
  local copies, waits for them, and re-layouts: 2.27 us -> 0.66 us
  other arithmetic: 1.61 us -> 0.67 us
    pallas_call x4 -> x8, Pallas kernels: 11.6 us -> 18.7 us  [the longest x4 9.7 us: base(): pl.pallas_call(functools.partial(base_kernel, len(pieces), start), out_sh...]
    dot_general x3 -> x0, matrix products: 2.98 us -> none  [the longest x1 1.26 us: local(): jnp.einsum('bhgd,bhpd->bhgp', query, cache_keys, preferred_element_type=j...]
    ppermute x31, waiting for transfers between devices: 12.3 us -> 9.96 us  [swap(): return lax.ppermute(x, AXIS, [(i, i ^ offset) for i in range(count)])]
    unnamed x35 -> x13, local copies, waits for them, and re-layouts: 1.65 us -> 0.66 us
  transfers between devices with their start and end apart: 31 -> 31, of which waited for: 9 -> 8; matrix products, arithmetic and copies ran while one was open for 1% -> 1% of each run, Pallas kernels for 15% -> 18%
where the time goes in v7:
time: 88.6 us; the launch traced here: 88.3 us
  starting transfers between devices  31.7 us (36%)
  Pallas kernels  23.7 us (27%)
  blocking collectives  21.3 us (24%)
  waiting for transfers between devices  9.96 us (11%)
    ppermute x31, starting transfers between devices, swap(): return lax.ppermute(x, AXIS, [(i, i ^ offset) for i in range(count)])  31.7 us
    all_to_all x2, blocking collectives, exchange(): lax.all_to_all(x, AXIS, split_axis=0, concat_axis=0, axis_index_groups=gr...  21.3 us
    ppermute x31, waiting for transfers between devices, swap(): return lax.ppermute(x, AXIS, [(i, i ^ offset) for i in range(count)])  9.96 us
    pallas_call x4, Pallas kernels, base(): pl.pallas_call(functools.partial(base_kernel, len(pieces), start), out_sh...  9.7 us
    pallas_call x1, Pallas kernels, local(): pl.pallas_call(attend_kernel, out_shape=jax.ShapeDtypeStruct((rows, width...  4.51 us
    pallas_call x3, Pallas kernels, load(): pl.pallas_call(functools.partial(load_kernel, start), out_shape=VMEM((len...  4.49 us
    pallas_call x1, Pallas kernels, local(): pl.pallas_call(norm_kernel, out_shape=[VMEM((rows, width + LANES), bf16),...  2.04 us
  transfers between devices with their start and end apart: 31, of which 8 were waited for; matrix products, arithmetic and copies ran while one was open for 1% of the time, Pallas kernels for 18%

profile of v7, /device:TPU:0, one launch (start us, length us, event | category | flops | bytes accessed | tf_op | source)
XLA Modules:
  0.0 88.3 jit_solution(14098157245021624638)
XLA Ops:
  0.0 2.0 %norm.1 = (bf16[4,8320]{1,0:T(4,128)(2,1)S(1)}, bf16[2,48,8192]{2,1,0:T(8,128)(2,1)S(1)}, bf16[1024,640]{1,0:T(8,128)(2,1)S(1)}) custom-call(bf16[4,8192]{1,0:T(4,128)(2,1)} %hidden_hbm.1, bf16[8192]{0:T(1024)(128)(2,1)} %gain_hbm.1, s32[4]{0:T(128)} %bitcast.14, s32[32]{0:T(128)} %slots_hbm.1, bf16[2,64,8192]{2,1,0:T(8,128)(2,1)} %bitcast.9, ...), custom_call_target="tpu_custom_call" | custom-call | tf_op jit(solution)/shard_map/norm/pallas_call | solution.py:349
  2.0 4.1 %collective-permute-start.1 = (bf16[4,8320]{1,0:T(4,128)(2,1)S(1)}, bf16[4,8320]{1,0:T(4,128)(2,1)S(1)}, u32[]{:S(2)}, u32[]{:S(2)}) collective-permute-start(bf16[4,8320]{1,0:T(4,128)(2,1)S(1)} %get-tuple-element.40), channel_id=1, source_target_pairs={{0,8},{1,9},{2,10},{3,11},{4,12},{5,13},{6,14},{7,15},{8,0},{9,1},... | collective-permute-start | bytes 199688 | tf_op jit(solution)/shard_map/ppermute | solution.py:18
  6.2 1.3 %collective-permute-start.2 = (bf16[4,8320]{1,0:T(4,128)(2,1)S(1)}, bf16[4,8320]{1,0:T(4,128)(2,1)S(1)}, u32[]{:S(2)}, u32[]{:S(2)}) collective-permute-start(bf16[4,8320]{1,0:T(4,128)(2,1)S(1)} %get-tuple-element.40), channel_id=1, source_target_pairs={{0,12},{1,13},{2,14},{3,15},{4,8},{5,9},{6,10},{7,11},{8,4},{9,5},... | collective-permute-start | bytes 199688 | tf_op jit(solution)/shard_map/ppermute | solution.py:18
  7.5 0.2 collective-permute-start
  7.7 1.5 %collective-permute-start.3 = (bf16[4,8320]{1,0:T(4,128)(2,1)S(1)}, bf16[4,8320]{1,0:T(4,128)(2,1)S(1)}, u32[]{:S(2)}, u32[]{:S(2)}) collective-permute-start(bf16[4,8320]{1,0:T(4,128)(2,1)S(1)} %get-tuple-element.40), channel_id=1, source_target_pairs={{0,2},{1,3},{2,0},{3,1},{4,6},{5,7},{6,4},{7,5},{8,10},{9,11},{10,... | collective-permute-start | bytes 199688 | tf_op jit(solution)/shard_map/ppermute | solution.py:18
  9.2 0.7 collective-permute-done.1
  9.9 2.6 %collective-permute-start.6 = (bf16[4,8320]{1,0:T(4,128)(2,1)S(1)}, bf16[4,8320]{1,0:T(4,128)(2,1)S(1)}, u32[]{:S(2)}, u32[]{:S(2)}) collective-permute-start(bf16[4,8320]{1,0:T(4,128)(2,1)S(1)} %collective-permute-done.1), channel_id=1, source_target_pairs={{0,2},{1,3},{2,0},{3,1},{4,6},{5,7},{6,4},{7,5},{8,10},{9,11},{10,... | collective-permute-start | bytes 199688 | tf_op jit(solution)/shard_map/ppermute | solution.py:18
  12.5 0.0 collective-permute-done.2
  12.5 1.4 %collective-permute-start.4 = (bf16[4,8320]{1,0:T(4,128)(2,1)S(1)}, bf16[4,8320]{1,0:T(4,128)(2,1)S(1)}, u32[]{:S(2)}, u32[]{:S(2)}) collective-permute-start(bf16[4,8320]{1,0:T(4,128)(2,1)S(1)} %collective-permute-done.2), channel_id=1, source_target_pairs={{0,2},{1,3},{2,0},{3,1},{4,6},{5,7},{6,4},{7,5},{8,10},{9,11},{10,... | collective-permute-start | bytes 199688 | tf_op jit(solution)/shard_map/ppermute | solution.py:18
  13.9 0.0 collective-permute-done
  13.9 0.7 collective-permute-start.5
  14.6 0.2 pad_maximum_fusion.after_ref.refs_2_.refs_4_.refs_0_
  14.8 1.7 %load.3.refs_4_ = bf16[2048,640]{1,0:T(8,128)(2,1)S(1)} custom-call(bf16[16,8320]{1,0:T(8,128)(2,1)S(1)} %pad_maximum_fusion.after_ref.refs_2_.refs_4_.refs_0_, bf16[8192,640]{1,0:T(8,128)(2,1)} %refs_5_.7), custom_call_target="tpu_custom_call" | custom-call | bytes 5242880 | tf_op jit(solution)/shard_map/load/pallas_call | solution.py:407
  16.5 0.0 collective-permute-done.3
  16.5 0.1 collective-permute-start.7
  16.6 0.0 collective-permute-done.6
  16.6 0.9 %collective-permute-done.4 = bf16[4,8320]{1,0:T(4,128)(2,1)S(1)} collective-permute-done((bf16[4,8320]{1,0:T(4,128)(2,1)S(1)}, bf16[4,8320]{1,0:T(4,128)(2,1)S(1)}, u32[]{:S(2)}, u32[]{:S(2)}) %collective-permute-start.4) | collective-permute-done | bytes 66592 | tf_op jit(solution)/shard_map/ppermute | solution.py:18
  17.5 1.0 %collective-permute-done.5 = bf16[4,8320]{1,0:T(4,128)(2,1)S(1)} collective-permute-done((bf16[4,8320]{1,0:T(4,128)(2,1)S(1)}, bf16[4,8320]{1,0:T(4,128)(2,1)S(1)}, u32[]{:S(2)}, u32[]{:S(2)}) %collective-permute-start.5) | collective-permute-done | bytes 66592 | tf_op jit(solution)/shard_map/ppermute | solution.py:18
  18.5 0.2 pad_maximum_fusion.1.refs_3_.refs_5_.refs_1_
  18.6 0.1 collective-permute-start.8
  18.7 0.0 collective-permute-done.9
  18.7 1.1 %down.2 = (bf16[24,128]{1,0:T(8,128)(2,1)S(1)}, bf16[2,16,8192]{2,1,0:T(8,128)(2,1)S(1)}) custom-call(bf16[2,48,8192]{2,1,0:T(8,128)(2,1)S(1)} %get-tuple-element.47.refs_0_, bf16[2,64,8192]{2,1,0:T(8,128)(2,1)S(1)} %bitcast.11, bf16[16,8320]{1,0:T(8,128)(2,1)S(1)} %pad_maximum_fusion.after_ref.refs_2_.refs_4_.refs_0_, ...), custom_call_target="tpu_custom_call" | custom-call | flops 100663296 | bytes 4194304 | tf_op jit(solution)/shard_map/down/pallas_call | solution.py:388
  19.8 1.2 %collective-permute-start.10 = (bf16[24,128]{1,0:T(8,128)(2,1)S(1)}, bf16[24,128]{1,0:T(8,128)(2,1)S(1)}, u32[]{:S(2)}, u32[]{:S(2)}) collective-permute-start(bf16[24,128]{1,0:T(8,128)(2,1)S(1)} %get-tuple-element.50.refs_6_), channel_id=1, source_target_pairs={{0,4},{1,5},{2,6},{3,7},{4,0},{5,1},{6,2},{7,3},{8,12},{9,13},{10,... | collective-permute-start | bytes 18440 | tf_op jit(solution)/shard_map/ppermute | solution.py:18
  21.0 3.5 %collective-permute-start.11 = (bf16[24,128]{1,0:T(8,128)(2,1)S(1)}, bf16[24,128]{1,0:T(8,128)(2,1)S(1)}, u32[]{:S(2)}, u32[]{:S(2)}) collective-permute-start(bf16[24,128]{1,0:T(8,128)(2,1)S(1)} %get-tuple-element.50.refs_6_), channel_id=1, source_target_pairs={{0,8},{1,9},{2,10},{3,11},{4,12},{5,13},{6,14},{7,15},{8,0},{9,1},... | collective-permute-start | bytes 18440 | tf_op jit(solution)/shard_map/ppermute | solution.py:18
  24.5 0.0 collective-permute-start.12
  24.5 0.0 collective-permute-done.7.refs_2_
  24.5 0.0 collective-permute-done.8.refs_3_
  24.5 2.8 %base.4.refs_6_ = f32[64,640]{1,0:T(8,128)S(1)} custom-call(bf16[16,8320]{1,0:T(8,128)(2,1)S(1)} %pad_maximum_fusion.after_ref.refs_2_.refs_4_.refs_0_, bf16[16,8320]{1,0:T(8,128)(2,1)S(1)} %pad_maximum_fusion.1.refs_3_.refs_5_.refs_1_, bf16[16,8320]{1,0:T(8,128)(2,1)S(1)} %collective-permute-done.7.refs_2_, ...), custom_call_target="tpu_custom_call" | custom-call | flops 335544320 | bytes 10485760 | tf_op jit(solution)/shard_map/base/pallas_call | solution.py:423
  27.4 2.6 %collective-permute-done.12 = bf16[24,128]{1,0:T(8,128)(2,1)S(1)} collective-permute-done((bf16[24,128]{1,0:T(8,128)(2,1)S(1)}, bf16[24,128]{1,0:T(8,128)(2,1)S(1)}, u32[]{:S(2)}, u32[]{:S(2)}) %collective-permute-start.12) | collective-permute-done | bytes 6176 | tf_op jit(solution)/shard_map/ppermute | solution.py:18
  30.0 0.0 copy-start.3
  30.0 0.0 copy-start.5
  30.0 0.1 collective-permute-start.13
  30.1 1.2 %collective-permute-start.14 = (bf16[24,128]{1,0:T(8,128)(2,1)S(1)}, bf16[24,128]{1,0:T(8,128)(2,1)S(1)}, u32[]{:S(2)}, u32[]{:S(2)}) collective-permute-start(bf16[24,128]{1,0:T(8,128)(2,1)S(1)} %add_add_fusion.1.refs_6_), channel_id=1, source_target_pairs={{0,2},{1,3},{2,0},{3,1},{4,6},{5,7},{6,4},{7,5},{8,10},{9,11},{10,... | collective-permute-start | bytes 18440 | tf_op jit(solution)/shard_map/ppermute | solution.py:18
  31.3 0.6 collective-permute-start.15
  31.9 2.8 %base.5.refs_7_ = f32[64,640]{1,0:T(8,128)S(1)} custom-call(bf16[16,8320]{1,0:T(8,128)(2,1)S(1)} %pad_maximum_fusion.after_ref.refs_2_.refs_4_.refs_0_, bf16[16,8320]{1,0:T(8,128)(2,1)S(1)} %pad_maximum_fusion.1.refs_3_.refs_5_.refs_1_, bf16[16,8320]{1,0:T(8,128)(2,1)S(1)} %collective-permute-done.7.refs_2_, ...), custom_call_target="tpu_custom_call" | custom-call | flops 335544320 | bytes 10485760 | tf_op jit(solution)/shard_map/base/pallas_call | solution.py:423
  34.8 0.7 lift.2
  35.5 10.5 %all_to_all.10 = bf16[16,4,640]{2,1,0:T(4,128)(2,1)S(1)} all-to-all(bf16[16,4,640]{2,1,0:T(4,128)(2,1)S(1)} %lift.2), channel_id=1, replica_groups=mesh['groups'=2,'tensor'=16] {'tensor'}, dimensions={0} | all-to-all | bytes 163840 | tf_op jit(solution)/shard_map/all_to_all | solution.py:22
  46.0 4.5 %attend.1 = bf16[4,8192]{1,0:T(4,128)(2,1)S(1)} custom-call(s32[4]{0:T(128)S(1)} %copy-done.5, bf16[4,10240]{1,0:T(4,128)(2,1)S(1)} %bitcast.12, bf16[4,8,384,128]{3,2,1,0:T(8,128)(2,1)S(1)} %copy-done.1, bf16[4,8,384,128]{3,2,1,0:T(8,128)(2,1)S(1)} %copy-done.2), custom_call_target="tpu_custom_call" | custom-call | flops 50331648 | bytes 6291456 | tf_op jit(solution)/shard_map/attend/pallas_call | solution.py:491
  50.6 0.7 collective-permute-start.18
  51.2 0.1 collective-permute-start.16
  51.3 3.7 %collective-permute-start.17 = (bf16[4,8192]{1,0:T(4,128)(2,1)S(1)}, bf16[4,8192]{1,0:T(4,128)(2,1)S(1)}, u32[]{:S(2)}, u32[]{:S(2)}) collective-permute-start(bf16[4,8192]{1,0:T(4,128)(2,1)S(1)} %attend.1), channel_id=1, source_target_pairs={{0,8},{1,9},{2,10},{3,11},{4,12},{5,13},{6,14},{7,15},{8,0},{9,1},... | collective-permute-start | bytes 196616 | tf_op jit(solution)/shard_map/ppermute | solution.py:18
  55.0 2.4 %collective-permute-done.18 = bf16[4,8192]{1,0:T(4,128)(2,1)S(1)} collective-permute-done((bf16[4,8192]{1,0:T(4,128)(2,1)S(1)}, bf16[4,8192]{1,0:T(4,128)(2,1)S(1)}, u32[]{:S(2)}, u32[]{:S(2)}) %collective-permute-start.18) | collective-permute-done | bytes 65568 | tf_op jit(solution)/shard_map/ppermute | solution.py:18
  57.4 2.0 %collective-permute-start.21 = (bf16[4,8192]{1,0:T(4,128)(2,1)S(1)}, bf16[4,8192]{1,0:T(4,128)(2,1)S(1)}, u32[]{:S(2)}, u32[]{:S(2)}) collective-permute-start(bf16[4,8192]{1,0:T(4,128)(2,1)S(1)} %collective-permute-done.16), channel_id=1, source_target_pairs={{0,2},{1,3},{2,0},{3,1},{4,6},{5,7},{6,4},{7,5},{8,10},{9,11},{10,... | collective-permute-start | bytes 196616 | tf_op jit(solution)/shard_map/ppermute | solution.py:18
  59.4 0.1 collective-permute-start.22
  59.5 0.2 pad_maximum_fusion.2.after_ref.refs_2_.refs_0_
  59.7 1.6 %load.5.refs_4_ = bf16[2048,512]{1,0:T(8,128)(2,1)S(1)} custom-call(bf16[16,8192]{1,0:T(8,128)(2,1)S(1)} %pad_maximum_fusion.2.after_ref.refs_2_.refs_0_, bf16[8192,512]{1,0:T(8,128)(2,1)} %refs_5_.10), custom_call_target="tpu_custom_call" | custom-call | bytes 4194304 | tf_op jit(solution)/shard_map/load/pallas_call | solution.py:407
  61.2 1.2 %load.4.refs_4_ = bf16[1024,512]{1,0:T(8,128)(2,1)S(1)} custom-call(bf16[16,8192]{1,0:T(8,128)(2,1)S(1)} %pad_maximum_fusion.2.after_ref.refs_2_.refs_0_, bf16[8192,512]{1,0:T(8,128)(2,1)} %refs_5_.10), custom_call_target="tpu_custom_call" | custom-call | bytes 2097152 | tf_op jit(solution)/shard_map/load/pallas_call | solution.py:407
  62.5 0.1 collective-permute-start.26
  62.6 1.1 %collective-permute-done.22 = bf16[4,8192]{1,0:T(4,128)(2,1)S(1)} collective-permute-done((bf16[4,8192]{1,0:T(4,128)(2,1)S(1)}, bf16[4,8192]{1,0:T(4,128)(2,1)S(1)}, u32[]{:S(2)}, u32[]{:S(2)}) %collective-permute-start.22) | collective-permute-done | bytes 65568 | tf_op jit(solution)/shard_map/ppermute | solution.py:18
  63.7 0.2 pad_maximum_fusion.3.refs_3_.refs_1_
  63.9 0.1 collective-permute-start.27
  63.9 0.5 down.3.refs_6_
  64.5 1.9 %collective-permute-start.24 = (bf16[8,128]{1,0:T(8,128)(2,1)S(1)}, bf16[8,128]{1,0:T(8,128)(2,1)S(1)}, u32[]{:S(2)}, u32[]{:S(2)}) collective-permute-start(bf16[8,128]{1,0:T(8,128)(2,1)S(1)} %down.3.refs_6_), channel_id=1, source_target_pairs={{0,8},{1,9},{2,10},{3,11},{4,12},{5,13},{6,14},{7,15},{8,0},{9,1},... | collective-permute-start | bytes 6152 | tf_op jit(solution)/shard_map/ppermute | solution.py:18
  66.4 2.5 %collective-permute-start.25 = (bf16[8,128]{1,0:T(8,128)(2,1)S(1)}, bf16[8,128]{1,0:T(8,128)(2,1)S(1)}, u32[]{:S(2)}, u32[]{:S(2)}) collective-permute-start(bf16[8,128]{1,0:T(8,128)(2,1)S(1)} %down.3.refs_6_), channel_id=1, source_target_pairs={{0,12},{1,13},{2,14},{3,15},{4,8},{5,9},{6,10},{7,11},{8,4},{9,5},... | collective-permute-start | bytes 6152 | tf_op jit(solution)/shard_map/ppermute | solution.py:18
  68.9 2.2 %base.6.refs_6_ = f32[64,512]{1,0:T(8,128)S(1)} custom-call(bf16[16,8192]{1,0:T(8,128)(2,1)S(1)} %pad_maximum_fusion.2.after_ref.refs_2_.refs_0_, bf16[16,8192]{1,0:T(8,128)(2,1)S(1)} %pad_maximum_fusion.3.refs_3_.refs_1_, bf16[16,8192]{1,0:T(8,128)(2,1)S(1)} %collective-permute-done.26.refs_2_, bf16[16,8192]{1,0:T(8,128)(2,1)S(1)} %collective-permute-done.27.refs_3_, ...), custom_call_target="tpu_custom_call" | custom-call | flops 268435456 | bytes 8388608 | tf_op jit(solution)/shard_map/base/pallas_call | solution.py:423
  71.2 0.6 collective-permute-done.25
  71.8 0.1 collective-permute-start.28
  71.9 1.4 %collective-permute-start.29 = (bf16[8,128]{1,0:T(8,128)(2,1)S(1)}, bf16[8,128]{1,0:T(8,128)(2,1)S(1)}, u32[]{:S(2)}, u32[]{:S(2)}) collective-permute-start(bf16[8,128]{1,0:T(8,128)(2,1)S(1)} %add_add_fusion.3.refs_6_), channel_id=1, source_target_pairs={{0,2},{1,3},{2,0},{3,1},{4,6},{5,7},{6,4},{7,5},{8,10},{9,11},{10,... | collective-permute-start | bytes 6152 | tf_op jit(solution)/shard_map/ppermute | solution.py:18
  73.2 0.5 collective-permute-start.30
  73.7 1.9 %base.7.refs_7_ = f32[64,512]{1,0:T(8,128)S(1)} custom-call(bf16[16,8192]{1,0:T(8,128)(2,1)S(1)} %pad_maximum_fusion.2.after_ref.refs_2_.refs_0_, bf16[16,8192]{1,0:T(8,128)(2,1)S(1)} %pad_maximum_fusion.3.refs_3_.refs_1_, bf16[16,8192]{1,0:T(8,128)(2,1)S(1)} %collective-permute-done.26.refs_2_, bf16[16,8192]{1,0:T(8,128)(2,1)S(1)} %collective-permute-done.27.refs_3_, ...), custom_call_target="tpu_custom_call" | custom-call | flops 268435456 | bytes 8388608 | tf_op jit(solution)/shard_map/base/pallas_call | solution.py:423
  75.6 0.6 collective-permute-done.30
  76.2 0.6 lift.3
  76.9 10.8 %all_to_all.11 = bf16[16,4,512]{2,1,0:T(4,128)(2,1)S(1)} all-to-all(bf16[16,4,512]{2,1,0:T(4,128)(2,1)S(1)} %lift.3), channel_id=1, replica_groups=mesh['groups'=2,'tensor'=16] {'tensor'}, dimensions={0} | all-to-all | bytes 131072 | tf_op jit(solution)/shard_map/all_to_all | solution.py:22
  87.7 0.6 copy.14
  (34 shorter events, 0.1 us)
Async XLA Ops:
  0.0 12.5 %copy-start = (bf16[2,8192,64]{1,2,0:T(8,128)(2,1)S(1)}, bf16[2,8192,64]{1,2,0:T(8,128)(2,1)}, u32[]{:S(2)}) copy-start(bf16[2,8192,64]{1,2,0:T(8,128)(2,1)} %param.19) | copy-start | bytes 6291460
  2.0 7.9 %collective-permute-start.1 = (bf16[4,8320]{1,0:T(4,128)(2,1)S(1)}, bf16[4,8320]{1,0:T(4,128)(2,1)S(1)}, u32[]{:S(2)}, u32[]{:S(2)}) collective-permute-start(bf16[4,8320]{1,0:T(4,128)(2,1)S(1)} %get-tuple-element.40), channel_id=1, source_target_pairs={{0,8},{1,9},{2,10},{3,11},{4,12},{5,13},{6,14},{7,15},{8,0},{9,1},... | collective-permute-start | bytes 199688 | tf_op jit(solution)/shard_map/ppermute | solution.py:18
  6.2 6.4 %collective-permute-start.2 = (bf16[4,8320]{1,0:T(4,128)(2,1)S(1)}, bf16[4,8320]{1,0:T(4,128)(2,1)S(1)}, u32[]{:S(2)}, u32[]{:S(2)}) collective-permute-start(bf16[4,8320]{1,0:T(4,128)(2,1)S(1)} %get-tuple-element.40), channel_id=1, source_target_pairs={{0,12},{1,13},{2,14},{3,15},{4,8},{5,9},{6,10},{7,11},{8,4},{9,5},... | collective-permute-start | bytes 199688 | tf_op jit(solution)/shard_map/ppermute | solution.py:18
  7.5 6.4 %collective-permute-start = (bf16[4,8320]{1,0:T(4,128)(2,1)S(1)}, bf16[4,8320]{1,0:T(4,128)(2,1)S(1)}, u32[]{:S(2)}, u32[]{:S(2)}) collective-permute-start(bf16[4,8320]{1,0:T(4,128)(2,1)S(1)} %get-tuple-element.40), channel_id=1, source_target_pairs={{0,4},{1,5},{2,6},{3,7},{4,0},{5,1},{6,2},{7,3},{8,12},{9,13},{10,... | collective-permute-start | bytes 199688 | tf_op jit(solution)/shard_map/ppermute | solution.py:18
  7.7 8.8 %collective-permute-start.3 = (bf16[4,8320]{1,0:T(4,128)(2,1)S(1)}, bf16[4,8320]{1,0:T(4,128)(2,1)S(1)}, u32[]{:S(2)}, u32[]{:S(2)}) collective-permute-start(bf16[4,8320]{1,0:T(4,128)(2,1)S(1)} %get-tuple-element.40), channel_id=1, source_target_pairs={{0,2},{1,3},{2,0},{3,1},{4,6},{5,7},{6,4},{7,5},{8,10},{9,11},{10,... | collective-permute-start | bytes 199688 | tf_op jit(solution)/shard_map/ppermute | solution.py:18
  9.9 6.6 %collective-permute-start.6 = (bf16[4,8320]{1,0:T(4,128)(2,1)S(1)}, bf16[4,8320]{1,0:T(4,128)(2,1)S(1)}, u32[]{:S(2)}, u32[]{:S(2)}) collective-permute-start(bf16[4,8320]{1,0:T(4,128)(2,1)S(1)} %collective-permute-done.1), channel_id=1, source_target_pairs={{0,2},{1,3},{2,0},{3,1},{4,6},{5,7},{6,4},{7,5},{8,10},{9,11},{10,... | collective-permute-start | bytes 199688 | tf_op jit(solution)/shard_map/ppermute | solution.py:18
  12.5 6.2 %collective-permute-start.9 = (bf16[2,8192,64]{1,2,0:T(8,128)(2,1)S(1)}, bf16[2,8192,64]{1,2,0:T(8,128)(2,1)S(1)}, u32[]{:S(2)}, u32[]{:S(2)}) collective-permute-start(bf16[2,8192,64]{1,2,0:T(8,128)(2,1)S(1)} %copy-done), channel_id=1, source_target_pairs={{0,1},{1,0},{2,3},{3,2},{4,5},{5,4},{6,7},{7,6},{8,9},{9,8},{10,11... | collective-permute-start | bytes 6291464 | tf_op jit(solution)/shard_map/ppermute | solution.py:18
  12.5 5.0 %collective-permute-start.4 = (bf16[4,8320]{1,0:T(4,128)(2,1)S(1)}, bf16[4,8320]{1,0:T(4,128)(2,1)S(1)}, u32[]{:S(2)}, u32[]{:S(2)}) collective-permute-start(bf16[4,8320]{1,0:T(4,128)(2,1)S(1)} %collective-permute-done.2), channel_id=1, source_target_pairs={{0,2},{1,3},{2,0},{3,1},{4,6},{5,7},{6,4},{7,5},{8,10},{9,11},{10,... | collective-permute-start | bytes 199688 | tf_op jit(solution)/shard_map/ppermute | solution.py:18
  13.9 4.6 %collective-permute-start.5 = (bf16[4,8320]{1,0:T(4,128)(2,1)S(1)}, bf16[4,8320]{1,0:T(4,128)(2,1)S(1)}, u32[]{:S(2)}, u32[]{:S(2)}) collective-permute-start(bf16[4,8320]{1,0:T(4,128)(2,1)S(1)} %collective-permute-done), channel_id=1, source_target_pairs={{0,2},{1,3},{2,0},{3,1},{4,6},{5,7},{6,4},{7,5},{8,10},{9,11},{10,... | collective-permute-start | bytes 199688 | tf_op jit(solution)/shard_map/ppermute | solution.py:18
  16.5 8.0 %collective-permute-start.7 = (bf16[16,8320]{1,0:T(8,128)(2,1)S(1)}, bf16[16,8320]{1,0:T(8,128)(2,1)S(1)}, u32[]{:S(2)}, u32[]{:S(2)}) collective-permute-start(bf16[16,8320]{1,0:T(8,128)(2,1)S(1)} %pad_maximum_fusion.after_ref.refs_2_.refs_4_.refs_0_), channel_id=1, source_target_pairs={{0,1},{1,0},{2,3},{3,2},{4,5},{5,4},{6,7},{7,6},{8,9},{9,8},{10,11... | collective-permute-start | bytes 798728 | tf_op jit(solution)/shard_map/ppermute | solution.py:18
  18.6 5.9 %collective-permute-start.8 = (bf16[16,8320]{1,0:T(8,128)(2,1)S(1)}, bf16[16,8320]{1,0:T(8,128)(2,1)S(1)}, u32[]{:S(2)}, u32[]{:S(2)}) collective-permute-start(bf16[16,8320]{1,0:T(8,128)(2,1)S(1)} %pad_maximum_fusion.1.refs_3_.refs_5_.refs_1_), channel_id=1, source_target_pairs={{0,1},{1,0},{2,3},{3,2},{4,5},{5,4},{6,7},{7,6},{8,9},{9,8},{10,11... | collective-permute-start | bytes 798728 | tf_op jit(solution)/shard_map/ppermute | solution.py:18
  19.8 7.5 %collective-permute-start.10 = (bf16[24,128]{1,0:T(8,128)(2,1)S(1)}, bf16[24,128]{1,0:T(8,128)(2,1)S(1)}, u32[]{:S(2)}, u32[]{:S(2)}) collective-permute-start(bf16[24,128]{1,0:T(8,128)(2,1)S(1)} %get-tuple-element.50.refs_6_), channel_id=1, source_target_pairs={{0,4},{1,5},{2,6},{3,7},{4,0},{5,1},{6,2},{7,3},{8,12},{9,13},{10,... | collective-permute-start | bytes 18440 | tf_op jit(solution)/shard_map/ppermute | solution.py:18
  21.0 6.4 %collective-permute-start.11 = (bf16[24,128]{1,0:T(8,128)(2,1)S(1)}, bf16[24,128]{1,0:T(8,128)(2,1)S(1)}, u32[]{:S(2)}, u32[]{:S(2)}) collective-permute-start(bf16[24,128]{1,0:T(8,128)(2,1)S(1)} %get-tuple-element.50.refs_6_), channel_id=1, source_target_pairs={{0,8},{1,9},{2,10},{3,11},{4,12},{5,13},{6,14},{7,15},{8,0},{9,1},... | collective-permute-start | bytes 18440 | tf_op jit(solution)/shard_map/ppermute | solution.py:18
  24.5 5.4 %collective-permute-start.12 = (bf16[24,128]{1,0:T(8,128)(2,1)S(1)}, bf16[24,128]{1,0:T(8,128)(2,1)S(1)}, u32[]{:S(2)}, u32[]{:S(2)}) collective-permute-start(bf16[24,128]{1,0:T(8,128)(2,1)S(1)} %get-tuple-element.50.refs_6_), channel_id=1, source_target_pairs={{0,12},{1,13},{2,14},{3,15},{4,8},{5,9},{6,10},{7,11},{8,4},{9,5},... | collective-permute-start | bytes 18440 | tf_op jit(solution)/shard_map/ppermute | solution.py:18
  30.0 4.9 %copy-start.3 = (bf16[32,16,640]{2,1,0:T(8,128)(2,1)S(1)}, bf16[32,16,640]{2,1,0:T(8,128)(2,1)}, u32[]{:S(2)}) copy-start(bf16[32,16,640]{2,1,0:T(8,128)(2,1)} %refs_5_.8) | copy-start | bytes 1966084
  30.0 16.1 %copy-start.5 = (s32[4]{0:T(128)S(1)}, s32[4]{0:T(128)}, u32[]{:S(2)}) copy-start(s32[4]{0:T(128)} %lengths_ref.1) | copy-start | bytes 52
  30.0 4.8 %collective-permute-start.13 = (bf16[24,128]{1,0:T(8,128)(2,1)S(1)}, bf16[24,128]{1,0:T(8,128)(2,1)S(1)}, u32[]{:S(2)}, u32[]{:S(2)}) collective-permute-start(bf16[24,128]{1,0:T(8,128)(2,1)S(1)} %add_add_fusion.1.refs_6_), channel_id=1, source_target_pairs={{0,1},{1,0},{2,3},{3,2},{4,5},{5,4},{6,7},{7,6},{8,9},{9,8},{10,11... | collective-permute-start | bytes 18440 | tf_op jit(solution)/shard_map/ppermute | solution.py:18
  30.1 4.7 %collective-permute-start.14 = (bf16[24,128]{1,0:T(8,128)(2,1)S(1)}, bf16[24,128]{1,0:T(8,128)(2,1)S(1)}, u32[]{:S(2)}, u32[]{:S(2)}) collective-permute-start(bf16[24,128]{1,0:T(8,128)(2,1)S(1)} %add_add_fusion.1.refs_6_), channel_id=1, source_target_pairs={{0,2},{1,3},{2,0},{3,1},{4,6},{5,7},{6,4},{7,5},{8,10},{9,11},{10,... | collective-permute-start | bytes 18440 | tf_op jit(solution)/shard_map/ppermute | solution.py:18
  31.3 3.5 %collective-permute-start.15 = (bf16[24,128]{1,0:T(8,128)(2,1)S(1)}, bf16[24,128]{1,0:T(8,128)(2,1)S(1)}, u32[]{:S(2)}, u32[]{:S(2)}) collective-permute-start(bf16[24,128]{1,0:T(8,128)(2,1)S(1)} %add_add_fusion.1.refs_6_), channel_id=1, source_target_pairs={{0,3},{1,2},{2,1},{3,0},{4,7},{5,6},{6,5},{7,4},{8,11},{9,10},{10,... | collective-permute-start | bytes 18440 | tf_op jit(solution)/shard_map/ppermute | solution.py:18
  31.9 14.1 %copy-start.1 = (bf16[4,8,384,128]{3,2,1,0:T(8,128)(2,1)S(1)}, bf16[4,8,384,128]{3,2,1,0:T(8,128)(2,1)}, u32[]{:S(2)}) copy-start(bf16[4,8,384,128]{3,2,1,0:T(8,128)(2,1)} %keys_ref.1) | copy-start | bytes 9437188
  31.9 14.1 %copy-start.2 = (bf16[4,8,384,128]{3,2,1,0:T(8,128)(2,1)S(1)}, bf16[4,8,384,128]{3,2,1,0:T(8,128)(2,1)}, u32[]{:S(2)}) copy-start(bf16[4,8,384,128]{3,2,1,0:T(8,128)(2,1)} %values_ref.1) | copy-start | bytes 9437188
  50.6 6.8 %collective-permute-start.18 = (bf16[4,8192]{1,0:T(4,128)(2,1)S(1)}, bf16[4,8192]{1,0:T(4,128)(2,1)S(1)}, u32[]{:S(2)}, u32[]{:S(2)}) collective-permute-start(bf16[4,8192]{1,0:T(4,128)(2,1)S(1)} %attend.1), channel_id=1, source_target_pairs={{0,12},{1,13},{2,14},{3,15},{4,8},{5,9},{6,10},{7,11},{8,4},{9,5},... | collective-permute-start | bytes 196616 | tf_op jit(solution)/shard_map/ppermute | solution.py:18
  51.2 6.2 %collective-permute-start.16 = (bf16[4,8192]{1,0:T(4,128)(2,1)S(1)}, bf16[4,8192]{1,0:T(4,128)(2,1)S(1)}, u32[]{:S(2)}, u32[]{:S(2)}) collective-permute-start(bf16[4,8192]{1,0:T(4,128)(2,1)S(1)} %attend.1), channel_id=1, source_target_pairs={{0,4},{1,5},{2,6},{3,7},{4,0},{5,1},{6,2},{7,3},{8,12},{9,13},{10,... | collective-permute-start | bytes 196616 | tf_op jit(solution)/shard_map/ppermute | solution.py:18
  51.3 8.1 %collective-permute-start.17 = (bf16[4,8192]{1,0:T(4,128)(2,1)S(1)}, bf16[4,8192]{1,0:T(4,128)(2,1)S(1)}, u32[]{:S(2)}, u32[]{:S(2)}) collective-permute-start(bf16[4,8192]{1,0:T(4,128)(2,1)S(1)} %attend.1), channel_id=1, source_target_pairs={{0,8},{1,9},{2,10},{3,11},{4,12},{5,13},{6,14},{7,15},{8,0},{9,1},... | collective-permute-start | bytes 196616 | tf_op jit(solution)/shard_map/ppermute | solution.py:18
  55.0 7.5 %collective-permute-start.19 = (bf16[4,8192]{1,0:T(4,128)(2,1)S(1)}, bf16[4,8192]{1,0:T(4,128)(2,1)S(1)}, u32[]{:S(2)}, u32[]{:S(2)}) collective-permute-start(bf16[4,8192]{1,0:T(4,128)(2,1)S(1)} %attend.1), channel_id=1, source_target_pairs={{0,2},{1,3},{2,0},{3,1},{4,6},{5,7},{6,4},{7,5},{8,10},{9,11},{10,... | collective-permute-start | bytes 196616 | tf_op jit(solution)/shard_map/ppermute | solution.py:18
  57.4 5.1 %collective-permute-start.20 = (bf16[4,8192]{1,0:T(4,128)(2,1)S(1)}, bf16[4,8192]{1,0:T(4,128)(2,1)S(1)}, u32[]{:S(2)}, u32[]{:S(2)}) collective-permute-start(bf16[4,8192]{1,0:T(4,128)(2,1)S(1)} %collective-permute-done.18), channel_id=1, source_target_pairs={{0,2},{1,3},{2,0},{3,1},{4,6},{5,7},{6,4},{7,5},{8,10},{9,11},{10,... | collective-permute-start | bytes 196616 | tf_op jit(solution)/shard_map/ppermute | solution.py:18
  57.4 5.2 %collective-permute-start.21 = (bf16[4,8192]{1,0:T(4,128)(2,1)S(1)}, bf16[4,8192]{1,0:T(4,128)(2,1)S(1)}, u32[]{:S(2)}, u32[]{:S(2)}) collective-permute-start(bf16[4,8192]{1,0:T(4,128)(2,1)S(1)} %collective-permute-done.16), channel_id=1, source_target_pairs={{0,2},{1,3},{2,0},{3,1},{4,6},{5,7},{6,4},{7,5},{8,10},{9,11},{10,... | collective-permute-start | bytes 196616 | tf_op jit(solution)/shard_map/ppermute | solution.py:18
  59.4 4.3 %collective-permute-start.22 = (bf16[4,8192]{1,0:T(4,128)(2,1)S(1)}, bf16[4,8192]{1,0:T(4,128)(2,1)S(1)}, u32[]{:S(2)}, u32[]{:S(2)}) collective-permute-start(bf16[4,8192]{1,0:T(4,128)(2,1)S(1)} %collective-permute-done.17), channel_id=1, source_target_pairs={{0,2},{1,3},{2,0},{3,1},{4,6},{5,7},{6,4},{7,5},{8,10},{9,11},{10,... | collective-permute-start | bytes 196616 | tf_op jit(solution)/shard_map/ppermute | solution.py:18
  62.5 6.5 %collective-permute-start.26 = (bf16[16,8192]{1,0:T(8,128)(2,1)S(1)}, bf16[16,8192]{1,0:T(8,128)(2,1)S(1)}, u32[]{:S(2)}, u32[]{:S(2)}) collective-permute-start(bf16[16,8192]{1,0:T(8,128)(2,1)S(1)} %pad_maximum_fusion.2.after_ref.refs_2_.refs_0_), channel_id=1, source_target_pairs={{0,1},{1,0},{2,3},{3,2},{4,5},{5,4},{6,7},{7,6},{8,9},{9,8},{10,11... | collective-permute-start | bytes 786440 | tf_op jit(solution)/shard_map/ppermute | solution.py:18
  63.9 5.1 %collective-permute-start.27 = (bf16[16,8192]{1,0:T(8,128)(2,1)S(1)}, bf16[16,8192]{1,0:T(8,128)(2,1)S(1)}, u32[]{:S(2)}, u32[]{:S(2)}) collective-permute-start(bf16[16,8192]{1,0:T(8,128)(2,1)S(1)} %pad_maximum_fusion.3.refs_3_.refs_1_), channel_id=1, source_target_pairs={{0,1},{1,0},{2,3},{3,2},{4,5},{5,4},{6,7},{7,6},{8,9},{9,8},{10,11... | collective-permute-start | bytes 786440 | tf_op jit(solution)/shard_map/ppermute | solution.py:18
  64.5 6.7 %collective-permute-start.23 = (bf16[8,128]{1,0:T(8,128)(2,1)S(1)}, bf16[8,128]{1,0:T(8,128)(2,1)S(1)}, u32[]{:S(2)}, u32[]{:S(2)}) collective-permute-start(bf16[8,128]{1,0:T(8,128)(2,1)S(1)} %down.3.refs_6_), channel_id=1, source_target_pairs={{0,4},{1,5},{2,6},{3,7},{4,0},{5,1},{6,2},{7,3},{8,12},{9,13},{10,... | collective-permute-start | bytes 6152 | tf_op jit(solution)/shard_map/ppermute | solution.py:18
  64.5 6.7 %collective-permute-start.24 = (bf16[8,128]{1,0:T(8,128)(2,1)S(1)}, bf16[8,128]{1,0:T(8,128)(2,1)S(1)}, u32[]{:S(2)}, u32[]{:S(2)}) collective-permute-start(bf16[8,128]{1,0:T(8,128)(2,1)S(1)} %down.3.refs_6_), channel_id=1, source_target_pairs={{0,8},{1,9},{2,10},{3,11},{4,12},{5,13},{6,14},{7,15},{8,0},{9,1},... | collective-permute-start | bytes 6152 | tf_op jit(solution)/shard_map/ppermute | solution.py:18
  66.4 5.4 %collective-permute-start.25 = (bf16[8,128]{1,0:T(8,128)(2,1)S(1)}, bf16[8,128]{1,0:T(8,128)(2,1)S(1)}, u32[]{:S(2)}, u32[]{:S(2)}) collective-permute-start(bf16[8,128]{1,0:T(8,128)(2,1)S(1)} %down.3.refs_6_), channel_id=1, source_target_pairs={{0,12},{1,13},{2,14},{3,15},{4,8},{5,9},{6,10},{7,11},{8,4},{9,5},... | collective-permute-start | bytes 6152 | tf_op jit(solution)/shard_map/ppermute | solution.py:18
  71.8 4.5 %copy-start.4 = (bf16[32,16,512]{2,1,0:T(8,128)(2,1)S(1)}, bf16[32,16,512]{2,1,0:T(8,128)(2,1)}, u32[]{:S(2)}) copy-start(bf16[32,16,512]{2,1,0:T(8,128)(2,1)} %refs_5_.11) | copy-start | bytes 1572868
  71.8 3.8 %collective-permute-start.28 = (bf16[8,128]{1,0:T(8,128)(2,1)S(1)}, bf16[8,128]{1,0:T(8,128)(2,1)S(1)}, u32[]{:S(2)}, u32[]{:S(2)}) collective-permute-start(bf16[8,128]{1,0:T(8,128)(2,1)S(1)} %add_add_fusion.3.refs_6_), channel_id=1, source_target_pairs={{0,1},{1,0},{2,3},{3,2},{4,5},{5,4},{6,7},{7,6},{8,9},{9,8},{10,11... | collective-permute-start | bytes 6152 | tf_op jit(solution)/shard_map/ppermute | solution.py:18
  71.9 3.7 %collective-permute-start.29 = (bf16[8,128]{1,0:T(8,128)(2,1)S(1)}, bf16[8,128]{1,0:T(8,128)(2,1)S(1)}, u32[]{:S(2)}, u32[]{:S(2)}) collective-permute-start(bf16[8,128]{1,0:T(8,128)(2,1)S(1)} %add_add_fusion.3.refs_6_), channel_id=1, source_target_pairs={{0,2},{1,3},{2,0},{3,1},{4,6},{5,7},{6,4},{7,5},{8,10},{9,11},{10,... | collective-permute-start | bytes 6152 | tf_op jit(solution)/shard_map/ppermute | solution.py:18
  73.2 3.0 %collective-permute-start.30 = (bf16[8,128]{1,0:T(8,128)(2,1)S(1)}, bf16[8,128]{1,0:T(8,128)(2,1)S(1)}, u32[]{:S(2)}, u32[]{:S(2)}) collective-permute-start(bf16[8,128]{1,0:T(8,128)(2,1)S(1)} %add_add_fusion.3.refs_6_), channel_id=1, source_target_pairs={{0,3},{1,2},{2,1},{3,0},{4,7},{5,6},{6,5},{7,4},{8,11},{9,10},{10,... | collective-permute-start | bytes 6152 | tf_op jit(solution)/shard_map/ppermute | solution.py:18

commit v8 on v7

--- a/solution.py
+++ b/solution.py
@@ -42,9 +42,9 @@
 
 def gather_rows(x, count, beside, other=None):
     step = count // 4
-    far, middle, near = (swap(x, count, k * step) for k in (3, 2, 1))
+    far, near = swap(x, count, 3 * step), swap(x, count, step)
+    middle = swap(far, count, step)
     if other is not None:
-        middle, other = lax.optimization_barrier((middle, other))
         other = swap(other, count, 1)
     step //= 2
     held = [jnp.concatenate([x, near, middle, far], axis=0)]
@@ -145,7 +145,7 @@
     held, _, width = map_refs[0].shape
     rank = ranks[1] - ranks[0]
     total, half = count * rows, count * rows // 2
-    chunk = 1024
+    chunk = 4096
     sums = jnp.zeros((2 * held * rank, half), jnp.float32)
     for k in range(0, width, chunk):
         x = jnp.concatenate([p[:, k : k + chunk] for p in piece_refs], axis=0)
@@ -191,11 +191,12 @@
         copy.wait()
 
 
-def base_kernel(pieces, start, *refs):
-    ready_ref, weight_hbm, _, out_ref, weight_ref, sems = refs[pieces:]
+def base_kernel(pieces, start, ready, *refs):
+    ready_ref = refs[pieces] if ready else None
+    weight_hbm, _, out_ref, weight_ref, sems = refs[-5:]
     total, columns = out_ref.shape
     whole = columns // 256 * 256
-    ready = ready_ref.shape[0]
+    stream = weight_ref.shape[0]
     chunk = 1024
     copies = [
         pltpu.make_async_copy(
@@ -203,35 +204,38 @@
             weight_ref.at[k : k + chunk],
             sems.at[k // chunk],
         )
-        for k in range(0, weight_ref.shape[0], chunk)
+        for k in range(0, stream, chunk)
     ]
     for copy in copies:
         copy.start()
-    for k in range(0, ready + weight_ref.shape[0], chunk):
-        x = jnp.concatenate([p[:, start + k : start + k + chunk] for p in refs[:pieces]], axis=0)
-        from_ref, at = (ready_ref, k) if k < ready else (weight_ref, k - ready)
-        if k >= ready:
-            copies[at // chunk].wait()
-        terms = []
+
+    def rows_of(at, length):
+        return jnp.concatenate([p[:, at : at + length] for p in refs[:pieces]], axis=0)
+
+    def dot(x, weight):
+        return jnp.dot(x, weight, preferred_element_type=jnp.float32)
+
+    if whole and ready:
+        out_ref[:, :whole] = dot(rows_of(start, ready), ready_ref[:, :whole])
+    last = stream - chunk
+    for k, length in ((0, last), (last, chunk)):
+        for copy in copies[k // chunk : (k + length) // chunk]:
+            copy.wait()
         if whole:
-            weight = from_ref[at : at + chunk, :whole]
-            terms.append(jnp.dot(x, weight, preferred_element_type=jnp.float32))
+            x = rows_of(start + ready + k, length)
+            term = dot(x, weight_ref[k : k + length, :whole])
+            out_ref[:, :whole] = term if k == 0 and not ready else out_ref[:, :whole] + term
+    if columns > whole:
+        weight = weight_ref[:, whole:]
+        if ready:
+            weight = jnp.concatenate([ready_ref[:, whole:], weight], axis=0)
+        half = (ready + stream) // 2
         if columns - whole == 128:
-            half = chunk // 2
-            left = jnp.concatenate([x[:, :half], x[:, half:]], axis=0)
-            right = [from_ref[at + h : at + h + half, whole:] for h in (0, half)]
-            both = jnp.dot(
-                left, jnp.concatenate(right, axis=1), preferred_element_type=jnp.float32
-            )
-            terms.append(both[:total, :128] + both[total:, 128:])
-        elif columns > whole:
-            weight = from_ref[at : at + chunk, whole:]
-            terms.append(jnp.dot(x, weight, preferred_element_type=jnp.float32))
-        term = terms[0] if len(terms) == 1 else jnp.concatenate(terms, axis=1)
-        if k == 0:
-            out_ref[...] = term
+            left = jnp.concatenate([rows_of(start, half), rows_of(start + half, half)], axis=0)
+            both = dot(left, jnp.concatenate([weight[:half], weight[half:]], axis=1))
+            out_ref[:, whole:] = both[:total, :128] + both[total:, 128:]
         else:
-            out_ref[...] += term
+            out_ref[:, whole:] = dot(rows_of(start, ready + stream), weight)
 
 
 def lift_kernel(count, rows, pieces, bounds, rank, *refs):
@@ -282,42 +286,55 @@
     rows, kv_heads, context, dim = keys_ref.shape
     width = out_ref.shape[1]
     groups = width // dim // kv_heads
-    mixed_rows = groups * rows
-    request = iota((mixed_rows, 1), 0) % rows
-    length = jnp.zeros((mixed_rows, 1), jnp.int32)
+    per_head = groups * rows
+    together = max(1, LANES // per_head)
+    lanes = together * per_head
+    lane = iota((1, lanes), 1)
+    length = jnp.zeros((1, lanes), jnp.int32)
     for b in range(rows):
-        length = jnp.where(request == b, lengths_ref[b], length)
-    live = iota((mixed_rows, context), 1) < length
+        length = jnp.where(lane % rows == b, lengths_ref[b], length)
+    live = iota((context, lanes), 0) < length
+    request = iota((per_head, 1), 0) % rows
     scale = dim ** (-0.5)
 
     def columns(at):
         return qkv_ref[:, at : at + dim].astype(jnp.float32)
 
-    for h in range(kv_heads):
-        at = [(h * groups + g) * dim for g in range(groups)]
-        query = jnp.concatenate([columns(a) for a in at], axis=0)
-        key = jnp.concatenate([columns(width + h * dim)] * groups, axis=0)
-        value = jnp.concatenate([columns(width + (kv_heads + h) * dim)] * groups, axis=0)
+    for first in range(0, kv_heads, together):
+        heads = range(first, first + together)
+        query = jnp.concatenate(
+            [columns((h * groups + g) * dim) for h in heads for g in range(groups)], axis=0
+        )
+        key = jnp.concatenate([columns(width + h * dim) for h in heads for _ in range(groups)], axis=0)
+        at = width + kv_heads * dim
+        value = jnp.concatenate([columns(at + h * dim) for h in heads for _ in range(groups)], axis=0)
         half = query.astype(jnp.bfloat16)
-        scores = jnp.zeros((mixed_rows, context), jnp.float32)
-        for b in range(rows):
-            one = lax.dot_general(half, keys_ref[b, h], NT, preferred_element_type=jnp.float32)
-            scores = jnp.where(request == b, one, scores)
+        scores = jnp.zeros((context, lanes), jnp.float32)
+        for n, h in enumerate(heads):
+            cached = keys_ref[:, h].reshape(rows * context, dim)
+            every = lax.dot_general(cached, half, NT, preferred_element_type=jnp.float32)
+            for b in range(rows):
+                mine = (lane // per_head == n) & (lane % rows == b)
+                scores = jnp.where(mine, every[b * context : (b + 1) * context], scores)
         scores = jnp.where(live, scores * scale, -1e30)
-        own = jnp.sum(query * key, axis=1, keepdims=True) * scale
-        peak = jnp.maximum(jnp.max(scores, axis=1, keepdims=True), own)
+        own = jnp.sum((query * key).T, axis=0, keepdims=True) * scale
+        peak = jnp.maximum(jnp.max(scores, axis=0, keepdims=True), own)
         weights = jnp.exp(scores - peak)
         own_weight = jnp.exp(own - peak)
-        denominator = jnp.sum(weights, axis=1, keepdims=True) + own_weight
-        probs = (weights / denominator).astype(jnp.bfloat16)
+        denominator = jnp.sum(weights, axis=0, keepdims=True) + own_weight
+        probs = (weights / denominator).T.astype(jnp.bfloat16)
         own_prob = (own_weight / denominator).astype(jnp.bfloat16).astype(jnp.float32)
-        mixed = jnp.zeros((mixed_rows, dim), jnp.float32)
-        for b in range(rows):
-            one = jnp.dot(probs, values_ref[b, h], preferred_element_type=jnp.float32)
-            mixed = jnp.where(request == b, one, mixed)
-        mixed = (mixed + own_prob * value).astype(jnp.bfloat16)
-        for g in range(groups):
-            out_ref[:, at[g] : at[g] + dim] = mixed[g * rows : (g + 1) * rows]
+        own_term = jnp.broadcast_to(own_prob, (dim, lanes)).T * value
+        for n, h in enumerate(heads):
+            span = slice(n * per_head, (n + 1) * per_head)
+            mixed = jnp.zeros((per_head, dim), jnp.float32)
+            for b in range(rows):
+                one = jnp.dot(probs[span], values_ref[b, h], preferred_element_type=jnp.float32)
+                mixed = jnp.where(request == b, one, mixed)
+            mixed = (mixed + own_term[span]).astype(jnp.bfloat16)
+            for g in range(groups):
+                at = (h * groups + g) * dim
+                out_ref[:, at : at + dim] = mixed[g * rows : (g + 1) * rows]
 
 
 def local(
@@ -419,11 +436,12 @@
 
     def base(pieces, weight, after, start, ready, length):
         columns = weight.shape[1]
-        stream = length - ready.shape[0]
+        first = [] if ready is None else [ready]
+        stream = length - sum(r.shape[0] for r in first)
         return pl.pallas_call(
-            functools.partial(base_kernel, len(pieces), start),
+            functools.partial(base_kernel, len(pieces), start, length - stream),
             out_shape=jax.ShapeDtypeStruct((total, columns), f32),
-            in_specs=[spec()] * (len(pieces) + 1) + [spec(pltpu.HBM), spec(pl.ANY)],
+            in_specs=[spec()] * (len(pieces) + len(first)) + [spec(pltpu.HBM), spec(pl.ANY)],
             out_specs=spec(),
             scratch_shapes=[
                 VMEM((stream, columns), bf16),
@@ -436,7 +454,7 @@
                 transcendentals=0,
             ),
             name="base",
-        )(*pieces, ready, hbm(weight), after)
+        )(*pieces, *first, hbm(weight), after)
 
     def lift(down, tagged, up, base_terms, bounds, ranks):
         columns = up.shape[2]
@@ -454,11 +472,10 @@
         )(*tagged, *operands)
 
     def project(x, tagged, own, sibling, ready, low, high, weight, up, bounds):
-        half, quarter = width // 2, width // 4
+        half = width // 2
 
         def beside(rows_here):
-            last = load(rows_here, weight, half, quarter)
-            return (load(rows_here, weight, 0, 1024) if ready is None else ready), last
+            return None if ready is None else load(rows_here, weight, half, ready.shape[0])
 
         column, pieces, loaded, swapped = gather_rows(x, count, beside, sibling[0])
         tagged = pieces if tagged is None else tagged
@@ -467,7 +484,7 @@
         def term(turn, after):
             if turn > 1:
                 return None
-            return base(pieces, weight, after, turn * half, loaded[turn], half)
+            return base(pieces, weight, after, turn * half, (ready, loaded)[turn], half)
 
         down, *rest = downs(own, theirs, column, tagged[: len(column)], low, high)
         down, base_terms = sum_over(down, count, term)

time: 88.6 us -> 89 us (level)
  waiting for transfers between devices: 9.96 us -> 16.9 us
  Pallas kernels: 23.7 us -> 20.2 us
  starting transfers between devices: 31.7 us -> 28.7 us
    ppermute x31, waiting for transfers between devices: 9.96 us -> 16.9 us  [swap(): return lax.ppermute(x, AXIS, [(i, i ^ offset) for i in range(count)])]
    pallas_call x3 -> x1, Pallas kernels: 4.49 us -> 1.31 us  [load(): pl.pallas_call(functools.partial(load_kernel, start), out_shape=VMEM((len...]
    ppermute x31, starting transfers between devices: 31.7 us -> 28.7 us  [swap(): return lax.ppermute(x, AXIS, [(i, i ^ offset) for i in range(count)])]
    pallas_call x1, Pallas kernels: 4.51 us -> 2.78 us  [local(): pl.pallas_call(attend_kernel, out_shape=jax.ShapeDtypeStruct((rows, width...]
    pallas_call x4, Pallas kernels: 9.7 us -> 11.1 us  [base(): pl.pallas_call(functools.partial(base_kernel, len(pieces), start, length...]
  transfers between devices with their start and end apart: 31 -> 31, of which waited for: 8 -> 10; matrix products, arithmetic and copies ran while one was open for 1% -> 1% of each run, Pallas kernels for 18% -> 16%
where the time goes in v8:
time: 89 us; the launch traced here: 88.8 us
  starting transfers between devices  28.7 us (32%)
  blocking collectives  21.3 us (24%)
  Pallas kernels  20.2 us (23%)
  waiting for transfers between devices  16.9 us (19%)
    ppermute x31, starting transfers between devices, swap(): return lax.ppermute(x, AXIS, [(i, i ^ offset) for i in range(count)])  28.7 us
    all_to_all x2, blocking collectives, exchange(): lax.all_to_all(x, AXIS, split_axis=0, concat_axis=0, axis_index_groups=gr...  21.3 us
    ppermute x31, waiting for transfers between devices, swap(): return lax.ppermute(x, AXIS, [(i, i ^ offset) for i in range(count)])  16.9 us
    pallas_call x4, Pallas kernels, base(): pl.pallas_call(functools.partial(base_kernel, len(pieces), start, length...  11.1 us
    pallas_call x1, Pallas kernels, local(): pl.pallas_call(attend_kernel, out_shape=jax.ShapeDtypeStruct((rows, width...  2.78 us
    pallas_call x1, Pallas kernels, local(): pl.pallas_call(norm_kernel, out_shape=[VMEM((rows, width + LANES), bf16),...  2.04 us
  transfers between devices with their start and end apart: 31, of which 10 were waited for; matrix products, arithmetic and copies ran while one was open for 1% of the time, Pallas kernels for 16%

profile of v8, /device:TPU:0, one launch (start us, length us, event | category | flops | bytes accessed | tf_op | source)
XLA Modules:
  0.0 88.8 jit_solution(12359410591355899177)
XLA Ops:
  0.0 2.0 %norm.1 = (bf16[4,8320]{1,0:T(4,128)(2,1)S(1)}, bf16[2,48,8192]{2,1,0:T(8,128)(2,1)S(1)}, bf16[1024,640]{1,0:T(8,128)(2,1)S(1)}) custom-call(bf16[4,8192]{1,0:T(4,128)(2,1)} %hidden_hbm.1, bf16[8192]{0:T(1024)(128)(2,1)} %gain_hbm.1, s32[4]{0:T(128)} %bitcast.14, s32[32]{0:T(128)} %slots_hbm.1, bf16[2,64,8192]{2,1,0:T(8,128)(2,1)} %bitcast.9, ...), custom_call_target="tpu_custom_call" | custom-call | tf_op jit(solution)/shard_map/norm/pallas_call | solution.py:366
  2.0 5.1 %collective-permute-start.1 = (bf16[4,8320]{1,0:T(4,128)(2,1)S(1)}, bf16[4,8320]{1,0:T(4,128)(2,1)S(1)}, u32[]{:S(2)}, u32[]{:S(2)}) collective-permute-start(bf16[4,8320]{1,0:T(4,128)(2,1)S(1)} %get-tuple-element.35), channel_id=1, source_target_pairs={{0,12},{1,13},{2,14},{3,15},{4,8},{5,9},{6,10},{7,11},{8,4},{9,5},... | collective-permute-start | bytes 199688 | tf_op jit(solution)/shard_map/ppermute | solution.py:18
  7.2 2.9 %collective-permute-done.1 = bf16[4,8320]{1,0:T(4,128)(2,1)S(1)} collective-permute-done((bf16[4,8320]{1,0:T(4,128)(2,1)S(1)}, bf16[4,8320]{1,0:T(4,128)(2,1)S(1)}, u32[]{:S(2)}, u32[]{:S(2)}) %collective-permute-start.1) | collective-permute-done | bytes 66592 | tf_op jit(solution)/shard_map/ppermute | solution.py:18
  10.1 0.3 collective-permute-start.2
  10.4 1.2 %collective-permute-start.3 = (bf16[4,8320]{1,0:T(4,128)(2,1)S(1)}, bf16[4,8320]{1,0:T(4,128)(2,1)S(1)}, u32[]{:S(2)}, u32[]{:S(2)}) collective-permute-start(bf16[4,8320]{1,0:T(4,128)(2,1)S(1)} %get-tuple-element.35), channel_id=1, source_target_pairs={{0,2},{1,3},{2,0},{3,1},{4,6},{5,7},{6,4},{7,5},{8,10},{9,11},{10,... | collective-permute-start | bytes 199688 | tf_op jit(solution)/shard_map/ppermute | solution.py:18
  11.7 0.8 collective-permute-start.4
  12.5 0.0 collective-permute-done
  12.5 1.2 %collective-permute-start.5 = (bf16[4,8320]{1,0:T(4,128)(2,1)S(1)}, bf16[4,8320]{1,0:T(4,128)(2,1)S(1)}, u32[]{:S(2)}, u32[]{:S(2)}) collective-permute-start(bf16[4,8320]{1,0:T(4,128)(2,1)S(1)} %collective-permute-done), channel_id=1, source_target_pairs={{0,2},{1,3},{2,0},{3,1},{4,6},{5,7},{6,4},{7,5},{8,10},{9,11},{10,... | collective-permute-start | bytes 199688 | tf_op jit(solution)/shard_map/ppermute | solution.py:18
  13.7 0.7 collective-permute-done.2
  14.4 1.5 %collective-permute-start.6 = (bf16[4,8320]{1,0:T(4,128)(2,1)S(1)}, bf16[4,8320]{1,0:T(4,128)(2,1)S(1)}, u32[]{:S(2)}, u32[]{:S(2)}) collective-permute-start(bf16[4,8320]{1,0:T(4,128)(2,1)S(1)} %collective-permute-done.2), channel_id=1, source_target_pairs={{0,2},{1,3},{2,0},{3,1},{4,6},{5,7},{6,4},{7,5},{8,10},{9,11},{10,... | collective-permute-start | bytes 199688 | tf_op jit(solution)/shard_map/ppermute | solution.py:18
  15.9 0.2 pad_maximum_fusion.after_ref.refs_2_.refs_4_.refs_0_
  16.0 1.3 %load.1.refs_4_ = bf16[1024,640]{1,0:T(8,128)(2,1)S(1)} custom-call(bf16[16,8320]{1,0:T(8,128)(2,1)S(1)} %pad_maximum_fusion.after_ref.refs_2_.refs_4_.refs_0_, bf16[8192,640]{1,0:T(8,128)(2,1)} %refs_5_.5), custom_call_target="tpu_custom_call" | custom-call | bytes 2621440 | tf_op jit(solution)/shard_map/load/pallas_call | solution.py:424
  17.4 0.1 collective-permute-start.7
  17.4 0.0 collective-permute-done.4
  17.4 0.6 collective-permute-done.5
  18.0 1.0 %collective-permute-done.6 = bf16[4,8320]{1,0:T(4,128)(2,1)S(1)} collective-permute-done((bf16[4,8320]{1,0:T(4,128)(2,1)S(1)}, bf16[4,8320]{1,0:T(4,128)(2,1)S(1)}, u32[]{:S(2)}, u32[]{:S(2)}) %collective-permute-start.6) | collective-permute-done | bytes 66592 | tf_op jit(solution)/shard_map/ppermute | solution.py:18
  19.1 0.2 pad_maximum_fusion.1.refs_3_.refs_5_.refs_1_
  19.2 0.1 collective-permute-start.8
  19.3 0.0 collective-permute-done.9
  19.3 1.1 %down.2 = (bf16[24,128]{1,0:T(8,128)(2,1)S(1)}, bf16[2,16,8192]{2,1,0:T(8,128)(2,1)S(1)}) custom-call(bf16[2,48,8192]{2,1,0:T(8,128)(2,1)S(1)} %get-tuple-element.40.refs_0_, bf16[2,64,8192]{2,1,0:T(8,128)(2,1)S(1)} %bitcast.11, bf16[16,8320]{1,0:T(8,128)(2,1)S(1)} %pad_maximum_fusion.after_ref.refs_2_.refs_4_.refs_0_, ...), custom_call_target="tpu_custom_call" | custom-call | flops 100663296 | bytes 4194304 | tf_op jit(solution)/shard_map/down/pallas_call | solution.py:405
  20.4 2.0 %collective-permute-start.10 = (bf16[24,128]{1,0:T(8,128)(2,1)S(1)}, bf16[24,128]{1,0:T(8,128)(2,1)S(1)}, u32[]{:S(2)}, u32[]{:S(2)}) collective-permute-start(bf16[24,128]{1,0:T(8,128)(2,1)S(1)} %get-tuple-element.42.refs_6_), channel_id=1, source_target_pairs={{0,4},{1,5},{2,6},{3,7},{4,0},{5,1},{6,2},{7,3},{8,12},{9,13},{10,... | collective-permute-start | bytes 18440 | tf_op jit(solution)/shard_map/ppermute | solution.py:18
  22.4 2.5 %collective-permute-start.11 = (bf16[24,128]{1,0:T(8,128)(2,1)S(1)}, bf16[24,128]{1,0:T(8,128)(2,1)S(1)}, u32[]{:S(2)}, u32[]{:S(2)}) collective-permute-start(bf16[24,128]{1,0:T(8,128)(2,1)S(1)} %get-tuple-element.42.refs_6_), channel_id=1, source_target_pairs={{0,8},{1,9},{2,10},{3,11},{4,12},{5,13},{6,14},{7,15},{8,0},{9,1},... | collective-permute-start | bytes 18440 | tf_op jit(solution)/shard_map/ppermute | solution.py:18
  24.9 1.4 %collective-permute-start.12 = (bf16[24,128]{1,0:T(8,128)(2,1)S(1)}, bf16[24,128]{1,0:T(8,128)(2,1)S(1)}, u32[]{:S(2)}, u32[]{:S(2)}) collective-permute-start(bf16[24,128]{1,0:T(8,128)(2,1)S(1)} %get-tuple-element.42.refs_6_), channel_id=1, source_target_pairs={{0,12},{1,13},{2,14},{3,15},{4,8},{5,9},{6,10},{7,11},{8,4},{9,5},... | collective-permute-start | bytes 18440 | tf_op jit(solution)/shard_map/ppermute | solution.py:18
  26.3 0.0 collective-permute-done.7.refs_2_
  26.3 0.0 collective-permute-done.8.refs_3_
  26.3 2.7 %base.4.refs_6_ = f32[64,640]{1,0:T(8,128)S(1)} custom-call(bf16[16,8320]{1,0:T(8,128)(2,1)S(1)} %pad_maximum_fusion.after_ref.refs_2_.refs_4_.refs_0_, bf16[16,8320]{1,0:T(8,128)(2,1)S(1)} %pad_maximum_fusion.1.refs_3_.refs_5_.refs_1_, bf16[16,8320]{1,0:T(8,128)(2,1)S(1)} %collective-permute-done.7.refs_2_, ...), custom_call_target="tpu_custom_call" | custom-call | flops 335544320 | bytes 10485760 | tf_op jit(solution)/shard_map/base/pallas_call | solution.py:441
  29.0 1.3 %collective-permute-done.12 = bf16[24,128]{1,0:T(8,128)(2,1)S(1)} collective-permute-done((bf16[24,128]{1,0:T(8,128)(2,1)S(1)}, bf16[24,128]{1,0:T(8,128)(2,1)S(1)}, u32[]{:S(2)}, u32[]{:S(2)}) %collective-permute-start.12) | collective-permute-done | bytes 6176 | tf_op jit(solution)/shard_map/ppermute | solution.py:18
  30.3 0.0 copy-start.3
  30.3 0.1 collective-permute-start.13
  30.4 1.2 %collective-permute-start.14 = (bf16[24,128]{1,0:T(8,128)(2,1)S(1)}, bf16[24,128]{1,0:T(8,128)(2,1)S(1)}, u32[]{:S(2)}, u32[]{:S(2)}) collective-permute-start(bf16[24,128]{1,0:T(8,128)(2,1)S(1)} %add_add_fusion.1.refs_6_), channel_id=1, source_target_pairs={{0,2},{1,3},{2,0},{3,1},{4,6},{5,7},{6,4},{7,5},{8,10},{9,11},{10,... | collective-permute-start | bytes 18440 | tf_op jit(solution)/shard_map/ppermute | solution.py:18
  31.6 0.6 collective-permute-start.15
  32.3 2.9 %base.5.refs_7_ = f32[64,640]{1,0:T(8,128)S(1)} custom-call(bf16[16,8320]{1,0:T(8,128)(2,1)S(1)} %pad_maximum_fusion.after_ref.refs_2_.refs_4_.refs_0_, bf16[16,8320]{1,0:T(8,128)(2,1)S(1)} %pad_maximum_fusion.1.refs_3_.refs_5_.refs_1_, bf16[16,8320]{1,0:T(8,128)(2,1)S(1)} %collective-permute-done.7.refs_2_, ...), custom_call_target="tpu_custom_call" | custom-call | flops 335544320 | bytes 10485760 | tf_op jit(solution)/shard_map/base/pallas_call | solution.py:441
  35.2 0.0 copy-start.5
  35.2 0.7 lift.2
  35.9 10.7 %all_to_all.10 = bf16[16,4,640]{2,1,0:T(4,128)(2,1)S(1)} all-to-all(bf16[16,4,640]{2,1,0:T(4,128)(2,1)S(1)} %lift.2), channel_id=1, replica_groups=mesh['groups'=2,'tensor'=16] {'tensor'}, dimensions={0} | all-to-all | bytes 163840 | tf_op jit(solution)/shard_map/all_to_all | solution.py:22
  46.6 2.8 %attend.1 = bf16[4,8192]{1,0:T(4,128)(2,1)S(1)} custom-call(s32[4]{0:T(128)S(1)} %copy-done.5, bf16[4,10240]{1,0:T(4,128)(2,1)S(1)} %bitcast.12, bf16[4,8,384,128]{3,2,1,0:T(8,128)(2,1)S(1)} %copy-done.1, bf16[4,8,384,128]{3,2,1,0:T(8,128)(2,1)S(1)} %copy-done.2), custom_call_target="tpu_custom_call" | custom-call | flops 50331648 | bytes 6291456 | tf_op jit(solution)/shard_map/attend/pallas_call | solution.py:508
  49.4 0.7 collective-permute-start.17
  50.1 0.1 collective-permute-start.16
  50.2 5.4 %collective-permute-done.17 = bf16[4,8192]{1,0:T(4,128)(2,1)S(1)} collective-permute-done((bf16[4,8192]{1,0:T(4,128)(2,1)S(1)}, bf16[4,8192]{1,0:T(4,128)(2,1)S(1)}, u32[]{:S(2)}, u32[]{:S(2)}) %collective-permute-start.17) | collective-permute-done | bytes 65568 | tf_op jit(solution)/shard_map/ppermute | solution.py:18
  55.5 0.6 collective-permute-start.19
  56.1 1.4 %collective-permute-start.20 = (bf16[4,8192]{1,0:T(4,128)(2,1)S(1)}, bf16[4,8192]{1,0:T(4,128)(2,1)S(1)}, u32[]{:S(2)}, u32[]{:S(2)}) collective-permute-start(bf16[4,8192]{1,0:T(4,128)(2,1)S(1)} %collective-permute-done.17), channel_id=1, source_target_pairs={{0,2},{1,3},{2,0},{3,1},{4,6},{5,7},{6,4},{7,5},{8,10},{9,11},{10,... | collective-permute-start | bytes 196616 | tf_op jit(solution)/shard_map/ppermute | solution.py:18
  57.6 0.6 collective-permute-start.21
  58.1 1.6 %collective-permute-done.18 = bf16[4,8192]{1,0:T(4,128)(2,1)S(1)} collective-permute-done((bf16[4,8192]{1,0:T(4,128)(2,1)S(1)}, bf16[4,8192]{1,0:T(4,128)(2,1)S(1)}, u32[]{:S(2)}, u32[]{:S(2)}) %collective-permute-start.18) | collective-permute-done | bytes 65568 | tf_op jit(solution)/shard_map/ppermute | solution.py:18
  59.8 0.6 collective-permute-start.22
  60.4 0.2 pad_maximum_fusion.2.refs_2_.refs_0_
  60.5 0.1 collective-permute-start.26
  60.6 0.6 collective-permute-done.20
  61.2 0.7 collective-permute-done.21
  61.9 2.2 %collective-permute-done.22 = bf16[4,8192]{1,0:T(4,128)(2,1)S(1)} collective-permute-done((bf16[4,8192]{1,0:T(4,128)(2,1)S(1)}, bf16[4,8192]{1,0:T(4,128)(2,1)S(1)}, u32[]{:S(2)}, u32[]{:S(2)}) %collective-permute-start.22) | collective-permute-done | bytes 65568 | tf_op jit(solution)/shard_map/ppermute | solution.py:18
  64.1 0.2 pad_maximum_fusion.3.refs_3_.refs_1_
  64.2 0.1 collective-permute-start.27
  64.3 0.5 down.3.refs_5_
  64.8 0.6 collective-permute-start.23
  65.4 1.2 %collective-permute-start.24 = (bf16[8,128]{1,0:T(8,128)(2,1)S(1)}, bf16[8,128]{1,0:T(8,128)(2,1)S(1)}, u32[]{:S(2)}, u32[]{:S(2)}) collective-permute-start(bf16[8,128]{1,0:T(8,128)(2,1)S(1)} %down.3.refs_5_), channel_id=1, source_target_pairs={{0,8},{1,9},{2,10},{3,11},{4,12},{5,13},{6,14},{7,15},{8,0},{9,1},... | collective-permute-start | bytes 6152 | tf_op jit(solution)/shard_map/ppermute | solution.py:18
  66.6 2.7 %collective-permute-start.25 = (bf16[8,128]{1,0:T(8,128)(2,1)S(1)}, bf16[8,128]{1,0:T(8,128)(2,1)S(1)}, u32[]{:S(2)}, u32[]{:S(2)}) collective-permute-start(bf16[8,128]{1,0:T(8,128)(2,1)S(1)} %down.3.refs_5_), channel_id=1, source_target_pairs={{0,12},{1,13},{2,14},{3,15},{4,8},{5,9},{6,10},{7,11},{8,4},{9,5},... | collective-permute-start | bytes 6152 | tf_op jit(solution)/shard_map/ppermute | solution.py:18
  69.3 2.7 %base.6.refs_6_ = f32[64,512]{1,0:T(8,128)S(1)} custom-call(bf16[16,8192]{1,0:T(8,128)(2,1)S(1)} %pad_maximum_fusion.2.refs_2_.refs_0_, bf16[16,8192]{1,0:T(8,128)(2,1)S(1)} %pad_maximum_fusion.3.refs_3_.refs_1_, bf16[16,8192]{1,0:T(8,128)(2,1)S(1)} %collective-permute-done.26.refs_2_, bf16[16,8192]{1,0:T(8,128)(2,1)S(1)} %collective-permute-done.27.refs_3_, ...), custom_call_target="tpu_custom_call" | custom-call | flops 268435456 | bytes 8388608 | tf_op jit(solution)/shard_map/base/pallas_call | solution.py:441
  72.1 0.0 copy-start.4
  72.1 0.1 collective-permute-start.28
  72.2 0.7 collective-permute-start.29
  72.8 1.2 %collective-permute-start.30 = (bf16[8,128]{1,0:T(8,128)(2,1)S(1)}, bf16[8,128]{1,0:T(8,128)(2,1)S(1)}, u32[]{:S(2)}, u32[]{:S(2)}) collective-permute-start(bf16[8,128]{1,0:T(8,128)(2,1)S(1)} %add_add_fusion.3.refs_5_), channel_id=1, source_target_pairs={{0,3},{1,2},{2,1},{3,0},{4,7},{5,6},{6,5},{7,4},{8,11},{9,10},{10,... | collective-permute-start | bytes 6152 | tf_op jit(solution)/shard_map/ppermute | solution.py:18
  74.0 2.7 %base.7.refs_7_ = f32[64,512]{1,0:T(8,128)S(1)} custom-call(bf16[16,8192]{1,0:T(8,128)(2,1)S(1)} %pad_maximum_fusion.2.refs_2_.refs_0_, bf16[16,8192]{1,0:T(8,128)(2,1)S(1)} %pad_maximum_fusion.3.refs_3_.refs_1_, bf16[16,8192]{1,0:T(8,128)(2,1)S(1)} %collective-permute-done.26.refs_2_, bf16[16,8192]{1,0:T(8,128)(2,1)S(1)} %collective-permute-done.27.refs_3_, ...), custom_call_target="tpu_custom_call" | custom-call | flops 268435456 | bytes 8388608 | tf_op jit(solution)/shard_map/base/pallas_call | solution.py:441
  76.9 0.6 lift.3
  77.5 10.7 %all_to_all.11 = bf16[16,4,512]{2,1,0:T(4,128)(2,1)S(1)} all-to-all(bf16[16,4,512]{2,1,0:T(4,128)(2,1)S(1)} %lift.3), channel_id=1, replica_groups=mesh['groups'=2,'tensor'=16] {'tensor'}, dimensions={0} | all-to-all | bytes 131072 | tf_op jit(solution)/shard_map/all_to_all | solution.py:22
  88.2 0.6 copy.14
  (32 shorter events, 0.1 us)
Async XLA Ops:
  0.0 11.7 %copy-start = (bf16[2,8192,64]{1,2,0:T(8,128)(2,1)S(1)}, bf16[2,8192,64]{1,2,0:T(8,128)(2,1)}, u32[]{:S(2)}) copy-start(bf16[2,8192,64]{1,2,0:T(8,128)(2,1)} %param.19) | copy-start | bytes 6291460
  2.0 8.0 %collective-permute-start.1 = (bf16[4,8320]{1,0:T(4,128)(2,1)S(1)}, bf16[4,8320]{1,0:T(4,128)(2,1)S(1)}, u32[]{:S(2)}, u32[]{:S(2)}) collective-permute-start(bf16[4,8320]{1,0:T(4,128)(2,1)S(1)} %get-tuple-element.35), channel_id=1, source_target_pairs={{0,12},{1,13},{2,14},{3,15},{4,8},{5,9},{6,10},{7,11},{8,4},{9,5},... | collective-permute-start | bytes 199688 | tf_op jit(solution)/shard_map/ppermute | solution.py:18
  7.2 5.3 %collective-permute-start = (bf16[4,8320]{1,0:T(4,128)(2,1)S(1)}, bf16[4,8320]{1,0:T(4,128)(2,1)S(1)}, u32[]{:S(2)}, u32[]{:S(2)}) collective-permute-start(bf16[4,8320]{1,0:T(4,128)(2,1)S(1)} %get-tuple-element.35), channel_id=1, source_target_pairs={{0,4},{1,5},{2,6},{3,7},{4,0},{5,1},{6,2},{7,3},{8,12},{9,13},{10,... | collective-permute-start | bytes 199688 | tf_op jit(solution)/shard_map/ppermute | solution.py:18
  10.1 4.3 %collective-permute-start.2 = (bf16[4,8320]{1,0:T(4,128)(2,1)S(1)}, bf16[4,8320]{1,0:T(4,128)(2,1)S(1)}, u32[]{:S(2)}, u32[]{:S(2)}) collective-permute-start(bf16[4,8320]{1,0:T(4,128)(2,1)S(1)} %collective-permute-done.1), channel_id=1, source_target_pairs={{0,4},{1,5},{2,6},{3,7},{4,0},{5,1},{6,2},{7,3},{8,12},{9,13},{10,... | collective-permute-start | bytes 199688 | tf_op jit(solution)/shard_map/ppermute | solution.py:18
  10.4 6.9 %collective-permute-start.3 = (bf16[4,8320]{1,0:T(4,128)(2,1)S(1)}, bf16[4,8320]{1,0:T(4,128)(2,1)S(1)}, u32[]{:S(2)}, u32[]{:S(2)}) collective-permute-start(bf16[4,8320]{1,0:T(4,128)(2,1)S(1)} %get-tuple-element.35), channel_id=1, source_target_pairs={{0,2},{1,3},{2,0},{3,1},{4,6},{5,7},{6,4},{7,5},{8,10},{9,11},{10,... | collective-permute-start | bytes 199688 | tf_op jit(solution)/shard_map/ppermute | solution.py:18
  11.7 7.6 %collective-permute-start.9 = (bf16[2,8192,64]{1,2,0:T(8,128)(2,1)S(1)}, bf16[2,8192,64]{1,2,0:T(8,128)(2,1)S(1)}, u32[]{:S(2)}, u32[]{:S(2)}) collective-permute-start(bf16[2,8192,64]{1,2,0:T(8,128)(2,1)S(1)} %copy-done), channel_id=1, source_target_pairs={{0,1},{1,0},{2,3},{3,2},{4,5},{5,4},{6,7},{7,6},{8,9},{9,8},{10,11... | collective-permute-start | bytes 6291464 | tf_op jit(solution)/shard_map/ppermute | solution.py:18
  11.7 5.7 %collective-permute-start.4 = (bf16[4,8320]{1,0:T(4,128)(2,1)S(1)}, bf16[4,8320]{1,0:T(4,128)(2,1)S(1)}, u32[]{:S(2)}, u32[]{:S(2)}) collective-permute-start(bf16[4,8320]{1,0:T(4,128)(2,1)S(1)} %collective-permute-done.1), channel_id=1, source_target_pairs={{0,2},{1,3},{2,0},{3,1},{4,6},{5,7},{6,4},{7,5},{8,10},{9,11},{10,... | collective-permute-start | bytes 199688 | tf_op jit(solution)/shard_map/ppermute | solution.py:18
  12.5 5.6 %collective-permute-start.5 = (bf16[4,8320]{1,0:T(4,128)(2,1)S(1)}, bf16[4,8320]{1,0:T(4,128)(2,1)S(1)}, u32[]{:S(2)}, u32[]{:S(2)}) collective-permute-start(bf16[4,8320]{1,0:T(4,128)(2,1)S(1)} %collective-permute-done), channel_id=1, source_target_pairs={{0,2},{1,3},{2,0},{3,1},{4,6},{5,7},{6,4},{7,5},{8,10},{9,11},{10,... | collective-permute-start | bytes 199688 | tf_op jit(solution)/shard_map/ppermute | solution.py:18
  14.4 4.7 %collective-permute-start.6 = (bf16[4,8320]{1,0:T(4,128)(2,1)S(1)}, bf16[4,8320]{1,0:T(4,128)(2,1)S(1)}, u32[]{:S(2)}, u32[]{:S(2)}) collective-permute-start(bf16[4,8320]{1,0:T(4,128)(2,1)S(1)} %collective-permute-done.2), channel_id=1, source_target_pairs={{0,2},{1,3},{2,0},{3,1},{4,6},{5,7},{6,4},{7,5},{8,10},{9,11},{10,... | collective-permute-start | bytes 199688 | tf_op jit(solution)/shard_map/ppermute | solution.py:18
  17.4 8.9 %collective-permute-start.7 = (bf16[16,8320]{1,0:T(8,128)(2,1)S(1)}, bf16[16,8320]{1,0:T(8,128)(2,1)S(1)}, u32[]{:S(2)}, u32[]{:S(2)}) collective-permute-start(bf16[16,8320]{1,0:T(8,128)(2,1)S(1)} %pad_maximum_fusion.after_ref.refs_2_.refs_4_.refs_0_), channel_id=1, source_target_pairs={{0,1},{1,0},{2,3},{3,2},{4,5},{5,4},{6,7},{7,6},{8,9},{9,8},{10,11... | collective-permute-start | bytes 798728 | tf_op jit(solution)/shard_map/ppermute | solution.py:18
  19.2 7.0 %collective-permute-start.8 = (bf16[16,8320]{1,0:T(8,128)(2,1)S(1)}, bf16[16,8320]{1,0:T(8,128)(2,1)S(1)}, u32[]{:S(2)}, u32[]{:S(2)}) collective-permute-start(bf16[16,8320]{1,0:T(8,128)(2,1)S(1)} %pad_maximum_fusion.1.refs_3_.refs_5_.refs_1_), channel_id=1, source_target_pairs={{0,1},{1,0},{2,3},{3,2},{4,5},{5,4},{6,7},{7,6},{8,9},{9,8},{10,11... | collective-permute-start | bytes 798728 | tf_op jit(solution)/shard_map/ppermute | solution.py:18
  20.4 8.6 %collective-permute-start.10 = (bf16[24,128]{1,0:T(8,128)(2,1)S(1)}, bf16[24,128]{1,0:T(8,128)(2,1)S(1)}, u32[]{:S(2)}, u32[]{:S(2)}) collective-permute-start(bf16[24,128]{1,0:T(8,128)(2,1)S(1)} %get-tuple-element.42.refs_6_), channel_id=1, source_target_pairs={{0,4},{1,5},{2,6},{3,7},{4,0},{5,1},{6,2},{7,3},{8,12},{9,13},{10,... | collective-permute-start | bytes 18440 | tf_op jit(solution)/shard_map/ppermute | solution.py:18
  22.4 6.6 %collective-permute-start.11 = (bf16[24,128]{1,0:T(8,128)(2,1)S(1)}, bf16[24,128]{1,0:T(8,128)(2,1)S(1)}, u32[]{:S(2)}, u32[]{:S(2)}) collective-permute-start(bf16[24,128]{1,0:T(8,128)(2,1)S(1)} %get-tuple-element.42.refs_6_), channel_id=1, source_target_pairs={{0,8},{1,9},{2,10},{3,11},{4,12},{5,13},{6,14},{7,15},{8,0},{9,1},... | collective-permute-start | bytes 18440 | tf_op jit(solution)/shard_map/ppermute | solution.py:18
  24.9 5.4 %collective-permute-start.12 = (bf16[24,128]{1,0:T(8,128)(2,1)S(1)}, bf16[24,128]{1,0:T(8,128)(2,1)S(1)}, u32[]{:S(2)}, u32[]{:S(2)}) collective-permute-start(bf16[24,128]{1,0:T(8,128)(2,1)S(1)} %get-tuple-element.42.refs_6_), channel_id=1, source_target_pairs={{0,12},{1,13},{2,14},{3,15},{4,8},{5,9},{6,10},{7,11},{8,4},{9,5},... | collective-permute-start | bytes 18440 | tf_op jit(solution)/shard_map/ppermute | solution.py:18
  30.3 4.9 %copy-start.3 = (bf16[32,16,640]{2,1,0:T(8,128)(2,1)S(1)}, bf16[32,16,640]{2,1,0:T(8,128)(2,1)}, u32[]{:S(2)}) copy-start(bf16[32,16,640]{2,1,0:T(8,128)(2,1)} %refs_5_.6) | copy-start | bytes 1966084
  30.3 4.9 %collective-permute-start.13 = (bf16[24,128]{1,0:T(8,128)(2,1)S(1)}, bf16[24,128]{1,0:T(8,128)(2,1)S(1)}, u32[]{:S(2)}, u32[]{:S(2)}) collective-permute-start(bf16[24,128]{1,0:T(8,128)(2,1)S(1)} %add_add_fusion.1.refs_6_), channel_id=1, source_target_pairs={{0,1},{1,0},{2,3},{3,2},{4,5},{5,4},{6,7},{7,6},{8,9},{9,8},{10,11... | collective-permute-start | bytes 18440 | tf_op jit(solution)/shard_map/ppermute | solution.py:18
  30.4 4.8 %collective-permute-start.14 = (bf16[24,128]{1,0:T(8,128)(2,1)S(1)}, bf16[24,128]{1,0:T(8,128)(2,1)S(1)}, u32[]{:S(2)}, u32[]{:S(2)}) collective-permute-start(bf16[24,128]{1,0:T(8,128)(2,1)S(1)} %add_add_fusion.1.refs_6_), channel_id=1, source_target_pairs={{0,2},{1,3},{2,0},{3,1},{4,6},{5,7},{6,4},{7,5},{8,10},{9,11},{10,... | collective-permute-start | bytes 18440 | tf_op jit(solution)/shard_map/ppermute | solution.py:18
  31.6 3.6 %collective-permute-start.15 = (bf16[24,128]{1,0:T(8,128)(2,1)S(1)}, bf16[24,128]{1,0:T(8,128)(2,1)S(1)}, u32[]{:S(2)}, u32[]{:S(2)}) collective-permute-start(bf16[24,128]{1,0:T(8,128)(2,1)S(1)} %add_add_fusion.1.refs_6_), channel_id=1, source_target_pairs={{0,3},{1,2},{2,1},{3,0},{4,7},{5,6},{6,5},{7,4},{8,11},{9,10},{10,... | collective-permute-start | bytes 18440 | tf_op jit(solution)/shard_map/ppermute | solution.py:18
  32.3 14.3 %copy-start.1 = (bf16[4,8,384,128]{3,2,1,0:T(8,128)(2,1)S(1)}, bf16[4,8,384,128]{3,2,1,0:T(8,128)(2,1)}, u32[]{:S(2)}) copy-start(bf16[4,8,384,128]{3,2,1,0:T(8,128)(2,1)} %keys_ref.1) | copy-start | bytes 9437188
  32.3 14.3 %copy-start.2 = (bf16[4,8,384,128]{3,2,1,0:T(8,128)(2,1)S(1)}, bf16[4,8,384,128]{3,2,1,0:T(8,128)(2,1)}, u32[]{:S(2)}) copy-start(bf16[4,8,384,128]{3,2,1,0:T(8,128)(2,1)} %values_ref.1) | copy-start | bytes 9437188
  35.2 11.4 %copy-start.5 = (s32[4]{0:T(128)S(1)}, s32[4]{0:T(128)}, u32[]{:S(2)}) copy-start(s32[4]{0:T(128)} %lengths_ref.1) | copy-start | bytes 52
  49.4 6.1 %collective-permute-start.17 = (bf16[4,8192]{1,0:T(4,128)(2,1)S(1)}, bf16[4,8192]{1,0:T(4,128)(2,1)S(1)}, u32[]{:S(2)}, u32[]{:S(2)}) collective-permute-start(bf16[4,8192]{1,0:T(4,128)(2,1)S(1)} %attend.1), channel_id=1, source_target_pairs={{0,12},{1,13},{2,14},{3,15},{4,8},{5,9},{6,10},{7,11},{8,4},{9,5},... | collective-permute-start | bytes 196616 | tf_op jit(solution)/shard_map/ppermute | solution.py:18
  50.1 7.5 %collective-permute-start.16 = (bf16[4,8192]{1,0:T(4,128)(2,1)S(1)}, bf16[4,8192]{1,0:T(4,128)(2,1)S(1)}, u32[]{:S(2)}, u32[]{:S(2)}) collective-permute-start(bf16[4,8192]{1,0:T(4,128)(2,1)S(1)} %attend.1), channel_id=1, source_target_pairs={{0,4},{1,5},{2,6},{3,7},{4,0},{5,1},{6,2},{7,3},{8,12},{9,13},{10,... | collective-permute-start | bytes 196616 | tf_op jit(solution)/shard_map/ppermute | solution.py:18
  55.5 4.3 %collective-permute-start.18 = (bf16[4,8192]{1,0:T(4,128)(2,1)S(1)}, bf16[4,8192]{1,0:T(4,128)(2,1)S(1)}, u32[]{:S(2)}, u32[]{:S(2)}) collective-permute-start(bf16[4,8192]{1,0:T(4,128)(2,1)S(1)} %collective-permute-done.17), channel_id=1, source_target_pairs={{0,4},{1,5},{2,6},{3,7},{4,0},{5,1},{6,2},{7,3},{8,12},{9,13},{10,... | collective-permute-start | bytes 196616 | tf_op jit(solution)/shard_map/ppermute | solution.py:18
  55.5 5.1 %collective-permute-start.19 = (bf16[4,8192]{1,0:T(4,128)(2,1)S(1)}, bf16[4,8192]{1,0:T(4,128)(2,1)S(1)}, u32[]{:S(2)}, u32[]{:S(2)}) collective-permute-start(bf16[4,8192]{1,0:T(4,128)(2,1)S(1)} %attend.1), channel_id=1, source_target_pairs={{0,2},{1,3},{2,0},{3,1},{4,6},{5,7},{6,4},{7,5},{8,10},{9,11},{10,... | collective-permute-start | bytes 196616 | tf_op jit(solution)/shard_map/ppermute | solution.py:18
  56.1 5.1 %collective-permute-start.20 = (bf16[4,8192]{1,0:T(4,128)(2,1)S(1)}, bf16[4,8192]{1,0:T(4,128)(2,1)S(1)}, u32[]{:S(2)}, u32[]{:S(2)}) collective-permute-start(bf16[4,8192]{1,0:T(4,128)(2,1)S(1)} %collective-permute-done.17), channel_id=1, source_target_pairs={{0,2},{1,3},{2,0},{3,1},{4,6},{5,7},{6,4},{7,5},{8,10},{9,11},{10,... | collective-permute-start | bytes 196616 | tf_op jit(solution)/shard_map/ppermute | solution.py:18
  57.6 4.3 %collective-permute-start.21 = (bf16[4,8192]{1,0:T(4,128)(2,1)S(1)}, bf16[4,8192]{1,0:T(4,128)(2,1)S(1)}, u32[]{:S(2)}, u32[]{:S(2)}) collective-permute-start(bf16[4,8192]{1,0:T(4,128)(2,1)S(1)} %collective-permute-done.16), channel_id=1, source_target_pairs={{0,2},{1,3},{2,0},{3,1},{4,6},{5,7},{6,4},{7,5},{8,10},{9,11},{10,... | collective-permute-start | bytes 196616 | tf_op jit(solution)/shard_map/ppermute | solution.py:18
  59.8 4.3 %collective-permute-start.22 = (bf16[4,8192]{1,0:T(4,128)(2,1)S(1)}, bf16[4,8192]{1,0:T(4,128)(2,1)S(1)}, u32[]{:S(2)}, u32[]{:S(2)}) collective-permute-start(bf16[4,8192]{1,0:T(4,128)(2,1)S(1)} %collective-permute-done.18), channel_id=1, source_target_pairs={{0,2},{1,3},{2,0},{3,1},{4,6},{5,7},{6,4},{7,5},{8,10},{9,11},{10,... | collective-permute-start | bytes 196616 | tf_op jit(solution)/shard_map/ppermute | solution.py:18
  60.5 8.8 %collective-permute-start.26 = (bf16[16,8192]{1,0:T(8,128)(2,1)S(1)}, bf16[16,8192]{1,0:T(8,128)(2,1)S(1)}, u32[]{:S(2)}, u32[]{:S(2)}) collective-permute-start(bf16[16,8192]{1,0:T(8,128)(2,1)S(1)} %pad_maximum_fusion.2.refs_2_.refs_0_), channel_id=1, source_target_pairs={{0,1},{1,0},{2,3},{3,2},{4,5},{5,4},{6,7},{7,6},{8,9},{9,8},{10,11... | collective-permute-start | bytes 786440 | tf_op jit(solution)/shard_map/ppermute | solution.py:18
  64.2 5.1 %collective-permute-start.27 = (bf16[16,8192]{1,0:T(8,128)(2,1)S(1)}, bf16[16,8192]{1,0:T(8,128)(2,1)S(1)}, u32[]{:S(2)}, u32[]{:S(2)}) collective-permute-start(bf16[16,8192]{1,0:T(8,128)(2,1)S(1)} %pad_maximum_fusion.3.refs_3_.refs_1_), channel_id=1, source_target_pairs={{0,1},{1,0},{2,3},{3,2},{4,5},{5,4},{6,7},{7,6},{8,9},{9,8},{10,11... | collective-permute-start | bytes 786440 | tf_op jit(solution)/shard_map/ppermute | solution.py:18
  64.8 7.2 %collective-permute-start.23 = (bf16[8,128]{1,0:T(8,128)(2,1)S(1)}, bf16[8,128]{1,0:T(8,128)(2,1)S(1)}, u32[]{:S(2)}, u32[]{:S(2)}) collective-permute-start(bf16[8,128]{1,0:T(8,128)(2,1)S(1)} %down.3.refs_5_), channel_id=1, source_target_pairs={{0,4},{1,5},{2,6},{3,7},{4,0},{5,1},{6,2},{7,3},{8,12},{9,13},{10,... | collective-permute-start | bytes 6152 | tf_op jit(solution)/shard_map/ppermute | solution.py:18
  65.4 6.7 %collective-permute-start.24 = (bf16[8,128]{1,0:T(8,128)(2,1)S(1)}, bf16[8,128]{1,0:T(8,128)(2,1)S(1)}, u32[]{:S(2)}, u32[]{:S(2)}) collective-permute-start(bf16[8,128]{1,0:T(8,128)(2,1)S(1)} %down.3.refs_5_), channel_id=1, source_target_pairs={{0,8},{1,9},{2,10},{3,11},{4,12},{5,13},{6,14},{7,15},{8,0},{9,1},... | collective-permute-start | bytes 6152 | tf_op jit(solution)/shard_map/ppermute | solution.py:18
  66.6 5.4 %collective-permute-start.25 = (bf16[8,128]{1,0:T(8,128)(2,1)S(1)}, bf16[8,128]{1,0:T(8,128)(2,1)S(1)}, u32[]{:S(2)}, u32[]{:S(2)}) collective-permute-start(bf16[8,128]{1,0:T(8,128)(2,1)S(1)} %down.3.refs_5_), channel_id=1, source_target_pairs={{0,12},{1,13},{2,14},{3,15},{4,8},{5,9},{6,10},{7,11},{8,4},{9,5},... | collective-permute-start | bytes 6152 | tf_op jit(solution)/shard_map/ppermute | solution.py:18
  72.1 4.8 %copy-start.4 = (bf16[32,16,512]{2,1,0:T(8,128)(2,1)S(1)}, bf16[32,16,512]{2,1,0:T(8,128)(2,1)}, u32[]{:S(2)}) copy-start(bf16[32,16,512]{2,1,0:T(8,128)(2,1)} %refs_5_.7) | copy-start | bytes 1572868
  72.1 4.7 %collective-permute-start.28 = (bf16[8,128]{1,0:T(8,128)(2,1)S(1)}, bf16[8,128]{1,0:T(8,128)(2,1)S(1)}, u32[]{:S(2)}, u32[]{:S(2)}) collective-permute-start(bf16[8,128]{1,0:T(8,128)(2,1)S(1)} %add_add_fusion.3.refs_5_), channel_id=1, source_target_pairs={{0,1},{1,0},{2,3},{3,2},{4,5},{5,4},{6,7},{7,6},{8,9},{9,8},{10,11... | collective-permute-start | bytes 6152 | tf_op jit(solution)/shard_map/ppermute | solution.py:18
  72.2 4.6 %collective-permute-start.29 = (bf16[8,128]{1,0:T(8,128)(2,1)S(1)}, bf16[8,128]{1,0:T(8,128)(2,1)S(1)}, u32[]{:S(2)}, u32[]{:S(2)}) collective-permute-start(bf16[8,128]{1,0:T(8,128)(2,1)S(1)} %add_add_fusion.3.refs_5_), channel_id=1, source_target_pairs={{0,2},{1,3},{2,0},{3,1},{4,6},{5,7},{6,4},{7,5},{8,10},{9,11},{10,... | collective-permute-start | bytes 6152 | tf_op jit(solution)/shard_map/ppermute | solution.py:18
  72.8 4.0 %collective-permute-start.30 = (bf16[8,128]{1,0:T(8,128)(2,1)S(1)}, bf16[8,128]{1,0:T(8,128)(2,1)S(1)}, u32[]{:S(2)}, u32[]{:S(2)}) collective-permute-start(bf16[8,128]{1,0:T(8,128)(2,1)S(1)} %add_add_fusion.3.refs_5_), channel_id=1, source_target_pairs={{0,3},{1,2},{2,1},{3,0},{4,7},{5,6},{6,5},{7,4},{8,11},{9,10},{10,... | collective-permute-start | bytes 6152 | tf_op jit(solution)/shard_map/ppermute | solution.py:18

commit v9 on v8

--- a/solution.py
+++ b/solution.py
@@ -40,22 +40,40 @@
     return x, [t for t in terms if t is not None]
 
 
-def gather_rows(x, count, beside, other=None):
+def pack_kernel(*refs):
+    *in_refs, out_ref = refs
+    rows, width = in_refs[0].shape
+    per = 16 // rows
+    for first in range(0, len(in_refs), per):
+        parts = [r[...].astype(jnp.float32) for r in in_refs[first : first + per]]
+        at = slice(first * rows, (first + per) * rows)
+        out_ref[at] = jnp.concatenate(parts, axis=0).astype(jnp.bfloat16)
+
+
+def pack(parts):
+    rows, width = parts[0].shape
+    return pl.pallas_call(
+        pack_kernel,
+        out_shape=jax.ShapeDtypeStruct((rows * len(parts), width), jnp.bfloat16),
+        in_specs=[spec()] * len(parts),
+        out_specs=spec(),
+        compiler_params=pltpu.CompilerParams(vmem_limit_bytes=16 * 1024 * 1024),
+        name="pack",
+    )(*parts)
+
+
+def gather_rows(x, count):
     step = count // 4
-    far, near = swap(x, count, 3 * step), swap(x, count, step)
-    middle = swap(far, count, step)
-    if other is not None:
-        other = swap(other, count, 1)
+    far, middle, near = (swap(x, count, k * step) for k in (3, 2, 1))
     step //= 2
-    held = [jnp.concatenate([x, near, middle, far], axis=0)]
-    across = [swap(p, count, step) for p in (x, far, near, middle)]
-    *across, result = lax.optimization_barrier((*across, beside(held[0])))
-    held.append(jnp.concatenate([across[i] for i in (0, 2, 3, 1)], axis=0))
+    across = [swap(p, count, step) for p in (x, far, middle, near)]
+    parts = [x, near, middle, far] + [across[i] for i in (0, 3, 2, 1)]
+    held = [pack(parts)]
     step //= 2
     while step > 1:
         held = held + [swap(h, count, step) for h in held]
         step //= 2
-    return held, held + [swap(h, count, 1) for h in held], result, other
+    return held, held + [swap(h, count, 1) for h in held]
 
 
 def place_of(row, me, count, rows):
@@ -137,10 +155,19 @@
 NT = (((1,), (1,)), ((), ()))
 
 
+def rows_copy(weight_hbm, start, rows_ref, sem):
+    return pltpu.make_async_copy(weight_hbm.at[start : start + rows_ref.shape[0]], rows_ref, sem)
+
+
 def down_kernel(count, rows, pieces, ranks, *refs):
     map_refs, piece_refs = refs[:2], refs[2 : 2 + pieces]
-    tag_refs, out_refs = refs[2 + pieces : 2 + 2 * pieces], refs[2 + 2 * pieces :]
-    out_ref = out_refs[0]
+    tag_refs, refs = refs[2 + pieces : 2 + 2 * pieces], refs[2 + 2 * pieces :]
+    if len(refs) > 1:
+        weight_hbm, out_ref, rest_ref, rows_ref, sems = refs
+        copy = rows_copy(weight_hbm, weight_hbm.shape[0] // 2, rows_ref, sems.at[0])
+        copy.start()
+    else:
+        (out_ref,) = refs
     me = lax.axis_index(AXIS)
     held, _, width = map_refs[0].shape
     rank = ranks[1] - ranks[0]
@@ -153,8 +180,8 @@
             [m[:, :rank, k : k + chunk].reshape(held * rank, chunk) for m in map_refs], axis=0
         )
         sums = sums + lax.dot_general(maps, x, NT, preferred_element_type=jnp.float32)
-    if len(out_refs) > 1:
-        out_refs[1][...] = map_refs[1][:, rank:]
+    if len(refs) > 1:
+        rest_ref[...] = map_refs[1][:, rank:]
     tags = jnp.concatenate([t[...] for t in tag_refs], axis=0)
     pick = one_hot(iota((16, LANES), 1) == LANES // 2)
     slots = lax.dot_general(pick, tags, NT, preferred_element_type=jnp.float32)[:1]
@@ -172,70 +199,52 @@
     folded = [placed[f * part : (f + 1) * part] for f in range(folds)]
     value = jnp.concatenate(folded, axis=1).astype(jnp.bfloat16)
     out_ref[...] = value
-
-
-def load_kernel(start, after_ref, weight_hbm, out_ref, sems):
-    rows = out_ref.shape[0]
-    chunk = 512
+    if len(refs) > 1:
+        copy.wait()
+
+
+def base_kernel(pieces, start, ready, *refs):
+    ready_ref = refs[pieces]
+    weight_hbm, _, out_ref, weight_ref, sems = refs[pieces + 1 :]
+    total, columns = out_ref.shape
+    whole = columns // 256 * 256
+    stream = weight_ref.shape[0]
+    spans = [(k, 1024) for k in range(0, stream - 1024, 1024)]
+    spans += [(stream - 1024, 512), (stream - 512, 512)]
     copies = [
         pltpu.make_async_copy(
-            weight_hbm.at[start + k : start + k + chunk],
-            out_ref.at[k : k + chunk],
-            sems.at[k // chunk],
+            weight_hbm.at[start + ready + k : start + ready + k + length],
+            weight_ref.at[k : k + length],
+            sems.at[i],
         )
-        for k in range(0, rows, chunk)
+        for i, (k, length) in enumerate(spans)
     ]
     for copy in copies:
         copy.start()
-    for copy in copies:
-        copy.wait()
-
-
-def base_kernel(pieces, start, ready, *refs):
-    ready_ref = refs[pieces] if ready else None
-    weight_hbm, _, out_ref, weight_ref, sems = refs[-5:]
-    total, columns = out_ref.shape
-    whole = columns // 256 * 256
-    stream = weight_ref.shape[0]
-    chunk = 1024
-    copies = [
-        pltpu.make_async_copy(
-            weight_hbm.at[start + ready + k : start + ready + k + chunk],
-            weight_ref.at[k : k + chunk],
-            sems.at[k // chunk],
-        )
-        for k in range(0, stream, chunk)
-    ]
-    for copy in copies:
-        copy.start()
-
-    def rows_of(at, length):
-        return jnp.concatenate([p[:, at : at + length] for p in refs[:pieces]], axis=0)
 
     def dot(x, weight):
         return jnp.dot(x, weight, preferred_element_type=jnp.float32)
 
-    if whole and ready:
-        out_ref[:, :whole] = dot(rows_of(start, ready), ready_ref[:, :whole])
-    last = stream - chunk
-    for k, length in ((0, last), (last, chunk)):
-        for copy in copies[k // chunk : (k + length) // chunk]:
+    steps = [(ready_ref, k, 1024, k, None) for k in range(0, ready, 1024)]
+    steps += [(weight_ref, k, n, ready + k, copy) for (k, n), copy in zip(spans, copies)]
+    for from_ref, k, length, offset, copy in steps:
+        at = start + offset
+        x = jnp.concatenate([p[:, at : at + length] for p in refs[:pieces]], axis=0)
+        if copy is not None:
             copy.wait()
+        terms = []
         if whole:
-            x = rows_of(start + ready + k, length)
-            term = dot(x, weight_ref[k : k + length, :whole])
-            out_ref[:, :whole] = term if k == 0 and not ready else out_ref[:, :whole] + term
-    if columns > whole:
-        weight = weight_ref[:, whole:]
-        if ready:
-            weight = jnp.concatenate([ready_ref[:, whole:], weight], axis=0)
-        half = (ready + stream) // 2
+            terms.append(dot(x, from_ref[k : k + length, :whole]))
         if columns - whole == 128:
-            left = jnp.concatenate([rows_of(start, half), rows_of(start + half, half)], axis=0)
-            both = dot(left, jnp.concatenate([weight[:half], weight[half:]], axis=1))
-            out_ref[:, whole:] = both[:total, :128] + both[total:, 128:]
-        else:
-            out_ref[:, whole:] = dot(rows_of(start, ready + stream), weight)
+            half = length // 2
+            left = jnp.concatenate([x[:, :half], x[:, half:]], axis=0)
+            right = [from_ref[k + h : k + h + half, whole:] for h in (0, half)]
+            both = dot(left, jnp.concatenate(right, axis=1))
+            terms.append(both[:total, :128] + both[total:, 128:])
+        elif columns > whole:
+            terms.append(dot(x, from_ref[k : k + length, whole:]))
+        term = terms[0] if len(terms) == 1 else jnp.concatenate(terms, axis=1)
+        out_ref[...] = term if offset == 0 else out_ref[...] + term
 
 
 def lift_kernel(count, rows, pieces, bounds, rank, *refs):
@@ -282,7 +291,15 @@
         out_ref[d] = placed[d * rows : (d + 1) * rows]
 
 
-def attend_kernel(lengths_ref, qkv_ref, keys_ref, values_ref, out_ref):
+def attend_kernel(
+    lengths_ref, qkv_ref, keys_ref, values_ref, weight_hbm, out_ref, low_ref, high_ref, sems
+):
+    copies = [
+        rows_copy(weight_hbm, 0, low_ref, sems.at[0]),
+        rows_copy(weight_hbm, weight_hbm.shape[0] // 2, high_ref, sems.at[1]),
+    ]
+    for copy in copies:
+        copy.start()
     rows, kv_heads, context, dim = keys_ref.shape
     width = out_ref.shape[1]
     groups = width // dim // kv_heads
@@ -335,6 +352,8 @@
             for g in range(groups):
                 at = (h * groups + g) * dim
                 out_ref[:, at : at + dim] = mixed[g * rows : (g + 1) * rows]
+    for copy in copies:
+        copy.wait()
 
 
 def local(
@@ -393,23 +412,31 @@
     def tag_specs(pieces):
         return [pl.BlockSpec((p.shape[0], LANES), lambda i: (0, width // LANES)) for p in pieces]
 
-    def downs(own, sibling, pieces, tagged, low, high):
+    def downs(own, sibling, pieces, tagged, low, high, weight):
         ranks = high - low
         lanes = max(LANES, total)
-        whole = lambda x: pl.BlockSpec(x.shape, lambda i: (0,) * x.ndim)
+        whole = lambda x: pl.BlockSpec(x.shape, lambda i: (0,) * len(x.shape))
         own_spec = pl.BlockSpec((held, ranks, width), lambda i: (0, low // ranks, 0))
-        shapes = [jax.ShapeDtypeStruct((ranks * total // lanes, lanes), bf16)]
+        outs = [jax.ShapeDtypeStruct((ranks * total // lanes, lanes), bf16)]
+        extra = []
         if low == 0:
             rest = sibling.shape[1] - ranks
-            shapes.append(jax.ShapeDtypeStruct((held, rest, width), bf16))
+            outs.append(jax.ShapeDtypeStruct((held, rest, width), bf16))
+            extra = [hbm(weight)]
+        out_specs = [whole(x) for x in outs]
+        if extra:
+            outs.append(VMEM((1024, weight.shape[1]), bf16))
+            out_specs.append(spec(pl.ANY))
         return pl.pallas_call(
             functools.partial(down_kernel, count, rows, len(pieces), (low, high)),
             grid=(1,),
-            out_shape=shapes,
+            out_shape=outs,
             in_specs=[own_spec, whole(sibling)]
             + [pl.BlockSpec((p.shape[0], width), lambda i: (0, 0)) for p in pieces]
-            + tag_specs(tagged),
-            out_specs=[whole(x) for x in shapes],
+            + tag_specs(tagged)
+            + [spec(pltpu.HBM)] * len(extra),
+            out_specs=out_specs,
+            scratch_shapes=[pltpu.SemaphoreType.DMA((1,))] * len(extra),
             compiler_params=params,
             cost_estimate=pl.CostEstimate(
                 flops=2 * total * width * held * ranks,
@@ -417,35 +444,19 @@
                 transcendentals=0,
             ),
             name="down",
-        )(own, sibling, *pieces, *tagged)
-
-    def load(after, weight, start, length):
-        columns = weight.shape[1]
-        return pl.pallas_call(
-            functools.partial(load_kernel, start),
-            out_shape=VMEM((length, columns), bf16),
-            in_specs=[spec(pl.ANY), spec(pltpu.HBM)],
-            out_specs=spec(),
-            scratch_shapes=[pltpu.SemaphoreType.DMA((length // 512,))],
-            compiler_params=params,
-            cost_estimate=pl.CostEstimate(
-                flops=0, bytes_accessed=4 * length * columns, transcendentals=0
-            ),
-            name="load",
-        )(after, hbm(weight))
+        )(own, sibling, *pieces, *tagged, *extra)
 
     def base(pieces, weight, after, start, ready, length):
         columns = weight.shape[1]
-        first = [] if ready is None else [ready]
-        stream = length - sum(r.shape[0] for r in first)
+        stream = length - ready.shape[0]
         return pl.pallas_call(
             functools.partial(base_kernel, len(pieces), start, length - stream),
             out_shape=jax.ShapeDtypeStruct((total, columns), f32),
-            in_specs=[spec()] * (len(pieces) + len(first)) + [spec(pltpu.HBM), spec(pl.ANY)],
+            in_specs=[spec()] * (len(pieces) + 1) + [spec(pltpu.HBM), spec(pl.ANY)],
             out_specs=spec(),
             scratch_shapes=[
                 VMEM((stream, columns), bf16),
-                pltpu.SemaphoreType.DMA((stream // 1024,)),
+                pltpu.SemaphoreType.DMA((stream // 1024 + 1,)),
             ],
             compiler_params=params,
             cost_estimate=pl.CostEstimate(
@@ -454,7 +465,7 @@
                 transcendentals=0,
             ),
             name="base",
-        )(*pieces, *first, hbm(weight), after)
+        )(*pieces, ready, hbm(weight), after)
 
     def lift(down, tagged, up, base_terms, bounds, ranks):
         columns = up.shape[2]
@@ -471,45 +482,45 @@
             name="lift",
         )(*tagged, *operands)
 
-    def project(x, tagged, own, sibling, ready, low, high, weight, up, bounds):
+    def project(column, pieces, tagged, own, sibling, ready, low, high, weight, up, bounds):
         half = width // 2
-
-        def beside(rows_here):
-            return None if ready is None else load(rows_here, weight, half, ready.shape[0])
-
-        column, pieces, loaded, swapped = gather_rows(x, count, beside, sibling[0])
-        tagged = pieces if tagged is None else tagged
-        theirs = sibling[1] if swapped is None else jnp.swapaxes(swapped, 1, 2)
+        down, *rest = downs(own, sibling, column, tagged[: len(column)], low, high, weight)
+        ready = ready + rest[1:]
 
         def term(turn, after):
             if turn > 1:
                 return None
-            return base(pieces, weight, after, turn * half, (ready, loaded)[turn], half)
-
-        down, *rest = downs(own, theirs, column, tagged[: len(column)], low, high)
+            return base(pieces, weight, after, turn * half, ready[turn], half)
+
         down, base_terms = sum_over(down, count, term)
         columns = lift(down, tagged, up, base_terms, bounds, high - low)
         mine = exchange(columns)
-        return jnp.swapaxes(mine, 0, 1).reshape(rows, -1), tagged, rest
+        return jnp.swapaxes(mine, 0, 1).reshape(rows, -1), rest
 
     bounds = (0, width, width + kv_width, width + 2 * kv_width)
-    qkv_mine, tagged, rest = project(
-        normed,
-        None,
+    sibling_maps = jnp.swapaxes(swap(adapter_down, count, 1), 1, 2)
+    column, tagged = gather_rows(normed, count)
+    qkv_mine, rest = project(
+        column,
+        tagged,
+        tagged,
         first_maps,
-        (adapter_down, None),
-        first_rows,
+        sibling_maps,
+        [first_rows],
         0,
         3 * rank,
         projection_weight,
         projection_up_adapter,
         bounds,
     )
-    attended = pl.pallas_call(
+    columns = output_weight.shape[1]
+    ahead = min(2048, width // 2 - 1024)
+    attended, *ready = pl.pallas_call(
         attend_kernel,
-        out_shape=jax.ShapeDtypeStruct((rows, width), bf16),
-        in_specs=[spec(SMEM)] + [spec()] * 3,
-        out_specs=spec(),
+        out_shape=[jax.ShapeDtypeStruct((rows, width), bf16)] + [VMEM((ahead, columns), bf16)] * 2,
+        in_specs=[spec(SMEM)] + [spec()] * 3 + [spec(pltpu.HBM)],
+        out_specs=[spec()] * 3,
+        scratch_shapes=[pltpu.SemaphoreType.DMA((2,))],
         compiler_params=params,
         cost_estimate=pl.CostEstimate(
             flops=4 * rows * width * context,
@@ -517,13 +528,15 @@
             transcendentals=rows * width // head_dim * context,
         ),
         name="attend",
-    )(lengths, qkv_mine, cache_keys, cache_values)
-    output, _, _ = project(
-        attended,
+    )(lengths, qkv_mine, cache_keys, cache_values, hbm(output_weight))
+    column, pieces = gather_rows(attended, count)
+    output, _ = project(
+        column,
+        pieces,
         tagged,
         own_maps,
-        (None, rest[0]),
-        None,
+        rest[0],
+        ready,
         3 * rank,
         4 * rank,
         output_weight,

time: 89 us -> 86.3 us (0.970)
  waiting for transfers between devices: 16.9 us -> 13.6 us
  starting transfers between devices: 28.7 us -> 30.3 us
  Pallas kernels: 20.2 us -> 19.2 us
    ppermute x31 -> x29, waiting for transfers between devices: 16.9 us -> 13.6 us  [swap(): return lax.ppermute(x, AXIS, [(i, i ^ offset) for i in range(count)])]
    ppermute x31 -> x29, starting transfers between devices: 28.7 us -> 30.3 us  [swap(): return lax.ppermute(x, AXIS, [(i, i ^ offset) for i in range(count)])]
    pallas_call x4, Pallas kernels: 11.1 us -> 9.65 us  [base(): pl.pallas_call(functools.partial(base_kernel, len(pieces), start, length...]
    pallas_call x2 -> x3, Pallas kernels: 4.09 us -> 4.5 us  [the longest x1 4.26 us: local(): pl.pallas_call(attend_kernel, out_shape=[jax.ShapeDtypeStruct((rows, widt...]
  transfers between devices with their start and end apart: 31 -> 29, of which waited for: 10 -> 9; matrix products, arithmetic and copies ran while one was open for 1% -> 0% of each run, Pallas kernels for 16% -> 16%
where the time goes in v9:
time: 86.3 us; the launch traced here: 85.9 us
  starting transfers between devices  30.3 us (35%)
  blocking collectives  21.8 us (25%)
  Pallas kernels  19.2 us (22%)
  waiting for transfers between devices  13.6 us (16%)
    ppermute x29, starting transfers between devices, swap(): return lax.ppermute(x, AXIS, [(i, i ^ offset) for i in range(count)])  30.3 us
    all_to_all x2, blocking collectives, exchange(): lax.all_to_all(x, AXIS, split_axis=0, concat_axis=0, axis_index_groups=gr...  21.8 us
    ppermute x29, waiting for transfers between devices, swap(): return lax.ppermute(x, AXIS, [(i, i ^ offset) for i in range(count)])  13.6 us
    pallas_call x4, Pallas kernels, base(): pl.pallas_call(functools.partial(base_kernel, len(pieces), start, length...  9.65 us
    pallas_call x1, Pallas kernels, local(): pl.pallas_call(attend_kernel, out_shape=[jax.ShapeDtypeStruct((rows, widt...  4.26 us
    pallas_call x1, Pallas kernels, local(): pl.pallas_call(norm_kernel, out_shape=[VMEM((rows, width + LANES), bf16),...  1.9 us
    pallas_call x2, Pallas kernels, downs(): pl.pallas_call(functools.partial(down_kernel, count, rows, len(pieces), (...  1.86 us
  transfers between devices with their start and end apart: 29, of which 9 were waited for; matrix products, arithmetic and copies ran while one was open for 0% of the time, Pallas kernels for 16%

profile of v9, /device:TPU:0, one launch (start us, length us, event | category | flops | bytes accessed | tf_op | source)
XLA Modules:
  0.0 85.9 jit_solution(15897217461472322764)
XLA Ops:
  0.0 0.5 collective-permute-start.8
  0.5 1.9 %norm.1 = (bf16[4,8320]{1,0:T(4,128)(2,1)S(1)}, bf16[2,48,8192]{2,1,0:T(8,128)(2,1)S(1)}, bf16[1024,640]{1,0:T(8,128)(2,1)S(1)}) custom-call(bf16[4,8192]{1,0:T(4,128)(2,1)} %hidden_hbm.1, bf16[8192]{0:T(1024)(128)(2,1)} %gain_hbm.1, s32[4]{0:T(128)} %bitcast.14, s32[32]{0:T(128)} %slots_hbm.1, bf16[2,64,8192]{2,1,0:T(8,128)(2,1)} %bitcast.9, ...), custom_call_target="tpu_custom_call" | custom-call | tf_op jit(solution)/shard_map/norm/pallas_call | solution.py:385
  2.4 4.7 %collective-permute-start.2 = (bf16[4,8320]{1,0:T(4,128)(2,1)S(1)}, bf16[4,8320]{1,0:T(4,128)(2,1)S(1)}, u32[]{:S(2)}, u32[]{:S(2)}) collective-permute-start(bf16[4,8320]{1,0:T(4,128)(2,1)S(1)} %get-tuple-element.30.refs_0_), channel_id=1, source_target_pairs={{0,12},{1,13},{2,14},{3,15},{4,8},{5,9},{6,10},{7,11},{8,4},{9,5},... | collective-permute-start | bytes 199688 | tf_op jit(solution)/shard_map/ppermute | solution.py:18
  7.0 0.0 collective-permute-start.1
  7.0 0.6 collective-permute-start
  7.7 1.6 %collective-permute-start.3 = (bf16[4,8320]{1,0:T(4,128)(2,1)S(1)}, bf16[4,8320]{1,0:T(4,128)(2,1)S(1)}, u32[]{:S(2)}, u32[]{:S(2)}) collective-permute-start(bf16[4,8320]{1,0:T(4,128)(2,1)S(1)} %get-tuple-element.30.refs_0_), channel_id=1, source_target_pairs={{0,2},{1,3},{2,0},{3,1},{4,6},{5,7},{6,4},{7,5},{8,10},{9,11},{10,... | collective-permute-start | bytes 199688 | tf_op jit(solution)/shard_map/ppermute | solution.py:18
  9.3 0.7 collective-permute-done.2.refs_3_
  10.0 1.5 %collective-permute-start.6 = (bf16[4,8320]{1,0:T(4,128)(2,1)S(1)}, bf16[4,8320]{1,0:T(4,128)(2,1)S(1)}, u32[]{:S(2)}, u32[]{:S(2)}) collective-permute-start(bf16[4,8320]{1,0:T(4,128)(2,1)S(1)} %collective-permute-done.2.refs_3_), channel_id=1, source_target_pairs={{0,2},{1,3},{2,0},{3,1},{4,6},{5,7},{6,4},{7,5},{8,10},{9,11},{10,... | collective-permute-start | bytes 199688 | tf_op jit(solution)/shard_map/ppermute | solution.py:18
  11.5 1.7 %collective-permute-done.1.refs_2_ = bf16[4,8320]{1,0:T(4,128)(2,1)S(1)} collective-permute-done((bf16[4,8320]{1,0:T(4,128)(2,1)S(1)}, bf16[4,8320]{1,0:T(4,128)(2,1)S(1)}, u32[]{:S(2)}, u32[]{:S(2)}) %collective-permute-start.1) | collective-permute-done | bytes 66592 | tf_op jit(solution)/shard_map/ppermute | solution.py:18
  13.2 1.5 %collective-permute-start.5 = (bf16[4,8320]{1,0:T(4,128)(2,1)S(1)}, bf16[4,8320]{1,0:T(4,128)(2,1)S(1)}, u32[]{:S(2)}, u32[]{:S(2)}) collective-permute-start(bf16[4,8320]{1,0:T(4,128)(2,1)S(1)} %collective-permute-done.1.refs_2_), channel_id=1, source_target_pairs={{0,2},{1,3},{2,0},{3,1},{4,6},{5,7},{6,4},{7,5},{8,10},{9,11},{10,... | collective-permute-start | bytes 199688 | tf_op jit(solution)/shard_map/ppermute | solution.py:18
  14.7 0.0 collective-permute-done.refs_1_
  14.7 0.5 collective-permute-start.4
  15.3 0.0 collective-permute-done.3.refs_4_
  15.3 2.9 %collective-permute-done.5.refs_6_ = bf16[4,8320]{1,0:T(4,128)(2,1)S(1)} collective-permute-done((bf16[4,8320]{1,0:T(4,128)(2,1)S(1)}, bf16[4,8320]{1,0:T(4,128)(2,1)S(1)}, u32[]{:S(2)}, u32[]{:S(2)}) %collective-permute-start.5) | collective-permute-done | bytes 66592 | tf_op jit(solution)/shard_map/ppermute | solution.py:18
  18.2 0.8 collective-permute-done.4.refs_5_
  19.0 0.1 pack.2.refs_2_.refs_3_.refs_0_
  19.1 0.1 collective-permute-start.7
  19.2 0.0 collective-permute-done.8
  19.2 1.3 %down.2 = (bf16[24,128]{1,0:T(8,128)(2,1)S(1)}, bf16[2,16,8192]{2,1,0:T(8,128)(2,1)S(1)}, bf16[1024,640]{1,0:T(8,128)(2,1)S(1)}) custom-call(bf16[2,48,8192]{2,1,0:T(8,128)(2,1)S(1)} %get-tuple-element.31.refs_0_, bf16[2,64,8192]{2,1,0:T(8,128)(2,1)S(1)} %bitcast.11, bf16[32,8320]{1,0:T(8,128)(2,1)S(1)} %pack.2.refs_2_.refs_3_.refs_0_, ...), custom_call_target="tpu_custom_call" | custom-call | flops 100663296 | bytes 4194304 | tf_op jit(solution)/shard_map/down/pallas_call | solution.py:430
  20.6 2.5 %collective-permute-start.11 = (bf16[24,128]{1,0:T(8,128)(2,1)S(1)}, bf16[24,128]{1,0:T(8,128)(2,1)S(1)}, u32[]{:S(2)}, u32[]{:S(2)}) collective-permute-start(bf16[24,128]{1,0:T(8,128)(2,1)S(1)} %get-tuple-element.33.refs_4_), channel_id=1, source_target_pairs={{0,12},{1,13},{2,14},{3,15},{4,8},{5,9},{6,10},{7,11},{8,4},{9,5},... | collective-permute-start | bytes 18440 | tf_op jit(solution)/shard_map/ppermute | solution.py:18
  23.1 0.0 collective-permute-start.10
  23.1 1.9 %collective-permute-start.9 = (bf16[24,128]{1,0:T(8,128)(2,1)S(1)}, bf16[24,128]{1,0:T(8,128)(2,1)S(1)}, u32[]{:S(2)}, u32[]{:S(2)}) collective-permute-start(bf16[24,128]{1,0:T(8,128)(2,1)S(1)} %get-tuple-element.33.refs_4_), channel_id=1, source_target_pairs={{0,4},{1,5},{2,6},{3,7},{4,0},{5,1},{6,2},{7,3},{8,12},{9,13},{10,... | collective-permute-start | bytes 18440 | tf_op jit(solution)/shard_map/ppermute | solution.py:18
  25.0 0.0 collective-permute-done.7.refs_1_
  25.0 2.9 %base.4.refs_4_ = f32[64,640]{1,0:T(8,128)S(1)} custom-call(bf16[32,8320]{1,0:T(8,128)(2,1)S(1)} %pack.2.refs_2_.refs_3_.refs_0_, bf16[32,8320]{1,0:T(8,128)(2,1)S(1)} %collective-permute-done.7.refs_1_, bf16[1024,640]{1,0:T(8,128)(2,1)S(1)} %get-tuple-element.34.refs_2_, bf16[8192,640]{1,0:T(8,128)(2,1)} %refs_3_.7, ...), custom_call_target="tpu_custom_call" | custom-call | flops 335544320 | bytes 10485760 | tf_op jit(solution)/shard_map/base/pallas_call | solution.py:452
  28.0 0.0 collective-permute-done.11
  28.0 0.0 collective-permute-done.10
  28.0 0.2 collective-permute-start.14
  28.2 1.1 %collective-permute-start.13 = (bf16[24,128]{1,0:T(8,128)(2,1)S(1)}, bf16[24,128]{1,0:T(8,128)(2,1)S(1)}, u32[]{:S(2)}, u32[]{:S(2)}) collective-permute-start(bf16[24,128]{1,0:T(8,128)(2,1)S(1)} %add_add_fusion.1.refs_4_), channel_id=1, source_target_pairs={{0,2},{1,3},{2,0},{3,1},{4,6},{5,7},{6,4},{7,5},{8,10},{9,11},{10,... | collective-permute-start | bytes 18440 | tf_op jit(solution)/shard_map/ppermute | solution.py:18
  29.4 0.6 collective-permute-start.12
  30.0 3.1 %base.5.refs_5_ = f32[64,640]{1,0:T(8,128)S(1)} custom-call(bf16[32,8320]{1,0:T(8,128)(2,1)S(1)} %pack.2.refs_2_.refs_3_.refs_0_, bf16[32,8320]{1,0:T(8,128)(2,1)S(1)} %collective-permute-done.7.refs_1_, bf16[1024,640]{1,0:T(8,128)(2,1)S(1)} %get-tuple-element.38.refs_2_, bf16[8192,640]{1,0:T(8,128)(2,1)} %refs_3_.7, bf16[24,128]{1,0:T(8,128)(2,1)S(1)} %add_add_fusion.1.refs_4_), custom_call_target="tpu_custom_call" | custom-call | flops 335544320 | bytes 10485760 | tf_op jit(solution)/shard_map/base/pallas_call | solution.py:452
  33.1 0.0 copy-start.5
  33.1 0.0 collective-permute-done.14
  33.1 0.7 lift.2
  33.8 11.5 %all_to_all.10 = bf16[16,4,640]{2,1,0:T(4,128)(2,1)S(1)} all-to-all(bf16[16,4,640]{2,1,0:T(4,128)(2,1)S(1)} %lift.2), channel_id=1, replica_groups=mesh['groups'=2,'tensor'=16] {'tensor'}, dimensions={0} | all-to-all | bytes 163840 | tf_op jit(solution)/shard_map/all_to_all | solution.py:22
  45.4 0.0 copy-start
  45.4 4.3 %attend.1 = (bf16[4,8192]{1,0:T(4,128)(2,1)S(1)}, bf16[2048,512]{1,0:T(8,128)(2,1)S(1)}, bf16[2048,512]{1,0:T(8,128)(2,1)S(1)}) custom-call(s32[4]{0:T(128)S(1)} %copy-done.5, bf16[4,10240]{1,0:T(4,128)(2,1)S(1)} %bitcast.12, bf16[4,8,384,128]{3,2,1,0:T(8,128)(2,1)S(1)} %copy-done.1, bf16[4,8,384,128]{3,2,1,0:T(8,128)(2,1)S(1)} %copy-done.2, ...), custom_call_target="tpu_custom_call" | custom-call | flops 50331648 | bytes 6291456 | tf_op jit(solution)/shard_map/attend/pallas_call | solution.py:518
  49.6 0.7 collective-permute-start.17
  50.3 0.8 collective-permute-start.16
  51.1 3.0 %collective-permute-start.15 = (bf16[4,8192]{1,0:T(4,128)(2,1)S(1)}, bf16[4,8192]{1,0:T(4,128)(2,1)S(1)}, u32[]{:S(2)}, u32[]{:S(2)}) collective-permute-start(bf16[4,8192]{1,0:T(4,128)(2,1)S(1)} %get-tuple-element.44.refs_0_), channel_id=1, source_target_pairs={{0,4},{1,5},{2,6},{3,7},{4,0},{5,1},{6,2},{7,3},{8,12},{9,13},{10,... | collective-permute-start | bytes 196616 | tf_op jit(solution)/shard_map/ppermute | solution.py:18
  54.1 2.4 %collective-permute-done.17.refs_3_ = bf16[4,8192]{1,0:T(4,128)(2,1)S(1)} collective-permute-done((bf16[4,8192]{1,0:T(4,128)(2,1)S(1)}, bf16[4,8192]{1,0:T(4,128)(2,1)S(1)}, u32[]{:S(2)}, u32[]{:S(2)}) %collective-permute-start.17) | collective-permute-done | bytes 65568 | tf_op jit(solution)/shard_map/ppermute | solution.py:18
  56.5 0.0 collective-permute-start.21
  56.5 1.3 %collective-permute-done.16.refs_2_ = bf16[4,8192]{1,0:T(4,128)(2,1)S(1)} collective-permute-done((bf16[4,8192]{1,0:T(4,128)(2,1)S(1)}, bf16[4,8192]{1,0:T(4,128)(2,1)S(1)}, u32[]{:S(2)}, u32[]{:S(2)}) %collective-permute-start.16) | collective-permute-done | bytes 65568 | tf_op jit(solution)/shard_map/ppermute | solution.py:18
  57.8 0.7 collective-permute-start.20
  58.5 0.0 collective-permute-done.15.refs_1_
  58.5 1.3 %collective-permute-start.19 = (bf16[4,8192]{1,0:T(4,128)(2,1)S(1)}, bf16[4,8192]{1,0:T(4,128)(2,1)S(1)}, u32[]{:S(2)}, u32[]{:S(2)}) collective-permute-start(bf16[4,8192]{1,0:T(4,128)(2,1)S(1)} %collective-permute-done.15.refs_1_), channel_id=1, source_target_pairs={{0,2},{1,3},{2,0},{3,1},{4,6},{5,7},{6,4},{7,5},{8,10},{9,11},{10,... | collective-permute-start | bytes 196616 | tf_op jit(solution)/shard_map/ppermute | solution.py:18
  59.8 1.3 %collective-permute-done.21.refs_7_ = bf16[4,8192]{1,0:T(4,128)(2,1)S(1)} collective-permute-done((bf16[4,8192]{1,0:T(4,128)(2,1)S(1)}, bf16[4,8192]{1,0:T(4,128)(2,1)S(1)}, u32[]{:S(2)}, u32[]{:S(2)}) %collective-permute-start.21) | collective-permute-done | bytes 65568 | tf_op jit(solution)/shard_map/ppermute | solution.py:18
  61.2 1.6 %collective-permute-done.20.refs_6_ = bf16[4,8192]{1,0:T(4,128)(2,1)S(1)} collective-permute-done((bf16[4,8192]{1,0:T(4,128)(2,1)S(1)}, bf16[4,8192]{1,0:T(4,128)(2,1)S(1)}, u32[]{:S(2)}, u32[]{:S(2)}) %collective-permute-start.20) | collective-permute-done | bytes 65568 | tf_op jit(solution)/shard_map/ppermute | solution.py:18
  62.8 0.8 collective-permute-done.19.refs_5_
  63.6 0.1 pack.3.refs_2_.refs_0_
  63.7 0.1 collective-permute-start.25
  63.8 0.5 down.3.refs_4_
  64.3 1.1 %collective-permute-start.24 = (bf16[8,128]{1,0:T(8,128)(2,1)S(1)}, bf16[8,128]{1,0:T(8,128)(2,1)S(1)}, u32[]{:S(2)}, u32[]{:S(2)}) collective-permute-start(bf16[8,128]{1,0:T(8,128)(2,1)S(1)} %down.3.refs_4_), channel_id=1, source_target_pairs={{0,12},{1,13},{2,14},{3,15},{4,8},{5,9},{6,10},{7,11},{8,4},{9,5},... | collective-permute-start | bytes 6152 | tf_op jit(solution)/shard_map/ppermute | solution.py:18
  65.4 0.0 collective-permute-start.23
  65.4 3.3 %collective-permute-start.22 = (bf16[8,128]{1,0:T(8,128)(2,1)S(1)}, bf16[8,128]{1,0:T(8,128)(2,1)S(1)}, u32[]{:S(2)}, u32[]{:S(2)}) collective-permute-start(bf16[8,128]{1,0:T(8,128)(2,1)S(1)} %down.3.refs_4_), channel_id=1, source_target_pairs={{0,4},{1,5},{2,6},{3,7},{4,0},{5,1},{6,2},{7,3},{8,12},{9,13},{10,... | collective-permute-start | bytes 6152 | tf_op jit(solution)/shard_map/ppermute | solution.py:18
  68.8 1.8 %base.6.refs_4_ = f32[64,512]{1,0:T(8,128)S(1)} custom-call(bf16[32,8192]{1,0:T(8,128)(2,1)S(1)} %pack.3.refs_2_.refs_0_, bf16[32,8192]{1,0:T(8,128)(2,1)S(1)} %collective-permute-done.25.refs_1_, bf16[2048,512]{1,0:T(8,128)(2,1)S(1)} %get-tuple-element.45.refs_2_, bf16[8192,512]{1,0:T(8,128)(2,1)} %refs_3_.10, bf16[8,128]{1,0:T(8,128)(2,1)S(1)} %down.3.refs_4_), custom_call_target="tpu_custom_call" | custom-call | flops 268435456 | bytes 8388608 | tf_op jit(solution)/shard_map/base/pallas_call | solution.py:452
  70.6 0.0 collective-permute-done.23
  70.6 0.1 collective-permute-start.28
  70.7 1.3 %collective-permute-start.27 = (bf16[8,128]{1,0:T(8,128)(2,1)S(1)}, bf16[8,128]{1,0:T(8,128)(2,1)S(1)}, u32[]{:S(2)}, u32[]{:S(2)}) collective-permute-start(bf16[8,128]{1,0:T(8,128)(2,1)S(1)} %add_add_fusion.3.refs_4_), channel_id=1, source_target_pairs={{0,2},{1,3},{2,0},{3,1},{4,6},{5,7},{6,4},{7,5},{8,10},{9,11},{10,... | collective-permute-start | bytes 6152 | tf_op jit(solution)/shard_map/ppermute | solution.py:18
  72.0 0.6 collective-permute-start.26
  72.5 1.8 %base.7.refs_5_ = f32[64,512]{1,0:T(8,128)S(1)} custom-call(bf16[32,8192]{1,0:T(8,128)(2,1)S(1)} %pack.3.refs_2_.refs_0_, bf16[32,8192]{1,0:T(8,128)(2,1)S(1)} %collective-permute-done.25.refs_1_, bf16[2048,512]{1,0:T(8,128)(2,1)S(1)} %get-tuple-element.49.refs_2_, bf16[8192,512]{1,0:T(8,128)(2,1)} %refs_3_.10, bf16[8,128]{1,0:T(8,128)(2,1)S(1)} %add_add_fusion.3.refs_4_), custom_call_target="tpu_custom_call" | custom-call | flops 268435456 | bytes 8388608 | tf_op jit(solution)/shard_map/base/pallas_call | solution.py:452
  74.4 0.0 collective-permute-done.26
  74.4 0.6 lift.3
  75.1 10.3 %all_to_all.11 = bf16[16,4,512]{2,1,0:T(4,128)(2,1)S(1)} all-to-all(bf16[16,4,512]{2,1,0:T(4,128)(2,1)S(1)} %lift.3), channel_id=1, replica_groups=mesh['groups'=2,'tensor'=16] {'tensor'}, dimensions={0} | all-to-all | bytes 131072 | tf_op jit(solution)/shard_map/all_to_all | solution.py:22
  85.3 0.6 copy.14
  (25 shorter events, 0.1 us)
Async XLA Ops:
  0.0 19.2 %collective-permute-start.8 = (bf16[2,8192,64]{1,2,0:T(8,128)(2,1)}, bf16[2,8192,64]{1,2,0:T(8,128)(2,1)S(1)}, u32[]{:S(2)}, u32[]{:S(2)}) collective-permute-start(bf16[2,8192,64]{1,2,0:T(8,128)(2,1)} %param.19), channel_id=1, source_target_pairs={{0,1},{1,0},{2,3},{3,2},{4,5},{5,4},{6,7},{7,6},{8,9},{9,8},{10,11... | collective-permute-start | bytes 6291464 | tf_op jit(solution)/shard_map/ppermute | solution.py:18
  2.4 7.7 %collective-permute-start.2 = (bf16[4,8320]{1,0:T(4,128)(2,1)S(1)}, bf16[4,8320]{1,0:T(4,128)(2,1)S(1)}, u32[]{:S(2)}, u32[]{:S(2)}) collective-permute-start(bf16[4,8320]{1,0:T(4,128)(2,1)S(1)} %get-tuple-element.30.refs_0_), channel_id=1, source_target_pairs={{0,12},{1,13},{2,14},{3,15},{4,8},{5,9},{6,10},{7,11},{8,4},{9,5},... | collective-permute-start | bytes 199688 | tf_op jit(solution)/shard_map/ppermute | solution.py:18
  7.0 6.2 %collective-permute-start.1 = (bf16[4,8320]{1,0:T(4,128)(2,1)S(1)}, bf16[4,8320]{1,0:T(4,128)(2,1)S(1)}, u32[]{:S(2)}, u32[]{:S(2)}) collective-permute-start(bf16[4,8320]{1,0:T(4,128)(2,1)S(1)} %get-tuple-element.30.refs_0_), channel_id=1, source_target_pairs={{0,8},{1,9},{2,10},{3,11},{4,12},{5,13},{6,14},{7,15},{8,0},{9,1},... | collective-permute-start | bytes 199688 | tf_op jit(solution)/shard_map/ppermute | solution.py:18
  7.0 7.7 %collective-permute-start = (bf16[4,8320]{1,0:T(4,128)(2,1)S(1)}, bf16[4,8320]{1,0:T(4,128)(2,1)S(1)}, u32[]{:S(2)}, u32[]{:S(2)}) collective-permute-start(bf16[4,8320]{1,0:T(4,128)(2,1)S(1)} %get-tuple-element.30.refs_0_), channel_id=1, source_target_pairs={{0,4},{1,5},{2,6},{3,7},{4,0},{5,1},{6,2},{7,3},{8,12},{9,13},{10,... | collective-permute-start | bytes 199688 | tf_op jit(solution)/shard_map/ppermute | solution.py:18
  7.7 7.6 %collective-permute-start.3 = (bf16[4,8320]{1,0:T(4,128)(2,1)S(1)}, bf16[4,8320]{1,0:T(4,128)(2,1)S(1)}, u32[]{:S(2)}, u32[]{:S(2)}) collective-permute-start(bf16[4,8320]{1,0:T(4,128)(2,1)S(1)} %get-tuple-element.30.refs_0_), channel_id=1, source_target_pairs={{0,2},{1,3},{2,0},{3,1},{4,6},{5,7},{6,4},{7,5},{8,10},{9,11},{10,... | collective-permute-start | bytes 199688 | tf_op jit(solution)/shard_map/ppermute | solution.py:18
  10.0 5.3 %collective-permute-start.6 = (bf16[4,8320]{1,0:T(4,128)(2,1)S(1)}, bf16[4,8320]{1,0:T(4,128)(2,1)S(1)}, u32[]{:S(2)}, u32[]{:S(2)}) collective-permute-start(bf16[4,8320]{1,0:T(4,128)(2,1)S(1)} %collective-permute-done.2.refs_3_), channel_id=1, source_target_pairs={{0,2},{1,3},{2,0},{3,1},{4,6},{5,7},{6,4},{7,5},{8,10},{9,11},{10,... | collective-permute-start | bytes 199688 | tf_op jit(solution)/shard_map/ppermute | solution.py:18
  13.2 5.0 %collective-permute-start.5 = (bf16[4,8320]{1,0:T(4,128)(2,1)S(1)}, bf16[4,8320]{1,0:T(4,128)(2,1)S(1)}, u32[]{:S(2)}, u32[]{:S(2)}) collective-permute-start(bf16[4,8320]{1,0:T(4,128)(2,1)S(1)} %collective-permute-done.1.refs_2_), channel_id=1, source_target_pairs={{0,2},{1,3},{2,0},{3,1},{4,6},{5,7},{6,4},{7,5},{8,10},{9,11},{10,... | collective-permute-start | bytes 199688 | tf_op jit(solution)/shard_map/ppermute | solution.py:18
  14.7 4.3 %collective-permute-start.4 = (bf16[4,8320]{1,0:T(4,128)(2,1)S(1)}, bf16[4,8320]{1,0:T(4,128)(2,1)S(1)}, u32[]{:S(2)}, u32[]{:S(2)}) collective-permute-start(bf16[4,8320]{1,0:T(4,128)(2,1)S(1)} %collective-permute-done.refs_1_), channel_id=1, source_target_pairs={{0,2},{1,3},{2,0},{3,1},{4,6},{5,7},{6,4},{7,5},{8,10},{9,11},{10,... | collective-permute-start | bytes 199688 | tf_op jit(solution)/shard_map/ppermute | solution.py:18
  19.1 5.9 %collective-permute-start.7 = (bf16[32,8320]{1,0:T(8,128)(2,1)S(1)}, bf16[32,8320]{1,0:T(8,128)(2,1)S(1)}, u32[]{:S(2)}, u32[]{:S(2)}) collective-permute-start(bf16[32,8320]{1,0:T(8,128)(2,1)S(1)} %pack.2.refs_2_.refs_3_.refs_0_), channel_id=1, source_target_pairs={{0,1},{1,0},{2,3},{3,2},{4,5},{5,4},{6,7},{7,6},{8,9},{9,8},{10,11... | collective-permute-start | bytes 1597448 | tf_op jit(solution)/shard_map/ppermute | solution.py:18
  20.6 7.4 %collective-permute-start.11 = (bf16[24,128]{1,0:T(8,128)(2,1)S(1)}, bf16[24,128]{1,0:T(8,128)(2,1)S(1)}, u32[]{:S(2)}, u32[]{:S(2)}) collective-permute-start(bf16[24,128]{1,0:T(8,128)(2,1)S(1)} %get-tuple-element.33.refs_4_), channel_id=1, source_target_pairs={{0,12},{1,13},{2,14},{3,15},{4,8},{5,9},{6,10},{7,11},{8,4},{9,5},... | collective-permute-start | bytes 18440 | tf_op jit(solution)/shard_map/ppermute | solution.py:18
  23.1 4.9 %collective-permute-start.10 = (bf16[24,128]{1,0:T(8,128)(2,1)S(1)}, bf16[24,128]{1,0:T(8,128)(2,1)S(1)}, u32[]{:S(2)}, u32[]{:S(2)}) collective-permute-start(bf16[24,128]{1,0:T(8,128)(2,1)S(1)} %get-tuple-element.33.refs_4_), channel_id=1, source_target_pairs={{0,8},{1,9},{2,10},{3,11},{4,12},{5,13},{6,14},{7,15},{8,0},{9,1},... | collective-permute-start | bytes 18440 | tf_op jit(solution)/shard_map/ppermute | solution.py:18
  23.1 4.9 %collective-permute-start.9 = (bf16[24,128]{1,0:T(8,128)(2,1)S(1)}, bf16[24,128]{1,0:T(8,128)(2,1)S(1)}, u32[]{:S(2)}, u32[]{:S(2)}) collective-permute-start(bf16[24,128]{1,0:T(8,128)(2,1)S(1)} %get-tuple-element.33.refs_4_), channel_id=1, source_target_pairs={{0,4},{1,5},{2,6},{3,7},{4,0},{5,1},{6,2},{7,3},{8,12},{9,13},{10,... | collective-permute-start | bytes 18440 | tf_op jit(solution)/shard_map/ppermute | solution.py:18
  28.0 5.0 %collective-permute-start.14 = (bf16[24,128]{1,0:T(8,128)(2,1)S(1)}, bf16[24,128]{1,0:T(8,128)(2,1)S(1)}, u32[]{:S(2)}, u32[]{:S(2)}) collective-permute-start(bf16[24,128]{1,0:T(8,128)(2,1)S(1)} %add_add_fusion.1.refs_4_), channel_id=1, source_target_pairs={{0,3},{1,2},{2,1},{3,0},{4,7},{5,6},{6,5},{7,4},{8,11},{9,10},{10,... | collective-permute-start | bytes 18440 | tf_op jit(solution)/shard_map/ppermute | solution.py:18
  28.2 4.8 %collective-permute-start.13 = (bf16[24,128]{1,0:T(8,128)(2,1)S(1)}, bf16[24,128]{1,0:T(8,128)(2,1)S(1)}, u32[]{:S(2)}, u32[]{:S(2)}) collective-permute-start(bf16[24,128]{1,0:T(8,128)(2,1)S(1)} %add_add_fusion.1.refs_4_), channel_id=1, source_target_pairs={{0,2},{1,3},{2,0},{3,1},{4,6},{5,7},{6,4},{7,5},{8,10},{9,11},{10,... | collective-permute-start | bytes 18440 | tf_op jit(solution)/shard_map/ppermute | solution.py:18
  29.4 3.7 %collective-permute-start.12 = (bf16[24,128]{1,0:T(8,128)(2,1)S(1)}, bf16[24,128]{1,0:T(8,128)(2,1)S(1)}, u32[]{:S(2)}, u32[]{:S(2)}) collective-permute-start(bf16[24,128]{1,0:T(8,128)(2,1)S(1)} %add_add_fusion.1.refs_4_), channel_id=1, source_target_pairs={{0,1},{1,0},{2,3},{3,2},{4,5},{5,4},{6,7},{7,6},{8,9},{9,8},{10,11... | collective-permute-start | bytes 18440 | tf_op jit(solution)/shard_map/ppermute | solution.py:18
  30.0 3.2 %copy-start.3 = (bf16[32,16,640]{2,1,0:T(8,128)(2,1)S(1)}, bf16[32,16,640]{2,1,0:T(8,128)(2,1)}, u32[]{:S(2)}) copy-start(bf16[32,16,640]{2,1,0:T(8,128)(2,1)} %refs_3_.8) | copy-start | bytes 1966084
  30.0 15.4 %copy-start.1 = (bf16[4,8,384,128]{3,2,1,0:T(8,128)(2,1)S(1)}, bf16[4,8,384,128]{3,2,1,0:T(8,128)(2,1)}, u32[]{:S(2)}) copy-start(bf16[4,8,384,128]{3,2,1,0:T(8,128)(2,1)} %keys_ref.1) | copy-start | bytes 9437188
  30.0 15.4 %copy-start.2 = (bf16[4,8,384,128]{3,2,1,0:T(8,128)(2,1)S(1)}, bf16[4,8,384,128]{3,2,1,0:T(8,128)(2,1)}, u32[]{:S(2)}) copy-start(bf16[4,8,384,128]{3,2,1,0:T(8,128)(2,1)} %values_ref.1) | copy-start | bytes 9437188
  33.1 12.3 %copy-start.5 = (s32[4]{0:T(128)S(1)}, s32[4]{0:T(128)}, u32[]{:S(2)}) copy-start(s32[4]{0:T(128)} %lengths_ref.1) | copy-start | bytes 52
  45.4 18.4 %copy-start = (bf16[2,8192,64]{1,2,0:T(8,128)(2,1)S(1)}, bf16[2,8192,64]{1,2,0:T(8,128)(2,1)}, u32[]{:S(2)}) copy-start(bf16[2,8192,64]{1,2,0:T(8,128)(2,1)} %param.19) | copy-start | bytes 6291460
  49.6 6.8 %collective-permute-start.17 = (bf16[4,8192]{1,0:T(4,128)(2,1)S(1)}, bf16[4,8192]{1,0:T(4,128)(2,1)S(1)}, u32[]{:S(2)}, u32[]{:S(2)}) collective-permute-start(bf16[4,8192]{1,0:T(4,128)(2,1)S(1)} %get-tuple-element.44.refs_0_), channel_id=1, source_target_pairs={{0,12},{1,13},{2,14},{3,15},{4,8},{5,9},{6,10},{7,11},{8,4},{9,5},... | collective-permute-start | bytes 196616 | tf_op jit(solution)/shard_map/ppermute | solution.py:18
  50.3 7.5 %collective-permute-start.16 = (bf16[4,8192]{1,0:T(4,128)(2,1)S(1)}, bf16[4,8192]{1,0:T(4,128)(2,1)S(1)}, u32[]{:S(2)}, u32[]{:S(2)}) collective-permute-start(bf16[4,8192]{1,0:T(4,128)(2,1)S(1)} %get-tuple-element.44.refs_0_), channel_id=1, source_target_pairs={{0,8},{1,9},{2,10},{3,11},{4,12},{5,13},{6,14},{7,15},{8,0},{9,1},... | collective-permute-start | bytes 196616 | tf_op jit(solution)/shard_map/ppermute | solution.py:18
  51.1 7.4 %collective-permute-start.15 = (bf16[4,8192]{1,0:T(4,128)(2,1)S(1)}, bf16[4,8192]{1,0:T(4,128)(2,1)S(1)}, u32[]{:S(2)}, u32[]{:S(2)}) collective-permute-start(bf16[4,8192]{1,0:T(4,128)(2,1)S(1)} %get-tuple-element.44.refs_0_), channel_id=1, source_target_pairs={{0,4},{1,5},{2,6},{3,7},{4,0},{5,1},{6,2},{7,3},{8,12},{9,13},{10,... | collective-permute-start | bytes 196616 | tf_op jit(solution)/shard_map/ppermute | solution.py:18
  54.1 5.7 %collective-permute-start.18 = (bf16[4,8192]{1,0:T(4,128)(2,1)S(1)}, bf16[4,8192]{1,0:T(4,128)(2,1)S(1)}, u32[]{:S(2)}, u32[]{:S(2)}) collective-permute-start(bf16[4,8192]{1,0:T(4,128)(2,1)S(1)} %get-tuple-element.44.refs_0_), channel_id=1, source_target_pairs={{0,2},{1,3},{2,0},{3,1},{4,6},{5,7},{6,4},{7,5},{8,10},{9,11},{10,... | collective-permute-start | bytes 196616 | tf_op jit(solution)/shard_map/ppermute | solution.py:18
  56.5 4.7 %collective-permute-start.21 = (bf16[4,8192]{1,0:T(4,128)(2,1)S(1)}, bf16[4,8192]{1,0:T(4,128)(2,1)S(1)}, u32[]{:S(2)}, u32[]{:S(2)}) collective-permute-start(bf16[4,8192]{1,0:T(4,128)(2,1)S(1)} %collective-permute-done.17.refs_3_), channel_id=1, source_target_pairs={{0,2},{1,3},{2,0},{3,1},{4,6},{5,7},{6,4},{7,5},{8,10},{9,11},{10,... | collective-permute-start | bytes 196616 | tf_op jit(solution)/shard_map/ppermute | solution.py:18
  57.8 5.0 %collective-permute-start.20 = (bf16[4,8192]{1,0:T(4,128)(2,1)S(1)}, bf16[4,8192]{1,0:T(4,128)(2,1)S(1)}, u32[]{:S(2)}, u32[]{:S(2)}) collective-permute-start(bf16[4,8192]{1,0:T(4,128)(2,1)S(1)} %collective-permute-done.16.refs_2_), channel_id=1, source_target_pairs={{0,2},{1,3},{2,0},{3,1},{4,6},{5,7},{6,4},{7,5},{8,10},{9,11},{10,... | collective-permute-start | bytes 196616 | tf_op jit(solution)/shard_map/ppermute | solution.py:18
  58.5 5.0 %collective-permute-start.19 = (bf16[4,8192]{1,0:T(4,128)(2,1)S(1)}, bf16[4,8192]{1,0:T(4,128)(2,1)S(1)}, u32[]{:S(2)}, u32[]{:S(2)}) collective-permute-start(bf16[4,8192]{1,0:T(4,128)(2,1)S(1)} %collective-permute-done.15.refs_1_), channel_id=1, source_target_pairs={{0,2},{1,3},{2,0},{3,1},{4,6},{5,7},{6,4},{7,5},{8,10},{9,11},{10,... | collective-permute-start | bytes 196616 | tf_op jit(solution)/shard_map/ppermute | solution.py:18
  63.7 5.1 %collective-permute-start.25 = (bf16[32,8192]{1,0:T(8,128)(2,1)S(1)}, bf16[32,8192]{1,0:T(8,128)(2,1)S(1)}, u32[]{:S(2)}, u32[]{:S(2)}) collective-permute-start(bf16[32,8192]{1,0:T(8,128)(2,1)S(1)} %pack.3.refs_2_.refs_0_), channel_id=1, source_target_pairs={{0,1},{1,0},{2,3},{3,2},{4,5},{5,4},{6,7},{7,6},{8,9},{9,8},{10,11... | collective-permute-start | bytes 1572872 | tf_op jit(solution)/shard_map/ppermute | solution.py:18
  64.3 6.3 %collective-permute-start.24 = (bf16[8,128]{1,0:T(8,128)(2,1)S(1)}, bf16[8,128]{1,0:T(8,128)(2,1)S(1)}, u32[]{:S(2)}, u32[]{:S(2)}) collective-permute-start(bf16[8,128]{1,0:T(8,128)(2,1)S(1)} %down.3.refs_4_), channel_id=1, source_target_pairs={{0,12},{1,13},{2,14},{3,15},{4,8},{5,9},{6,10},{7,11},{8,4},{9,5},... | collective-permute-start | bytes 6152 | tf_op jit(solution)/shard_map/ppermute | solution.py:18
  65.4 5.1 %collective-permute-start.23 = (bf16[8,128]{1,0:T(8,128)(2,1)S(1)}, bf16[8,128]{1,0:T(8,128)(2,1)S(1)}, u32[]{:S(2)}, u32[]{:S(2)}) collective-permute-start(bf16[8,128]{1,0:T(8,128)(2,1)S(1)} %down.3.refs_4_), channel_id=1, source_target_pairs={{0,8},{1,9},{2,10},{3,11},{4,12},{5,13},{6,14},{7,15},{8,0},{9,1},... | collective-permute-start | bytes 6152 | tf_op jit(solution)/shard_map/ppermute | solution.py:18
  65.4 5.2 %collective-permute-start.22 = (bf16[8,128]{1,0:T(8,128)(2,1)S(1)}, bf16[8,128]{1,0:T(8,128)(2,1)S(1)}, u32[]{:S(2)}, u32[]{:S(2)}) collective-permute-start(bf16[8,128]{1,0:T(8,128)(2,1)S(1)} %down.3.refs_4_), channel_id=1, source_target_pairs={{0,4},{1,5},{2,6},{3,7},{4,0},{5,1},{6,2},{7,3},{8,12},{9,13},{10,... | collective-permute-start | bytes 6152 | tf_op jit(solution)/shard_map/ppermute | solution.py:18
  70.6 3.8 %collective-permute-start.28 = (bf16[8,128]{1,0:T(8,128)(2,1)S(1)}, bf16[8,128]{1,0:T(8,128)(2,1)S(1)}, u32[]{:S(2)}, u32[]{:S(2)}) collective-permute-start(bf16[8,128]{1,0:T(8,128)(2,1)S(1)} %add_add_fusion.3.refs_4_), channel_id=1, source_target_pairs={{0,3},{1,2},{2,1},{3,0},{4,7},{5,6},{6,5},{7,4},{8,11},{9,10},{10,... | collective-permute-start | bytes 6152 | tf_op jit(solution)/shard_map/ppermute | solution.py:18
  70.7 3.7 %collective-permute-start.27 = (bf16[8,128]{1,0:T(8,128)(2,1)S(1)}, bf16[8,128]{1,0:T(8,128)(2,1)S(1)}, u32[]{:S(2)}, u32[]{:S(2)}) collective-permute-start(bf16[8,128]{1,0:T(8,128)(2,1)S(1)} %add_add_fusion.3.refs_4_), channel_id=1, source_target_pairs={{0,2},{1,3},{2,0},{3,1},{4,6},{5,7},{6,4},{7,5},{8,10},{9,11},{10,... | collective-permute-start | bytes 6152 | tf_op jit(solution)/shard_map/ppermute | solution.py:18
  72.0 2.4 %collective-permute-start.26 = (bf16[8,128]{1,0:T(8,128)(2,1)S(1)}, bf16[8,128]{1,0:T(8,128)(2,1)S(1)}, u32[]{:S(2)}, u32[]{:S(2)}) collective-permute-start(bf16[8,128]{1,0:T(8,128)(2,1)S(1)} %add_add_fusion.3.refs_4_), channel_id=1, source_target_pairs={{0,1},{1,0},{2,3},{3,2},{4,5},{5,4},{6,7},{7,6},{8,9},{9,8},{10,11... | collective-permute-start | bytes 6152 | tf_op jit(solution)/shard_map/ppermute | solution.py:18
  72.5 1.9 %copy-start.4 = (bf16[32,16,512]{2,1,0:T(8,128)(2,1)S(1)}, bf16[32,16,512]{2,1,0:T(8,128)(2,1)}, u32[]{:S(2)}) copy-start(bf16[32,16,512]{2,1,0:T(8,128)(2,1)} %refs_3_.11) | copy-start | bytes 1572868

commit v10 on v9

--- a/solution.py
+++ b/solution.py
@@ -41,7 +41,7 @@
 
 
 def pack_kernel(*refs):
-    *in_refs, out_ref = refs
+    in_refs, out_ref = refs[-2::-1], refs[-1]
     rows, width = in_refs[0].shape
     per = 16 // rows
     for first in range(0, len(in_refs), per):
@@ -59,16 +59,15 @@
         out_specs=spec(),
         compiler_params=pltpu.CompilerParams(vmem_limit_bytes=16 * 1024 * 1024),
         name="pack",
-    )(*parts)
+    )(*parts[::-1])
 
 
 def gather_rows(x, count):
     step = count // 4
-    far, middle, near = (swap(x, count, k * step) for k in (3, 2, 1))
+    near, middle, far = (swap(x, count, k * step) for k in (1, 2, 3))
     step //= 2
-    across = [swap(p, count, step) for p in (x, far, middle, near)]
-    parts = [x, near, middle, far] + [across[i] for i in (0, 3, 2, 1)]
-    held = [pack(parts)]
+    across = [swap(p, count, step) for p in (x, near, middle, far)]
+    held = [pack([x, near, middle, far] + across)]
     step //= 2
     while step > 1:
         held = held + [swap(h, count, step) for h in held]
@@ -117,6 +116,7 @@
     names_ref,
     slots_ref,
     sems,
+    row_sems,
 ):
     ranks = maps_ref.shape[1]
     copies = [
@@ -128,10 +128,9 @@
                 (names_hbm, names_ref),
                 (slots_hbm, slots_ref),
                 (maps_hbm.at[:, :ranks], maps_ref),
-                (weight_hbm.at[: weight_ref.shape[0]], weight_ref),
             )
         )
-    ]
+    ] + rows_copies(weight_hbm, 0, weight_ref, row_sems)
     for copy in copies:
         copy.start()
     for copy in copies[:4]:
@@ -155,8 +154,16 @@
 NT = (((1,), (1,)), ((), ()))
 
 
-def rows_copy(weight_hbm, start, rows_ref, sem):
-    return pltpu.make_async_copy(weight_hbm.at[start : start + rows_ref.shape[0]], rows_ref, sem)
+def rows_copies(weight_hbm, start, rows_ref, sems):
+    length = rows_ref.shape[0] // sems.shape[0]
+    return [
+        pltpu.make_async_copy(
+            weight_hbm.at[start + i * length : start + (i + 1) * length],
+            rows_ref.at[i * length : (i + 1) * length],
+            sems.at[i],
+        )
+        for i in range(sems.shape[0])
+    ]
 
 
 def down_kernel(count, rows, pieces, ranks, *refs):
@@ -164,8 +171,9 @@
     tag_refs, refs = refs[2 + pieces : 2 + 2 * pieces], refs[2 + 2 * pieces :]
     if len(refs) > 1:
         weight_hbm, out_ref, rest_ref, rows_ref, sems = refs
-        copy = rows_copy(weight_hbm, weight_hbm.shape[0] // 2, rows_ref, sems.at[0])
-        copy.start()
+        copies = rows_copies(weight_hbm, weight_hbm.shape[0] // 2, rows_ref, sems)
+        for copy in copies:
+            copy.start()
     else:
         (out_ref,) = refs
     me = lax.axis_index(AXIS)
@@ -200,51 +208,62 @@
     value = jnp.concatenate(folded, axis=1).astype(jnp.bfloat16)
     out_ref[...] = value
     if len(refs) > 1:
-        copy.wait()
+        for copy in copies:
+            copy.wait()
 
 
 def base_kernel(pieces, start, ready, *refs):
     ready_ref = refs[pieces]
-    weight_hbm, _, out_ref, weight_ref, sems = refs[pieces + 1 :]
+    weight_hbm, _, out_ref, weight_ref, sems, side_ref = refs[pieces + 1 :]
     total, columns = out_ref.shape
     whole = columns // 256 * 256
+    narrow = columns - whole == 128
     stream = weight_ref.shape[0]
-    spans = [(k, 1024) for k in range(0, stream - 1024, 1024)]
-    spans += [(stream - 1024, 512), (stream - 512, 512)]
-    copies = [
-        pltpu.make_async_copy(
-            weight_hbm.at[start + ready + k : start + ready + k + length],
-            weight_ref.at[k : k + length],
-            sems.at[i],
-        )
-        for i, (k, length) in enumerate(spans)
-    ]
+    copies = rows_copies(weight_hbm, start + ready, weight_ref, sems)
     for copy in copies:
         copy.start()
+    each = stream // len(copies)
+
+    def rows_of(at, length):
+        return jnp.concatenate([p[:, at : at + length] for p in refs[:pieces]], axis=0)
 
     def dot(x, weight):
         return jnp.dot(x, weight, preferred_element_type=jnp.float32)
 
-    steps = [(ready_ref, k, 1024, k, None) for k in range(0, ready, 1024)]
-    steps += [(weight_ref, k, n, ready + k, copy) for (k, n), copy in zip(spans, copies)]
-    for from_ref, k, length, offset, copy in steps:
-        at = start + offset
-        x = jnp.concatenate([p[:, at : at + length] for p in refs[:pieces]], axis=0)
-        if copy is not None:
-            copy.wait()
-        terms = []
+    def wide(from_ref, k, length, offset):
         if whole:
-            terms.append(dot(x, from_ref[k : k + length, :whole]))
-        if columns - whole == 128:
+            x = rows_of(start + offset, length)
+            term = dot(x, from_ref[k : k + length, :whole])
+            out_ref[:, :whole] = term if offset == 0 else out_ref[:, :whole] + term
+
+    def rest(weight, offset):
+        length = weight.shape[0]
+        if narrow:
             half = length // 2
-            left = jnp.concatenate([x[:, :half], x[:, half:]], axis=0)
-            right = [from_ref[k + h : k + h + half, whole:] for h in (0, half)]
-            both = dot(left, jnp.concatenate(right, axis=1))
-            terms.append(both[:total, :128] + both[total:, 128:])
-        elif columns > whole:
-            terms.append(dot(x, from_ref[k : k + length, whole:]))
-        term = terms[0] if len(terms) == 1 else jnp.concatenate(terms, axis=1)
-        out_ref[...] = term if offset == 0 else out_ref[...] + term
+            left = [rows_of(start + offset + h, half) for h in (0, half)]
+            right = [weight[:half], weight[half:]]
+            term = dot(jnp.concatenate(left, axis=0), jnp.concatenate(right, axis=1))
+        else:
+            term = dot(rows_of(start + offset, length), weight)
+        side_ref[...] = term if offset == 0 else side_ref[...] + term
+
+    wide(ready_ref, 0, ready, 0)
+    early = stream - 1024
+    for i, copy in enumerate(copies):
+        copy.wait()
+        at = (i + 1) * each
+        if at % 1024 == 0 and at <= early:
+            wide(weight_ref, at - 1024, 1024, ready + at - 1024)
+        if at == early and columns > whole:
+            parts = [ready_ref[:, whole:], weight_ref[:early, whole:]]
+            rest(jnp.concatenate(parts, axis=0), 0)
+    wide(weight_ref, early, 1024, ready + early)
+    if columns > whole:
+        rest(weight_ref[early:, whole:], ready + early)
+        if narrow:
+            out_ref[:, whole:] = side_ref[:total, :128] + side_ref[total:, 128:]
+        else:
+            out_ref[:, whole:] = side_ref[...]
 
 
 def lift_kernel(count, rows, pieces, bounds, rank, *refs):
@@ -294,10 +313,8 @@
 def attend_kernel(
     lengths_ref, qkv_ref, keys_ref, values_ref, weight_hbm, out_ref, low_ref, high_ref, sems
 ):
-    copies = [
-        rows_copy(weight_hbm, 0, low_ref, sems.at[0]),
-        rows_copy(weight_hbm, weight_hbm.shape[0] // 2, high_ref, sems.at[1]),
-    ]
+    copies = rows_copies(weight_hbm, 0, low_ref, sems.at[0])
+    copies += rows_copies(weight_hbm, weight_hbm.shape[0] // 2, high_ref, sems.at[1])
     for copy in copies:
         copy.start()
     rows, kv_heads, context, dim = keys_ref.shape
@@ -396,7 +413,8 @@
             VMEM((width,), bf16),
             SMEM((rows,), jnp.int32),
             SMEM(adapter_storage.shape, jnp.int32),
-            pltpu.SemaphoreType.DMA((6,)),
+            pltpu.SemaphoreType.DMA((5,)),
+            pltpu.SemaphoreType.DMA((4,)),
         ],
         compiler_params=params,
         name="norm",
@@ -436,7 +454,7 @@
             + tag_specs(tagged)
             + [spec(pltpu.HBM)] * len(extra),
             out_specs=out_specs,
-            scratch_shapes=[pltpu.SemaphoreType.DMA((1,))] * len(extra),
+            scratch_shapes=[pltpu.SemaphoreType.DMA((4,))] * len(extra),
             compiler_params=params,
             cost_estimate=pl.CostEstimate(
                 flops=2 * total * width * held * ranks,
@@ -449,6 +467,8 @@
     def base(pieces, weight, after, start, ready, length):
         columns = weight.shape[1]
         stream = length - ready.shape[0]
+        rest = columns % 256
+        side = (2 * total, 256) if rest == 128 else (total, max(rest, 1))
         return pl.pallas_call(
             functools.partial(base_kernel, len(pieces), start, length - stream),
             out_shape=jax.ShapeDtypeStruct((total, columns), f32),
@@ -456,7 +476,8 @@
             out_specs=spec(),
             scratch_shapes=[
                 VMEM((stream, columns), bf16),
-                pltpu.SemaphoreType.DMA((stream // 1024 + 1,)),
+                pltpu.SemaphoreType.DMA((stream // 512,)),
+                VMEM(side, f32),
             ],
             compiler_params=params,
             cost_estimate=pl.CostEstimate(
@@ -520,7 +541,7 @@
         out_shape=[jax.ShapeDtypeStruct((rows, width), bf16)] + [VMEM((ahead, columns), bf16)] * 2,
         in_specs=[spec(SMEM)] + [spec()] * 3 + [spec(pltpu.HBM)],
         out_specs=[spec()] * 3,
-        scratch_shapes=[pltpu.SemaphoreType.DMA((2,))],
+        scratch_shapes=[pltpu.SemaphoreType.DMA((2, 4))],
         compiler_params=params,
         cost_estimate=pl.CostEstimate(
             flops=4 * rows * width * context,

time: 86.3 us -> 87 us (level)
  starting transfers between devices: 30.3 us -> 31.2 us
    ppermute x29, starting transfers between devices: 30.3 us -> 31.2 us  [swap(): return lax.ppermute(x, AXIS, [(i, i ^ offset) for i in range(count)])]
where the time goes in v10:
time: 87 us; the launch traced here: 86.7 us
  starting transfers between devices  31.2 us (36%)
  blocking collectives  21.8 us (25%)
  Pallas kernels  19.8 us (23%)
  waiting for transfers between devices  13 us (15%)
    ppermute x29, starting transfers between devices, swap(): return lax.ppermute(x, AXIS, [(i, i ^ offset) for i in range(count)])  31.2 us
    all_to_all x2, blocking collectives, exchange(): lax.all_to_all(x, AXIS, split_axis=0, concat_axis=0, axis_index_groups=gr...  21.8 us
    ppermute x29, waiting for transfers between devices, swap(): return lax.ppermute(x, AXIS, [(i, i ^ offset) for i in range(count)])  13 us
    pallas_call x4, Pallas kernels, base(): pl.pallas_call(functools.partial(base_kernel, len(pieces), start, length...  9.06 us
    pallas_call x1, Pallas kernels, local(): pl.pallas_call(attend_kernel, out_shape=[jax.ShapeDtypeStruct((rows, widt...  4.71 us
    pallas_call x2, Pallas kernels, downs(): pl.pallas_call(functools.partial(down_kernel, count, rows, len(pieces), (...  2.57 us
    pallas_call x1, Pallas kernels, local(): pl.pallas_call(norm_kernel, out_shape=[VMEM((rows, width + LANES), bf16),...  1.88 us
  transfers between devices with their start and end apart: 29, of which 9 were waited for; matrix products, arithmetic and copies ran while one was open for 0% of the time, Pallas kernels for 16%

profile of v10, /device:TPU:0, one launch (start us, length us, event | category | flops | bytes accessed | tf_op | source)
XLA Modules:
  0.0 86.7 jit_solution(15943391839706900466)
XLA Ops:
  0.0 0.5 collective-permute-start.8
  0.5 1.9 %norm.1 = (bf16[4,8320]{1,0:T(4,128)(2,1)S(1)}, bf16[2,48,8192]{2,1,0:T(8,128)(2,1)S(1)}, bf16[1024,640]{1,0:T(8,128)(2,1)S(1)}) custom-call(bf16[4,8192]{1,0:T(4,128)(2,1)} %hidden_hbm.1, bf16[8192]{0:T(1024)(128)(2,1)} %gain_hbm.1, s32[4]{0:T(128)} %bitcast.14, s32[32]{0:T(128)} %slots_hbm.1, bf16[2,64,8192]{2,1,0:T(8,128)(2,1)} %bitcast.9, ...), custom_call_target="tpu_custom_call" | custom-call | tf_op jit(solution)/shard_map/norm/pallas_call | solution.py:402
  2.3 2.6 %collective-permute-start.4 = (bf16[4,8320]{1,0:T(4,128)(2,1)S(1)}, bf16[4,8320]{1,0:T(4,128)(2,1)S(1)}, u32[]{:S(2)}, u32[]{:S(2)}) collective-permute-start(bf16[4,8320]{1,0:T(4,128)(2,1)S(1)} %get-tuple-element.30.refs_7_), channel_id=1, source_target_pairs={{0,4},{1,5},{2,6},{3,7},{4,0},{5,1},{6,2},{7,3},{8,12},{9,13},{10,... | collective-permute-start | bytes 199688 | tf_op jit(solution)/shard_map/ppermute | solution.py:18
  5.0 2.6 %collective-permute-start.2 = (bf16[4,8320]{1,0:T(4,128)(2,1)S(1)}, bf16[4,8320]{1,0:T(4,128)(2,1)S(1)}, u32[]{:S(2)}, u32[]{:S(2)}) collective-permute-start(bf16[4,8320]{1,0:T(4,128)(2,1)S(1)} %get-tuple-element.30.refs_7_), channel_id=1, source_target_pairs={{0,8},{1,9},{2,10},{3,11},{4,12},{5,13},{6,14},{7,15},{8,0},{9,1},... | collective-permute-start | bytes 199688 | tf_op jit(solution)/shard_map/ppermute | solution.py:18
  7.6 0.0 collective-permute-start
  7.6 1.7 %collective-permute-start.6 = (bf16[4,8320]{1,0:T(4,128)(2,1)S(1)}, bf16[4,8320]{1,0:T(4,128)(2,1)S(1)}, u32[]{:S(2)}, u32[]{:S(2)}) collective-permute-start(bf16[4,8320]{1,0:T(4,128)(2,1)S(1)} %get-tuple-element.30.refs_7_), channel_id=1, source_target_pairs={{0,2},{1,3},{2,0},{3,1},{4,6},{5,7},{6,4},{7,5},{8,10},{9,11},{10,... | collective-permute-start | bytes 199688 | tf_op jit(solution)/shard_map/ppermute | solution.py:18
  9.3 0.0 collective-permute-done.4.refs_6_
  9.3 0.3 collective-permute-start.5
  9.6 3.1 %collective-permute-done.2.refs_5_ = bf16[4,8320]{1,0:T(4,128)(2,1)S(1)} collective-permute-done((bf16[4,8320]{1,0:T(4,128)(2,1)S(1)}, bf16[4,8320]{1,0:T(4,128)(2,1)S(1)}, u32[]{:S(2)}, u32[]{:S(2)}) %collective-permute-start.2) | collective-permute-done | bytes 66592 | tf_op jit(solution)/shard_map/ppermute | solution.py:18
  12.7 1.5 %collective-permute-start.3 = (bf16[4,8320]{1,0:T(4,128)(2,1)S(1)}, bf16[4,8320]{1,0:T(4,128)(2,1)S(1)}, u32[]{:S(2)}, u32[]{:S(2)}) collective-permute-start(bf16[4,8320]{1,0:T(4,128)(2,1)S(1)} %collective-permute-done.2.refs_5_), channel_id=1, source_target_pairs={{0,2},{1,3},{2,0},{3,1},{4,6},{5,7},{6,4},{7,5},{8,10},{9,11},{10,... | collective-permute-start | bytes 199688 | tf_op jit(solution)/shard_map/ppermute | solution.py:18
  14.2 0.0 collective-permute-done.refs_4_
  14.2 1.0 %collective-permute-start.1 = (bf16[4,8320]{1,0:T(4,128)(2,1)S(1)}, bf16[4,8320]{1,0:T(4,128)(2,1)S(1)}, u32[]{:S(2)}, u32[]{:S(2)}) collective-permute-start(bf16[4,8320]{1,0:T(4,128)(2,1)S(1)} %collective-permute-done.refs_4_), channel_id=1, source_target_pairs={{0,2},{1,3},{2,0},{3,1},{4,6},{5,7},{6,4},{7,5},{8,10},{9,11},{10,... | collective-permute-start | bytes 199688 | tf_op jit(solution)/shard_map/ppermute | solution.py:18
  15.2 0.0 collective-permute-done.6.refs_3_
  15.2 0.0 collective-permute-done.5.refs_2_
  15.2 1.7 %collective-permute-done.3.refs_1_ = bf16[4,8320]{1,0:T(4,128)(2,1)S(1)} collective-permute-done((bf16[4,8320]{1,0:T(4,128)(2,1)S(1)}, bf16[4,8320]{1,0:T(4,128)(2,1)S(1)}, u32[]{:S(2)}, u32[]{:S(2)}) %collective-permute-start.3) | collective-permute-done | bytes 66592 | tf_op jit(solution)/shard_map/ppermute | solution.py:18
  16.9 1.5 %collective-permute-done.1.refs_0_ = bf16[4,8320]{1,0:T(4,128)(2,1)S(1)} collective-permute-done((bf16[4,8320]{1,0:T(4,128)(2,1)S(1)}, bf16[4,8320]{1,0:T(4,128)(2,1)S(1)}, u32[]{:S(2)}, u32[]{:S(2)}) %collective-permute-start.1) | collective-permute-done | bytes 66592 | tf_op jit(solution)/shard_map/ppermute | solution.py:18
  18.4 0.1 pack.2.refs_2_.refs_3_.refs_0_
  18.6 0.1 collective-permute-start.7
  18.6 0.0 collective-permute-done.8
  18.7 2.0 %down.2 = (bf16[24,128]{1,0:T(8,128)(2,1)S(1)}, bf16[2,16,8192]{2,1,0:T(8,128)(2,1)S(1)}, bf16[1024,640]{1,0:T(8,128)(2,1)S(1)}) custom-call(bf16[2,48,8192]{2,1,0:T(8,128)(2,1)S(1)} %get-tuple-element.31.refs_0_, bf16[2,64,8192]{2,1,0:T(8,128)(2,1)S(1)} %bitcast.11, bf16[32,8320]{1,0:T(8,128)(2,1)S(1)} %pack.2.refs_2_.refs_3_.refs_0_, ...), custom_call_target="tpu_custom_call" | custom-call | flops 100663296 | bytes 4194304 | tf_op jit(solution)/shard_map/down/pallas_call | solution.py:448
  20.7 3.6 %collective-permute-start.11 = (bf16[24,128]{1,0:T(8,128)(2,1)S(1)}, bf16[24,128]{1,0:T(8,128)(2,1)S(1)}, u32[]{:S(2)}, u32[]{:S(2)}) collective-permute-start(bf16[24,128]{1,0:T(8,128)(2,1)S(1)} %get-tuple-element.33.refs_4_), channel_id=1, source_target_pairs={{0,12},{1,13},{2,14},{3,15},{4,8},{5,9},{6,10},{7,11},{8,4},{9,5},... | collective-permute-start | bytes 18440 | tf_op jit(solution)/shard_map/ppermute | solution.py:18
  24.3 0.9 %collective-permute-start.9 = (bf16[24,128]{1,0:T(8,128)(2,1)S(1)}, bf16[24,128]{1,0:T(8,128)(2,1)S(1)}, u32[]{:S(2)}, u32[]{:S(2)}) collective-permute-start(bf16[24,128]{1,0:T(8,128)(2,1)S(1)} %get-tuple-element.33.refs_4_), channel_id=1, source_target_pairs={{0,4},{1,5},{2,6},{3,7},{4,0},{5,1},{6,2},{7,3},{8,12},{9,13},{10,... | collective-permute-start | bytes 18440 | tf_op jit(solution)/shard_map/ppermute | solution.py:18
  25.2 2.6 %base.4.refs_4_ = f32[64,640]{1,0:T(8,128)S(1)} custom-call(bf16[32,8320]{1,0:T(8,128)(2,1)S(1)} %pack.2.refs_2_.refs_3_.refs_0_, bf16[32,8320]{1,0:T(8,128)(2,1)S(1)} %collective-permute-done.7.refs_1_, bf16[1024,640]{1,0:T(8,128)(2,1)S(1)} %get-tuple-element.34.refs_2_, bf16[8192,640]{1,0:T(8,128)(2,1)} %refs_3_.7, ...), custom_call_target="tpu_custom_call" | custom-call | flops 335544320 | bytes 10485760 | tf_op jit(solution)/shard_map/base/pallas_call | solution.py:472
  27.7 0.0 collective-permute-done.11
  27.8 1.0 %collective-permute-done.10 = bf16[24,128]{1,0:T(8,128)(2,1)S(1)} collective-permute-done((bf16[24,128]{1,0:T(8,128)(2,1)S(1)}, bf16[24,128]{1,0:T(8,128)(2,1)S(1)}, u32[]{:S(2)}, u32[]{:S(2)}) %collective-permute-start.10) | collective-permute-done | bytes 6176 | tf_op jit(solution)/shard_map/ppermute | solution.py:18
  28.8 0.0 collective-permute-done.9
  28.8 0.1 collective-permute-start.14
  28.9 0.8 collective-permute-start.13
  29.7 1.1 %collective-permute-start.12 = (bf16[24,128]{1,0:T(8,128)(2,1)S(1)}, bf16[24,128]{1,0:T(8,128)(2,1)S(1)}, u32[]{:S(2)}, u32[]{:S(2)}) collective-permute-start(bf16[24,128]{1,0:T(8,128)(2,1)S(1)} %add_add_fusion.1.refs_4_), channel_id=1, source_target_pairs={{0,1},{1,0},{2,3},{3,2},{4,5},{5,4},{6,7},{7,6},{8,9},{9,8},{10,11... | collective-permute-start | bytes 18440 | tf_op jit(solution)/shard_map/ppermute | solution.py:18
  30.7 2.7 %base.5.refs_5_ = f32[64,640]{1,0:T(8,128)S(1)} custom-call(bf16[32,8320]{1,0:T(8,128)(2,1)S(1)} %pack.2.refs_2_.refs_3_.refs_0_, bf16[32,8320]{1,0:T(8,128)(2,1)S(1)} %collective-permute-done.7.refs_1_, bf16[1024,640]{1,0:T(8,128)(2,1)S(1)} %get-tuple-element.38.refs_2_, bf16[8192,640]{1,0:T(8,128)(2,1)} %refs_3_.7, bf16[24,128]{1,0:T(8,128)(2,1)S(1)} %add_add_fusion.1.refs_4_), custom_call_target="tpu_custom_call" | custom-call | flops 335544320 | bytes 10485760 | tf_op jit(solution)/shard_map/base/pallas_call | solution.py:472
  33.5 0.0 copy-start.5
  33.5 0.0 collective-permute-done.13
  33.5 0.0 collective-permute-done.12
  33.5 0.7 lift.2
  34.2 11.3 %all_to_all.10 = bf16[16,4,640]{2,1,0:T(4,128)(2,1)S(1)} all-to-all(bf16[16,4,640]{2,1,0:T(4,128)(2,1)S(1)} %lift.2), channel_id=1, replica_groups=mesh['groups'=2,'tensor'=16] {'tensor'}, dimensions={0} | all-to-all | bytes 163840 | tf_op jit(solution)/shard_map/all_to_all | solution.py:22
  45.5 0.0 copy-start
  45.5 4.7 %attend.1 = (bf16[4,8192]{1,0:T(4,128)(2,1)S(1)}, bf16[2048,512]{1,0:T(8,128)(2,1)S(1)}, bf16[2048,512]{1,0:T(8,128)(2,1)S(1)}) custom-call(s32[4]{0:T(128)S(1)} %copy-done.5, bf16[4,10240]{1,0:T(4,128)(2,1)S(1)} %bitcast.12, bf16[4,8,384,128]{3,2,1,0:T(8,128)(2,1)S(1)} %copy-done.1, bf16[4,8,384,128]{3,2,1,0:T(8,128)(2,1)S(1)} %copy-done.2, ...), custom_call_target="tpu_custom_call" | custom-call | flops 50331648 | bytes 6291456 | tf_op jit(solution)/shard_map/attend/pallas_call | solution.py:539
  50.2 0.1 collective-permute-start.19
  50.3 1.2 %collective-permute-start.17 = (bf16[4,8192]{1,0:T(4,128)(2,1)S(1)}, bf16[4,8192]{1,0:T(4,128)(2,1)S(1)}, u32[]{:S(2)}, u32[]{:S(2)}) collective-permute-start(bf16[4,8192]{1,0:T(4,128)(2,1)S(1)} %get-tuple-element.44.refs_7_), channel_id=1, source_target_pairs={{0,8},{1,9},{2,10},{3,11},{4,12},{5,13},{6,14},{7,15},{8,0},{9,1},... | collective-permute-start | bytes 196616 | tf_op jit(solution)/shard_map/ppermute | solution.py:18
  51.5 3.2 %collective-permute-start.15 = (bf16[4,8192]{1,0:T(4,128)(2,1)S(1)}, bf16[4,8192]{1,0:T(4,128)(2,1)S(1)}, u32[]{:S(2)}, u32[]{:S(2)}) collective-permute-start(bf16[4,8192]{1,0:T(4,128)(2,1)S(1)} %get-tuple-element.44.refs_7_), channel_id=1, source_target_pairs={{0,12},{1,13},{2,14},{3,15},{4,8},{5,9},{6,10},{7,11},{8,4},{9,5},... | collective-permute-start | bytes 196616 | tf_op jit(solution)/shard_map/ppermute | solution.py:18
  54.7 0.0 collective-permute-start.21
  54.7 0.4 collective-permute-done.19.refs_6_
  55.1 1.6 %collective-permute-start.20 = (bf16[4,8192]{1,0:T(4,128)(2,1)S(1)}, bf16[4,8192]{1,0:T(4,128)(2,1)S(1)}, u32[]{:S(2)}, u32[]{:S(2)}) collective-permute-start(bf16[4,8192]{1,0:T(4,128)(2,1)S(1)} %collective-permute-done.19.refs_6_), channel_id=1, source_target_pairs={{0,2},{1,3},{2,0},{3,1},{4,6},{5,7},{6,4},{7,5},{8,10},{9,11},{10,... | collective-permute-start | bytes 196616 | tf_op jit(solution)/shard_map/ppermute | solution.py:18
  56.7 1.9 %collective-permute-done.17.refs_5_ = bf16[4,8192]{1,0:T(4,128)(2,1)S(1)} collective-permute-done((bf16[4,8192]{1,0:T(4,128)(2,1)S(1)}, bf16[4,8192]{1,0:T(4,128)(2,1)S(1)}, u32[]{:S(2)}, u32[]{:S(2)}) %collective-permute-start.17) | collective-permute-done | bytes 65568 | tf_op jit(solution)/shard_map/ppermute | solution.py:18
  58.6 0.7 collective-permute-start.18
  59.3 1.4 %collective-permute-start.16 = (bf16[4,8192]{1,0:T(4,128)(2,1)S(1)}, bf16[4,8192]{1,0:T(4,128)(2,1)S(1)}, u32[]{:S(2)}, u32[]{:S(2)}) collective-permute-start(bf16[4,8192]{1,0:T(4,128)(2,1)S(1)} %collective-permute-done.15.refs_4_), channel_id=1, source_target_pairs={{0,2},{1,3},{2,0},{3,1},{4,6},{5,7},{6,4},{7,5},{8,10},{9,11},{10,... | collective-permute-start | bytes 196616 | tf_op jit(solution)/shard_map/ppermute | solution.py:18
  60.6 0.0 collective-permute-done.21.refs_3_
  60.6 2.2 %collective-permute-done.18.refs_1_ = bf16[4,8192]{1,0:T(4,128)(2,1)S(1)} collective-permute-done((bf16[4,8192]{1,0:T(4,128)(2,1)S(1)}, bf16[4,8192]{1,0:T(4,128)(2,1)S(1)}, u32[]{:S(2)}, u32[]{:S(2)}) %collective-permute-start.18) | collective-permute-done | bytes 65568 | tf_op jit(solution)/shard_map/ppermute | solution.py:18
  62.9 0.7 collective-permute-done.16.refs_0_
  63.6 0.1 pack.3.refs_2_.refs_0_
  63.7 0.1 collective-permute-start.25
  63.8 0.5 down.3.refs_4_
  64.3 1.7 %collective-permute-start.24 = (bf16[8,128]{1,0:T(8,128)(2,1)S(1)}, bf16[8,128]{1,0:T(8,128)(2,1)S(1)}, u32[]{:S(2)}, u32[]{:S(2)}) collective-permute-start(bf16[8,128]{1,0:T(8,128)(2,1)S(1)} %down.3.refs_4_), channel_id=1, source_target_pairs={{0,12},{1,13},{2,14},{3,15},{4,8},{5,9},{6,10},{7,11},{8,4},{9,5},... | collective-permute-start | bytes 6152 | tf_op jit(solution)/shard_map/ppermute | solution.py:18
  66.0 0.4 collective-permute-start.23
  66.4 2.4 %collective-permute-start.22 = (bf16[8,128]{1,0:T(8,128)(2,1)S(1)}, bf16[8,128]{1,0:T(8,128)(2,1)S(1)}, u32[]{:S(2)}, u32[]{:S(2)}) collective-permute-start(bf16[8,128]{1,0:T(8,128)(2,1)S(1)} %down.3.refs_4_), channel_id=1, source_target_pairs={{0,4},{1,5},{2,6},{3,7},{4,0},{5,1},{6,2},{7,3},{8,12},{9,13},{10,... | collective-permute-start | bytes 6152 | tf_op jit(solution)/shard_map/ppermute | solution.py:18
  68.8 1.9 %base.6.refs_4_ = f32[64,512]{1,0:T(8,128)S(1)} custom-call(bf16[32,8192]{1,0:T(8,128)(2,1)S(1)} %pack.3.refs_2_.refs_0_, bf16[32,8192]{1,0:T(8,128)(2,1)S(1)} %collective-permute-done.25.refs_1_, bf16[2048,512]{1,0:T(8,128)(2,1)S(1)} %get-tuple-element.45.refs_2_, bf16[8192,512]{1,0:T(8,128)(2,1)} %refs_3_.10, bf16[8,128]{1,0:T(8,128)(2,1)S(1)} %down.3.refs_4_), custom_call_target="tpu_custom_call" | custom-call | flops 268435456 | bytes 8388608 | tf_op jit(solution)/shard_map/base/pallas_call | solution.py:472
  70.7 0.7 collective-permute-start.28
  71.4 0.8 collective-permute-start.27
  72.2 0.5 collective-permute-start.26
  72.6 1.9 %base.7.refs_5_ = f32[64,512]{1,0:T(8,128)S(1)} custom-call(bf16[32,8192]{1,0:T(8,128)(2,1)S(1)} %pack.3.refs_2_.refs_0_, bf16[32,8192]{1,0:T(8,128)(2,1)S(1)} %collective-permute-done.25.refs_1_, bf16[2048,512]{1,0:T(8,128)(2,1)S(1)} %get-tuple-element.49.refs_2_, bf16[8192,512]{1,0:T(8,128)(2,1)} %refs_3_.10, bf16[8,128]{1,0:T(8,128)(2,1)S(1)} %add_add_fusion.3.refs_4_), custom_call_target="tpu_custom_call" | custom-call | flops 268435456 | bytes 8388608 | tf_op jit(solution)/shard_map/base/pallas_call | solution.py:472
  74.6 0.4 collective-permute-done.27
  75.0 0.6 lift.3
  75.6 10.5 %all_to_all.11 = bf16[16,4,512]{2,1,0:T(4,128)(2,1)S(1)} all-to-all(bf16[16,4,512]{2,1,0:T(4,128)(2,1)S(1)} %lift.3), channel_id=1, replica_groups=mesh['groups'=2,'tensor'=16] {'tensor'}, dimensions={0} | all-to-all | bytes 131072 | tf_op jit(solution)/shard_map/all_to_all | solution.py:22
  86.1 0.6 copy.14
  (25 shorter events, 0.1 us)
Async XLA Ops:
  0.0 18.6 %collective-permute-start.8 = (bf16[2,8192,64]{1,2,0:T(8,128)(2,1)}, bf16[2,8192,64]{1,2,0:T(8,128)(2,1)S(1)}, u32[]{:S(2)}, u32[]{:S(2)}) collective-permute-start(bf16[2,8192,64]{1,2,0:T(8,128)(2,1)} %param.19), channel_id=1, source_target_pairs={{0,1},{1,0},{2,3},{3,2},{4,5},{5,4},{6,7},{7,6},{8,9},{9,8},{10,11... | collective-permute-start | bytes 6291464 | tf_op jit(solution)/shard_map/ppermute | solution.py:18
  2.3 6.9 %collective-permute-start.4 = (bf16[4,8320]{1,0:T(4,128)(2,1)S(1)}, bf16[4,8320]{1,0:T(4,128)(2,1)S(1)}, u32[]{:S(2)}, u32[]{:S(2)}) collective-permute-start(bf16[4,8320]{1,0:T(4,128)(2,1)S(1)} %get-tuple-element.30.refs_7_), channel_id=1, source_target_pairs={{0,4},{1,5},{2,6},{3,7},{4,0},{5,1},{6,2},{7,3},{8,12},{9,13},{10,... | collective-permute-start | bytes 199688 | tf_op jit(solution)/shard_map/ppermute | solution.py:18
  5.0 7.7 %collective-permute-start.2 = (bf16[4,8320]{1,0:T(4,128)(2,1)S(1)}, bf16[4,8320]{1,0:T(4,128)(2,1)S(1)}, u32[]{:S(2)}, u32[]{:S(2)}) collective-permute-start(bf16[4,8320]{1,0:T(4,128)(2,1)S(1)} %get-tuple-element.30.refs_7_), channel_id=1, source_target_pairs={{0,8},{1,9},{2,10},{3,11},{4,12},{5,13},{6,14},{7,15},{8,0},{9,1},... | collective-permute-start | bytes 199688 | tf_op jit(solution)/shard_map/ppermute | solution.py:18
  7.6 6.6 %collective-permute-start = (bf16[4,8320]{1,0:T(4,128)(2,1)S(1)}, bf16[4,8320]{1,0:T(4,128)(2,1)S(1)}, u32[]{:S(2)}, u32[]{:S(2)}) collective-permute-start(bf16[4,8320]{1,0:T(4,128)(2,1)S(1)} %get-tuple-element.30.refs_7_), channel_id=1, source_target_pairs={{0,12},{1,13},{2,14},{3,15},{4,8},{5,9},{6,10},{7,11},{8,4},{9,5},... | collective-permute-start | bytes 199688 | tf_op jit(solution)/shard_map/ppermute | solution.py:18
  7.6 7.6 %collective-permute-start.6 = (bf16[4,8320]{1,0:T(4,128)(2,1)S(1)}, bf16[4,8320]{1,0:T(4,128)(2,1)S(1)}, u32[]{:S(2)}, u32[]{:S(2)}) collective-permute-start(bf16[4,8320]{1,0:T(4,128)(2,1)S(1)} %get-tuple-element.30.refs_7_), channel_id=1, source_target_pairs={{0,2},{1,3},{2,0},{3,1},{4,6},{5,7},{6,4},{7,5},{8,10},{9,11},{10,... | collective-permute-start | bytes 199688 | tf_op jit(solution)/shard_map/ppermute | solution.py:18
  9.3 5.9 %collective-permute-start.5 = (bf16[4,8320]{1,0:T(4,128)(2,1)S(1)}, bf16[4,8320]{1,0:T(4,128)(2,1)S(1)}, u32[]{:S(2)}, u32[]{:S(2)}) collective-permute-start(bf16[4,8320]{1,0:T(4,128)(2,1)S(1)} %collective-permute-done.4.refs_6_), channel_id=1, source_target_pairs={{0,2},{1,3},{2,0},{3,1},{4,6},{5,7},{6,4},{7,5},{8,10},{9,11},{10,... | collective-permute-start | bytes 199688 | tf_op jit(solution)/shard_map/ppermute | solution.py:18
  12.7 4.3 %collective-permute-start.3 = (bf16[4,8320]{1,0:T(4,128)(2,1)S(1)}, bf16[4,8320]{1,0:T(4,128)(2,1)S(1)}, u32[]{:S(2)}, u32[]{:S(2)}) collective-permute-start(bf16[4,8320]{1,0:T(4,128)(2,1)S(1)} %collective-permute-done.2.refs_5_), channel_id=1, source_target_pairs={{0,2},{1,3},{2,0},{3,1},{4,6},{5,7},{6,4},{7,5},{8,10},{9,11},{10,... | collective-permute-start | bytes 199688 | tf_op jit(solution)/shard_map/ppermute | solution.py:18
  14.2 4.3 %collective-permute-start.1 = (bf16[4,8320]{1,0:T(4,128)(2,1)S(1)}, bf16[4,8320]{1,0:T(4,128)(2,1)S(1)}, u32[]{:S(2)}, u32[]{:S(2)}) collective-permute-start(bf16[4,8320]{1,0:T(4,128)(2,1)S(1)} %collective-permute-done.refs_4_), channel_id=1, source_target_pairs={{0,2},{1,3},{2,0},{3,1},{4,6},{5,7},{6,4},{7,5},{8,10},{9,11},{10,... | collective-permute-start | bytes 199688 | tf_op jit(solution)/shard_map/ppermute | solution.py:18
  18.6 6.6 %collective-permute-start.7 = (bf16[32,8320]{1,0:T(8,128)(2,1)S(1)}, bf16[32,8320]{1,0:T(8,128)(2,1)S(1)}, u32[]{:S(2)}, u32[]{:S(2)}) collective-permute-start(bf16[32,8320]{1,0:T(8,128)(2,1)S(1)} %pack.2.refs_2_.refs_3_.refs_0_), channel_id=1, source_target_pairs={{0,1},{1,0},{2,3},{3,2},{4,5},{5,4},{6,7},{7,6},{8,9},{9,8},{10,11... | collective-permute-start | bytes 1597448 | tf_op jit(solution)/shard_map/ppermute | solution.py:18
  20.7 7.0 %collective-permute-start.11 = (bf16[24,128]{1,0:T(8,128)(2,1)S(1)}, bf16[24,128]{1,0:T(8,128)(2,1)S(1)}, u32[]{:S(2)}, u32[]{:S(2)}) collective-permute-start(bf16[24,128]{1,0:T(8,128)(2,1)S(1)} %get-tuple-element.33.refs_4_), channel_id=1, source_target_pairs={{0,12},{1,13},{2,14},{3,15},{4,8},{5,9},{6,10},{7,11},{8,4},{9,5},... | collective-permute-start | bytes 18440 | tf_op jit(solution)/shard_map/ppermute | solution.py:18
  24.3 4.5 %collective-permute-start.10 = (bf16[24,128]{1,0:T(8,128)(2,1)S(1)}, bf16[24,128]{1,0:T(8,128)(2,1)S(1)}, u32[]{:S(2)}, u32[]{:S(2)}) collective-permute-start(bf16[24,128]{1,0:T(8,128)(2,1)S(1)} %get-tuple-element.33.refs_4_), channel_id=1, source_target_pairs={{0,8},{1,9},{2,10},{3,11},{4,12},{5,13},{6,14},{7,15},{8,0},{9,1},... | collective-permute-start | bytes 18440 | tf_op jit(solution)/shard_map/ppermute | solution.py:18
  24.3 4.5 %collective-permute-start.9 = (bf16[24,128]{1,0:T(8,128)(2,1)S(1)}, bf16[24,128]{1,0:T(8,128)(2,1)S(1)}, u32[]{:S(2)}, u32[]{:S(2)}) collective-permute-start(bf16[24,128]{1,0:T(8,128)(2,1)S(1)} %get-tuple-element.33.refs_4_), channel_id=1, source_target_pairs={{0,4},{1,5},{2,6},{3,7},{4,0},{5,1},{6,2},{7,3},{8,12},{9,13},{10,... | collective-permute-start | bytes 18440 | tf_op jit(solution)/shard_map/ppermute | solution.py:18
  28.8 4.7 %collective-permute-start.14 = (bf16[24,128]{1,0:T(8,128)(2,1)S(1)}, bf16[24,128]{1,0:T(8,128)(2,1)S(1)}, u32[]{:S(2)}, u32[]{:S(2)}) collective-permute-start(bf16[24,128]{1,0:T(8,128)(2,1)S(1)} %add_add_fusion.1.refs_4_), channel_id=1, source_target_pairs={{0,3},{1,2},{2,1},{3,0},{4,7},{5,6},{6,5},{7,4},{8,11},{9,10},{10,... | collective-permute-start | bytes 18440 | tf_op jit(solution)/shard_map/ppermute | solution.py:18
  28.9 4.6 %collective-permute-start.13 = (bf16[24,128]{1,0:T(8,128)(2,1)S(1)}, bf16[24,128]{1,0:T(8,128)(2,1)S(1)}, u32[]{:S(2)}, u32[]{:S(2)}) collective-permute-start(bf16[24,128]{1,0:T(8,128)(2,1)S(1)} %add_add_fusion.1.refs_4_), channel_id=1, source_target_pairs={{0,2},{1,3},{2,0},{3,1},{4,6},{5,7},{6,4},{7,5},{8,10},{9,11},{10,... | collective-permute-start | bytes 18440 | tf_op jit(solution)/shard_map/ppermute | solution.py:18
  29.7 3.8 %collective-permute-start.12 = (bf16[24,128]{1,0:T(8,128)(2,1)S(1)}, bf16[24,128]{1,0:T(8,128)(2,1)S(1)}, u32[]{:S(2)}, u32[]{:S(2)}) collective-permute-start(bf16[24,128]{1,0:T(8,128)(2,1)S(1)} %add_add_fusion.1.refs_4_), channel_id=1, source_target_pairs={{0,1},{1,0},{2,3},{3,2},{4,5},{5,4},{6,7},{7,6},{8,9},{9,8},{10,11... | collective-permute-start | bytes 18440 | tf_op jit(solution)/shard_map/ppermute | solution.py:18
  30.7 2.8 %copy-start.3 = (bf16[32,16,640]{2,1,0:T(8,128)(2,1)S(1)}, bf16[32,16,640]{2,1,0:T(8,128)(2,1)}, u32[]{:S(2)}) copy-start(bf16[32,16,640]{2,1,0:T(8,128)(2,1)} %refs_3_.8) | copy-start | bytes 1966084
  30.7 14.8 %copy-start.1 = (bf16[4,8,384,128]{3,2,1,0:T(8,128)(2,1)S(1)}, bf16[4,8,384,128]{3,2,1,0:T(8,128)(2,1)}, u32[]{:S(2)}) copy-start(bf16[4,8,384,128]{3,2,1,0:T(8,128)(2,1)} %keys_ref.1) | copy-start | bytes 9437188
  30.7 14.8 %copy-start.2 = (bf16[4,8,384,128]{3,2,1,0:T(8,128)(2,1)S(1)}, bf16[4,8,384,128]{3,2,1,0:T(8,128)(2,1)}, u32[]{:S(2)}) copy-start(bf16[4,8,384,128]{3,2,1,0:T(8,128)(2,1)} %values_ref.1) | copy-start | bytes 9437188
  33.5 12.0 %copy-start.5 = (s32[4]{0:T(128)S(1)}, s32[4]{0:T(128)}, u32[]{:S(2)}) copy-start(s32[4]{0:T(128)} %lengths_ref.1) | copy-start | bytes 52
  45.5 18.3 %copy-start = (bf16[2,8192,64]{1,2,0:T(8,128)(2,1)S(1)}, bf16[2,8192,64]{1,2,0:T(8,128)(2,1)}, u32[]{:S(2)}) copy-start(bf16[2,8192,64]{1,2,0:T(8,128)(2,1)} %param.19) | copy-start | bytes 6291460
  50.2 4.9 %collective-permute-start.19 = (bf16[4,8192]{1,0:T(4,128)(2,1)S(1)}, bf16[4,8192]{1,0:T(4,128)(2,1)S(1)}, u32[]{:S(2)}, u32[]{:S(2)}) collective-permute-start(bf16[4,8192]{1,0:T(4,128)(2,1)S(1)} %get-tuple-element.44.refs_7_), channel_id=1, source_target_pairs={{0,4},{1,5},{2,6},{3,7},{4,0},{5,1},{6,2},{7,3},{8,12},{9,13},{10,... | collective-permute-start | bytes 196616 | tf_op jit(solution)/shard_map/ppermute | solution.py:18
  50.3 8.3 %collective-permute-start.17 = (bf16[4,8192]{1,0:T(4,128)(2,1)S(1)}, bf16[4,8192]{1,0:T(4,128)(2,1)S(1)}, u32[]{:S(2)}, u32[]{:S(2)}) collective-permute-start(bf16[4,8192]{1,0:T(4,128)(2,1)S(1)} %get-tuple-element.44.refs_7_), channel_id=1, source_target_pairs={{0,8},{1,9},{2,10},{3,11},{4,12},{5,13},{6,14},{7,15},{8,0},{9,1},... | collective-permute-start | bytes 196616 | tf_op jit(solution)/shard_map/ppermute | solution.py:18
  51.5 7.8 %collective-permute-start.15 = (bf16[4,8192]{1,0:T(4,128)(2,1)S(1)}, bf16[4,8192]{1,0:T(4,128)(2,1)S(1)}, u32[]{:S(2)}, u32[]{:S(2)}) collective-permute-start(bf16[4,8192]{1,0:T(4,128)(2,1)S(1)} %get-tuple-element.44.refs_7_), channel_id=1, source_target_pairs={{0,12},{1,13},{2,14},{3,15},{4,8},{5,9},{6,10},{7,11},{8,4},{9,5},... | collective-permute-start | bytes 196616 | tf_op jit(solution)/shard_map/ppermute | solution.py:18
  54.7 5.9 %collective-permute-start.21 = (bf16[4,8192]{1,0:T(4,128)(2,1)S(1)}, bf16[4,8192]{1,0:T(4,128)(2,1)S(1)}, u32[]{:S(2)}, u32[]{:S(2)}) collective-permute-start(bf16[4,8192]{1,0:T(4,128)(2,1)S(1)} %get-tuple-element.44.refs_7_), channel_id=1, source_target_pairs={{0,2},{1,3},{2,0},{3,1},{4,6},{5,7},{6,4},{7,5},{8,10},{9,11},{10,... | collective-permute-start | bytes 196616 | tf_op jit(solution)/shard_map/ppermute | solution.py:18
  55.1 5.5 %collective-permute-start.20 = (bf16[4,8192]{1,0:T(4,128)(2,1)S(1)}, bf16[4,8192]{1,0:T(4,128)(2,1)S(1)}, u32[]{:S(2)}, u32[]{:S(2)}) collective-permute-start(bf16[4,8192]{1,0:T(4,128)(2,1)S(1)} %collective-permute-done.19.refs_6_), channel_id=1, source_target_pairs={{0,2},{1,3},{2,0},{3,1},{4,6},{5,7},{6,4},{7,5},{8,10},{9,11},{10,... | collective-permute-start | bytes 196616 | tf_op jit(solution)/shard_map/ppermute | solution.py:18
  58.6 4.3 %collective-permute-start.18 = (bf16[4,8192]{1,0:T(4,128)(2,1)S(1)}, bf16[4,8192]{1,0:T(4,128)(2,1)S(1)}, u32[]{:S(2)}, u32[]{:S(2)}) collective-permute-start(bf16[4,8192]{1,0:T(4,128)(2,1)S(1)} %collective-permute-done.17.refs_5_), channel_id=1, source_target_pairs={{0,2},{1,3},{2,0},{3,1},{4,6},{5,7},{6,4},{7,5},{8,10},{9,11},{10,... | collective-permute-start | bytes 196616 | tf_op jit(solution)/shard_map/ppermute | solution.py:18
  59.3 4.3 %collective-permute-start.16 = (bf16[4,8192]{1,0:T(4,128)(2,1)S(1)}, bf16[4,8192]{1,0:T(4,128)(2,1)S(1)}, u32[]{:S(2)}, u32[]{:S(2)}) collective-permute-start(bf16[4,8192]{1,0:T(4,128)(2,1)S(1)} %collective-permute-done.15.refs_4_), channel_id=1, source_target_pairs={{0,2},{1,3},{2,0},{3,1},{4,6},{5,7},{6,4},{7,5},{8,10},{9,11},{10,... | collective-permute-start | bytes 196616 | tf_op jit(solution)/shard_map/ppermute | solution.py:18
  63.7 5.1 %collective-permute-start.25 = (bf16[32,8192]{1,0:T(8,128)(2,1)S(1)}, bf16[32,8192]{1,0:T(8,128)(2,1)S(1)}, u32[]{:S(2)}, u32[]{:S(2)}) collective-permute-start(bf16[32,8192]{1,0:T(8,128)(2,1)S(1)} %pack.3.refs_2_.refs_0_), channel_id=1, source_target_pairs={{0,1},{1,0},{2,3},{3,2},{4,5},{5,4},{6,7},{7,6},{8,9},{9,8},{10,11... | collective-permute-start | bytes 1572872 | tf_op jit(solution)/shard_map/ppermute | solution.py:18
  64.3 6.3 %collective-permute-start.24 = (bf16[8,128]{1,0:T(8,128)(2,1)S(1)}, bf16[8,128]{1,0:T(8,128)(2,1)S(1)}, u32[]{:S(2)}, u32[]{:S(2)}) collective-permute-start(bf16[8,128]{1,0:T(8,128)(2,1)S(1)} %down.3.refs_4_), channel_id=1, source_target_pairs={{0,12},{1,13},{2,14},{3,15},{4,8},{5,9},{6,10},{7,11},{8,4},{9,5},... | collective-permute-start | bytes 6152 | tf_op jit(solution)/shard_map/ppermute | solution.py:18
  66.0 4.7 %collective-permute-start.23 = (bf16[8,128]{1,0:T(8,128)(2,1)S(1)}, bf16[8,128]{1,0:T(8,128)(2,1)S(1)}, u32[]{:S(2)}, u32[]{:S(2)}) collective-permute-start(bf16[8,128]{1,0:T(8,128)(2,1)S(1)} %down.3.refs_4_), channel_id=1, source_target_pairs={{0,8},{1,9},{2,10},{3,11},{4,12},{5,13},{6,14},{7,15},{8,0},{9,1},... | collective-permute-start | bytes 6152 | tf_op jit(solution)/shard_map/ppermute | solution.py:18
  66.4 4.3 %collective-permute-start.22 = (bf16[8,128]{1,0:T(8,128)(2,1)S(1)}, bf16[8,128]{1,0:T(8,128)(2,1)S(1)}, u32[]{:S(2)}, u32[]{:S(2)}) collective-permute-start(bf16[8,128]{1,0:T(8,128)(2,1)S(1)} %down.3.refs_4_), channel_id=1, source_target_pairs={{0,4},{1,5},{2,6},{3,7},{4,0},{5,1},{6,2},{7,3},{8,12},{9,13},{10,... | collective-permute-start | bytes 6152 | tf_op jit(solution)/shard_map/ppermute | solution.py:18
  70.7 3.9 %collective-permute-start.28 = (bf16[8,128]{1,0:T(8,128)(2,1)S(1)}, bf16[8,128]{1,0:T(8,128)(2,1)S(1)}, u32[]{:S(2)}, u32[]{:S(2)}) collective-permute-start(bf16[8,128]{1,0:T(8,128)(2,1)S(1)} %add_add_fusion.3.refs_4_), channel_id=1, source_target_pairs={{0,3},{1,2},{2,1},{3,0},{4,7},{5,6},{6,5},{7,4},{8,11},{9,10},{10,... | collective-permute-start | bytes 6152 | tf_op jit(solution)/shard_map/ppermute | solution.py:18
  71.4 3.6 %collective-permute-start.27 = (bf16[8,128]{1,0:T(8,128)(2,1)S(1)}, bf16[8,128]{1,0:T(8,128)(2,1)S(1)}, u32[]{:S(2)}, u32[]{:S(2)}) collective-permute-start(bf16[8,128]{1,0:T(8,128)(2,1)S(1)} %add_add_fusion.3.refs_4_), channel_id=1, source_target_pairs={{0,2},{1,3},{2,0},{3,1},{4,6},{5,7},{6,4},{7,5},{8,10},{9,11},{10,... | collective-permute-start | bytes 6152 | tf_op jit(solution)/shard_map/ppermute | solution.py:18
  72.2 2.8 %collective-permute-start.26 = (bf16[8,128]{1,0:T(8,128)(2,1)S(1)}, bf16[8,128]{1,0:T(8,128)(2,1)S(1)}, u32[]{:S(2)}, u32[]{:S(2)}) collective-permute-start(bf16[8,128]{1,0:T(8,128)(2,1)S(1)} %add_add_fusion.3.refs_4_), channel_id=1, source_target_pairs={{0,1},{1,0},{2,3},{3,2},{4,5},{5,4},{6,7},{7,6},{8,9},{9,8},{10,11... | collective-permute-start | bytes 6152 | tf_op jit(solution)/shard_map/ppermute | solution.py:18
  72.6 2.3 %copy-start.4 = (bf16[32,16,512]{2,1,0:T(8,128)(2,1)S(1)}, bf16[32,16,512]{2,1,0:T(8,128)(2,1)}, u32[]{:S(2)}) copy-start(bf16[32,16,512]{2,1,0:T(8,128)(2,1)} %refs_3_.11) | copy-start | bytes 1572868

commit v11 on v10

--- a/solution.py
+++ b/solution.py
@@ -213,8 +213,8 @@
 
 
 def base_kernel(pieces, start, ready, *refs):
-    ready_ref = refs[pieces]
-    weight_hbm, _, out_ref, weight_ref, sems, side_ref = refs[pieces + 1 :]
+    ready_ref = refs[pieces] if ready else None
+    weight_hbm, _, out_ref, weight_ref, sems, side_ref = refs[-6:]
     total, columns = out_ref.shape
     whole = columns // 256 * 256
     narrow = columns - whole == 128
@@ -247,7 +247,8 @@
             term = dot(rows_of(start + offset, length), weight)
         side_ref[...] = term if offset == 0 else side_ref[...] + term
 
-    wide(ready_ref, 0, ready, 0)
+    if ready:
+        wide(ready_ref, 0, ready, 0)
     early = stream - 1024
     for i, copy in enumerate(copies):
         copy.wait()
@@ -255,8 +256,10 @@
         if at % 1024 == 0 and at <= early:
             wide(weight_ref, at - 1024, 1024, ready + at - 1024)
         if at == early and columns > whole:
-            parts = [ready_ref[:, whole:], weight_ref[:early, whole:]]
-            rest(jnp.concatenate(parts, axis=0), 0)
+            weight = weight_ref[:early, whole:]
+            if ready:
+                weight = jnp.concatenate([ready_ref[:, whole:], weight], axis=0)
+            rest(weight, 0)
     wide(weight_ref, early, 1024, ready + early)
     if columns > whole:
         rest(weight_ref[early:, whole:], ready + early)
@@ -310,25 +313,20 @@
         out_ref[d] = placed[d * rows : (d + 1) * rows]
 
 
-def attend_kernel(
-    lengths_ref, qkv_ref, keys_ref, values_ref, weight_hbm, out_ref, low_ref, high_ref, sems
-):
-    copies = rows_copies(weight_hbm, 0, low_ref, sems.at[0])
-    copies += rows_copies(weight_hbm, weight_hbm.shape[0] // 2, high_ref, sems.at[1])
-    for copy in copies:
-        copy.start()
+def attend_kernel(lengths_ref, qkv_ref, keys_ref, values_ref, out_ref):
     rows, kv_heads, context, dim = keys_ref.shape
     width = out_ref.shape[1]
     groups = width // dim // kv_heads
     per_head = groups * rows
-    together = max(1, LANES // per_head)
+    together = max(2, LANES // per_head)
     lanes = together * per_head
     lane = iota((1, lanes), 1)
     length = jnp.zeros((1, lanes), jnp.int32)
     for b in range(rows):
         length = jnp.where(lane % rows == b, lengths_ref[b], length)
     live = iota((context, lanes), 0) < length
-    request = iota((per_head, 1), 0) % rows
+    odd = iota((lanes, 1), 0) // per_head % 2 == 1
+    pair_row = iota((2 * per_head, 1), 0)
     scale = dim ** (-0.5)
 
     def columns(at):
@@ -342,13 +340,16 @@
         key = jnp.concatenate([columns(width + h * dim) for h in heads for _ in range(groups)], axis=0)
         at = width + kv_heads * dim
         value = jnp.concatenate([columns(at + h * dim) for h in heads for _ in range(groups)], axis=0)
-        half = query.astype(jnp.bfloat16)
+        half = jnp.concatenate([jnp.where(odd, 0.0, query), jnp.where(odd, query, 0.0)], axis=1)
+        half = half.astype(jnp.bfloat16)
         scores = jnp.zeros((context, lanes), jnp.float32)
-        for n, h in enumerate(heads):
-            cached = keys_ref[:, h].reshape(rows * context, dim)
-            every = lax.dot_general(cached, half, NT, preferred_element_type=jnp.float32)
+        for n in range(0, together, 2):
+            cached = [keys_ref[:, first + n + m].reshape(rows * context, dim) for m in range(2)]
+            every = lax.dot_general(
+                jnp.concatenate(cached, axis=1), half, NT, preferred_element_type=jnp.float32
+            )
             for b in range(rows):
-                mine = (lane // per_head == n) & (lane % rows == b)
+                mine = (lane // (2 * per_head) == n // 2) & (lane % rows == b)
                 scores = jnp.where(mine, every[b * context : (b + 1) * context], scores)
         scores = jnp.where(live, scores * scale, -1e30)
         own = jnp.sum((query * key).T, axis=0, keepdims=True) * scale
@@ -359,18 +360,18 @@
         probs = (weights / denominator).T.astype(jnp.bfloat16)
         own_prob = (own_weight / denominator).astype(jnp.bfloat16).astype(jnp.float32)
         own_term = jnp.broadcast_to(own_prob, (dim, lanes)).T * value
-        for n, h in enumerate(heads):
-            span = slice(n * per_head, (n + 1) * per_head)
-            mixed = jnp.zeros((per_head, dim), jnp.float32)
+        for n in range(0, together, 2):
+            span = slice(n * per_head, (n + 2) * per_head)
+            mixed = jnp.zeros((2 * per_head, dim), jnp.float32)
             for b in range(rows):
-                one = jnp.dot(probs[span], values_ref[b, h], preferred_element_type=jnp.float32)
-                mixed = jnp.where(request == b, one, mixed)
+                both = jnp.concatenate([values_ref[b, first + n + m] for m in range(2)], axis=1)
+                one = jnp.dot(probs[span], both, preferred_element_type=jnp.float32)
+                one = jnp.where(pair_row < per_head, one[:, :dim], one[:, dim:])
+                mixed = jnp.where(pair_row % rows == b, one, mixed)
             mixed = (mixed + own_term[span]).astype(jnp.bfloat16)
-            for g in range(groups):
-                at = (h * groups + g) * dim
+            for g in range(2 * groups):
+                at = ((first + n) * groups + g) * dim
                 out_ref[:, at : at + dim] = mixed[g * rows : (g + 1) * rows]
-    for copy in copies:
-        copy.wait()
 
 
 def local(
@@ -414,7 +415,7 @@
             SMEM((rows,), jnp.int32),
             SMEM(adapter_storage.shape, jnp.int32),
             pltpu.SemaphoreType.DMA((5,)),
-            pltpu.SemaphoreType.DMA((4,)),
+            pltpu.SemaphoreType.DMA((1,)),
         ],
         compiler_params=params,
         name="norm",
@@ -454,7 +455,7 @@
             + tag_specs(tagged)
             + [spec(pltpu.HBM)] * len(extra),
             out_specs=out_specs,
-            scratch_shapes=[pltpu.SemaphoreType.DMA((4,))] * len(extra),
+            scratch_shapes=[pltpu.SemaphoreType.DMA((1,))] * len(extra),
             compiler_params=params,
             cost_estimate=pl.CostEstimate(
                 flops=2 * total * width * held * ranks,
@@ -466,17 +467,18 @@
 
     def base(pieces, weight, after, start, ready, length):
         columns = weight.shape[1]
-        stream = length - ready.shape[0]
+        first = [] if ready is None else [ready]
+        stream = length - sum(r.shape[0] for r in first)
         rest = columns % 256
         side = (2 * total, 256) if rest == 128 else (total, max(rest, 1))
         return pl.pallas_call(
             functools.partial(base_kernel, len(pieces), start, length - stream),
             out_shape=jax.ShapeDtypeStruct((total, columns), f32),
-            in_specs=[spec()] * (len(pieces) + 1) + [spec(pltpu.HBM), spec(pl.ANY)],
+            in_specs=[spec()] * (len(pieces) + len(first)) + [spec(pltpu.HBM), spec(pl.ANY)],
             out_specs=spec(),
             scratch_shapes=[
                 VMEM((stream, columns), bf16),
-                pltpu.SemaphoreType.DMA((stream // 512,)),
+                pltpu.SemaphoreType.DMA((stream // 1024,)),
                 VMEM(side, f32),
             ],
             compiler_params=params,
@@ -486,7 +488,7 @@
                 transcendentals=0,
             ),
             name="base",
-        )(*pieces, ready, hbm(weight), after)
+        )(*pieces, *first, hbm(weight), after)
 
     def lift(down, tagged, up, base_terms, bounds, ranks):
         columns = up.shape[2]
@@ -534,14 +536,11 @@
         projection_up_adapter,
         bounds,
     )
-    columns = output_weight.shape[1]
-    ahead = min(2048, width // 2 - 1024)
-    attended, *ready = pl.pallas_call(
+    attended = pl.pallas_call(
         attend_kernel,
-        out_shape=[jax.ShapeDtypeStruct((rows, width), bf16)] + [VMEM((ahead, columns), bf16)] * 2,
-        in_specs=[spec(SMEM)] + [spec()] * 3 + [spec(pltpu.HBM)],
-        out_specs=[spec()] * 3,
-        scratch_shapes=[pltpu.SemaphoreType.DMA((2, 4))],
+        out_shape=jax.ShapeDtypeStruct((rows, width), bf16),
+        in_specs=[spec(SMEM)] + [spec()] * 3,
+        out_specs=spec(),
         compiler_params=params,
         cost_estimate=pl.CostEstimate(
             flops=4 * rows * width * context,
@@ -549,7 +548,7 @@
             transcendentals=rows * width // head_dim * context,
         ),
         name="attend",
-    )(lengths, qkv_mine, cache_keys, cache_values, hbm(output_weight))
+    )(lengths, qkv_mine, cache_keys, cache_values)
     column, pieces = gather_rows(attended, count)
     output, _ = project(
         column,
@@ -557,7 +556,7 @@
         tagged,
         own_maps,
         rest[0],
-        ready,
+        [None, None],
         3 * rank,
         4 * rank,
         output_weight,

time: 87 us -> 84.8 us (0.975)
  Pallas kernels: 19.8 us -> 18.3 us
    pallas_call x1, Pallas kernels: 4.71 us -> 2.64 us  [local(): pl.pallas_call(attend_kernel, out_shape=jax.ShapeDtypeStruct((rows, width...]
    pallas_call x4, Pallas kernels: 9.06 us -> 10.3 us  [base(): pl.pallas_call(functools.partial(base_kernel, len(pieces), start, length...]
  transfers between devices with their start and end apart: 29 -> 29, of which waited for: 9 -> 8; matrix products, arithmetic and copies ran while one was open for 0% -> 0% of each run, Pallas kernels for 16% -> 17%
where the time goes in v11:
time: 84.8 us; the launch traced here: 84.6 us
  starting transfers between devices  31.2 us (37%)
  blocking collectives  21.5 us (25%)
  Pallas kernels  18.3 us (22%)
  waiting for transfers between devices  12.6 us (15%)
    ppermute x29, starting transfers between devices, swap(): return lax.ppermute(x, AXIS, [(i, i ^ offset) for i in range(count)])  31.2 us
    all_to_all x2, blocking collectives, exchange(): lax.all_to_all(x, AXIS, split_axis=0, concat_axis=0, axis_index_groups=gr...  21.5 us
    ppermute x29, waiting for transfers between devices, swap(): return lax.ppermute(x, AXIS, [(i, i ^ offset) for i in range(count)])  12.6 us
    pallas_call x4, Pallas kernels, base(): pl.pallas_call(functools.partial(base_kernel, len(pieces), start, length...  10.3 us
    pallas_call x1, Pallas kernels, local(): pl.pallas_call(attend_kernel, out_shape=jax.ShapeDtypeStruct((rows, width...  2.64 us
    pallas_call x1, Pallas kernels, local(): pl.pallas_call(norm_kernel, out_shape=[VMEM((rows, width + LANES), bf16),...  1.9 us
    pallas_call x2, Pallas kernels, downs(): pl.pallas_call(functools.partial(down_kernel, count, rows, len(pieces), (...  1.86 us
  transfers between devices with their start and end apart: 29, of which 8 were waited for; matrix products, arithmetic and copies ran while one was open for 0% of the time, Pallas kernels for 17%

profile of v11, /device:TPU:0, one launch (start us, length us, event | category | flops | bytes accessed | tf_op | source)
XLA Modules:
  0.0 84.6 jit_solution(644480748057658898)
XLA Ops:
  0.0 0.5 collective-permute-start.8
  0.5 1.9 %norm.1 = (bf16[4,8320]{1,0:T(4,128)(2,1)S(1)}, bf16[2,48,8192]{2,1,0:T(8,128)(2,1)S(1)}, bf16[1024,640]{1,0:T(8,128)(2,1)S(1)}) custom-call(bf16[4,8192]{1,0:T(4,128)(2,1)} %hidden_hbm.1, bf16[8192]{0:T(1024)(128)(2,1)} %gain_hbm.1, s32[4]{0:T(128)} %bitcast.14, s32[32]{0:T(128)} %slots_hbm.1, bf16[2,64,8192]{2,1,0:T(8,128)(2,1)} %bitcast.9, ...), custom_call_target="tpu_custom_call" | custom-call | tf_op jit(solution)/shard_map/norm/pallas_call | solution.py:403
  2.4 2.6 %collective-permute-start.4 = (bf16[4,8320]{1,0:T(4,128)(2,1)S(1)}, bf16[4,8320]{1,0:T(4,128)(2,1)S(1)}, u32[]{:S(2)}, u32[]{:S(2)}) collective-permute-start(bf16[4,8320]{1,0:T(4,128)(2,1)S(1)} %get-tuple-element.27.refs_7_), channel_id=1, source_target_pairs={{0,4},{1,5},{2,6},{3,7},{4,0},{5,1},{6,2},{7,3},{8,12},{9,13},{10,... | collective-permute-start | bytes 199688 | tf_op jit(solution)/shard_map/ppermute | solution.py:18
  5.0 2.6 %collective-permute-start.2 = (bf16[4,8320]{1,0:T(4,128)(2,1)S(1)}, bf16[4,8320]{1,0:T(4,128)(2,1)S(1)}, u32[]{:S(2)}, u32[]{:S(2)}) collective-permute-start(bf16[4,8320]{1,0:T(4,128)(2,1)S(1)} %get-tuple-element.27.refs_7_), channel_id=1, source_target_pairs={{0,8},{1,9},{2,10},{3,11},{4,12},{5,13},{6,14},{7,15},{8,0},{9,1},... | collective-permute-start | bytes 199688 | tf_op jit(solution)/shard_map/ppermute | solution.py:18
  7.6 0.0 collective-permute-start
  7.6 1.7 %collective-permute-start.6 = (bf16[4,8320]{1,0:T(4,128)(2,1)S(1)}, bf16[4,8320]{1,0:T(4,128)(2,1)S(1)}, u32[]{:S(2)}, u32[]{:S(2)}) collective-permute-start(bf16[4,8320]{1,0:T(4,128)(2,1)S(1)} %get-tuple-element.27.refs_7_), channel_id=1, source_target_pairs={{0,2},{1,3},{2,0},{3,1},{4,6},{5,7},{6,4},{7,5},{8,10},{9,11},{10,... | collective-permute-start | bytes 199688 | tf_op jit(solution)/shard_map/ppermute | solution.py:18
  9.3 0.0 collective-permute-done.4.refs_6_
  9.3 0.3 collective-permute-start.5
  9.6 3.1 %collective-permute-done.2.refs_5_ = bf16[4,8320]{1,0:T(4,128)(2,1)S(1)} collective-permute-done((bf16[4,8320]{1,0:T(4,128)(2,1)S(1)}, bf16[4,8320]{1,0:T(4,128)(2,1)S(1)}, u32[]{:S(2)}, u32[]{:S(2)}) %collective-permute-start.2) | collective-permute-done | bytes 66592 | tf_op jit(solution)/shard_map/ppermute | solution.py:18
  12.7 1.5 %collective-permute-start.3 = (bf16[4,8320]{1,0:T(4,128)(2,1)S(1)}, bf16[4,8320]{1,0:T(4,128)(2,1)S(1)}, u32[]{:S(2)}, u32[]{:S(2)}) collective-permute-start(bf16[4,8320]{1,0:T(4,128)(2,1)S(1)} %collective-permute-done.2.refs_5_), channel_id=1, source_target_pairs={{0,2},{1,3},{2,0},{3,1},{4,6},{5,7},{6,4},{7,5},{8,10},{9,11},{10,... | collective-permute-start | bytes 199688 | tf_op jit(solution)/shard_map/ppermute | solution.py:18
  14.2 0.0 collective-permute-done.refs_4_
  14.2 1.0 %collective-permute-start.1 = (bf16[4,8320]{1,0:T(4,128)(2,1)S(1)}, bf16[4,8320]{1,0:T(4,128)(2,1)S(1)}, u32[]{:S(2)}, u32[]{:S(2)}) collective-permute-start(bf16[4,8320]{1,0:T(4,128)(2,1)S(1)} %collective-permute-done.refs_4_), channel_id=1, source_target_pairs={{0,2},{1,3},{2,0},{3,1},{4,6},{5,7},{6,4},{7,5},{8,10},{9,11},{10,... | collective-permute-start | bytes 199688 | tf_op jit(solution)/shard_map/ppermute | solution.py:18
  15.2 0.0 collective-permute-done.6.refs_3_
  15.2 0.0 collective-permute-done.5.refs_2_
  15.2 1.7 %collective-permute-done.3.refs_1_ = bf16[4,8320]{1,0:T(4,128)(2,1)S(1)} collective-permute-done((bf16[4,8320]{1,0:T(4,128)(2,1)S(1)}, bf16[4,8320]{1,0:T(4,128)(2,1)S(1)}, u32[]{:S(2)}, u32[]{:S(2)}) %collective-permute-start.3) | collective-permute-done | bytes 66592 | tf_op jit(solution)/shard_map/ppermute | solution.py:18
  17.0 1.5 %collective-permute-done.1.refs_0_ = bf16[4,8320]{1,0:T(4,128)(2,1)S(1)} collective-permute-done((bf16[4,8320]{1,0:T(4,128)(2,1)S(1)}, bf16[4,8320]{1,0:T(4,128)(2,1)S(1)}, u32[]{:S(2)}, u32[]{:S(2)}) %collective-permute-start.1) | collective-permute-done | bytes 66592 | tf_op jit(solution)/shard_map/ppermute | solution.py:18
  18.5 0.1 pack.2.refs_2_.refs_3_.refs_0_
  18.6 0.1 collective-permute-start.7
  18.7 0.0 collective-permute-done.8
  18.7 1.3 %down.2 = (bf16[24,128]{1,0:T(8,128)(2,1)S(1)}, bf16[2,16,8192]{2,1,0:T(8,128)(2,1)S(1)}, bf16[1024,640]{1,0:T(8,128)(2,1)S(1)}) custom-call(bf16[2,48,8192]{2,1,0:T(8,128)(2,1)S(1)} %get-tuple-element.28.refs_0_, bf16[2,64,8192]{2,1,0:T(8,128)(2,1)S(1)} %bitcast.11, bf16[32,8320]{1,0:T(8,128)(2,1)S(1)} %pack.2.refs_2_.refs_3_.refs_0_, ...), custom_call_target="tpu_custom_call" | custom-call | flops 100663296 | bytes 4194304 | tf_op jit(solution)/shard_map/down/pallas_call | solution.py:449
  20.0 3.6 %collective-permute-start.11 = (bf16[24,128]{1,0:T(8,128)(2,1)S(1)}, bf16[24,128]{1,0:T(8,128)(2,1)S(1)}, u32[]{:S(2)}, u32[]{:S(2)}) collective-permute-start(bf16[24,128]{1,0:T(8,128)(2,1)S(1)} %get-tuple-element.30.refs_4_), channel_id=1, source_target_pairs={{0,12},{1,13},{2,14},{3,15},{4,8},{5,9},{6,10},{7,11},{8,4},{9,5},... | collective-permute-start | bytes 18440 | tf_op jit(solution)/shard_map/ppermute | solution.py:18
  23.6 0.0 collective-permute-start.10
  23.6 0.9 %collective-permute-start.9 = (bf16[24,128]{1,0:T(8,128)(2,1)S(1)}, bf16[24,128]{1,0:T(8,128)(2,1)S(1)}, u32[]{:S(2)}, u32[]{:S(2)}) collective-permute-start(bf16[24,128]{1,0:T(8,128)(2,1)S(1)} %get-tuple-element.30.refs_4_), channel_id=1, source_target_pairs={{0,4},{1,5},{2,6},{3,7},{4,0},{5,1},{6,2},{7,3},{8,12},{9,13},{10,... | collective-permute-start | bytes 18440 | tf_op jit(solution)/shard_map/ppermute | solution.py:18
  24.5 2.6 %base.4.refs_4_ = f32[64,640]{1,0:T(8,128)S(1)} custom-call(bf16[32,8320]{1,0:T(8,128)(2,1)S(1)} %pack.2.refs_2_.refs_3_.refs_0_, bf16[32,8320]{1,0:T(8,128)(2,1)S(1)} %collective-permute-done.7.refs_1_, bf16[1024,640]{1,0:T(8,128)(2,1)S(1)} %get-tuple-element.31.refs_2_, bf16[8192,640]{1,0:T(8,128)(2,1)} %refs_3_.5, ...), custom_call_target="tpu_custom_call" | custom-call | flops 335544320 | bytes 10485760 | tf_op jit(solution)/shard_map/base/pallas_call | solution.py:474
  27.1 0.0 collective-permute-done.11
  27.1 1.0 %collective-permute-done.10 = bf16[24,128]{1,0:T(8,128)(2,1)S(1)} collective-permute-done((bf16[24,128]{1,0:T(8,128)(2,1)S(1)}, bf16[24,128]{1,0:T(8,128)(2,1)S(1)}, u32[]{:S(2)}, u32[]{:S(2)}) %collective-permute-start.10) | collective-permute-done | bytes 6176 | tf_op jit(solution)/shard_map/ppermute | solution.py:18
  28.1 0.0 collective-permute-done.9
  28.1 0.1 collective-permute-start.14
  28.2 0.8 collective-permute-start.13
  29.0 1.1 %collective-permute-start.12 = (bf16[24,128]{1,0:T(8,128)(2,1)S(1)}, bf16[24,128]{1,0:T(8,128)(2,1)S(1)}, u32[]{:S(2)}, u32[]{:S(2)}) collective-permute-start(bf16[24,128]{1,0:T(8,128)(2,1)S(1)} %add_add_fusion.1.refs_4_), channel_id=1, source_target_pairs={{0,1},{1,0},{2,3},{3,2},{4,5},{5,4},{6,7},{7,6},{8,9},{9,8},{10,11... | collective-permute-start | bytes 18440 | tf_op jit(solution)/shard_map/ppermute | solution.py:18
  30.1 2.7 %base.5.refs_5_ = f32[64,640]{1,0:T(8,128)S(1)} custom-call(bf16[32,8320]{1,0:T(8,128)(2,1)S(1)} %pack.2.refs_2_.refs_3_.refs_0_, bf16[32,8320]{1,0:T(8,128)(2,1)S(1)} %collective-permute-done.7.refs_1_, bf16[1024,640]{1,0:T(8,128)(2,1)S(1)} %get-tuple-element.35.refs_2_, bf16[8192,640]{1,0:T(8,128)(2,1)} %refs_3_.5, bf16[24,128]{1,0:T(8,128)(2,1)S(1)} %add_add_fusion.1.refs_4_), custom_call_target="tpu_custom_call" | custom-call | flops 335544320 | bytes 10485760 | tf_op jit(solution)/shard_map/base/pallas_call | solution.py:474
  32.8 0.0 copy-start.5
  32.8 0.0 collective-permute-done.14
  32.8 0.0 collective-permute-done.12
  32.8 0.7 lift.2
  33.5 11.3 %all_to_all.10 = bf16[16,4,640]{2,1,0:T(4,128)(2,1)S(1)} all-to-all(bf16[16,4,640]{2,1,0:T(4,128)(2,1)S(1)} %lift.2), channel_id=1, replica_groups=mesh['groups'=2,'tensor'=16] {'tensor'}, dimensions={0} | all-to-all | bytes 163840 | tf_op jit(solution)/shard_map/all_to_all | solution.py:22
  44.8 0.0 copy-start
  44.8 2.6 %attend.1.refs_7_ = bf16[4,8192]{1,0:T(4,128)(2,1)S(1)} custom-call(s32[4]{0:T(128)S(1)} %copy-done.5, bf16[4,10240]{1,0:T(4,128)(2,1)S(1)} %bitcast.12, bf16[4,8,384,128]{3,2,1,0:T(8,128)(2,1)S(1)} %copy-done.1, bf16[4,8,384,128]{3,2,1,0:T(8,128)(2,1)S(1)} %copy-done.2), custom_call_target="tpu_custom_call" | custom-call | flops 50331648 | bytes 6291456 | tf_op jit(solution)/shard_map/attend/pallas_call | solution.py:539
  47.5 0.1 collective-permute-start.19
  47.6 1.2 %collective-permute-start.17 = (bf16[4,8192]{1,0:T(4,128)(2,1)S(1)}, bf16[4,8192]{1,0:T(4,128)(2,1)S(1)}, u32[]{:S(2)}, u32[]{:S(2)}) collective-permute-start(bf16[4,8192]{1,0:T(4,128)(2,1)S(1)} %attend.1.refs_7_), channel_id=1, source_target_pairs={{0,8},{1,9},{2,10},{3,11},{4,12},{5,13},{6,14},{7,15},{8,0},{9,1},... | collective-permute-start | bytes 196616 | tf_op jit(solution)/shard_map/ppermute | solution.py:18
  48.7 3.2 %collective-permute-start.15 = (bf16[4,8192]{1,0:T(4,128)(2,1)S(1)}, bf16[4,8192]{1,0:T(4,128)(2,1)S(1)}, u32[]{:S(2)}, u32[]{:S(2)}) collective-permute-start(bf16[4,8192]{1,0:T(4,128)(2,1)S(1)} %attend.1.refs_7_), channel_id=1, source_target_pairs={{0,12},{1,13},{2,14},{3,15},{4,8},{5,9},{6,10},{7,11},{8,4},{9,5},... | collective-permute-start | bytes 196616 | tf_op jit(solution)/shard_map/ppermute | solution.py:18
  51.9 0.4 collective-permute-done.19.refs_6_
  52.3 1.6 %collective-permute-start.20 = (bf16[4,8192]{1,0:T(4,128)(2,1)S(1)}, bf16[4,8192]{1,0:T(4,128)(2,1)S(1)}, u32[]{:S(2)}, u32[]{:S(2)}) collective-permute-start(bf16[4,8192]{1,0:T(4,128)(2,1)S(1)} %collective-permute-done.19.refs_6_), channel_id=1, source_target_pairs={{0,2},{1,3},{2,0},{3,1},{4,6},{5,7},{6,4},{7,5},{8,10},{9,11},{10,... | collective-permute-start | bytes 196616 | tf_op jit(solution)/shard_map/ppermute | solution.py:18
  54.0 1.9 %collective-permute-done.17.refs_5_ = bf16[4,8192]{1,0:T(4,128)(2,1)S(1)} collective-permute-done((bf16[4,8192]{1,0:T(4,128)(2,1)S(1)}, bf16[4,8192]{1,0:T(4,128)(2,1)S(1)}, u32[]{:S(2)}, u32[]{:S(2)}) %collective-permute-start.17) | collective-permute-done | bytes 65568 | tf_op jit(solution)/shard_map/ppermute | solution.py:18
  55.8 0.7 collective-permute-start.18
  56.5 0.0 collective-permute-done.15.refs_4_
  56.5 1.4 %collective-permute-start.16 = (bf16[4,8192]{1,0:T(4,128)(2,1)S(1)}, bf16[4,8192]{1,0:T(4,128)(2,1)S(1)}, u32[]{:S(2)}, u32[]{:S(2)}) collective-permute-start(bf16[4,8192]{1,0:T(4,128)(2,1)S(1)} %collective-permute-done.15.refs_4_), channel_id=1, source_target_pairs={{0,2},{1,3},{2,0},{3,1},{4,6},{5,7},{6,4},{7,5},{8,10},{9,11},{10,... | collective-permute-start | bytes 196616 | tf_op jit(solution)/shard_map/ppermute | solution.py:18
  57.9 2.2 %collective-permute-done.18.refs_1_ = bf16[4,8192]{1,0:T(4,128)(2,1)S(1)} collective-permute-done((bf16[4,8192]{1,0:T(4,128)(2,1)S(1)}, bf16[4,8192]{1,0:T(4,128)(2,1)S(1)}, u32[]{:S(2)}, u32[]{:S(2)}) %collective-permute-start.18) | collective-permute-done | bytes 65568 | tf_op jit(solution)/shard_map/ppermute | solution.py:18
  60.1 0.7 collective-permute-done.16.refs_0_
  60.8 0.1 pack.3.refs_2_.refs_0_
  60.9 0.1 collective-permute-start.25
  61.0 0.5 down.3.refs_3_
  61.6 1.7 %collective-permute-start.24 = (bf16[8,128]{1,0:T(8,128)(2,1)S(1)}, bf16[8,128]{1,0:T(8,128)(2,1)S(1)}, u32[]{:S(2)}, u32[]{:S(2)}) collective-permute-start(bf16[8,128]{1,0:T(8,128)(2,1)S(1)} %down.3.refs_3_), channel_id=1, source_target_pairs={{0,12},{1,13},{2,14},{3,15},{4,8},{5,9},{6,10},{7,11},{8,4},{9,5},... | collective-permute-start | bytes 6152 | tf_op jit(solution)/shard_map/ppermute | solution.py:18
  63.2 0.4 collective-permute-start.23
  63.6 2.4 %collective-permute-start.22 = (bf16[8,128]{1,0:T(8,128)(2,1)S(1)}, bf16[8,128]{1,0:T(8,128)(2,1)S(1)}, u32[]{:S(2)}, u32[]{:S(2)}) collective-permute-start(bf16[8,128]{1,0:T(8,128)(2,1)S(1)} %down.3.refs_3_), channel_id=1, source_target_pairs={{0,4},{1,5},{2,6},{3,7},{4,0},{5,1},{6,2},{7,3},{8,12},{9,13},{10,... | collective-permute-start | bytes 6152 | tf_op jit(solution)/shard_map/ppermute | solution.py:18
  66.0 2.5 %base.6.refs_4_ = f32[64,512]{1,0:T(8,128)S(1)} custom-call(bf16[32,8192]{1,0:T(8,128)(2,1)S(1)} %pack.3.refs_2_.refs_0_, bf16[32,8192]{1,0:T(8,128)(2,1)S(1)} %collective-permute-done.25.refs_1_, bf16[8192,512]{1,0:T(8,128)(2,1)} %refs_2_.3, bf16[8,128]{1,0:T(8,128)(2,1)S(1)} %down.3.refs_3_), custom_call_target="tpu_custom_call" | custom-call | flops 268435456 | bytes 8388608 | tf_op jit(solution)/shard_map/base/pallas_call | solution.py:474
  68.6 0.0 copy-start.4
  68.6 0.6 collective-permute-start.28
  69.2 0.8 collective-permute-start.27
  70.1 0.4 collective-permute-start.26
  70.5 2.5 %base.7.refs_5_ = f32[64,512]{1,0:T(8,128)S(1)} custom-call(bf16[32,8192]{1,0:T(8,128)(2,1)S(1)} %pack.3.refs_2_.refs_0_, bf16[32,8192]{1,0:T(8,128)(2,1)S(1)} %collective-permute-done.25.refs_1_, bf16[8192,512]{1,0:T(8,128)(2,1)} %refs_2_.3, bf16[8,128]{1,0:T(8,128)(2,1)S(1)} %add_add_fusion.3.refs_3_), custom_call_target="tpu_custom_call" | custom-call | flops 268435456 | bytes 8388608 | tf_op jit(solution)/shard_map/base/pallas_call | solution.py:474
  73.1 0.6 lift.3
  73.7 10.2 %all_to_all.11 = bf16[16,4,512]{2,1,0:T(4,128)(2,1)S(1)} all-to-all(bf16[16,4,512]{2,1,0:T(4,128)(2,1)S(1)} %lift.3), channel_id=1, replica_groups=mesh['groups'=2,'tensor'=16] {'tensor'}, dimensions={0} | all-to-all | bytes 131072 | tf_op jit(solution)/shard_map/all_to_all | solution.py:22
  83.9 0.6 copy.14
  (25 shorter events, 0.1 us)
Async XLA Ops:
  0.0 18.7 %collective-permute-start.8 = (bf16[2,8192,64]{1,2,0:T(8,128)(2,1)}, bf16[2,8192,64]{1,2,0:T(8,128)(2,1)S(1)}, u32[]{:S(2)}, u32[]{:S(2)}) collective-permute-start(bf16[2,8192,64]{1,2,0:T(8,128)(2,1)} %param.19), channel_id=1, source_target_pairs={{0,1},{1,0},{2,3},{3,2},{4,5},{5,4},{6,7},{7,6},{8,9},{9,8},{10,11... | collective-permute-start | bytes 6291464 | tf_op jit(solution)/shard_map/ppermute | solution.py:18
  2.4 6.9 %collective-permute-start.4 = (bf16[4,8320]{1,0:T(4,128)(2,1)S(1)}, bf16[4,8320]{1,0:T(4,128)(2,1)S(1)}, u32[]{:S(2)}, u32[]{:S(2)}) collective-permute-start(bf16[4,8320]{1,0:T(4,128)(2,1)S(1)} %get-tuple-element.27.refs_7_), channel_id=1, source_target_pairs={{0,4},{1,5},{2,6},{3,7},{4,0},{5,1},{6,2},{7,3},{8,12},{9,13},{10,... | collective-permute-start | bytes 199688 | tf_op jit(solution)/shard_map/ppermute | solution.py:18
  5.0 7.7 %collective-permute-start.2 = (bf16[4,8320]{1,0:T(4,128)(2,1)S(1)}, bf16[4,8320]{1,0:T(4,128)(2,1)S(1)}, u32[]{:S(2)}, u32[]{:S(2)}) collective-permute-start(bf16[4,8320]{1,0:T(4,128)(2,1)S(1)} %get-tuple-element.27.refs_7_), channel_id=1, source_target_pairs={{0,8},{1,9},{2,10},{3,11},{4,12},{5,13},{6,14},{7,15},{8,0},{9,1},... | collective-permute-start | bytes 199688 | tf_op jit(solution)/shard_map/ppermute | solution.py:18
  7.6 6.6 %collective-permute-start = (bf16[4,8320]{1,0:T(4,128)(2,1)S(1)}, bf16[4,8320]{1,0:T(4,128)(2,1)S(1)}, u32[]{:S(2)}, u32[]{:S(2)}) collective-permute-start(bf16[4,8320]{1,0:T(4,128)(2,1)S(1)} %get-tuple-element.27.refs_7_), channel_id=1, source_target_pairs={{0,12},{1,13},{2,14},{3,15},{4,8},{5,9},{6,10},{7,11},{8,4},{9,5},... | collective-permute-start | bytes 199688 | tf_op jit(solution)/shard_map/ppermute | solution.py:18
  7.6 7.6 %collective-permute-start.6 = (bf16[4,8320]{1,0:T(4,128)(2,1)S(1)}, bf16[4,8320]{1,0:T(4,128)(2,1)S(1)}, u32[]{:S(2)}, u32[]{:S(2)}) collective-permute-start(bf16[4,8320]{1,0:T(4,128)(2,1)S(1)} %get-tuple-element.27.refs_7_), channel_id=1, source_target_pairs={{0,2},{1,3},{2,0},{3,1},{4,6},{5,7},{6,4},{7,5},{8,10},{9,11},{10,... | collective-permute-start | bytes 199688 | tf_op jit(solution)/shard_map/ppermute | solution.py:18
  9.3 5.9 %collective-permute-start.5 = (bf16[4,8320]{1,0:T(4,128)(2,1)S(1)}, bf16[4,8320]{1,0:T(4,128)(2,1)S(1)}, u32[]{:S(2)}, u32[]{:S(2)}) collective-permute-start(bf16[4,8320]{1,0:T(4,128)(2,1)S(1)} %collective-permute-done.4.refs_6_), channel_id=1, source_target_pairs={{0,2},{1,3},{2,0},{3,1},{4,6},{5,7},{6,4},{7,5},{8,10},{9,11},{10,... | collective-permute-start | bytes 199688 | tf_op jit(solution)/shard_map/ppermute | solution.py:18
  12.7 4.3 %collective-permute-start.3 = (bf16[4,8320]{1,0:T(4,128)(2,1)S(1)}, bf16[4,8320]{1,0:T(4,128)(2,1)S(1)}, u32[]{:S(2)}, u32[]{:S(2)}) collective-permute-start(bf16[4,8320]{1,0:T(4,128)(2,1)S(1)} %collective-permute-done.2.refs_5_), channel_id=1, source_target_pairs={{0,2},{1,3},{2,0},{3,1},{4,6},{5,7},{6,4},{7,5},{8,10},{9,11},{10,... | collective-permute-start | bytes 199688 | tf_op jit(solution)/shard_map/ppermute | solution.py:18
  14.2 4.3 %collective-permute-start.1 = (bf16[4,8320]{1,0:T(4,128)(2,1)S(1)}, bf16[4,8320]{1,0:T(4,128)(2,1)S(1)}, u32[]{:S(2)}, u32[]{:S(2)}) collective-permute-start(bf16[4,8320]{1,0:T(4,128)(2,1)S(1)} %collective-permute-done.refs_4_), channel_id=1, source_target_pairs={{0,2},{1,3},{2,0},{3,1},{4,6},{5,7},{6,4},{7,5},{8,10},{9,11},{10,... | collective-permute-start | bytes 199688 | tf_op jit(solution)/shard_map/ppermute | solution.py:18
  18.6 5.9 %collective-permute-start.7 = (bf16[32,8320]{1,0:T(8,128)(2,1)S(1)}, bf16[32,8320]{1,0:T(8,128)(2,1)S(1)}, u32[]{:S(2)}, u32[]{:S(2)}) collective-permute-start(bf16[32,8320]{1,0:T(8,128)(2,1)S(1)} %pack.2.refs_2_.refs_3_.refs_0_), channel_id=1, source_target_pairs={{0,1},{1,0},{2,3},{3,2},{4,5},{5,4},{6,7},{7,6},{8,9},{9,8},{10,11... | collective-permute-start | bytes 1597448 | tf_op jit(solution)/shard_map/ppermute | solution.py:18
  20.0 7.0 %collective-permute-start.11 = (bf16[24,128]{1,0:T(8,128)(2,1)S(1)}, bf16[24,128]{1,0:T(8,128)(2,1)S(1)}, u32[]{:S(2)}, u32[]{:S(2)}) collective-permute-start(bf16[24,128]{1,0:T(8,128)(2,1)S(1)} %get-tuple-element.30.refs_4_), channel_id=1, source_target_pairs={{0,12},{1,13},{2,14},{3,15},{4,8},{5,9},{6,10},{7,11},{8,4},{9,5},... | collective-permute-start | bytes 18440 | tf_op jit(solution)/shard_map/ppermute | solution.py:18
  23.6 4.5 %collective-permute-start.10 = (bf16[24,128]{1,0:T(8,128)(2,1)S(1)}, bf16[24,128]{1,0:T(8,128)(2,1)S(1)}, u32[]{:S(2)}, u32[]{:S(2)}) collective-permute-start(bf16[24,128]{1,0:T(8,128)(2,1)S(1)} %get-tuple-element.30.refs_4_), channel_id=1, source_target_pairs={{0,8},{1,9},{2,10},{3,11},{4,12},{5,13},{6,14},{7,15},{8,0},{9,1},... | collective-permute-start | bytes 18440 | tf_op jit(solution)/shard_map/ppermute | solution.py:18
  23.6 4.5 %collective-permute-start.9 = (bf16[24,128]{1,0:T(8,128)(2,1)S(1)}, bf16[24,128]{1,0:T(8,128)(2,1)S(1)}, u32[]{:S(2)}, u32[]{:S(2)}) collective-permute-start(bf16[24,128]{1,0:T(8,128)(2,1)S(1)} %get-tuple-element.30.refs_4_), channel_id=1, source_target_pairs={{0,4},{1,5},{2,6},{3,7},{4,0},{5,1},{6,2},{7,3},{8,12},{9,13},{10,... | collective-permute-start | bytes 18440 | tf_op jit(solution)/shard_map/ppermute | solution.py:18
  28.1 4.7 %collective-permute-start.14 = (bf16[24,128]{1,0:T(8,128)(2,1)S(1)}, bf16[24,128]{1,0:T(8,128)(2,1)S(1)}, u32[]{:S(2)}, u32[]{:S(2)}) collective-permute-start(bf16[24,128]{1,0:T(8,128)(2,1)S(1)} %add_add_fusion.1.refs_4_), channel_id=1, source_target_pairs={{0,3},{1,2},{2,1},{3,0},{4,7},{5,6},{6,5},{7,4},{8,11},{9,10},{10,... | collective-permute-start | bytes 18440 | tf_op jit(solution)/shard_map/ppermute | solution.py:18
  28.2 4.6 %collective-permute-start.13 = (bf16[24,128]{1,0:T(8,128)(2,1)S(1)}, bf16[24,128]{1,0:T(8,128)(2,1)S(1)}, u32[]{:S(2)}, u32[]{:S(2)}) collective-permute-start(bf16[24,128]{1,0:T(8,128)(2,1)S(1)} %add_add_fusion.1.refs_4_), channel_id=1, source_target_pairs={{0,2},{1,3},{2,0},{3,1},{4,6},{5,7},{6,4},{7,5},{8,10},{9,11},{10,... | collective-permute-start | bytes 18440 | tf_op jit(solution)/shard_map/ppermute | solution.py:18
  29.0 3.8 %collective-permute-start.12 = (bf16[24,128]{1,0:T(8,128)(2,1)S(1)}, bf16[24,128]{1,0:T(8,128)(2,1)S(1)}, u32[]{:S(2)}, u32[]{:S(2)}) collective-permute-start(bf16[24,128]{1,0:T(8,128)(2,1)S(1)} %add_add_fusion.1.refs_4_), channel_id=1, source_target_pairs={{0,1},{1,0},{2,3},{3,2},{4,5},{5,4},{6,7},{7,6},{8,9},{9,8},{10,11... | collective-permute-start | bytes 18440 | tf_op jit(solution)/shard_map/ppermute | solution.py:18
  30.0 2.8 %copy-start.3 = (bf16[32,16,640]{2,1,0:T(8,128)(2,1)S(1)}, bf16[32,16,640]{2,1,0:T(8,128)(2,1)}, u32[]{:S(2)}) copy-start(bf16[32,16,640]{2,1,0:T(8,128)(2,1)} %refs_3_.6) | copy-start | bytes 1966084
  30.0 14.8 %copy-start.1 = (bf16[4,8,384,128]{3,2,1,0:T(8,128)(2,1)S(1)}, bf16[4,8,384,128]{3,2,1,0:T(8,128)(2,1)}, u32[]{:S(2)}) copy-start(bf16[4,8,384,128]{3,2,1,0:T(8,128)(2,1)} %keys_ref.1) | copy-start | bytes 9437188
  30.1 14.8 %copy-start.2 = (bf16[4,8,384,128]{3,2,1,0:T(8,128)(2,1)S(1)}, bf16[4,8,384,128]{3,2,1,0:T(8,128)(2,1)}, u32[]{:S(2)}) copy-start(bf16[4,8,384,128]{3,2,1,0:T(8,128)(2,1)} %values_ref.1) | copy-start | bytes 9437188
  32.8 12.0 %copy-start.5 = (s32[4]{0:T(128)S(1)}, s32[4]{0:T(128)}, u32[]{:S(2)}) copy-start(s32[4]{0:T(128)} %lengths_ref.1) | copy-start | bytes 52
  44.8 16.2 %copy-start = (bf16[2,8192,64]{1,2,0:T(8,128)(2,1)S(1)}, bf16[2,8192,64]{1,2,0:T(8,128)(2,1)}, u32[]{:S(2)}) copy-start(bf16[2,8192,64]{1,2,0:T(8,128)(2,1)} %param.19) | copy-start | bytes 6291460
  47.5 4.8 %collective-permute-start.19 = (bf16[4,8192]{1,0:T(4,128)(2,1)S(1)}, bf16[4,8192]{1,0:T(4,128)(2,1)S(1)}, u32[]{:S(2)}, u32[]{:S(2)}) collective-permute-start(bf16[4,8192]{1,0:T(4,128)(2,1)S(1)} %attend.1.refs_7_), channel_id=1, source_target_pairs={{0,4},{1,5},{2,6},{3,7},{4,0},{5,1},{6,2},{7,3},{8,12},{9,13},{10,... | collective-permute-start | bytes 196616 | tf_op jit(solution)/shard_map/ppermute | solution.py:18
  47.6 8.3 %collective-permute-start.17 = (bf16[4,8192]{1,0:T(4,128)(2,1)S(1)}, bf16[4,8192]{1,0:T(4,128)(2,1)S(1)}, u32[]{:S(2)}, u32[]{:S(2)}) collective-permute-start(bf16[4,8192]{1,0:T(4,128)(2,1)S(1)} %attend.1.refs_7_), channel_id=1, source_target_pairs={{0,8},{1,9},{2,10},{3,11},{4,12},{5,13},{6,14},{7,15},{8,0},{9,1},... | collective-permute-start | bytes 196616 | tf_op jit(solution)/shard_map/ppermute | solution.py:18
  48.7 7.8 %collective-permute-start.15 = (bf16[4,8192]{1,0:T(4,128)(2,1)S(1)}, bf16[4,8192]{1,0:T(4,128)(2,1)S(1)}, u32[]{:S(2)}, u32[]{:S(2)}) collective-permute-start(bf16[4,8192]{1,0:T(4,128)(2,1)S(1)} %attend.1.refs_7_), channel_id=1, source_target_pairs={{0,12},{1,13},{2,14},{3,15},{4,8},{5,9},{6,10},{7,11},{8,4},{9,5},... | collective-permute-start | bytes 196616 | tf_op jit(solution)/shard_map/ppermute | solution.py:18
  51.9 5.9 %collective-permute-start.21 = (bf16[4,8192]{1,0:T(4,128)(2,1)S(1)}, bf16[4,8192]{1,0:T(4,128)(2,1)S(1)}, u32[]{:S(2)}, u32[]{:S(2)}) collective-permute-start(bf16[4,8192]{1,0:T(4,128)(2,1)S(1)} %attend.1.refs_7_), channel_id=1, source_target_pairs={{0,2},{1,3},{2,0},{3,1},{4,6},{5,7},{6,4},{7,5},{8,10},{9,11},{10,... | collective-permute-start | bytes 196616 | tf_op jit(solution)/shard_map/ppermute | solution.py:18
  52.3 5.5 %collective-permute-start.20 = (bf16[4,8192]{1,0:T(4,128)(2,1)S(1)}, bf16[4,8192]{1,0:T(4,128)(2,1)S(1)}, u32[]{:S(2)}, u32[]{:S(2)}) collective-permute-start(bf16[4,8192]{1,0:T(4,128)(2,1)S(1)} %collective-permute-done.19.refs_6_), channel_id=1, source_target_pairs={{0,2},{1,3},{2,0},{3,1},{4,6},{5,7},{6,4},{7,5},{8,10},{9,11},{10,... | collective-permute-start | bytes 196616 | tf_op jit(solution)/shard_map/ppermute | solution.py:18
  55.8 4.3 %collective-permute-start.18 = (bf16[4,8192]{1,0:T(4,128)(2,1)S(1)}, bf16[4,8192]{1,0:T(4,128)(2,1)S(1)}, u32[]{:S(2)}, u32[]{:S(2)}) collective-permute-start(bf16[4,8192]{1,0:T(4,128)(2,1)S(1)} %collective-permute-done.17.refs_5_), channel_id=1, source_target_pairs={{0,2},{1,3},{2,0},{3,1},{4,6},{5,7},{6,4},{7,5},{8,10},{9,11},{10,... | collective-permute-start | bytes 196616 | tf_op jit(solution)/shard_map/ppermute | solution.py:18
  56.5 4.3 %collective-permute-start.16 = (bf16[4,8192]{1,0:T(4,128)(2,1)S(1)}, bf16[4,8192]{1,0:T(4,128)(2,1)S(1)}, u32[]{:S(2)}, u32[]{:S(2)}) collective-permute-start(bf16[4,8192]{1,0:T(4,128)(2,1)S(1)} %collective-permute-done.15.refs_4_), channel_id=1, source_target_pairs={{0,2},{1,3},{2,0},{3,1},{4,6},{5,7},{6,4},{7,5},{8,10},{9,11},{10,... | collective-permute-start | bytes 196616 | tf_op jit(solution)/shard_map/ppermute | solution.py:18
  60.9 5.1 %collective-permute-start.25 = (bf16[32,8192]{1,0:T(8,128)(2,1)S(1)}, bf16[32,8192]{1,0:T(8,128)(2,1)S(1)}, u32[]{:S(2)}, u32[]{:S(2)}) collective-permute-start(bf16[32,8192]{1,0:T(8,128)(2,1)S(1)} %pack.3.refs_2_.refs_0_), channel_id=1, source_target_pairs={{0,1},{1,0},{2,3},{3,2},{4,5},{5,4},{6,7},{7,6},{8,9},{9,8},{10,11... | collective-permute-start | bytes 1572872 | tf_op jit(solution)/shard_map/ppermute | solution.py:18
  61.6 7.0 %collective-permute-start.24 = (bf16[8,128]{1,0:T(8,128)(2,1)S(1)}, bf16[8,128]{1,0:T(8,128)(2,1)S(1)}, u32[]{:S(2)}, u32[]{:S(2)}) collective-permute-start(bf16[8,128]{1,0:T(8,128)(2,1)S(1)} %down.3.refs_3_), channel_id=1, source_target_pairs={{0,12},{1,13},{2,14},{3,15},{4,8},{5,9},{6,10},{7,11},{8,4},{9,5},... | collective-permute-start | bytes 6152 | tf_op jit(solution)/shard_map/ppermute | solution.py:18
  63.2 5.3 %collective-permute-start.23 = (bf16[8,128]{1,0:T(8,128)(2,1)S(1)}, bf16[8,128]{1,0:T(8,128)(2,1)S(1)}, u32[]{:S(2)}, u32[]{:S(2)}) collective-permute-start(bf16[8,128]{1,0:T(8,128)(2,1)S(1)} %down.3.refs_3_), channel_id=1, source_target_pairs={{0,8},{1,9},{2,10},{3,11},{4,12},{5,13},{6,14},{7,15},{8,0},{9,1},... | collective-permute-start | bytes 6152 | tf_op jit(solution)/shard_map/ppermute | solution.py:18
  63.6 4.9 %collective-permute-start.22 = (bf16[8,128]{1,0:T(8,128)(2,1)S(1)}, bf16[8,128]{1,0:T(8,128)(2,1)S(1)}, u32[]{:S(2)}, u32[]{:S(2)}) collective-permute-start(bf16[8,128]{1,0:T(8,128)(2,1)S(1)} %down.3.refs_3_), channel_id=1, source_target_pairs={{0,4},{1,5},{2,6},{3,7},{4,0},{5,1},{6,2},{7,3},{8,12},{9,13},{10,... | collective-permute-start | bytes 6152 | tf_op jit(solution)/shard_map/ppermute | solution.py:18
  68.6 4.5 %copy-start.4 = (bf16[32,16,512]{2,1,0:T(8,128)(2,1)S(1)}, bf16[32,16,512]{2,1,0:T(8,128)(2,1)}, u32[]{:S(2)}) copy-start(bf16[32,16,512]{2,1,0:T(8,128)(2,1)} %refs_3_.7) | copy-start | bytes 1572868
  68.6 4.4 %collective-permute-start.28 = (bf16[8,128]{1,0:T(8,128)(2,1)S(1)}, bf16[8,128]{1,0:T(8,128)(2,1)S(1)}, u32[]{:S(2)}, u32[]{:S(2)}) collective-permute-start(bf16[8,128]{1,0:T(8,128)(2,1)S(1)} %add_add_fusion.3.refs_3_), channel_id=1, source_target_pairs={{0,3},{1,2},{2,1},{3,0},{4,7},{5,6},{6,5},{7,4},{8,11},{9,10},{10,... | collective-permute-start | bytes 6152 | tf_op jit(solution)/shard_map/ppermute | solution.py:18
  69.2 3.8 %collective-permute-start.27 = (bf16[8,128]{1,0:T(8,128)(2,1)S(1)}, bf16[8,128]{1,0:T(8,128)(2,1)S(1)}, u32[]{:S(2)}, u32[]{:S(2)}) collective-permute-start(bf16[8,128]{1,0:T(8,128)(2,1)S(1)} %add_add_fusion.3.refs_3_), channel_id=1, source_target_pairs={{0,2},{1,3},{2,0},{3,1},{4,6},{5,7},{6,4},{7,5},{8,10},{9,11},{10,... | collective-permute-start | bytes 6152 | tf_op jit(solution)/shard_map/ppermute | solution.py:18
  70.1 3.0 %collective-permute-start.26 = (bf16[8,128]{1,0:T(8,128)(2,1)S(1)}, bf16[8,128]{1,0:T(8,128)(2,1)S(1)}, u32[]{:S(2)}, u32[]{:S(2)}) collective-permute-start(bf16[8,128]{1,0:T(8,128)(2,1)S(1)} %add_add_fusion.3.refs_3_), channel_id=1, source_target_pairs={{0,1},{1,0},{2,3},{3,2},{4,5},{5,4},{6,7},{7,6},{8,9},{9,8},{10,11... | collective-permute-start | bytes 6152 | tf_op jit(solution)/shard_map/ppermute | solution.py:18

commit v12 on v11

--- a/solution.py
+++ b/solution.py
@@ -27,17 +27,17 @@
 def sum_over(x, count, beside):
     step, turn, terms = count, 0, []
     while step > 1:
-        radix = 4 if step % 4 == 0 else 2
+        radix = 4 if turn > 1 and step % 4 == 0 else 2
         step //= radix
         others = [swap(x, count, k * step) for k in range(1, radix)]
         term = beside(turn, x)
         if term is not None:
             *others, term = lax.optimization_barrier((*others, term))
-        terms.append(term)
+            terms.append(term)
         for other in others:
             x = x + other
         turn += 1
-    return x, [t for t in terms if t is not None]
+    return x, terms
 
 
 def pack_kernel(*refs):
@@ -166,12 +166,12 @@
     ]
 
 
-def down_kernel(count, rows, pieces, ranks, *refs):
+def down_kernel(count, rows, pieces, ranks, start, *refs):
     map_refs, piece_refs = refs[:2], refs[2 : 2 + pieces]
     tag_refs, refs = refs[2 + pieces : 2 + 2 * pieces], refs[2 + 2 * pieces :]
     if len(refs) > 1:
         weight_hbm, out_ref, rest_ref, rows_ref, sems = refs
-        copies = rows_copies(weight_hbm, weight_hbm.shape[0] // 2, rows_ref, sems)
+        copies = rows_copies(weight_hbm, start, rows_ref, sems)
         for copy in copies:
             copy.start()
     else:
@@ -212,17 +212,33 @@
             copy.wait()
 
 
+def spans_of(length):
+    spans, at = [], 0
+    while at < length:
+        left = length - at
+        size = 1024 if left > 1024 else min(left, 512)
+        spans.append((at, size))
+        at += size
+    return spans
+
+
 def base_kernel(pieces, start, ready, *refs):
     ready_ref = refs[pieces] if ready else None
     weight_hbm, _, out_ref, weight_ref, sems, side_ref = refs[-6:]
     total, columns = out_ref.shape
     whole = columns // 256 * 256
     narrow = columns - whole == 128
-    stream = weight_ref.shape[0]
-    copies = rows_copies(weight_hbm, start + ready, weight_ref, sems)
+    spans = spans_of(weight_ref.shape[0])
+    copies = [
+        pltpu.make_async_copy(
+            weight_hbm.at[start + ready + k : start + ready + k + length],
+            weight_ref.at[k : k + length],
+            sems.at[i],
+        )
+        for i, (k, length) in enumerate(spans)
+    ]
     for copy in copies:
         copy.start()
-    each = stream // len(copies)
 
     def rows_of(at, length):
         return jnp.concatenate([p[:, at : at + length] for p in refs[:pieces]], axis=0)
@@ -249,24 +265,18 @@
 
     if ready:
         wide(ready_ref, 0, ready, 0)
-    early = stream - 1024
-    for i, copy in enumerate(copies):
-        copy.wait()
-        at = (i + 1) * each
-        if at % 1024 == 0 and at <= early:
-            wide(weight_ref, at - 1024, 1024, ready + at - 1024)
-        if at == early and columns > whole:
-            weight = weight_ref[:early, whole:]
+    for (k, length), copy in zip(spans, copies):
+        if (k, length) == spans[-1] and columns > whole:
+            weight = weight_ref[:k, whole:]
             if ready:
                 weight = jnp.concatenate([ready_ref[:, whole:], weight], axis=0)
             rest(weight, 0)
-    wide(weight_ref, early, 1024, ready + early)
+        copy.wait()
+        wide(weight_ref, k, length, ready + k)
     if columns > whole:
-        rest(weight_ref[early:, whole:], ready + early)
-        if narrow:
-            out_ref[:, whole:] = side_ref[:total, :128] + side_ref[total:, 128:]
-        else:
-            out_ref[:, whole:] = side_ref[...]
+        rest(weight_ref[k:, whole:], ready + k)
+        side = side_ref[...]
+        out_ref[:, whole:] = side[:total, :128] + side[total:, 128:] if narrow else side
 
 
 def lift_kernel(count, rows, pieces, bounds, rank, *refs):
@@ -332,14 +342,12 @@
     def columns(at):
         return qkv_ref[:, at : at + dim].astype(jnp.float32)
 
+    steps = []
     for first in range(0, kv_heads, together):
         heads = range(first, first + together)
         query = jnp.concatenate(
             [columns((h * groups + g) * dim) for h in heads for g in range(groups)], axis=0
         )
-        key = jnp.concatenate([columns(width + h * dim) for h in heads for _ in range(groups)], axis=0)
-        at = width + kv_heads * dim
-        value = jnp.concatenate([columns(at + h * dim) for h in heads for _ in range(groups)], axis=0)
         half = jnp.concatenate([jnp.where(odd, 0.0, query), jnp.where(odd, query, 0.0)], axis=1)
         half = half.astype(jnp.bfloat16)
         scores = jnp.zeros((context, lanes), jnp.float32)
@@ -351,6 +359,12 @@
             for b in range(rows):
                 mine = (lane // (2 * per_head) == n // 2) & (lane % rows == b)
                 scores = jnp.where(mine, every[b * context : (b + 1) * context], scores)
+        steps.append((first, heads, query, scores))
+
+    for i, (first, heads, query, scores) in enumerate(steps):
+        key = jnp.concatenate([columns(width + h * dim) for h in heads for _ in range(groups)], axis=0)
+        at = width + kv_heads * dim
+        value = jnp.concatenate([columns(at + h * dim) for h in heads for _ in range(groups)], axis=0)
         scores = jnp.where(live, scores * scale, -1e30)
         own = jnp.sum((query * key).T, axis=0, keepdims=True) * scale
         peak = jnp.maximum(jnp.max(scores, axis=0, keepdims=True), own)
@@ -359,7 +373,9 @@
         denominator = jnp.sum(weights, axis=0, keepdims=True) + own_weight
         probs = (weights / denominator).T.astype(jnp.bfloat16)
         own_prob = (own_weight / denominator).astype(jnp.bfloat16).astype(jnp.float32)
-        own_term = jnp.broadcast_to(own_prob, (dim, lanes)).T * value
+        steps[i] = (first, probs, jnp.broadcast_to(own_prob, (dim, lanes)).T * value)
+
+    for first, probs, own_term in steps:
         for n in range(0, together, 2):
             span = slice(n * per_head, (n + 2) * per_head)
             mixed = jnp.zeros((2 * per_head, dim), jnp.float32)
@@ -431,7 +447,7 @@
     def tag_specs(pieces):
         return [pl.BlockSpec((p.shape[0], LANES), lambda i: (0, width // LANES)) for p in pieces]
 
-    def downs(own, sibling, pieces, tagged, low, high, weight):
+    def downs(own, sibling, pieces, tagged, low, high, weight, start):
         ranks = high - low
         lanes = max(LANES, total)
         whole = lambda x: pl.BlockSpec(x.shape, lambda i: (0,) * len(x.shape))
@@ -447,7 +463,7 @@
             outs.append(VMEM((1024, weight.shape[1]), bf16))
             out_specs.append(spec(pl.ANY))
         return pl.pallas_call(
-            functools.partial(down_kernel, count, rows, len(pieces), (low, high)),
+            functools.partial(down_kernel, count, rows, len(pieces), (low, high), start),
             grid=(1,),
             out_shape=outs,
             in_specs=[own_spec, whole(sibling)]
@@ -478,7 +494,7 @@
             out_specs=spec(),
             scratch_shapes=[
                 VMEM((stream, columns), bf16),
-                pltpu.SemaphoreType.DMA((stream // 1024,)),
+                pltpu.SemaphoreType.DMA((len(spans_of(stream)),)),
                 VMEM(side, f32),
             ],
             compiler_params=params,
@@ -505,15 +521,18 @@
             name="lift",
         )(*tagged, *operands)
 
-    def project(column, pieces, tagged, own, sibling, ready, low, high, weight, up, bounds):
-        half = width // 2
-        down, *rest = downs(own, sibling, column, tagged[: len(column)], low, high, weight)
-        ready = ready + rest[1:]
+    def project(column, pieces, tagged, own, sibling, first_rows, low, high, weight, up, bounds):
+        eighth = width // 8
+        cuts = (0, 3 * eighth, 11 * eighth // 2 if first_rows is not None else 6 * eighth, width)
+        down, *rest = downs(
+            own, sibling, column, tagged[: len(column)], low, high, weight, cuts[2]
+        )
+        ready = [first_rows, None, rest[1] if rest[1:] else None]
 
         def term(turn, after):
-            if turn > 1:
+            if turn > 2:
                 return None
-            return base(pieces, weight, after, turn * half, ready[turn], half)
+            return base(pieces, weight, after, cuts[turn], ready[turn], cuts[turn + 1] - cuts[turn])
 
         down, base_terms = sum_over(down, count, term)
         columns = lift(down, tagged, up, base_terms, bounds, high - low)
@@ -529,7 +548,7 @@
         tagged,
         first_maps,
         sibling_maps,
-        [first_rows],
+        first_rows,
         0,
         3 * rank,
         projection_weight,
@@ -556,7 +575,7 @@
         tagged,
         own_maps,
         rest[0],
-        [None, None],
+        None,
         3 * rank,
         4 * rank,
         output_weight,

time: 84.8 us -> 85 us (level)
  starting transfers between devices: 31.2 us -> 27.4 us
  Pallas kernels: 18.3 us -> 20.3 us
  waiting for transfers between devices: 12.6 us -> 14.6 us
    ppermute x29 -> x27, starting transfers between devices: 31.2 us -> 27.4 us  [swap(): return lax.ppermute(x, AXIS, [(i, i ^ offset) for i in range(count)])]
    pallas_call x4 -> x6, Pallas kernels: 10.3 us -> 12.9 us  [base(): pl.pallas_call(functools.partial(base_kernel, len(pieces), start, length...]
    ppermute x29 -> x27, waiting for transfers between devices: 12.6 us -> 14.6 us  [swap(): return lax.ppermute(x, AXIS, [(i, i ^ offset) for i in range(count)])]
  transfers between devices with their start and end apart: 29 -> 27, of which waited for: 8 -> 11; matrix products, arithmetic and copies ran while one was open for 0% -> 0% of each run, Pallas kernels for 17% -> 20%
where the time goes in v12:
time: 85 us; the launch traced here: 84.7 us
  starting transfers between devices  27.4 us (32%)
  blocking collectives  21.4 us (25%)
  Pallas kernels  20.3 us (24%)
  waiting for transfers between devices  14.6 us (17%)
    ppermute x27, starting transfers between devices, swap(): return lax.ppermute(x, AXIS, [(i, i ^ offset) for i in range(count)])  27.4 us
    all_to_all x2, blocking collectives, exchange(): lax.all_to_all(x, AXIS, split_axis=0, concat_axis=0, axis_index_groups=gr...  21.4 us
    ppermute x27, waiting for transfers between devices, swap(): return lax.ppermute(x, AXIS, [(i, i ^ offset) for i in range(count)])  14.6 us
    pallas_call x6, Pallas kernels, base(): pl.pallas_call(functools.partial(base_kernel, len(pieces), start, length...  12.9 us
    pallas_call x1, Pallas kernels, local(): pl.pallas_call(attend_kernel, out_shape=jax.ShapeDtypeStruct((rows, width...  2.16 us
    pallas_call x1, Pallas kernels, local(): pl.pallas_call(norm_kernel, out_shape=[VMEM((rows, width + LANES), bf16),...  1.9 us
    pallas_call x2, Pallas kernels, downs(): pl.pallas_call(functools.partial(down_kernel, count, rows, len(pieces), (...  1.85 us
  transfers between devices with their start and end apart: 27, of which 11 were waited for; matrix products, arithmetic and copies ran while one was open for 0% of the time, Pallas kernels for 20%

profile of v12, /device:TPU:0, one launch (start us, length us, event | category | flops | bytes accessed | tf_op | source)
XLA Modules:
  0.0 84.7 jit_solution(2314356316777732058)
XLA Ops:
  0.0 0.5 collective-permute-start.8
  0.5 1.9 %norm.1 = (bf16[4,8320]{1,0:T(4,128)(2,1)S(1)}, bf16[2,48,8192]{2,1,0:T(8,128)(2,1)S(1)}, bf16[1024,640]{1,0:T(8,128)(2,1)S(1)}) custom-call(bf16[4,8192]{1,0:T(4,128)(2,1)} %hidden_hbm.1, bf16[8192]{0:T(1024)(128)(2,1)} %gain_hbm.1, s32[4]{0:T(128)} %bitcast.14, s32[32]{0:T(128)} %slots_hbm.1, bf16[2,64,8192]{2,1,0:T(8,128)(2,1)} %bitcast.9, ...), custom_call_target="tpu_custom_call" | custom-call | tf_op jit(solution)/shard_map/norm/pallas_call | solution.py:419
  2.4 2.6 %collective-permute-start.4 = (bf16[4,8320]{1,0:T(4,128)(2,1)S(1)}, bf16[4,8320]{1,0:T(4,128)(2,1)S(1)}, u32[]{:S(2)}, u32[]{:S(2)}) collective-permute-start(bf16[4,8320]{1,0:T(4,128)(2,1)S(1)} %get-tuple-element.27.refs_7_), channel_id=1, source_target_pairs={{0,4},{1,5},{2,6},{3,7},{4,0},{5,1},{6,2},{7,3},{8,12},{9,13},{10,... | collective-permute-start | bytes 199688 | tf_op jit(solution)/shard_map/ppermute | solution.py:18
  5.0 2.6 %collective-permute-start.2 = (bf16[4,8320]{1,0:T(4,128)(2,1)S(1)}, bf16[4,8320]{1,0:T(4,128)(2,1)S(1)}, u32[]{:S(2)}, u32[]{:S(2)}) collective-permute-start(bf16[4,8320]{1,0:T(4,128)(2,1)S(1)} %get-tuple-element.27.refs_7_), channel_id=1, source_target_pairs={{0,8},{1,9},{2,10},{3,11},{4,12},{5,13},{6,14},{7,15},{8,0},{9,1},... | collective-permute-start | bytes 199688 | tf_op jit(solution)/shard_map/ppermute | solution.py:18
  7.6 0.0 collective-permute-start
  7.6 1.7 %collective-permute-start.6 = (bf16[4,8320]{1,0:T(4,128)(2,1)S(1)}, bf16[4,8320]{1,0:T(4,128)(2,1)S(1)}, u32[]{:S(2)}, u32[]{:S(2)}) collective-permute-start(bf16[4,8320]{1,0:T(4,128)(2,1)S(1)} %get-tuple-element.27.refs_7_), channel_id=1, source_target_pairs={{0,2},{1,3},{2,0},{3,1},{4,6},{5,7},{6,4},{7,5},{8,10},{9,11},{10,... | collective-permute-start | bytes 199688 | tf_op jit(solution)/shard_map/ppermute | solution.py:18
  9.3 0.0 collective-permute-done.4.refs_6_
  9.3 0.3 collective-permute-start.5
  9.6 3.1 %collective-permute-done.2.refs_5_ = bf16[4,8320]{1,0:T(4,128)(2,1)S(1)} collective-permute-done((bf16[4,8320]{1,0:T(4,128)(2,1)S(1)}, bf16[4,8320]{1,0:T(4,128)(2,1)S(1)}, u32[]{:S(2)}, u32[]{:S(2)}) %collective-permute-start.2) | collective-permute-done | bytes 66592 | tf_op jit(solution)/shard_map/ppermute | solution.py:18
  12.7 1.5 %collective-permute-start.3 = (bf16[4,8320]{1,0:T(4,128)(2,1)S(1)}, bf16[4,8320]{1,0:T(4,128)(2,1)S(1)}, u32[]{:S(2)}, u32[]{:S(2)}) collective-permute-start(bf16[4,8320]{1,0:T(4,128)(2,1)S(1)} %collective-permute-done.2.refs_5_), channel_id=1, source_target_pairs={{0,2},{1,3},{2,0},{3,1},{4,6},{5,7},{6,4},{7,5},{8,10},{9,11},{10,... | collective-permute-start | bytes 199688 | tf_op jit(solution)/shard_map/ppermute | solution.py:18
  14.2 0.0 collective-permute-done.refs_4_
  14.2 1.0 %collective-permute-start.1 = (bf16[4,8320]{1,0:T(4,128)(2,1)S(1)}, bf16[4,8320]{1,0:T(4,128)(2,1)S(1)}, u32[]{:S(2)}, u32[]{:S(2)}) collective-permute-start(bf16[4,8320]{1,0:T(4,128)(2,1)S(1)} %collective-permute-done.refs_4_), channel_id=1, source_target_pairs={{0,2},{1,3},{2,0},{3,1},{4,6},{5,7},{6,4},{7,5},{8,10},{9,11},{10,... | collective-permute-start | bytes 199688 | tf_op jit(solution)/shard_map/ppermute | solution.py:18
  15.2 0.0 collective-permute-done.6.refs_3_
  15.2 0.0 collective-permute-done.5.refs_2_
  15.2 1.7 %collective-permute-done.3.refs_1_ = bf16[4,8320]{1,0:T(4,128)(2,1)S(1)} collective-permute-done((bf16[4,8320]{1,0:T(4,128)(2,1)S(1)}, bf16[4,8320]{1,0:T(4,128)(2,1)S(1)}, u32[]{:S(2)}, u32[]{:S(2)}) %collective-permute-start.3) | collective-permute-done | bytes 66592 | tf_op jit(solution)/shard_map/ppermute | solution.py:18
  17.0 1.5 %collective-permute-done.1.refs_0_ = bf16[4,8320]{1,0:T(4,128)(2,1)S(1)} collective-permute-done((bf16[4,8320]{1,0:T(4,128)(2,1)S(1)}, bf16[4,8320]{1,0:T(4,128)(2,1)S(1)}, u32[]{:S(2)}, u32[]{:S(2)}) %collective-permute-start.1) | collective-permute-done | bytes 66592 | tf_op jit(solution)/shard_map/ppermute | solution.py:18
  18.5 0.1 pack.2.refs_2_.refs_3_.refs_0_
  18.6 0.1 collective-permute-start.7
  18.7 0.0 collective-permute-done.8
  18.7 1.3 %down.2 = (bf16[24,128]{1,0:T(8,128)(2,1)S(1)}, bf16[2,16,8192]{2,1,0:T(8,128)(2,1)S(1)}, bf16[1024,640]{1,0:T(8,128)(2,1)S(1)}) custom-call(bf16[2,48,8192]{2,1,0:T(8,128)(2,1)S(1)} %get-tuple-element.28.refs_0_, bf16[2,64,8192]{2,1,0:T(8,128)(2,1)S(1)} %bitcast.11, bf16[32,8320]{1,0:T(8,128)(2,1)S(1)} %pack.2.refs_2_.refs_3_.refs_0_, ...), custom_call_target="tpu_custom_call" | custom-call | flops 100663296 | bytes 4194304 | tf_op jit(solution)/shard_map/down/pallas_call | solution.py:465
  20.0 1.9 %collective-permute-start.9 = (bf16[24,128]{1,0:T(8,128)(2,1)S(1)}, bf16[24,128]{1,0:T(8,128)(2,1)S(1)}, u32[]{:S(2)}, u32[]{:S(2)}) collective-permute-start(bf16[24,128]{1,0:T(8,128)(2,1)S(1)} %get-tuple-element.30.refs_4_), channel_id=1, source_target_pairs={{0,8},{1,9},{2,10},{3,11},{4,12},{5,13},{6,14},{7,15},{8,0},{9,1},... | collective-permute-start | bytes 18440 | tf_op jit(solution)/shard_map/ppermute | solution.py:18
  21.9 0.0 collective-permute-done.7.refs_1_
  21.9 2.2 %base.6.refs_4_ = f32[64,640]{1,0:T(8,128)S(1)} custom-call(bf16[32,8320]{1,0:T(8,128)(2,1)S(1)} %pack.2.refs_2_.refs_3_.refs_0_, bf16[32,8320]{1,0:T(8,128)(2,1)S(1)} %collective-permute-done.7.refs_1_, bf16[1024,640]{1,0:T(8,128)(2,1)S(1)} %get-tuple-element.31.refs_2_, bf16[8192,640]{1,0:T(8,128)(2,1)} %refs_3_.5, ...), custom_call_target="tpu_custom_call" | custom-call | flops 251658240 | bytes 7864320 | tf_op jit(solution)/shard_map/base/pallas_call | solution.py:490
  24.2 0.5 collective-permute-done.9
  24.6 1.9 %collective-permute-start.10 = (bf16[24,128]{1,0:T(8,128)(2,1)S(1)}, bf16[24,128]{1,0:T(8,128)(2,1)S(1)}, u32[]{:S(2)}, u32[]{:S(2)}) collective-permute-start(bf16[24,128]{1,0:T(8,128)(2,1)S(1)} %add.30.refs_3_), channel_id=1, source_target_pairs={{0,4},{1,5},{2,6},{3,7},{4,0},{5,1},{6,2},{7,3},{8,12},{9,13},{10,... | collective-permute-start | bytes 18440 | tf_op jit(solution)/shard_map/ppermute | solution.py:18
  26.5 2.5 %base.7.refs_5_ = f32[64,640]{1,0:T(8,128)S(1)} custom-call(bf16[32,8320]{1,0:T(8,128)(2,1)S(1)} %pack.2.refs_2_.refs_3_.refs_0_, bf16[32,8320]{1,0:T(8,128)(2,1)S(1)} %collective-permute-done.7.refs_1_, bf16[8192,640]{1,0:T(8,128)(2,1)} %refs_3_.5, bf16[24,128]{1,0:T(8,128)(2,1)S(1)} %add.30.refs_3_), custom_call_target="tpu_custom_call" | custom-call | flops 209715200 | bytes 6553600 | tf_op jit(solution)/shard_map/base/pallas_call | solution.py:490
  29.0 0.3 collective-permute-start.13
  29.3 1.3 %collective-permute-start.12 = (bf16[24,128]{1,0:T(8,128)(2,1)S(1)}, bf16[24,128]{1,0:T(8,128)(2,1)S(1)}, u32[]{:S(2)}, u32[]{:S(2)}) collective-permute-start(bf16[24,128]{1,0:T(8,128)(2,1)S(1)} %add.31.refs_4_), channel_id=1, source_target_pairs={{0,2},{1,3},{2,0},{3,1},{4,6},{5,7},{6,4},{7,5},{8,10},{9,11},{10,... | collective-permute-start | bytes 18440 | tf_op jit(solution)/shard_map/ppermute | solution.py:18
  30.6 0.3 collective-permute-start.11
  30.9 2.2 %base.8.refs_6_ = f32[64,640]{1,0:T(8,128)S(1)} custom-call(bf16[32,8320]{1,0:T(8,128)(2,1)S(1)} %pack.2.refs_2_.refs_3_.refs_0_, bf16[32,8320]{1,0:T(8,128)(2,1)S(1)} %collective-permute-done.7.refs_1_, bf16[1024,640]{1,0:T(8,128)(2,1)S(1)} %get-tuple-element.34.refs_2_, bf16[8192,640]{1,0:T(8,128)(2,1)} %refs_3_.5, bf16[24,128]{1,0:T(8,128)(2,1)S(1)} %add.31.refs_4_), custom_call_target="tpu_custom_call" | custom-call | flops 209715200 | bytes 6553600 | tf_op jit(solution)/shard_map/base/pallas_call | solution.py:490
  33.2 0.0 copy-start.5
  33.2 0.0 collective-permute-done.11
  33.2 0.7 lift.2
  33.9 11.6 %all_to_all.10 = bf16[16,4,640]{2,1,0:T(4,128)(2,1)S(1)} all-to-all(bf16[16,4,640]{2,1,0:T(4,128)(2,1)S(1)} %lift.2), channel_id=1, replica_groups=mesh['groups'=2,'tensor'=16] {'tensor'}, dimensions={0} | all-to-all | bytes 163840 | tf_op jit(solution)/shard_map/all_to_all | solution.py:22
  45.5 0.0 copy-start
  45.5 2.2 %attend.1.refs_7_ = bf16[4,8192]{1,0:T(4,128)(2,1)S(1)} custom-call(s32[4]{0:T(128)S(1)} %copy-done.5, bf16[4,10240]{1,0:T(4,128)(2,1)S(1)} %bitcast.12, bf16[4,8,384,128]{3,2,1,0:T(8,128)(2,1)S(1)} %copy-done.1, bf16[4,8,384,128]{3,2,1,0:T(8,128)(2,1)S(1)} %copy-done.2), custom_call_target="tpu_custom_call" | custom-call | flops 50331648 | bytes 6291456 | tf_op jit(solution)/shard_map/attend/pallas_call | solution.py:558
  47.7 0.1 collective-permute-start.18
  47.8 1.2 %collective-permute-start.16 = (bf16[4,8192]{1,0:T(4,128)(2,1)S(1)}, bf16[4,8192]{1,0:T(4,128)(2,1)S(1)}, u32[]{:S(2)}, u32[]{:S(2)}) collective-permute-start(bf16[4,8192]{1,0:T(4,128)(2,1)S(1)} %attend.1.refs_7_), channel_id=1, source_target_pairs={{0,8},{1,9},{2,10},{3,11},{4,12},{5,13},{6,14},{7,15},{8,0},{9,1},... | collective-permute-start | bytes 196616 | tf_op jit(solution)/shard_map/ppermute | solution.py:18
  48.9 3.2 %collective-permute-start.14 = (bf16[4,8192]{1,0:T(4,128)(2,1)S(1)}, bf16[4,8192]{1,0:T(4,128)(2,1)S(1)}, u32[]{:S(2)}, u32[]{:S(2)}) collective-permute-start(bf16[4,8192]{1,0:T(4,128)(2,1)S(1)} %attend.1.refs_7_), channel_id=1, source_target_pairs={{0,12},{1,13},{2,14},{3,15},{4,8},{5,9},{6,10},{7,11},{8,4},{9,5},... | collective-permute-start | bytes 196616 | tf_op jit(solution)/shard_map/ppermute | solution.py:18
  52.1 0.0 collective-permute-start.20
  52.1 0.4 collective-permute-done.18.refs_6_
  52.5 1.6 %collective-permute-start.19 = (bf16[4,8192]{1,0:T(4,128)(2,1)S(1)}, bf16[4,8192]{1,0:T(4,128)(2,1)S(1)}, u32[]{:S(2)}, u32[]{:S(2)}) collective-permute-start(bf16[4,8192]{1,0:T(4,128)(2,1)S(1)} %collective-permute-done.18.refs_6_), channel_id=1, source_target_pairs={{0,2},{1,3},{2,0},{3,1},{4,6},{5,7},{6,4},{7,5},{8,10},{9,11},{10,... | collective-permute-start | bytes 196616 | tf_op jit(solution)/shard_map/ppermute | solution.py:18
  54.2 1.9 %collective-permute-done.16.refs_5_ = bf16[4,8192]{1,0:T(4,128)(2,1)S(1)} collective-permute-done((bf16[4,8192]{1,0:T(4,128)(2,1)S(1)}, bf16[4,8192]{1,0:T(4,128)(2,1)S(1)}, u32[]{:S(2)}, u32[]{:S(2)}) %collective-permute-start.16) | collective-permute-done | bytes 65568 | tf_op jit(solution)/shard_map/ppermute | solution.py:18
  56.0 0.7 collective-permute-start.17
  56.7 1.4 %collective-permute-start.15 = (bf16[4,8192]{1,0:T(4,128)(2,1)S(1)}, bf16[4,8192]{1,0:T(4,128)(2,1)S(1)}, u32[]{:S(2)}, u32[]{:S(2)}) collective-permute-start(bf16[4,8192]{1,0:T(4,128)(2,1)S(1)} %collective-permute-done.14.refs_4_), channel_id=1, source_target_pairs={{0,2},{1,3},{2,0},{3,1},{4,6},{5,7},{6,4},{7,5},{8,10},{9,11},{10,... | collective-permute-start | bytes 196616 | tf_op jit(solution)/shard_map/ppermute | solution.py:18
  58.1 2.2 %collective-permute-done.17.refs_1_ = bf16[4,8192]{1,0:T(4,128)(2,1)S(1)} collective-permute-done((bf16[4,8192]{1,0:T(4,128)(2,1)S(1)}, bf16[4,8192]{1,0:T(4,128)(2,1)S(1)}, u32[]{:S(2)}, u32[]{:S(2)}) %collective-permute-start.17) | collective-permute-done | bytes 65568 | tf_op jit(solution)/shard_map/ppermute | solution.py:18
  60.3 0.7 collective-permute-done.15.refs_0_
  61.0 0.1 pack.3.refs_2_.refs_0_
  61.1 0.1 collective-permute-start.22
  61.2 0.5 down.3.refs_3_
  61.7 0.8 collective-permute-start.21
  62.6 0.5 collective-permute-done.22.refs_1_
  63.1 2.1 %base.9.refs_4_ = f32[64,512]{1,0:T(8,128)S(1)} custom-call(bf16[32,8192]{1,0:T(8,128)(2,1)S(1)} %pack.3.refs_2_.refs_0_, bf16[32,8192]{1,0:T(8,128)(2,1)S(1)} %collective-permute-done.22.refs_1_, bf16[8192,512]{1,0:T(8,128)(2,1)} %refs_2_.7, bf16[8,128]{1,0:T(8,128)(2,1)S(1)} %down.3.refs_3_), custom_call_target="tpu_custom_call" | custom-call | flops 201326592 | bytes 6291456 | tf_op jit(solution)/shard_map/base/pallas_call | solution.py:490
  65.2 1.1 %collective-permute-done.21 = bf16[8,128]{1,0:T(8,128)(2,1)S(1)} collective-permute-done((bf16[8,128]{1,0:T(8,128)(2,1)S(1)}, bf16[8,128]{1,0:T(8,128)(2,1)S(1)}, u32[]{:S(2)}, u32[]{:S(2)}) %collective-permute-start.21) | collective-permute-done | bytes 2080 | tf_op jit(solution)/shard_map/ppermute | solution.py:18
  66.3 0.6 collective-permute-start.23
  66.9 2.1 %base.10.refs_5_ = f32[64,512]{1,0:T(8,128)S(1)} custom-call(bf16[32,8192]{1,0:T(8,128)(2,1)S(1)} %pack.3.refs_2_.refs_0_, bf16[32,8192]{1,0:T(8,128)(2,1)S(1)} %collective-permute-done.22.refs_1_, bf16[8192,512]{1,0:T(8,128)(2,1)} %refs_2_.7, bf16[8,128]{1,0:T(8,128)(2,1)S(1)} %add.35.refs_3_), custom_call_target="tpu_custom_call" | custom-call | flops 201326592 | bytes 6291456 | tf_op jit(solution)/shard_map/base/pallas_call | solution.py:490
  69.0 0.9 %collective-permute-done.23 = bf16[8,128]{1,0:T(8,128)(2,1)S(1)} collective-permute-done((bf16[8,128]{1,0:T(8,128)(2,1)S(1)}, bf16[8,128]{1,0:T(8,128)(2,1)S(1)}, u32[]{:S(2)}, u32[]{:S(2)}) %collective-permute-start.23) | collective-permute-done | bytes 2080 | tf_op jit(solution)/shard_map/ppermute | solution.py:18
  69.9 1.4 %collective-permute-start.25 = (bf16[8,128]{1,0:T(8,128)(2,1)S(1)}, bf16[8,128]{1,0:T(8,128)(2,1)S(1)}, u32[]{:S(2)}, u32[]{:S(2)}) collective-permute-start(bf16[8,128]{1,0:T(8,128)(2,1)S(1)} %add.36.refs_3_), channel_id=1, source_target_pairs={{0,2},{1,3},{2,0},{3,1},{4,6},{5,7},{6,4},{7,5},{8,10},{9,11},{10,... | collective-permute-start | bytes 6152 | tf_op jit(solution)/shard_map/ppermute | solution.py:18
  71.3 0.5 collective-permute-start.24
  71.8 1.8 %base.11.refs_6_ = f32[64,512]{1,0:T(8,128)S(1)} custom-call(bf16[32,8192]{1,0:T(8,128)(2,1)S(1)} %pack.3.refs_2_.refs_0_, bf16[32,8192]{1,0:T(8,128)(2,1)S(1)} %collective-permute-done.22.refs_1_, bf16[8192,512]{1,0:T(8,128)(2,1)} %refs_2_.7, bf16[8,128]{1,0:T(8,128)(2,1)S(1)} %add.36.refs_3_), custom_call_target="tpu_custom_call" | custom-call | flops 134217728 | bytes 4194304 | tf_op jit(solution)/shard_map/base/pallas_call | solution.py:490
  73.5 0.0 collective-permute-done.25
  73.6 0.6 lift.3
  74.2 9.8 %all_to_all.11 = bf16[16,4,512]{2,1,0:T(4,128)(2,1)S(1)} all-to-all(bf16[16,4,512]{2,1,0:T(4,128)(2,1)S(1)} %lift.3), channel_id=1, replica_groups=mesh['groups'=2,'tensor'=16] {'tensor'}, dimensions={0} | all-to-all | bytes 131072 | tf_op jit(solution)/shard_map/all_to_all | solution.py:22
  84.1 0.6 copy.14
  (25 shorter events, 0.1 us)
Async XLA Ops:
  0.0 18.7 %collective-permute-start.8 = (bf16[2,8192,64]{1,2,0:T(8,128)(2,1)}, bf16[2,8192,64]{1,2,0:T(8,128)(2,1)S(1)}, u32[]{:S(2)}, u32[]{:S(2)}) collective-permute-start(bf16[2,8192,64]{1,2,0:T(8,128)(2,1)} %param.19), channel_id=1, source_target_pairs={{0,1},{1,0},{2,3},{3,2},{4,5},{5,4},{6,7},{7,6},{8,9},{9,8},{10,11... | collective-permute-start | bytes 6291464 | tf_op jit(solution)/shard_map/ppermute | solution.py:18
  2.4 6.9 %collective-permute-start.4 = (bf16[4,8320]{1,0:T(4,128)(2,1)S(1)}, bf16[4,8320]{1,0:T(4,128)(2,1)S(1)}, u32[]{:S(2)}, u32[]{:S(2)}) collective-permute-start(bf16[4,8320]{1,0:T(4,128)(2,1)S(1)} %get-tuple-element.27.refs_7_), channel_id=1, source_target_pairs={{0,4},{1,5},{2,6},{3,7},{4,0},{5,1},{6,2},{7,3},{8,12},{9,13},{10,... | collective-permute-start | bytes 199688 | tf_op jit(solution)/shard_map/ppermute | solution.py:18
  5.0 7.7 %collective-permute-start.2 = (bf16[4,8320]{1,0:T(4,128)(2,1)S(1)}, bf16[4,8320]{1,0:T(4,128)(2,1)S(1)}, u32[]{:S(2)}, u32[]{:S(2)}) collective-permute-start(bf16[4,8320]{1,0:T(4,128)(2,1)S(1)} %get-tuple-element.27.refs_7_), channel_id=1, source_target_pairs={{0,8},{1,9},{2,10},{3,11},{4,12},{5,13},{6,14},{7,15},{8,0},{9,1},... | collective-permute-start | bytes 199688 | tf_op jit(solution)/shard_map/ppermute | solution.py:18
  7.6 6.6 %collective-permute-start = (bf16[4,8320]{1,0:T(4,128)(2,1)S(1)}, bf16[4,8320]{1,0:T(4,128)(2,1)S(1)}, u32[]{:S(2)}, u32[]{:S(2)}) collective-permute-start(bf16[4,8320]{1,0:T(4,128)(2,1)S(1)} %get-tuple-element.27.refs_7_), channel_id=1, source_target_pairs={{0,12},{1,13},{2,14},{3,15},{4,8},{5,9},{6,10},{7,11},{8,4},{9,5},... | collective-permute-start | bytes 199688 | tf_op jit(solution)/shard_map/ppermute | solution.py:18
  7.6 7.6 %collective-permute-start.6 = (bf16[4,8320]{1,0:T(4,128)(2,1)S(1)}, bf16[4,8320]{1,0:T(4,128)(2,1)S(1)}, u32[]{:S(2)}, u32[]{:S(2)}) collective-permute-start(bf16[4,8320]{1,0:T(4,128)(2,1)S(1)} %get-tuple-element.27.refs_7_), channel_id=1, source_target_pairs={{0,2},{1,3},{2,0},{3,1},{4,6},{5,7},{6,4},{7,5},{8,10},{9,11},{10,... | collective-permute-start | bytes 199688 | tf_op jit(solution)/shard_map/ppermute | solution.py:18
  9.3 5.9 %collective-permute-start.5 = (bf16[4,8320]{1,0:T(4,128)(2,1)S(1)}, bf16[4,8320]{1,0:T(4,128)(2,1)S(1)}, u32[]{:S(2)}, u32[]{:S(2)}) collective-permute-start(bf16[4,8320]{1,0:T(4,128)(2,1)S(1)} %collective-permute-done.4.refs_6_), channel_id=1, source_target_pairs={{0,2},{1,3},{2,0},{3,1},{4,6},{5,7},{6,4},{7,5},{8,10},{9,11},{10,... | collective-permute-start | bytes 199688 | tf_op jit(solution)/shard_map/ppermute | solution.py:18
  12.7 4.3 %collective-permute-start.3 = (bf16[4,8320]{1,0:T(4,128)(2,1)S(1)}, bf16[4,8320]{1,0:T(4,128)(2,1)S(1)}, u32[]{:S(2)}, u32[]{:S(2)}) collective-permute-start(bf16[4,8320]{1,0:T(4,128)(2,1)S(1)} %collective-permute-done.2.refs_5_), channel_id=1, source_target_pairs={{0,2},{1,3},{2,0},{3,1},{4,6},{5,7},{6,4},{7,5},{8,10},{9,11},{10,... | collective-permute-start | bytes 199688 | tf_op jit(solution)/shard_map/ppermute | solution.py:18
  14.2 4.3 %collective-permute-start.1 = (bf16[4,8320]{1,0:T(4,128)(2,1)S(1)}, bf16[4,8320]{1,0:T(4,128)(2,1)S(1)}, u32[]{:S(2)}, u32[]{:S(2)}) collective-permute-start(bf16[4,8320]{1,0:T(4,128)(2,1)S(1)} %collective-permute-done.refs_4_), channel_id=1, source_target_pairs={{0,2},{1,3},{2,0},{3,1},{4,6},{5,7},{6,4},{7,5},{8,10},{9,11},{10,... | collective-permute-start | bytes 199688 | tf_op jit(solution)/shard_map/ppermute | solution.py:18
  18.6 3.3 %collective-permute-start.7 = (bf16[32,8320]{1,0:T(8,128)(2,1)S(1)}, bf16[32,8320]{1,0:T(8,128)(2,1)S(1)}, u32[]{:S(2)}, u32[]{:S(2)}) collective-permute-start(bf16[32,8320]{1,0:T(8,128)(2,1)S(1)} %pack.2.refs_2_.refs_3_.refs_0_), channel_id=1, source_target_pairs={{0,1},{1,0},{2,3},{3,2},{4,5},{5,4},{6,7},{7,6},{8,9},{9,8},{10,11... | collective-permute-start | bytes 1597448 | tf_op jit(solution)/shard_map/ppermute | solution.py:18
  20.0 4.6 %collective-permute-start.9 = (bf16[24,128]{1,0:T(8,128)(2,1)S(1)}, bf16[24,128]{1,0:T(8,128)(2,1)S(1)}, u32[]{:S(2)}, u32[]{:S(2)}) collective-permute-start(bf16[24,128]{1,0:T(8,128)(2,1)S(1)} %get-tuple-element.30.refs_4_), channel_id=1, source_target_pairs={{0,8},{1,9},{2,10},{3,11},{4,12},{5,13},{6,14},{7,15},{8,0},{9,1},... | collective-permute-start | bytes 18440 | tf_op jit(solution)/shard_map/ppermute | solution.py:18
  24.6 4.3 %collective-permute-start.10 = (bf16[24,128]{1,0:T(8,128)(2,1)S(1)}, bf16[24,128]{1,0:T(8,128)(2,1)S(1)}, u32[]{:S(2)}, u32[]{:S(2)}) collective-permute-start(bf16[24,128]{1,0:T(8,128)(2,1)S(1)} %add.30.refs_3_), channel_id=1, source_target_pairs={{0,4},{1,5},{2,6},{3,7},{4,0},{5,1},{6,2},{7,3},{8,12},{9,13},{10,... | collective-permute-start | bytes 18440 | tf_op jit(solution)/shard_map/ppermute | solution.py:18
  29.0 4.2 %collective-permute-start.13 = (bf16[24,128]{1,0:T(8,128)(2,1)S(1)}, bf16[24,128]{1,0:T(8,128)(2,1)S(1)}, u32[]{:S(2)}, u32[]{:S(2)}) collective-permute-start(bf16[24,128]{1,0:T(8,128)(2,1)S(1)} %add.31.refs_4_), channel_id=1, source_target_pairs={{0,3},{1,2},{2,1},{3,0},{4,7},{5,6},{6,5},{7,4},{8,11},{9,10},{10,... | collective-permute-start | bytes 18440 | tf_op jit(solution)/shard_map/ppermute | solution.py:18
  29.3 3.9 %collective-permute-start.12 = (bf16[24,128]{1,0:T(8,128)(2,1)S(1)}, bf16[24,128]{1,0:T(8,128)(2,1)S(1)}, u32[]{:S(2)}, u32[]{:S(2)}) collective-permute-start(bf16[24,128]{1,0:T(8,128)(2,1)S(1)} %add.31.refs_4_), channel_id=1, source_target_pairs={{0,2},{1,3},{2,0},{3,1},{4,6},{5,7},{6,4},{7,5},{8,10},{9,11},{10,... | collective-permute-start | bytes 18440 | tf_op jit(solution)/shard_map/ppermute | solution.py:18
  30.6 2.6 %collective-permute-start.11 = (bf16[24,128]{1,0:T(8,128)(2,1)S(1)}, bf16[24,128]{1,0:T(8,128)(2,1)S(1)}, u32[]{:S(2)}, u32[]{:S(2)}) collective-permute-start(bf16[24,128]{1,0:T(8,128)(2,1)S(1)} %add.31.refs_4_), channel_id=1, source_target_pairs={{0,1},{1,0},{2,3},{3,2},{4,5},{5,4},{6,7},{7,6},{8,9},{9,8},{10,11... | collective-permute-start | bytes 18440 | tf_op jit(solution)/shard_map/ppermute | solution.py:18
  30.9 2.3 %copy-start.3 = (bf16[32,16,640]{2,1,0:T(8,128)(2,1)S(1)}, bf16[32,16,640]{2,1,0:T(8,128)(2,1)}, u32[]{:S(2)}) copy-start(bf16[32,16,640]{2,1,0:T(8,128)(2,1)} %refs_3_.6) | copy-start | bytes 1966084
  30.9 14.6 %copy-start.1 = (bf16[4,8,384,128]{3,2,1,0:T(8,128)(2,1)S(1)}, bf16[4,8,384,128]{3,2,1,0:T(8,128)(2,1)}, u32[]{:S(2)}) copy-start(bf16[4,8,384,128]{3,2,1,0:T(8,128)(2,1)} %keys_ref.1) | copy-start | bytes 9437188
  30.9 14.6 %copy-start.2 = (bf16[4,8,384,128]{3,2,1,0:T(8,128)(2,1)S(1)}, bf16[4,8,384,128]{3,2,1,0:T(8,128)(2,1)}, u32[]{:S(2)}) copy-start(bf16[4,8,384,128]{3,2,1,0:T(8,128)(2,1)} %values_ref.1) | copy-start | bytes 9437188
  33.2 12.3 %copy-start.5 = (s32[4]{0:T(128)S(1)}, s32[4]{0:T(128)}, u32[]{:S(2)}) copy-start(s32[4]{0:T(128)} %lengths_ref.1) | copy-start | bytes 52
  45.5 15.7 %copy-start = (bf16[2,8192,64]{1,2,0:T(8,128)(2,1)S(1)}, bf16[2,8192,64]{1,2,0:T(8,128)(2,1)}, u32[]{:S(2)}) copy-start(bf16[2,8192,64]{1,2,0:T(8,128)(2,1)} %param.19) | copy-start | bytes 6291460
  47.7 4.8 %collective-permute-start.18 = (bf16[4,8192]{1,0:T(4,128)(2,1)S(1)}, bf16[4,8192]{1,0:T(4,128)(2,1)S(1)}, u32[]{:S(2)}, u32[]{:S(2)}) collective-permute-start(bf16[4,8192]{1,0:T(4,128)(2,1)S(1)} %attend.1.refs_7_), channel_id=1, source_target_pairs={{0,4},{1,5},{2,6},{3,7},{4,0},{5,1},{6,2},{7,3},{8,12},{9,13},{10,... | collective-permute-start | bytes 196616 | tf_op jit(solution)/shard_map/ppermute | solution.py:18
  47.8 8.3 %collective-permute-start.16 = (bf16[4,8192]{1,0:T(4,128)(2,1)S(1)}, bf16[4,8192]{1,0:T(4,128)(2,1)S(1)}, u32[]{:S(2)}, u32[]{:S(2)}) collective-permute-start(bf16[4,8192]{1,0:T(4,128)(2,1)S(1)} %attend.1.refs_7_), channel_id=1, source_target_pairs={{0,8},{1,9},{2,10},{3,11},{4,12},{5,13},{6,14},{7,15},{8,0},{9,1},... | collective-permute-start | bytes 196616 | tf_op jit(solution)/shard_map/ppermute | solution.py:18
  48.9 7.8 %collective-permute-start.14 = (bf16[4,8192]{1,0:T(4,128)(2,1)S(1)}, bf16[4,8192]{1,0:T(4,128)(2,1)S(1)}, u32[]{:S(2)}, u32[]{:S(2)}) collective-permute-start(bf16[4,8192]{1,0:T(4,128)(2,1)S(1)} %attend.1.refs_7_), channel_id=1, source_target_pairs={{0,12},{1,13},{2,14},{3,15},{4,8},{5,9},{6,10},{7,11},{8,4},{9,5},... | collective-permute-start | bytes 196616 | tf_op jit(solution)/shard_map/ppermute | solution.py:18
  52.1 5.9 %collective-permute-start.20 = (bf16[4,8192]{1,0:T(4,128)(2,1)S(1)}, bf16[4,8192]{1,0:T(4,128)(2,1)S(1)}, u32[]{:S(2)}, u32[]{:S(2)}) collective-permute-start(bf16[4,8192]{1,0:T(4,128)(2,1)S(1)} %attend.1.refs_7_), channel_id=1, source_target_pairs={{0,2},{1,3},{2,0},{3,1},{4,6},{5,7},{6,4},{7,5},{8,10},{9,11},{10,... | collective-permute-start | bytes 196616 | tf_op jit(solution)/shard_map/ppermute | solution.py:18
  52.5 5.5 %collective-permute-start.19 = (bf16[4,8192]{1,0:T(4,128)(2,1)S(1)}, bf16[4,8192]{1,0:T(4,128)(2,1)S(1)}, u32[]{:S(2)}, u32[]{:S(2)}) collective-permute-start(bf16[4,8192]{1,0:T(4,128)(2,1)S(1)} %collective-permute-done.18.refs_6_), channel_id=1, source_target_pairs={{0,2},{1,3},{2,0},{3,1},{4,6},{5,7},{6,4},{7,5},{8,10},{9,11},{10,... | collective-permute-start | bytes 196616 | tf_op jit(solution)/shard_map/ppermute | solution.py:18
  56.0 4.3 %collective-permute-start.17 = (bf16[4,8192]{1,0:T(4,128)(2,1)S(1)}, bf16[4,8192]{1,0:T(4,128)(2,1)S(1)}, u32[]{:S(2)}, u32[]{:S(2)}) collective-permute-start(bf16[4,8192]{1,0:T(4,128)(2,1)S(1)} %collective-permute-done.16.refs_5_), channel_id=1, source_target_pairs={{0,2},{1,3},{2,0},{3,1},{4,6},{5,7},{6,4},{7,5},{8,10},{9,11},{10,... | collective-permute-start | bytes 196616 | tf_op jit(solution)/shard_map/ppermute | solution.py:18
  56.7 4.3 %collective-permute-start.15 = (bf16[4,8192]{1,0:T(4,128)(2,1)S(1)}, bf16[4,8192]{1,0:T(4,128)(2,1)S(1)}, u32[]{:S(2)}, u32[]{:S(2)}) collective-permute-start(bf16[4,8192]{1,0:T(4,128)(2,1)S(1)} %collective-permute-done.14.refs_4_), channel_id=1, source_target_pairs={{0,2},{1,3},{2,0},{3,1},{4,6},{5,7},{6,4},{7,5},{8,10},{9,11},{10,... | collective-permute-start | bytes 196616 | tf_op jit(solution)/shard_map/ppermute | solution.py:18
  61.1 2.0 %collective-permute-start.22 = (bf16[32,8192]{1,0:T(8,128)(2,1)S(1)}, bf16[32,8192]{1,0:T(8,128)(2,1)S(1)}, u32[]{:S(2)}, u32[]{:S(2)}) collective-permute-start(bf16[32,8192]{1,0:T(8,128)(2,1)S(1)} %pack.3.refs_2_.refs_0_), channel_id=1, source_target_pairs={{0,1},{1,0},{2,3},{3,2},{4,5},{5,4},{6,7},{7,6},{8,9},{9,8},{10,11... | collective-permute-start | bytes 1572872 | tf_op jit(solution)/shard_map/ppermute | solution.py:18
  61.7 4.6 %collective-permute-start.21 = (bf16[8,128]{1,0:T(8,128)(2,1)S(1)}, bf16[8,128]{1,0:T(8,128)(2,1)S(1)}, u32[]{:S(2)}, u32[]{:S(2)}) collective-permute-start(bf16[8,128]{1,0:T(8,128)(2,1)S(1)} %down.3.refs_3_), channel_id=1, source_target_pairs={{0,8},{1,9},{2,10},{3,11},{4,12},{5,13},{6,14},{7,15},{8,0},{9,1},... | collective-permute-start | bytes 6152 | tf_op jit(solution)/shard_map/ppermute | solution.py:18
  66.3 3.6 %collective-permute-start.23 = (bf16[8,128]{1,0:T(8,128)(2,1)S(1)}, bf16[8,128]{1,0:T(8,128)(2,1)S(1)}, u32[]{:S(2)}, u32[]{:S(2)}) collective-permute-start(bf16[8,128]{1,0:T(8,128)(2,1)S(1)} %add.35.refs_3_), channel_id=1, source_target_pairs={{0,4},{1,5},{2,6},{3,7},{4,0},{5,1},{6,2},{7,3},{8,12},{9,13},{10,... | collective-permute-start | bytes 6152 | tf_op jit(solution)/shard_map/ppermute | solution.py:18
  69.9 3.7 %copy-start.4 = (bf16[32,16,512]{2,1,0:T(8,128)(2,1)S(1)}, bf16[32,16,512]{2,1,0:T(8,128)(2,1)}, u32[]{:S(2)}) copy-start(bf16[32,16,512]{2,1,0:T(8,128)(2,1)} %refs_3_.7) | copy-start | bytes 1572868
  69.9 3.6 %collective-permute-start.26 = (bf16[8,128]{1,0:T(8,128)(2,1)S(1)}, bf16[8,128]{1,0:T(8,128)(2,1)S(1)}, u32[]{:S(2)}, u32[]{:S(2)}) collective-permute-start(bf16[8,128]{1,0:T(8,128)(2,1)S(1)} %add.36.refs_3_), channel_id=1, source_target_pairs={{0,3},{1,2},{2,1},{3,0},{4,7},{5,6},{6,5},{7,4},{8,11},{9,10},{10,... | collective-permute-start | bytes 6152 | tf_op jit(solution)/shard_map/ppermute | solution.py:18
  69.9 3.7 %collective-permute-start.25 = (bf16[8,128]{1,0:T(8,128)(2,1)S(1)}, bf16[8,128]{1,0:T(8,128)(2,1)S(1)}, u32[]{:S(2)}, u32[]{:S(2)}) collective-permute-start(bf16[8,128]{1,0:T(8,128)(2,1)S(1)} %add.36.refs_3_), channel_id=1, source_target_pairs={{0,2},{1,3},{2,0},{3,1},{4,6},{5,7},{6,4},{7,5},{8,10},{9,11},{10,... | collective-permute-start | bytes 6152 | tf_op jit(solution)/shard_map/ppermute | solution.py:18
  71.3 2.3 %collective-permute-start.24 = (bf16[8,128]{1,0:T(8,128)(2,1)S(1)}, bf16[8,128]{1,0:T(8,128)(2,1)S(1)}, u32[]{:S(2)}, u32[]{:S(2)}) collective-permute-start(bf16[8,128]{1,0:T(8,128)(2,1)S(1)} %add.36.refs_3_), channel_id=1, source_target_pairs={{0,1},{1,0},{2,3},{3,2},{4,5},{5,4},{6,7},{7,6},{8,9},{9,8},{10,11... | collective-permute-start | bytes 6152 | tf_op jit(solution)/shard_map/ppermute | solution.py:18

commit v13 on v12

--- a/solution.py
+++ b/solution.py
@@ -27,7 +27,7 @@
 def sum_over(x, count, beside):
     step, turn, terms = count, 0, []
     while step > 1:
-        radix = 4 if turn > 1 and step % 4 == 0 else 2
+        radix = 4 if step % 4 == 0 else 2
         step //= radix
         others = [swap(x, count, k * step) for k in range(1, radix)]
         term = beside(turn, x)
@@ -62,17 +62,18 @@
     )(*parts[::-1])
 
 
-def gather_rows(x, count):
+def gather_rows(x, count, beside):
     step = count // 4
     near, middle, far = (swap(x, count, k * step) for k in (1, 2, 3))
     step //= 2
     across = [swap(p, count, step) for p in (x, near, middle, far)]
-    held = [pack([x, near, middle, far] + across)]
+    *across, loaded = lax.optimization_barrier((*across[::-1], beside(far)))
+    held = [pack([x, near, middle, far] + across[::-1])]
     step //= 2
     while step > 1:
         held = held + [swap(h, count, step) for h in held]
         step //= 2
-    return held, held + [swap(h, count, 1) for h in held]
+    return held, held + [swap(h, count, 1) for h in held], loaded
 
 
 def place_of(row, me, count, rows):
@@ -102,23 +103,8 @@
 
 
 def norm_kernel(
-    hidden_hbm,
-    gain_hbm,
-    names_hbm,
-    slots_hbm,
-    maps_hbm,
-    weight_hbm,
-    out_ref,
-    maps_ref,
-    weight_ref,
-    hidden_ref,
-    gain_ref,
-    names_ref,
-    slots_ref,
-    sems,
-    row_sems,
+    hidden_hbm, gain_hbm, names_hbm, slots_hbm, out_ref, hidden_ref, gain_ref, names_ref, slots_ref, sems
 ):
-    ranks = maps_ref.shape[1]
     copies = [
         pltpu.make_async_copy(source, target, sems.at[i])
         for i, (source, target) in enumerate(
@@ -127,13 +113,12 @@
                 (gain_hbm, gain_ref),
                 (names_hbm, names_ref),
                 (slots_hbm, slots_ref),
-                (maps_hbm.at[:, :ranks], maps_ref),
             )
         )
-    ] + rows_copies(weight_hbm, 0, weight_ref, row_sems)
+    ]
     for copy in copies:
         copy.start()
-    for copy in copies[:4]:
+    for copy in copies:
         copy.wait()
     rows, width = hidden_ref.shape
     hidden = hidden_ref[...].astype(jnp.float32)
@@ -147,35 +132,34 @@
         tag = jnp.where(lane < LANES // 2, name, slots_ref[name]).astype(jnp.float32)
         tags = jnp.where(row == r, tag, tags)
     out_ref[:, width:] = tags.astype(jnp.bfloat16)
-    for copy in copies[4:]:
+
+
+NT = (((1,), (1,)), ((), ()))
+
+
+def load_kernel(starts, *refs):
+    _, weight_hbm, *refs = refs
+    *refs, sems = refs
+    rows_refs, refs = refs[-len(starts) :], refs[: -len(starts)]
+    copies = []
+    if refs:
+        maps_hbm, maps_ref = refs
+        for s in range(maps_ref.shape[0]):
+            copies.append((maps_hbm.at[s, : maps_ref.shape[1]], maps_ref.at[s]))
+    for start, rows_ref in zip(starts, rows_refs):
+        for k in range(0, rows_ref.shape[0], 1024):
+            copies.append((weight_hbm.at[start + k : start + k + 1024], rows_ref.at[k : k + 1024]))
+    copies = [pltpu.make_async_copy(*ends, sems.at[i]) for i, ends in enumerate(copies)]
+    for copy in copies:
+        copy.start()
+    for copy in copies:
         copy.wait()
 
 
-NT = (((1,), (1,)), ((), ()))
-
-
-def rows_copies(weight_hbm, start, rows_ref, sems):
-    length = rows_ref.shape[0] // sems.shape[0]
-    return [
-        pltpu.make_async_copy(
-            weight_hbm.at[start + i * length : start + (i + 1) * length],
-            rows_ref.at[i * length : (i + 1) * length],
-            sems.at[i],
-        )
-        for i in range(sems.shape[0])
-    ]
-
-
-def down_kernel(count, rows, pieces, ranks, start, *refs):
+def down_kernel(count, rows, pieces, ranks, *refs):
     map_refs, piece_refs = refs[:2], refs[2 : 2 + pieces]
     tag_refs, refs = refs[2 + pieces : 2 + 2 * pieces], refs[2 + 2 * pieces :]
-    if len(refs) > 1:
-        weight_hbm, out_ref, rest_ref, rows_ref, sems = refs
-        copies = rows_copies(weight_hbm, start, rows_ref, sems)
-        for copy in copies:
-            copy.start()
-    else:
-        (out_ref,) = refs
+    out_ref = refs[0]
     me = lax.axis_index(AXIS)
     held, _, width = map_refs[0].shape
     rank = ranks[1] - ranks[0]
@@ -189,7 +173,7 @@
         )
         sums = sums + lax.dot_general(maps, x, NT, preferred_element_type=jnp.float32)
     if len(refs) > 1:
-        rest_ref[...] = map_refs[1][:, rank:]
+        refs[1][...] = map_refs[1][:, rank:]
     tags = jnp.concatenate([t[...] for t in tag_refs], axis=0)
     pick = one_hot(iota((16, LANES), 1) == LANES // 2)
     slots = lax.dot_general(pick, tags, NT, preferred_element_type=jnp.float32)[:1]
@@ -207,9 +191,6 @@
     folded = [placed[f * part : (f + 1) * part] for f in range(folds)]
     value = jnp.concatenate(folded, axis=1).astype(jnp.bfloat16)
     out_ref[...] = value
-    if len(refs) > 1:
-        for copy in copies:
-            copy.wait()
 
 
 def spans_of(length):
@@ -416,22 +397,17 @@
     params = pltpu.CompilerParams(vmem_limit_bytes=(16 if total <= 64 else 60) * 1024 * 1024)
     own_maps = jnp.swapaxes(adapter_down, 1, 2)
 
-    normed, first_maps, first_rows = pl.pallas_call(
+    normed = pl.pallas_call(
         norm_kernel,
-        out_shape=[
-            VMEM((rows, width + LANES), bf16),
-            VMEM((held, 3 * rank, width), bf16),
-            VMEM((1024, projection_weight.shape[1]), bf16),
-        ],
-        in_specs=[spec(pltpu.HBM)] * 6,
-        out_specs=[spec()] * 3,
+        out_shape=VMEM((rows, width + LANES), bf16),
+        in_specs=[spec(pltpu.HBM)] * 4,
+        out_specs=spec(),
         scratch_shapes=[
             VMEM((rows, width), bf16),
             VMEM((width,), bf16),
             SMEM((rows,), jnp.int32),
             SMEM(adapter_storage.shape, jnp.int32),
-            pltpu.SemaphoreType.DMA((5,)),
-            pltpu.SemaphoreType.DMA((1,)),
+            pltpu.SemaphoreType.DMA((4,)),
         ],
         compiler_params=params,
         name="norm",
@@ -440,38 +416,50 @@
         hbm(input_norm_gain),
         hbm(request_adapter.reshape(rows)),
         hbm(adapter_storage),
-        hbm(own_maps),
-        hbm(projection_weight),
     )
+
+    def load(after, weight, parts, maps=None):
+        columns = weight.shape[1]
+        outs = [VMEM((length, columns), bf16) for _, length in parts]
+        sources, copies = [], sum(length // 1024 for _, length in parts)
+        if maps is not None:
+            outs = [VMEM((held, 3 * rank, width), bf16)] + outs
+            sources, copies = [hbm(maps)], copies + held
+        return pl.pallas_call(
+            functools.partial(load_kernel, [start for start, _ in parts]),
+            out_shape=outs,
+            in_specs=[spec(pl.ANY)] + [spec(pltpu.HBM)] * (1 + len(sources)),
+            out_specs=[spec()] * len(outs),
+            scratch_shapes=[pltpu.SemaphoreType.DMA((copies,))],
+            compiler_params=params,
+            cost_estimate=pl.CostEstimate(
+                flops=0,
+                bytes_accessed=4 * columns * sum(length for _, length in parts),
+                transcendentals=0,
+            ),
+            name="load",
+        )(after, hbm(weight), *sources)
 
     def tag_specs(pieces):
         return [pl.BlockSpec((p.shape[0], LANES), lambda i: (0, width // LANES)) for p in pieces]
 
-    def downs(own, sibling, pieces, tagged, low, high, weight, start):
+    def downs(own, sibling, pieces, tagged, low, high):
         ranks = high - low
         lanes = max(LANES, total)
         whole = lambda x: pl.BlockSpec(x.shape, lambda i: (0,) * len(x.shape))
         own_spec = pl.BlockSpec((held, ranks, width), lambda i: (0, low // ranks, 0))
         outs = [jax.ShapeDtypeStruct((ranks * total // lanes, lanes), bf16)]
-        extra = []
         if low == 0:
             rest = sibling.shape[1] - ranks
             outs.append(jax.ShapeDtypeStruct((held, rest, width), bf16))
-            extra = [hbm(weight)]
-        out_specs = [whole(x) for x in outs]
-        if extra:
-            outs.append(VMEM((1024, weight.shape[1]), bf16))
-            out_specs.append(spec(pl.ANY))
         return pl.pallas_call(
-            functools.partial(down_kernel, count, rows, len(pieces), (low, high), start),
+            functools.partial(down_kernel, count, rows, len(pieces), (low, high)),
             grid=(1,),
             out_shape=outs,
             in_specs=[own_spec, whole(sibling)]
             + [pl.BlockSpec((p.shape[0], width), lambda i: (0, 0)) for p in pieces]
-            + tag_specs(tagged)
-            + [spec(pltpu.HBM)] * len(extra),
-            out_specs=out_specs,
-            scratch_shapes=[pltpu.SemaphoreType.DMA((1,))] * len(extra),
+            + tag_specs(tagged),
+            out_specs=[whole(x) for x in outs],
             compiler_params=params,
             cost_estimate=pl.CostEstimate(
                 flops=2 * total * width * held * ranks,
@@ -479,7 +467,7 @@
                 transcendentals=0,
             ),
             name="down",
-        )(own, sibling, *pieces, *tagged, *extra)
+        )(own, sibling, *pieces, *tagged)
 
     def base(pieces, weight, after, start, ready, length):
         columns = weight.shape[1]
@@ -521,18 +509,14 @@
             name="lift",
         )(*tagged, *operands)
 
-    def project(column, pieces, tagged, own, sibling, first_rows, low, high, weight, up, bounds):
-        eighth = width // 8
-        cuts = (0, 3 * eighth, 11 * eighth // 2 if first_rows is not None else 6 * eighth, width)
-        down, *rest = downs(
-            own, sibling, column, tagged[: len(column)], low, high, weight, cuts[2]
-        )
-        ready = [first_rows, None, rest[1] if rest[1:] else None]
+    def project(column, pieces, tagged, own, sibling, ready, low, high, weight, up, bounds):
+        half = width // 2
+        down, *rest = downs(own, sibling, column, tagged[: len(column)], low, high)
 
         def term(turn, after):
-            if turn > 2:
+            if turn > 1:
                 return None
-            return base(pieces, weight, after, cuts[turn], ready[turn], cuts[turn + 1] - cuts[turn])
+            return base(pieces, weight, after, turn * half, ready[turn], half)
 
         down, base_terms = sum_over(down, count, term)
         columns = lift(down, tagged, up, base_terms, bounds, high - low)
@@ -541,14 +525,17 @@
 
     bounds = (0, width, width + kv_width, width + 2 * kv_width)
     sibling_maps = jnp.swapaxes(swap(adapter_down, count, 1), 1, 2)
-    column, tagged = gather_rows(normed, count)
+    parts = ((0, 1024), (width // 2, 1024))
+    column, tagged, (first_maps, *ready) = gather_rows(
+        normed, count, lambda piece: load(piece, projection_weight, parts, own_maps)
+    )
     qkv_mine, rest = project(
         column,
         tagged,
         tagged,
         first_maps,
         sibling_maps,
-        first_rows,
+        ready,
         0,
         3 * rank,
         projection_weight,
@@ -568,14 +555,17 @@
         ),
         name="attend",
     )(lengths, qkv_mine, cache_keys, cache_values)
-    column, pieces = gather_rows(attended, count)
+    parts = ((0, 1024), (width // 2, 2048))
+    column, pieces, ready = gather_rows(
+        attended, count, lambda piece: load(piece, output_weight, parts)
+    )
     output, _ = project(
         column,
         pieces,
         tagged,
         own_maps,
         rest[0],
-        None,
+        ready,
         3 * rank,
         4 * rank,
         output_weight,

time: 85 us -> 83.9 us (0.987)
  waiting for transfers between devices: 14.6 us -> 10.4 us
  starting transfers between devices: 27.4 us -> 29.5 us
  blocking collectives: 21.4 us -> 22.6 us
    ppermute x27 -> x29, waiting for transfers between devices: 14.6 us -> 10.4 us  [swap(): return lax.ppermute(x, AXIS, [(i, i ^ offset) for i in range(count)])]
    pallas_call x1 -> x3, Pallas kernels: 1.9 us -> 5.33 us  [the longest x2 4.25 us: load(): pl.pallas_call(functools.partial(load_kernel, [start for start, _ in part...]
    pallas_call x6 -> x4, Pallas kernels: 12.9 us -> 9.44 us  [base(): pl.pallas_call(functools.partial(base_kernel, len(pieces), start, length...]
    ppermute x27 -> x29, starting transfers between devices: 27.4 us -> 29.5 us  [swap(): return lax.ppermute(x, AXIS, [(i, i ^ offset) for i in range(count)])]
    all_to_all x2, blocking collectives: 21.4 us -> 22.6 us  [exchange(): lax.all_to_all(x, AXIS, split_axis=0, concat_axis=0, axis_index_groups=gr...]
  transfers between devices with their start and end apart: 27 -> 29, of which waited for: 11 -> 11; matrix products, arithmetic and copies ran while one was open for 0% -> 0% of each run, Pallas kernels for 20% -> 20%
where the time goes in v13:
time: 83.9 us; the launch traced here: 83.6 us
  starting transfers between devices  29.5 us (35%)
  blocking collectives  22.6 us (27%)
  Pallas kernels  20.1 us (24%)
  waiting for transfers between devices  10.4 us (12%)
    ppermute x29, starting transfers between devices, swap(): return lax.ppermute(x, AXIS, [(i, i ^ offset) for i in range(count)])  29.5 us
    all_to_all x2, blocking collectives, exchange(): lax.all_to_all(x, AXIS, split_axis=0, concat_axis=0, axis_index_groups=gr...  22.6 us
    ppermute x29, waiting for transfers between devices, swap(): return lax.ppermute(x, AXIS, [(i, i ^ offset) for i in range(count)])  10.4 us
    pallas_call x4, Pallas kernels, base(): pl.pallas_call(functools.partial(base_kernel, len(pieces), start, length...  9.44 us
    pallas_call x2, Pallas kernels, load(): pl.pallas_call(functools.partial(load_kernel, [start for start, _ in part...  4.25 us
    pallas_call x1, Pallas kernels, local(): pl.pallas_call(attend_kernel, out_shape=jax.ShapeDtypeStruct((rows, width...  2.17 us
  transfers between devices with their start and end apart: 29, of which 11 were waited for; matrix products, arithmetic and copies ran while one was open for 0% of the time, Pallas kernels for 20%

profile of v13, /device:TPU:0, one launch (start us, length us, event | category | flops | bytes accessed | tf_op | source)
XLA Modules:
  0.0 83.6 jit_solution(193676737187405228)
XLA Ops:
  0.0 0.5 collective-permute-start.8
  0.5 1.1 %norm.1.refs_7_ = bf16[4,8320]{1,0:T(4,128)(2,1)S(1)} custom-call(bf16[4,8192]{1,0:T(4,128)(2,1)} %hidden_hbm.1, bf16[8192]{0:T(1024)(128)(2,1)} %gain_hbm.1, s32[4]{0:T(128)} %bitcast.14, s32[32]{0:T(128)} %slots_hbm.1), custom_call_target="tpu_custom_call" | custom-call | tf_op jit(solution)/shard_map/norm/pallas_call | solution.py:400
  1.5 4.7 %collective-permute-start = (bf16[4,8320]{1,0:T(4,128)(2,1)S(1)}, bf16[4,8320]{1,0:T(4,128)(2,1)S(1)}, u32[]{:S(2)}, u32[]{:S(2)}) collective-permute-start(bf16[4,8320]{1,0:T(4,128)(2,1)S(1)} %norm.1.refs_7_), channel_id=1, source_target_pairs={{0,12},{1,13},{2,14},{3,15},{4,8},{5,9},{6,10},{7,11},{8,4},{9,5},... | collective-permute-start | bytes 199688 | tf_op jit(solution)/shard_map/ppermute | solution.py:18
  6.2 0.6 collective-permute-start.4
  6.8 1.6 %collective-permute-start.6 = (bf16[4,8320]{1,0:T(4,128)(2,1)S(1)}, bf16[4,8320]{1,0:T(4,128)(2,1)S(1)}, u32[]{:S(2)}, u32[]{:S(2)}) collective-permute-start(bf16[4,8320]{1,0:T(4,128)(2,1)S(1)} %norm.1.refs_7_), channel_id=1, source_target_pairs={{0,2},{1,3},{2,0},{3,1},{4,6},{5,7},{6,4},{7,5},{8,10},{9,11},{10,... | collective-permute-start | bytes 199688 | tf_op jit(solution)/shard_map/ppermute | solution.py:18
  8.5 0.7 collective-permute-done.refs_0_.refs_4_
  9.2 1.5 %collective-permute-start.1 = (bf16[4,8320]{1,0:T(4,128)(2,1)S(1)}, bf16[4,8320]{1,0:T(4,128)(2,1)S(1)}, u32[]{:S(2)}, u32[]{:S(2)}) collective-permute-start(bf16[4,8320]{1,0:T(4,128)(2,1)S(1)} %collective-permute-done.refs_0_.refs_4_), channel_id=1, source_target_pairs={{0,2},{1,3},{2,0},{3,1},{4,6},{5,7},{6,4},{7,5},{8,10},{9,11},{10,... | collective-permute-start | bytes 199688 | tf_op jit(solution)/shard_map/ppermute | solution.py:18
  10.7 1.7 %collective-permute-done.2.refs_5_ = bf16[4,8320]{1,0:T(4,128)(2,1)S(1)} collective-permute-done((bf16[4,8320]{1,0:T(4,128)(2,1)S(1)}, bf16[4,8320]{1,0:T(4,128)(2,1)S(1)}, u32[]{:S(2)}, u32[]{:S(2)}) %collective-permute-start.2) | collective-permute-done | bytes 66592 | tf_op jit(solution)/shard_map/ppermute | solution.py:18
  12.4 1.5 %collective-permute-start.3 = (bf16[4,8320]{1,0:T(4,128)(2,1)S(1)}, bf16[4,8320]{1,0:T(4,128)(2,1)S(1)}, u32[]{:S(2)}, u32[]{:S(2)}) collective-permute-start(bf16[4,8320]{1,0:T(4,128)(2,1)S(1)} %collective-permute-done.2.refs_5_), channel_id=1, source_target_pairs={{0,2},{1,3},{2,0},{3,1},{4,6},{5,7},{6,4},{7,5},{8,10},{9,11},{10,... | collective-permute-start | bytes 199688 | tf_op jit(solution)/shard_map/ppermute | solution.py:18
  13.9 0.5 collective-permute-start.5
  14.5 2.2 %load.2 = (bf16[2,48,8192]{2,1,0:T(8,128)(2,1)S(1)}, bf16[1024,640]{1,0:T(8,128)(2,1)S(1)}, bf16[1024,640]{1,0:T(8,128)(2,1)S(1)}) custom-call(bf16[4,8320]{1,0:T(4,128)(2,1)S(1)} %collective-permute-done.refs_0_.refs_4_, bf16[8192,640]{1,0:T(8,128)(2,1)} %refs_3_.7, bf16[2,64,8192]{2,1,0:T(8,128)(2,1)} %bitcast.9), custom_call_target="tpu_custom_call" | custom-call | bytes 5242880 | tf_op jit(solution)/shard_map/load/pallas_call | solution.py:428
  16.7 0.0 collective-permute-done.6.refs_3_
  16.7 0.0 collective-permute-done.1.refs_0_
  16.7 0.7 collective-permute-done.3.refs_1_
  17.4 0.8 collective-permute-done.5.refs_2_
  18.2 0.1 pack.2.refs_2_.refs_3_.refs_0_
  18.3 0.1 collective-permute-start.7
  18.4 1.1 %down.2 = (bf16[24,128]{1,0:T(8,128)(2,1)S(1)}, bf16[2,16,8192]{2,1,0:T(8,128)(2,1)S(1)}) custom-call(bf16[2,48,8192]{2,1,0:T(8,128)(2,1)S(1)} %get-tuple-element.48.refs_0_, bf16[2,64,8192]{2,1,0:T(8,128)(2,1)S(1)} %bitcast.11, bf16[32,8320]{1,0:T(8,128)(2,1)S(1)} %pack.2.refs_2_.refs_3_.refs_0_, bf16[32,8320]{1,0:T(8,128)(2,1)S(1)} %pack.2.refs_2_.refs_3_.refs_0_), custom_call_target="tpu_custom_call" | custom-call | flops 100663296 | bytes 4194304 | tf_op jit(solution)/shard_map/down/pallas_call | solution.py:455
  19.5 1.1 %collective-permute-start.10 = (bf16[24,128]{1,0:T(8,128)(2,1)S(1)}, bf16[24,128]{1,0:T(8,128)(2,1)S(1)}, u32[]{:S(2)}, u32[]{:S(2)}) collective-permute-start(bf16[24,128]{1,0:T(8,128)(2,1)S(1)} %get-tuple-element.50.refs_4_), channel_id=1, source_target_pairs={{0,8},{1,9},{2,10},{3,11},{4,12},{5,13},{6,14},{7,15},{8,0},{9,1},... | collective-permute-start | bytes 18440 | tf_op jit(solution)/shard_map/ppermute | solution.py:18
  20.6 1.8 %collective-permute-start.11 = (bf16[24,128]{1,0:T(8,128)(2,1)S(1)}, bf16[24,128]{1,0:T(8,128)(2,1)S(1)}, u32[]{:S(2)}, u32[]{:S(2)}) collective-permute-start(bf16[24,128]{1,0:T(8,128)(2,1)S(1)} %get-tuple-element.50.refs_4_), channel_id=1, source_target_pairs={{0,12},{1,13},{2,14},{3,15},{4,8},{5,9},{6,10},{7,11},{8,4},{9,5},... | collective-permute-start | bytes 18440 | tf_op jit(solution)/shard_map/ppermute | solution.py:18
  22.4 0.7 collective-permute-start.9
  23.1 0.0 collective-permute-done.7.refs_1_
  23.1 2.7 %base.4.refs_4_ = f32[64,640]{1,0:T(8,128)S(1)} custom-call(bf16[32,8320]{1,0:T(8,128)(2,1)S(1)} %pack.2.refs_2_.refs_3_.refs_0_, bf16[32,8320]{1,0:T(8,128)(2,1)S(1)} %collective-permute-done.7.refs_1_, bf16[1024,640]{1,0:T(8,128)(2,1)S(1)} %get-tuple-element.51.refs_2_, bf16[8192,640]{1,0:T(8,128)(2,1)} %refs_3_.7, ...), custom_call_target="tpu_custom_call" | custom-call | flops 335544320 | bytes 10485760 | tf_op jit(solution)/shard_map/base/pallas_call | solution.py:478
  25.8 0.0 collective-permute-done.10
  25.8 0.3 collective-permute-done.11
  26.1 0.0 collective-permute-done.9
  26.1 0.0 copy-start.3
  26.1 0.1 collective-permute-start.12
  26.2 1.2 %collective-permute-start.13 = (bf16[24,128]{1,0:T(8,128)(2,1)S(1)}, bf16[24,128]{1,0:T(8,128)(2,1)S(1)}, u32[]{:S(2)}, u32[]{:S(2)}) collective-permute-start(bf16[24,128]{1,0:T(8,128)(2,1)S(1)} %add_add_fusion.1.refs_4_), channel_id=1, source_target_pairs={{0,2},{1,3},{2,0},{3,1},{4,6},{5,7},{6,4},{7,5},{8,10},{9,11},{10,... | collective-permute-start | bytes 18440 | tf_op jit(solution)/shard_map/ppermute | solution.py:18
  27.4 0.7 collective-permute-start.14
  28.1 2.9 %base.5.refs_5_ = f32[64,640]{1,0:T(8,128)S(1)} custom-call(bf16[32,8320]{1,0:T(8,128)(2,1)S(1)} %pack.2.refs_2_.refs_3_.refs_0_, bf16[32,8320]{1,0:T(8,128)(2,1)S(1)} %collective-permute-done.7.refs_1_, bf16[1024,640]{1,0:T(8,128)(2,1)S(1)} %get-tuple-element.55.refs_2_, bf16[8192,640]{1,0:T(8,128)(2,1)} %refs_3_.7, bf16[24,128]{1,0:T(8,128)(2,1)S(1)} %add_add_fusion.1.refs_4_), custom_call_target="tpu_custom_call" | custom-call | flops 335544320 | bytes 10485760 | tf_op jit(solution)/shard_map/base/pallas_call | solution.py:478
  30.9 0.0 copy-start.5
  31.0 0.0 collective-permute-done.13
  31.0 0.0 collective-permute-done.14
  31.0 0.7 lift.2
  31.7 11.3 %all_to_all.10 = bf16[16,4,640]{2,1,0:T(4,128)(2,1)S(1)} all-to-all(bf16[16,4,640]{2,1,0:T(4,128)(2,1)S(1)} %lift.2), channel_id=1, replica_groups=mesh['groups'=2,'tensor'=16] {'tensor'}, dimensions={0} | all-to-all | bytes 163840 | tf_op jit(solution)/shard_map/all_to_all | solution.py:22
  43.0 2.2 %attend.1.refs_7_ = bf16[4,8192]{1,0:T(4,128)(2,1)S(1)} custom-call(s32[4]{0:T(128)S(1)} %copy-done.5, bf16[4,10240]{1,0:T(4,128)(2,1)S(1)} %bitcast.12, bf16[4,8,384,128]{3,2,1,0:T(8,128)(2,1)S(1)} %copy-done.1, bf16[4,8,384,128]{3,2,1,0:T(8,128)(2,1)S(1)} %copy-done.2), custom_call_target="tpu_custom_call" | custom-call | flops 50331648 | bytes 6291456 | tf_op jit(solution)/shard_map/attend/pallas_call | solution.py:545
  45.1 0.7 collective-permute-start.15
  45.8 0.8 collective-permute-start.17
  46.6 3.0 %collective-permute-start.19 = (bf16[4,8192]{1,0:T(4,128)(2,1)S(1)}, bf16[4,8192]{1,0:T(4,128)(2,1)S(1)}, u32[]{:S(2)}, u32[]{:S(2)}) collective-permute-start(bf16[4,8192]{1,0:T(4,128)(2,1)S(1)} %attend.1.refs_7_), channel_id=1, source_target_pairs={{0,4},{1,5},{2,6},{3,7},{4,0},{5,1},{6,2},{7,3},{8,12},{9,13},{10,... | collective-permute-start | bytes 196616 | tf_op jit(solution)/shard_map/ppermute | solution.py:18
  49.6 2.4 %collective-permute-done.15.refs_0_.refs_4_ = bf16[4,8192]{1,0:T(4,128)(2,1)S(1)} collective-permute-done((bf16[4,8192]{1,0:T(4,128)(2,1)S(1)}, bf16[4,8192]{1,0:T(4,128)(2,1)S(1)}, u32[]{:S(2)}, u32[]{:S(2)}) %collective-permute-start.15) | collective-permute-done | bytes 65568 | tf_op jit(solution)/shard_map/ppermute | solution.py:18
  52.0 0.0 collective-permute-start.16
  52.0 1.3 %collective-permute-done.17.refs_5_ = bf16[4,8192]{1,0:T(4,128)(2,1)S(1)} collective-permute-done((bf16[4,8192]{1,0:T(4,128)(2,1)S(1)}, bf16[4,8192]{1,0:T(4,128)(2,1)S(1)}, u32[]{:S(2)}, u32[]{:S(2)}) %collective-permute-start.17) | collective-permute-done | bytes 65568 | tf_op jit(solution)/shard_map/ppermute | solution.py:18
  53.3 0.7 collective-permute-start.18
  54.0 0.0 collective-permute-done.19.refs_6_
  54.0 1.3 %collective-permute-start.20 = (bf16[4,8192]{1,0:T(4,128)(2,1)S(1)}, bf16[4,8192]{1,0:T(4,128)(2,1)S(1)}, u32[]{:S(2)}, u32[]{:S(2)}) collective-permute-start(bf16[4,8192]{1,0:T(4,128)(2,1)S(1)} %collective-permute-done.19.refs_6_), channel_id=1, source_target_pairs={{0,2},{1,3},{2,0},{3,1},{4,6},{5,7},{6,4},{7,5},{8,10},{9,11},{10,... | collective-permute-start | bytes 196616 | tf_op jit(solution)/shard_map/ppermute | solution.py:18
  55.3 2.0 %load.3 = (bf16[1024,512]{1,0:T(8,128)(2,1)S(1)}, bf16[2048,512]{1,0:T(8,128)(2,1)S(1)}) custom-call(bf16[4,8192]{1,0:T(4,128)(2,1)S(1)} %collective-permute-done.15.refs_0_.refs_4_, bf16[8192,512]{1,0:T(8,128)(2,1)} %refs_3_.10), custom_call_target="tpu_custom_call" | custom-call | bytes 6291456 | tf_op jit(solution)/shard_map/load/pallas_call | solution.py:428
  57.4 0.9 %collective-permute-done.18.refs_1_ = bf16[4,8192]{1,0:T(4,128)(2,1)S(1)} collective-permute-done((bf16[4,8192]{1,0:T(4,128)(2,1)S(1)}, bf16[4,8192]{1,0:T(4,128)(2,1)S(1)}, u32[]{:S(2)}, u32[]{:S(2)}) %collective-permute-start.18) | collective-permute-done | bytes 65568 | tf_op jit(solution)/shard_map/ppermute | solution.py:18
  58.2 0.8 collective-permute-done.20.refs_2_
  59.0 0.1 pack.3.refs_2_.refs_0_
  59.2 0.1 collective-permute-start.25
  59.3 0.5 down.3.refs_4_
  59.8 1.6 %collective-permute-start.23 = (bf16[8,128]{1,0:T(8,128)(2,1)S(1)}, bf16[8,128]{1,0:T(8,128)(2,1)S(1)}, u32[]{:S(2)}, u32[]{:S(2)}) collective-permute-start(bf16[8,128]{1,0:T(8,128)(2,1)S(1)} %down.3.refs_4_), channel_id=1, source_target_pairs={{0,8},{1,9},{2,10},{3,11},{4,12},{5,13},{6,14},{7,15},{8,0},{9,1},... | collective-permute-start | bytes 6152 | tf_op jit(solution)/shard_map/ppermute | solution.py:18
  61.5 2.8 %collective-permute-start.24 = (bf16[8,128]{1,0:T(8,128)(2,1)S(1)}, bf16[8,128]{1,0:T(8,128)(2,1)S(1)}, u32[]{:S(2)}, u32[]{:S(2)}) collective-permute-start(bf16[8,128]{1,0:T(8,128)(2,1)S(1)} %down.3.refs_4_), channel_id=1, source_target_pairs={{0,12},{1,13},{2,14},{3,15},{4,8},{5,9},{6,10},{7,11},{8,4},{9,5},... | collective-permute-start | bytes 6152 | tf_op jit(solution)/shard_map/ppermute | solution.py:18
  64.3 2.1 %base.6.refs_4_ = f32[64,512]{1,0:T(8,128)S(1)} custom-call(bf16[32,8192]{1,0:T(8,128)(2,1)S(1)} %pack.3.refs_2_.refs_0_, bf16[32,8192]{1,0:T(8,128)(2,1)S(1)} %collective-permute-done.25.refs_1_, bf16[1024,512]{1,0:T(8,128)(2,1)S(1)} %get-tuple-element.67.refs_2_, bf16[8192,512]{1,0:T(8,128)(2,1)} %refs_3_.10, bf16[8,128]{1,0:T(8,128)(2,1)S(1)} %down.3.refs_4_), custom_call_target="tpu_custom_call" | custom-call | flops 268435456 | bytes 8388608 | tf_op jit(solution)/shard_map/base/pallas_call | solution.py:478
  66.4 0.4 collective-permute-done.24
  66.8 0.1 collective-permute-start.26
  66.9 1.0 %collective-permute-start.27 = (bf16[8,128]{1,0:T(8,128)(2,1)S(1)}, bf16[8,128]{1,0:T(8,128)(2,1)S(1)}, u32[]{:S(2)}, u32[]{:S(2)}) collective-permute-start(bf16[8,128]{1,0:T(8,128)(2,1)S(1)} %add_add_fusion.3.refs_4_), channel_id=1, source_target_pairs={{0,2},{1,3},{2,0},{3,1},{4,6},{5,7},{6,4},{7,5},{8,10},{9,11},{10,... | collective-permute-start | bytes 6152 | tf_op jit(solution)/shard_map/ppermute | solution.py:18
  68.0 0.8 collective-permute-start.28
  68.8 1.8 %base.7.refs_5_ = f32[64,512]{1,0:T(8,128)S(1)} custom-call(bf16[32,8192]{1,0:T(8,128)(2,1)S(1)} %pack.3.refs_2_.refs_0_, bf16[32,8192]{1,0:T(8,128)(2,1)S(1)} %collective-permute-done.25.refs_1_, bf16[2048,512]{1,0:T(8,128)(2,1)S(1)} %get-tuple-element.71.refs_2_, bf16[8192,512]{1,0:T(8,128)(2,1)} %refs_3_.10, bf16[8,128]{1,0:T(8,128)(2,1)S(1)} %add_add_fusion.3.refs_4_), custom_call_target="tpu_custom_call" | custom-call | flops 268435456 | bytes 8388608 | tf_op jit(solution)/shard_map/base/pallas_call | solution.py:478
  70.6 0.4 collective-permute-done.28
  71.0 0.6 lift.3
  71.6 11.4 %all_to_all.11 = bf16[16,4,512]{2,1,0:T(4,128)(2,1)S(1)} all-to-all(bf16[16,4,512]{2,1,0:T(4,128)(2,1)S(1)} %lift.3), channel_id=1, replica_groups=mesh['groups'=2,'tensor'=16] {'tensor'}, dimensions={0} | all-to-all | bytes 131072 | tf_op jit(solution)/shard_map/all_to_all | solution.py:22
  83.0 0.6 copy.14
  (27 shorter events, 0.1 us)
Async XLA Ops:
  0.0 18.4 %collective-permute-start.8 = (bf16[2,8192,64]{1,2,0:T(8,128)(2,1)}, bf16[2,8192,64]{1,2,0:T(8,128)(2,1)S(1)}, u32[]{:S(2)}, u32[]{:S(2)}) collective-permute-start(bf16[2,8192,64]{1,2,0:T(8,128)(2,1)} %param.19), channel_id=1, source_target_pairs={{0,1},{1,0},{2,3},{3,2},{4,5},{5,4},{6,7},{7,6},{8,9},{9,8},{10,11... | collective-permute-start | bytes 6291464 | tf_op jit(solution)/shard_map/ppermute | solution.py:18
  1.5 7.7 %collective-permute-start = (bf16[4,8320]{1,0:T(4,128)(2,1)S(1)}, bf16[4,8320]{1,0:T(4,128)(2,1)S(1)}, u32[]{:S(2)}, u32[]{:S(2)}) collective-permute-start(bf16[4,8320]{1,0:T(4,128)(2,1)S(1)} %norm.1.refs_7_), channel_id=1, source_target_pairs={{0,12},{1,13},{2,14},{3,15},{4,8},{5,9},{6,10},{7,11},{8,4},{9,5},... | collective-permute-start | bytes 199688 | tf_op jit(solution)/shard_map/ppermute | solution.py:18
  6.2 6.2 %collective-permute-start.2 = (bf16[4,8320]{1,0:T(4,128)(2,1)S(1)}, bf16[4,8320]{1,0:T(4,128)(2,1)S(1)}, u32[]{:S(2)}, u32[]{:S(2)}) collective-permute-start(bf16[4,8320]{1,0:T(4,128)(2,1)S(1)} %norm.1.refs_7_), channel_id=1, source_target_pairs={{0,8},{1,9},{2,10},{3,11},{4,12},{5,13},{6,14},{7,15},{8,0},{9,1},... | collective-permute-start | bytes 199688 | tf_op jit(solution)/shard_map/ppermute | solution.py:18
  6.2 7.7 %collective-permute-start.4 = (bf16[4,8320]{1,0:T(4,128)(2,1)S(1)}, bf16[4,8320]{1,0:T(4,128)(2,1)S(1)}, u32[]{:S(2)}, u32[]{:S(2)}) collective-permute-start(bf16[4,8320]{1,0:T(4,128)(2,1)S(1)} %norm.1.refs_7_), channel_id=1, source_target_pairs={{0,4},{1,5},{2,6},{3,7},{4,0},{5,1},{6,2},{7,3},{8,12},{9,13},{10,... | collective-permute-start | bytes 199688 | tf_op jit(solution)/shard_map/ppermute | solution.py:18
  6.8 9.8 %collective-permute-start.6 = (bf16[4,8320]{1,0:T(4,128)(2,1)S(1)}, bf16[4,8320]{1,0:T(4,128)(2,1)S(1)}, u32[]{:S(2)}, u32[]{:S(2)}) collective-permute-start(bf16[4,8320]{1,0:T(4,128)(2,1)S(1)} %norm.1.refs_7_), channel_id=1, source_target_pairs={{0,2},{1,3},{2,0},{3,1},{4,6},{5,7},{6,4},{7,5},{8,10},{9,11},{10,... | collective-permute-start | bytes 199688 | tf_op jit(solution)/shard_map/ppermute | solution.py:18
  9.2 7.5 %collective-permute-start.1 = (bf16[4,8320]{1,0:T(4,128)(2,1)S(1)}, bf16[4,8320]{1,0:T(4,128)(2,1)S(1)}, u32[]{:S(2)}, u32[]{:S(2)}) collective-permute-start(bf16[4,8320]{1,0:T(4,128)(2,1)S(1)} %collective-permute-done.refs_0_.refs_4_), channel_id=1, source_target_pairs={{0,2},{1,3},{2,0},{3,1},{4,6},{5,7},{6,4},{7,5},{8,10},{9,11},{10,... | collective-permute-start | bytes 199688 | tf_op jit(solution)/shard_map/ppermute | solution.py:18
  12.4 5.0 %collective-permute-start.3 = (bf16[4,8320]{1,0:T(4,128)(2,1)S(1)}, bf16[4,8320]{1,0:T(4,128)(2,1)S(1)}, u32[]{:S(2)}, u32[]{:S(2)}) collective-permute-start(bf16[4,8320]{1,0:T(4,128)(2,1)S(1)} %collective-permute-done.2.refs_5_), channel_id=1, source_target_pairs={{0,2},{1,3},{2,0},{3,1},{4,6},{5,7},{6,4},{7,5},{8,10},{9,11},{10,... | collective-permute-start | bytes 199688 | tf_op jit(solution)/shard_map/ppermute | solution.py:18
  13.9 4.3 %collective-permute-start.5 = (bf16[4,8320]{1,0:T(4,128)(2,1)S(1)}, bf16[4,8320]{1,0:T(4,128)(2,1)S(1)}, u32[]{:S(2)}, u32[]{:S(2)}) collective-permute-start(bf16[4,8320]{1,0:T(4,128)(2,1)S(1)} %collective-permute-done.4.refs_6_), channel_id=1, source_target_pairs={{0,2},{1,3},{2,0},{3,1},{4,6},{5,7},{6,4},{7,5},{8,10},{9,11},{10,... | collective-permute-start | bytes 199688 | tf_op jit(solution)/shard_map/ppermute | solution.py:18
  18.3 4.7 %collective-permute-start.7 = (bf16[32,8320]{1,0:T(8,128)(2,1)S(1)}, bf16[32,8320]{1,0:T(8,128)(2,1)S(1)}, u32[]{:S(2)}, u32[]{:S(2)}) collective-permute-start(bf16[32,8320]{1,0:T(8,128)(2,1)S(1)} %pack.2.refs_2_.refs_3_.refs_0_), channel_id=1, source_target_pairs={{0,1},{1,0},{2,3},{3,2},{4,5},{5,4},{6,7},{7,6},{8,9},{9,8},{10,11... | collective-permute-start | bytes 1597448 | tf_op jit(solution)/shard_map/ppermute | solution.py:18
  19.5 6.3 %collective-permute-start.10 = (bf16[24,128]{1,0:T(8,128)(2,1)S(1)}, bf16[24,128]{1,0:T(8,128)(2,1)S(1)}, u32[]{:S(2)}, u32[]{:S(2)}) collective-permute-start(bf16[24,128]{1,0:T(8,128)(2,1)S(1)} %get-tuple-element.50.refs_4_), channel_id=1, source_target_pairs={{0,8},{1,9},{2,10},{3,11},{4,12},{5,13},{6,14},{7,15},{8,0},{9,1},... | collective-permute-start | bytes 18440 | tf_op jit(solution)/shard_map/ppermute | solution.py:18
  20.6 5.5 %collective-permute-start.11 = (bf16[24,128]{1,0:T(8,128)(2,1)S(1)}, bf16[24,128]{1,0:T(8,128)(2,1)S(1)}, u32[]{:S(2)}, u32[]{:S(2)}) collective-permute-start(bf16[24,128]{1,0:T(8,128)(2,1)S(1)} %get-tuple-element.50.refs_4_), channel_id=1, source_target_pairs={{0,12},{1,13},{2,14},{3,15},{4,8},{5,9},{6,10},{7,11},{8,4},{9,5},... | collective-permute-start | bytes 18440 | tf_op jit(solution)/shard_map/ppermute | solution.py:18
  22.4 3.7 %collective-permute-start.9 = (bf16[24,128]{1,0:T(8,128)(2,1)S(1)}, bf16[24,128]{1,0:T(8,128)(2,1)S(1)}, u32[]{:S(2)}, u32[]{:S(2)}) collective-permute-start(bf16[24,128]{1,0:T(8,128)(2,1)S(1)} %get-tuple-element.50.refs_4_), channel_id=1, source_target_pairs={{0,4},{1,5},{2,6},{3,7},{4,0},{5,1},{6,2},{7,3},{8,12},{9,13},{10,... | collective-permute-start | bytes 18440 | tf_op jit(solution)/shard_map/ppermute | solution.py:18
  26.1 4.9 %copy-start.3 = (bf16[32,16,640]{2,1,0:T(8,128)(2,1)S(1)}, bf16[32,16,640]{2,1,0:T(8,128)(2,1)}, u32[]{:S(2)}) copy-start(bf16[32,16,640]{2,1,0:T(8,128)(2,1)} %refs_3_.8) | copy-start | bytes 1966084
  26.1 4.8 %collective-permute-start.12 = (bf16[24,128]{1,0:T(8,128)(2,1)S(1)}, bf16[24,128]{1,0:T(8,128)(2,1)S(1)}, u32[]{:S(2)}, u32[]{:S(2)}) collective-permute-start(bf16[24,128]{1,0:T(8,128)(2,1)S(1)} %add_add_fusion.1.refs_4_), channel_id=1, source_target_pairs={{0,1},{1,0},{2,3},{3,2},{4,5},{5,4},{6,7},{7,6},{8,9},{9,8},{10,11... | collective-permute-start | bytes 18440 | tf_op jit(solution)/shard_map/ppermute | solution.py:18
  26.2 4.8 %collective-permute-start.13 = (bf16[24,128]{1,0:T(8,128)(2,1)S(1)}, bf16[24,128]{1,0:T(8,128)(2,1)S(1)}, u32[]{:S(2)}, u32[]{:S(2)}) collective-permute-start(bf16[24,128]{1,0:T(8,128)(2,1)S(1)} %add_add_fusion.1.refs_4_), channel_id=1, source_target_pairs={{0,2},{1,3},{2,0},{3,1},{4,6},{5,7},{6,4},{7,5},{8,10},{9,11},{10,... | collective-permute-start | bytes 18440 | tf_op jit(solution)/shard_map/ppermute | solution.py:18
  27.4 3.6 %collective-permute-start.14 = (bf16[24,128]{1,0:T(8,128)(2,1)S(1)}, bf16[24,128]{1,0:T(8,128)(2,1)S(1)}, u32[]{:S(2)}, u32[]{:S(2)}) collective-permute-start(bf16[24,128]{1,0:T(8,128)(2,1)S(1)} %add_add_fusion.1.refs_4_), channel_id=1, source_target_pairs={{0,3},{1,2},{2,1},{3,0},{4,7},{5,6},{6,5},{7,4},{8,11},{9,10},{10,... | collective-permute-start | bytes 18440 | tf_op jit(solution)/shard_map/ppermute | solution.py:18
  28.1 14.9 %copy-start.1 = (bf16[4,8,384,128]{3,2,1,0:T(8,128)(2,1)S(1)}, bf16[4,8,384,128]{3,2,1,0:T(8,128)(2,1)}, u32[]{:S(2)}) copy-start(bf16[4,8,384,128]{3,2,1,0:T(8,128)(2,1)} %keys_ref.1) | copy-start | bytes 9437188
  28.1 14.9 %copy-start.2 = (bf16[4,8,384,128]{3,2,1,0:T(8,128)(2,1)S(1)}, bf16[4,8,384,128]{3,2,1,0:T(8,128)(2,1)}, u32[]{:S(2)}) copy-start(bf16[4,8,384,128]{3,2,1,0:T(8,128)(2,1)} %values_ref.1) | copy-start | bytes 9437188
  30.9 12.0 %copy-start.5 = (s32[4]{0:T(128)S(1)}, s32[4]{0:T(128)}, u32[]{:S(2)}) copy-start(s32[4]{0:T(128)} %lengths_ref.1) | copy-start | bytes 52
  45.1 6.8 %collective-permute-start.15 = (bf16[4,8192]{1,0:T(4,128)(2,1)S(1)}, bf16[4,8192]{1,0:T(4,128)(2,1)S(1)}, u32[]{:S(2)}, u32[]{:S(2)}) collective-permute-start(bf16[4,8192]{1,0:T(4,128)(2,1)S(1)} %attend.1.refs_7_), channel_id=1, source_target_pairs={{0,12},{1,13},{2,14},{3,15},{4,8},{5,9},{6,10},{7,11},{8,4},{9,5},... | collective-permute-start | bytes 196616 | tf_op jit(solution)/shard_map/ppermute | solution.py:18
  45.8 7.5 %collective-permute-start.17 = (bf16[4,8192]{1,0:T(4,128)(2,1)S(1)}, bf16[4,8192]{1,0:T(4,128)(2,1)S(1)}, u32[]{:S(2)}, u32[]{:S(2)}) collective-permute-start(bf16[4,8192]{1,0:T(4,128)(2,1)S(1)} %attend.1.refs_7_), channel_id=1, source_target_pairs={{0,8},{1,9},{2,10},{3,11},{4,12},{5,13},{6,14},{7,15},{8,0},{9,1},... | collective-permute-start | bytes 196616 | tf_op jit(solution)/shard_map/ppermute | solution.py:18
  46.6 7.4 %collective-permute-start.19 = (bf16[4,8192]{1,0:T(4,128)(2,1)S(1)}, bf16[4,8192]{1,0:T(4,128)(2,1)S(1)}, u32[]{:S(2)}, u32[]{:S(2)}) collective-permute-start(bf16[4,8192]{1,0:T(4,128)(2,1)S(1)} %attend.1.refs_7_), channel_id=1, source_target_pairs={{0,4},{1,5},{2,6},{3,7},{4,0},{5,1},{6,2},{7,3},{8,12},{9,13},{10,... | collective-permute-start | bytes 196616 | tf_op jit(solution)/shard_map/ppermute | solution.py:18
  49.6 7.8 %collective-permute-start.21 = (bf16[4,8192]{1,0:T(4,128)(2,1)S(1)}, bf16[4,8192]{1,0:T(4,128)(2,1)S(1)}, u32[]{:S(2)}, u32[]{:S(2)}) collective-permute-start(bf16[4,8192]{1,0:T(4,128)(2,1)S(1)} %attend.1.refs_7_), channel_id=1, source_target_pairs={{0,2},{1,3},{2,0},{3,1},{4,6},{5,7},{6,4},{7,5},{8,10},{9,11},{10,... | collective-permute-start | bytes 196616 | tf_op jit(solution)/shard_map/ppermute | solution.py:18
  52.0 5.4 %collective-permute-start.16 = (bf16[4,8192]{1,0:T(4,128)(2,1)S(1)}, bf16[4,8192]{1,0:T(4,128)(2,1)S(1)}, u32[]{:S(2)}, u32[]{:S(2)}) collective-permute-start(bf16[4,8192]{1,0:T(4,128)(2,1)S(1)} %collective-permute-done.15.refs_0_.refs_4_), channel_id=1, source_target_pairs={{0,2},{1,3},{2,0},{3,1},{4,6},{5,7},{6,4},{7,5},{8,10},{9,11},{10,... | collective-permute-start | bytes 196616 | tf_op jit(solution)/shard_map/ppermute | solution.py:18
  53.3 5.0 %collective-permute-start.18 = (bf16[4,8192]{1,0:T(4,128)(2,1)S(1)}, bf16[4,8192]{1,0:T(4,128)(2,1)S(1)}, u32[]{:S(2)}, u32[]{:S(2)}) collective-permute-start(bf16[4,8192]{1,0:T(4,128)(2,1)S(1)} %collective-permute-done.17.refs_5_), channel_id=1, source_target_pairs={{0,2},{1,3},{2,0},{3,1},{4,6},{5,7},{6,4},{7,5},{8,10},{9,11},{10,... | collective-permute-start | bytes 196616 | tf_op jit(solution)/shard_map/ppermute | solution.py:18
  54.0 5.0 %collective-permute-start.20 = (bf16[4,8192]{1,0:T(4,128)(2,1)S(1)}, bf16[4,8192]{1,0:T(4,128)(2,1)S(1)}, u32[]{:S(2)}, u32[]{:S(2)}) collective-permute-start(bf16[4,8192]{1,0:T(4,128)(2,1)S(1)} %collective-permute-done.19.refs_6_), channel_id=1, source_target_pairs={{0,2},{1,3},{2,0},{3,1},{4,6},{5,7},{6,4},{7,5},{8,10},{9,11},{10,... | collective-permute-start | bytes 196616 | tf_op jit(solution)/shard_map/ppermute | solution.py:18
  55.3 3.9 %copy-start = (bf16[2,8192,64]{1,2,0:T(8,128)(2,1)S(1)}, bf16[2,8192,64]{1,2,0:T(8,128)(2,1)}, u32[]{:S(2)}) copy-start(bf16[2,8192,64]{1,2,0:T(8,128)(2,1)} %param.19) | copy-start | bytes 6291460
  59.2 5.1 %collective-permute-start.25 = (bf16[32,8192]{1,0:T(8,128)(2,1)S(1)}, bf16[32,8192]{1,0:T(8,128)(2,1)S(1)}, u32[]{:S(2)}, u32[]{:S(2)}) collective-permute-start(bf16[32,8192]{1,0:T(8,128)(2,1)S(1)} %pack.3.refs_2_.refs_0_), channel_id=1, source_target_pairs={{0,1},{1,0},{2,3},{3,2},{4,5},{5,4},{6,7},{7,6},{8,9},{9,8},{10,11... | collective-permute-start | bytes 1572872 | tf_op jit(solution)/shard_map/ppermute | solution.py:18
  59.8 6.6 %collective-permute-start.22 = (bf16[8,128]{1,0:T(8,128)(2,1)S(1)}, bf16[8,128]{1,0:T(8,128)(2,1)S(1)}, u32[]{:S(2)}, u32[]{:S(2)}) collective-permute-start(bf16[8,128]{1,0:T(8,128)(2,1)S(1)} %down.3.refs_4_), channel_id=1, source_target_pairs={{0,4},{1,5},{2,6},{3,7},{4,0},{5,1},{6,2},{7,3},{8,12},{9,13},{10,... | collective-permute-start | bytes 6152 | tf_op jit(solution)/shard_map/ppermute | solution.py:18
  59.8 6.6 %collective-permute-start.23 = (bf16[8,128]{1,0:T(8,128)(2,1)S(1)}, bf16[8,128]{1,0:T(8,128)(2,1)S(1)}, u32[]{:S(2)}, u32[]{:S(2)}) collective-permute-start(bf16[8,128]{1,0:T(8,128)(2,1)S(1)} %down.3.refs_4_), channel_id=1, source_target_pairs={{0,8},{1,9},{2,10},{3,11},{4,12},{5,13},{6,14},{7,15},{8,0},{9,1},... | collective-permute-start | bytes 6152 | tf_op jit(solution)/shard_map/ppermute | solution.py:18
  61.5 5.4 %collective-permute-start.24 = (bf16[8,128]{1,0:T(8,128)(2,1)S(1)}, bf16[8,128]{1,0:T(8,128)(2,1)S(1)}, u32[]{:S(2)}, u32[]{:S(2)}) collective-permute-start(bf16[8,128]{1,0:T(8,128)(2,1)S(1)} %down.3.refs_4_), channel_id=1, source_target_pairs={{0,12},{1,13},{2,14},{3,15},{4,8},{5,9},{6,10},{7,11},{8,4},{9,5},... | collective-permute-start | bytes 6152 | tf_op jit(solution)/shard_map/ppermute | solution.py:18
  66.8 4.2 %copy-start.4 = (bf16[32,16,512]{2,1,0:T(8,128)(2,1)S(1)}, bf16[32,16,512]{2,1,0:T(8,128)(2,1)}, u32[]{:S(2)}) copy-start(bf16[32,16,512]{2,1,0:T(8,128)(2,1)} %refs_3_.11) | copy-start | bytes 1572868
  66.8 3.7 %collective-permute-start.26 = (bf16[8,128]{1,0:T(8,128)(2,1)S(1)}, bf16[8,128]{1,0:T(8,128)(2,1)S(1)}, u32[]{:S(2)}, u32[]{:S(2)}) collective-permute-start(bf16[8,128]{1,0:T(8,128)(2,1)S(1)} %add_add_fusion.3.refs_4_), channel_id=1, source_target_pairs={{0,1},{1,0},{2,3},{3,2},{4,5},{5,4},{6,7},{7,6},{8,9},{9,8},{10,11... | collective-permute-start | bytes 6152 | tf_op jit(solution)/shard_map/ppermute | solution.py:18
  66.9 3.7 %collective-permute-start.27 = (bf16[8,128]{1,0:T(8,128)(2,1)S(1)}, bf16[8,128]{1,0:T(8,128)(2,1)S(1)}, u32[]{:S(2)}, u32[]{:S(2)}) collective-permute-start(bf16[8,128]{1,0:T(8,128)(2,1)S(1)} %add_add_fusion.3.refs_4_), channel_id=1, source_target_pairs={{0,2},{1,3},{2,0},{3,1},{4,6},{5,7},{6,4},{7,5},{8,10},{9,11},{10,... | collective-permute-start | bytes 6152 | tf_op jit(solution)/shard_map/ppermute | solution.py:18
  68.0 3.0 %collective-permute-start.28 = (bf16[8,128]{1,0:T(8,128)(2,1)S(1)}, bf16[8,128]{1,0:T(8,128)(2,1)S(1)}, u32[]{:S(2)}, u32[]{:S(2)}) collective-permute-start(bf16[8,128]{1,0:T(8,128)(2,1)S(1)} %add_add_fusion.3.refs_4_), channel_id=1, source_target_pairs={{0,3},{1,2},{2,1},{3,0},{4,7},{5,6},{6,5},{7,4},{8,11},{9,10},{10,... | collective-permute-start | bytes 6152 | tf_op jit(solution)/shard_map/ppermute | solution.py:18

commit v14 on v13

--- a/solution.py
+++ b/solution.py
@@ -66,9 +66,9 @@
     step = count // 4
     near, middle, far = (swap(x, count, k * step) for k in (1, 2, 3))
     step //= 2
-    across = [swap(p, count, step) for p in (x, near, middle, far)]
-    *across, loaded = lax.optimization_barrier((*across[::-1], beside(far)))
-    held = [pack([x, near, middle, far] + across[::-1])]
+    across = [swap(p, count, step) for p in (far, near, middle, x)]
+    *across, loaded = lax.optimization_barrier((*across, beside(far)))
+    held = [pack([x, near, middle, far] + [across[i] for i in (3, 1, 2, 0)])]
     step //= 2
     while step > 1:
         held = held + [swap(h, count, step) for h in held]
@@ -525,7 +525,7 @@
 
     bounds = (0, width, width + kv_width, width + 2 * kv_width)
     sibling_maps = jnp.swapaxes(swap(adapter_down, count, 1), 1, 2)
-    parts = ((0, 1024), (width // 2, 1024))
+    parts = ((0, 1024), (width // 2, 2048))
     column, tagged, (first_maps, *ready) = gather_rows(
         normed, count, lambda piece: load(piece, projection_weight, parts, own_maps)
     )

time: 83.9 us -> 82.6 us (0.985)
  waiting for transfers between devices: 10.4 us -> 8.97 us
    ppermute x29, waiting for transfers between devices: 10.4 us -> 8.97 us  [swap(): return lax.ppermute(x, AXIS, [(i, i ^ offset) for i in range(count)])]
  transfers between devices with their start and end apart: 29 -> 29, of which waited for: 11 -> 13; matrix products, arithmetic and copies ran while one was open for 0% -> 0% of each run, Pallas kernels for 20% -> 20%
where the time goes in v14:
time: 82.6 us; the launch traced here: 82.3 us
  starting transfers between devices  29.6 us (36%)
  blocking collectives  22.7 us (27%)
  Pallas kernels  20 us (24%)
  waiting for transfers between devices  8.97 us (11%)
    ppermute x29, starting transfers between devices, swap(): return lax.ppermute(x, AXIS, [(i, i ^ offset) for i in range(count)])  29.6 us
    all_to_all x2, blocking collectives, exchange(): lax.all_to_all(x, AXIS, split_axis=0, concat_axis=0, axis_index_groups=gr...  22.7 us
    pallas_call x4, Pallas kernels, base(): pl.pallas_call(functools.partial(base_kernel, len(pieces), start, length...  9.05 us
    ppermute x29, waiting for transfers between devices, swap(): return lax.ppermute(x, AXIS, [(i, i ^ offset) for i in range(count)])  8.97 us
    pallas_call x2, Pallas kernels, load(): pl.pallas_call(functools.partial(load_kernel, [start for start, _ in part...  4.51 us
    pallas_call x1, Pallas kernels, local(): pl.pallas_call(attend_kernel, out_shape=jax.ShapeDtypeStruct((rows, width...  2.17 us
  transfers between devices with their start and end apart: 29, of which 13 were waited for; matrix products, arithmetic and copies ran while one was open for 0% of the time, Pallas kernels for 20%

profile of v14, /device:TPU:0, one launch (start us, length us, event | category | flops | bytes accessed | tf_op | source)
XLA Modules:
  0.0 82.3 jit_solution(1209371703371265386)
XLA Ops:
  0.0 0.5 collective-permute-start.8
  0.5 1.1 %norm.1.refs_7_ = bf16[4,8320]{1,0:T(4,128)(2,1)S(1)} custom-call(bf16[4,8192]{1,0:T(4,128)(2,1)} %hidden_hbm.1, bf16[8192]{0:T(1024)(128)(2,1)} %gain_hbm.1, s32[4]{0:T(128)} %bitcast.14, s32[32]{0:T(128)} %slots_hbm.1), custom_call_target="tpu_custom_call" | custom-call | tf_op jit(solution)/shard_map/norm/pallas_call | solution.py:400
  1.5 4.7 %collective-permute-start = (bf16[4,8320]{1,0:T(4,128)(2,1)S(1)}, bf16[4,8320]{1,0:T(4,128)(2,1)S(1)}, u32[]{:S(2)}, u32[]{:S(2)}) collective-permute-start(bf16[4,8320]{1,0:T(4,128)(2,1)S(1)} %norm.1.refs_7_), channel_id=1, source_target_pairs={{0,12},{1,13},{2,14},{3,15},{4,8},{5,9},{6,10},{7,11},{8,4},{9,5},... | collective-permute-start | bytes 199688 | tf_op jit(solution)/shard_map/ppermute | solution.py:18
  6.2 0.6 collective-permute-start.4
  6.8 1.6 %collective-permute-start.6 = (bf16[4,8320]{1,0:T(4,128)(2,1)S(1)}, bf16[4,8320]{1,0:T(4,128)(2,1)S(1)}, u32[]{:S(2)}, u32[]{:S(2)}) collective-permute-start(bf16[4,8320]{1,0:T(4,128)(2,1)S(1)} %norm.1.refs_7_), channel_id=1, source_target_pairs={{0,2},{1,3},{2,0},{3,1},{4,6},{5,7},{6,4},{7,5},{8,10},{9,11},{10,... | collective-permute-start | bytes 199688 | tf_op jit(solution)/shard_map/ppermute | solution.py:18
  8.5 0.7 collective-permute-done.refs_0_.refs_4_
  9.2 1.6 %collective-permute-start.1 = (bf16[4,8320]{1,0:T(4,128)(2,1)S(1)}, bf16[4,8320]{1,0:T(4,128)(2,1)S(1)}, u32[]{:S(2)}, u32[]{:S(2)}) collective-permute-start(bf16[4,8320]{1,0:T(4,128)(2,1)S(1)} %collective-permute-done.refs_0_.refs_4_), channel_id=1, source_target_pairs={{0,2},{1,3},{2,0},{3,1},{4,6},{5,7},{6,4},{7,5},{8,10},{9,11},{10,... | collective-permute-start | bytes 199688 | tf_op jit(solution)/shard_map/ppermute | solution.py:18
  10.8 0.9 %collective-permute-done.2.refs_6_ = bf16[4,8320]{1,0:T(4,128)(2,1)S(1)} collective-permute-done((bf16[4,8320]{1,0:T(4,128)(2,1)S(1)}, bf16[4,8320]{1,0:T(4,128)(2,1)S(1)}, u32[]{:S(2)}, u32[]{:S(2)}) %collective-permute-start.2) | collective-permute-done | bytes 66592 | tf_op jit(solution)/shard_map/ppermute | solution.py:18
  11.8 1.6 %collective-permute-start.3 = (bf16[4,8320]{1,0:T(4,128)(2,1)S(1)}, bf16[4,8320]{1,0:T(4,128)(2,1)S(1)}, u32[]{:S(2)}, u32[]{:S(2)}) collective-permute-start(bf16[4,8320]{1,0:T(4,128)(2,1)S(1)} %collective-permute-done.2.refs_6_), channel_id=1, source_target_pairs={{0,2},{1,3},{2,0},{3,1},{4,6},{5,7},{6,4},{7,5},{8,10},{9,11},{10,... | collective-permute-start | bytes 199688 | tf_op jit(solution)/shard_map/ppermute | solution.py:18
  13.3 0.5 collective-permute-start.5
  13.8 2.6 %load.2 = (bf16[2,48,8192]{2,1,0:T(8,128)(2,1)S(1)}, bf16[1024,640]{1,0:T(8,128)(2,1)S(1)}, bf16[2048,640]{1,0:T(8,128)(2,1)S(1)}) custom-call(bf16[4,8320]{1,0:T(4,128)(2,1)S(1)} %collective-permute-done.refs_0_.refs_4_, bf16[8192,640]{1,0:T(8,128)(2,1)} %refs_3_.7, bf16[2,64,8192]{2,1,0:T(8,128)(2,1)} %bitcast.9), custom_call_target="tpu_custom_call" | custom-call | bytes 7864320 | tf_op jit(solution)/shard_map/load/pallas_call | solution.py:428
  16.5 0.0 collective-permute-done.1.refs_0_
  16.5 0.2 collective-permute-done.3.refs_2_
  16.6 1.0 %collective-permute-done.5.refs_1_ = bf16[4,8320]{1,0:T(4,128)(2,1)S(1)} collective-permute-done((bf16[4,8320]{1,0:T(4,128)(2,1)S(1)}, bf16[4,8320]{1,0:T(4,128)(2,1)S(1)}, u32[]{:S(2)}, u32[]{:S(2)}) %collective-permute-start.5) | collective-permute-done | bytes 66592 | tf_op jit(solution)/shard_map/ppermute | solution.py:18
  17.6 0.1 pack.2.refs_2_.refs_3_.refs_0_
  17.7 0.1 collective-permute-start.7
  17.8 0.0 collective-permute-done.8
  17.8 1.1 %down.2 = (bf16[24,128]{1,0:T(8,128)(2,1)S(1)}, bf16[2,16,8192]{2,1,0:T(8,128)(2,1)S(1)}) custom-call(bf16[2,48,8192]{2,1,0:T(8,128)(2,1)S(1)} %get-tuple-element.48.refs_0_, bf16[2,64,8192]{2,1,0:T(8,128)(2,1)S(1)} %bitcast.11, bf16[32,8320]{1,0:T(8,128)(2,1)S(1)} %pack.2.refs_2_.refs_3_.refs_0_, bf16[32,8320]{1,0:T(8,128)(2,1)S(1)} %pack.2.refs_2_.refs_3_.refs_0_), custom_call_target="tpu_custom_call" | custom-call | flops 100663296 | bytes 4194304 | tf_op jit(solution)/shard_map/down/pallas_call | solution.py:455
  18.9 1.2 %collective-permute-start.10 = (bf16[24,128]{1,0:T(8,128)(2,1)S(1)}, bf16[24,128]{1,0:T(8,128)(2,1)S(1)}, u32[]{:S(2)}, u32[]{:S(2)}) collective-permute-start(bf16[24,128]{1,0:T(8,128)(2,1)S(1)} %get-tuple-element.50.refs_4_), channel_id=1, source_target_pairs={{0,8},{1,9},{2,10},{3,11},{4,12},{5,13},{6,14},{7,15},{8,0},{9,1},... | collective-permute-start | bytes 18440 | tf_op jit(solution)/shard_map/ppermute | solution.py:18
  20.1 1.9 %collective-permute-start.11 = (bf16[24,128]{1,0:T(8,128)(2,1)S(1)}, bf16[24,128]{1,0:T(8,128)(2,1)S(1)}, u32[]{:S(2)}, u32[]{:S(2)}) collective-permute-start(bf16[24,128]{1,0:T(8,128)(2,1)S(1)} %get-tuple-element.50.refs_4_), channel_id=1, source_target_pairs={{0,12},{1,13},{2,14},{3,15},{4,8},{5,9},{6,10},{7,11},{8,4},{9,5},... | collective-permute-start | bytes 18440 | tf_op jit(solution)/shard_map/ppermute | solution.py:18
  22.1 0.4 collective-permute-start.9
  22.5 0.0 collective-permute-done.7.refs_1_
  22.5 2.7 %base.4.refs_4_ = f32[64,640]{1,0:T(8,128)S(1)} custom-call(bf16[32,8320]{1,0:T(8,128)(2,1)S(1)} %pack.2.refs_2_.refs_3_.refs_0_, bf16[32,8320]{1,0:T(8,128)(2,1)S(1)} %collective-permute-done.7.refs_1_, bf16[1024,640]{1,0:T(8,128)(2,1)S(1)} %get-tuple-element.51.refs_2_, bf16[8192,640]{1,0:T(8,128)(2,1)} %refs_3_.7, ...), custom_call_target="tpu_custom_call" | custom-call | flops 335544320 | bytes 10485760 | tf_op jit(solution)/shard_map/base/pallas_call | solution.py:478
  25.2 0.3 collective-permute-done.11
  25.6 0.1 collective-permute-done.9
  25.7 0.0 copy-start.3
  25.7 0.0 copy-start.5
  25.7 0.1 collective-permute-start.12
  25.8 1.4 %collective-permute-start.13 = (bf16[24,128]{1,0:T(8,128)(2,1)S(1)}, bf16[24,128]{1,0:T(8,128)(2,1)S(1)}, u32[]{:S(2)}, u32[]{:S(2)}) collective-permute-start(bf16[24,128]{1,0:T(8,128)(2,1)S(1)} %add_add_fusion.1.refs_4_), channel_id=1, source_target_pairs={{0,2},{1,3},{2,0},{3,1},{4,6},{5,7},{6,4},{7,5},{8,10},{9,11},{10,... | collective-permute-start | bytes 18440 | tf_op jit(solution)/shard_map/ppermute | solution.py:18
  27.2 0.4 collective-permute-start.14
  27.7 2.5 %base.5.refs_5_ = f32[64,640]{1,0:T(8,128)S(1)} custom-call(bf16[32,8320]{1,0:T(8,128)(2,1)S(1)} %pack.2.refs_2_.refs_3_.refs_0_, bf16[32,8320]{1,0:T(8,128)(2,1)S(1)} %collective-permute-done.7.refs_1_, bf16[2048,640]{1,0:T(8,128)(2,1)S(1)} %get-tuple-element.55.refs_2_, bf16[8192,640]{1,0:T(8,128)(2,1)} %refs_3_.7, bf16[24,128]{1,0:T(8,128)(2,1)S(1)} %add_add_fusion.1.refs_4_), custom_call_target="tpu_custom_call" | custom-call | flops 335544320 | bytes 10485760 | tf_op jit(solution)/shard_map/base/pallas_call | solution.py:478
  30.1 0.0 collective-permute-done.12
  30.2 0.1 collective-permute-done.14
  30.3 0.7 lift.2
  31.0 11.4 %all_to_all.10 = bf16[16,4,640]{2,1,0:T(4,128)(2,1)S(1)} all-to-all(bf16[16,4,640]{2,1,0:T(4,128)(2,1)S(1)} %lift.2), channel_id=1, replica_groups=mesh['groups'=2,'tensor'=16] {'tensor'}, dimensions={0} | all-to-all | bytes 163840 | tf_op jit(solution)/shard_map/all_to_all | solution.py:22
  42.4 2.2 %attend.1.refs_7_ = bf16[4,8192]{1,0:T(4,128)(2,1)S(1)} custom-call(s32[4]{0:T(128)S(1)} %copy-done.5, bf16[4,10240]{1,0:T(4,128)(2,1)S(1)} %bitcast.12, bf16[4,8,384,128]{3,2,1,0:T(8,128)(2,1)S(1)} %copy-done.1, bf16[4,8,384,128]{3,2,1,0:T(8,128)(2,1)S(1)} %copy-done.2), custom_call_target="tpu_custom_call" | custom-call | flops 50331648 | bytes 6291456 | tf_op jit(solution)/shard_map/attend/pallas_call | solution.py:545
  44.6 0.0 copy-start
  44.6 0.7 collective-permute-start.15
  45.2 0.1 collective-permute-start.17
  45.3 3.7 %collective-permute-start.19 = (bf16[4,8192]{1,0:T(4,128)(2,1)S(1)}, bf16[4,8192]{1,0:T(4,128)(2,1)S(1)}, u32[]{:S(2)}, u32[]{:S(2)}) collective-permute-start(bf16[4,8192]{1,0:T(4,128)(2,1)S(1)} %attend.1.refs_7_), channel_id=1, source_target_pairs={{0,8},{1,9},{2,10},{3,11},{4,12},{5,13},{6,14},{7,15},{8,0},{9,1},... | collective-permute-start | bytes 196616 | tf_op jit(solution)/shard_map/ppermute | solution.py:18
  49.0 2.4 %collective-permute-done.15.refs_0_.refs_4_ = bf16[4,8192]{1,0:T(4,128)(2,1)S(1)} collective-permute-done((bf16[4,8192]{1,0:T(4,128)(2,1)S(1)}, bf16[4,8192]{1,0:T(4,128)(2,1)S(1)}, u32[]{:S(2)}, u32[]{:S(2)}) %collective-permute-start.15) | collective-permute-done | bytes 65568 | tf_op jit(solution)/shard_map/ppermute | solution.py:18
  51.4 0.0 collective-permute-done.17.refs_6_
  51.4 2.0 %collective-permute-start.18 = (bf16[4,8192]{1,0:T(4,128)(2,1)S(1)}, bf16[4,8192]{1,0:T(4,128)(2,1)S(1)}, u32[]{:S(2)}, u32[]{:S(2)}) collective-permute-start(bf16[4,8192]{1,0:T(4,128)(2,1)S(1)} %collective-permute-done.17.refs_6_), channel_id=1, source_target_pairs={{0,2},{1,3},{2,0},{3,1},{4,6},{5,7},{6,4},{7,5},{8,10},{9,11},{10,... | collective-permute-start | bytes 196616 | tf_op jit(solution)/shard_map/ppermute | solution.py:18
  53.4 0.1 collective-permute-start.20
  53.5 1.9 %load.3 = (bf16[1024,512]{1,0:T(8,128)(2,1)S(1)}, bf16[2048,512]{1,0:T(8,128)(2,1)S(1)}) custom-call(bf16[4,8192]{1,0:T(4,128)(2,1)S(1)} %collective-permute-done.15.refs_0_.refs_4_, bf16[8192,512]{1,0:T(8,128)(2,1)} %refs_3_.10), custom_call_target="tpu_custom_call" | custom-call | bytes 6291456 | tf_op jit(solution)/shard_map/load/pallas_call | solution.py:428
  55.4 0.0 collective-permute-done.21.refs_3_
  55.4 0.3 collective-permute-done.16.refs_0_
  55.7 0.7 collective-permute-done.18.refs_2_
  56.4 1.3 %collective-permute-done.20.refs_1_ = bf16[4,8192]{1,0:T(4,128)(2,1)S(1)} collective-permute-done((bf16[4,8192]{1,0:T(4,128)(2,1)S(1)}, bf16[4,8192]{1,0:T(4,128)(2,1)S(1)}, u32[]{:S(2)}, u32[]{:S(2)}) %collective-permute-start.20) | collective-permute-done | bytes 65568 | tf_op jit(solution)/shard_map/ppermute | solution.py:18
  57.7 0.1 pack.3.refs_2_.refs_0_
  57.8 0.1 collective-permute-start.25
  57.9 0.5 down.3.refs_4_
  58.5 1.9 %collective-permute-start.23 = (bf16[8,128]{1,0:T(8,128)(2,1)S(1)}, bf16[8,128]{1,0:T(8,128)(2,1)S(1)}, u32[]{:S(2)}, u32[]{:S(2)}) collective-permute-start(bf16[8,128]{1,0:T(8,128)(2,1)S(1)} %down.3.refs_4_), channel_id=1, source_target_pairs={{0,8},{1,9},{2,10},{3,11},{4,12},{5,13},{6,14},{7,15},{8,0},{9,1},... | collective-permute-start | bytes 6152 | tf_op jit(solution)/shard_map/ppermute | solution.py:18
  60.4 2.6 %collective-permute-start.24 = (bf16[8,128]{1,0:T(8,128)(2,1)S(1)}, bf16[8,128]{1,0:T(8,128)(2,1)S(1)}, u32[]{:S(2)}, u32[]{:S(2)}) collective-permute-start(bf16[8,128]{1,0:T(8,128)(2,1)S(1)} %down.3.refs_4_), channel_id=1, source_target_pairs={{0,12},{1,13},{2,14},{3,15},{4,8},{5,9},{6,10},{7,11},{8,4},{9,5},... | collective-permute-start | bytes 6152 | tf_op jit(solution)/shard_map/ppermute | solution.py:18
  62.9 2.1 %base.6.refs_4_ = f32[64,512]{1,0:T(8,128)S(1)} custom-call(bf16[32,8192]{1,0:T(8,128)(2,1)S(1)} %pack.3.refs_2_.refs_0_, bf16[32,8192]{1,0:T(8,128)(2,1)S(1)} %collective-permute-done.25.refs_1_, bf16[1024,512]{1,0:T(8,128)(2,1)S(1)} %get-tuple-element.67.refs_2_, bf16[8192,512]{1,0:T(8,128)(2,1)} %refs_3_.10, bf16[8,128]{1,0:T(8,128)(2,1)S(1)} %down.3.refs_4_), custom_call_target="tpu_custom_call" | custom-call | flops 268435456 | bytes 8388608 | tf_op jit(solution)/shard_map/base/pallas_call | solution.py:478
  65.1 0.7 collective-permute-done.24
  65.8 0.1 collective-permute-start.26
  65.8 0.8 collective-permute-start.27
  66.6 1.1 %collective-permute-start.28 = (bf16[8,128]{1,0:T(8,128)(2,1)S(1)}, bf16[8,128]{1,0:T(8,128)(2,1)S(1)}, u32[]{:S(2)}, u32[]{:S(2)}) collective-permute-start(bf16[8,128]{1,0:T(8,128)(2,1)S(1)} %add_add_fusion.3.refs_4_), channel_id=1, source_target_pairs={{0,3},{1,2},{2,1},{3,0},{4,7},{5,6},{6,5},{7,4},{8,11},{9,10},{10,... | collective-permute-start | bytes 6152 | tf_op jit(solution)/shard_map/ppermute | solution.py:18
  67.7 1.8 %base.7.refs_5_ = f32[64,512]{1,0:T(8,128)S(1)} custom-call(bf16[32,8192]{1,0:T(8,128)(2,1)S(1)} %pack.3.refs_2_.refs_0_, bf16[32,8192]{1,0:T(8,128)(2,1)S(1)} %collective-permute-done.25.refs_1_, bf16[2048,512]{1,0:T(8,128)(2,1)S(1)} %get-tuple-element.71.refs_2_, bf16[8192,512]{1,0:T(8,128)(2,1)} %refs_3_.10, bf16[8,128]{1,0:T(8,128)(2,1)S(1)} %add_add_fusion.3.refs_4_), custom_call_target="tpu_custom_call" | custom-call | flops 268435456 | bytes 8388608 | tf_op jit(solution)/shard_map/base/pallas_call | solution.py:478
  69.5 0.1 collective-permute-done.28
  69.6 0.6 lift.3
  70.3 11.4 %all_to_all.11 = bf16[16,4,512]{2,1,0:T(4,128)(2,1)S(1)} all-to-all(bf16[16,4,512]{2,1,0:T(4,128)(2,1)S(1)} %lift.3), channel_id=1, replica_groups=mesh['groups'=2,'tensor'=16] {'tensor'}, dimensions={0} | all-to-all | bytes 131072 | tf_op jit(solution)/shard_map/all_to_all | solution.py:22
  81.7 0.6 copy.14
  (27 shorter events, 0.1 us)
Async XLA Ops:
  0.0 17.8 %collective-permute-start.8 = (bf16[2,8192,64]{1,2,0:T(8,128)(2,1)}, bf16[2,8192,64]{1,2,0:T(8,128)(2,1)S(1)}, u32[]{:S(2)}, u32[]{:S(2)}) collective-permute-start(bf16[2,8192,64]{1,2,0:T(8,128)(2,1)} %param.19), channel_id=1, source_target_pairs={{0,1},{1,0},{2,3},{3,2},{4,5},{5,4},{6,7},{7,6},{8,9},{9,8},{10,11... | collective-permute-start | bytes 6291464 | tf_op jit(solution)/shard_map/ppermute | solution.py:18
  1.5 7.7 %collective-permute-start = (bf16[4,8320]{1,0:T(4,128)(2,1)S(1)}, bf16[4,8320]{1,0:T(4,128)(2,1)S(1)}, u32[]{:S(2)}, u32[]{:S(2)}) collective-permute-start(bf16[4,8320]{1,0:T(4,128)(2,1)S(1)} %norm.1.refs_7_), channel_id=1, source_target_pairs={{0,12},{1,13},{2,14},{3,15},{4,8},{5,9},{6,10},{7,11},{8,4},{9,5},... | collective-permute-start | bytes 199688 | tf_op jit(solution)/shard_map/ppermute | solution.py:18
  6.2 5.6 %collective-permute-start.2 = (bf16[4,8320]{1,0:T(4,128)(2,1)S(1)}, bf16[4,8320]{1,0:T(4,128)(2,1)S(1)}, u32[]{:S(2)}, u32[]{:S(2)}) collective-permute-start(bf16[4,8320]{1,0:T(4,128)(2,1)S(1)} %norm.1.refs_7_), channel_id=1, source_target_pairs={{0,4},{1,5},{2,6},{3,7},{4,0},{5,1},{6,2},{7,3},{8,12},{9,13},{10,... | collective-permute-start | bytes 199688 | tf_op jit(solution)/shard_map/ppermute | solution.py:18
  6.2 7.1 %collective-permute-start.4 = (bf16[4,8320]{1,0:T(4,128)(2,1)S(1)}, bf16[4,8320]{1,0:T(4,128)(2,1)S(1)}, u32[]{:S(2)}, u32[]{:S(2)}) collective-permute-start(bf16[4,8320]{1,0:T(4,128)(2,1)S(1)} %norm.1.refs_7_), channel_id=1, source_target_pairs={{0,8},{1,9},{2,10},{3,11},{4,12},{5,13},{6,14},{7,15},{8,0},{9,1},... | collective-permute-start | bytes 199688 | tf_op jit(solution)/shard_map/ppermute | solution.py:18
  6.8 9.6 %collective-permute-start.6 = (bf16[4,8320]{1,0:T(4,128)(2,1)S(1)}, bf16[4,8320]{1,0:T(4,128)(2,1)S(1)}, u32[]{:S(2)}, u32[]{:S(2)}) collective-permute-start(bf16[4,8320]{1,0:T(4,128)(2,1)S(1)} %norm.1.refs_7_), channel_id=1, source_target_pairs={{0,2},{1,3},{2,0},{3,1},{4,6},{5,7},{6,4},{7,5},{8,10},{9,11},{10,... | collective-permute-start | bytes 199688 | tf_op jit(solution)/shard_map/ppermute | solution.py:18
  9.2 7.2 %collective-permute-start.1 = (bf16[4,8320]{1,0:T(4,128)(2,1)S(1)}, bf16[4,8320]{1,0:T(4,128)(2,1)S(1)}, u32[]{:S(2)}, u32[]{:S(2)}) collective-permute-start(bf16[4,8320]{1,0:T(4,128)(2,1)S(1)} %collective-permute-done.refs_0_.refs_4_), channel_id=1, source_target_pairs={{0,2},{1,3},{2,0},{3,1},{4,6},{5,7},{6,4},{7,5},{8,10},{9,11},{10,... | collective-permute-start | bytes 199688 | tf_op jit(solution)/shard_map/ppermute | solution.py:18
  11.8 4.9 %collective-permute-start.3 = (bf16[4,8320]{1,0:T(4,128)(2,1)S(1)}, bf16[4,8320]{1,0:T(4,128)(2,1)S(1)}, u32[]{:S(2)}, u32[]{:S(2)}) collective-permute-start(bf16[4,8320]{1,0:T(4,128)(2,1)S(1)} %collective-permute-done.2.refs_6_), channel_id=1, source_target_pairs={{0,2},{1,3},{2,0},{3,1},{4,6},{5,7},{6,4},{7,5},{8,10},{9,11},{10,... | collective-permute-start | bytes 199688 | tf_op jit(solution)/shard_map/ppermute | solution.py:18
  13.3 4.3 %collective-permute-start.5 = (bf16[4,8320]{1,0:T(4,128)(2,1)S(1)}, bf16[4,8320]{1,0:T(4,128)(2,1)S(1)}, u32[]{:S(2)}, u32[]{:S(2)}) collective-permute-start(bf16[4,8320]{1,0:T(4,128)(2,1)S(1)} %collective-permute-done.4.refs_5_), channel_id=1, source_target_pairs={{0,2},{1,3},{2,0},{3,1},{4,6},{5,7},{6,4},{7,5},{8,10},{9,11},{10,... | collective-permute-start | bytes 199688 | tf_op jit(solution)/shard_map/ppermute | solution.py:18
  17.7 4.7 %collective-permute-start.7 = (bf16[32,8320]{1,0:T(8,128)(2,1)S(1)}, bf16[32,8320]{1,0:T(8,128)(2,1)S(1)}, u32[]{:S(2)}, u32[]{:S(2)}) collective-permute-start(bf16[32,8320]{1,0:T(8,128)(2,1)S(1)} %pack.2.refs_2_.refs_3_.refs_0_), channel_id=1, source_target_pairs={{0,1},{1,0},{2,3},{3,2},{4,5},{5,4},{6,7},{7,6},{8,9},{9,8},{10,11... | collective-permute-start | bytes 1597448 | tf_op jit(solution)/shard_map/ppermute | solution.py:18
  18.9 6.3 %collective-permute-start.10 = (bf16[24,128]{1,0:T(8,128)(2,1)S(1)}, bf16[24,128]{1,0:T(8,128)(2,1)S(1)}, u32[]{:S(2)}, u32[]{:S(2)}) collective-permute-start(bf16[24,128]{1,0:T(8,128)(2,1)S(1)} %get-tuple-element.50.refs_4_), channel_id=1, source_target_pairs={{0,8},{1,9},{2,10},{3,11},{4,12},{5,13},{6,14},{7,15},{8,0},{9,1},... | collective-permute-start | bytes 18440 | tf_op jit(solution)/shard_map/ppermute | solution.py:18
  20.1 5.4 %collective-permute-start.11 = (bf16[24,128]{1,0:T(8,128)(2,1)S(1)}, bf16[24,128]{1,0:T(8,128)(2,1)S(1)}, u32[]{:S(2)}, u32[]{:S(2)}) collective-permute-start(bf16[24,128]{1,0:T(8,128)(2,1)S(1)} %get-tuple-element.50.refs_4_), channel_id=1, source_target_pairs={{0,12},{1,13},{2,14},{3,15},{4,8},{5,9},{6,10},{7,11},{8,4},{9,5},... | collective-permute-start | bytes 18440 | tf_op jit(solution)/shard_map/ppermute | solution.py:18
  22.1 3.6 %collective-permute-start.9 = (bf16[24,128]{1,0:T(8,128)(2,1)S(1)}, bf16[24,128]{1,0:T(8,128)(2,1)S(1)}, u32[]{:S(2)}, u32[]{:S(2)}) collective-permute-start(bf16[24,128]{1,0:T(8,128)(2,1)S(1)} %get-tuple-element.50.refs_4_), channel_id=1, source_target_pairs={{0,4},{1,5},{2,6},{3,7},{4,0},{5,1},{6,2},{7,3},{8,12},{9,13},{10,... | collective-permute-start | bytes 18440 | tf_op jit(solution)/shard_map/ppermute | solution.py:18
  25.7 4.6 %copy-start.3 = (bf16[32,16,640]{2,1,0:T(8,128)(2,1)S(1)}, bf16[32,16,640]{2,1,0:T(8,128)(2,1)}, u32[]{:S(2)}) copy-start(bf16[32,16,640]{2,1,0:T(8,128)(2,1)} %refs_3_.8) | copy-start | bytes 1966084
  25.7 16.7 %copy-start.5 = (s32[4]{0:T(128)S(1)}, s32[4]{0:T(128)}, u32[]{:S(2)}) copy-start(s32[4]{0:T(128)} %lengths_ref.1) | copy-start | bytes 52
  25.7 4.4 %collective-permute-start.12 = (bf16[24,128]{1,0:T(8,128)(2,1)S(1)}, bf16[24,128]{1,0:T(8,128)(2,1)S(1)}, u32[]{:S(2)}, u32[]{:S(2)}) collective-permute-start(bf16[24,128]{1,0:T(8,128)(2,1)S(1)} %add_add_fusion.1.refs_4_), channel_id=1, source_target_pairs={{0,1},{1,0},{2,3},{3,2},{4,5},{5,4},{6,7},{7,6},{8,9},{9,8},{10,11... | collective-permute-start | bytes 18440 | tf_op jit(solution)/shard_map/ppermute | solution.py:18
  25.8 4.3 %collective-permute-start.13 = (bf16[24,128]{1,0:T(8,128)(2,1)S(1)}, bf16[24,128]{1,0:T(8,128)(2,1)S(1)}, u32[]{:S(2)}, u32[]{:S(2)}) collective-permute-start(bf16[24,128]{1,0:T(8,128)(2,1)S(1)} %add_add_fusion.1.refs_4_), channel_id=1, source_target_pairs={{0,2},{1,3},{2,0},{3,1},{4,6},{5,7},{6,4},{7,5},{8,10},{9,11},{10,... | collective-permute-start | bytes 18440 | tf_op jit(solution)/shard_map/ppermute | solution.py:18
  27.2 3.1 %collective-permute-start.14 = (bf16[24,128]{1,0:T(8,128)(2,1)S(1)}, bf16[24,128]{1,0:T(8,128)(2,1)S(1)}, u32[]{:S(2)}, u32[]{:S(2)}) collective-permute-start(bf16[24,128]{1,0:T(8,128)(2,1)S(1)} %add_add_fusion.1.refs_4_), channel_id=1, source_target_pairs={{0,3},{1,2},{2,1},{3,0},{4,7},{5,6},{6,5},{7,4},{8,11},{9,10},{10,... | collective-permute-start | bytes 18440 | tf_op jit(solution)/shard_map/ppermute | solution.py:18
  27.7 14.7 %copy-start.1 = (bf16[4,8,384,128]{3,2,1,0:T(8,128)(2,1)S(1)}, bf16[4,8,384,128]{3,2,1,0:T(8,128)(2,1)}, u32[]{:S(2)}) copy-start(bf16[4,8,384,128]{3,2,1,0:T(8,128)(2,1)} %keys_ref.1) | copy-start | bytes 9437188
  27.7 14.7 %copy-start.2 = (bf16[4,8,384,128]{3,2,1,0:T(8,128)(2,1)S(1)}, bf16[4,8,384,128]{3,2,1,0:T(8,128)(2,1)}, u32[]{:S(2)}) copy-start(bf16[4,8,384,128]{3,2,1,0:T(8,128)(2,1)} %values_ref.1) | copy-start | bytes 9437188
  44.6 13.4 %copy-start = (bf16[2,8192,64]{1,2,0:T(8,128)(2,1)S(1)}, bf16[2,8192,64]{1,2,0:T(8,128)(2,1)}, u32[]{:S(2)}) copy-start(bf16[2,8192,64]{1,2,0:T(8,128)(2,1)} %param.19) | copy-start | bytes 6291460
  44.6 6.8 %collective-permute-start.15 = (bf16[4,8192]{1,0:T(4,128)(2,1)S(1)}, bf16[4,8192]{1,0:T(4,128)(2,1)S(1)}, u32[]{:S(2)}, u32[]{:S(2)}) collective-permute-start(bf16[4,8192]{1,0:T(4,128)(2,1)S(1)} %attend.1.refs_7_), channel_id=1, source_target_pairs={{0,12},{1,13},{2,14},{3,15},{4,8},{5,9},{6,10},{7,11},{8,4},{9,5},... | collective-permute-start | bytes 196616 | tf_op jit(solution)/shard_map/ppermute | solution.py:18
  45.2 6.2 %collective-permute-start.17 = (bf16[4,8192]{1,0:T(4,128)(2,1)S(1)}, bf16[4,8192]{1,0:T(4,128)(2,1)S(1)}, u32[]{:S(2)}, u32[]{:S(2)}) collective-permute-start(bf16[4,8192]{1,0:T(4,128)(2,1)S(1)} %attend.1.refs_7_), channel_id=1, source_target_pairs={{0,4},{1,5},{2,6},{3,7},{4,0},{5,1},{6,2},{7,3},{8,12},{9,13},{10,... | collective-permute-start | bytes 196616 | tf_op jit(solution)/shard_map/ppermute | solution.py:18
  45.3 8.1 %collective-permute-start.19 = (bf16[4,8192]{1,0:T(4,128)(2,1)S(1)}, bf16[4,8192]{1,0:T(4,128)(2,1)S(1)}, u32[]{:S(2)}, u32[]{:S(2)}) collective-permute-start(bf16[4,8192]{1,0:T(4,128)(2,1)S(1)} %attend.1.refs_7_), channel_id=1, source_target_pairs={{0,8},{1,9},{2,10},{3,11},{4,12},{5,13},{6,14},{7,15},{8,0},{9,1},... | collective-permute-start | bytes 196616 | tf_op jit(solution)/shard_map/ppermute | solution.py:18
  49.0 6.4 %collective-permute-start.21 = (bf16[4,8192]{1,0:T(4,128)(2,1)S(1)}, bf16[4,8192]{1,0:T(4,128)(2,1)S(1)}, u32[]{:S(2)}, u32[]{:S(2)}) collective-permute-start(bf16[4,8192]{1,0:T(4,128)(2,1)S(1)} %attend.1.refs_7_), channel_id=1, source_target_pairs={{0,2},{1,3},{2,0},{3,1},{4,6},{5,7},{6,4},{7,5},{8,10},{9,11},{10,... | collective-permute-start | bytes 196616 | tf_op jit(solution)/shard_map/ppermute | solution.py:18
  51.4 4.3 %collective-permute-start.16 = (bf16[4,8192]{1,0:T(4,128)(2,1)S(1)}, bf16[4,8192]{1,0:T(4,128)(2,1)S(1)}, u32[]{:S(2)}, u32[]{:S(2)}) collective-permute-start(bf16[4,8192]{1,0:T(4,128)(2,1)S(1)} %collective-permute-done.15.refs_0_.refs_4_), channel_id=1, source_target_pairs={{0,2},{1,3},{2,0},{3,1},{4,6},{5,7},{6,4},{7,5},{8,10},{9,11},{10,... | collective-permute-start | bytes 196616 | tf_op jit(solution)/shard_map/ppermute | solution.py:18
  51.4 5.0 %collective-permute-start.18 = (bf16[4,8192]{1,0:T(4,128)(2,1)S(1)}, bf16[4,8192]{1,0:T(4,128)(2,1)S(1)}, u32[]{:S(2)}, u32[]{:S(2)}) collective-permute-start(bf16[4,8192]{1,0:T(4,128)(2,1)S(1)} %collective-permute-done.17.refs_6_), channel_id=1, source_target_pairs={{0,2},{1,3},{2,0},{3,1},{4,6},{5,7},{6,4},{7,5},{8,10},{9,11},{10,... | collective-permute-start | bytes 196616 | tf_op jit(solution)/shard_map/ppermute | solution.py:18
  53.4 4.3 %collective-permute-start.20 = (bf16[4,8192]{1,0:T(4,128)(2,1)S(1)}, bf16[4,8192]{1,0:T(4,128)(2,1)S(1)}, u32[]{:S(2)}, u32[]{:S(2)}) collective-permute-start(bf16[4,8192]{1,0:T(4,128)(2,1)S(1)} %collective-permute-done.19.refs_5_), channel_id=1, source_target_pairs={{0,2},{1,3},{2,0},{3,1},{4,6},{5,7},{6,4},{7,5},{8,10},{9,11},{10,... | collective-permute-start | bytes 196616 | tf_op jit(solution)/shard_map/ppermute | solution.py:18
  57.8 5.1 %collective-permute-start.25 = (bf16[32,8192]{1,0:T(8,128)(2,1)S(1)}, bf16[32,8192]{1,0:T(8,128)(2,1)S(1)}, u32[]{:S(2)}, u32[]{:S(2)}) collective-permute-start(bf16[32,8192]{1,0:T(8,128)(2,1)S(1)} %pack.3.refs_2_.refs_0_), channel_id=1, source_target_pairs={{0,1},{1,0},{2,3},{3,2},{4,5},{5,4},{6,7},{7,6},{8,9},{9,8},{10,11... | collective-permute-start | bytes 1572872 | tf_op jit(solution)/shard_map/ppermute | solution.py:18
  58.5 6.6 %collective-permute-start.22 = (bf16[8,128]{1,0:T(8,128)(2,1)S(1)}, bf16[8,128]{1,0:T(8,128)(2,1)S(1)}, u32[]{:S(2)}, u32[]{:S(2)}) collective-permute-start(bf16[8,128]{1,0:T(8,128)(2,1)S(1)} %down.3.refs_4_), channel_id=1, source_target_pairs={{0,4},{1,5},{2,6},{3,7},{4,0},{5,1},{6,2},{7,3},{8,12},{9,13},{10,... | collective-permute-start | bytes 6152 | tf_op jit(solution)/shard_map/ppermute | solution.py:18
  58.5 6.6 %collective-permute-start.23 = (bf16[8,128]{1,0:T(8,128)(2,1)S(1)}, bf16[8,128]{1,0:T(8,128)(2,1)S(1)}, u32[]{:S(2)}, u32[]{:S(2)}) collective-permute-start(bf16[8,128]{1,0:T(8,128)(2,1)S(1)} %down.3.refs_4_), channel_id=1, source_target_pairs={{0,8},{1,9},{2,10},{3,11},{4,12},{5,13},{6,14},{7,15},{8,0},{9,1},... | collective-permute-start | bytes 6152 | tf_op jit(solution)/shard_map/ppermute | solution.py:18
  60.4 5.4 %collective-permute-start.24 = (bf16[8,128]{1,0:T(8,128)(2,1)S(1)}, bf16[8,128]{1,0:T(8,128)(2,1)S(1)}, u32[]{:S(2)}, u32[]{:S(2)}) collective-permute-start(bf16[8,128]{1,0:T(8,128)(2,1)S(1)} %down.3.refs_4_), channel_id=1, source_target_pairs={{0,12},{1,13},{2,14},{3,15},{4,8},{5,9},{6,10},{7,11},{8,4},{9,5},... | collective-permute-start | bytes 6152 | tf_op jit(solution)/shard_map/ppermute | solution.py:18
  65.8 3.9 %copy-start.4 = (bf16[32,16,512]{2,1,0:T(8,128)(2,1)S(1)}, bf16[32,16,512]{2,1,0:T(8,128)(2,1)}, u32[]{:S(2)}) copy-start(bf16[32,16,512]{2,1,0:T(8,128)(2,1)} %refs_3_.11) | copy-start | bytes 1572868
  65.8 3.7 %collective-permute-start.26 = (bf16[8,128]{1,0:T(8,128)(2,1)S(1)}, bf16[8,128]{1,0:T(8,128)(2,1)S(1)}, u32[]{:S(2)}, u32[]{:S(2)}) collective-permute-start(bf16[8,128]{1,0:T(8,128)(2,1)S(1)} %add_add_fusion.3.refs_4_), channel_id=1, source_target_pairs={{0,1},{1,0},{2,3},{3,2},{4,5},{5,4},{6,7},{7,6},{8,9},{9,8},{10,11... | collective-permute-start | bytes 6152 | tf_op jit(solution)/shard_map/ppermute | solution.py:18
  65.8 3.7 %collective-permute-start.27 = (bf16[8,128]{1,0:T(8,128)(2,1)S(1)}, bf16[8,128]{1,0:T(8,128)(2,1)S(1)}, u32[]{:S(2)}, u32[]{:S(2)}) collective-permute-start(bf16[8,128]{1,0:T(8,128)(2,1)S(1)} %add_add_fusion.3.refs_4_), channel_id=1, source_target_pairs={{0,2},{1,3},{2,0},{3,1},{4,6},{5,7},{6,4},{7,5},{8,10},{9,11},{10,... | collective-permute-start | bytes 6152 | tf_op jit(solution)/shard_map/ppermute | solution.py:18
  66.6 3.0 %collective-permute-start.28 = (bf16[8,128]{1,0:T(8,128)(2,1)S(1)}, bf16[8,128]{1,0:T(8,128)(2,1)S(1)}, u32[]{:S(2)}, u32[]{:S(2)}) collective-permute-start(bf16[8,128]{1,0:T(8,128)(2,1)S(1)} %add_add_fusion.3.refs_4_), channel_id=1, source_target_pairs={{0,3},{1,2},{2,1},{3,0},{4,7},{5,6},{6,5},{7,4},{8,11},{9,10},{10,... | collective-permute-start | bytes 6152 | tf_op jit(solution)/shard_map/ppermute | solution.py:18

commit v15 on v14

--- a/solution.py
+++ b/solution.py
@@ -352,8 +352,9 @@
         weights = jnp.exp(scores - peak)
         own_weight = jnp.exp(own - peak)
         denominator = jnp.sum(weights, axis=0, keepdims=True) + own_weight
-        probs = (weights / denominator).T.astype(jnp.bfloat16)
-        own_prob = (own_weight / denominator).astype(jnp.bfloat16).astype(jnp.float32)
+        share = 1.0 / denominator
+        probs = (weights * share).T.astype(jnp.bfloat16)
+        own_prob = (own_weight * share).astype(jnp.bfloat16).astype(jnp.float32)
         steps[i] = (first, probs, jnp.broadcast_to(own_prob, (dim, lanes)).T * value)
 
     for first, probs, own_term in steps:
@@ -525,7 +526,7 @@
 
     bounds = (0, width, width + kv_width, width + 2 * kv_width)
     sibling_maps = jnp.swapaxes(swap(adapter_down, count, 1), 1, 2)
-    parts = ((0, 1024), (width // 2, 2048))
+    parts = ((0, 2048), (width // 2, 2048))
     column, tagged, (first_maps, *ready) = gather_rows(
         normed, count, lambda piece: load(piece, projection_weight, parts, own_maps)
     )

time: 82.6 us -> 82.6 us (level)
  transfers between devices with their start and end apart: 29 -> 29, of which waited for: 13 -> 10; matrix products, arithmetic and copies ran while one was open for 0% -> 0% of each run, Pallas kernels for 20% -> 20%
where the time goes in v15:
time: 82.6 us; the launch traced here: 82.2 us
  starting transfers between devices  29.6 us (36%)
  blocking collectives  22.7 us (27%)
  Pallas kernels  19.9 us (24%)
  waiting for transfers between devices  9.01 us (11%)
    ppermute x29, starting transfers between devices, swap(): return lax.ppermute(x, AXIS, [(i, i ^ offset) for i in range(count)])  29.6 us
    all_to_all x2, blocking collectives, exchange(): lax.all_to_all(x, AXIS, split_axis=0, concat_axis=0, axis_index_groups=gr...  22.7 us
    ppermute x29, waiting for transfers between devices, swap(): return lax.ppermute(x, AXIS, [(i, i ^ offset) for i in range(count)])  9.01 us
    pallas_call x4, Pallas kernels, base(): pl.pallas_call(functools.partial(base_kernel, len(pieces), start, length...  8.64 us
    pallas_call x2, Pallas kernels, load(): pl.pallas_call(functools.partial(load_kernel, [start for start, _ in part...  4.91 us
    pallas_call x1, Pallas kernels, local(): pl.pallas_call(attend_kernel, out_shape=jax.ShapeDtypeStruct((rows, width...  2.16 us
  transfers between devices with their start and end apart: 29, of which 10 were waited for; matrix products, arithmetic and copies ran while one was open for 0% of the time, Pallas kernels for 20%

profile of v15, /device:TPU:0, one launch (start us, length us, event | category | flops | bytes accessed | tf_op | source)
XLA Modules:
  0.0 82.2 jit_solution(3131995262049123895)
XLA Ops:
  0.0 0.5 collective-permute-start.8
  0.5 1.1 %norm.1.refs_7_ = bf16[4,8320]{1,0:T(4,128)(2,1)S(1)} custom-call(bf16[4,8192]{1,0:T(4,128)(2,1)} %hidden_hbm.1, bf16[8192]{0:T(1024)(128)(2,1)} %gain_hbm.1, s32[4]{0:T(128)} %bitcast.14, s32[32]{0:T(128)} %slots_hbm.1), custom_call_target="tpu_custom_call" | custom-call | tf_op jit(solution)/shard_map/norm/pallas_call | solution.py:401
  1.5 4.7 %collective-permute-start = (bf16[4,8320]{1,0:T(4,128)(2,1)S(1)}, bf16[4,8320]{1,0:T(4,128)(2,1)S(1)}, u32[]{:S(2)}, u32[]{:S(2)}) collective-permute-start(bf16[4,8320]{1,0:T(4,128)(2,1)S(1)} %norm.1.refs_7_), channel_id=1, source_target_pairs={{0,12},{1,13},{2,14},{3,15},{4,8},{5,9},{6,10},{7,11},{8,4},{9,5},... | collective-permute-start | bytes 199688 | tf_op jit(solution)/shard_map/ppermute | solution.py:18
  6.2 0.6 collective-permute-start.4
  6.8 1.6 %collective-permute-start.6 = (bf16[4,8320]{1,0:T(4,128)(2,1)S(1)}, bf16[4,8320]{1,0:T(4,128)(2,1)S(1)}, u32[]{:S(2)}, u32[]{:S(2)}) collective-permute-start(bf16[4,8320]{1,0:T(4,128)(2,1)S(1)} %norm.1.refs_7_), channel_id=1, source_target_pairs={{0,2},{1,3},{2,0},{3,1},{4,6},{5,7},{6,4},{7,5},{8,10},{9,11},{10,... | collective-permute-start | bytes 199688 | tf_op jit(solution)/shard_map/ppermute | solution.py:18
  8.5 0.7 collective-permute-done.refs_0_.refs_4_
  9.2 1.6 %collective-permute-start.1 = (bf16[4,8320]{1,0:T(4,128)(2,1)S(1)}, bf16[4,8320]{1,0:T(4,128)(2,1)S(1)}, u32[]{:S(2)}, u32[]{:S(2)}) collective-permute-start(bf16[4,8320]{1,0:T(4,128)(2,1)S(1)} %collective-permute-done.refs_0_.refs_4_), channel_id=1, source_target_pairs={{0,2},{1,3},{2,0},{3,1},{4,6},{5,7},{6,4},{7,5},{8,10},{9,11},{10,... | collective-permute-start | bytes 199688 | tf_op jit(solution)/shard_map/ppermute | solution.py:18
  10.8 0.9 %collective-permute-done.2.refs_6_ = bf16[4,8320]{1,0:T(4,128)(2,1)S(1)} collective-permute-done((bf16[4,8320]{1,0:T(4,128)(2,1)S(1)}, bf16[4,8320]{1,0:T(4,128)(2,1)S(1)}, u32[]{:S(2)}, u32[]{:S(2)}) %collective-permute-start.2) | collective-permute-done | bytes 66592 | tf_op jit(solution)/shard_map/ppermute | solution.py:18
  11.8 1.6 %collective-permute-start.3 = (bf16[4,8320]{1,0:T(4,128)(2,1)S(1)}, bf16[4,8320]{1,0:T(4,128)(2,1)S(1)}, u32[]{:S(2)}, u32[]{:S(2)}) collective-permute-start(bf16[4,8320]{1,0:T(4,128)(2,1)S(1)} %collective-permute-done.2.refs_6_), channel_id=1, source_target_pairs={{0,2},{1,3},{2,0},{3,1},{4,6},{5,7},{6,4},{7,5},{8,10},{9,11},{10,... | collective-permute-start | bytes 199688 | tf_op jit(solution)/shard_map/ppermute | solution.py:18
  13.3 0.5 collective-permute-start.5
  13.8 3.0 %load.2 = (bf16[2,48,8192]{2,1,0:T(8,128)(2,1)S(1)}, bf16[2048,640]{1,0:T(8,128)(2,1)S(1)}, bf16[2048,640]{1,0:T(8,128)(2,1)S(1)}) custom-call(bf16[4,8320]{1,0:T(4,128)(2,1)S(1)} %collective-permute-done.refs_0_.refs_4_, bf16[8192,640]{1,0:T(8,128)(2,1)} %refs_3_.7, bf16[2,64,8192]{2,1,0:T(8,128)(2,1)} %bitcast.9), custom_call_target="tpu_custom_call" | custom-call | bytes 10485760 | tf_op jit(solution)/shard_map/load/pallas_call | solution.py:429
  16.8 0.0 collective-permute-done.6.refs_3_
  16.9 0.0 collective-permute-done.3.refs_2_
  16.9 0.7 collective-permute-done.5.refs_1_
  17.6 0.1 pack.2.refs_2_.refs_3_.refs_0_
  17.7 0.1 collective-permute-start.7
  17.8 1.1 %down.2 = (bf16[24,128]{1,0:T(8,128)(2,1)S(1)}, bf16[2,16,8192]{2,1,0:T(8,128)(2,1)S(1)}) custom-call(bf16[2,48,8192]{2,1,0:T(8,128)(2,1)S(1)} %get-tuple-element.48.refs_0_, bf16[2,64,8192]{2,1,0:T(8,128)(2,1)S(1)} %bitcast.11, bf16[32,8320]{1,0:T(8,128)(2,1)S(1)} %pack.2.refs_2_.refs_3_.refs_0_, bf16[32,8320]{1,0:T(8,128)(2,1)S(1)} %pack.2.refs_2_.refs_3_.refs_0_), custom_call_target="tpu_custom_call" | custom-call | flops 100663296 | bytes 4194304 | tf_op jit(solution)/shard_map/down/pallas_call | solution.py:456
  18.9 1.5 %collective-permute-start.10 = (bf16[24,128]{1,0:T(8,128)(2,1)S(1)}, bf16[24,128]{1,0:T(8,128)(2,1)S(1)}, u32[]{:S(2)}, u32[]{:S(2)}) collective-permute-start(bf16[24,128]{1,0:T(8,128)(2,1)S(1)} %get-tuple-element.50.refs_4_), channel_id=1, source_target_pairs={{0,8},{1,9},{2,10},{3,11},{4,12},{5,13},{6,14},{7,15},{8,0},{9,1},... | collective-permute-start | bytes 18440 | tf_op jit(solution)/shard_map/ppermute | solution.py:18
  20.4 1.6 %collective-permute-start.11 = (bf16[24,128]{1,0:T(8,128)(2,1)S(1)}, bf16[24,128]{1,0:T(8,128)(2,1)S(1)}, u32[]{:S(2)}, u32[]{:S(2)}) collective-permute-start(bf16[24,128]{1,0:T(8,128)(2,1)S(1)} %get-tuple-element.50.refs_4_), channel_id=1, source_target_pairs={{0,12},{1,13},{2,14},{3,15},{4,8},{5,9},{6,10},{7,11},{8,4},{9,5},... | collective-permute-start | bytes 18440 | tf_op jit(solution)/shard_map/ppermute | solution.py:18
  22.0 0.4 collective-permute-start.9
  22.5 2.3 %base.4.refs_4_ = f32[64,640]{1,0:T(8,128)S(1)} custom-call(bf16[32,8320]{1,0:T(8,128)(2,1)S(1)} %pack.2.refs_2_.refs_3_.refs_0_, bf16[32,8320]{1,0:T(8,128)(2,1)S(1)} %collective-permute-done.7.refs_1_, bf16[2048,640]{1,0:T(8,128)(2,1)S(1)} %get-tuple-element.51.refs_2_, bf16[8192,640]{1,0:T(8,128)(2,1)} %refs_3_.7, ...), custom_call_target="tpu_custom_call" | custom-call | flops 335544320 | bytes 10485760 | tf_op jit(solution)/shard_map/base/pallas_call | solution.py:479
  24.8 1.0 %collective-permute-done.11 = bf16[24,128]{1,0:T(8,128)(2,1)S(1)} collective-permute-done((bf16[24,128]{1,0:T(8,128)(2,1)S(1)}, bf16[24,128]{1,0:T(8,128)(2,1)S(1)}, u32[]{:S(2)}, u32[]{:S(2)}) %collective-permute-start.11) | collective-permute-done | bytes 6176 | tf_op jit(solution)/shard_map/ppermute | solution.py:18
  25.9 0.0 copy-start.3
  25.9 0.0 copy-start.5
  25.9 0.1 collective-permute-start.12
  26.0 1.3 %collective-permute-start.13 = (bf16[24,128]{1,0:T(8,128)(2,1)S(1)}, bf16[24,128]{1,0:T(8,128)(2,1)S(1)}, u32[]{:S(2)}, u32[]{:S(2)}) collective-permute-start(bf16[24,128]{1,0:T(8,128)(2,1)S(1)} %add_add_fusion.1.refs_4_), channel_id=1, source_target_pairs={{0,2},{1,3},{2,0},{3,1},{4,6},{5,7},{6,4},{7,5},{8,10},{9,11},{10,... | collective-permute-start | bytes 18440 | tf_op jit(solution)/shard_map/ppermute | solution.py:18
  27.2 0.6 collective-permute-start.14
  27.8 2.5 %base.5.refs_5_ = f32[64,640]{1,0:T(8,128)S(1)} custom-call(bf16[32,8320]{1,0:T(8,128)(2,1)S(1)} %pack.2.refs_2_.refs_3_.refs_0_, bf16[32,8320]{1,0:T(8,128)(2,1)S(1)} %collective-permute-done.7.refs_1_, bf16[2048,640]{1,0:T(8,128)(2,1)S(1)} %get-tuple-element.55.refs_2_, bf16[8192,640]{1,0:T(8,128)(2,1)} %refs_3_.7, bf16[24,128]{1,0:T(8,128)(2,1)S(1)} %add_add_fusion.1.refs_4_), custom_call_target="tpu_custom_call" | custom-call | flops 335544320 | bytes 10485760 | tf_op jit(solution)/shard_map/base/pallas_call | solution.py:479
  30.3 0.0 collective-permute-done.12
  30.4 0.7 lift.2
  31.0 11.3 %all_to_all.10 = bf16[16,4,640]{2,1,0:T(4,128)(2,1)S(1)} all-to-all(bf16[16,4,640]{2,1,0:T(4,128)(2,1)S(1)} %lift.2), channel_id=1, replica_groups=mesh['groups'=2,'tensor'=16] {'tensor'}, dimensions={0} | all-to-all | bytes 163840 | tf_op jit(solution)/shard_map/all_to_all | solution.py:22
  42.4 2.2 %attend.1.refs_7_ = bf16[4,8192]{1,0:T(4,128)(2,1)S(1)} custom-call(s32[4]{0:T(128)S(1)} %copy-done.5, bf16[4,10240]{1,0:T(4,128)(2,1)S(1)} %bitcast.12, bf16[4,8,384,128]{3,2,1,0:T(8,128)(2,1)S(1)} %copy-done.1, bf16[4,8,384,128]{3,2,1,0:T(8,128)(2,1)S(1)} %copy-done.2), custom_call_target="tpu_custom_call" | custom-call | flops 50331648 | bytes 6291456 | tf_op jit(solution)/shard_map/attend/pallas_call | solution.py:546
  44.5 0.0 copy-start
  44.5 0.7 collective-permute-start.15
  45.2 0.1 collective-permute-start.17
  45.3 3.7 %collective-permute-start.19 = (bf16[4,8192]{1,0:T(4,128)(2,1)S(1)}, bf16[4,8192]{1,0:T(4,128)(2,1)S(1)}, u32[]{:S(2)}, u32[]{:S(2)}) collective-permute-start(bf16[4,8192]{1,0:T(4,128)(2,1)S(1)} %attend.1.refs_7_), channel_id=1, source_target_pairs={{0,8},{1,9},{2,10},{3,11},{4,12},{5,13},{6,14},{7,15},{8,0},{9,1},... | collective-permute-start | bytes 196616 | tf_op jit(solution)/shard_map/ppermute | solution.py:18
  49.0 0.0 collective-permute-start.21
  49.0 2.4 %collective-permute-done.15.refs_0_.refs_4_ = bf16[4,8192]{1,0:T(4,128)(2,1)S(1)} collective-permute-done((bf16[4,8192]{1,0:T(4,128)(2,1)S(1)}, bf16[4,8192]{1,0:T(4,128)(2,1)S(1)}, u32[]{:S(2)}, u32[]{:S(2)}) %collective-permute-start.15) | collective-permute-done | bytes 65568 | tf_op jit(solution)/shard_map/ppermute | solution.py:18
  51.4 0.0 collective-permute-start.16
  51.4 0.0 collective-permute-done.17.refs_6_
  51.4 2.0 %collective-permute-start.18 = (bf16[4,8192]{1,0:T(4,128)(2,1)S(1)}, bf16[4,8192]{1,0:T(4,128)(2,1)S(1)}, u32[]{:S(2)}, u32[]{:S(2)}) collective-permute-start(bf16[4,8192]{1,0:T(4,128)(2,1)S(1)} %collective-permute-done.17.refs_6_), channel_id=1, source_target_pairs={{0,2},{1,3},{2,0},{3,1},{4,6},{5,7},{6,4},{7,5},{8,10},{9,11},{10,... | collective-permute-start | bytes 196616 | tf_op jit(solution)/shard_map/ppermute | solution.py:18
  53.4 0.1 collective-permute-start.20
  53.5 1.9 %load.3 = (bf16[1024,512]{1,0:T(8,128)(2,1)S(1)}, bf16[2048,512]{1,0:T(8,128)(2,1)S(1)}) custom-call(bf16[4,8192]{1,0:T(4,128)(2,1)S(1)} %collective-permute-done.15.refs_0_.refs_4_, bf16[8192,512]{1,0:T(8,128)(2,1)} %refs_3_.10), custom_call_target="tpu_custom_call" | custom-call | bytes 6291456 | tf_op jit(solution)/shard_map/load/pallas_call | solution.py:429
  55.4 0.0 collective-permute-done.21.refs_3_
  55.4 0.3 collective-permute-done.16.refs_0_
  55.6 0.7 collective-permute-done.18.refs_2_
  56.3 1.3 %collective-permute-done.20.refs_1_ = bf16[4,8192]{1,0:T(4,128)(2,1)S(1)} collective-permute-done((bf16[4,8192]{1,0:T(4,128)(2,1)S(1)}, bf16[4,8192]{1,0:T(4,128)(2,1)S(1)}, u32[]{:S(2)}, u32[]{:S(2)}) %collective-permute-start.20) | collective-permute-done | bytes 65568 | tf_op jit(solution)/shard_map/ppermute | solution.py:18
  57.7 0.1 pack.3.refs_2_.refs_0_
  57.8 0.1 collective-permute-start.25
  57.9 0.5 down.3.refs_4_
  58.4 0.0 collective-permute-start.22
  58.4 1.9 %collective-permute-start.23 = (bf16[8,128]{1,0:T(8,128)(2,1)S(1)}, bf16[8,128]{1,0:T(8,128)(2,1)S(1)}, u32[]{:S(2)}, u32[]{:S(2)}) collective-permute-start(bf16[8,128]{1,0:T(8,128)(2,1)S(1)} %down.3.refs_4_), channel_id=1, source_target_pairs={{0,8},{1,9},{2,10},{3,11},{4,12},{5,13},{6,14},{7,15},{8,0},{9,1},... | collective-permute-start | bytes 6152 | tf_op jit(solution)/shard_map/ppermute | solution.py:18
  60.3 2.5 %collective-permute-start.24 = (bf16[8,128]{1,0:T(8,128)(2,1)S(1)}, bf16[8,128]{1,0:T(8,128)(2,1)S(1)}, u32[]{:S(2)}, u32[]{:S(2)}) collective-permute-start(bf16[8,128]{1,0:T(8,128)(2,1)S(1)} %down.3.refs_4_), channel_id=1, source_target_pairs={{0,12},{1,13},{2,14},{3,15},{4,8},{5,9},{6,10},{7,11},{8,4},{9,5},... | collective-permute-start | bytes 6152 | tf_op jit(solution)/shard_map/ppermute | solution.py:18
  62.9 0.0 collective-permute-done.25.refs_1_
  62.9 2.1 %base.6.refs_4_ = f32[64,512]{1,0:T(8,128)S(1)} custom-call(bf16[32,8192]{1,0:T(8,128)(2,1)S(1)} %pack.3.refs_2_.refs_0_, bf16[32,8192]{1,0:T(8,128)(2,1)S(1)} %collective-permute-done.25.refs_1_, bf16[1024,512]{1,0:T(8,128)(2,1)S(1)} %get-tuple-element.67.refs_2_, bf16[8192,512]{1,0:T(8,128)(2,1)} %refs_3_.10, bf16[8,128]{1,0:T(8,128)(2,1)S(1)} %down.3.refs_4_), custom_call_target="tpu_custom_call" | custom-call | flops 268435456 | bytes 8388608 | tf_op jit(solution)/shard_map/base/pallas_call | solution.py:479
  65.0 0.7 collective-permute-done.24
  65.7 0.1 collective-permute-start.26
  65.8 0.8 collective-permute-start.27
  66.6 1.1 %collective-permute-start.28 = (bf16[8,128]{1,0:T(8,128)(2,1)S(1)}, bf16[8,128]{1,0:T(8,128)(2,1)S(1)}, u32[]{:S(2)}, u32[]{:S(2)}) collective-permute-start(bf16[8,128]{1,0:T(8,128)(2,1)S(1)} %add_add_fusion.3.refs_4_), channel_id=1, source_target_pairs={{0,3},{1,2},{2,1},{3,0},{4,7},{5,6},{6,5},{7,4},{8,11},{9,10},{10,... | collective-permute-start | bytes 6152 | tf_op jit(solution)/shard_map/ppermute | solution.py:18
  67.7 1.8 %base.7.refs_5_ = f32[64,512]{1,0:T(8,128)S(1)} custom-call(bf16[32,8192]{1,0:T(8,128)(2,1)S(1)} %pack.3.refs_2_.refs_0_, bf16[32,8192]{1,0:T(8,128)(2,1)S(1)} %collective-permute-done.25.refs_1_, bf16[2048,512]{1,0:T(8,128)(2,1)S(1)} %get-tuple-element.71.refs_2_, bf16[8192,512]{1,0:T(8,128)(2,1)} %refs_3_.10, bf16[8,128]{1,0:T(8,128)(2,1)S(1)} %add_add_fusion.3.refs_4_), custom_call_target="tpu_custom_call" | custom-call | flops 268435456 | bytes 8388608 | tf_op jit(solution)/shard_map/base/pallas_call | solution.py:479
  69.5 0.1 collective-permute-done.28
  69.6 0.6 lift.3
  70.3 11.4 %all_to_all.11 = bf16[16,4,512]{2,1,0:T(4,128)(2,1)S(1)} all-to-all(bf16[16,4,512]{2,1,0:T(4,128)(2,1)S(1)} %lift.3), channel_id=1, replica_groups=mesh['groups'=2,'tensor'=16] {'tensor'}, dimensions={0} | all-to-all | bytes 131072 | tf_op jit(solution)/shard_map/all_to_all | solution.py:22
  81.6 0.6 copy.14
  (27 shorter events, 0.1 us)
Async XLA Ops:
  0.0 17.8 %collective-permute-start.8 = (bf16[2,8192,64]{1,2,0:T(8,128)(2,1)}, bf16[2,8192,64]{1,2,0:T(8,128)(2,1)S(1)}, u32[]{:S(2)}, u32[]{:S(2)}) collective-permute-start(bf16[2,8192,64]{1,2,0:T(8,128)(2,1)} %param.19), channel_id=1, source_target_pairs={{0,1},{1,0},{2,3},{3,2},{4,5},{5,4},{6,7},{7,6},{8,9},{9,8},{10,11... | collective-permute-start | bytes 6291464 | tf_op jit(solution)/shard_map/ppermute | solution.py:18
  1.5 7.7 %collective-permute-start = (bf16[4,8320]{1,0:T(4,128)(2,1)S(1)}, bf16[4,8320]{1,0:T(4,128)(2,1)S(1)}, u32[]{:S(2)}, u32[]{:S(2)}) collective-permute-start(bf16[4,8320]{1,0:T(4,128)(2,1)S(1)} %norm.1.refs_7_), channel_id=1, source_target_pairs={{0,12},{1,13},{2,14},{3,15},{4,8},{5,9},{6,10},{7,11},{8,4},{9,5},... | collective-permute-start | bytes 199688 | tf_op jit(solution)/shard_map/ppermute | solution.py:18
  6.2 5.6 %collective-permute-start.2 = (bf16[4,8320]{1,0:T(4,128)(2,1)S(1)}, bf16[4,8320]{1,0:T(4,128)(2,1)S(1)}, u32[]{:S(2)}, u32[]{:S(2)}) collective-permute-start(bf16[4,8320]{1,0:T(4,128)(2,1)S(1)} %norm.1.refs_7_), channel_id=1, source_target_pairs={{0,4},{1,5},{2,6},{3,7},{4,0},{5,1},{6,2},{7,3},{8,12},{9,13},{10,... | collective-permute-start | bytes 199688 | tf_op jit(solution)/shard_map/ppermute | solution.py:18
  6.2 7.1 %collective-permute-start.4 = (bf16[4,8320]{1,0:T(4,128)(2,1)S(1)}, bf16[4,8320]{1,0:T(4,128)(2,1)S(1)}, u32[]{:S(2)}, u32[]{:S(2)}) collective-permute-start(bf16[4,8320]{1,0:T(4,128)(2,1)S(1)} %norm.1.refs_7_), channel_id=1, source_target_pairs={{0,8},{1,9},{2,10},{3,11},{4,12},{5,13},{6,14},{7,15},{8,0},{9,1},... | collective-permute-start | bytes 199688 | tf_op jit(solution)/shard_map/ppermute | solution.py:18
  6.8 10.0 %collective-permute-start.6 = (bf16[4,8320]{1,0:T(4,128)(2,1)S(1)}, bf16[4,8320]{1,0:T(4,128)(2,1)S(1)}, u32[]{:S(2)}, u32[]{:S(2)}) collective-permute-start(bf16[4,8320]{1,0:T(4,128)(2,1)S(1)} %norm.1.refs_7_), channel_id=1, source_target_pairs={{0,2},{1,3},{2,0},{3,1},{4,6},{5,7},{6,4},{7,5},{8,10},{9,11},{10,... | collective-permute-start | bytes 199688 | tf_op jit(solution)/shard_map/ppermute | solution.py:18
  9.2 7.6 %collective-permute-start.1 = (bf16[4,8320]{1,0:T(4,128)(2,1)S(1)}, bf16[4,8320]{1,0:T(4,128)(2,1)S(1)}, u32[]{:S(2)}, u32[]{:S(2)}) collective-permute-start(bf16[4,8320]{1,0:T(4,128)(2,1)S(1)} %collective-permute-done.refs_0_.refs_4_), channel_id=1, source_target_pairs={{0,2},{1,3},{2,0},{3,1},{4,6},{5,7},{6,4},{7,5},{8,10},{9,11},{10,... | collective-permute-start | bytes 199688 | tf_op jit(solution)/shard_map/ppermute | solution.py:18
  11.8 5.1 %collective-permute-start.3 = (bf16[4,8320]{1,0:T(4,128)(2,1)S(1)}, bf16[4,8320]{1,0:T(4,128)(2,1)S(1)}, u32[]{:S(2)}, u32[]{:S(2)}) collective-permute-start(bf16[4,8320]{1,0:T(4,128)(2,1)S(1)} %collective-permute-done.2.refs_6_), channel_id=1, source_target_pairs={{0,2},{1,3},{2,0},{3,1},{4,6},{5,7},{6,4},{7,5},{8,10},{9,11},{10,... | collective-permute-start | bytes 199688 | tf_op jit(solution)/shard_map/ppermute | solution.py:18
  13.3 4.3 %collective-permute-start.5 = (bf16[4,8320]{1,0:T(4,128)(2,1)S(1)}, bf16[4,8320]{1,0:T(4,128)(2,1)S(1)}, u32[]{:S(2)}, u32[]{:S(2)}) collective-permute-start(bf16[4,8320]{1,0:T(4,128)(2,1)S(1)} %collective-permute-done.4.refs_5_), channel_id=1, source_target_pairs={{0,2},{1,3},{2,0},{3,1},{4,6},{5,7},{6,4},{7,5},{8,10},{9,11},{10,... | collective-permute-start | bytes 199688 | tf_op jit(solution)/shard_map/ppermute | solution.py:18
  17.7 4.7 %collective-permute-start.7 = (bf16[32,8320]{1,0:T(8,128)(2,1)S(1)}, bf16[32,8320]{1,0:T(8,128)(2,1)S(1)}, u32[]{:S(2)}, u32[]{:S(2)}) collective-permute-start(bf16[32,8320]{1,0:T(8,128)(2,1)S(1)} %pack.2.refs_2_.refs_3_.refs_0_), channel_id=1, source_target_pairs={{0,1},{1,0},{2,3},{3,2},{4,5},{5,4},{6,7},{7,6},{8,9},{9,8},{10,11... | collective-permute-start | bytes 1597448 | tf_op jit(solution)/shard_map/ppermute | solution.py:18
  18.9 5.9 %collective-permute-start.10 = (bf16[24,128]{1,0:T(8,128)(2,1)S(1)}, bf16[24,128]{1,0:T(8,128)(2,1)S(1)}, u32[]{:S(2)}, u32[]{:S(2)}) collective-permute-start(bf16[24,128]{1,0:T(8,128)(2,1)S(1)} %get-tuple-element.50.refs_4_), channel_id=1, source_target_pairs={{0,8},{1,9},{2,10},{3,11},{4,12},{5,13},{6,14},{7,15},{8,0},{9,1},... | collective-permute-start | bytes 18440 | tf_op jit(solution)/shard_map/ppermute | solution.py:18
  20.4 5.4 %collective-permute-start.11 = (bf16[24,128]{1,0:T(8,128)(2,1)S(1)}, bf16[24,128]{1,0:T(8,128)(2,1)S(1)}, u32[]{:S(2)}, u32[]{:S(2)}) collective-permute-start(bf16[24,128]{1,0:T(8,128)(2,1)S(1)} %get-tuple-element.50.refs_4_), channel_id=1, source_target_pairs={{0,12},{1,13},{2,14},{3,15},{4,8},{5,9},{6,10},{7,11},{8,4},{9,5},... | collective-permute-start | bytes 18440 | tf_op jit(solution)/shard_map/ppermute | solution.py:18
  22.0 3.8 %collective-permute-start.9 = (bf16[24,128]{1,0:T(8,128)(2,1)S(1)}, bf16[24,128]{1,0:T(8,128)(2,1)S(1)}, u32[]{:S(2)}, u32[]{:S(2)}) collective-permute-start(bf16[24,128]{1,0:T(8,128)(2,1)S(1)} %get-tuple-element.50.refs_4_), channel_id=1, source_target_pairs={{0,4},{1,5},{2,6},{3,7},{4,0},{5,1},{6,2},{7,3},{8,12},{9,13},{10,... | collective-permute-start | bytes 18440 | tf_op jit(solution)/shard_map/ppermute | solution.py:18
  25.9 4.5 %copy-start.3 = (bf16[32,16,640]{2,1,0:T(8,128)(2,1)S(1)}, bf16[32,16,640]{2,1,0:T(8,128)(2,1)}, u32[]{:S(2)}) copy-start(bf16[32,16,640]{2,1,0:T(8,128)(2,1)} %refs_3_.8) | copy-start | bytes 1966084
  25.9 16.5 %copy-start.5 = (s32[4]{0:T(128)S(1)}, s32[4]{0:T(128)}, u32[]{:S(2)}) copy-start(s32[4]{0:T(128)} %lengths_ref.1) | copy-start | bytes 52
  25.9 4.4 %collective-permute-start.12 = (bf16[24,128]{1,0:T(8,128)(2,1)S(1)}, bf16[24,128]{1,0:T(8,128)(2,1)S(1)}, u32[]{:S(2)}, u32[]{:S(2)}) collective-permute-start(bf16[24,128]{1,0:T(8,128)(2,1)S(1)} %add_add_fusion.1.refs_4_), channel_id=1, source_target_pairs={{0,1},{1,0},{2,3},{3,2},{4,5},{5,4},{6,7},{7,6},{8,9},{9,8},{10,11... | collective-permute-start | bytes 18440 | tf_op jit(solution)/shard_map/ppermute | solution.py:18
  26.0 4.3 %collective-permute-start.13 = (bf16[24,128]{1,0:T(8,128)(2,1)S(1)}, bf16[24,128]{1,0:T(8,128)(2,1)S(1)}, u32[]{:S(2)}, u32[]{:S(2)}) collective-permute-start(bf16[24,128]{1,0:T(8,128)(2,1)S(1)} %add_add_fusion.1.refs_4_), channel_id=1, source_target_pairs={{0,2},{1,3},{2,0},{3,1},{4,6},{5,7},{6,4},{7,5},{8,10},{9,11},{10,... | collective-permute-start | bytes 18440 | tf_op jit(solution)/shard_map/ppermute | solution.py:18
  27.2 3.1 %collective-permute-start.14 = (bf16[24,128]{1,0:T(8,128)(2,1)S(1)}, bf16[24,128]{1,0:T(8,128)(2,1)S(1)}, u32[]{:S(2)}, u32[]{:S(2)}) collective-permute-start(bf16[24,128]{1,0:T(8,128)(2,1)S(1)} %add_add_fusion.1.refs_4_), channel_id=1, source_target_pairs={{0,3},{1,2},{2,1},{3,0},{4,7},{5,6},{6,5},{7,4},{8,11},{9,10},{10,... | collective-permute-start | bytes 18440 | tf_op jit(solution)/shard_map/ppermute | solution.py:18
  27.8 14.5 %copy-start.1 = (bf16[4,8,384,128]{3,2,1,0:T(8,128)(2,1)S(1)}, bf16[4,8,384,128]{3,2,1,0:T(8,128)(2,1)}, u32[]{:S(2)}) copy-start(bf16[4,8,384,128]{3,2,1,0:T(8,128)(2,1)} %keys_ref.1) | copy-start | bytes 9437188
  27.8 14.5 %copy-start.2 = (bf16[4,8,384,128]{3,2,1,0:T(8,128)(2,1)S(1)}, bf16[4,8,384,128]{3,2,1,0:T(8,128)(2,1)}, u32[]{:S(2)}) copy-start(bf16[4,8,384,128]{3,2,1,0:T(8,128)(2,1)} %values_ref.1) | copy-start | bytes 9437188
  44.5 13.4 %copy-start = (bf16[2,8192,64]{1,2,0:T(8,128)(2,1)S(1)}, bf16[2,8192,64]{1,2,0:T(8,128)(2,1)}, u32[]{:S(2)}) copy-start(bf16[2,8192,64]{1,2,0:T(8,128)(2,1)} %param.19) | copy-start | bytes 6291460
  44.5 6.8 %collective-permute-start.15 = (bf16[4,8192]{1,0:T(4,128)(2,1)S(1)}, bf16[4,8192]{1,0:T(4,128)(2,1)S(1)}, u32[]{:S(2)}, u32[]{:S(2)}) collective-permute-start(bf16[4,8192]{1,0:T(4,128)(2,1)S(1)} %attend.1.refs_7_), channel_id=1, source_target_pairs={{0,12},{1,13},{2,14},{3,15},{4,8},{5,9},{6,10},{7,11},{8,4},{9,5},... | collective-permute-start | bytes 196616 | tf_op jit(solution)/shard_map/ppermute | solution.py:18
  45.2 6.2 %collective-permute-start.17 = (bf16[4,8192]{1,0:T(4,128)(2,1)S(1)}, bf16[4,8192]{1,0:T(4,128)(2,1)S(1)}, u32[]{:S(2)}, u32[]{:S(2)}) collective-permute-start(bf16[4,8192]{1,0:T(4,128)(2,1)S(1)} %attend.1.refs_7_), channel_id=1, source_target_pairs={{0,4},{1,5},{2,6},{3,7},{4,0},{5,1},{6,2},{7,3},{8,12},{9,13},{10,... | collective-permute-start | bytes 196616 | tf_op jit(solution)/shard_map/ppermute | solution.py:18
  45.3 8.1 %collective-permute-start.19 = (bf16[4,8192]{1,0:T(4,128)(2,1)S(1)}, bf16[4,8192]{1,0:T(4,128)(2,1)S(1)}, u32[]{:S(2)}, u32[]{:S(2)}) collective-permute-start(bf16[4,8192]{1,0:T(4,128)(2,1)S(1)} %attend.1.refs_7_), channel_id=1, source_target_pairs={{0,8},{1,9},{2,10},{3,11},{4,12},{5,13},{6,14},{7,15},{8,0},{9,1},... | collective-permute-start | bytes 196616 | tf_op jit(solution)/shard_map/ppermute | solution.py:18
  49.0 6.4 %collective-permute-start.21 = (bf16[4,8192]{1,0:T(4,128)(2,1)S(1)}, bf16[4,8192]{1,0:T(4,128)(2,1)S(1)}, u32[]{:S(2)}, u32[]{:S(2)}) collective-permute-start(bf16[4,8192]{1,0:T(4,128)(2,1)S(1)} %attend.1.refs_7_), channel_id=1, source_target_pairs={{0,2},{1,3},{2,0},{3,1},{4,6},{5,7},{6,4},{7,5},{8,10},{9,11},{10,... | collective-permute-start | bytes 196616 | tf_op jit(solution)/shard_map/ppermute | solution.py:18
  51.4 4.3 %collective-permute-start.16 = (bf16[4,8192]{1,0:T(4,128)(2,1)S(1)}, bf16[4,8192]{1,0:T(4,128)(2,1)S(1)}, u32[]{:S(2)}, u32[]{:S(2)}) collective-permute-start(bf16[4,8192]{1,0:T(4,128)(2,1)S(1)} %collective-permute-done.15.refs_0_.refs_4_), channel_id=1, source_target_pairs={{0,2},{1,3},{2,0},{3,1},{4,6},{5,7},{6,4},{7,5},{8,10},{9,11},{10,... | collective-permute-start | bytes 196616 | tf_op jit(solution)/shard_map/ppermute | solution.py:18
  51.4 5.0 %collective-permute-start.18 = (bf16[4,8192]{1,0:T(4,128)(2,1)S(1)}, bf16[4,8192]{1,0:T(4,128)(2,1)S(1)}, u32[]{:S(2)}, u32[]{:S(2)}) collective-permute-start(bf16[4,8192]{1,0:T(4,128)(2,1)S(1)} %collective-permute-done.17.refs_6_), channel_id=1, source_target_pairs={{0,2},{1,3},{2,0},{3,1},{4,6},{5,7},{6,4},{7,5},{8,10},{9,11},{10,... | collective-permute-start | bytes 196616 | tf_op jit(solution)/shard_map/ppermute | solution.py:18
  53.4 4.3 %collective-permute-start.20 = (bf16[4,8192]{1,0:T(4,128)(2,1)S(1)}, bf16[4,8192]{1,0:T(4,128)(2,1)S(1)}, u32[]{:S(2)}, u32[]{:S(2)}) collective-permute-start(bf16[4,8192]{1,0:T(4,128)(2,1)S(1)} %collective-permute-done.19.refs_5_), channel_id=1, source_target_pairs={{0,2},{1,3},{2,0},{3,1},{4,6},{5,7},{6,4},{7,5},{8,10},{9,11},{10,... | collective-permute-start | bytes 196616 | tf_op jit(solution)/shard_map/ppermute | solution.py:18
  57.8 5.1 %collective-permute-start.25 = (bf16[32,8192]{1,0:T(8,128)(2,1)S(1)}, bf16[32,8192]{1,0:T(8,128)(2,1)S(1)}, u32[]{:S(2)}, u32[]{:S(2)}) collective-permute-start(bf16[32,8192]{1,0:T(8,128)(2,1)S(1)} %pack.3.refs_2_.refs_0_), channel_id=1, source_target_pairs={{0,1},{1,0},{2,3},{3,2},{4,5},{5,4},{6,7},{7,6},{8,9},{9,8},{10,11... | collective-permute-start | bytes 1572872 | tf_op jit(solution)/shard_map/ppermute | solution.py:18
  58.4 6.6 %collective-permute-start.22 = (bf16[8,128]{1,0:T(8,128)(2,1)S(1)}, bf16[8,128]{1,0:T(8,128)(2,1)S(1)}, u32[]{:S(2)}, u32[]{:S(2)}) collective-permute-start(bf16[8,128]{1,0:T(8,128)(2,1)S(1)} %down.3.refs_4_), channel_id=1, source_target_pairs={{0,4},{1,5},{2,6},{3,7},{4,0},{5,1},{6,2},{7,3},{8,12},{9,13},{10,... | collective-permute-start | bytes 6152 | tf_op jit(solution)/shard_map/ppermute | solution.py:18
  58.4 6.6 %collective-permute-start.23 = (bf16[8,128]{1,0:T(8,128)(2,1)S(1)}, bf16[8,128]{1,0:T(8,128)(2,1)S(1)}, u32[]{:S(2)}, u32[]{:S(2)}) collective-permute-start(bf16[8,128]{1,0:T(8,128)(2,1)S(1)} %down.3.refs_4_), channel_id=1, source_target_pairs={{0,8},{1,9},{2,10},{3,11},{4,12},{5,13},{6,14},{7,15},{8,0},{9,1},... | collective-permute-start | bytes 6152 | tf_op jit(solution)/shard_map/ppermute | solution.py:18
  60.3 5.4 %collective-permute-start.24 = (bf16[8,128]{1,0:T(8,128)(2,1)S(1)}, bf16[8,128]{1,0:T(8,128)(2,1)S(1)}, u32[]{:S(2)}, u32[]{:S(2)}) collective-permute-start(bf16[8,128]{1,0:T(8,128)(2,1)S(1)} %down.3.refs_4_), channel_id=1, source_target_pairs={{0,12},{1,13},{2,14},{3,15},{4,8},{5,9},{6,10},{7,11},{8,4},{9,5},... | collective-permute-start | bytes 6152 | tf_op jit(solution)/shard_map/ppermute | solution.py:18
  65.7 3.9 %copy-start.4 = (bf16[32,16,512]{2,1,0:T(8,128)(2,1)S(1)}, bf16[32,16,512]{2,1,0:T(8,128)(2,1)}, u32[]{:S(2)}) copy-start(bf16[32,16,512]{2,1,0:T(8,128)(2,1)} %refs_3_.11) | copy-start | bytes 1572868
  65.7 3.7 %collective-permute-start.26 = (bf16[8,128]{1,0:T(8,128)(2,1)S(1)}, bf16[8,128]{1,0:T(8,128)(2,1)S(1)}, u32[]{:S(2)}, u32[]{:S(2)}) collective-permute-start(bf16[8,128]{1,0:T(8,128)(2,1)S(1)} %add_add_fusion.3.refs_4_), channel_id=1, source_target_pairs={{0,1},{1,0},{2,3},{3,2},{4,5},{5,4},{6,7},{7,6},{8,9},{9,8},{10,11... | collective-permute-start | bytes 6152 | tf_op jit(solution)/shard_map/ppermute | solution.py:18
  65.8 3.7 %collective-permute-start.27 = (bf16[8,128]{1,0:T(8,128)(2,1)S(1)}, bf16[8,128]{1,0:T(8,128)(2,1)S(1)}, u32[]{:S(2)}, u32[]{:S(2)}) collective-permute-start(bf16[8,128]{1,0:T(8,128)(2,1)S(1)} %add_add_fusion.3.refs_4_), channel_id=1, source_target_pairs={{0,2},{1,3},{2,0},{3,1},{4,6},{5,7},{6,4},{7,5},{8,10},{9,11},{10,... | collective-permute-start | bytes 6152 | tf_op jit(solution)/shard_map/ppermute | solution.py:18
  66.6 3.0 %collective-permute-start.28 = (bf16[8,128]{1,0:T(8,128)(2,1)S(1)}, bf16[8,128]{1,0:T(8,128)(2,1)S(1)}, u32[]{:S(2)}, u32[]{:S(2)}) collective-permute-start(bf16[8,128]{1,0:T(8,128)(2,1)S(1)} %add_add_fusion.3.refs_4_), channel_id=1, source_target_pairs={{0,3},{1,2},{2,1},{3,0},{4,7},{5,6},{6,5},{7,4},{8,11},{9,10},{10,... | collective-permute-start | bytes 6152 | tf_op jit(solution)/shard_map/ppermute | solution.py:18

commit v16 on v15

--- a/solution.py
+++ b/solution.py
@@ -66,9 +66,9 @@
     step = count // 4
     near, middle, far = (swap(x, count, k * step) for k in (1, 2, 3))
     step //= 2
-    across = [swap(p, count, step) for p in (far, near, middle, x)]
-    *across, loaded = lax.optimization_barrier((*across, beside(far)))
-    held = [pack([x, near, middle, far] + [across[i] for i in (3, 1, 2, 0)])]
+    across = [swap(p, count, step) for p in (middle, near, far, x)]
+    *across, loaded = lax.optimization_barrier((*across, beside(middle)))
+    held = [pack([x, near, middle, far] + [across[i] for i in (3, 1, 0, 2)])]
     step //= 2
     while step > 1:
         held = held + [swap(h, count, step) for h in held]

time: 82.6 us -> 83.7 us (1.013)
  transfers between devices with their start and end apart: 29 -> 29, of which waited for: 10 -> 8; matrix products, arithmetic and copies ran while one was open for 0% -> 0% of each run, Pallas kernels for 20% -> 20%
where the time goes in v16:
time: 83.7 us; the launch traced here: 83.4 us
  starting transfers between devices  29.8 us (36%)
  blocking collectives  23.1 us (28%)
  Pallas kernels  20 us (24%)
  waiting for transfers between devices  9.43 us (11%)
    ppermute x29, starting transfers between devices, swap(): return lax.ppermute(x, AXIS, [(i, i ^ offset) for i in range(count)])  29.8 us
    all_to_all x2, blocking collectives, exchange(): lax.all_to_all(x, AXIS, split_axis=0, concat_axis=0, axis_index_groups=gr...  23.1 us
    ppermute x29, waiting for transfers between devices, swap(): return lax.ppermute(x, AXIS, [(i, i ^ offset) for i in range(count)])  9.43 us
    pallas_call x4, Pallas kernels, base(): pl.pallas_call(functools.partial(base_kernel, len(pieces), start, length...  8.64 us
    pallas_call x2, Pallas kernels, load(): pl.pallas_call(functools.partial(load_kernel, [start for start, _ in part...  4.91 us
    pallas_call x1, Pallas kernels, local(): pl.pallas_call(attend_kernel, out_shape=jax.ShapeDtypeStruct((rows, width...  2.16 us
  transfers between devices with their start and end apart: 29, of which 8 were waited for; matrix products, arithmetic and copies ran while one was open for 0% of the time, Pallas kernels for 20%

profile of v16, /device:TPU:0, one launch (start us, length us, event | category | flops | bytes accessed | tf_op | source)
XLA Modules:
  0.0 83.4 jit_solution(16114224125390305468)
XLA Ops:
  0.0 0.5 collective-permute-start.8
  0.5 1.1 %norm.1.refs_7_ = bf16[4,8320]{1,0:T(4,128)(2,1)S(1)} custom-call(bf16[4,8192]{1,0:T(4,128)(2,1)} %hidden_hbm.1, bf16[8192]{0:T(1024)(128)(2,1)} %gain_hbm.1, s32[4]{0:T(128)} %bitcast.14, s32[32]{0:T(128)} %slots_hbm.1), custom_call_target="tpu_custom_call" | custom-call | tf_op jit(solution)/shard_map/norm/pallas_call | solution.py:401
  1.5 3.7 %collective-permute-start = (bf16[4,8320]{1,0:T(4,128)(2,1)S(1)}, bf16[4,8320]{1,0:T(4,128)(2,1)S(1)}, u32[]{:S(2)}, u32[]{:S(2)}) collective-permute-start(bf16[4,8320]{1,0:T(4,128)(2,1)S(1)} %norm.1.refs_7_), channel_id=1, source_target_pairs={{0,8},{1,9},{2,10},{3,11},{4,12},{5,13},{6,14},{7,15},{8,0},{9,1},... | collective-permute-start | bytes 199688 | tf_op jit(solution)/shard_map/ppermute | solution.py:18
  5.2 1.6 %collective-permute-start.2 = (bf16[4,8320]{1,0:T(4,128)(2,1)S(1)}, bf16[4,8320]{1,0:T(4,128)(2,1)S(1)}, u32[]{:S(2)}, u32[]{:S(2)}) collective-permute-start(bf16[4,8320]{1,0:T(4,128)(2,1)S(1)} %norm.1.refs_7_), channel_id=1, source_target_pairs={{0,4},{1,5},{2,6},{3,7},{4,0},{5,1},{6,2},{7,3},{8,12},{9,13},{10,... | collective-permute-start | bytes 199688 | tf_op jit(solution)/shard_map/ppermute | solution.py:18
  6.8 1.7 %collective-permute-start.6 = (bf16[4,8320]{1,0:T(4,128)(2,1)S(1)}, bf16[4,8320]{1,0:T(4,128)(2,1)S(1)}, u32[]{:S(2)}, u32[]{:S(2)}) collective-permute-start(bf16[4,8320]{1,0:T(4,128)(2,1)S(1)} %norm.1.refs_7_), channel_id=1, source_target_pairs={{0,2},{1,3},{2,0},{3,1},{4,6},{5,7},{6,4},{7,5},{8,10},{9,11},{10,... | collective-permute-start | bytes 199688 | tf_op jit(solution)/shard_map/ppermute | solution.py:18
  8.5 0.9 %collective-permute-done.refs_0_.refs_5_ = bf16[4,8320]{1,0:T(4,128)(2,1)S(1)} collective-permute-done((bf16[4,8320]{1,0:T(4,128)(2,1)S(1)}, bf16[4,8320]{1,0:T(4,128)(2,1)S(1)}, u32[]{:S(2)}, u32[]{:S(2)}) %collective-permute-start) | collective-permute-done | bytes 66592 | tf_op jit(solution)/shard_map/ppermute | solution.py:18
  9.3 1.7 %collective-permute-start.1 = (bf16[4,8320]{1,0:T(4,128)(2,1)S(1)}, bf16[4,8320]{1,0:T(4,128)(2,1)S(1)}, u32[]{:S(2)}, u32[]{:S(2)}) collective-permute-start(bf16[4,8320]{1,0:T(4,128)(2,1)S(1)} %collective-permute-done.refs_0_.refs_5_), channel_id=1, source_target_pairs={{0,2},{1,3},{2,0},{3,1},{4,6},{5,7},{6,4},{7,5},{8,10},{9,11},{10,... | collective-permute-start | bytes 199688 | tf_op jit(solution)/shard_map/ppermute | solution.py:18
  11.0 0.0 collective-permute-done.2.refs_6_
  11.0 0.4 collective-permute-start.3
  11.4 1.5 %collective-permute-done.4.refs_4_ = bf16[4,8320]{1,0:T(4,128)(2,1)S(1)} collective-permute-done((bf16[4,8320]{1,0:T(4,128)(2,1)S(1)}, bf16[4,8320]{1,0:T(4,128)(2,1)S(1)}, u32[]{:S(2)}, u32[]{:S(2)}) %collective-permute-start.4) | collective-permute-done | bytes 66592 | tf_op jit(solution)/shard_map/ppermute | solution.py:18
  12.8 1.5 %collective-permute-start.5 = (bf16[4,8320]{1,0:T(4,128)(2,1)S(1)}, bf16[4,8320]{1,0:T(4,128)(2,1)S(1)}, u32[]{:S(2)}, u32[]{:S(2)}) collective-permute-start(bf16[4,8320]{1,0:T(4,128)(2,1)S(1)} %collective-permute-done.4.refs_4_), channel_id=1, source_target_pairs={{0,2},{1,3},{2,0},{3,1},{4,6},{5,7},{6,4},{7,5},{8,10},{9,11},{10,... | collective-permute-start | bytes 199688 | tf_op jit(solution)/shard_map/ppermute | solution.py:18
  14.3 3.0 %load.2 = (bf16[2,48,8192]{2,1,0:T(8,128)(2,1)S(1)}, bf16[2048,640]{1,0:T(8,128)(2,1)S(1)}, bf16[2048,640]{1,0:T(8,128)(2,1)S(1)}) custom-call(bf16[4,8320]{1,0:T(4,128)(2,1)S(1)} %collective-permute-done.refs_0_.refs_5_, bf16[8192,640]{1,0:T(8,128)(2,1)} %refs_3_.7, bf16[2,64,8192]{2,1,0:T(8,128)(2,1)} %bitcast.9), custom_call_target="tpu_custom_call" | custom-call | bytes 10485760 | tf_op jit(solution)/shard_map/load/pallas_call | solution.py:429
  17.4 0.0 collective-permute-done.6.refs_3_
  17.4 0.0 collective-permute-done.5.refs_0_
  17.4 0.1 pack.2.refs_2_.refs_3_.refs_0_
  17.5 0.1 collective-permute-start.7
  17.6 0.0 collective-permute-done.8
  17.6 1.1 %down.2 = (bf16[24,128]{1,0:T(8,128)(2,1)S(1)}, bf16[2,16,8192]{2,1,0:T(8,128)(2,1)S(1)}) custom-call(bf16[2,48,8192]{2,1,0:T(8,128)(2,1)S(1)} %get-tuple-element.48.refs_0_, bf16[2,64,8192]{2,1,0:T(8,128)(2,1)S(1)} %bitcast.11, bf16[32,8320]{1,0:T(8,128)(2,1)S(1)} %pack.2.refs_2_.refs_3_.refs_0_, bf16[32,8320]{1,0:T(8,128)(2,1)S(1)} %pack.2.refs_2_.refs_3_.refs_0_), custom_call_target="tpu_custom_call" | custom-call | flops 100663296 | bytes 4194304 | tf_op jit(solution)/shard_map/down/pallas_call | solution.py:456
  18.7 2.1 %collective-permute-start.10 = (bf16[24,128]{1,0:T(8,128)(2,1)S(1)}, bf16[24,128]{1,0:T(8,128)(2,1)S(1)}, u32[]{:S(2)}, u32[]{:S(2)}) collective-permute-start(bf16[24,128]{1,0:T(8,128)(2,1)S(1)} %get-tuple-element.50.refs_4_), channel_id=1, source_target_pairs={{0,8},{1,9},{2,10},{3,11},{4,12},{5,13},{6,14},{7,15},{8,0},{9,1},... | collective-permute-start | bytes 18440 | tf_op jit(solution)/shard_map/ppermute | solution.py:18
  20.8 1.3 %collective-permute-start.11 = (bf16[24,128]{1,0:T(8,128)(2,1)S(1)}, bf16[24,128]{1,0:T(8,128)(2,1)S(1)}, u32[]{:S(2)}, u32[]{:S(2)}) collective-permute-start(bf16[24,128]{1,0:T(8,128)(2,1)S(1)} %get-tuple-element.50.refs_4_), channel_id=1, source_target_pairs={{0,12},{1,13},{2,14},{3,15},{4,8},{5,9},{6,10},{7,11},{8,4},{9,5},... | collective-permute-start | bytes 18440 | tf_op jit(solution)/shard_map/ppermute | solution.py:18
  22.1 0.5 collective-permute-start.9
  22.6 0.0 collective-permute-done.7.refs_1_
  22.6 2.3 %base.4.refs_4_ = f32[64,640]{1,0:T(8,128)S(1)} custom-call(bf16[32,8320]{1,0:T(8,128)(2,1)S(1)} %pack.2.refs_2_.refs_3_.refs_0_, bf16[32,8320]{1,0:T(8,128)(2,1)S(1)} %collective-permute-done.7.refs_1_, bf16[2048,640]{1,0:T(8,128)(2,1)S(1)} %get-tuple-element.51.refs_2_, bf16[8192,640]{1,0:T(8,128)(2,1)} %refs_3_.7, ...), custom_call_target="tpu_custom_call" | custom-call | flops 335544320 | bytes 10485760 | tf_op jit(solution)/shard_map/base/pallas_call | solution.py:479
  24.9 0.0 collective-permute-done.10
  24.9 1.3 %collective-permute-done.11 = bf16[24,128]{1,0:T(8,128)(2,1)S(1)} collective-permute-done((bf16[24,128]{1,0:T(8,128)(2,1)S(1)}, bf16[24,128]{1,0:T(8,128)(2,1)S(1)}, u32[]{:S(2)}, u32[]{:S(2)}) %collective-permute-start.11) | collective-permute-done | bytes 6176 | tf_op jit(solution)/shard_map/ppermute | solution.py:18
  26.3 0.0 collective-permute-done.9
  26.3 0.0 copy-start.3
  26.3 0.0 copy-start.5
  26.3 0.1 collective-permute-start.12
  26.4 1.3 %collective-permute-start.13 = (bf16[24,128]{1,0:T(8,128)(2,1)S(1)}, bf16[24,128]{1,0:T(8,128)(2,1)S(1)}, u32[]{:S(2)}, u32[]{:S(2)}) collective-permute-start(bf16[24,128]{1,0:T(8,128)(2,1)S(1)} %add_add_fusion.1.refs_4_), channel_id=1, source_target_pairs={{0,2},{1,3},{2,0},{3,1},{4,6},{5,7},{6,4},{7,5},{8,10},{9,11},{10,... | collective-permute-start | bytes 18440 | tf_op jit(solution)/shard_map/ppermute | solution.py:18
  27.6 0.6 collective-permute-start.14
  28.2 2.5 %base.5.refs_5_ = f32[64,640]{1,0:T(8,128)S(1)} custom-call(bf16[32,8320]{1,0:T(8,128)(2,1)S(1)} %pack.2.refs_2_.refs_3_.refs_0_, bf16[32,8320]{1,0:T(8,128)(2,1)S(1)} %collective-permute-done.7.refs_1_, bf16[2048,640]{1,0:T(8,128)(2,1)S(1)} %get-tuple-element.55.refs_2_, bf16[8192,640]{1,0:T(8,128)(2,1)} %refs_3_.7, bf16[24,128]{1,0:T(8,128)(2,1)S(1)} %add_add_fusion.1.refs_4_), custom_call_target="tpu_custom_call" | custom-call | flops 335544320 | bytes 10485760 | tf_op jit(solution)/shard_map/base/pallas_call | solution.py:479
  30.7 0.0 collective-permute-done.12
  30.7 0.0 collective-permute-done.14
  30.8 0.7 lift.2
  31.5 11.3 %all_to_all.10 = bf16[16,4,640]{2,1,0:T(4,128)(2,1)S(1)} all-to-all(bf16[16,4,640]{2,1,0:T(4,128)(2,1)S(1)} %lift.2), channel_id=1, replica_groups=mesh['groups'=2,'tensor'=16] {'tensor'}, dimensions={0} | all-to-all | bytes 163840 | tf_op jit(solution)/shard_map/all_to_all | solution.py:22
  42.8 2.2 %attend.1.refs_7_ = bf16[4,8192]{1,0:T(4,128)(2,1)S(1)} custom-call(s32[4]{0:T(128)S(1)} %copy-done.5, bf16[4,10240]{1,0:T(4,128)(2,1)S(1)} %bitcast.12, bf16[4,8,384,128]{3,2,1,0:T(8,128)(2,1)S(1)} %copy-done.1, bf16[4,8,384,128]{3,2,1,0:T(8,128)(2,1)S(1)} %copy-done.2), custom_call_target="tpu_custom_call" | custom-call | flops 50331648 | bytes 6291456 | tf_op jit(solution)/shard_map/attend/pallas_call | solution.py:546
  44.9 0.0 copy-start
  45.0 0.2 collective-permute-start.15
  45.2 1.0 %collective-permute-start.17 = (bf16[4,8192]{1,0:T(4,128)(2,1)S(1)}, bf16[4,8192]{1,0:T(4,128)(2,1)S(1)}, u32[]{:S(2)}, u32[]{:S(2)}) collective-permute-start(bf16[4,8192]{1,0:T(4,128)(2,1)S(1)} %attend.1.refs_7_), channel_id=1, source_target_pairs={{0,4},{1,5},{2,6},{3,7},{4,0},{5,1},{6,2},{7,3},{8,12},{9,13},{10,... | collective-permute-start | bytes 196616 | tf_op jit(solution)/shard_map/ppermute | solution.py:18
  46.2 3.2 %collective-permute-start.19 = (bf16[4,8192]{1,0:T(4,128)(2,1)S(1)}, bf16[4,8192]{1,0:T(4,128)(2,1)S(1)}, u32[]{:S(2)}, u32[]{:S(2)}) collective-permute-start(bf16[4,8192]{1,0:T(4,128)(2,1)S(1)} %attend.1.refs_7_), channel_id=1, source_target_pairs={{0,12},{1,13},{2,14},{3,15},{4,8},{5,9},{6,10},{7,11},{8,4},{9,5},... | collective-permute-start | bytes 196616 | tf_op jit(solution)/shard_map/ppermute | solution.py:18
  49.4 0.0 collective-permute-start.21
  49.4 3.1 %collective-permute-done.15.refs_0_.refs_5_ = bf16[4,8192]{1,0:T(4,128)(2,1)S(1)} collective-permute-done((bf16[4,8192]{1,0:T(4,128)(2,1)S(1)}, bf16[4,8192]{1,0:T(4,128)(2,1)S(1)}, u32[]{:S(2)}, u32[]{:S(2)}) %collective-permute-start.15) | collective-permute-done | bytes 65568 | tf_op jit(solution)/shard_map/ppermute | solution.py:18
  52.5 0.0 collective-permute-start.16
  52.5 2.0 %collective-permute-start.18 = (bf16[4,8192]{1,0:T(4,128)(2,1)S(1)}, bf16[4,8192]{1,0:T(4,128)(2,1)S(1)}, u32[]{:S(2)}, u32[]{:S(2)}) collective-permute-start(bf16[4,8192]{1,0:T(4,128)(2,1)S(1)} %collective-permute-done.17.refs_6_), channel_id=1, source_target_pairs={{0,2},{1,3},{2,0},{3,1},{4,6},{5,7},{6,4},{7,5},{8,10},{9,11},{10,... | collective-permute-start | bytes 196616 | tf_op jit(solution)/shard_map/ppermute | solution.py:18
  54.6 0.1 collective-permute-start.20
  54.6 1.9 %load.3 = (bf16[1024,512]{1,0:T(8,128)(2,1)S(1)}, bf16[2048,512]{1,0:T(8,128)(2,1)S(1)}) custom-call(bf16[4,8192]{1,0:T(4,128)(2,1)S(1)} %collective-permute-done.15.refs_0_.refs_5_, bf16[8192,512]{1,0:T(8,128)(2,1)} %refs_3_.10), custom_call_target="tpu_custom_call" | custom-call | bytes 6291456 | tf_op jit(solution)/shard_map/load/pallas_call | solution.py:429
  56.5 0.3 collective-permute-done.16.refs_1_
  56.8 0.7 collective-permute-done.18.refs_2_
  57.5 1.3 %collective-permute-done.20.refs_0_ = bf16[4,8192]{1,0:T(4,128)(2,1)S(1)} collective-permute-done((bf16[4,8192]{1,0:T(4,128)(2,1)S(1)}, bf16[4,8192]{1,0:T(4,128)(2,1)S(1)}, u32[]{:S(2)}, u32[]{:S(2)}) %collective-permute-start.20) | collective-permute-done | bytes 65568 | tf_op jit(solution)/shard_map/ppermute | solution.py:18
  58.8 0.1 pack.3.refs_2_.refs_0_
  59.0 0.1 collective-permute-start.25
  59.0 0.5 down.3.refs_4_
  59.6 1.6 %collective-permute-start.23 = (bf16[8,128]{1,0:T(8,128)(2,1)S(1)}, bf16[8,128]{1,0:T(8,128)(2,1)S(1)}, u32[]{:S(2)}, u32[]{:S(2)}) collective-permute-start(bf16[8,128]{1,0:T(8,128)(2,1)S(1)} %down.3.refs_4_), channel_id=1, source_target_pairs={{0,8},{1,9},{2,10},{3,11},{4,12},{5,13},{6,14},{7,15},{8,0},{9,1},... | collective-permute-start | bytes 6152 | tf_op jit(solution)/shard_map/ppermute | solution.py:18
  61.1 2.9 %collective-permute-start.24 = (bf16[8,128]{1,0:T(8,128)(2,1)S(1)}, bf16[8,128]{1,0:T(8,128)(2,1)S(1)}, u32[]{:S(2)}, u32[]{:S(2)}) collective-permute-start(bf16[8,128]{1,0:T(8,128)(2,1)S(1)} %down.3.refs_4_), channel_id=1, source_target_pairs={{0,12},{1,13},{2,14},{3,15},{4,8},{5,9},{6,10},{7,11},{8,4},{9,5},... | collective-permute-start | bytes 6152 | tf_op jit(solution)/shard_map/ppermute | solution.py:18
  64.0 2.1 %base.6.refs_4_ = f32[64,512]{1,0:T(8,128)S(1)} custom-call(bf16[32,8192]{1,0:T(8,128)(2,1)S(1)} %pack.3.refs_2_.refs_0_, bf16[32,8192]{1,0:T(8,128)(2,1)S(1)} %collective-permute-done.25.refs_1_, bf16[1024,512]{1,0:T(8,128)(2,1)S(1)} %get-tuple-element.67.refs_2_, bf16[8192,512]{1,0:T(8,128)(2,1)} %refs_3_.10, bf16[8,128]{1,0:T(8,128)(2,1)S(1)} %down.3.refs_4_), custom_call_target="tpu_custom_call" | custom-call | flops 268435456 | bytes 8388608 | tf_op jit(solution)/shard_map/base/pallas_call | solution.py:479
  66.2 0.3 collective-permute-done.24
  66.5 0.1 collective-permute-start.26
  66.6 0.4 collective-permute-start.27
  67.1 1.4 %collective-permute-start.28 = (bf16[8,128]{1,0:T(8,128)(2,1)S(1)}, bf16[8,128]{1,0:T(8,128)(2,1)S(1)}, u32[]{:S(2)}, u32[]{:S(2)}) collective-permute-start(bf16[8,128]{1,0:T(8,128)(2,1)S(1)} %add_add_fusion.3.refs_4_), channel_id=1, source_target_pairs={{0,3},{1,2},{2,1},{3,0},{4,7},{5,6},{6,5},{7,4},{8,11},{9,10},{10,... | collective-permute-start | bytes 6152 | tf_op jit(solution)/shard_map/ppermute | solution.py:18
  68.5 1.8 %base.7.refs_5_ = f32[64,512]{1,0:T(8,128)S(1)} custom-call(bf16[32,8192]{1,0:T(8,128)(2,1)S(1)} %pack.3.refs_2_.refs_0_, bf16[32,8192]{1,0:T(8,128)(2,1)S(1)} %collective-permute-done.25.refs_1_, bf16[2048,512]{1,0:T(8,128)(2,1)S(1)} %get-tuple-element.71.refs_2_, bf16[8192,512]{1,0:T(8,128)(2,1)} %refs_3_.10, bf16[8,128]{1,0:T(8,128)(2,1)S(1)} %add_add_fusion.3.refs_4_), custom_call_target="tpu_custom_call" | custom-call | flops 268435456 | bytes 8388608 | tf_op jit(solution)/shard_map/base/pallas_call | solution.py:479
  70.3 0.6 lift.3
  70.9 11.8 %all_to_all.11 = bf16[16,4,512]{2,1,0:T(4,128)(2,1)S(1)} all-to-all(bf16[16,4,512]{2,1,0:T(4,128)(2,1)S(1)} %lift.3), channel_id=1, replica_groups=mesh['groups'=2,'tensor'=16] {'tensor'}, dimensions={0} | all-to-all | bytes 131072 | tf_op jit(solution)/shard_map/all_to_all | solution.py:22
  82.8 0.6 copy.14
  (27 shorter events, 0.1 us)
Async XLA Ops:
  0.0 17.6 %collective-permute-start.8 = (bf16[2,8192,64]{1,2,0:T(8,128)(2,1)}, bf16[2,8192,64]{1,2,0:T(8,128)(2,1)S(1)}, u32[]{:S(2)}, u32[]{:S(2)}) collective-permute-start(bf16[2,8192,64]{1,2,0:T(8,128)(2,1)} %param.19), channel_id=1, source_target_pairs={{0,1},{1,0},{2,3},{3,2},{4,5},{5,4},{6,7},{7,6},{8,9},{9,8},{10,11... | collective-permute-start | bytes 6291464 | tf_op jit(solution)/shard_map/ppermute | solution.py:18
  1.5 7.8 %collective-permute-start = (bf16[4,8320]{1,0:T(4,128)(2,1)S(1)}, bf16[4,8320]{1,0:T(4,128)(2,1)S(1)}, u32[]{:S(2)}, u32[]{:S(2)}) collective-permute-start(bf16[4,8320]{1,0:T(4,128)(2,1)S(1)} %norm.1.refs_7_), channel_id=1, source_target_pairs={{0,8},{1,9},{2,10},{3,11},{4,12},{5,13},{6,14},{7,15},{8,0},{9,1},... | collective-permute-start | bytes 199688 | tf_op jit(solution)/shard_map/ppermute | solution.py:18
  5.2 5.8 %collective-permute-start.2 = (bf16[4,8320]{1,0:T(4,128)(2,1)S(1)}, bf16[4,8320]{1,0:T(4,128)(2,1)S(1)}, u32[]{:S(2)}, u32[]{:S(2)}) collective-permute-start(bf16[4,8320]{1,0:T(4,128)(2,1)S(1)} %norm.1.refs_7_), channel_id=1, source_target_pairs={{0,4},{1,5},{2,6},{3,7},{4,0},{5,1},{6,2},{7,3},{8,12},{9,13},{10,... | collective-permute-start | bytes 199688 | tf_op jit(solution)/shard_map/ppermute | solution.py:18
  6.8 6.1 %collective-permute-start.4 = (bf16[4,8320]{1,0:T(4,128)(2,1)S(1)}, bf16[4,8320]{1,0:T(4,128)(2,1)S(1)}, u32[]{:S(2)}, u32[]{:S(2)}) collective-permute-start(bf16[4,8320]{1,0:T(4,128)(2,1)S(1)} %norm.1.refs_7_), channel_id=1, source_target_pairs={{0,12},{1,13},{2,14},{3,15},{4,8},{5,9},{6,10},{7,11},{8,4},{9,5},... | collective-permute-start | bytes 199688 | tf_op jit(solution)/shard_map/ppermute | solution.py:18
  6.8 10.6 %collective-permute-start.6 = (bf16[4,8320]{1,0:T(4,128)(2,1)S(1)}, bf16[4,8320]{1,0:T(4,128)(2,1)S(1)}, u32[]{:S(2)}, u32[]{:S(2)}) collective-permute-start(bf16[4,8320]{1,0:T(4,128)(2,1)S(1)} %norm.1.refs_7_), channel_id=1, source_target_pairs={{0,2},{1,3},{2,0},{3,1},{4,6},{5,7},{6,4},{7,5},{8,10},{9,11},{10,... | collective-permute-start | bytes 199688 | tf_op jit(solution)/shard_map/ppermute | solution.py:18
  9.3 8.0 %collective-permute-start.1 = (bf16[4,8320]{1,0:T(4,128)(2,1)S(1)}, bf16[4,8320]{1,0:T(4,128)(2,1)S(1)}, u32[]{:S(2)}, u32[]{:S(2)}) collective-permute-start(bf16[4,8320]{1,0:T(4,128)(2,1)S(1)} %collective-permute-done.refs_0_.refs_5_), channel_id=1, source_target_pairs={{0,2},{1,3},{2,0},{3,1},{4,6},{5,7},{6,4},{7,5},{8,10},{9,11},{10,... | collective-permute-start | bytes 199688 | tf_op jit(solution)/shard_map/ppermute | solution.py:18
  11.0 6.4 %collective-permute-start.3 = (bf16[4,8320]{1,0:T(4,128)(2,1)S(1)}, bf16[4,8320]{1,0:T(4,128)(2,1)S(1)}, u32[]{:S(2)}, u32[]{:S(2)}) collective-permute-start(bf16[4,8320]{1,0:T(4,128)(2,1)S(1)} %collective-permute-done.2.refs_6_), channel_id=1, source_target_pairs={{0,2},{1,3},{2,0},{3,1},{4,6},{5,7},{6,4},{7,5},{8,10},{9,11},{10,... | collective-permute-start | bytes 199688 | tf_op jit(solution)/shard_map/ppermute | solution.py:18
  12.8 4.6 %collective-permute-start.5 = (bf16[4,8320]{1,0:T(4,128)(2,1)S(1)}, bf16[4,8320]{1,0:T(4,128)(2,1)S(1)}, u32[]{:S(2)}, u32[]{:S(2)}) collective-permute-start(bf16[4,8320]{1,0:T(4,128)(2,1)S(1)} %collective-permute-done.4.refs_4_), channel_id=1, source_target_pairs={{0,2},{1,3},{2,0},{3,1},{4,6},{5,7},{6,4},{7,5},{8,10},{9,11},{10,... | collective-permute-start | bytes 199688 | tf_op jit(solution)/shard_map/ppermute | solution.py:18
  17.5 5.1 %collective-permute-start.7 = (bf16[32,8320]{1,0:T(8,128)(2,1)S(1)}, bf16[32,8320]{1,0:T(8,128)(2,1)S(1)}, u32[]{:S(2)}, u32[]{:S(2)}) collective-permute-start(bf16[32,8320]{1,0:T(8,128)(2,1)S(1)} %pack.2.refs_2_.refs_3_.refs_0_), channel_id=1, source_target_pairs={{0,1},{1,0},{2,3},{3,2},{4,5},{5,4},{6,7},{7,6},{8,9},{9,8},{10,11... | collective-permute-start | bytes 1597448 | tf_op jit(solution)/shard_map/ppermute | solution.py:18
  18.7 6.2 %collective-permute-start.10 = (bf16[24,128]{1,0:T(8,128)(2,1)S(1)}, bf16[24,128]{1,0:T(8,128)(2,1)S(1)}, u32[]{:S(2)}, u32[]{:S(2)}) collective-permute-start(bf16[24,128]{1,0:T(8,128)(2,1)S(1)} %get-tuple-element.50.refs_4_), channel_id=1, source_target_pairs={{0,8},{1,9},{2,10},{3,11},{4,12},{5,13},{6,14},{7,15},{8,0},{9,1},... | collective-permute-start | bytes 18440 | tf_op jit(solution)/shard_map/ppermute | solution.py:18
  20.8 5.4 %collective-permute-start.11 = (bf16[24,128]{1,0:T(8,128)(2,1)S(1)}, bf16[24,128]{1,0:T(8,128)(2,1)S(1)}, u32[]{:S(2)}, u32[]{:S(2)}) collective-permute-start(bf16[24,128]{1,0:T(8,128)(2,1)S(1)} %get-tuple-element.50.refs_4_), channel_id=1, source_target_pairs={{0,12},{1,13},{2,14},{3,15},{4,8},{5,9},{6,10},{7,11},{8,4},{9,5},... | collective-permute-start | bytes 18440 | tf_op jit(solution)/shard_map/ppermute | solution.py:18
  22.1 4.1 %collective-permute-start.9 = (bf16[24,128]{1,0:T(8,128)(2,1)S(1)}, bf16[24,128]{1,0:T(8,128)(2,1)S(1)}, u32[]{:S(2)}, u32[]{:S(2)}) collective-permute-start(bf16[24,128]{1,0:T(8,128)(2,1)S(1)} %get-tuple-element.50.refs_4_), channel_id=1, source_target_pairs={{0,4},{1,5},{2,6},{3,7},{4,0},{5,1},{6,2},{7,3},{8,12},{9,13},{10,... | collective-permute-start | bytes 18440 | tf_op jit(solution)/shard_map/ppermute | solution.py:18
  26.3 4.5 %copy-start.3 = (bf16[32,16,640]{2,1,0:T(8,128)(2,1)S(1)}, bf16[32,16,640]{2,1,0:T(8,128)(2,1)}, u32[]{:S(2)}) copy-start(bf16[32,16,640]{2,1,0:T(8,128)(2,1)} %refs_3_.8) | copy-start | bytes 1966084
  26.3 16.5 %copy-start.5 = (s32[4]{0:T(128)S(1)}, s32[4]{0:T(128)}, u32[]{:S(2)}) copy-start(s32[4]{0:T(128)} %lengths_ref.1) | copy-start | bytes 52
  26.3 4.4 %collective-permute-start.12 = (bf16[24,128]{1,0:T(8,128)(2,1)S(1)}, bf16[24,128]{1,0:T(8,128)(2,1)S(1)}, u32[]{:S(2)}, u32[]{:S(2)}) collective-permute-start(bf16[24,128]{1,0:T(8,128)(2,1)S(1)} %add_add_fusion.1.refs_4_), channel_id=1, source_target_pairs={{0,1},{1,0},{2,3},{3,2},{4,5},{5,4},{6,7},{7,6},{8,9},{9,8},{10,11... | collective-permute-start | bytes 18440 | tf_op jit(solution)/shard_map/ppermute | solution.py:18
  26.4 4.3 %collective-permute-start.13 = (bf16[24,128]{1,0:T(8,128)(2,1)S(1)}, bf16[24,128]{1,0:T(8,128)(2,1)S(1)}, u32[]{:S(2)}, u32[]{:S(2)}) collective-permute-start(bf16[24,128]{1,0:T(8,128)(2,1)S(1)} %add_add_fusion.1.refs_4_), channel_id=1, source_target_pairs={{0,2},{1,3},{2,0},{3,1},{4,6},{5,7},{6,4},{7,5},{8,10},{9,11},{10,... | collective-permute-start | bytes 18440 | tf_op jit(solution)/shard_map/ppermute | solution.py:18
  27.6 3.1 %collective-permute-start.14 = (bf16[24,128]{1,0:T(8,128)(2,1)S(1)}, bf16[24,128]{1,0:T(8,128)(2,1)S(1)}, u32[]{:S(2)}, u32[]{:S(2)}) collective-permute-start(bf16[24,128]{1,0:T(8,128)(2,1)S(1)} %add_add_fusion.1.refs_4_), channel_id=1, source_target_pairs={{0,3},{1,2},{2,1},{3,0},{4,7},{5,6},{6,5},{7,4},{8,11},{9,10},{10,... | collective-permute-start | bytes 18440 | tf_op jit(solution)/shard_map/ppermute | solution.py:18
  28.2 14.5 %copy-start.1 = (bf16[4,8,384,128]{3,2,1,0:T(8,128)(2,1)S(1)}, bf16[4,8,384,128]{3,2,1,0:T(8,128)(2,1)}, u32[]{:S(2)}) copy-start(bf16[4,8,384,128]{3,2,1,0:T(8,128)(2,1)} %keys_ref.1) | copy-start | bytes 9437188
  28.2 14.5 %copy-start.2 = (bf16[4,8,384,128]{3,2,1,0:T(8,128)(2,1)S(1)}, bf16[4,8,384,128]{3,2,1,0:T(8,128)(2,1)}, u32[]{:S(2)}) copy-start(bf16[4,8,384,128]{3,2,1,0:T(8,128)(2,1)} %values_ref.1) | copy-start | bytes 9437188
  44.9 14.1 %copy-start = (bf16[2,8192,64]{1,2,0:T(8,128)(2,1)S(1)}, bf16[2,8192,64]{1,2,0:T(8,128)(2,1)}, u32[]{:S(2)}) copy-start(bf16[2,8192,64]{1,2,0:T(8,128)(2,1)} %param.19) | copy-start | bytes 6291460
  45.0 7.6 %collective-permute-start.15 = (bf16[4,8192]{1,0:T(4,128)(2,1)S(1)}, bf16[4,8192]{1,0:T(4,128)(2,1)S(1)}, u32[]{:S(2)}, u32[]{:S(2)}) collective-permute-start(bf16[4,8192]{1,0:T(4,128)(2,1)S(1)} %attend.1.refs_7_), channel_id=1, source_target_pairs={{0,8},{1,9},{2,10},{3,11},{4,12},{5,13},{6,14},{7,15},{8,0},{9,1},... | collective-permute-start | bytes 196616 | tf_op jit(solution)/shard_map/ppermute | solution.py:18
  45.2 7.3 %collective-permute-start.17 = (bf16[4,8192]{1,0:T(4,128)(2,1)S(1)}, bf16[4,8192]{1,0:T(4,128)(2,1)S(1)}, u32[]{:S(2)}, u32[]{:S(2)}) collective-permute-start(bf16[4,8192]{1,0:T(4,128)(2,1)S(1)} %attend.1.refs_7_), channel_id=1, source_target_pairs={{0,4},{1,5},{2,6},{3,7},{4,0},{5,1},{6,2},{7,3},{8,12},{9,13},{10,... | collective-permute-start | bytes 196616 | tf_op jit(solution)/shard_map/ppermute | solution.py:18
  46.2 8.4 %collective-permute-start.19 = (bf16[4,8192]{1,0:T(4,128)(2,1)S(1)}, bf16[4,8192]{1,0:T(4,128)(2,1)S(1)}, u32[]{:S(2)}, u32[]{:S(2)}) collective-permute-start(bf16[4,8192]{1,0:T(4,128)(2,1)S(1)} %attend.1.refs_7_), channel_id=1, source_target_pairs={{0,12},{1,13},{2,14},{3,15},{4,8},{5,9},{6,10},{7,11},{8,4},{9,5},... | collective-permute-start | bytes 196616 | tf_op jit(solution)/shard_map/ppermute | solution.py:18
  49.4 7.1 %collective-permute-start.21 = (bf16[4,8192]{1,0:T(4,128)(2,1)S(1)}, bf16[4,8192]{1,0:T(4,128)(2,1)S(1)}, u32[]{:S(2)}, u32[]{:S(2)}) collective-permute-start(bf16[4,8192]{1,0:T(4,128)(2,1)S(1)} %attend.1.refs_7_), channel_id=1, source_target_pairs={{0,2},{1,3},{2,0},{3,1},{4,6},{5,7},{6,4},{7,5},{8,10},{9,11},{10,... | collective-permute-start | bytes 196616 | tf_op jit(solution)/shard_map/ppermute | solution.py:18
  52.5 4.3 %collective-permute-start.16 = (bf16[4,8192]{1,0:T(4,128)(2,1)S(1)}, bf16[4,8192]{1,0:T(4,128)(2,1)S(1)}, u32[]{:S(2)}, u32[]{:S(2)}) collective-permute-start(bf16[4,8192]{1,0:T(4,128)(2,1)S(1)} %collective-permute-done.15.refs_0_.refs_5_), channel_id=1, source_target_pairs={{0,2},{1,3},{2,0},{3,1},{4,6},{5,7},{6,4},{7,5},{8,10},{9,11},{10,... | collective-permute-start | bytes 196616 | tf_op jit(solution)/shard_map/ppermute | solution.py:18
  52.5 5.0 %collective-permute-start.18 = (bf16[4,8192]{1,0:T(4,128)(2,1)S(1)}, bf16[4,8192]{1,0:T(4,128)(2,1)S(1)}, u32[]{:S(2)}, u32[]{:S(2)}) collective-permute-start(bf16[4,8192]{1,0:T(4,128)(2,1)S(1)} %collective-permute-done.17.refs_6_), channel_id=1, source_target_pairs={{0,2},{1,3},{2,0},{3,1},{4,6},{5,7},{6,4},{7,5},{8,10},{9,11},{10,... | collective-permute-start | bytes 196616 | tf_op jit(solution)/shard_map/ppermute | solution.py:18
  54.6 4.3 %collective-permute-start.20 = (bf16[4,8192]{1,0:T(4,128)(2,1)S(1)}, bf16[4,8192]{1,0:T(4,128)(2,1)S(1)}, u32[]{:S(2)}, u32[]{:S(2)}) collective-permute-start(bf16[4,8192]{1,0:T(4,128)(2,1)S(1)} %collective-permute-done.19.refs_4_), channel_id=1, source_target_pairs={{0,2},{1,3},{2,0},{3,1},{4,6},{5,7},{6,4},{7,5},{8,10},{9,11},{10,... | collective-permute-start | bytes 196616 | tf_op jit(solution)/shard_map/ppermute | solution.py:18
  59.0 5.1 %collective-permute-start.25 = (bf16[32,8192]{1,0:T(8,128)(2,1)S(1)}, bf16[32,8192]{1,0:T(8,128)(2,1)S(1)}, u32[]{:S(2)}, u32[]{:S(2)}) collective-permute-start(bf16[32,8192]{1,0:T(8,128)(2,1)S(1)} %pack.3.refs_2_.refs_0_), channel_id=1, source_target_pairs={{0,1},{1,0},{2,3},{3,2},{4,5},{5,4},{6,7},{7,6},{8,9},{9,8},{10,11... | collective-permute-start | bytes 1572872 | tf_op jit(solution)/shard_map/ppermute | solution.py:18
  59.6 6.6 %collective-permute-start.22 = (bf16[8,128]{1,0:T(8,128)(2,1)S(1)}, bf16[8,128]{1,0:T(8,128)(2,1)S(1)}, u32[]{:S(2)}, u32[]{:S(2)}) collective-permute-start(bf16[8,128]{1,0:T(8,128)(2,1)S(1)} %down.3.refs_4_), channel_id=1, source_target_pairs={{0,4},{1,5},{2,6},{3,7},{4,0},{5,1},{6,2},{7,3},{8,12},{9,13},{10,... | collective-permute-start | bytes 6152 | tf_op jit(solution)/shard_map/ppermute | solution.py:18
  59.6 6.6 %collective-permute-start.23 = (bf16[8,128]{1,0:T(8,128)(2,1)S(1)}, bf16[8,128]{1,0:T(8,128)(2,1)S(1)}, u32[]{:S(2)}, u32[]{:S(2)}) collective-permute-start(bf16[8,128]{1,0:T(8,128)(2,1)S(1)} %down.3.refs_4_), channel_id=1, source_target_pairs={{0,8},{1,9},{2,10},{3,11},{4,12},{5,13},{6,14},{7,15},{8,0},{9,1},... | collective-permute-start | bytes 6152 | tf_op jit(solution)/shard_map/ppermute | solution.py:18
  61.1 5.4 %collective-permute-start.24 = (bf16[8,128]{1,0:T(8,128)(2,1)S(1)}, bf16[8,128]{1,0:T(8,128)(2,1)S(1)}, u32[]{:S(2)}, u32[]{:S(2)}) collective-permute-start(bf16[8,128]{1,0:T(8,128)(2,1)S(1)} %down.3.refs_4_), channel_id=1, source_target_pairs={{0,12},{1,13},{2,14},{3,15},{4,8},{5,9},{6,10},{7,11},{8,4},{9,5},... | collective-permute-start | bytes 6152 | tf_op jit(solution)/shard_map/ppermute | solution.py:18
  66.5 3.8 %copy-start.4 = (bf16[32,16,512]{2,1,0:T(8,128)(2,1)S(1)}, bf16[32,16,512]{2,1,0:T(8,128)(2,1)}, u32[]{:S(2)}) copy-start(bf16[32,16,512]{2,1,0:T(8,128)(2,1)} %refs_3_.11) | copy-start | bytes 1572868
  66.5 3.7 %collective-permute-start.26 = (bf16[8,128]{1,0:T(8,128)(2,1)S(1)}, bf16[8,128]{1,0:T(8,128)(2,1)S(1)}, u32[]{:S(2)}, u32[]{:S(2)}) collective-permute-start(bf16[8,128]{1,0:T(8,128)(2,1)S(1)} %add_add_fusion.3.refs_4_), channel_id=1, source_target_pairs={{0,1},{1,0},{2,3},{3,2},{4,5},{5,4},{6,7},{7,6},{8,9},{9,8},{10,11... | collective-permute-start | bytes 6152 | tf_op jit(solution)/shard_map/ppermute | solution.py:18
  66.6 3.7 %collective-permute-start.27 = (bf16[8,128]{1,0:T(8,128)(2,1)S(1)}, bf16[8,128]{1,0:T(8,128)(2,1)S(1)}, u32[]{:S(2)}, u32[]{:S(2)}) collective-permute-start(bf16[8,128]{1,0:T(8,128)(2,1)S(1)} %add_add_fusion.3.refs_4_), channel_id=1, source_target_pairs={{0,2},{1,3},{2,0},{3,1},{4,6},{5,7},{6,4},{7,5},{8,10},{9,11},{10,... | collective-permute-start | bytes 6152 | tf_op jit(solution)/shard_map/ppermute | solution.py:18
  67.1 3.2 %collective-permute-start.28 = (bf16[8,128]{1,0:T(8,128)(2,1)S(1)}, bf16[8,128]{1,0:T(8,128)(2,1)S(1)}, u32[]{:S(2)}, u32[]{:S(2)}) collective-permute-start(bf16[8,128]{1,0:T(8,128)(2,1)S(1)} %add_add_fusion.3.refs_4_), channel_id=1, source_target_pairs={{0,3},{1,2},{2,1},{3,0},{4,7},{5,6},{6,5},{7,4},{8,11},{9,10},{10,... | collective-permute-start | bytes 6152 | tf_op jit(solution)/shard_map/ppermute | solution.py:18
